TPU v7x, 32 devices: a whole 2x2x4 slice. The times are simulated.
32 devices in a mesh: groups: 2 (over x), domain: 4 (over y, core), band: 4 (over z).
Axes of the slice: x: 2, y: 2, z: 4, core: 2. Of those that a mesh axis runs over, the one named last changes fastest.
Arguments:
- orbitals: bfloat16 [256, 8, 128, 128], P('band', ('groups', 'domain')), parts along dimension 1, may hold values from -8 to 8
- potential: float32 [8, 128, 128], P(('groups', 'domain')), parts along dimension 0, may hold values from -3 to 0.5
- projectors: bfloat16 [3072, 16, 128], P(('groups', 'domain')), parts along dimension 0, may hold values from -0.5 to 0.5
- tile_atom: int32 [3072], P(('groups', 'domain')), parts along dimension 0, may hold values from 0 to 255, as said below
- tile_line: int32 [3072], P(('groups', 'domain')), parts along dimension 0, may hold values from 0 to 127
- tile_count: int32 [8], P(('groups', 'domain')), parts along dimension 0, may hold values from 96 to 384, as said below
- energies: float32 [512, 16], P('groups'), parts along dimension 0, may hold values from -1.5 to 1.5
Outputs:
- applied: bfloat16 [256, 8, 128, 128], P('band', ('groups', 'domain')), parts along dimension 1
- subspace: float32 [2, 512, 256], P(None, ('groups', 'band'), 'domain'), parts along dimension 1
There are 2 independent parts, one for each index of `groups`. A program takes and returns all parts, laid end to end along the dimension named above; each array names one. Nothing has to cross between parts.
Inputs may be any that keep to these rules, and one draw needn't show every extreme that they name: `tile_count`: each subdomain's number of live tile slots; one subdomain has exactly 384 in every draw. `tile_atom`: an atom number for every slot, live or not; subdomain e owns atoms e * 64 to (e + 1) * 64 - 1, and a slot of subdomain d names an atom owned by d, d - 1 or d + 1 (no wrap-round at the slab's ends).
All inputs are finite; a program needn't handle non-finite values.
Results may differ from a plain program's by a relative error of at most 0.0075.
Values may be sent and summed in bfloat16 or wider, within the bound.
No kernel may reach another device: no remote copies, remote signals or barrier semaphores. Data moves between devices by JAX's collectives and lax.ppermute only.
A program may use at most 192 MiB of HBM per device.

v0:
```python
import jax
import jax.numpy as jnp
from jax import lax
from jax.sharding import PartitionSpec as P

kinetic_weight = 0.5


def extended(cells, sides, width):
    for axis, dim in sides:
        count = lax.axis_size(axis)
        ends = count - 1
        head = lax.slice_in_dim(cells, 0, width, axis=dim)
        tail = lax.slice_in_dim(cells, cells.shape[dim] - width, cells.shape[dim], axis=dim)
        cells = jnp.concatenate(
            [
                lax.ppermute(tail, axis, [(i, (i + 1) % count) for i in range(ends)]),
                cells,
                lax.ppermute(head, axis, [((i + 1) % count, i) for i in range(ends)]),
            ],
            axis=dim,
        )
    return cells


def pair_products(left, right):
    return lax.dot_general(
        left, right, (((1,), (1,)), ((), ())), preferred_element_type=jnp.float32
    )


def local(orbitals, potential, projectors, tile_atom, tile_line, tile_count, energies):
    states_here, planes, rows_y, cols_z = orbitals.shape
    slots = projectors.shape[0]
    atom_total, proj_count = energies.shape
    live = (jnp.arange(slots, dtype=jnp.int32) < tile_count[0]).astype(jnp.bfloat16)
    live_proj = projectors * live[:, None, None]
    flat = orbitals.reshape(states_here, planes * rows_y, cols_z)
    lines = flat[:, tile_line, :]
    part = jnp.einsum("tpz,stz->tps", live_proj, lines, preferred_element_type=jnp.float32)
    proj = jax.ops.segment_sum(part, tile_atom, num_segments=atom_total)
    proj = proj.reshape(atom_total, proj_count * states_here)
    total = lax.psum(proj, "domain")
    scaled = (total.reshape(atom_total, proj_count, states_here) * energies[:, :, None]).astype(
        jnp.bfloat16
    )
    picked = scaled[tile_atom]
    back = jnp.einsum("tps,tpz->stz", picked, live_proj, preferred_element_type=jnp.float32)
    nonlocal_part = (
        jnp.zeros((states_here, planes * rows_y, cols_z), jnp.float32).at[:, tile_line, :].add(back)
    )
    padded = extended(orbitals, (("domain", 1),), 1)
    field = orbitals.astype(jnp.float32)
    beside_all = padded[:, 2:].astype(jnp.float32) + padded[:, :-2].astype(jnp.float32)
    beside_all = beside_all + jnp.roll(field, 1, axis=2) + jnp.roll(field, -1, axis=2)
    beside_all = beside_all + jnp.roll(field, 1, axis=3) + jnp.roll(field, -1, axis=3)
    result = kinetic_weight * (6.0 * field - beside_all) + potential[None] * field
    result = result + nonlocal_part.reshape(states_here, planes, rows_y, cols_z)
    applied = result.astype(jnp.bfloat16)
    domain_count = lax.axis_size("domain")
    scale = 1.0 / (planes * rows_y * cols_z * domain_count)
    orb_flat = orbitals.reshape(states_here, -1)
    app_flat = applied.reshape(states_here, -1)
    piece = lax.all_gather(orb_flat, "band", axis=0, tiled=True)
    fresh = jnp.stack([pair_products(orb_flat, piece), pair_products(app_flat, piece)])
    subspace = (
        lax.psum_scatter(
            fresh.astype(jnp.bfloat16), "domain", scatter_dimension=2, tiled=True
        ).astype(jnp.float32)
        * scale
    )
    return (applied, subspace)


def solution(mesh):
    in_specs = (
        P("band", ("groups", "domain"), None, None),
        P(("groups", "domain"), None, None),
        P(("groups", "domain"), None, None),
        P(("groups", "domain")),
        P(("groups", "domain")),
        P(("groups", "domain")),
        P("groups", None),
    )
    out_specs = (P("band", ("groups", "domain"), None, None), P(None, ("groups", "band"), "domain"))
    return jax.shard_map(local, mesh=mesh, in_specs=in_specs, out_specs=out_specs, check_vma=False)
```

profile of v0, /device:TPU:1, one launch (start us, length us, event | category | flops | bytes accessed | tf_op | source)
XLA Modules:
  0.0 284.4 jit_solution(15368046440467375030)
XLA Ops:
  8.1 6.0 %fusion.30 = (bf16[64,1,128,128]{3,0,2,1:T(8,128)(2,1)}, f32[64,1,128,128]{3,0,2,1:T(8,128)}, bf16[64,128,128]{2,0,1:T(8,128)(2,1)S(1)}) fusion(bf16[64,1,128,128]{3,2,1,0:T(8,128)(2,1)} %param.7), kind=kLoop, calls=%fused_computation.43 | loop fusion | flops 1048576 | bytes 10485760 | tf_op args[0]
  14.7 13.3 %gather_fusion = bf16[384,64,128]{2,1,0:T(8,128)(2,1)} fusion(bf16[64,128,128]{2,0,1:T(8,128)(2,1)S(1)} %get-tuple-element.18, s32[1024]{0:T(1024)S(1)} %pad_clamp_fusion.1), kind=kCustom, calls=%fused_computation | custom fusion | bytes 12584448 | tf_op jit(solution)/shard_map/gather | solution.py:39
  28.1 8.5 %fusion = f32[384,16,64]{2,1,0:T(8,128)} fusion(bf16[384,64,128]{2,1,0:T(8,128)(2,1)} %gather_fusion, bf16[384,16,128]{2,1,0:T(8,128)(2,1)} %param.9, bf16[384]{0:T(512)(128)(2,1)S(1)} %fusion.25), kind=kOutput, calls=%fused_computation.4 | convolution fusion | flops 101449728 | bytes 9437952 | tf_op jit(solution)/shard_map/tpz,stz->tps/dot_general | solution.py:40
  36.6 1.4 broadcast_in_dim.21
  38.0 47.4 %scatter_fusion = f32[256,16,64]{2,1,0:T(8,128)} fusion(f32[256,16,64]{2,1,0:T(8,128)} %broadcast_in_dim.21, s32[384]{0:T(512)S(1)} %copy-done.8, f32[384,16,64]{2,1,0:T(8,128)} %fusion), kind=kCustom, calls=%fused_computation.2 | custom fusion | flops 393216 | bytes 4720128 | tf_op jit(solution)/shard_map/scatter-add | solution.py:41
  85.6 2.8 copy.46
  88.4 1.9 collective-permute-start
  90.4 4.7 %collective-permute-start.1 = (bf16[64,1,128,128]{3,0,2,1:T(8,128)(2,1)}, bf16[64,1,128,128]{3,0,2,1:T(8,128)(2,1)}, u32[]{:S(2)}, u32[]{:S(2)}) collective-permute-start(bf16[64,1,128,128]{3,0,2,1:T(8,128)(2,1)} %get-tuple-element.16), channel_id=1, source_target_pairs={{0,4},{4,8},{8,12},{1,5},{5,9},{9,13},{2,6},{6,10},{10,14},{3,7},{... | collective-permute-start | bytes 6291464 | tf_op jit(solution)/shard_map/ppermute | solution.py:17
  96.0 9.6 %fusion.28 = (f32[64,1,127,128]{3,0,2,1:T(8,128)}, f32[64,1,127,128]{3,0,2,1:T(8,128)}) fusion(f32[64,1,128,128]{3,0,2,1:T(8,128)} %get-tuple-element.17), kind=kLoop, calls=%fused_computation.41 | loop fusion | bytes 16646144 | tf_op jit(solution)/shard_map/jit(_roll_static)/slice | solution.py:55
  105.6 4.7 %fusion.27 = (f32[64,1,128,1]{3,0,2,1:T(8,128)}, f32[64,1,128,1]{3,0,2,1:T(8,128)}) fusion(f32[64,1,128,128]{3,0,2,1:T(8,128)S(1)} %copy-done), kind=kLoop, calls=%fused_computation.40 | loop fusion | bytes 131072 | tf_op jit(solution)/shard_map/jit(_roll_static)/slice | solution.py:56
  110.3 4.7 %fusion.26 = (f32[64,1,128,127]{3,0,2,1:T(8,128)}, f32[64,1,128,127]{3,0,2,1:T(8,128)}) fusion(f32[64,1,128,128]{3,0,2,1:T(8,128)S(1)} %copy-done), kind=kLoop, calls=%fused_computation.39 | loop fusion | bytes 16646144 | tf_op jit(solution)/shard_map/jit(_roll_static)/slice | solution.py:56
  114.9 36.2 %all-reduce.2.cloned.1.call-done = f32[256,16,64]{2,1,0:T(8,128)} async-done(((f32[256,16,64]{2,1,0:T(8,128)}), f32[256,16,64]{2,1,0:T(8,128)}) %all-reduce.2.cloned.1.call-update) | async-done | bytes 1048592 | tf_op jit(solution)/shard_map/psum | solution.py:43
  151.2 1.9 multiply_convert_fusion
  153.1 2.6 gather_fusion.1
  155.7 8.7 %fusion.13 = f32[384,64,128]{2,1,0:T(8,128)} fusion(bf16[384,16,64]{2,1,0:T(8,128)(2,1)} %gather_fusion.1, bf16[384,16,128]{2,1,0:T(8,128)(2,1)} %param.9, bf16[384]{0:T(512)(128)(2,1)S(1)} %fusion.25), kind=kOutput, calls=%fused_computation.20 | convolution fusion | flops 101449728 | bytes 14942976 | tf_op jit(solution)/shard_map/tps,tpz->stz/dot_general | solution.py:48
  164.3 2.5 broadcast_in_dim.19
  166.8 60.1 %scatter_fusion.1 = f32[64,128,128]{2,0,1:T(8,128)} fusion(f32[64,128,128]{2,0,1:T(8,128)} %broadcast_in_dim.19, s32[384]{0:T(512)S(1)} %compare_select_fusion.1, f32[384,64,128]{2,1,0:T(8,128)} %fusion.13), kind=kCustom, calls=%fused_computation.3 | custom fusion | flops 3145728 | bytes 37750272 | tf_op jit(solution)/shard_map/scatter-add | solution.py:50
  226.9 14.8 %fusion.9 = bf16[64,1,128,128]{3,0,2,1:T(8,128)(2,1)S(1)} fusion(f32[64,1,127,128]{3,0,2,1:T(8,128)} %get-tuple-element.13, f32[64,1,1,128]{3,0,2,1:T(8,128)S(1)} %get-tuple-element.15, f32[64,1,1,128]{3,0,2,1:T(8,128)S(1)} %get-tuple-element.14, f32[64,1,127,128]{3,0,2,1:T(8,128)} %get-tuple-element.12, f32[64,1,128,127]{3,0,2,1:T(8,128)} %get-tuple-element.9, ...), kind=kLoop, calls=%fused_computation.14 | loop fusion | flops 19922944 | bytes 29425664 | tf_op jit(solution)/shard_map/convert_element_type | solution.py:59
  241.7 1.3 copy-done.3
  243.0 2.7 copy.26
  245.7 6.4 %fusion.19 = bf16[1,64,256]{2,1,0:T(8,128)(2,1)S(1)} fusion(bf16[256,16384]{1,0:T(8,128)(2,1)} %all-gather.2.cloned.1.call-done, bf16[8,8,128,128]{3,2,1,0:T(8,128)(2,1)S(1)} %bitcast.36), kind=kOutput, calls=%fused_computation.25 | convolution fusion | flops 536887296 | bytes 10518528 | tf_op jit(solution)/shard_map/dot_general | solution.py:27
  252.2 2.9 %fusion.20 = bf16[1,64,256]{2,1,0:T(8,128)(2,1)S(1)} fusion(bf16[256,16384]{1,0:T(8,128)(2,1)S(1)} %copy-done.2, bf16[8,8,128,128]{3,2,1,0:T(8,128)(2,1)S(1)} %bitcast.37), kind=kOutput, calls=%fused_computation.26 | convolution fusion | flops 536887296 | bytes 10518528 | tf_op jit(solution)/shard_map/dot_general | solution.py:27
  256.0 2.7 copy.27
  258.7 16.7 %reduce-scatter.4.cloned.1.call-done = bf16[64,128]{1,0:T(8,128)(2,1)} async-done(((bf16[256,128]{1,0:T(8,128)(2,1)}), bf16[64,128]{1,0:T(8,128)(2,1)}) %reduce-scatter.4.cloned.1.call-update) | async-done | bytes 16400
  (41 shorter events, 3.5 us)
Async XLA Ops:
  8.0 6.0 %copy-start.9 = (s32[384]{0:T(512)S(1)}, s32[384]{0:T(512)}, u32[]{:S(2)}) copy-start(s32[384]{0:T(512)} %param.11) | copy-start | bytes 4612
  8.0 143.2 %all-reduce.2.cloned.1.call-start = ((), (), s32[]{:S(2)}) async-start(), calls=%async_computation.1 | async-start | bytes 4194304 | tf_op jit(solution)/shard_map/psum | solution.py:43
  28.1 10.0 %copy-start.8 = (s32[384]{0:T(512)S(1)}, s32[384]{0:T(512)}, u32[]{:S(2)}) copy-start(s32[384]{0:T(512)} %param.10) | copy-start | bytes 4612
  38.0 47.5 %copy-start.1 = (bf16[64,1,128,128]{3,2,1,0:T(8,128)(2,1)S(1)}, bf16[64,1,128,128]{3,2,1,0:T(8,128)(2,1)}, u32[]{:S(2)}) copy-start(bf16[64,1,128,128]{3,2,1,0:T(8,128)(2,1)} %param.7) | copy-start | bytes 6291460
  85.5 9.6 %copy-start.7 = (f32[256,16]{0,1:T(8,128)S(1)}, f32[256,16]{0,1:T(8,128)}, u32[]{:S(2)}) copy-start(f32[256,16]{0,1:T(8,128)} %param.13) | copy-start | bytes 49156
  85.5 160.2 %all-gather.2.cloned.1.call-start = ((), (), s32[]{:S(2)}) async-start(), calls=%async_computation.2 | async-start | bytes 10485760 | tf_op jit(solution)/shard_map/all_gather | solution.py:64
  88.4 187.1 %reduce-scatter.4.cloned.1.call-start = ((), (), s32[]{:S(2)}) async-start(), calls=%async_computation.3 | async-start | bytes 81920
  88.4 138.5 %collective-permute-start = (bf16[64,1,128,128]{3,0,2,1:T(8,128)(2,1)}, bf16[64,1,128,128]{3,0,2,1:T(8,128)(2,1)}, u32[]{:S(2)}, u32[]{:S(2)}) collective-permute-start(bf16[64,1,128,128]{3,0,2,1:T(8,128)(2,1)} %get-tuple-element.16), channel_id=1, source_target_pairs={{4,0},{8,4},{12,8},{5,1},{9,5},{13,9},{6,2},{10,6},{14,10},{7,3},{... | collective-permute-start | bytes 6291464 | tf_op jit(solution)/shard_map/ppermute | solution.py:19
  90.4 136.5 %collective-permute-start.1 = (bf16[64,1,128,128]{3,0,2,1:T(8,128)(2,1)}, bf16[64,1,128,128]{3,0,2,1:T(8,128)(2,1)}, u32[]{:S(2)}, u32[]{:S(2)}) collective-permute-start(bf16[64,1,128,128]{3,0,2,1:T(8,128)(2,1)} %get-tuple-element.16), channel_id=1, source_target_pairs={{0,4},{4,8},{8,12},{1,5},{5,9},{9,13},{2,6},{6,10},{10,14},{3,7},{... | collective-permute-start | bytes 6291464 | tf_op jit(solution)/shard_map/ppermute | solution.py:17
  96.0 9.6 %copy-start = (f32[64,1,128,128]{3,0,2,1:T(8,128)S(1)}, f32[64,1,128,128]{3,0,2,1:T(8,128)}, u32[]{:S(2)}) copy-start(f32[64,1,128,128]{3,0,2,1:T(8,128)} %get-tuple-element.17) | copy-start | bytes 12582916
  166.8 60.1 %copy-start.6 = (f32[1,128,128]{2,1,0:T(8,128)S(1)}, f32[1,128,128]{2,1,0:T(8,128)}, u32[]{:S(2)}) copy-start(f32[1,128,128]{2,1,0:T(8,128)} %param.8) | copy-start | bytes 196612
  241.7 1.3 copy-start.3
  245.7 6.5 %copy-start.2 = (bf16[256,16384]{1,0:T(8,128)(2,1)S(1)}, bf16[256,16384]{1,0:T(8,128)(2,1)}, u32[]{:S(2)}) copy-start(bf16[256,16384]{1,0:T(8,128)(2,1)} %all-gather.2.cloned.1.call-done) | copy-start | bytes 25165828
  245.7 6.5 %copy-start.5 = (bf16[64,1,128,128]{3,2,0,1:T(8,128)(2,1)S(1)}, bf16[64,1,128,128]{3,2,0,1:T(8,128)(2,1)}, u32[]{:S(2)}) copy-start(bf16[64,1,128,128]{3,2,0,1:T(8,128)(2,1)} %copy.26) | copy-start | bytes 6291460
  252.2 3.8 %copy-start.4 = (bf16[64,1,128,128]{3,0,2,1:T(8,128)(2,1)S(1)}, bf16[64,1,128,128]{3,0,2,1:T(8,128)(2,1)}, u32[]{:S(2)}) copy-start(bf16[64,1,128,128]{3,0,2,1:T(8,128)(2,1)} %copy-done.3) | copy-start | bytes 6291460
Sparse Core Ops, SparseCore 0:
  85.6 65.5 all-reduce.1
  256.1 19.2 reduce-scatter.3
Sparse Core Ops, SparseCore 1:
  88.4 151.7 all-gather.1
where the time goes:
time: 287 us; the launch traced here: 284 us
  other arithmetic  131 us (46%)
  waiting for transfers between devices  53 us (18%)
  local copies, waits for them, and re-layouts  50.9 us (18%)
  matrix products  26.5 us (9%)
  between operations  16.3 us (6%)
  starting transfers between devices  6.75 us (2%)
    scatter-add x1, other arithmetic, local(): jnp.zeros((states_here, planes * rows_y, cols_z), jnp.float32)  60.1 us
    scatter-add x1, other arithmetic, local(): proj = jax.ops.segment_sum(part, tile_atom, num_segments=atom_total)  47.4 us
    psum x1, waiting for transfers between devices, local(): total = lax.psum(proj, 'domain')  36.2 us
    unnamed x4, waiting for transfers between devices  16.8 us
    convert_element_type x1, other arithmetic, local(): applied = result.astype(jnp.bfloat16)  14.8 us
    gather x1, local copies, waits for them, and re-layouts, local(): lines = flat[:, tile_line, :]  13.3 us
    slice x2, local copies, waits for them, and re-layouts, local(): jnp.roll(field, -1, axis=2)  10.4 us
    slice x2, local copies, waits for them, and re-layouts, local(): jnp.roll(field, -1, axis=3)  9.34 us
  transfers between devices with their start and end apart: 5, of which 2 were waited for; matrix products, arithmetic and copies ran while one was open for 42% of the time, Pallas kernels for 0%

commit v1 on v0

v1 whole, which is shorter than its diff:
```python
import functools

import jax
import jax.numpy as jnp
from jax import lax
from jax.experimental import pallas as pl
from jax.experimental.pallas import tpu as pltpu
from jax.sharding import PartitionSpec as P

F32 = jnp.float32
BF16 = jnp.bfloat16
LANES = 128
VMEM_BYTES = 48 * 1024 * 1024
NT = (((1,), (1,)), ((), ()))


def call(kernel, outs, ins, scratch=(), flops=0, moved=0):
    spaces = [pltpu.SMEM if kind == "smem" else pltpu.VMEM for kind, _ in ins]
    return pl.pallas_call(
        kernel,
        out_shape=[jax.ShapeDtypeStruct(shape, kind) for shape, kind in outs],
        in_specs=[pl.BlockSpec(memory_space=space) for space in spaces],
        out_specs=[pl.BlockSpec(memory_space=pltpu.VMEM)] * len(outs),
        scratch_shapes=list(scratch),
        compiler_params=pltpu.CompilerParams(vmem_limit_bytes=VMEM_BYTES),
        cost_estimate=pl.CostEstimate(flops=flops, bytes_accessed=moved, transcendentals=0),
    )(*[value for _, value in ins])


def pack_kernel(bands, first, ids_ref, x_ref, xt_ref, *piece_refs):
    states, lines, _ = x_ref.shape
    share = lines // bands
    step = 16

    def rows(i, carry):
        y0 = pl.multiple_of(i * step, step)
        for s0 in range(0, states, step):
            block = x_ref[s0 : s0 + step, pl.ds(y0, step), :].astype(F32)
            turned = jnp.swapaxes(block, 0, 1).astype(BF16)
            xt_ref[pl.ds(y0, step), s0 : s0 + step, :] = turned
        return carry

    lax.fori_loop(0, lines // step, rows, 0)
    band = ids_ref[1]
    later, early = piece_refs[:bands], piece_refs[bands:]
    for k in range(bands):
        start = (band ^ k) * share
        for i in range(share - first + 1):
            later[k][i] = xt_ref[lax.rem(start + first + i, lines)]
        for i in range(first):
            early[k][i] = xt_ref[start + i]


def spread(tile, place, count):
    nothing = jnp.zeros_like(tile)
    return jnp.concatenate([jnp.where(place == k, tile, nothing) for k in range(count)], axis=0)


def project_kernel(words_ref, xt_ref, p_ref, below_ref, own_ref, above_ref, total):
    slots, proj_count, _ = p_ref.shape
    per_group = LANES // proj_count
    groups = own_ref.shape[0]
    total[...] = jnp.zeros_like(total)
    unroll = 8

    def body(i, carry):
        for u in range(unroll):
            t = i * unroll + u
            word = words_ref[t]
            line, group, place = word >> 16, (word >> 4) & 0xFFF, word & 0xF
            tile = spread(p_ref[t], place, per_group)
            total[group] += lax.dot_general(xt_ref[line], tile, NT, preferred_element_type=F32)
        return carry

    lax.fori_loop(0, slots // unroll, body, 0)
    below_ref[...] = total[:groups].astype(BF16)
    own_ref[...] = total[groups : 2 * groups]
    above_ref[...] = total[2 * groups :].astype(BF16)


def owner_kernel(bands, ids_ref, own_ref, left_ref, right_ref, energy_ref, scaled_ref, *piece_refs):
    groups = own_ref.shape[0]
    share = groups // bands
    first = ids_ref[0] * groups
    for g in range(groups):
        whole = own_ref[g] + left_ref[g].astype(F32) + right_ref[g].astype(F32)
        scaled_ref[g] = (whole * energy_ref[pl.ds(first + g, 1), :]).astype(BF16)
        piece_refs[-1][g] = whole.astype(BF16)
    for k in range(bands):
        for i in range(share):
            piece_refs[k][i] = piece_refs[-1][(ids_ref[1] ^ k) * share + i]


def apply_kernel(
    words_ref, xt_ref, p_ref, below_ref, above_ref, low_ref, own_ref, high_ref, pot_ref, out_ref, total, scaled
):
    slots, proj_count, _ = p_ref.shape
    lines, states, _ = xt_ref.shape
    groups = own_ref.shape[0]
    per_group = LANES // proj_count
    total[...] = jnp.zeros_like(total)
    unroll = 8

    scaled[:groups] = low_ref[...]
    scaled[groups : 2 * groups] = own_ref[...]
    scaled[2 * groups :] = high_ref[...]

    def body(i, carry):
        for u in range(unroll):
            t = i * unroll + u
            word = words_ref[t]
            line, group, place = word >> 16, (word >> 4) & 0xFFF, word & 0xF
            tile = spread(p_ref[t], place, per_group)
            total[line] += jnp.dot(scaled[group], tile, preferred_element_type=F32)
        return carry

    lax.fori_loop(0, slots // unroll, body, 0)

    step = 16

    def rows(i, carry):
        y0 = pl.multiple_of(i * step, step)
        results = []
        for j in range(step):
            y = y0 + j
            x = xt_ref[y].astype(F32)
            beside = xt_ref[lax.rem(y + 1, lines)].astype(F32) + xt_ref[lax.rem(y + lines - 1, lines)].astype(F32)
            beside += below_ref[y].astype(F32) + above_ref[y].astype(F32)
            beside += pltpu.roll(x, 1, 1) + pltpu.roll(x, x.shape[1] - 1, 1)
            value = (3.0 + pot_ref[pl.ds(y, 1), :]) * x - 0.5 * beside + total[y]
            results.append(value)
        turned = jnp.swapaxes(jnp.stack(results, axis=0), 0, 1)
        out_ref[:, pl.ds(y0, step), :] = turned.astype(BF16)
        return carry

    lax.fori_loop(0, lines // step, rows, 0)


def assemble_kernel(bands, ids_ref, *refs):
    pieces, outs = refs[:bands], refs[bands:]
    states = pieces[0].shape[1]
    band = ids_ref[1]
    at = 0
    for out in outs:
        for i in range(out.shape[0]):
            for k in range(bands):
                row = pl.multiple_of((band ^ k) * states, states)
                out[i, pl.ds(row, states), :] = pieces[k][at + i]
        at += out.shape[0]


def add_products(first, ids_ref, low_ref, high_ref, next_ref, low_beside, high_beside, pot_ref, share, acc):
    half = low_ref.shape[0]
    row = ids_ref[1] * share + first
    for part, ref, beside in ((0, low_ref, low_beside), (1, high_ref, high_beside)):
        xs, ys = [], []
        for i in range(half):
            here = ref[i]
            x = here.astype(F32)
            if i + 1 < half:
                after = ref[i + 1]
            else:
                after = high_ref[0] if part == 0 else next_ref[0]
            pot = pot_ref[pl.ds(row + part * half + i, 1), :]
            y = (3.0 + pot) * x - pltpu.roll(x, x.shape[1] - 1, 1)
            y = y - after.astype(F32) - beside[i].astype(F32)
            xs.append(here)
            ys.append(y.astype(BF16))
            if len(xs) == 4 or i + 1 == half:
                flat_x = jnp.concatenate(xs, axis=1)
                flat_y = jnp.concatenate(ys, axis=1)
                acc[0] += lax.dot_general(flat_x, flat_x, NT, preferred_element_type=F32)
                acc[1] += lax.dot_general(flat_y, flat_x, NT, preferred_element_type=F32)
                xs, ys = [], []


def gram_kernel(first, share, ids_ref, low, high, after, low_beside, high_beside, pot_ref, acc):
    acc[...] = jnp.zeros_like(acc)
    add_products(first, ids_ref, low, high, after, low_beside, high_beside, pot_ref, share, acc)


def final_kernel(
    bands, domains, share, ids_ref, low, high, after, low_beside, high_beside, pot_ref, begun, energy_ref, *refs
):
    pieces, out_ref, acc, projs = refs[:bands], refs[bands], refs[bands + 1], refs[bands + 2]
    acc[...] = begun[...]
    add_products(0, ids_ref, low, high, after, low_beside, high_beside, pot_ref, share, acc)
    groups, states = pieces[0].shape[:2]
    band = ids_ref[1]
    for k in range(bands):
        row = pl.multiple_of((band ^ k) * states, states)
        for g in range(groups):
            projs[g, pl.ds(row, states), :] = pieces[k][g]
    first = ids_ref[0] * groups * bands + band * groups
    for g in range(groups):
        here = projs[g]
        scaled = (here.astype(F32) * energy_ref[pl.ds(first + g, 1), :]).astype(BF16)
        acc[1] += lax.dot_general(scaled, here, NT, preferred_element_type=F32)
    gram = acc[0]
    hamil = 0.5 * (acc[1] + acc[1].T)
    total = gram.shape[0]
    rows, cols = total // bands, total // domains
    for r in range(bands):
        for c in range(domains):
            r0, c0 = r * rows, c * cols
            out_ref[r * domains + c, :, :cols] = gram[r0 : r0 + rows, c0 : c0 + cols].astype(BF16)
            out_ref[r * domains + c, :, cols:] = hamil[r0 : r0 + rows, c0 : c0 + cols].astype(BF16)


def local(orbitals, potential, projectors, tile_atom, tile_line, tile_count, energies):
    states, _, lines, cols_z = orbitals.shape
    slots, proj_count, _ = projectors.shape
    atom_total = energies.shape[0]
    domains, bands = lax.axis_size("domain"), lax.axis_size("band")
    domain, band = lax.axis_index("domain"), lax.axis_index("band")
    total_states = states * bands
    atoms_here = atom_total // domains
    per_group = LANES // proj_count
    groups = atoms_here // per_group
    share = lines // bands
    first = share // 4
    rest = share - first

    up = [(i, i + 1) for i in range(domains - 1)]
    down = [(i + 1, i) for i in range(domains - 1)]

    def swap(value, k):
        return lax.ppermute(value, "band", [(i, i ^ k) for i in range(bands)])

    ids = jnp.stack([domain, band]).astype(jnp.int32)
    near = jnp.clip(tile_atom - (domain - 1) * atoms_here, 0, 3 * atoms_here - 1)
    live = jnp.arange(slots, dtype=jnp.int32) < tile_count[0]
    place = jnp.where(live, near % per_group, per_group)
    words = (tile_line << 16) | ((near // per_group) << 4) | place
    field = orbitals.reshape(states, lines, cols_z)
    pot = potential.reshape(lines, cols_z)
    energy = energies.reshape(atom_total // per_group, LANES)

    packed = call(
        functools.partial(pack_kernel, bands, first),
        [((lines, states, cols_z), BF16)]
        + [((rest + 1, states, cols_z), BF16)] * bands
        + [((first, states, cols_z), BF16)] * bands,
        [("smem", ids), ("vmem", field)],
        moved=3 * field.size * 2,
    )
    xt, later, early = packed[0], packed[1 : 1 + bands], packed[1 + bands :]
    later = [later[0]] + [swap(later[k], k) for k in range(1, bands)]
    below = lax.ppermute(xt, "domain", up)
    above = lax.ppermute(xt, "domain", down)
    early = [early[0]] + [swap(early[k], k) for k in range(1, bands)]

    to_below, own, to_above = call(
        project_kernel,
        [((groups, states, LANES), BF16), ((groups, states, LANES), F32), ((groups, states, LANES), BF16)],
        [("smem", words), ("vmem", xt), ("vmem", projectors)],
        [pltpu.VMEM((3 * groups, states, LANES), F32)],
        flops=2 * slots * states * LANES * LANES * 4,
        moved=field.size * 4,
    )
    from_left = lax.ppermute(to_above, "domain", up)
    from_right = lax.ppermute(to_below, "domain", down)
    mine = call(
        functools.partial(owner_kernel, bands),
        [((groups, states, LANES), BF16)]
        + [((groups // bands, states, LANES), BF16)] * bands
        + [((groups, states, LANES), BF16)],
        [("smem", ids), ("vmem", own), ("vmem", from_left), ("vmem", from_right), ("vmem", energy)],
        moved=own.size * 12,
    )
    scaled, shares = mine[0], mine[1 : 1 + bands]
    low = lax.ppermute(scaled, "domain", up)
    high = lax.ppermute(scaled, "domain", down)
    shares = [shares[0]] + [swap(shares[k], k) for k in range(1, bands)]

    (applied,) = call(
        apply_kernel,
        [((states, lines, cols_z), BF16)],
        [
            ("smem", words), ("vmem", xt), ("vmem", projectors), ("vmem", below), ("vmem", above),
            ("vmem", low), ("vmem", scaled), ("vmem", high), ("vmem", pot),
        ],
        [pltpu.VMEM((lines, states, cols_z), F32), pltpu.VMEM((3 * groups, states, LANES), BF16)],
        flops=2 * slots * states * LANES * LANES * 4,
        moved=field.size * 10,
    )

    def gathered(pieces, counts):
        return call(
            functools.partial(assemble_kernel, bands),
            [((count, total_states, cols_z), BF16) for count in counts],
            [("smem", ids)] + [("vmem", piece) for piece in pieces],
            moved=sum(counts) * total_states * cols_z * 4,
        )

    def passed(halves):
        return lax.ppermute(halves[0], "domain", up), lax.ppermute(halves[1], "domain", down)

    late = gathered(later, (rest // 2, rest // 2, 1))
    late_beside = passed(late)
    (begun,) = call(
        functools.partial(gram_kernel, first, share),
        [((2, total_states, total_states), F32)],
        [("smem", ids)] + [("vmem", v) for v in (*late, *late_beside, pot)],
        flops=4 * total_states * total_states * rest * cols_z,
        moved=2 * rest * total_states * cols_z * 2,
    )
    soon = gathered(early, (first // 2, first // 2))
    soon_beside = passed(soon)
    (blocks,) = call(
        functools.partial(final_kernel, bands, domains, share),
        [((bands * domains, states, 2 * total_states // domains), BF16)],
        [("smem", ids)] + [("vmem", v) for v in (*soon, late[0], *soon_beside, pot, begun, energy, *shares)],
        [
            pltpu.VMEM((2, total_states, total_states), F32),
            pltpu.VMEM((groups // bands, total_states, LANES), BF16),
        ],
        flops=4 * total_states * total_states * first * cols_z,
        moved=2 * first * total_states * cols_z * 2,
    )
    landed = lax.all_to_all(blocks, ("band", "domain"), split_axis=0, concat_axis=0, tiled=True)
    scale = 1.0 / (lines * cols_z * domains)
    whole = jnp.sum(landed.astype(F32), axis=0) * scale
    cols = total_states // domains
    subspace = jnp.stack([whole[:, :cols], whole[:, cols:]])
    return applied.reshape(orbitals.shape), subspace


def solution(mesh):
    in_specs = (
        P("band", ("groups", "domain"), None, None),
        P(("groups", "domain"), None, None),
        P(("groups", "domain"), None, None),
        P(("groups", "domain")),
        P(("groups", "domain")),
        P(("groups", "domain")),
        P("groups", None),
    )
    out_specs = (P("band", ("groups", "domain"), None, None), P(None, ("groups", "band"), "domain"))
    return jax.shard_map(local, mesh=mesh, in_specs=in_specs, out_specs=out_specs, check_vma=False)
```

time: 287 us -> 151 us (0.53)
  other arithmetic: 131 us -> 0.79 us
  starting transfers between devices: 6.75 us -> 59.4 us
  Pallas kernels: 0 us -> 44.3 us
  local copies, waits for them, and re-layouts: 50.9 us -> 12.8 us
  matrix products: 26.5 us -> 0 us
  waiting for transfers between devices: 53 us -> 30.5 us
  between operations: 16.3 us -> 1.6 us
    scatter-add x2 -> x0, other arithmetic: 107 us -> none  [the longest x1 60.1 us: local(): jnp.zeros((states_here, planes * rows_y, cols_z), jnp.float32)]
    ppermute x2 -> x19, starting transfers between devices: 6.63 us -> 54 us  [the longest x9 24.5 us: swap(): return lax.ppermute(value, 'band', [(i, i ^ k) for i in range(bands)])]
    pallas_call x0 -> x8, Pallas kernels: none -> 44.3 us  [call(): pl.pallas_call(kernel, out_shape=[jax.ShapeDtypeStruct(shape, kind) for s...]
    psum x1 -> x0, waiting for transfers between devices: 36.2 us -> none  [local(): total = lax.psum(proj, 'domain')]
    ppermute x2 -> x19, waiting for transfers between devices: 0.01 us -> 26.6 us  [the longest x9 18.5 us: swap(): return lax.ppermute(value, 'band', [(i, i ^ k) for i in range(bands)])]
    dot_general x4 -> x0, matrix products: 26.5 us -> none  [the longest x2 9.34 us: pair_products(): lax.dot_general(left, right, (((1,), (1,)), ((), ())), preferred_element_...]
    slice x4 -> x0, local copies, waits for them, and re-layouts: 19.7 us -> none  [the longest x2 10.4 us: local(): jnp.roll(field, -1, axis=2)]
    unnamed x4 -> x0, waiting for transfers between devices: 16.8 us -> none
  transfers between devices with their start and end apart: 5 -> 20, of which waited for: 2 -> 8; matrix products, arithmetic and copies ran while one was open for 42% -> 2% of each run, Pallas kernels for 0% -> 15%
where the time goes in v1:
time: 151 us; the launch traced here: 149 us
  starting transfers between devices  59.4 us (39%)
  Pallas kernels  44.3 us (29%)
  waiting for transfers between devices  30.5 us (20%)
  local copies, waits for them, and re-layouts  12.8 us (8%)
  between operations  1.6 us (1%)
    pallas_call x8, Pallas kernels, call(): pl.pallas_call(kernel, out_shape=[jax.ShapeDtypeStruct(shape, kind) for s...  44.3 us
    ppermute x9, starting transfers between devices, swap(): return lax.ppermute(value, 'band', [(i, i ^ k) for i in range(bands)])  24.5 us
    ppermute x9, waiting for transfers between devices, swap(): return lax.ppermute(value, 'band', [(i, i ^ k) for i in range(bands)])  18.5 us
    unnamed x45, local copies, waits for them, and re-layouts  11.8 us
    ppermute x2, starting transfers between devices, passed(): lax.ppermute(halves[1], 'domain', down)  6.97 us
    ppermute x2, starting transfers between devices, passed(): lax.ppermute(halves[0], 'domain', up)  6.25 us
    all_to_all x1, starting transfers between devices, local(): lax.all_to_all(blocks, ('band', 'domain'), split_axis=0, concat_axis=0, t...  5.36 us
    ppermute x1, waiting for transfers between devices, local(): from_right = lax.ppermute(to_below, 'domain', down)  5.07 us
  transfers between devices with their start and end apart: 20, of which 8 were waited for; matrix products, arithmetic and copies ran while one was open for 2% of the time, Pallas kernels for 15%

profile of v1, /device:TPU:1, one launch (start us, length us, event | category | flops | bytes accessed | tf_op | source)
XLA Modules:
  0.0 149.4 jit_solution(15837502199096755185)
XLA Ops:
  0.7 4.2 %shard_map.86 = (bf16[128,64,128]{2,1,0:T(8,128)(2,1)}, bf16[25,64,128]{2,1,0:T(8,128)(2,1)S(1)}, bf16[25,64,128]{2,1,0:T(8,128)(2,1)S(1)}, bf16[25,64,128]{2,1,...) custom-call(s32[2]{0:T(128)S(1)} %pad_add_fusion.ids_ref, ...), custom_call_target="tpu_custom_call" | custom-call | bytes 6291456 | tf_op jit(solution)/shard_map/pallas_call | solution.py:19
  5.6 2.1 %collective-permute-start.9 = (bf16[25,64,128]{2,1,0:T(8,128)(2,1)S(1)}, bf16[25,64,128]{2,1,0:T(8,128)(2,1)S(1)}, u32[]{:S(2)}, u32[]{:S(2)}) collective-permute-start(bf16[25,64,128]{2,1,0:T(8,128)(2,1)S(1)} %get-tuple-element.36), channel_id=1, source_target_pairs={{0,1},{1,0},{2,3},{3,2},{4,5},{5,4},{6,7},{7,6},{8,9},{9,8},{10,11... | collective-permute-start | bytes 1228808 | tf_op jit(solution)/shard_map/ppermute | solution.py:228
  7.7 2.3 %collective-permute-start.10 = (bf16[25,64,128]{2,1,0:T(8,128)(2,1)S(1)}, bf16[25,64,128]{2,1,0:T(8,128)(2,1)S(1)}, u32[]{:S(2)}, u32[]{:S(2)}) collective-permute-start(bf16[25,64,128]{2,1,0:T(8,128)(2,1)S(1)} %get-tuple-element.37), channel_id=1, source_target_pairs={{0,2},{1,3},{2,0},{3,1},{4,6},{5,7},{6,4},{7,5},{8,10},{9,11},{10,... | collective-permute-start | bytes 1228808 | tf_op jit(solution)/shard_map/ppermute | solution.py:228
  10.0 3.1 %collective-permute-start.1 = (bf16[128,64,128]{2,1,0:T(8,128)(2,1)}, bf16[128,64,128]{2,1,0:T(8,128)(2,1)}, u32[]{:S(2)}, u32[]{:S(2)}) collective-permute-start(bf16[128,64,128]{2,1,0:T(8,128)(2,1)} %get-tuple-element.24.xt_ref), channel_id=1, source_target_pairs={{4,0},{8,4},{12,8},{5,1},{9,5},{13,9},{6,2},{10,6},{14,10},{7,3},{... | collective-permute-start | bytes 6291464 | tf_op jit(solution)/shard_map/ppermute | solution.py:250
  13.1 3.3 %collective-permute-start = (bf16[128,64,128]{2,1,0:T(8,128)(2,1)}, bf16[128,64,128]{2,1,0:T(8,128)(2,1)}, u32[]{:S(2)}, u32[]{:S(2)}) collective-permute-start(bf16[128,64,128]{2,1,0:T(8,128)(2,1)} %get-tuple-element.24.xt_ref), channel_id=1, source_target_pairs={{0,4},{4,8},{8,12},{1,5},{5,9},{9,13},{2,6},{6,10},{10,14},{3,7},{... | collective-permute-start | bytes 6291464 | tf_op jit(solution)/shard_map/ppermute | solution.py:249
  17.1 7.8 %collective-permute-done.9.refs_1_ = bf16[25,64,128]{2,1,0:T(8,128)(2,1)S(1)} collective-permute-done((bf16[25,64,128]{2,1,0:T(8,128)(2,1)S(1)}, bf16[25,64,128]{2,1,0:T(8,128)(2,1)S(1)}, u32[]{:S(2)}, u32[]{:S(2)}) %collective-permute-start.9) | collective-permute-done | bytes 409632 | tf_op jit(solution)/shard_map/ppermute | solution.py:228
  24.9 2.9 %collective-permute-start.7 = (bf16[8,64,128]{2,1,0:T(8,128)(2,1)}, bf16[8,64,128]{2,1,0:T(8,128)(2,1)S(1)}, u32[]{:S(2)}, u32[]{:S(2)}) collective-permute-start(bf16[8,64,128]{2,1,0:T(8,128)(2,1)} %get-tuple-element.31), channel_id=1, source_target_pairs={{0,2},{1,3},{2,0},{3,1},{4,6},{5,7},{6,4},{7,5},{8,10},{9,11},{10,... | collective-permute-start | bytes 393224 | tf_op jit(solution)/shard_map/ppermute | solution.py:228
  27.8 8.6 %collective-permute-done.11.refs_3_ = bf16[25,64,128]{2,1,0:T(8,128)(2,1)S(1)} collective-permute-done((bf16[25,64,128]{2,1,0:T(8,128)(2,1)S(1)}, bf16[25,64,128]{2,1,0:T(8,128)(2,1)S(1)}, u32[]{:S(2)}, u32[]{:S(2)}) %collective-permute-start.11) | collective-permute-done | bytes 409632 | tf_op jit(solution)/shard_map/ppermute | solution.py:228
  37.1 5.0 %collective-permute-start.15 = (bf16[12,256,128]{2,1,0:T(8,128)(2,1)S(1)}, bf16[12,256,128]{2,1,0:T(8,128)(2,1)S(1)}, u32[]{:S(2)}, u32[]{:S(2)}) collective-permute-start(bf16[12,256,128]{2,1,0:T(8,128)(2,1)S(1)} %get-tuple-element.40.high), channel_id=1, source_target_pairs={{4,0},{8,4},{12,8},{5,1},{9,5},{13,9},{6,2},{10,6},{14,10},{7,3},{... | collective-permute-start | bytes 2359304 | tf_op jit(solution)/shard_map/ppermute | solution.py:297
  42.8 3.2 %collective-permute-start.14 = (bf16[12,256,128]{2,1,0:T(8,128)(2,1)S(1)}, bf16[12,256,128]{2,1,0:T(8,128)(2,1)S(1)}, u32[]{:S(2)}, u32[]{:S(2)}) collective-permute-start(bf16[12,256,128]{2,1,0:T(8,128)(2,1)S(1)} %get-tuple-element.39.low.after), channel_id=1, source_target_pairs={{0,4},{4,8},{8,12},{1,5},{5,9},{9,13},{2,6},{6,10},{10,14},{3,7},{... | collective-permute-start | bytes 2359304 | tf_op jit(solution)/shard_map/ppermute | solution.py:297
  47.4 15.8 %shard_map.87 = (bf16[8,64,128]{2,1,0:T(8,128)(2,1)S(1)}, f32[8,64,128]{2,1,0:T(8,128)S(1)}, bf16[8,64,128]{2,1,0:T(8,128)(2,1)S(1)}) custom-call(s32[384]{0:T(512)S(1)} %fusion.2.words_ref, bf16[128,64,128]{2,1,0:T(8,128)(2,1)} %get-tuple-element.24.xt_ref, bf16[384,16,128]{2,1,0:T(8,128)(2,1)S(1)} %copy-done.15), custom_call_target="tpu_custom_call" | custom-call | flops 3221225472 | bytes 4194304 | tf_op jit(solution)/shard_map/pallas_call | solution.py:19
  64.4 2.4 %collective-permute-start.2 = (bf16[8,64,128]{2,1,0:T(8,128)(2,1)S(1)}, bf16[8,64,128]{2,1,0:T(8,128)(2,1)S(1)}, u32[]{:S(2)}, u32[]{:S(2)}) collective-permute-start(bf16[8,64,128]{2,1,0:T(8,128)(2,1)S(1)} %get-tuple-element.26), channel_id=1, source_target_pairs={{0,4},{4,8},{8,12},{1,5},{5,9},{9,13},{2,6},{6,10},{10,14},{3,7},{... | collective-permute-start | bytes 393224 | tf_op jit(solution)/shard_map/ppermute | solution.py:261
  66.9 1.9 %collective-permute-done.2.left_ref = bf16[8,64,128]{2,1,0:T(8,128)(2,1)S(1)} collective-permute-done((bf16[8,64,128]{2,1,0:T(8,128)(2,1)S(1)}, bf16[8,64,128]{2,1,0:T(8,128)(2,1)S(1)}, u32[]{:S(2)}, u32[]{:S(2)}) %collective-permute-start.2) | collective-permute-done | bytes 131104 | tf_op jit(solution)/shard_map/ppermute | solution.py:261
  71.4 5.1 %collective-permute-done.3.right_ref = bf16[8,64,128]{2,1,0:T(8,128)(2,1)S(1)} collective-permute-done((bf16[8,64,128]{2,1,0:T(8,128)(2,1)S(1)}, bf16[8,64,128]{2,1,0:T(8,128)(2,1)S(1)}, u32[]{:S(2)}, u32[]{:S(2)}) %collective-permute-start.3) | collective-permute-done | bytes 131104 | tf_op jit(solution)/shard_map/ppermute | solution.py:262
  77.1 3.3 %collective-permute-start.8 = (bf16[8,64,128]{2,1,0:T(8,128)(2,1)}, bf16[8,64,128]{2,1,0:T(8,128)(2,1)}, u32[]{:S(2)}, u32[]{:S(2)}) collective-permute-start(bf16[8,64,128]{2,1,0:T(8,128)(2,1)} %get-tuple-element.32), channel_id=1, source_target_pairs={{0,3},{1,2},{2,1},{3,0},{4,7},{5,6},{6,5},{7,4},{8,11},{9,10},{10,... | collective-permute-start | bytes 393224 | tf_op jit(solution)/shard_map/ppermute | solution.py:228
  86.4 10.3 %collective-permute-start.16 = (bf16[2,64,128]{2,1,0:T(8,128)(2,1)S(1)}, bf16[2,64,128]{2,1,0:T(8,128)(2,1)S(1)}, u32[]{:S(2)}, u32[]{:S(2)}) collective-permute-start(bf16[2,64,128]{2,1,0:T(8,128)(2,1)S(1)} %get-tuple-element.43), channel_id=1, source_target_pairs={{0,1},{1,0},{2,3},{3,2},{4,5},{5,4},{6,7},{7,6},{8,9},{9,8},{10,11... | collective-permute-start | bytes 98312 | tf_op jit(solution)/shard_map/ppermute | solution.py:228
  103.0 3.1 %collective-permute-start.12 = (bf16[4,256,128]{2,1,0:T(8,128)(2,1)S(1)}, bf16[4,256,128]{2,1,0:T(8,128)(2,1)S(1)}, u32[]{:S(2)}, u32[]{:S(2)}) collective-permute-start(bf16[4,256,128]{2,1,0:T(8,128)(2,1)S(1)} %get-tuple-element.33.low), channel_id=1, source_target_pairs={{0,4},{4,8},{8,12},{1,5},{5,9},{9,13},{2,6},{6,10},{10,14},{3,7},{... | collective-permute-start | bytes 786440 | tf_op jit(solution)/shard_map/ppermute | solution.py:297
  108.1 2.3 %collective-permute-start.18 = (bf16[2,64,128]{2,1,0:T(8,128)(2,1)S(1)}, bf16[2,64,128]{2,1,0:T(8,128)(2,1)S(1)}, u32[]{:S(2)}, u32[]{:S(2)}) collective-permute-start(bf16[2,64,128]{2,1,0:T(8,128)(2,1)S(1)} %get-tuple-element.45), channel_id=1, source_target_pairs={{0,3},{1,2},{2,1},{3,0},{4,7},{5,6},{6,5},{7,4},{8,11},{9,10},{10,... | collective-permute-start | bytes 98312 | tf_op jit(solution)/shard_map/ppermute | solution.py:228
  113.8 2.2 %shard_map.93 = bf16[16,64,128]{2,1,0:T(8,128)(2,1)} custom-call(s32[2]{0:T(128)S(1)} %copy-done.12, bf16[4,256,128]{2,1,0:T(8,128)(2,1)S(1)} %get-tuple-element.33.low, bf16[4,256,128]{2,1,0:T(8,128)(2,1)S(1)} %get-tuple-element.34.high, bf16[12,256,128]{2,1,0:T(8,128)(2,1)S(1)} %get-tuple-element.39.low.after, ...), custom_call_target="tpu_custom_call" | custom-call | flops 268435456 | bytes 1048576 | tf_op jit(solution)/shard_map/pallas_call | solution.py:19
  116.0 5.4 %all-to-all-start = ((bf16[16,64,128]{2,1,0:T(8,128)(2,1)}), bf16[16,64,128]{2,1,0:T(8,128)(2,1)S(1)}, u32[]{:S(2)}, u32[]{:S(2)}) async-start(bf16[16,64,128]{2,1,0:T(8,128)(2,1)} %shard_map.93), calls=%async_computation | async-start | bytes 524288 | tf_op jit(solution)/shard_map/all_to_all | solution.py:321
  121.3 2.0 %collective-permute-start.5 = (bf16[8,64,128]{2,1,0:T(8,128)(2,1)S(1)}, bf16[8,64,128]{2,1,0:T(8,128)(2,1)S(1)}, u32[]{:S(2)}, u32[]{:S(2)}) collective-permute-start(bf16[8,64,128]{2,1,0:T(8,128)(2,1)S(1)} %copy-done.18), channel_id=1, source_target_pairs={{4,0},{8,4},{12,8},{5,1},{9,5},{13,9},{6,2},{10,6},{14,10},{7,3},{... | collective-permute-start | bytes 393224 | tf_op jit(solution)/shard_map/ppermute | solution.py:273
  123.3 3.5 %collective-permute-start.4 = (bf16[8,64,128]{2,1,0:T(8,128)(2,1)S(1)}, bf16[8,64,128]{2,1,0:T(8,128)(2,1)S(1)}, u32[]{:S(2)}, u32[]{:S(2)}) collective-permute-start(bf16[8,64,128]{2,1,0:T(8,128)(2,1)S(1)} %copy-done.18), channel_id=1, source_target_pairs={{0,4},{4,8},{8,12},{1,5},{5,9},{9,13},{2,6},{6,10},{10,14},{3,7},{... | collective-permute-start | bytes 393224 | tf_op jit(solution)/shard_map/ppermute | solution.py:272
  126.9 3.9 %all-to-all-done = bf16[16,64,128]{2,1,0:T(8,128)(2,1)S(1)} async-done(((bf16[16,64,128]{2,1,0:T(8,128)(2,1)}), bf16[16,64,128]{2,1,0:T(8,128)(2,1)S(1)}, u32[]{:S(2)}, u32[]{:S(2)}) %all-to-all-start) | async-done | bytes 262176 | tf_op jit(solution)/shard_map/all_to_all | solution.py:321
  131.6 17.8 %shard_map.89 = bf16[64,128,128]{2,1,0:T(8,128)(2,1)} custom-call(s32[384]{0:T(512)S(1)} %copy-done.14, bf16[128,64,128]{2,1,0:T(8,128)(2,1)} %get-tuple-element.24.xt_ref, bf16[384,16,128]{2,1,0:T(8,128)(2,1)S(1)} %copy-done.16, bf16[128,64,128]{2,1,0:T(8,128)(2,1)} %collective-permute-done.below_ref, ...), custom_call_target="tpu_custom_call" | custom-call | flops 3221225472 | bytes 10485760 | tf_op jit(solution)/shard_map/pallas_call | solution.py:19
  (76 shorter events, 26.4 us)
Async XLA Ops:
  0.6 41.5 %copy-start.20 = (s32[384]{0:T(512)S(1)}, s32[384]{0:T(512)}, u32[]{:S(2)}) copy-start(s32[384]{0:T(512)} %param.11) | copy-start | bytes 4612
  0.6 41.5 %copy-start.21 = (s32[384]{0:T(512)S(1)}, s32[384]{0:T(512)}, u32[]{:S(2)}) copy-start(s32[384]{0:T(512)} %param.10) | copy-start | bytes 4612
  0.7 42.1 %copy-start.11 = (s32[2]{0:T(128)}, s32[2]{0:T(128)S(1)}, u32[]{:S(2)}) copy-start(s32[2]{0:T(128)S(1)} %pad_add_fusion.ids_ref) | copy-start | bytes 28
  5.6 19.3 %collective-permute-start.9 = (bf16[25,64,128]{2,1,0:T(8,128)(2,1)S(1)}, bf16[25,64,128]{2,1,0:T(8,128)(2,1)S(1)}, u32[]{:S(2)}, u32[]{:S(2)}) collective-permute-start(bf16[25,64,128]{2,1,0:T(8,128)(2,1)S(1)} %get-tuple-element.36), channel_id=1, source_target_pairs={{0,1},{1,0},{2,3},{3,2},{4,5},{5,4},{6,7},{7,6},{8,9},{9,8},{10,11... | collective-permute-start | bytes 1228808 | tf_op jit(solution)/shard_map/ppermute | solution.py:228
  7.7 17.2 %collective-permute-start.10 = (bf16[25,64,128]{2,1,0:T(8,128)(2,1)S(1)}, bf16[25,64,128]{2,1,0:T(8,128)(2,1)S(1)}, u32[]{:S(2)}, u32[]{:S(2)}) collective-permute-start(bf16[25,64,128]{2,1,0:T(8,128)(2,1)S(1)} %get-tuple-element.37), channel_id=1, source_target_pairs={{0,2},{1,3},{2,0},{3,1},{4,6},{5,7},{6,4},{7,5},{8,10},{9,11},{10,... | collective-permute-start | bytes 1228808 | tf_op jit(solution)/shard_map/ppermute | solution.py:228
  10.0 26.4 %collective-permute-start.11 = (bf16[25,64,128]{2,1,0:T(8,128)(2,1)S(1)}, bf16[25,64,128]{2,1,0:T(8,128)(2,1)S(1)}, u32[]{:S(2)}, u32[]{:S(2)}) collective-permute-start(bf16[25,64,128]{2,1,0:T(8,128)(2,1)S(1)} %get-tuple-element.38), channel_id=1, source_target_pairs={{0,3},{1,2},{2,1},{3,0},{4,7},{5,6},{6,5},{7,4},{8,11},{9,10},{10,... | collective-permute-start | bytes 1228808 | tf_op jit(solution)/shard_map/ppermute | solution.py:228
  10.0 121.6 %collective-permute-start.1 = (bf16[128,64,128]{2,1,0:T(8,128)(2,1)}, bf16[128,64,128]{2,1,0:T(8,128)(2,1)}, u32[]{:S(2)}, u32[]{:S(2)}) collective-permute-start(bf16[128,64,128]{2,1,0:T(8,128)(2,1)} %get-tuple-element.24.xt_ref), channel_id=1, source_target_pairs={{4,0},{8,4},{12,8},{5,1},{9,5},{13,9},{6,2},{10,6},{14,10},{7,3},{... | collective-permute-start | bytes 6291464 | tf_op jit(solution)/shard_map/ppermute | solution.py:250
  13.1 118.5 %collective-permute-start = (bf16[128,64,128]{2,1,0:T(8,128)(2,1)}, bf16[128,64,128]{2,1,0:T(8,128)(2,1)}, u32[]{:S(2)}, u32[]{:S(2)}) collective-permute-start(bf16[128,64,128]{2,1,0:T(8,128)(2,1)} %get-tuple-element.24.xt_ref), channel_id=1, source_target_pairs={{0,4},{4,8},{8,12},{1,5},{5,9},{9,13},{2,6},{6,10},{10,14},{3,7},{... | collective-permute-start | bytes 6291464 | tf_op jit(solution)/shard_map/ppermute | solution.py:249
  24.9 17.3 %collective-permute-start.6 = (bf16[8,64,128]{2,1,0:T(8,128)(2,1)S(1)}, bf16[8,64,128]{2,1,0:T(8,128)(2,1)S(1)}, u32[]{:S(2)}, u32[]{:S(2)}) collective-permute-start(bf16[8,64,128]{2,1,0:T(8,128)(2,1)S(1)} %get-tuple-element.30), channel_id=1, source_target_pairs={{0,1},{1,0},{2,3},{3,2},{4,5},{5,4},{6,7},{7,6},{8,9},{9,8},{10,11... | collective-permute-start | bytes 393224 | tf_op jit(solution)/shard_map/ppermute | solution.py:228
  24.9 38.9 %collective-permute-start.7 = (bf16[8,64,128]{2,1,0:T(8,128)(2,1)}, bf16[8,64,128]{2,1,0:T(8,128)(2,1)S(1)}, u32[]{:S(2)}, u32[]{:S(2)}) collective-permute-start(bf16[8,64,128]{2,1,0:T(8,128)(2,1)} %get-tuple-element.31), channel_id=1, source_target_pairs={{0,2},{1,3},{2,0},{3,1},{4,6},{5,7},{6,4},{7,5},{8,10},{9,11},{10,... | collective-permute-start | bytes 393224 | tf_op jit(solution)/shard_map/ppermute | solution.py:228
  37.1 69.0 %collective-permute-start.15 = (bf16[12,256,128]{2,1,0:T(8,128)(2,1)S(1)}, bf16[12,256,128]{2,1,0:T(8,128)(2,1)S(1)}, u32[]{:S(2)}, u32[]{:S(2)}) collective-permute-start(bf16[12,256,128]{2,1,0:T(8,128)(2,1)S(1)} %get-tuple-element.40.high), channel_id=1, source_target_pairs={{4,0},{8,4},{12,8},{5,1},{9,5},{13,9},{6,2},{10,6},{14,10},{7,3},{... | collective-permute-start | bytes 2359304 | tf_op jit(solution)/shard_map/ppermute | solution.py:297
  42.8 67.5 %copy-start = (f32[1,128,128]{2,1,0:T(8,128)S(1)}, f32[1,128,128]{2,1,0:T(8,128)}, u32[]{:S(2)}) copy-start(f32[1,128,128]{2,1,0:T(8,128)} %param.8) | copy-start | bytes 196612
  42.8 65.2 %collective-permute-start.14 = (bf16[12,256,128]{2,1,0:T(8,128)(2,1)S(1)}, bf16[12,256,128]{2,1,0:T(8,128)(2,1)S(1)}, u32[]{:S(2)}, u32[]{:S(2)}) collective-permute-start(bf16[12,256,128]{2,1,0:T(8,128)(2,1)S(1)} %get-tuple-element.39.low.after), channel_id=1, source_target_pairs={{0,4},{4,8},{8,12},{1,5},{5,9},{9,13},{2,6},{6,10},{10,14},{3,7},{... | collective-permute-start | bytes 2359304 | tf_op jit(solution)/shard_map/ppermute | solution.py:297
  64.4 4.4 %collective-permute-start.2 = (bf16[8,64,128]{2,1,0:T(8,128)(2,1)S(1)}, bf16[8,64,128]{2,1,0:T(8,128)(2,1)S(1)}, u32[]{:S(2)}, u32[]{:S(2)}) collective-permute-start(bf16[8,64,128]{2,1,0:T(8,128)(2,1)S(1)} %get-tuple-element.26), channel_id=1, source_target_pairs={{0,4},{4,8},{8,12},{1,5},{5,9},{9,13},{2,6},{6,10},{10,14},{3,7},{... | collective-permute-start | bytes 393224 | tf_op jit(solution)/shard_map/ppermute | solution.py:261
  69.5 7.0 %collective-permute-start.3 = (bf16[8,64,128]{2,1,0:T(8,128)(2,1)S(1)}, bf16[8,64,128]{2,1,0:T(8,128)(2,1)S(1)}, u32[]{:S(2)}, u32[]{:S(2)}) collective-permute-start(bf16[8,64,128]{2,1,0:T(8,128)(2,1)S(1)} %get-tuple-element.27), channel_id=1, source_target_pairs={{4,0},{8,4},{12,8},{5,1},{9,5},{13,9},{6,2},{10,6},{14,10},{7,3},{... | collective-permute-start | bytes 393224 | tf_op jit(solution)/shard_map/ppermute | solution.py:262
  77.1 9.3 %collective-permute-start.8 = (bf16[8,64,128]{2,1,0:T(8,128)(2,1)}, bf16[8,64,128]{2,1,0:T(8,128)(2,1)}, u32[]{:S(2)}, u32[]{:S(2)}) collective-permute-start(bf16[8,64,128]{2,1,0:T(8,128)(2,1)} %get-tuple-element.32), channel_id=1, source_target_pairs={{0,3},{1,2},{2,1},{3,0},{4,7},{5,6},{6,5},{7,4},{8,11},{9,10},{10,... | collective-permute-start | bytes 393224 | tf_op jit(solution)/shard_map/ppermute | solution.py:228
  86.4 11.6 %collective-permute-start.16 = (bf16[2,64,128]{2,1,0:T(8,128)(2,1)S(1)}, bf16[2,64,128]{2,1,0:T(8,128)(2,1)S(1)}, u32[]{:S(2)}, u32[]{:S(2)}) collective-permute-start(bf16[2,64,128]{2,1,0:T(8,128)(2,1)S(1)} %get-tuple-element.43), channel_id=1, source_target_pairs={{0,1},{1,0},{2,3},{3,2},{4,5},{5,4},{6,7},{7,6},{8,9},{9,8},{10,11... | collective-permute-start | bytes 98312 | tf_op jit(solution)/shard_map/ppermute | solution.py:228
  98.0 5.0 %collective-permute-start.17 = (bf16[2,64,128]{2,1,0:T(8,128)(2,1)S(1)}, bf16[2,64,128]{2,1,0:T(8,128)(2,1)S(1)}, u32[]{:S(2)}, u32[]{:S(2)}) collective-permute-start(bf16[2,64,128]{2,1,0:T(8,128)(2,1)S(1)} %get-tuple-element.44), channel_id=1, source_target_pairs={{0,2},{1,3},{2,0},{3,1},{4,6},{5,7},{6,4},{7,5},{8,10},{9,11},{10,... | collective-permute-start | bytes 98312 | tf_op jit(solution)/shard_map/ppermute | solution.py:228
  103.0 9.7 %collective-permute-start.12 = (bf16[4,256,128]{2,1,0:T(8,128)(2,1)S(1)}, bf16[4,256,128]{2,1,0:T(8,128)(2,1)S(1)}, u32[]{:S(2)}, u32[]{:S(2)}) collective-permute-start(bf16[4,256,128]{2,1,0:T(8,128)(2,1)S(1)} %get-tuple-element.33.low), channel_id=1, source_target_pairs={{0,4},{4,8},{8,12},{1,5},{5,9},{9,13},{2,6},{6,10},{10,14},{3,7},{... | collective-permute-start | bytes 786440 | tf_op jit(solution)/shard_map/ppermute | solution.py:297
  106.1 7.7 %collective-permute-start.13 = (bf16[4,256,128]{2,1,0:T(8,128)(2,1)S(1)}, bf16[4,256,128]{2,1,0:T(8,128)(2,1)S(1)}, u32[]{:S(2)}, u32[]{:S(2)}) collective-permute-start(bf16[4,256,128]{2,1,0:T(8,128)(2,1)S(1)} %get-tuple-element.34.high), channel_id=1, source_target_pairs={{4,0},{8,4},{12,8},{5,1},{9,5},{13,9},{6,2},{10,6},{14,10},{7,3},{... | collective-permute-start | bytes 786440 | tf_op jit(solution)/shard_map/ppermute | solution.py:297
  108.1 4.6 %collective-permute-start.18 = (bf16[2,64,128]{2,1,0:T(8,128)(2,1)S(1)}, bf16[2,64,128]{2,1,0:T(8,128)(2,1)S(1)}, u32[]{:S(2)}, u32[]{:S(2)}) collective-permute-start(bf16[2,64,128]{2,1,0:T(8,128)(2,1)S(1)} %get-tuple-element.45), channel_id=1, source_target_pairs={{0,3},{1,2},{2,1},{3,0},{4,7},{5,6},{6,5},{7,4},{8,11},{9,10},{10,... | collective-permute-start | bytes 98312 | tf_op jit(solution)/shard_map/ppermute | solution.py:228
  116.0 14.9 %all-to-all-start = ((bf16[16,64,128]{2,1,0:T(8,128)(2,1)}), bf16[16,64,128]{2,1,0:T(8,128)(2,1)S(1)}, u32[]{:S(2)}, u32[]{:S(2)}) async-start(bf16[16,64,128]{2,1,0:T(8,128)(2,1)} %shard_map.93), calls=%async_computation | async-start | bytes 524288 | tf_op jit(solution)/shard_map/all_to_all | solution.py:321
  121.3 10.3 %collective-permute-start.5 = (bf16[8,64,128]{2,1,0:T(8,128)(2,1)S(1)}, bf16[8,64,128]{2,1,0:T(8,128)(2,1)S(1)}, u32[]{:S(2)}, u32[]{:S(2)}) collective-permute-start(bf16[8,64,128]{2,1,0:T(8,128)(2,1)S(1)} %copy-done.18), channel_id=1, source_target_pairs={{4,0},{8,4},{12,8},{5,1},{9,5},{13,9},{6,2},{10,6},{14,10},{7,3},{... | collective-permute-start | bytes 393224 | tf_op jit(solution)/shard_map/ppermute | solution.py:273
  123.3 8.2 %collective-permute-start.4 = (bf16[8,64,128]{2,1,0:T(8,128)(2,1)S(1)}, bf16[8,64,128]{2,1,0:T(8,128)(2,1)S(1)}, u32[]{:S(2)}, u32[]{:S(2)}) collective-permute-start(bf16[8,64,128]{2,1,0:T(8,128)(2,1)S(1)} %copy-done.18), channel_id=1, source_target_pairs={{0,4},{4,8},{8,12},{1,5},{5,9},{9,13},{2,6},{6,10},{10,14},{3,7},{... | collective-permute-start | bytes 393224 | tf_op jit(solution)/shard_map/ppermute | solution.py:272
  (18 other events, 92.8 us)

commit v2 on v0

v2 whole, which is shorter than its diff:
```python
import functools

import jax
import jax.numpy as jnp
from jax import lax
from jax.experimental import pallas as pl
from jax.experimental.pallas import tpu as pltpu
from jax.sharding import PartitionSpec as P

F32 = jnp.float32
BF16 = jnp.bfloat16
LANES = 128
ROWS = 16
VMEM_BYTES = 48 * 1024 * 1024
NT = (((1,), (1,)), ((), ()))
WHOLE = pl.BlockSpec(memory_space=pltpu.VMEM)
SCALARS = pl.BlockSpec(memory_space=pltpu.SMEM)
UNREAD = pl.BlockSpec(memory_space=pl.ANY)


def call(kernel, grid, in_specs, out_specs, outs, scratch, args, micros):
    return pl.pallas_call(
        kernel,
        grid=grid,
        out_shape=[jax.ShapeDtypeStruct(shape, kind) for shape, kind in outs],
        in_specs=in_specs,
        out_specs=out_specs,
        scratch_shapes=scratch,
        compiler_params=pltpu.CompilerParams(vmem_limit_bytes=VMEM_BYTES),
        cost_estimate=pl.CostEstimate(flops=int(micros * 1.1e9), bytes_accessed=1 << 20, transcendentals=0),
    )(*args)


def line_at(index, states):
    return pl.ds(pl.multiple_of(index * states, states), states)


def pack_kernel(share, x_hbm, pot_ref, xt_hbm, msg_hbm, x, xt, pots, in_sems, out_sems, msg_sems):
    states, lines, _ = x.shape
    parts = lines // share
    chunks = in_sems.shape[0]
    size = lines // chunks
    loads = []
    for c in range(chunks):
        where = (slice(None), pl.ds(c * size, size), slice(None))
        loads.append(pltpu.make_async_copy(x_hbm.at[where], x.at[where], in_sems.at[c]))
        loads[-1].start()

    here = pot_ref[...]
    high = here.astype(BF16)
    rest = (here - high.astype(F32)).astype(BF16)
    pots[...] = jnp.zeros_like(pots)
    for j in range(parts):
        both = jnp.concatenate([high[j * share : (j + 1) * share], rest[j * share : (j + 1) * share]], axis=0)
        pots[j, : 2 * share, :] = both
    span = (share + 1) * states
    tail = pltpu.make_async_copy(pots, msg_hbm.at[:, pl.ds(span, pots.shape[1]), :], msg_sems.at[parts + 1])
    tail.start()

    sends = []

    def send(j):
        last = j == parts - 1
        count = share * states if last else span
        sends.append(
            pltpu.make_async_copy(
                xt.at[pl.ds(j * share * states, count)], msg_hbm.at[j, pl.ds(0, count), :], msg_sems.at[j]
            )
        )
        sends[-1].start()
        if last:
            sends.append(
                pltpu.make_async_copy(
                    xt.at[pl.ds(0, states)], msg_hbm.at[j, pl.ds(count, states), :], msg_sems.at[parts]
                )
            )
            sends[-1].start()

    sent = 0
    for c in range(chunks):
        loads[c].wait()
        for y0 in range(c * size, (c + 1) * size, ROWS):
            for s0 in range(0, states, ROWS):
                block = x[s0 : s0 + ROWS, y0 : y0 + ROWS, :].astype(F32)
                turned = jnp.swapaxes(block, 0, 1).astype(BF16)
                for i in range(ROWS):
                    xt[(y0 + i) * states + s0 : (y0 + i) * states + s0 + ROWS, :] = turned[i]
        while sent < parts - 1 and (sent + 1) * share + 1 <= (c + 1) * size:
            send(sent)
            sent += 1
        where = pl.ds(c * size * states, size * states)
        sends.append(pltpu.make_async_copy(xt.at[where], xt_hbm.at[where], out_sems.at[c]))
        sends[-1].start()
    while sent < parts:
        send(sent)
        sent += 1
    for copy in sends:
        copy.wait()
    tail.wait()


def project_kernel(words_ref, ids_ref, xt_ref, p_ref, core_ref, own_ref, link_ref, total):
    slots, proj_count, _ = p_ref.shape
    groups, states, _ = own_ref.shape
    per_group = LANES // proj_count
    unroll = 16

    def clear(i, carry):
        for u in range(per_group):
            total[i * per_group + u] = jnp.zeros_like(total[0])
        return carry

    lax.fori_loop(0, 3 * groups, clear, 0)

    def body(i, carry):
        for u in range(unroll):
            t = i * unroll + u
            word = words_ref[t]
            line, atom = word >> 16, word & 0xFFFF
            total[atom] += lax.dot_general(
                p_ref[t], xt_ref[line_at(line, states), :], NT, preferred_element_type=F32
            )
        return carry

    lax.fori_loop(0, slots // unroll, body, 0)
    odd = ids_ref[0] & 1
    core_first, link_first = (1 - odd) * 2 * groups, odd * 2 * groups

    def turned(group):
        tiles = [total[group * per_group + u] for u in range(per_group)]
        return jnp.concatenate(tiles, axis=0).T

    for g in range(groups):
        core_ref[g] = turned(core_first + g).astype(BF16)
        link_ref[g] = turned(link_first + g).astype(BF16)
        own_ref[g] = turned(groups + g)


def owner_kernel(ids_ref, own_ref, core_ref, link_ref, energy_ref, scaled_ref, whole_ref):
    groups = own_ref.shape[0]
    first = ids_ref[0] * groups
    for g in range(groups):
        whole = own_ref[g] + core_ref[g].astype(F32) + link_ref[g].astype(F32)
        scaled_ref[g] = (whole * energy_ref[pl.ds(first + g, 1), :]).astype(BF16)
        whole_ref[g] = whole.astype(BF16)


def nonlocal_kernel(words_ref, ids_ref, p_ref, core_ref, own_ref, link_ref, out_ref, atoms):
    slots, proj_count, _ = p_ref.shape
    groups, states, _ = own_ref.shape
    per_group = LANES // proj_count
    lines = out_ref.shape[0] // states
    unroll = 16

    def clear(i, carry):
        out_ref[line_at(i, states), :] = jnp.zeros((states, LANES), F32)
        return carry

    lax.fori_loop(0, lines, clear, 0)
    odd = ids_ref[0] & 1
    for first, ref in (((1 - odd) * 2 * groups, core_ref), (groups, own_ref), (odd * 2 * groups, link_ref)):
        for g in range(groups):
            tile = ref[g]
            for u in range(per_group):
                atoms[(first + g) * per_group + u] = tile[:, u * proj_count : (u + 1) * proj_count]

    def body(i, carry):
        for u in range(unroll):
            t = i * unroll + u
            word = words_ref[t]
            line, atom = word >> 16, word & 0xFFFF
            out_ref[line_at(line, states), :] += jnp.dot(atoms[atom], p_ref[t], preferred_element_type=F32)
        return carry

    lax.fori_loop(0, slots // unroll, body, 0)


def stencil_kernel(xt_ref, before_ref, after_ref, core_ref, link_ref, nonlocal_ref, pot_ref, unread, out_ref):
    states, lines, _ = out_ref.shape

    def line(i):
        if i < 0:
            return before_ref[...].astype(F32)
        if i == lines:
            return after_ref[...].astype(F32)
        return xt_ref[i * states : (i + 1) * states, :].astype(F32)

    results = []
    for i in range(lines):
        rows = slice(i * states, (i + 1) * states)
        x = line(i)
        beside = line(i - 1) + line(i + 1)
        beside += core_ref[rows, :].astype(F32) + link_ref[rows, :].astype(F32)
        beside += pltpu.roll(x, 1, 1) + pltpu.roll(x, x.shape[1] - 1, 1)
        results.append((3.0 + pot_ref[i : i + 1, :]) * x - 0.5 * beside + nonlocal_ref[rows, :])
    out_ref[...] = jnp.swapaxes(jnp.stack(results, axis=0), 0, 1).astype(BF16)


def gram_kernel(
    bands, domains, states, share, ids_ref, here_ref, next_ref, proj_ref, energy_ref, unread, out_ref, acc
):
    plane = pl.program_id(0)

    @pl.when(plane == 0)
    def _():
        acc[...] = jnp.zeros_like(acc)

    keep = jnp.where(plane < domains - 1, 1.0, 0.0).astype(F32)

    def line(ref, i):
        return jnp.concatenate([ref[b, i * states : (i + 1) * states, :] for b in range(bands)], axis=0)

    span = (share + 1) * states
    pots = here_ref[0, span : span + 2 * share + (-2 * share) % ROWS, :].astype(F32)
    group = 4
    for i0 in range(0, share, group):
        xs, ys = [], []
        for i in range(i0, min(i0 + group, share)):
            cell = line(here_ref, i)
            x = cell.astype(F32)
            pot = pots[i : i + 1] + pots[share + i : share + i + 1]
            y = (3.0 + pot) * x - pltpu.roll(x, x.shape[1] - 1, 1)
            y = y - line(here_ref, i + 1).astype(F32) - keep * line(next_ref, i).astype(F32)
            xs.append(cell)
            ys.append(y.astype(BF16))
        flat_x = jnp.concatenate(xs, axis=1)
        flat_y = jnp.concatenate(ys, axis=1)
        acc[0] += lax.dot_general(flat_x, flat_x, NT, preferred_element_type=F32)
        acc[1] += lax.dot_general(flat_y, flat_x, NT, preferred_element_type=F32)

    @pl.when(plane == domains - 1)
    def _():
        groups = proj_ref.shape[0] // bands
        first = (ids_ref[0] * bands + ids_ref[1]) * groups
        for g in range(groups):
            here = jnp.concatenate([proj_ref[b * groups + g] for b in range(bands)], axis=0)
            scaled = (here.astype(F32) * energy_ref[pl.ds(first + g, 1), :]).astype(BF16)
            acc[1] += lax.dot_general(scaled, here, NT, preferred_element_type=F32)
        gram = acc[0]
        hamil = 0.5 * (acc[1] + acc[1].T)
        cols = gram.shape[0] // domains
        for c in range(domains):
            for r in range(bands):
                r0, c0 = r * states, c * cols
                out_ref[c * bands + r, :, :cols] = gram[r0 : r0 + states, c0 : c0 + cols].astype(BF16)
                out_ref[c * bands + r, :, cols:] = hamil[r0 : r0 + states, c0 : c0 + cols].astype(BF16)


def local(orbitals, potential, projectors, tile_atom, tile_line, tile_count, energies):
    states, _, lines, cols_z = orbitals.shape
    slots, proj_count, _ = projectors.shape
    atom_total = energies.shape[0]
    domains, bands = lax.axis_size("domain"), lax.axis_size("band")
    domain, band = lax.axis_index("domain"), lax.axis_index("band")
    total_states = states * bands
    atoms_here = atom_total // domains
    per_group = LANES // proj_count
    groups = atoms_here // per_group
    parts = domains * bands
    share = lines // parts
    pot_rows = 2 * share + (-2 * share) % ROWS
    message = (share + 1) * states + pot_rows

    core_pairs = [(i, i ^ 1) for i in range(domains) if i ^ 1 < domains]
    link_pairs = [(i, (i + 1 ^ 1) - 1) for i in range(1, domains) if (i + 1 ^ 1) - 1 < domains]

    ids = jnp.stack([domain, band]).astype(jnp.int32)
    near = jnp.clip(tile_atom - (domain - 1) * atoms_here, 0, 3 * atoms_here - 1)
    live = jnp.arange(slots, dtype=jnp.int32) < tile_count[0]
    project_words = (tile_line << 16) | jnp.where(live, near, 3 * atoms_here)
    nonlocal_words = (jnp.where(live, tile_line, lines) << 16) | near
    field = orbitals.reshape(states, lines, cols_z)
    pot = potential.reshape(lines, cols_z)
    energy = energies.reshape(atom_total // per_group, LANES)

    chunks = 4
    xt, msg = call(
        functools.partial(pack_kernel, share),
        (),
        [UNREAD, WHOLE],
        [UNREAD, UNREAD],
        [((lines * states, cols_z), BF16), ((parts, message, cols_z), BF16)],
        [
            pltpu.VMEM((states, lines, cols_z), BF16),
            pltpu.VMEM((lines * states, cols_z), BF16),
            pltpu.VMEM((parts, pot_rows, cols_z), BF16),
            pltpu.SemaphoreType.DMA((chunks,)),
            pltpu.SemaphoreType.DMA((chunks,)),
            pltpu.SemaphoreType.DMA((parts + 2,)),
        ],
        (field, pot),
        4,
    )
    landed = lax.all_to_all(msg, ("domain", "band"), split_axis=0, concat_axis=0, tiled=True)
    link_field = lax.ppermute(xt, "domain", link_pairs)
    core_field = lax.ppermute(xt, "domain", core_pairs)

    group_shape = (groups, states, LANES)
    to_core, own, to_link = call(
        project_kernel,
        (),
        [SCALARS, SCALARS, WHOLE, WHOLE],
        [WHOLE] * 3,
        [(group_shape, BF16), (group_shape, F32), (group_shape, BF16)],
        [pltpu.VMEM((3 * atoms_here + 1, proj_count, states), F32)],
        (project_words, ids, xt, projectors),
        9,
    )
    from_link = lax.ppermute(to_link, "domain", link_pairs)
    from_core = lax.ppermute(to_core, "domain", core_pairs)
    scaled, whole = call(
        owner_kernel,
        (),
        [SCALARS] + [WHOLE] * 4,
        [WHOLE] * 2,
        [(group_shape, BF16), (group_shape, BF16)],
        [],
        (ids, own, from_core, from_link, energy),
        1,
    )
    link_scaled = lax.ppermute(scaled, "domain", link_pairs)
    core_scaled = lax.ppermute(scaled, "domain", core_pairs)
    shares = lax.all_to_all(whole, "band", split_axis=0, concat_axis=0, tiled=True)

    (added,) = call(
        nonlocal_kernel,
        (),
        [SCALARS, SCALARS] + [WHOLE] * 4,
        [WHOLE],
        [(((lines + 1) * states, cols_z), F32)],
        [pltpu.VMEM((3 * atoms_here, states, proj_count), BF16)],
        (nonlocal_words, ids, projectors, core_scaled, scaled, link_scaled),
        9,
    )

    (blocks,) = call(
        functools.partial(gram_kernel, bands, domains, states, share),
        (domains,),
        [
            SCALARS,
            pl.BlockSpec((bands, message, cols_z), lambda d: (d, 0, 0)),
            pl.BlockSpec((bands, message, cols_z), lambda d: (jnp.minimum(d + 1, domains - 1), 0, 0)),
            WHOLE,
            WHOLE,
            UNREAD,
        ],
        [WHOLE],
        [((parts, states, 2 * total_states // domains), BF16)],
        [pltpu.VMEM((2, total_states, total_states), F32)],
        (ids, landed, landed, shares, energy, added),
        4,
    )
    summed = lax.all_to_all(blocks, ("domain", "band"), split_axis=0, concat_axis=0, tiled=True)

    steps = lines // ROWS
    rows = ROWS * states
    block = pl.BlockSpec((rows, cols_z), lambda i: (i, 0))
    (applied,) = call(
        stencil_kernel,
        (steps,),
        [
            block,
            pl.BlockSpec((states, cols_z), lambda i: (lax.rem(i * ROWS + lines - 1, lines), 0)),
            pl.BlockSpec((states, cols_z), lambda i: (lax.rem(i * ROWS + ROWS, lines), 0)),
            block,
            block,
            block,
            pl.BlockSpec((ROWS, cols_z), lambda i: (i, 0)),
            UNREAD,
        ],
        [pl.BlockSpec((states, ROWS, cols_z), lambda i: (0, i, 0))],
        [((states, lines, cols_z), BF16)],
        [],
        (xt, xt, xt, core_field, link_field, added, pot, blocks),
        7,
    )
    scale = 1.0 / (lines * cols_z * domains)
    result = jnp.sum(summed.astype(F32), axis=0) * scale
    cols = total_states // domains
    subspace = jnp.stack([result[:, :cols], result[:, cols:]])
    return applied.reshape(orbitals.shape), subspace


def solution(mesh):
    in_specs = (
        P("band", ("groups", "domain"), None, None),
        P(("groups", "domain"), None, None),
        P(("groups", "domain"), None, None),
        P(("groups", "domain")),
        P(("groups", "domain")),
        P(("groups", "domain")),
        P("groups", None),
    )
    out_specs = (P("band", ("groups", "domain"), None, None), P(None, ("groups", "band"), "domain"))
    return jax.shard_map(local, mesh=mesh, in_specs=in_specs, out_specs=out_specs, check_vma=False)
```

time: 287 us -> 123 us (0.43)
  other arithmetic: 131 us -> 0.77 us
  local copies, waits for them, and re-layouts: 50.9 us -> 9.79 us
  Pallas kernels: 0 us -> 30.7 us
  matrix products: 26.5 us -> 0 us
  starting transfers between devices: 6.75 us -> 22.4 us
  between operations: 16.3 us -> 1.48 us
  blocking collectives: 0 us -> 9.82 us
  waiting for transfers between devices: 53 us -> 47.1 us
    scatter-add x2 -> x0, other arithmetic: 107 us -> none  [the longest x1 60.1 us: local(): jnp.zeros((states_here, planes * rows_y, cols_z), jnp.float32)]
    ppermute x2 -> x6, waiting for transfers between devices: 0.01 us -> 47.1 us  [the longest x1 44.7 us: local(): link_scaled = lax.ppermute(scaled, 'domain', link_pairs)]
    psum x1 -> x0, waiting for transfers between devices: 36.2 us -> none  [local(): total = lax.psum(proj, 'domain')]
    pallas_call x0 -> x6, Pallas kernels: none -> 30.7 us  [call(): pl.pallas_call(kernel, grid=grid, out_shape=[jax.ShapeDtypeStruct(shape,...]
    dot_general x4 -> x0, matrix products: 26.5 us -> none  [the longest x2 9.34 us: pair_products(): lax.dot_general(left, right, (((1,), (1,)), ((), ())), preferred_element_...]
    slice x4 -> x0, local copies, waits for them, and re-layouts: 19.7 us -> none  [the longest x2 10.4 us: local(): jnp.roll(field, -1, axis=2)]
    unnamed x4 -> x0, waiting for transfers between devices: 16.8 us -> none
    convert_element_type x3 -> x0, other arithmetic: 16.7 us -> none  [the longest x1 14.8 us: local(): applied = result.astype(jnp.bfloat16)]
  transfers between devices with their start and end apart: 5 -> 8, of which waited for: 2 -> 2; matrix products, arithmetic and copies ran while one was open for 42% -> 0% of each run, Pallas kernels for 0% -> 17%
where the time goes in v2:
time: 123 us; the launch traced here: 122 us
  waiting for transfers between devices  47.1 us (38%)
  Pallas kernels  30.7 us (25%)
  starting transfers between devices  22.4 us (18%)
  blocking collectives  9.82 us (8%)
  local copies, waits for them, and re-layouts  9.79 us (8%)
  between operations  1.48 us (1%)
    ppermute x1, waiting for transfers between devices, local(): link_scaled = lax.ppermute(scaled, 'domain', link_pairs)  44.7 us
    pallas_call x6, Pallas kernels, call(): pl.pallas_call(kernel, grid=grid, out_shape=[jax.ShapeDtypeStruct(shape,...  30.7 us
    all_to_all x1, blocking collectives, local(): lax.all_to_all(whole, 'band', split_axis=0, concat_axis=0, tiled=True)  9.82 us
    unnamed x23, local copies, waits for them, and re-layouts  9.62 us
    all_to_all x1, starting transfers between devices, local(): lax.all_to_all(blocks, ('domain', 'band'), split_axis=0, concat_axis=0, t...  6.77 us
    all_to_all x1, starting transfers between devices, local(): lax.all_to_all(msg, ('domain', 'band'), split_axis=0, concat_axis=0, tile...  5.03 us
    ppermute x1, starting transfers between devices, local(): from_link = lax.ppermute(to_link, 'domain', link_pairs)  4.42 us
    ppermute x1, starting transfers between devices, local(): link_field = lax.ppermute(xt, 'domain', link_pairs)  3.52 us
  transfers between devices with their start and end apart: 8, of which 2 were waited for; matrix products, arithmetic and copies ran while one was open for 0% of the time, Pallas kernels for 17%

profile of v2, /device:TPU:1, one launch (start us, length us, event | category | flops | bytes accessed | tf_op | source)
XLA Modules:
  0.0 122.1 jit_solution(9019202490360119476)
XLA Ops:
  1.4 1.6 %copy-done = bf16[64,1,128,128]{3,2,1,0:T(8,128)(2,1)S(1)} copy-done((bf16[64,1,128,128]{3,2,1,0:T(8,128)(2,1)S(1)}, bf16[64,1,128,128]{3,2,1,0:T(8,128)(2,1)}, u32[]{:S(2)}) %copy-start) | copy-done | bytes 2097176
  3.0 0.8 copy-done.5
  3.8 2.7 %shard_map.86 = (bf16[8192,128]{1,0:T(8,128)(2,1)S(1)}, bf16[16,592,128]{2,1,0:T(8,128)(2,1)}) custom-call(bf16[64,128,128]{2,1,0:T(8,128)(2,1)S(1)} %bitcast.13, f32[128,128]{1,0:T(8,128)S(1)} %bitcast.14), custom_call_target="tpu_custom_call" | custom-call | flops 4400000000 | bytes 1048576 | tf_op jit(solution)/shard_map/pallas_call | solution.py:22
  6.5 2.1 %copy-done.3 = bf16[384,16,128]{2,1,0:T(8,128)(2,1)S(1)} copy-done((bf16[384,16,128]{2,1,0:T(8,128)(2,1)S(1)}, bf16[384,16,128]{2,1,0:T(8,128)(2,1)}, u32[]{:S(2)}) %copy-start.3) | copy-done | bytes 1572888
  8.6 7.2 %shard_map.87 = (bf16[8,64,128]{2,1,0:T(8,128)(2,1)S(1)}, f32[8,64,128]{2,1,0:T(8,128)S(1)}, bf16[8,64,128]{2,1,0:T(8,128)(2,1)S(1)}) custom-call(s32[384]{0:T(512)S(1)} %get-tuple-element.22.words_ref, s32[2]{0:T(128)S(1)} %pad_add_fusion.ids_ref, bf16[8192,128]{1,0:T(8,128)(2,1)S(1)} %get-tuple-element.9.xt_ref.before_ref.after_ref, ...), custom_call_target="tpu_custom_call" | custom-call | flops 9900000256 | bytes 1048576 | tf_op jit(solution)/shard_map/pallas_call | solution.py:22
  15.9 0.2 collective-permute-start.2
  16.1 4.4 %collective-permute-start.3 = (bf16[8,64,128]{2,1,0:T(8,128)(2,1)S(1)}, bf16[8,64,128]{2,1,0:T(8,128)(2,1)S(1)}, u32[]{:S(2)}, u32[]{:S(2)}) collective-permute-start(bf16[8,64,128]{2,1,0:T(8,128)(2,1)S(1)} %get-tuple-element.12), channel_id=1, source_target_pairs={{4,8},{8,4},{5,9},{9,5},{6,10},{10,6},{7,11},{11,7},{20,24},{24,20... | collective-permute-start | bytes 393224 | tf_op jit(solution)/shard_map/ppermute | solution.py:309
  20.5 0.1 copy.11
  20.7 2.4 %collective-permute-done.3.link_ref = bf16[8,64,128]{2,1,0:T(8,128)(2,1)S(1)} collective-permute-done((bf16[8,64,128]{2,1,0:T(8,128)(2,1)S(1)}, bf16[8,64,128]{2,1,0:T(8,128)(2,1)S(1)}, u32[]{:S(2)}, u32[]{:S(2)}) %collective-permute-start.3) | collective-permute-done | bytes 131104 | tf_op jit(solution)/shard_map/ppermute | solution.py:309
  23.1 0.6 shard_map.88
  23.7 9.8 %all_to_all.15.proj_ref = bf16[8,64,128]{2,1,0:T(8,128)(2,1)S(1)} all-to-all(bf16[8,64,128]{2,1,0:T(8,128)(2,1)S(1)} %get-tuple-element.15), channel_id=1, replica_groups=mesh['groups'=2,'domain'=4,'band'=4] {'band'}, dimensions={0} | all-to-all | bytes 262144 | tf_op jit(solution)/shard_map/all_to_all | solution.py:323
  33.6 5.0 %all-to-all-start = ((bf16[16,592,128]{2,1,0:T(8,128)(2,1)}), bf16[16,592,128]{2,1,0:T(8,128)(2,1)S(1)}, u32[]{:S(2)}, u32[]{:S(2)}) async-start(bf16[16,592,128]{2,1,0:T(8,128)(2,1)} %get-tuple-element.14), calls=%async_computation | async-start | bytes 4849664 | tf_op jit(solution)/shard_map/all_to_all | solution.py:294
  38.6 0.2 collective-permute-start
  38.8 3.5 %collective-permute-start.1 = (bf16[8192,128]{1,0:T(8,128)(2,1)}, bf16[8192,128]{1,0:T(8,128)(2,1)}, u32[]{:S(2)}, u32[]{:S(2)}) collective-permute-start(bf16[8192,128]{1,0:T(8,128)(2,1)} %copy-done.1), channel_id=1, source_target_pairs={{4,8},{8,4},{5,9},{9,5},{6,10},{10,6},{7,11},{11,7},{20,24},{24,20... | collective-permute-start | bytes 6291464 | tf_op jit(solution)/shard_map/ppermute | solution.py:295
  42.4 2.3 %collective-permute-start.5 = (bf16[8,64,128]{2,1,0:T(8,128)(2,1)S(1)}, bf16[8,64,128]{2,1,0:T(8,128)(2,1)S(1)}, u32[]{:S(2)}, u32[]{:S(2)}) collective-permute-start(bf16[8,64,128]{2,1,0:T(8,128)(2,1)S(1)} %get-tuple-element.13.own_ref), channel_id=1, source_target_pairs={{4,8},{8,4},{5,9},{9,5},{6,10},{10,6},{7,11},{11,7},{20,24},{24,20... | collective-permute-start | bytes 393224 | tf_op jit(solution)/shard_map/ppermute | solution.py:321
  44.6 44.7 %collective-permute-done.5.link_ref = bf16[8,64,128]{2,1,0:T(8,128)(2,1)S(1)} collective-permute-done((bf16[8,64,128]{2,1,0:T(8,128)(2,1)S(1)}, bf16[8,64,128]{2,1,0:T(8,128)(2,1)S(1)}, u32[]{:S(2)}, u32[]{:S(2)}) %collective-permute-start.5) | collective-permute-done | bytes 131104 | tf_op jit(solution)/shard_map/ppermute | solution.py:321
  89.4 1.4 %copy-done.4 = bf16[384,16,128]{2,1,0:T(8,128)(2,1)S(1)} copy-done((bf16[384,16,128]{2,1,0:T(8,128)(2,1)S(1)}, bf16[384,16,128]{2,1,0:T(8,128)(2,1)}, u32[]{:S(2)}) %copy-start.4) | copy-done | bytes 1572888
  90.8 8.3 %shard_map.89.unread.nonlocal_ref = f32[8256,128]{1,0:T(8,128)S(1)} custom-call(s32[384]{0:T(512)S(1)} %get-tuple-element.23.words_ref, s32[2]{0:T(128)S(1)} %pad_add_fusion.ids_ref, bf16[384,16,128]{2,1,0:T(8,128)(2,1)S(1)} %copy-done.4, bf16[8,64,128]{2,1,0:T(8,128)(2,1)S(1)} %collective-permute-done.4.core_ref, ...), custom_call_target="tpu_custom_call" | custom-call | flops 9900000256 | bytes 1048576 | tf_op jit(solution)/shard_map/pallas_call | solution.py:22
  99.1 1.9 %copy-done.7 = f32[8256,128]{1,0:T(8,128)} copy-done((f32[8256,128]{1,0:T(8,128)}, f32[8256,128]{1,0:T(8,128)S(1)}, u32[]{:S(2)}) %copy-start.7) | copy-done | bytes 4227096
  101.1 3.8 %shard_map.90.unread = bf16[16,64,128]{2,1,0:T(8,128)(2,1)} custom-call(s32[2]{0:T(128)S(1)} %pad_add_fusion.ids_ref, bf16[16,592,128]{2,1,0:T(8,128)(2,1)S(1)} %all-to-all-done.here_ref.next_ref, bf16[16,592,128]{2,1,0:T(8,128)(2,1)S(1)} %all-to-all-done.here_ref.next_ref, bf16[8,64,128]{2,1,0:T(8,128)(2,1)S(1)} %all_to_all.15.proj_ref, ...), custom_call_target="tpu_custom_call" | custom-call | flops 4400000000 | bytes 1048576 | tf_op jit(solution)/shard_map/pallas_call | solution.py:22
  104.8 6.8 %all-to-all-start.2 = ((bf16[16,64,128]{2,1,0:T(8,128)(2,1)}), bf16[16,64,128]{2,1,0:T(8,128)(2,1)S(1)}, u32[]{:S(2)}, u32[]{:S(2)}) async-start(bf16[16,64,128]{2,1,0:T(8,128)(2,1)} %shard_map.90.unread), calls=%async_computation.2 | async-start | bytes 524288 | tf_op jit(solution)/shard_map/all_to_all | solution.py:353
  111.7 1.6 %copy-done.2 = bf16[8192,128]{1,0:T(8,128)(2,1)S(1)} copy-done((bf16[8192,128]{1,0:T(8,128)(2,1)S(1)}, bf16[8192,128]{1,0:T(8,128)(2,1)}, u32[]{:S(2)}) %copy-start.2) | copy-done | bytes 2097176
  113.2 8.1 %shard_map.91 = bf16[64,128,128]{2,1,0:T(8,128)(2,1)} custom-call(bf16[8192,128]{1,0:T(8,128)(2,1)S(1)} %copy-done.2, bf16[8192,128]{1,0:T(8,128)(2,1)S(1)} %copy-done.2, bf16[8192,128]{1,0:T(8,128)(2,1)S(1)} %copy-done.2, bf16[8192,128]{1,0:T(8,128)(2,1)} %collective-permute-done.core_ref, bf16[8192,128]{1,0:T(8,128)(2,1)} %collective-permute-done.1.link_ref, ...), custom_call_target="tpu_custom_call" | custom-call | flops 7699999744 | bytes 1048576 | tf_op jit(solution)/shard_map/pallas_call | solution.py:22
  121.4 0.6 pad_maximum_fusion
  (29 shorter events, 0.4 us)
Async XLA Ops:
  1.4 1.6 %copy-start = (bf16[64,1,128,128]{3,2,1,0:T(8,128)(2,1)S(1)}, bf16[64,1,128,128]{3,2,1,0:T(8,128)(2,1)}, u32[]{:S(2)}) copy-start(bf16[64,1,128,128]{3,2,1,0:T(8,128)(2,1)} %param.7) | copy-start | bytes 6291460
  2.9 0.8 copy-start.5
  3.8 2.7 %copy-start.9 = (s32[384]{0:T(512)S(1)}, s32[384]{0:T(512)}, u32[]{:S(2)}) copy-start(s32[384]{0:T(512)} %param.11) | copy-start | bytes 4612
  3.8 2.7 %copy-start.10 = (s32[384]{0:T(512)S(1)}, s32[384]{0:T(512)}, u32[]{:S(2)}) copy-start(s32[384]{0:T(512)} %param.10) | copy-start | bytes 4612
  6.5 9.4 %copy-start.1 = (bf16[8192,128]{1,0:T(8,128)(2,1)}, bf16[8192,128]{1,0:T(8,128)(2,1)S(1)}, u32[]{:S(2)}) copy-start(bf16[8192,128]{1,0:T(8,128)(2,1)S(1)} %get-tuple-element.9.xt_ref.before_ref.after_ref) | copy-start | bytes 6291460
  6.5 2.1 %copy-start.3 = (bf16[384,16,128]{2,1,0:T(8,128)(2,1)S(1)}, bf16[384,16,128]{2,1,0:T(8,128)(2,1)}, u32[]{:S(2)}) copy-start(bf16[384,16,128]{2,1,0:T(8,128)(2,1)} %p_ref.3) | copy-start | bytes 4718596
  8.6 11.9 %copy-start.8 = (f32[256,16]{0,1:T(8,128)S(1)}, f32[256,16]{0,1:T(8,128)}, u32[]{:S(2)}) copy-start(f32[256,16]{0,1:T(8,128)} %param.13) | copy-start | bytes 49156
  15.9 4.8 %collective-permute-start.2 = (bf16[8,64,128]{2,1,0:T(8,128)(2,1)S(1)}, bf16[8,64,128]{2,1,0:T(8,128)(2,1)S(1)}, u32[]{:S(2)}, u32[]{:S(2)}) collective-permute-start(bf16[8,64,128]{2,1,0:T(8,128)(2,1)S(1)} %get-tuple-element.11), channel_id=1, source_target_pairs={{0,4},{4,0},{8,12},{12,8},{1,5},{5,1},{9,13},{13,9},{2,6},{6,2},{1... | collective-permute-start | bytes 393224 | tf_op jit(solution)/shard_map/ppermute | solution.py:310
  16.1 7.1 %collective-permute-start.3 = (bf16[8,64,128]{2,1,0:T(8,128)(2,1)S(1)}, bf16[8,64,128]{2,1,0:T(8,128)(2,1)S(1)}, u32[]{:S(2)}, u32[]{:S(2)}) collective-permute-start(bf16[8,64,128]{2,1,0:T(8,128)(2,1)S(1)} %get-tuple-element.12), channel_id=1, source_target_pairs={{4,8},{8,4},{5,9},{9,5},{6,10},{10,6},{7,11},{11,7},{20,24},{24,20... | collective-permute-start | bytes 393224 | tf_op jit(solution)/shard_map/ppermute | solution.py:309
  33.6 67.5 %all-to-all-start = ((bf16[16,592,128]{2,1,0:T(8,128)(2,1)}), bf16[16,592,128]{2,1,0:T(8,128)(2,1)S(1)}, u32[]{:S(2)}, u32[]{:S(2)}) async-start(bf16[16,592,128]{2,1,0:T(8,128)(2,1)} %get-tuple-element.14), calls=%async_computation | async-start | bytes 4849664 | tf_op jit(solution)/shard_map/all_to_all | solution.py:294
  38.6 73.0 %collective-permute-start = (bf16[8192,128]{1,0:T(8,128)(2,1)}, bf16[8192,128]{1,0:T(8,128)(2,1)}, u32[]{:S(2)}, u32[]{:S(2)}) collective-permute-start(bf16[8192,128]{1,0:T(8,128)(2,1)} %copy-done.1), channel_id=1, source_target_pairs={{0,4},{4,0},{8,12},{12,8},{1,5},{5,1},{9,13},{13,9},{2,6},{6,2},{1... | collective-permute-start | bytes 6291464 | tf_op jit(solution)/shard_map/ppermute | solution.py:296
  38.8 72.9 %collective-permute-start.1 = (bf16[8192,128]{1,0:T(8,128)(2,1)}, bf16[8192,128]{1,0:T(8,128)(2,1)}, u32[]{:S(2)}, u32[]{:S(2)}) collective-permute-start(bf16[8192,128]{1,0:T(8,128)(2,1)} %copy-done.1), channel_id=1, source_target_pairs={{4,8},{8,4},{5,9},{9,5},{6,10},{10,6},{7,11},{11,7},{20,24},{24,20... | collective-permute-start | bytes 6291464 | tf_op jit(solution)/shard_map/ppermute | solution.py:295
  42.3 2.4 %collective-permute-start.4 = (bf16[8,64,128]{2,1,0:T(8,128)(2,1)S(1)}, bf16[8,64,128]{2,1,0:T(8,128)(2,1)S(1)}, u32[]{:S(2)}, u32[]{:S(2)}) collective-permute-start(bf16[8,64,128]{2,1,0:T(8,128)(2,1)S(1)} %get-tuple-element.13.own_ref), channel_id=1, source_target_pairs={{0,4},{4,0},{8,12},{12,8},{1,5},{5,1},{9,13},{13,9},{2,6},{6,2},{1... | collective-permute-start | bytes 393224 | tf_op jit(solution)/shard_map/ppermute | solution.py:322
  42.4 47.0 %collective-permute-start.5 = (bf16[8,64,128]{2,1,0:T(8,128)(2,1)S(1)}, bf16[8,64,128]{2,1,0:T(8,128)(2,1)S(1)}, u32[]{:S(2)}, u32[]{:S(2)}) collective-permute-start(bf16[8,64,128]{2,1,0:T(8,128)(2,1)S(1)} %get-tuple-element.13.own_ref), channel_id=1, source_target_pairs={{4,8},{8,4},{5,9},{9,5},{6,10},{10,6},{7,11},{11,7},{20,24},{24,20... | collective-permute-start | bytes 393224 | tf_op jit(solution)/shard_map/ppermute | solution.py:321
  89.4 1.4 %copy-start.4 = (bf16[384,16,128]{2,1,0:T(8,128)(2,1)S(1)}, bf16[384,16,128]{2,1,0:T(8,128)(2,1)}, u32[]{:S(2)}) copy-start(bf16[384,16,128]{2,1,0:T(8,128)(2,1)} %p_ref.3) | copy-start | bytes 4718596
  99.1 2.0 %copy-start.7 = (f32[8256,128]{1,0:T(8,128)}, f32[8256,128]{1,0:T(8,128)S(1)}, u32[]{:S(2)}) copy-start(f32[8256,128]{1,0:T(8,128)S(1)} %shard_map.89.unread.nonlocal_ref) | copy-start | bytes 12681220
  101.1 10.6 %copy-start.6 = (f32[1,128,128]{2,1,0:T(8,128)S(1)}, f32[1,128,128]{2,1,0:T(8,128)}, u32[]{:S(2)}) copy-start(f32[1,128,128]{2,1,0:T(8,128)} %param.8) | copy-start | bytes 196612
  104.8 16.5 %all-to-all-start.2 = ((bf16[16,64,128]{2,1,0:T(8,128)(2,1)}), bf16[16,64,128]{2,1,0:T(8,128)(2,1)S(1)}, u32[]{:S(2)}, u32[]{:S(2)}) async-start(bf16[16,64,128]{2,1,0:T(8,128)(2,1)} %shard_map.90.unread), calls=%async_computation.2 | async-start | bytes 524288 | tf_op jit(solution)/shard_map/all_to_all | solution.py:353
  111.6 1.6 %copy-start.2 = (bf16[8192,128]{1,0:T(8,128)(2,1)S(1)}, bf16[8192,128]{1,0:T(8,128)(2,1)}, u32[]{:S(2)}) copy-start(bf16[8192,128]{1,0:T(8,128)(2,1)} %copy-done.1) | copy-start | bytes 6291460

commit v3 on v2

v3 whole, which is shorter than its diff:
```python
import functools

import jax
import jax.numpy as jnp
from jax import lax
from jax.experimental import pallas as pl
from jax.experimental.pallas import tpu as pltpu
from jax.sharding import PartitionSpec as P

F32 = jnp.float32
BF16 = jnp.bfloat16
LANES = 128
ROWS = 16
VMEM_BYTES = 32 * 1024 * 1024
NT = (((1,), (1,)), ((), ()))
WHOLE = pl.BlockSpec(memory_space=pltpu.VMEM)
SCALARS = pl.BlockSpec(memory_space=pltpu.SMEM)
FAR = pl.BlockSpec(memory_space=pltpu.HBM)
UNREAD = pl.BlockSpec(memory_space=pl.ANY)
copies = pltpu.SemaphoreType.DMA


def call(kernel, grid, in_specs, out_specs, outs, scratch, args, micros, aliases=None):
    return pl.pallas_call(
        kernel,
        grid=grid,
        out_shape=[jax.ShapeDtypeStruct(shape, kind) for shape, kind in outs],
        in_specs=in_specs,
        out_specs=out_specs,
        scratch_shapes=scratch,
        input_output_aliases=aliases or {},
        compiler_params=pltpu.CompilerParams(vmem_limit_bytes=VMEM_BYTES),
        cost_estimate=pl.CostEstimate(flops=int(micros * 1.1e9), bytes_accessed=1 << 20, transcendentals=0),
    )(*args)


def start(copy):
    copy.start()
    return copy


def pack_kernel(bands, first, ids_ref, x_hbm, xt, xt_hbm, *refs):
    halves, pieces, (x, in_sems, out_sems) = refs[:2], refs[2 : 1 + bands], refs[1 + bands :]
    states, lines, _ = x.shape
    share = lines // bands
    band = ids_ref[1]
    chunks = in_sems.shape[0]
    size = lines // chunks
    loads = []
    for c in range(chunks):
        where = (slice(None), pl.ds(c * size, size), slice(None))
        loads.append(start(pltpu.make_async_copy(x_hbm.at[where], x.at[where], in_sems.at[c])))

    for c in range(chunks):
        loads[c].wait()
        for y0 in range(c * size, (c + 1) * size, ROWS):
            for s0 in range(0, states, ROWS):
                block = x[s0 : s0 + ROWS, y0 : y0 + ROWS, :].astype(F32)
                turned = jnp.swapaxes(block, 0, 1).astype(BF16)
                xt[y0 : y0 + ROWS, s0 : s0 + ROWS, :] = turned

    sends = []

    def send(source, target):
        sends.append(start(pltpu.make_async_copy(source, target, out_sems.at[len(sends)])))

    for k in range(1, bands):
        begin = (band ^ k) * share
        count = share - first
        send(xt.at[pl.ds(begin + first, count)], pieces[k - 1].at[pl.ds(0, count)])
        send(xt.at[pl.ds(lax.rem(begin + share, lines), 1)], pieces[k - 1].at[pl.ds(count, 1)])
    send(xt.at[pl.ds(0, lines // 2)], halves[0])
    send(xt.at[pl.ds(lines // 2, lines // 2)], halves[1])
    send(xt, xt_hbm)
    for copy in sends:
        copy.wait()


def project_kernel(words_ref, ids_ref, xt_ref, p_hbm, core_ref, own_ref, link_ref, total, p_ref, sems):
    slots, proj_count, _ = p_ref.shape
    groups, states, _ = own_ref.shape
    per_group = LANES // proj_count
    chunks = sems.shape[0]
    size = slots // chunks
    unroll = 16
    loads = []
    for c in range(chunks):
        where = pl.ds(c * size, size)
        loads.append(start(pltpu.make_async_copy(p_hbm.at[where], p_ref.at[where], sems.at[c])))

    def clear(i, carry):
        for u in range(per_group):
            total[i * per_group + u] = jnp.zeros_like(total[0])
        return carry

    lax.fori_loop(0, 3 * groups, clear, 0)

    def body(i, carry):
        for u in range(unroll):
            t = i * unroll + u
            word = words_ref[t]
            line, atom = word >> 16, word & 0xFFFF
            total[atom] += lax.dot_general(p_ref[t], xt_ref[line], NT, preferred_element_type=F32)
        return carry

    for c in range(chunks):
        loads[c].wait()
        lax.fori_loop(c * size // unroll, (c + 1) * size // unroll, body, 0)
    odd = ids_ref[0] & 1
    core_first, link_first = (1 - odd) * 2 * groups, odd * 2 * groups

    def turned(group):
        tiles = [total[group * per_group + u] for u in range(per_group)]
        return jnp.concatenate(tiles, axis=0).T

    for g in range(groups):
        core_ref[g] = turned(core_first + g).astype(BF16)
        link_ref[g] = turned(link_first + g).astype(BF16)
        own_ref[g] = turned(groups + g)


def owner_kernel(bands, first, ids_ref, xt_ref, own_ref, core_hbm, link_hbm, energy_ref, half_in, *refs):
    half_out, scaled_ref, scaled_hbm, whole_ref = refs[:4]
    messages, (core_ref, link_ref, in_sems, out_sems) = refs[4 : 3 + bands], refs[3 + bands :]
    lines = xt_ref.shape[0]
    share = lines // bands
    band = ids_ref[1]
    groups = own_ref.shape[0]
    group_share = groups // bands
    loads = [
        start(pltpu.make_async_copy(core_hbm, core_ref, in_sems.at[0])),
        start(pltpu.make_async_copy(link_hbm, link_ref, in_sems.at[1])),
    ]
    sends = []

    def send(source, target):
        sends.append(start(pltpu.make_async_copy(source, target, out_sems.at[len(sends)])))

    for k in range(1, bands):
        send(xt_ref.at[pl.ds((band ^ k) * share, first)], messages[k - 1].at[pl.ds(0, first)])
    for copy in loads:
        copy.wait()
    row = ids_ref[0] * groups
    for g in range(groups):
        whole = own_ref[g] + core_ref[g].astype(F32) + link_ref[g].astype(F32)
        scaled_ref[g] = (whole * energy_ref[pl.ds(row + g, 1), :]).astype(BF16)
        whole_ref[g] = whole.astype(BF16)
    send(scaled_ref, scaled_hbm)
    for k in range(1, bands):
        send(whole_ref.at[pl.ds((band ^ k) * group_share, group_share)], messages[k - 1].at[pl.ds(first, group_share)])
    for copy in sends:
        copy.wait()


def nonlocal_kernel(words_ref, ids_ref, p_hbm, core_hbm, own_ref, link_hbm, out_ref, atoms, p_ref, core_ref, link_ref, sems):
    slots, proj_count, _ = p_ref.shape
    groups, states, _ = own_ref.shape
    per_group = LANES // proj_count
    lines = out_ref.shape[0]
    unroll = 16
    pairs = ((core_hbm, core_ref), (link_hbm, link_ref), (p_hbm, p_ref))
    loads = [start(pltpu.make_async_copy(far, near, sems.at[i])) for i, (far, near) in enumerate(pairs)]

    def clear(i, carry):
        out_ref[i] = jnp.zeros((states, LANES), F32)
        return carry

    lax.fori_loop(0, lines, clear, 0)
    odd = ids_ref[0] & 1

    def spread(first, ref):
        for g in range(groups):
            tile = ref[g]
            for u in range(per_group):
                atoms[(first + g) * per_group + u] = tile[:, u * proj_count : (u + 1) * proj_count]

    spread(groups, own_ref)
    loads[0].wait()
    spread((1 - odd) * 2 * groups, core_ref)
    loads[1].wait()
    spread(odd * 2 * groups, link_ref)
    loads[2].wait()

    def body(i, carry):
        for u in range(unroll):
            t = i * unroll + u
            word = words_ref[t]
            line, atom = word >> 16, word & 0xFFFF
            out_ref[line] += jnp.dot(atoms[atom], p_ref[t], preferred_element_type=F32)
        return carry

    lax.fori_loop(0, slots // unroll, body, 0)


def stencil_kernel(xt_ref, core_ref, early_ref, late_ref, added_ref, pot_ref, ring_ref, unread, out_ref):
    states, here, _ = out_ref.shape
    lines = xt_ref.shape[0]
    step = pl.program_id(0)
    y0 = step * here
    early = step < pl.num_programs(0) // 2
    for s0 in range(0, states, ROWS):
        rows = slice(s0, s0 + ROWS)
        results = []
        cells = jnp.concatenate([xt_ref[y0 + i, rows, :] for i in range(here)], axis=0)
        along = jnp.dot(cells, ring_ref[...], preferred_element_type=F32)
        before = xt_ref[lax.rem(y0 + lines - 1, lines), rows, :].astype(F32)
        x = xt_ref[y0, rows, :].astype(F32)
        for i in range(here):
            after = xt_ref[lax.rem(y0 + i + 1, lines), rows, :].astype(F32)
            link = jnp.where(early, early_ref[i, rows, :].astype(F32), late_ref[i, rows, :].astype(F32))
            beside = (before + after) + (core_ref[i, rows, :].astype(F32) + link)
            value = along[i * ROWS : (i + 1) * ROWS] + pot_ref[i : i + 1, :] * x
            results.append(value + added_ref[y0 + i, rows, :] - 0.5 * beside)
            before, x = x, after
        out_ref[rows, :, :] = jnp.swapaxes(jnp.stack(results, axis=0), 0, 1).astype(BF16)


def gather_kernel(bands, first, share, ids_ref, xt_ref, shares_ref, after_hbm, unread, *refs):
    pieces, outs = refs[: bands - 1], refs[bands - 1 :]
    later = after_hbm is None
    all_ref, pass_hbm = outs[:2]
    projs_ref = None if later else outs[2]
    sems, pass_sem = outs[-2:]
    lines, states, _ = xt_ref.shape
    band = ids_ref[1]
    begin = band * share + first
    count = all_ref.shape[0] - 1
    loads = []

    def load(source, target):
        loads.append(start(pltpu.make_async_copy(source, target, sems.at[len(loads)])))

    def at(k):
        return pl.ds(pl.multiple_of((band ^ k) * states, states), states)

    brought = count + 1 if later else count
    load(xt_ref.at[pl.ds(begin, count)], all_ref.at[pl.ds(0, count), at(0), :])
    for k in range(1, bands):
        load(pieces[k - 1].at[pl.ds(0, brought)], all_ref.at[pl.ds(0, brought), at(k), :])
    if later:
        load(xt_ref.at[pl.ds(lax.rem(begin + count, lines), 1)], all_ref.at[pl.ds(count, 1), at(0), :])
    else:
        load(after_hbm.at[pl.ds(0, 1)], all_ref.at[pl.ds(count, 1)])
        held = projs_ref.shape[0]
        load(shares_ref.at[pl.ds(band * held, held)], projs_ref.at[:, at(0), :])
        for k in range(1, bands):
            load(pieces[k - 1].at[pl.ds(count, held)], projs_ref.at[:, at(k), :])
    for copy in loads:
        copy.wait()
    half = count // 2
    passed = pltpu.make_async_copy(all_ref.at[pl.ds((1 - (ids_ref[0] & 1)) * half, half)], pass_hbm, pass_sem)
    passed.start()
    passed.wait()


def add_products(row, ids_ref, all_ref, core_ref, link_ref, pot_ref, acc):
    half = core_ref.shape[0]
    group = 4
    mine = (ids_ref[0] & 1) * half
    for part, base in ((0, mine), (1, half - mine)):
        for i0 in range(0, half, group):
            xs, ys = [], []
            for i in range(i0, min(i0 + group, half)):
                cell = all_ref[base + i]
                x = cell.astype(F32)
                y = (3.0 + pot_ref[pl.ds(row + base + i, 1), :]) * x - pltpu.roll(x, x.shape[1] - 1, 1)
                y = y - all_ref[base + i + 1].astype(F32)
                if part == 0:
                    y = y - core_ref[i].astype(F32) - link_ref[i].astype(F32)
                xs.append(cell)
                ys.append(y.astype(BF16))
            flat_x = jnp.concatenate(xs, axis=1)
            flat_y = jnp.concatenate(ys, axis=1)
            acc[0] += lax.dot_general(flat_x, flat_x, NT, preferred_element_type=F32)
            acc[1] += lax.dot_general(flat_y, flat_x, NT, preferred_element_type=F32)


def gram_kernel(first, share, ids_ref, all_ref, core_ref, link_ref, pot_ref, unread, acc):
    acc[...] = jnp.zeros_like(acc)
    add_products(ids_ref[1] * share + first, ids_ref, all_ref, core_ref, link_ref, pot_ref, acc)


def final_kernel(
    bands, domains, share, ids_ref, all_ref, core_ref, link_ref, pot_ref, begun_ref, proj_ref, energy_ref, out_ref, acc
):
    acc[...] = begun_ref[...]
    add_products(ids_ref[1] * share, ids_ref, all_ref, core_ref, link_ref, pot_ref, acc)
    groups = proj_ref.shape[0]
    first = (ids_ref[0] * bands + ids_ref[1]) * groups
    for g in range(groups):
        here = proj_ref[g]
        scaled = (here.astype(F32) * energy_ref[pl.ds(first + g, 1), :]).astype(BF16)
        acc[1] += lax.dot_general(scaled, here, NT, preferred_element_type=F32)
    gram = acc[0]
    hamil = 0.5 * (acc[1] + acc[1].T)
    rows, cols = gram.shape[0] // bands, gram.shape[0] // domains
    for c in range(domains):
        for r in range(bands):
            r0, c0 = r * rows, c * cols
            out_ref[c * bands + r, :, :cols] = gram[r0 : r0 + rows, c0 : c0 + cols].astype(BF16)
            out_ref[c * bands + r, :, cols:] = hamil[r0 : r0 + rows, c0 : c0 + cols].astype(BF16)


def local(orbitals, potential, projectors, tile_atom, tile_line, tile_count, energies):
    states, _, lines, cols_z = orbitals.shape
    slots, proj_count, _ = projectors.shape
    atom_total = energies.shape[0]
    domains, bands = lax.axis_size("domain"), lax.axis_size("band")
    domain, band = lax.axis_index("domain"), lax.axis_index("band")
    total_states = states * bands
    atoms_here = atom_total // domains
    per_group = LANES // proj_count
    groups = atoms_here // per_group
    group_share = groups // bands
    parts = domains * bands
    share = lines // bands
    first = share // 4
    rest = share - first

    core_pairs = [(i, i ^ 1) for i in range(domains) if i ^ 1 < domains]
    link_pairs = [(i, ((i + 1) ^ 1) - 1) for i in range(1, domains) if ((i + 1) ^ 1) - 1 < domains]
    band_pairs = [[(i, i ^ k) for i in range(bands)] for k in range(bands)]
    far_first = sorted(range(1, bands), key=lambda k: -k)

    def swapped(values):
        got = {k: lax.ppermute(values[k - 1], "band", band_pairs[k]) for k in far_first}
        return [got[k] for k in range(1, bands)]

    ids = jnp.stack([domain, band]).astype(jnp.int32)
    near = jnp.clip(tile_atom - (domain - 1) * atoms_here, 0, 3 * atoms_here - 1)
    live = jnp.arange(slots, dtype=jnp.int32) < tile_count[0]
    project_words = (tile_line << 16) | jnp.where(live, near, 3 * atoms_here)
    nonlocal_words = (jnp.where(live, tile_line, lines) << 16) | near
    field = orbitals.reshape(states, lines, cols_z)
    pot = potential.reshape(lines, cols_z)
    energy = energies.reshape(atom_total // per_group, LANES)
    eye = jnp.eye(cols_z, dtype=F32)
    ring = (3.0 * eye - 0.5 * (jnp.roll(eye, 1, axis=0) + jnp.roll(eye, -1, axis=0))).astype(BF16)

    chunks = 4
    line_shape, half_shape = (lines, states, cols_z), (lines // 2, states, cols_z)
    packed = call(
        functools.partial(pack_kernel, bands, first),
        (),
        [SCALARS, FAR],
        [WHOLE] + [FAR] * (2 + bands),
        [(line_shape, BF16), (line_shape, BF16), (half_shape, BF16), (half_shape, BF16)]
        + [((rest + 1, states, cols_z), BF16)] * (bands - 1),
        [pltpu.VMEM((states, lines, cols_z), BF16), copies((chunks,)), copies((2 * bands + 1,))],
        (ids, field),
        3,
    )
    xt, xt_far, early_half, late_half = packed[:4]
    later = swapped(packed[4:])
    link_early = lax.ppermute(early_half, "domain", link_pairs)
    core_field = lax.ppermute(xt_far, "domain", core_pairs)

    group_shape = (groups, states, LANES)
    to_core, own, to_link = call(
        project_kernel,
        (),
        [SCALARS, SCALARS, WHOLE, FAR],
        [WHOLE] * 3,
        [(group_shape, BF16), (group_shape, F32), (group_shape, BF16)],
        [
            pltpu.VMEM((3 * atoms_here + 1, proj_count, states), F32),
            pltpu.VMEM(projectors.shape, BF16),
            copies((4,)),
        ],
        (project_words, ids, xt, projectors),
        8,
    )
    from_link = lax.ppermute(to_link, "domain", link_pairs)
    from_core = lax.ppermute(to_core, "domain", core_pairs)
    owned = call(
        functools.partial(owner_kernel, bands, first),
        (),
        [SCALARS, WHOLE, WHOLE, FAR, FAR, WHOLE, FAR],
        [FAR, WHOLE, FAR, WHOLE] + [FAR] * (bands - 1),
        [(half_shape, BF16)]
        + [(group_shape, BF16)] * 3
        + [((first + group_share, states, cols_z), BF16)] * (bands - 1),
        [pltpu.VMEM(group_shape, BF16), pltpu.VMEM(group_shape, BF16), copies((2,)), copies((2 * bands - 1,))],
        (ids, xt, own, from_core, from_link, energy, late_half),
        1,
        aliases={6: 0},
    )
    late_half, scaled, scaled_far, whole = owned[:4]
    link_scaled = lax.ppermute(scaled_far, "domain", link_pairs)
    core_scaled = lax.ppermute(scaled_far, "domain", core_pairs)
    link_late = lax.ppermute(late_half, "domain", link_pairs)
    early = swapped(owned[4:])

    (added,) = call(
        nonlocal_kernel,
        (),
        [SCALARS, SCALARS, FAR, FAR, WHOLE, FAR],
        [WHOLE],
        [((lines + 1, states, cols_z), F32)],
        [
            pltpu.VMEM((3 * atoms_here, states, proj_count), BF16),
            pltpu.VMEM(projectors.shape, BF16),
            pltpu.VMEM(group_shape, BF16),
            pltpu.VMEM(group_shape, BF16),
            copies((3,)),
        ],
        (nonlocal_words, ids, projectors, core_scaled, scaled, link_scaled),
        9,
    )

    def later_kernel(ids_ref, xt_ref, unread, *refs):
        gather_kernel(bands, first, share, ids_ref, xt_ref, None, None, unread, *refs)

    later_all, later_pass = call(
        later_kernel,
        (),
        [SCALARS, WHOLE, UNREAD] + [FAR] * (bands - 1),
        [WHOLE, FAR],
        [((rest + 1, total_states, cols_z), BF16), ((rest // 2, total_states, cols_z), BF16)],
        [copies((bands + 1,)), copies],
        (ids, xt, added, *later),
        2,
    )
    later_link = lax.ppermute(later_pass, "domain", link_pairs)
    later_core = lax.ppermute(later_pass, "domain", core_pairs)

    steps = lines // ROWS
    block = pl.BlockSpec((ROWS, states, cols_z), lambda i: (i, 0, 0))
    (applied,) = call(
        stencil_kernel,
        (steps,),
        [
            WHOLE,
            block,
            pl.BlockSpec((ROWS, states, cols_z), lambda i: (jnp.minimum(i, steps // 2 - 1), 0, 0)),
            pl.BlockSpec((ROWS, states, cols_z), lambda i: (jnp.maximum(i - steps // 2, 0), 0, 0)),
            WHOLE,
            pl.BlockSpec((ROWS, cols_z), lambda i: (i, 0)),
            WHOLE,
            UNREAD,
        ],
        [pl.BlockSpec((states, ROWS, cols_z), lambda i: (0, i, 0))],
        [((states, lines, cols_z), BF16)],
        [],
        (xt, core_field, link_early, link_late, added, pot, ring, later_all),
        6,
    )

    def early_kernel(ids_ref, xt_ref, shares_ref, after_ref, unread, *refs):
        gather_kernel(bands, 0, share, ids_ref, xt_ref, shares_ref, after_ref, unread, *refs)

    early_all, early_pass, projs = call(
        early_kernel,
        (),
        [SCALARS, WHOLE, WHOLE, WHOLE, UNREAD] + [FAR] * (bands - 1),
        [WHOLE, FAR, WHOLE],
        [
            ((first + 1, total_states, cols_z), BF16),
            ((first // 2, total_states, cols_z), BF16),
            ((group_share, total_states, LANES), BF16),
        ],
        [copies((2 * bands + 1,)), copies],
        (ids, xt, whole, later_all, applied, *early),
        1,
    )
    early_link = lax.ppermute(early_pass, "domain", link_pairs)
    early_core = lax.ppermute(early_pass, "domain", core_pairs)
    (begun,) = call(
        functools.partial(gram_kernel, first, share),
        (),
        [SCALARS, WHOLE, WHOLE, WHOLE, WHOLE, UNREAD],
        [WHOLE],
        [((2, total_states, total_states), F32)],
        [],
        (ids, later_all, later_core, later_link, pot, early_all),
        2,
    )
    (blocks,) = call(
        functools.partial(final_kernel, bands, domains, share),
        (),
        [SCALARS] + [WHOLE] * 7,
        [WHOLE],
        [((parts, states, 2 * total_states // domains), BF16)],
        [pltpu.VMEM((2, total_states, total_states), F32)],
        (ids, early_all, early_core, early_link, pot, begun, projs, energy),
        2,
    )
    summed = lax.all_to_all(blocks, ("domain", "band"), split_axis=0, concat_axis=0, tiled=True)
    scale = 1.0 / (lines * cols_z * domains)
    result = jnp.sum(summed.astype(F32), axis=0) * scale
    cols = total_states // domains
    subspace = jnp.stack([result[:, :cols], result[:, cols:]])
    return applied.reshape(orbitals.shape), subspace


def solution(mesh):
    in_specs = (
        P("band", ("groups", "domain"), None, None),
        P(("groups", "domain"), None, None),
        P(("groups", "domain"), None, None),
        P(("groups", "domain")),
        P(("groups", "domain")),
        P(("groups", "domain")),
        P("groups", None),
    )
    out_specs = (P("band", ("groups", "domain"), None, None), P(None, ("groups", "band"), "domain"))
    return jax.shard_map(local, mesh=mesh, in_specs=in_specs, out_specs=out_specs, check_vma=False)
```

time: 123 us -> 107 us (0.87)
  waiting for transfers between devices: 47.1 us -> 12 us
  starting transfers between devices: 22.4 us -> 30.6 us
  Pallas kernels: 30.7 us -> 36.9 us
  blocking collectives: 9.82 us -> 13.9 us
    ppermute x4 -> x15, waiting for transfers between devices: 44.7 us -> 11.6 us  [the longest x1 5.4 us: local(): link_late = lax.ppermute(late_half, 'domain', link_pairs)]
    ppermute x4 -> x15, starting transfers between devices: 6.02 us -> 27.1 us  [the longest x6 9.67 us: swapped(): lax.ppermute(values[k - 1], 'band', band_pairs[k])]
    all_to_all x2 -> x0, starting transfers between devices: 11.8 us -> none  [the longest x1 6.77 us: local(): lax.all_to_all(blocks, ('domain', 'band'), split_axis=0, concat_axis=0, t...]
    pallas_call x6 -> x9, Pallas kernels: 30.7 us -> 36.9 us  [call(): pl.pallas_call(kernel, grid=grid, out_shape=[jax.ShapeDtypeStruct(shape,...]
    all_to_all x1, blocking collectives: 9.82 us -> 13.9 us  [local(): lax.all_to_all(blocks, ('domain', 'band'), split_axis=0, concat_axis=0, t...]
    ppermute x1, waiting for transfers between devices: 2.41 us -> 0.44 us  [local(): from_link = lax.ppermute(to_link, 'domain', link_pairs)]
    unnamed x23 -> x29, local copies, waits for them, and re-layouts: 9.62 us -> 7.94 us
  transfers between devices with their start and end apart: 8 -> 17, of which waited for: 2 -> 5; matrix products, arithmetic and copies ran while one was open for 0% -> 2% of each run, Pallas kernels for 17% -> 30%
where the time goes in v3:
time: 107 us; the launch traced here: 106 us
  Pallas kernels  36.9 us (34%)
  starting transfers between devices  30.6 us (29%)
  blocking collectives  13.9 us (13%)
  waiting for transfers between devices  12 us (11%)
  local copies, waits for them, and re-layouts  9.67 us (9%)
  between operations  1.63 us (2%)
    pallas_call x9, Pallas kernels, call(): pl.pallas_call(kernel, grid=grid, out_shape=[jax.ShapeDtypeStruct(shape,...  36.9 us
    all_to_all x1, blocking collectives, local(): lax.all_to_all(blocks, ('domain', 'band'), split_axis=0, concat_axis=0, t...  13.9 us
    ppermute x6, starting transfers between devices, swapped(): lax.ppermute(values[k - 1], 'band', band_pairs[k])  9.67 us
    unnamed x29, local copies, waits for them, and re-layouts  7.94 us
    ppermute x1, waiting for transfers between devices, local(): link_late = lax.ppermute(late_half, 'domain', link_pairs)  5.4 us
    ppermute x1, starting transfers between devices, local(): later_link = lax.ppermute(later_pass, 'domain', link_pairs)  3.66 us
    ppermute x1, starting transfers between devices, local(): from_link = lax.ppermute(to_link, 'domain', link_pairs)  3.56 us
    ppermute x1, starting transfers between devices, local(): link_early = lax.ppermute(early_half, 'domain', link_pairs)  3.51 us
  transfers between devices with their start and end apart: 17, of which 5 were waited for; matrix products, arithmetic and copies ran while one was open for 2% of the time, Pallas kernels for 30%

profile of v3, /device:TPU:1, one launch (start us, length us, event | category | flops | bytes accessed | tf_op | source)
XLA Modules:
  0.0 105.6 jit_solution(18266753536884742676)
XLA Ops:
  0.7 1.6 %copy-done.1 = bf16[64,1,128,128]{3,2,1,0:T(8,128)(2,1)S(1)} copy-done((bf16[64,1,128,128]{3,2,1,0:T(8,128)(2,1)S(1)}, bf16[64,1,128,128]{3,2,1,0:T(8,128)(2,1)}, u32[]{:S(2)}) %copy-start.1) | copy-done | bytes 2097176
  2.3 4.0 %shard_map.86 = (bf16[128,64,128]{2,1,0:T(8,128)(2,1)S(1)}, bf16[128,64,128]{2,1,0:T(8,128)(2,1)}, bf16[64,64,128]{2,1,0:T(8,128)(2,1)S(1)}, bf16[64,64,128]{2,1...) custom-call(s32[2]{0:T(128)S(1)} %pad_add_fusion.ids_ref, ...), custom_call_target="tpu_custom_call" | custom-call | flops 3300000000 | bytes 1048576 | tf_op jit(solution)/shard_map/pallas_call | solution.py:24
  7.1 2.1 %collective-permute-start.7 = (bf16[25,64,128]{2,1,0:T(8,128)(2,1)}, bf16[25,64,128]{2,1,0:T(8,128)(2,1)}, u32[]{:S(2)}, u32[]{:S(2)}) collective-permute-start(bf16[25,64,128]{2,1,0:T(8,128)(2,1)} %get-tuple-element.34), channel_id=1, source_target_pairs={{0,1},{1,0},{2,3},{3,2},{4,5},{5,4},{6,7},{7,6},{8,9},{9,8},{10,11... | collective-permute-start | bytes 1228808 | tf_op jit(solution)/shard_map/ppermute | solution.py:326
  9.3 2.3 %collective-permute-start.8 = (bf16[25,64,128]{2,1,0:T(8,128)(2,1)}, bf16[25,64,128]{2,1,0:T(8,128)(2,1)}, u32[]{:S(2)}, u32[]{:S(2)}) collective-permute-start(bf16[25,64,128]{2,1,0:T(8,128)(2,1)} %get-tuple-element.35), channel_id=1, source_target_pairs={{0,2},{1,3},{2,0},{3,1},{4,6},{5,7},{6,4},{7,5},{8,10},{9,11},{10,... | collective-permute-start | bytes 1228808 | tf_op jit(solution)/shard_map/ppermute | solution.py:326
  14.9 8.8 %shard_map.87 = (bf16[8,64,128]{2,1,0:T(8,128)(2,1)}, f32[8,64,128]{2,1,0:T(8,128)S(1)}, bf16[8,64,128]{2,1,0:T(8,128)(2,1)}) custom-call(s32[384]{0:T(512)S(1)} %get-tuple-element.57.words_ref, s32[2]{0:T(128)S(1)} %pad_add_fusion.ids_ref, bf16[128,64,128]{2,1,0:T(8,128)(2,1)S(1)} %get-tuple-element.24.xt_ref, bf16[384,16,128]{2,1,0:T(8,128)(2,1)S(1)} %copy-done.2), custom_call_target="tpu_custom_call" | custom-call | flops 8800000000 | bytes 1048576 | tf_op jit(solution)/shard_map/pallas_call | solution.py:24
  24.4 3.6 %collective-permute-start.3 = (bf16[8,64,128]{2,1,0:T(8,128)(2,1)}, bf16[8,64,128]{2,1,0:T(8,128)(2,1)S(1)}, u32[]{:S(2)}, u32[]{:S(2)}) collective-permute-start(bf16[8,64,128]{2,1,0:T(8,128)(2,1)} %get-tuple-element.29), channel_id=1, source_target_pairs={{4,8},{8,4},{5,9},{9,5},{6,10},{10,6},{7,11},{11,7},{20,24},{24,20... | collective-permute-start | bytes 393224 | tf_op jit(solution)/shard_map/ppermute | solution.py:373
  32.0 1.8 %shard_map.88 = (bf16[64,64,128]{2,1,0:T(8,128)(2,1)}, bf16[8,64,128]{2,1,0:T(8,128)(2,1)S(1)}, bf16[8,64,128]{2,1,0:T(8,128)(2,1)S(1)}, bf16[8,64,128]{2,1,0:T(...) custom-call(s32[2]{0:T(128)S(1)} %pad_add_fusion.ids_ref, ...), custom_call_target="tpu_custom_call", output_to_operand_aliasing={{0}: (6, {})} | custom-call | flops 1100000000 | bytes 1048576 | tf_op jit(solution)/shard_map/pallas_call | solution.py:24
  33.8 3.5 %collective-permute-start.6 = (bf16[8,64,128]{2,1,0:T(8,128)(2,1)S(1)}, bf16[8,64,128]{2,1,0:T(8,128)(2,1)S(1)}, u32[]{:S(2)}, u32[]{:S(2)}) collective-permute-start(bf16[8,64,128]{2,1,0:T(8,128)(2,1)S(1)} %get-tuple-element.32), channel_id=1, source_target_pairs={{4,8},{8,4},{5,9},{9,5},{6,10},{10,6},{7,11},{11,7},{20,24},{24,20... | collective-permute-start | bytes 393224 | tf_op jit(solution)/shard_map/ppermute | solution.py:389
  37.4 2.7 %collective-permute-done.6.link_hbm = bf16[8,64,128]{2,1,0:T(8,128)(2,1)S(1)} collective-permute-done((bf16[8,64,128]{2,1,0:T(8,128)(2,1)S(1)}, bf16[8,64,128]{2,1,0:T(8,128)(2,1)S(1)}, u32[]{:S(2)}, u32[]{:S(2)}) %collective-permute-start.6) | collective-permute-done | bytes 131104 | tf_op jit(solution)/shard_map/ppermute | solution.py:389
  40.3 3.5 %collective-permute-start.1 = (bf16[64,64,128]{2,1,0:T(8,128)(2,1)S(1)}, bf16[64,64,128]{2,1,0:T(8,128)(2,1)S(1)}, u32[]{:S(2)}, u32[]{:S(2)}) collective-permute-start(bf16[64,64,128]{2,1,0:T(8,128)(2,1)S(1)} %get-tuple-element.26), channel_id=1, source_target_pairs={{4,8},{8,4},{5,9},{9,5},{6,10},{10,6},{7,11},{11,7},{20,24},{24,20... | collective-permute-start | bytes 3145736 | tf_op jit(solution)/shard_map/ppermute | solution.py:355
  43.8 2.0 %collective-permute-start.4 = (bf16[64,64,128]{2,1,0:T(8,128)(2,1)}, bf16[64,64,128]{2,1,0:T(8,128)(2,1)S(1)}, u32[]{:S(2)}, u32[]{:S(2)}) collective-permute-start(bf16[64,64,128]{2,1,0:T(8,128)(2,1)} %get-tuple-element.31), channel_id=1, source_target_pairs={{4,8},{8,4},{5,9},{9,5},{6,10},{10,6},{7,11},{11,7},{20,24},{24,20... | collective-permute-start | bytes 3145736 | tf_op jit(solution)/shard_map/ppermute | solution.py:391
  45.8 9.1 %shard_map.89.unread.added_ref = f32[129,64,128]{2,1,0:T(8,128)S(1)} custom-call(s32[384]{0:T(512)S(1)} %get-tuple-element.56.words_ref, s32[2]{0:T(128)S(1)} %pad_add_fusion.ids_ref, bf16[384,16,128]{2,1,0:T(8,128)(2,1)S(1)} %copy-done.3, bf16[8,64,128]{2,1,0:T(8,128)(2,1)S(1)} %collective-permute-done.5.core_hbm, ...), custom_call_target="tpu_custom_call" | custom-call | flops 9900000256 | bytes 1048576 | tf_op jit(solution)/shard_map/pallas_call | solution.py:24
  55.0 1.8 %shard_map.90 = (bf16[25,256,128]{2,1,0:T(8,128)(2,1)S(1)}, bf16[12,256,128]{2,1,0:T(8,128)(2,1)S(1)}) custom-call(s32[2]{0:T(128)S(1)} %pad_add_fusion.ids_ref, bf16[128,64,128]{2,1,0:T(8,128)(2,1)S(1)} %get-tuple-element.24.xt_ref, f32[129,64,128]{2,1,0:T(8,128)S(1)} %shard_map.89.unread.added_ref, bf16[25,64,128]{2,1,0:T(8,128)(2,1)} %collective-permute-done.7.refs_0_, ...), custom_call_target="tpu_custom_call" | custom-call | flops 2200000000 | bytes 1048576 | tf_op jit(solution)/shard_map/pallas_call | solution.py:24
  56.8 3.7 %collective-permute-start.16 = (bf16[12,256,128]{2,1,0:T(8,128)(2,1)S(1)}, bf16[12,256,128]{2,1,0:T(8,128)(2,1)S(1)}, u32[]{:S(2)}, u32[]{:S(2)}) collective-permute-start(bf16[12,256,128]{2,1,0:T(8,128)(2,1)S(1)} %get-tuple-element.44), channel_id=1, source_target_pairs={{4,8},{8,4},{5,9},{9,5},{6,10},{10,6},{7,11},{11,7},{20,24},{24,20... | collective-permute-start | bytes 2359304 | tf_op jit(solution)/shard_map/ppermute | solution.py:424
  60.6 1.9 %collective-permute-start.10 = (bf16[10,64,128]{2,1,0:T(8,128)(2,1)S(1)}, bf16[10,64,128]{2,1,0:T(8,128)(2,1)S(1)}, u32[]{:S(2)}, u32[]{:S(2)}) collective-permute-start(bf16[10,64,128]{2,1,0:T(8,128)(2,1)S(1)} %get-tuple-element.39), channel_id=1, source_target_pairs={{0,1},{1,0},{2,3},{3,2},{4,5},{5,4},{6,7},{7,6},{8,9},{9,8},{10,11... | collective-permute-start | bytes 491528 | tf_op jit(solution)/shard_map/ppermute | solution.py:326
  62.5 5.4 %collective-permute-done.4.late_ref = bf16[64,64,128]{2,1,0:T(8,128)(2,1)S(1)} collective-permute-done((bf16[64,64,128]{2,1,0:T(8,128)(2,1)}, bf16[64,64,128]{2,1,0:T(8,128)(2,1)S(1)}, u32[]{:S(2)}, u32[]{:S(2)}) %collective-permute-start.4) | collective-permute-done | bytes 1048608 | tf_op jit(solution)/shard_map/ppermute | solution.py:391
  69.1 2.0 %collective-permute-start.12 = (bf16[10,64,128]{2,1,0:T(8,128)(2,1)S(1)}, bf16[10,64,128]{2,1,0:T(8,128)(2,1)S(1)}, u32[]{:S(2)}, u32[]{:S(2)}) collective-permute-start(bf16[10,64,128]{2,1,0:T(8,128)(2,1)S(1)} %get-tuple-element.41), channel_id=1, source_target_pairs={{0,3},{1,2},{2,1},{3,0},{4,7},{5,6},{6,5},{7,4},{8,11},{9,10},{10,... | collective-permute-start | bytes 491528 | tf_op jit(solution)/shard_map/ppermute | solution.py:326
  71.1 7.3 %shard_map.91.unread = bf16[64,128,128]{2,1,0:T(8,128)(2,1)} custom-call(bf16[128,64,128]{2,1,0:T(8,128)(2,1)S(1)} %get-tuple-element.24.xt_ref, bf16[128,64,128]{2,1,0:T(8,128)(2,1)} %collective-permute-done.core_ref, bf16[64,64,128]{2,1,0:T(8,128)(2,1)S(1)} %collective-permute-done.1.early_ref, bf16[64,64,128]{2,1,0:T(8,128)(2,1)S(1)} %collective-permute-done.4.late_ref, ...), custom_call_target="tpu_custom_call" | custom-call | flops 6600000000 | bytes 1048576 | tf_op jit(solution)/shard_map/pallas_call | solution.py:24
  79.2 1.6 %copy-done = bf16[64,128,128]{2,1,0:T(8,128)(2,1)S(1)} copy-done((bf16[64,128,128]{2,1,0:T(8,128)(2,1)S(1)}, bf16[64,128,128]{2,1,0:T(8,128)(2,1)}, u32[]{:S(2)}) %copy-start) | copy-done | bytes 2097176
  81.7 3.3 %collective-permute-start.14 = (bf16[4,256,128]{2,1,0:T(8,128)(2,1)S(1)}, bf16[4,256,128]{2,1,0:T(8,128)(2,1)S(1)}, u32[]{:S(2)}, u32[]{:S(2)}) collective-permute-start(bf16[4,256,128]{2,1,0:T(8,128)(2,1)S(1)} %get-tuple-element.43), channel_id=1, source_target_pairs={{4,8},{8,4},{5,9},{9,5},{6,10},{10,6},{7,11},{11,7},{20,24},{24,20... | collective-permute-start | bytes 786440 | tf_op jit(solution)/shard_map/ppermute | solution.py:466
  85.1 1.7 %shard_map.93.begun_ref = f32[2,256,256]{2,1,0:T(8,128)S(1)} custom-call(s32[2]{0:T(128)S(1)} %pad_add_fusion.ids_ref, bf16[25,256,128]{2,1,0:T(8,128)(2,1)S(1)} %get-tuple-element.37.unread.after_ref.all_ref, bf16[12,256,128]{2,1,0:T(8,128)(2,1)S(1)} %collective-permute-done.15.core_ref, bf16[12,256,128]{2,1,0:T(8,128)(2,1)S(1)} %collective-permute-done.16.link_ref, ...), custom_call_target="tpu_custom_call" | custom-call | flops 2200000000 | bytes 1048576 | tf_op jit(solution)/shard_map/pallas_call | solution.py:24
  86.8 2.6 %collective-permute-done.14.link_ref = bf16[4,256,128]{2,1,0:T(8,128)(2,1)S(1)} collective-permute-done((bf16[4,256,128]{2,1,0:T(8,128)(2,1)S(1)}, bf16[4,256,128]{2,1,0:T(8,128)(2,1)S(1)}, u32[]{:S(2)}, u32[]{:S(2)}) %collective-permute-start.14) | collective-permute-done | bytes 262176 | tf_op jit(solution)/shard_map/ppermute | solution.py:466
  89.4 1.4 %shard_map.94 = bf16[16,64,128]{2,1,0:T(8,128)(2,1)S(1)} custom-call(s32[2]{0:T(128)S(1)} %pad_add_fusion.ids_ref, bf16[9,256,128]{2,1,0:T(8,128)(2,1)S(1)} %get-tuple-element.42.unread.all_ref, bf16[4,256,128]{2,1,0:T(8,128)(2,1)S(1)} %collective-permute-done.13.core_ref, bf16[4,256,128]{2,1,0:T(8,128)(2,1)S(1)} %collective-permute-done.14.link_ref, ...), custom_call_target="tpu_custom_call" | custom-call | flops 2200000000 | bytes 1048576 | tf_op jit(solution)/shard_map/pallas_call | solution.py:24
  90.9 13.9 %all_to_all.5 = bf16[16,64,128]{2,1,0:T(8,128)(2,1)S(1)} all-to-all(bf16[16,64,128]{2,1,0:T(8,128)(2,1)S(1)} %shard_map.94), channel_id=1, replica_groups=mesh['groups'=2,'domain'=4,'band'=4] {'domain','band'}, dimensions={0} | all-to-all | bytes 524288 | tf_op jit(solution)/shard_map/all_to_all | solution.py:488
  (60 shorter events, 12.3 us)
Async XLA Ops:
  2.3 11.2 %copy-start.12 = (s32[384]{0:T(512)S(1)}, s32[384]{0:T(512)}, u32[]{:S(2)}) copy-start(s32[384]{0:T(512)} %param.11) | copy-start | bytes 4612
  2.3 11.2 %copy-start.13 = (s32[384]{0:T(512)S(1)}, s32[384]{0:T(512)}, u32[]{:S(2)}) copy-start(s32[384]{0:T(512)} %param.10) | copy-start | bytes 4612
  7.1 36.6 %collective-permute-start.7 = (bf16[25,64,128]{2,1,0:T(8,128)(2,1)}, bf16[25,64,128]{2,1,0:T(8,128)(2,1)}, u32[]{:S(2)}, u32[]{:S(2)}) collective-permute-start(bf16[25,64,128]{2,1,0:T(8,128)(2,1)} %get-tuple-element.34), channel_id=1, source_target_pairs={{0,1},{1,0},{2,3},{3,2},{4,5},{5,4},{6,7},{7,6},{8,9},{9,8},{10,11... | collective-permute-start | bytes 1228808 | tf_op jit(solution)/shard_map/ppermute | solution.py:326
  9.3 45.7 %collective-permute-start.8 = (bf16[25,64,128]{2,1,0:T(8,128)(2,1)}, bf16[25,64,128]{2,1,0:T(8,128)(2,1)}, u32[]{:S(2)}, u32[]{:S(2)}) collective-permute-start(bf16[25,64,128]{2,1,0:T(8,128)(2,1)} %get-tuple-element.35), channel_id=1, source_target_pairs={{0,2},{1,3},{2,0},{3,1},{4,6},{5,7},{6,4},{7,5},{8,10},{9,11},{10,... | collective-permute-start | bytes 1228808 | tf_op jit(solution)/shard_map/ppermute | solution.py:326
  11.6 57.5 %collective-permute-start = (bf16[128,64,128]{2,1,0:T(8,128)(2,1)}, bf16[128,64,128]{2,1,0:T(8,128)(2,1)}, u32[]{:S(2)}, u32[]{:S(2)}) collective-permute-start(bf16[128,64,128]{2,1,0:T(8,128)(2,1)} %get-tuple-element.25), channel_id=1, source_target_pairs={{0,4},{4,0},{8,12},{12,8},{1,5},{5,1},{9,13},{13,9},{2,6},{6,2},{1... | collective-permute-start | bytes 6291464 | tf_op jit(solution)/shard_map/ppermute | solution.py:356
  14.9 13.8 %copy-start.11 = (f32[256,16]{0,1:T(8,128)S(1)}, f32[256,16]{0,1:T(8,128)}, u32[]{:S(2)}) copy-start(f32[256,16]{0,1:T(8,128)} %param.13) | copy-start | bytes 49156
  24.4 6.0 %collective-permute-start.2 = (bf16[8,64,128]{2,1,0:T(8,128)(2,1)}, bf16[8,64,128]{2,1,0:T(8,128)(2,1)S(1)}, u32[]{:S(2)}, u32[]{:S(2)}) collective-permute-start(bf16[8,64,128]{2,1,0:T(8,128)(2,1)} %get-tuple-element.28), channel_id=1, source_target_pairs={{0,4},{4,0},{8,12},{12,8},{1,5},{5,1},{9,13},{13,9},{2,6},{6,2},{1... | collective-permute-start | bytes 393224 | tf_op jit(solution)/shard_map/ppermute | solution.py:374
  24.4 6.5 %collective-permute-start.3 = (bf16[8,64,128]{2,1,0:T(8,128)(2,1)}, bf16[8,64,128]{2,1,0:T(8,128)(2,1)S(1)}, u32[]{:S(2)}, u32[]{:S(2)}) collective-permute-start(bf16[8,64,128]{2,1,0:T(8,128)(2,1)} %get-tuple-element.29), channel_id=1, source_target_pairs={{4,8},{8,4},{5,9},{9,5},{6,10},{10,6},{7,11},{11,7},{20,24},{24,20... | collective-permute-start | bytes 393224 | tf_op jit(solution)/shard_map/ppermute | solution.py:373
  30.4 9.7 %copy-start.5 = (bf16[25,64,128]{2,1,0:T(8,128)(2,1)S(1)}, bf16[25,64,128]{2,1,0:T(8,128)(2,1)}, u32[]{:S(2)}) copy-start(bf16[25,64,128]{2,1,0:T(8,128)(2,1)} %copy-done.4) | copy-start | bytes 1228804
  30.4 15.4 %copy-start.3 = (bf16[384,16,128]{2,1,0:T(8,128)(2,1)S(1)}, bf16[384,16,128]{2,1,0:T(8,128)(2,1)}, u32[]{:S(2)}) copy-start(bf16[384,16,128]{2,1,0:T(8,128)(2,1)} %p_hbm.3) | copy-start | bytes 4718596
  33.8 6.3 %collective-permute-start.6 = (bf16[8,64,128]{2,1,0:T(8,128)(2,1)S(1)}, bf16[8,64,128]{2,1,0:T(8,128)(2,1)S(1)}, u32[]{:S(2)}, u32[]{:S(2)}) collective-permute-start(bf16[8,64,128]{2,1,0:T(8,128)(2,1)S(1)} %get-tuple-element.32), channel_id=1, source_target_pairs={{4,8},{8,4},{5,9},{9,5},{6,10},{10,6},{7,11},{11,7},{20,24},{24,20... | collective-permute-start | bytes 393224 | tf_op jit(solution)/shard_map/ppermute | solution.py:389
  37.3 3.0 %collective-permute-start.5 = (bf16[8,64,128]{2,1,0:T(8,128)(2,1)S(1)}, bf16[8,64,128]{2,1,0:T(8,128)(2,1)S(1)}, u32[]{:S(2)}, u32[]{:S(2)}) collective-permute-start(bf16[8,64,128]{2,1,0:T(8,128)(2,1)S(1)} %get-tuple-element.32), channel_id=1, source_target_pairs={{0,4},{4,0},{8,12},{12,8},{1,5},{5,1},{9,13},{13,9},{2,6},{6,2},{1... | collective-permute-start | bytes 393224 | tf_op jit(solution)/shard_map/ppermute | solution.py:390
  40.1 14.9 %collective-permute-start.9 = (bf16[25,64,128]{2,1,0:T(8,128)(2,1)S(1)}, bf16[25,64,128]{2,1,0:T(8,128)(2,1)S(1)}, u32[]{:S(2)}, u32[]{:S(2)}) collective-permute-start(bf16[25,64,128]{2,1,0:T(8,128)(2,1)S(1)} %copy-done.5), channel_id=1, source_target_pairs={{0,3},{1,2},{2,1},{3,0},{4,7},{5,6},{6,5},{7,4},{8,11},{9,10},{10,... | collective-permute-start | bytes 1228808 | tf_op jit(solution)/shard_map/ppermute | solution.py:326
  40.3 20.4 %collective-permute-start.1 = (bf16[64,64,128]{2,1,0:T(8,128)(2,1)S(1)}, bf16[64,64,128]{2,1,0:T(8,128)(2,1)S(1)}, u32[]{:S(2)}, u32[]{:S(2)}) collective-permute-start(bf16[64,64,128]{2,1,0:T(8,128)(2,1)S(1)} %get-tuple-element.26), channel_id=1, source_target_pairs={{4,8},{8,4},{5,9},{9,5},{6,10},{10,6},{7,11},{11,7},{20,24},{24,20... | collective-permute-start | bytes 3145736 | tf_op jit(solution)/shard_map/ppermute | solution.py:355
  43.8 24.1 %collective-permute-start.4 = (bf16[64,64,128]{2,1,0:T(8,128)(2,1)}, bf16[64,64,128]{2,1,0:T(8,128)(2,1)S(1)}, u32[]{:S(2)}, u32[]{:S(2)}) collective-permute-start(bf16[64,64,128]{2,1,0:T(8,128)(2,1)} %get-tuple-element.31), channel_id=1, source_target_pairs={{4,8},{8,4},{5,9},{9,5},{6,10},{10,6},{7,11},{11,7},{20,24},{24,20... | collective-permute-start | bytes 3145736 | tf_op jit(solution)/shard_map/ppermute | solution.py:391
  54.9 5.6 %copy-start.9 = (f32[127,128]{1,0:T(8,128)S(1)}, f32[127,128]{1,0:T(8,128)}, u32[]{:S(2)}) copy-start(f32[127,128]{1,0:T(8,128)} %get-tuple-element.50) | copy-start | bytes 195076
  54.9 16.2 %copy-start.6 = (f32[1,128,128]{2,1,0:T(8,128)S(1)}, f32[1,128,128]{2,1,0:T(8,128)}, u32[]{:S(2)}) copy-start(f32[1,128,128]{2,1,0:T(8,128)} %param.8) | copy-start | bytes 196612
  56.8 28.3 %collective-permute-start.16 = (bf16[12,256,128]{2,1,0:T(8,128)(2,1)S(1)}, bf16[12,256,128]{2,1,0:T(8,128)(2,1)S(1)}, u32[]{:S(2)}, u32[]{:S(2)}) collective-permute-start(bf16[12,256,128]{2,1,0:T(8,128)(2,1)S(1)} %get-tuple-element.44), channel_id=1, source_target_pairs={{4,8},{8,4},{5,9},{9,5},{6,10},{10,6},{7,11},{11,7},{20,24},{24,20... | collective-permute-start | bytes 2359304 | tf_op jit(solution)/shard_map/ppermute | solution.py:424
  60.5 24.6 %collective-permute-start.15 = (bf16[12,256,128]{2,1,0:T(8,128)(2,1)S(1)}, bf16[12,256,128]{2,1,0:T(8,128)(2,1)S(1)}, u32[]{:S(2)}, u32[]{:S(2)}) collective-permute-start(bf16[12,256,128]{2,1,0:T(8,128)(2,1)S(1)} %get-tuple-element.44), channel_id=1, source_target_pairs={{0,4},{4,0},{8,12},{12,8},{1,5},{5,1},{9,13},{13,9},{2,6},{6,2},{1... | collective-permute-start | bytes 2359304 | tf_op jit(solution)/shard_map/ppermute | solution.py:425
  60.6 17.7 %collective-permute-start.10 = (bf16[10,64,128]{2,1,0:T(8,128)(2,1)S(1)}, bf16[10,64,128]{2,1,0:T(8,128)(2,1)S(1)}, u32[]{:S(2)}, u32[]{:S(2)}) collective-permute-start(bf16[10,64,128]{2,1,0:T(8,128)(2,1)S(1)} %get-tuple-element.39), channel_id=1, source_target_pairs={{0,1},{1,0},{2,3},{3,2},{4,5},{5,4},{6,7},{7,6},{8,9},{9,8},{10,11... | collective-permute-start | bytes 491528 | tf_op jit(solution)/shard_map/ppermute | solution.py:326
  67.9 11.3 %collective-permute-start.11 = (bf16[10,64,128]{2,1,0:T(8,128)(2,1)S(1)}, bf16[10,64,128]{2,1,0:T(8,128)(2,1)S(1)}, u32[]{:S(2)}, u32[]{:S(2)}) collective-permute-start(bf16[10,64,128]{2,1,0:T(8,128)(2,1)S(1)} %get-tuple-element.40), channel_id=1, source_target_pairs={{0,2},{1,3},{2,0},{3,1},{4,6},{5,7},{6,4},{7,5},{8,10},{9,11},{10,... | collective-permute-start | bytes 491528 | tf_op jit(solution)/shard_map/ppermute | solution.py:326
  69.1 10.1 %collective-permute-start.12 = (bf16[10,64,128]{2,1,0:T(8,128)(2,1)S(1)}, bf16[10,64,128]{2,1,0:T(8,128)(2,1)S(1)}, u32[]{:S(2)}, u32[]{:S(2)}) collective-permute-start(bf16[10,64,128]{2,1,0:T(8,128)(2,1)S(1)} %get-tuple-element.41), channel_id=1, source_target_pairs={{0,3},{1,2},{2,1},{3,0},{4,7},{5,6},{6,5},{7,4},{8,11},{9,10},{10,... | collective-permute-start | bytes 491528 | tf_op jit(solution)/shard_map/ppermute | solution.py:326
  81.7 7.7 %collective-permute-start.14 = (bf16[4,256,128]{2,1,0:T(8,128)(2,1)S(1)}, bf16[4,256,128]{2,1,0:T(8,128)(2,1)S(1)}, u32[]{:S(2)}, u32[]{:S(2)}) collective-permute-start(bf16[4,256,128]{2,1,0:T(8,128)(2,1)S(1)} %get-tuple-element.43), channel_id=1, source_target_pairs={{4,8},{8,4},{5,9},{9,5},{6,10},{10,6},{7,11},{11,7},{20,24},{24,20... | collective-permute-start | bytes 786440 | tf_op jit(solution)/shard_map/ppermute | solution.py:466
  85.0 4.4 %collective-permute-start.13 = (bf16[4,256,128]{2,1,0:T(8,128)(2,1)S(1)}, bf16[4,256,128]{2,1,0:T(8,128)(2,1)S(1)}, u32[]{:S(2)}, u32[]{:S(2)}) collective-permute-start(bf16[4,256,128]{2,1,0:T(8,128)(2,1)S(1)} %get-tuple-element.43), channel_id=1, source_target_pairs={{0,4},{4,0},{8,12},{12,8},{1,5},{5,1},{9,13},{13,9},{2,6},{6,2},{1... | collective-permute-start | bytes 786440 | tf_op jit(solution)/shard_map/ppermute | solution.py:467
  (7 other events, 12.8 us)

commit v4 on v3

--- a/solution.py
+++ b/solution.py
@@ -2,6 +2,7 @@
 
 import jax
 import jax.numpy as jnp
+import numpy as np
 from jax import lax
 from jax.experimental import pallas as pl
 from jax.experimental.pallas import tpu as pltpu
@@ -11,26 +12,35 @@
 BF16 = jnp.bfloat16
 LANES = 128
 ROWS = 16
-VMEM_BYTES = 32 * 1024 * 1024
+VMEM_BYTES = 50 * 1024 * 1024
 NT = (((1,), (1,)), ((), ()))
 WHOLE = pl.BlockSpec(memory_space=pltpu.VMEM)
+NEAR = pl.BlockSpec(memory_space=pltpu.VMEM)
 SCALARS = pl.BlockSpec(memory_space=pltpu.SMEM)
 FAR = pl.BlockSpec(memory_space=pltpu.HBM)
 UNREAD = pl.BlockSpec(memory_space=pl.ANY)
 copies = pltpu.SemaphoreType.DMA
 
 
-def call(kernel, grid, in_specs, out_specs, outs, scratch, args, micros, aliases=None):
+def call(kernel, grid, in_specs, out_specs, outs, scratch, args, aliases=None):
+    def place(spec):
+        return pltpu.VMEM if spec is NEAR else None
+
+    args = [
+        pltpu.with_memory_space_constraint(arg, place(spec)) if place(spec) else arg
+        for spec, arg in zip(in_specs, args)
+    ]
+    shapes = [(place(spec) or jax.ShapeDtypeStruct)(shape, kind) for spec, (shape, kind) in zip(out_specs, outs)]
     return pl.pallas_call(
         kernel,
         grid=grid,
-        out_shape=[jax.ShapeDtypeStruct(shape, kind) for shape, kind in outs],
+        out_shape=shapes,
         in_specs=in_specs,
         out_specs=out_specs,
         scratch_shapes=scratch,
         input_output_aliases=aliases or {},
         compiler_params=pltpu.CompilerParams(vmem_limit_bytes=VMEM_BYTES),
-        cost_estimate=pl.CostEstimate(flops=int(micros * 1.1e9), bytes_accessed=1 << 20, transcendentals=0),
+        cost_estimate=pl.CostEstimate(flops=1 << 20, bytes_accessed=1 << 10, transcendentals=0),
     )(*args)
 
 
@@ -39,39 +49,35 @@
     return copy
 
 
-def pack_kernel(bands, first, ids_ref, x_hbm, xt, xt_hbm, *refs):
-    halves, pieces, (x, in_sems, out_sems) = refs[:2], refs[2 : 1 + bands], refs[1 + bands :]
+def pack_kernel(first, x_hbm, xt, xt_hbm, early_half, late_half, message, x, in_sems, out_sems):
     states, lines, _ = x.shape
+    bands = in_sems.shape[0]
     share = lines // bands
-    band = ids_ref[1]
-    chunks = in_sems.shape[0]
-    size = lines // chunks
-    loads = []
-    for c in range(chunks):
-        where = (slice(None), pl.ds(c * size, size), slice(None))
+    count = share - first
+    loads, sends = [], []
+    for c in range(bands):
+        where = (slice(None), pl.ds(c * share, share), slice(None))
         loads.append(start(pltpu.make_async_copy(x_hbm.at[where], x.at[where], in_sems.at[c])))
 
-    for c in range(chunks):
+    def send(line, number, target, at):
+        copy = pltpu.make_async_copy(
+            xt.at[pl.ds(line, number)], target.at[pl.ds(at, number)], out_sems.at[len(sends)]
+        )
+        sends.append(start(copy))
+
+    for c in range(bands):
         loads[c].wait()
-        for y0 in range(c * size, (c + 1) * size, ROWS):
+        for y0 in range(c * share, (c + 1) * share, ROWS):
             for s0 in range(0, states, ROWS):
                 block = x[s0 : s0 + ROWS, y0 : y0 + ROWS, :].astype(F32)
                 turned = jnp.swapaxes(block, 0, 1).astype(BF16)
                 xt[y0 : y0 + ROWS, s0 : s0 + ROWS, :] = turned
-
-    sends = []
-
-    def send(source, target):
-        sends.append(start(pltpu.make_async_copy(source, target, out_sems.at[len(sends)])))
-
-    for k in range(1, bands):
-        begin = (band ^ k) * share
-        count = share - first
-        send(xt.at[pl.ds(begin + first, count)], pieces[k - 1].at[pl.ds(0, count)])
-        send(xt.at[pl.ds(lax.rem(begin + share, lines), 1)], pieces[k - 1].at[pl.ds(count, 1)])
-    send(xt.at[pl.ds(0, lines // 2)], halves[0])
-    send(xt.at[pl.ds(lines // 2, lines // 2)], halves[1])
-    send(xt, xt_hbm)
+        send(c * share + first, count, message, c * (count + 1))
+        send(c * share, 1, message, (c + bands - 1) % bands * (count + 1) + count)
+        if c == bands // 2 - 1:
+            send(0, lines // 2, early_half, 0)
+    send(lines // 2, lines // 2, late_half, 0)
+    send(0, lines, xt_hbm, 0)
     for copy in sends:
         copy.wait()
 
@@ -192,9 +198,10 @@
     lax.fori_loop(0, slots // unroll, body, 0)
 
 
-def stencil_kernel(xt_ref, core_ref, early_ref, late_ref, added_ref, pot_ref, ring_ref, unread, out_ref):
+def stencil_kernel(xt_ref, core_ref, early_ref, late_ref, added_ref, pot_ref, ring_ref, unread, out_ref, done_ref):
     states, here, _ = out_ref.shape
     lines = xt_ref.shape[0]
+    done_ref[...] = jnp.zeros_like(done_ref)
     step = pl.program_id(0)
     y0 = step * here
     early = step < pl.num_programs(0) // 2
@@ -215,42 +222,49 @@
         out_ref[rows, :, :] = jnp.swapaxes(jnp.stack(results, axis=0), 0, 1).astype(BF16)
 
 
-def gather_kernel(bands, first, share, ids_ref, xt_ref, shares_ref, after_hbm, unread, *refs):
-    pieces, outs = refs[: bands - 1], refs[bands - 1 :]
-    later = after_hbm is None
-    all_ref, pass_hbm = outs[:2]
-    projs_ref = None if later else outs[2]
-    sems, pass_sem = outs[-2:]
-    lines, states, _ = xt_ref.shape
+def pass_half(ids_ref, all_ref, pass_hbm, sem):
+    half = pass_hbm.shape[0]
+    copy = start(pltpu.make_async_copy(all_ref.at[pl.ds((1 - (ids_ref[0] & 1)) * half, half)], pass_hbm, sem))
+    copy.wait()
+
+
+def later_kernel(bands, ids_ref, landed, unread, all_ref, pass_hbm, sems, pass_sem):
+    count, states = all_ref.shape[0], landed.shape[1]
+    loads = [
+        start(
+            pltpu.make_async_copy(
+                landed.at[pl.ds(b * count, count)], all_ref.at[:, pl.ds(b * states, states), :], sems.at[b]
+            )
+        )
+        for b in range(bands)
+    ]
+    for copy in loads:
+        copy.wait()
+    pass_half(ids_ref, all_ref, pass_hbm, pass_sem)
+
+
+def early_kernel(bands, share, ids_ref, xt_ref, whole_ref, after_ref, unread, *refs):
+    pieces, (all_ref, pass_hbm, projs_ref, sems, pass_sem) = refs[: bands - 1], refs[bands - 1 :]
+    states = xt_ref.shape[1]
     band = ids_ref[1]
-    begin = band * share + first
-    count = all_ref.shape[0] - 1
+    count, held = all_ref.shape[0] - 1, projs_ref.shape[0]
     loads = []
 
     def load(source, target):
         loads.append(start(pltpu.make_async_copy(source, target, sems.at[len(loads)])))
 
-    def at(k):
-        return pl.ds(pl.multiple_of((band ^ k) * states, states), states)
-
-    brought = count + 1 if later else count
-    load(xt_ref.at[pl.ds(begin, count)], all_ref.at[pl.ds(0, count), at(0), :])
-    for k in range(1, bands):
-        load(pieces[k - 1].at[pl.ds(0, brought)], all_ref.at[pl.ds(0, brought), at(k), :])
-    if later:
-        load(xt_ref.at[pl.ds(lax.rem(begin + count, lines), 1)], all_ref.at[pl.ds(count, 1), at(0), :])
-    else:
-        load(after_hbm.at[pl.ds(0, 1)], all_ref.at[pl.ds(count, 1)])
-        held = projs_ref.shape[0]
-        load(shares_ref.at[pl.ds(band * held, held)], projs_ref.at[:, at(0), :])
-        for k in range(1, bands):
-            load(pieces[k - 1].at[pl.ds(count, held)], projs_ref.at[:, at(k), :])
+    for k in range(bands):
+        at = pl.ds(pl.multiple_of((band ^ k) * states, states), states)
+        if k == 0:
+            load(xt_ref.at[pl.ds(band * share, count)], all_ref.at[pl.ds(0, count), at, :])
+            load(whole_ref.at[pl.ds(band * held, held)], projs_ref.at[:, at, :])
+        else:
+            load(pieces[k - 1].at[pl.ds(0, count)], all_ref.at[pl.ds(0, count), at, :])
+            load(pieces[k - 1].at[pl.ds(count, held)], projs_ref.at[:, at, :])
+    load(after_ref.at[pl.ds(0, 1)], all_ref.at[pl.ds(count, 1)])
     for copy in loads:
         copy.wait()
-    half = count // 2
-    passed = pltpu.make_async_copy(all_ref.at[pl.ds((1 - (ids_ref[0] & 1)) * half, half)], pass_hbm, pass_sem)
-    passed.start()
-    passed.wait()
+    pass_half(ids_ref, all_ref, pass_hbm, pass_sem)
 
 
 def add_products(row, ids_ref, all_ref, core_ref, link_ref, pot_ref, acc):
@@ -281,8 +295,9 @@
 
 
 def final_kernel(
-    bands, domains, share, ids_ref, all_ref, core_ref, link_ref, pot_ref, begun_ref, proj_ref, energy_ref, out_ref, acc
+    bands, share, ids_ref, all_ref, core_ref, link_ref, pot_ref, begun_ref, proj_ref, energy_ref, *refs
 ):
+    out_refs, (acc, blocks) = refs[:-2], refs[-2:]
     acc[...] = begun_ref[...]
     add_products(ids_ref[1] * share, ids_ref, all_ref, core_ref, link_ref, pot_ref, acc)
     groups = proj_ref.shape[0]
@@ -291,14 +306,38 @@
         here = proj_ref[g]
         scaled = (here.astype(F32) * energy_ref[pl.ds(first + g, 1), :]).astype(BF16)
         acc[1] += lax.dot_general(scaled, here, NT, preferred_element_type=F32)
-    gram = acc[0]
     hamil = 0.5 * (acc[1] + acc[1].T)
-    rows, cols = gram.shape[0] // bands, gram.shape[0] // domains
-    for c in range(domains):
-        for r in range(bands):
-            r0, c0 = r * rows, c * cols
-            out_ref[c * bands + r, :, :cols] = gram[r0 : r0 + rows, c0 : c0 + cols].astype(BF16)
-            out_ref[c * bands + r, :, cols:] = hamil[r0 : r0 + rows, c0 : c0 + cols].astype(BF16)
+    cols = blocks.shape[2] // 2
+    for c in range(blocks.shape[0]):
+        blocks[c, :, :cols] = acc[0, :, c * cols : (c + 1) * cols].astype(BF16)
+        blocks[c, :, cols:] = hamil[:, c * cols : (c + 1) * cols].astype(BF16)
+    for k, out_ref in enumerate(out_refs):
+        out_ref[...] = blocks[ids_ref[0] ^ k]
+
+
+def load_all(sources, slots, sems):
+    copies_in = [start(pltpu.make_async_copy(far, slots.at[i], sems.at[i])) for i, far in enumerate(sources)]
+    for copy in copies_in:
+        copy.wait()
+
+
+def rows_kernel(domains, ids_ref, own_ref, *refs):
+    landed, (own_out, *outs, slots, total, sems) = refs[: domains - 1], refs[domains - 1 :]
+    load_all(landed, slots, sems)
+    rows = own_out.shape[0]
+    total[...] = own_ref[...].astype(F32) + jnp.sum(slots[...].astype(F32), axis=0)
+    for k, out_ref in enumerate((own_out, *outs)):
+        begin = pl.multiple_of((ids_ref[1] ^ k) * rows, rows)
+        out_ref[...] = total[pl.ds(begin, rows), :].astype(out_ref.dtype)
+
+
+def result_kernel(bands, scale, own_ref, *refs):
+    landed, (out_ref, slots, sems) = refs[: bands - 1], refs[bands - 1 :]
+    load_all(landed, slots, sems)
+    total = (own_ref[...] + jnp.sum(slots[...].astype(F32), axis=0)) * scale
+    cols = out_ref.shape[2]
+    out_ref[0] = total[:, :cols]
+    out_ref[1] = total[:, cols:]
 
 
 def local(orbitals, potential, projectors, tile_atom, tile_line, tile_count, energies):
@@ -312,19 +351,17 @@
     per_group = LANES // proj_count
     groups = atoms_here // per_group
     group_share = groups // bands
-    parts = domains * bands
     share = lines // bands
     first = share // 4
     rest = share - first
 
     core_pairs = [(i, i ^ 1) for i in range(domains) if i ^ 1 < domains]
     link_pairs = [(i, ((i + 1) ^ 1) - 1) for i in range(1, domains) if ((i + 1) ^ 1) - 1 < domains]
-    band_pairs = [[(i, i ^ k) for i in range(bands)] for k in range(bands)]
-    far_first = sorted(range(1, bands), key=lambda k: -k)
-
-    def swapped(values):
-        got = {k: lax.ppermute(values[k - 1], "band", band_pairs[k]) for k in far_first}
-        return [got[k] for k in range(1, bands)]
+
+    def swapped(values, axis):
+        size = lax.axis_size(axis)
+        got = {k: lax.ppermute(values[k - 1], axis, [(i, i ^ k) for i in range(size)]) for k in range(size - 1, 0, -1)}
+        return [got[k] for k in range(1, size)]
 
     ids = jnp.stack([domain, band]).astype(jnp.int32)
     near = jnp.clip(tile_atom - (domain - 1) * atoms_here, 0, 3 * atoms_here - 1)
@@ -334,24 +371,26 @@
     field = orbitals.reshape(states, lines, cols_z)
     pot = potential.reshape(lines, cols_z)
     energy = energies.reshape(atom_total // per_group, LANES)
-    eye = jnp.eye(cols_z, dtype=F32)
-    ring = (3.0 * eye - 0.5 * (jnp.roll(eye, 1, axis=0) + jnp.roll(eye, -1, axis=0))).astype(BF16)
-
-    chunks = 4
+    eye = np.eye(cols_z, dtype=np.float32)
+    ring = jnp.asarray(3.0 * eye - 0.5 * (np.roll(eye, 1, axis=0) + np.roll(eye, -1, axis=0)), dtype=BF16)
+
     line_shape, half_shape = (lines, states, cols_z), (lines // 2, states, cols_z)
-    packed = call(
-        functools.partial(pack_kernel, bands, first),
-        (),
-        [SCALARS, FAR],
-        [WHOLE] + [FAR] * (2 + bands),
-        [(line_shape, BF16), (line_shape, BF16), (half_shape, BF16), (half_shape, BF16)]
-        + [((rest + 1, states, cols_z), BF16)] * (bands - 1),
-        [pltpu.VMEM((states, lines, cols_z), BF16), copies((chunks,)), copies((2 * bands + 1,))],
-        (ids, field),
-        3,
-    )
-    xt, xt_far, early_half, late_half = packed[:4]
-    later = swapped(packed[4:])
+    xt, xt_far, early_half, late_half, message = call(
+        functools.partial(pack_kernel, first),
+        (),
+        [FAR],
+        [NEAR, FAR, FAR, FAR, FAR],
+        [
+            (line_shape, BF16),
+            (line_shape, BF16),
+            (half_shape, BF16),
+            (half_shape, BF16),
+            ((bands * (rest + 1), states, cols_z), BF16),
+        ],
+        [pltpu.VMEM((states, lines, cols_z), BF16), copies((bands,)), copies((2 * bands + 3,))],
+        (field,),
+    )
+    landed = lax.all_to_all(message, "band", split_axis=0, concat_axis=0, tiled=True)
     link_early = lax.ppermute(early_half, "domain", link_pairs)
     core_field = lax.ppermute(xt_far, "domain", core_pairs)
 
@@ -359,8 +398,8 @@
     to_core, own, to_link = call(
         project_kernel,
         (),
-        [SCALARS, SCALARS, WHOLE, FAR],
-        [WHOLE] * 3,
+        [SCALARS, SCALARS, NEAR, FAR],
+        [WHOLE, NEAR, WHOLE],
         [(group_shape, BF16), (group_shape, F32), (group_shape, BF16)],
         [
             pltpu.VMEM((3 * atoms_here + 1, proj_count, states), F32),
@@ -368,34 +407,31 @@
             copies((4,)),
         ],
         (project_words, ids, xt, projectors),
-        8,
     )
     from_link = lax.ppermute(to_link, "domain", link_pairs)
     from_core = lax.ppermute(to_core, "domain", core_pairs)
-    owned = call(
+    late_half, scaled, scaled_far, whole, *messages = call(
         functools.partial(owner_kernel, bands, first),
         (),
-        [SCALARS, WHOLE, WHOLE, FAR, FAR, WHOLE, FAR],
-        [FAR, WHOLE, FAR, WHOLE] + [FAR] * (bands - 1),
+        [SCALARS, NEAR, NEAR, FAR, FAR, WHOLE, FAR],
+        [FAR, NEAR, FAR, NEAR] + [FAR] * (bands - 1),
         [(half_shape, BF16)]
         + [(group_shape, BF16)] * 3
         + [((first + group_share, states, cols_z), BF16)] * (bands - 1),
         [pltpu.VMEM(group_shape, BF16), pltpu.VMEM(group_shape, BF16), copies((2,)), copies((2 * bands - 1,))],
         (ids, xt, own, from_core, from_link, energy, late_half),
-        1,
         aliases={6: 0},
     )
-    late_half, scaled, scaled_far, whole = owned[:4]
     link_scaled = lax.ppermute(scaled_far, "domain", link_pairs)
     core_scaled = lax.ppermute(scaled_far, "domain", core_pairs)
     link_late = lax.ppermute(late_half, "domain", link_pairs)
-    early = swapped(owned[4:])
+    early = swapped(messages, "band")
 
     (added,) = call(
         nonlocal_kernel,
         (),
-        [SCALARS, SCALARS, FAR, FAR, WHOLE, FAR],
-        [WHOLE],
+        [SCALARS, SCALARS, FAR, FAR, NEAR, FAR],
+        [NEAR],
         [((lines + 1, states, cols_z), F32)],
         [
             pltpu.VMEM((3 * atoms_here, states, proj_count), BF16),
@@ -405,91 +441,94 @@
             copies((3,)),
         ],
         (nonlocal_words, ids, projectors, core_scaled, scaled, link_scaled),
-        9,
-    )
-
-    def later_kernel(ids_ref, xt_ref, unread, *refs):
-        gather_kernel(bands, first, share, ids_ref, xt_ref, None, None, unread, *refs)
+    )
 
     later_all, later_pass = call(
-        later_kernel,
-        (),
-        [SCALARS, WHOLE, UNREAD] + [FAR] * (bands - 1),
-        [WHOLE, FAR],
+        functools.partial(later_kernel, bands),
+        (),
+        [SCALARS, FAR, NEAR],
+        [NEAR, FAR],
         [((rest + 1, total_states, cols_z), BF16), ((rest // 2, total_states, cols_z), BF16)],
-        [copies((bands + 1,)), copies],
-        (ids, xt, added, *later),
-        2,
+        [copies((bands,)), copies],
+        (ids, landed, added),
     )
     later_link = lax.ppermute(later_pass, "domain", link_pairs)
     later_core = lax.ppermute(later_pass, "domain", core_pairs)
 
     steps = lines // ROWS
     block = pl.BlockSpec((ROWS, states, cols_z), lambda i: (i, 0, 0))
-    (applied,) = call(
+    applied, done = call(
         stencil_kernel,
         (steps,),
         [
-            WHOLE,
+            NEAR,
             block,
             pl.BlockSpec((ROWS, states, cols_z), lambda i: (jnp.minimum(i, steps // 2 - 1), 0, 0)),
             pl.BlockSpec((ROWS, states, cols_z), lambda i: (jnp.maximum(i - steps // 2, 0), 0, 0)),
-            WHOLE,
+            NEAR,
             pl.BlockSpec((ROWS, cols_z), lambda i: (i, 0)),
             WHOLE,
-            UNREAD,
+            NEAR,
         ],
-        [pl.BlockSpec((states, ROWS, cols_z), lambda i: (0, i, 0))],
-        [((states, lines, cols_z), BF16)],
+        [pl.BlockSpec((states, ROWS, cols_z), lambda i: (0, i, 0)), WHOLE],
+        [((states, lines, cols_z), BF16), ((8, LANES), F32)],
         [],
         (xt, core_field, link_early, link_late, added, pot, ring, later_all),
-        6,
-    )
-
-    def early_kernel(ids_ref, xt_ref, shares_ref, after_ref, unread, *refs):
-        gather_kernel(bands, 0, share, ids_ref, xt_ref, shares_ref, after_ref, unread, *refs)
+    )
 
     early_all, early_pass, projs = call(
-        early_kernel,
-        (),
-        [SCALARS, WHOLE, WHOLE, WHOLE, UNREAD] + [FAR] * (bands - 1),
-        [WHOLE, FAR, WHOLE],
+        functools.partial(early_kernel, bands, share),
+        (),
+        [SCALARS, NEAR, NEAR, NEAR, WHOLE] + [FAR] * (bands - 1),
+        [NEAR, FAR, NEAR],
         [
             ((first + 1, total_states, cols_z), BF16),
             ((first // 2, total_states, cols_z), BF16),
             ((group_share, total_states, LANES), BF16),
         ],
         [copies((2 * bands + 1,)), copies],
-        (ids, xt, whole, later_all, applied, *early),
-        1,
+        (ids, xt, whole, later_all, done, *early),
     )
     early_link = lax.ppermute(early_pass, "domain", link_pairs)
     early_core = lax.ppermute(early_pass, "domain", core_pairs)
     (begun,) = call(
         functools.partial(gram_kernel, first, share),
         (),
-        [SCALARS, WHOLE, WHOLE, WHOLE, WHOLE, UNREAD],
-        [WHOLE],
+        [SCALARS, NEAR, WHOLE, WHOLE, WHOLE, NEAR],
+        [NEAR],
         [((2, total_states, total_states), F32)],
         [],
         (ids, later_all, later_core, later_link, pot, early_all),
-        2,
-    )
-    (blocks,) = call(
-        functools.partial(final_kernel, bands, domains, share),
-        (),
-        [SCALARS] + [WHOLE] * 7,
+    )
+    columns = (total_states, 2 * total_states // domains)
+    own_columns, *far_columns = call(
+        functools.partial(final_kernel, bands, share),
+        (),
+        [SCALARS, NEAR, WHOLE, WHOLE, WHOLE, NEAR, NEAR, WHOLE],
+        [NEAR] + [WHOLE] * (domains - 1),
+        [(columns, BF16)] * domains,
+        [pltpu.VMEM((2, total_states, total_states), F32), pltpu.VMEM((domains, *columns), BF16)],
+        (ids, early_all, early_core, early_link, pot, begun, projs, energy),
+    )
+    piece = (states, columns[1])
+    own_rows, *far_rows = call(
+        functools.partial(rows_kernel, domains),
+        (),
+        [SCALARS, NEAR] + [FAR] * (domains - 1),
+        [NEAR] + [WHOLE] * (bands - 1),
+        [(piece, F32)] + [(piece, BF16)] * (bands - 1),
+        [pltpu.VMEM((domains - 1, *columns), BF16), pltpu.VMEM(columns, F32), copies((domains - 1,))],
+        (ids, own_columns, *swapped(far_columns, "domain")),
+    )
+    (subspace,) = call(
+        functools.partial(result_kernel, bands, 1.0 / (lines * cols_z * domains)),
+        (),
+        [NEAR] + [FAR] * (bands - 1),
         [WHOLE],
-        [((parts, states, 2 * total_states // domains), BF16)],
-        [pltpu.VMEM((2, total_states, total_states), F32)],
-        (ids, early_all, early_core, early_link, pot, begun, projs, energy),
-        2,
-    )
-    summed = lax.all_to_all(blocks, ("domain", "band"), split_axis=0, concat_axis=0, tiled=True)
-    scale = 1.0 / (lines * cols_z * domains)
-    result = jnp.sum(summed.astype(F32), axis=0) * scale
-    cols = total_states // domains
-    subspace = jnp.stack([result[:, :cols], result[:, cols:]])
+        [((2, states, total_states // domains), F32)],
+        [pltpu.VMEM((bands - 1, *piece), BF16), copies((bands - 1,))],
+        (own_rows, *swapped(far_rows, "band")),
+    )
     return applied.reshape(orbitals.shape), subspace
 
 

time: 107 us -> 122 us (1.14); the launches traced: 106 us -> 119 us
  waiting for transfers between devices: 12 us -> 30.4 us
  blocking collectives: 13.9 us -> 0 us
  starting transfers between devices: 30.6 us -> 37.2 us
  Pallas kernels: 36.9 us -> 41.8 us
  local copies, waits for them, and re-layouts: 9.67 us -> 7.61 us
    ppermute x1, waiting for transfers between devices: 2.73 us -> 18.3 us  [local(): link_scaled = lax.ppermute(scaled_far, 'domain', link_pairs)]
    all_to_all x1 -> x0, blocking collectives: 13.9 us -> none  [local(): lax.all_to_all(blocks, ('domain', 'band'), split_axis=0, concat_axis=0, t...]
    ppermute x6 -> x9, waiting for transfers between devices: 0.82 us -> 10.2 us  [swapped(): lax.ppermute(values[k - 1], axis, [(i, i ^ k) for i in range(size)])]
    all_to_all x0 -> x1, starting transfers between devices: none -> 5.55 us  [local(): lax.all_to_all(message, 'band', split_axis=0, concat_axis=0, tiled=True)]
    ppermute x1, waiting for transfers between devices: 5.4 us -> 0.01 us  [local(): link_late = lax.ppermute(late_half, 'domain', link_pairs)]
    pallas_call x9 -> x11, Pallas kernels: 36.9 us -> 41.8 us  [call(): pl.pallas_call(kernel, grid=grid, out_shape=shapes, in_specs=in_specs, ou...]
    ppermute x1, starting transfers between devices: 3.27 us -> 5.61 us  [local(): early_link = lax.ppermute(early_pass, 'domain', link_pairs)]
    ppermute x6 -> x9, starting transfers between devices: 9.67 us -> 11.3 us  [swapped(): lax.ppermute(values[k - 1], axis, [(i, i ^ k) for i in range(size)])]
  transfers between devices with their start and end apart: 17 -> 21, of which waited for: 5 -> 8; matrix products, arithmetic and copies ran while one was open for 2% -> 1% of each run, Pallas kernels for 30% -> 29%
where the time goes in v4:
time: 122 us; the launch traced here: 119 us
  Pallas kernels  41.8 us (34%)
  starting transfers between devices  37.2 us (30%)
  waiting for transfers between devices  30.4 us (25%)
  local copies, waits for them, and re-layouts  7.61 us (6%)
  between operations  1.56 us (1%)
    pallas_call x11, Pallas kernels, call(): pl.pallas_call(kernel, grid=grid, out_shape=shapes, in_specs=in_specs, ou...  41.8 us
    ppermute x1, waiting for transfers between devices, local(): link_scaled = lax.ppermute(scaled_far, 'domain', link_pairs)  18.3 us
    ppermute x9, starting transfers between devices, swapped(): lax.ppermute(values[k - 1], axis, [(i, i ^ k) for i in range(size)])  11.3 us
    ppermute x9, waiting for transfers between devices, swapped(): lax.ppermute(values[k - 1], axis, [(i, i ^ k) for i in range(size)])  10.2 us
    unnamed x33, local copies, waits for them, and re-layouts  7.51 us
    ppermute x1, starting transfers between devices, local(): early_link = lax.ppermute(early_pass, 'domain', link_pairs)  5.61 us
    all_to_all x1, starting transfers between devices, local(): lax.all_to_all(message, 'band', split_axis=0, concat_axis=0, tiled=True)  5.55 us
    ppermute x1, starting transfers between devices, local(): from_link = lax.ppermute(to_link, 'domain', link_pairs)  3.49 us
  transfers between devices with their start and end apart: 21, of which 8 were waited for; matrix products, arithmetic and copies ran while one was open for 1% of the time, Pallas kernels for 29%

profile of v4, /device:TPU:1, one launch (start us, length us, event | category | flops | bytes accessed | tf_op | source)
XLA Modules:
  0.0 119.2 jit_solution(4271470712424321422)
XLA Ops:
  0.6 4.0 %shard_map.95 = (bf16[128,64,128]{2,1,0:T(8,128)(2,1)S(1)}, bf16[128,64,128]{2,1,0:T(8,128)(2,1)}, bf16[64,64,128]{2,1,0:T(8,128)(2,1)S(1)}, bf16[64,64,128]{2,1,0:T(8,128)(2,1)}, bf16[100,64,128]{2,1,0:T(8,128)(2,1)}) custom-call(bf16[64,128,128]{2,1,0:T(8,128)(2,1)} %bitcast.12), custom_call_target="tpu_custom_call" | custom-call | flops 1048576 | bytes 1024 | tf_op jit(solution)/shard_map/pallas_call | solution.py:34
  5.6 5.6 %all-to-all-start = ((bf16[100,64,128]{2,1,0:T(8,128)(2,1)}), bf16[100,64,128]{2,1,0:T(8,128)(2,1)}, u32[]{:S(2)}, u32[]{:S(2)}) async-start(bf16[100,64,128]{2,1,0:T(8,128)(2,1)} %get-tuple-element.42), calls=%async_computation | async-start | bytes 3276800 | tf_op jit(solution)/shard_map/all_to_all | solution.py:393
  13.4 8.2 %shard_map.96 = (bf16[8,64,128]{2,1,0:T(8,128)(2,1)S(1)}, f32[8,64,128]{2,1,0:T(8,128)S(1)}, bf16[8,64,128]{2,1,0:T(8,128)(2,1)S(1)}) custom-call(s32[384]{0:T(512)S(1)} %get-tuple-element.67.words_ref, s32[2]{0:T(128)S(1)} %pad_add_fusion.ids_ref, bf16[128,64,128]{2,1,0:T(8,128)(2,1)S(1)} %get-tuple-element.32.xt_ref, bf16[384,16,128]{2,1,0:T(8,128)(2,1)} %p_hbm.3), custom_call_target="tpu_custom_call" | custom-call | flops 1048576 | bytes 1024 | tf_op jit(solution)/shard_map/pallas_call | solution.py:34
  21.6 3.5 %collective-permute-start.3 = (bf16[8,64,128]{2,1,0:T(8,128)(2,1)S(1)}, bf16[8,64,128]{2,1,0:T(8,128)(2,1)S(1)}, u32[]{:S(2)}, u32[]{:S(2)}) collective-permute-start(bf16[8,64,128]{2,1,0:T(8,128)(2,1)S(1)} %get-tuple-element.37), channel_id=1, source_target_pairs={{4,8},{8,4},{5,9},{9,5},{6,10},{10,6},{7,11},{11,7},{20,24},{24,20... | collective-permute-start | bytes 393224 | tf_op jit(solution)/shard_map/ppermute | solution.py:411
  25.1 2.1 %collective-permute-start.1 = (bf16[64,64,128]{2,1,0:T(8,128)(2,1)}, bf16[64,64,128]{2,1,0:T(8,128)(2,1)}, u32[]{:S(2)}, u32[]{:S(2)}) collective-permute-start(bf16[64,64,128]{2,1,0:T(8,128)(2,1)} %copy-done.6), channel_id=1, source_target_pairs={{4,8},{8,4},{5,9},{9,5},{6,10},{10,6},{7,11},{11,7},{20,24},{24,20... | collective-permute-start | bytes 3145736 | tf_op jit(solution)/shard_map/ppermute | solution.py:394
  28.3 1.8 %shard_map.97 = (bf16[64,64,128]{2,1,0:T(8,128)(2,1)}, bf16[8,64,128]{2,1,0:T(8,128)(2,1)S(1)}, bf16[8,64,128]{2,1,0:T(8,128)(2,1)S(1)}, bf16[8,64,128]{2,1,0:T(...) custom-call(s32[2]{0:T(128)S(1)} %pad_add_fusion.ids_ref, ...), custom_call_target="tpu_custom_call", output_to_operand_aliasing={{0}: (6, {})} | custom-call | flops 1048576 | bytes 1024 | tf_op jit(solution)/shard_map/pallas_call | solution.py:34
  30.2 3.1 %collective-permute-start.4 = (bf16[64,64,128]{2,1,0:T(8,128)(2,1)}, bf16[64,64,128]{2,1,0:T(8,128)(2,1)}, u32[]{:S(2)}, u32[]{:S(2)}) collective-permute-start(bf16[64,64,128]{2,1,0:T(8,128)(2,1)} %get-tuple-element.39), channel_id=1, source_target_pairs={{4,8},{8,4},{5,9},{9,5},{6,10},{10,6},{7,11},{11,7},{20,24},{24,20... | collective-permute-start | bytes 3145736 | tf_op jit(solution)/shard_map/ppermute | solution.py:427
  33.3 2.5 %collective-permute-start.6 = (bf16[8,64,128]{2,1,0:T(8,128)(2,1)S(1)}, bf16[8,64,128]{2,1,0:T(8,128)(2,1)S(1)}, u32[]{:S(2)}, u32[]{:S(2)}) collective-permute-start(bf16[8,64,128]{2,1,0:T(8,128)(2,1)S(1)} %get-tuple-element.40), channel_id=1, source_target_pairs={{4,8},{8,4},{5,9},{9,5},{6,10},{10,6},{7,11},{11,7},{20,24},{24,20... | collective-permute-start | bytes 393224 | tf_op jit(solution)/shard_map/ppermute | solution.py:425
  35.8 18.3 %collective-permute-done.6.link_hbm = bf16[8,64,128]{2,1,0:T(8,128)(2,1)S(1)} collective-permute-done((bf16[8,64,128]{2,1,0:T(8,128)(2,1)S(1)}, bf16[8,64,128]{2,1,0:T(8,128)(2,1)S(1)}, u32[]{:S(2)}, u32[]{:S(2)}) %collective-permute-start.6) | collective-permute-done | bytes 131104 | tf_op jit(solution)/shard_map/ppermute | solution.py:425
  54.8 8.6 %shard_map.98.unread.added_ref = f32[129,64,128]{2,1,0:T(8,128)S(1)} custom-call(s32[384]{0:T(512)} %get-tuple-element.66.words_ref, s32[2]{0:T(128)} %copy-done.4, bf16[384,16,128]{2,1,0:T(8,128)(2,1)} %p_hbm.3, bf16[8,64,128]{2,1,0:T(8,128)(2,1)} %copy-done.12, bf16[8,64,128]{2,1,0:T(8,128)(2,1)S(1)} %get-tuple-element.41.own_ref, ...), custom_call_target="tpu_custom_call" | custom-call | flops 1048576 | bytes 1024 | tf_op jit(solution)/shard_map/pallas_call | solution.py:34
  63.5 2.0 %copy-done = f32[129,64,128]{2,1,0:T(8,128)} copy-done((f32[129,64,128]{2,1,0:T(8,128)}, f32[129,64,128]{2,1,0:T(8,128)S(1)}, u32[]{:S(2)}) %copy-start) | copy-done | bytes 4227096
  65.4 2.2 %copy-done.1 = f32[129,64,128]{2,1,0:T(8,128)S(1)} copy-done((f32[129,64,128]{2,1,0:T(8,128)S(1)}, f32[129,64,128]{2,1,0:T(8,128)}, u32[]{:S(2)}) %copy-start.1) | copy-done | bytes 4227096
  67.6 3.6 %shard_map.99 = (bf16[25,256,128]{2,1,0:T(8,128)(2,1)S(1)}, bf16[12,256,128]{2,1,0:T(8,128)(2,1)}) custom-call(s32[2]{0:T(128)} %copy-done.4, bf16[100,64,128]{2,1,0:T(8,128)(2,1)} %all-to-all-done.landed, f32[129,64,128]{2,1,0:T(8,128)S(1)} %copy-done.1), custom_call_target="tpu_custom_call" | custom-call | flops 1048576 | bytes 1024 | tf_op jit(solution)/shard_map/pallas_call | solution.py:34
  71.2 2.3 %collective-permute-start.13 = (bf16[12,256,128]{2,1,0:T(8,128)(2,1)}, bf16[12,256,128]{2,1,0:T(8,128)(2,1)S(1)}, u32[]{:S(2)}, u32[]{:S(2)}) collective-permute-start(bf16[12,256,128]{2,1,0:T(8,128)(2,1)} %get-tuple-element.52), channel_id=1, source_target_pairs={{4,8},{8,4},{5,9},{9,5},{6,10},{10,6},{7,11},{11,7},{20,24},{24,20... | collective-permute-start | bytes 2359304 | tf_op jit(solution)/shard_map/ppermute | solution.py:455
  75.4 2.1 %collective-permute-start.8 = (bf16[10,64,128]{2,1,0:T(8,128)(2,1)S(1)}, bf16[10,64,128]{2,1,0:T(8,128)(2,1)S(1)}, u32[]{:S(2)}, u32[]{:S(2)}) collective-permute-start(bf16[10,64,128]{2,1,0:T(8,128)(2,1)S(1)} %get-tuple-element.48), channel_id=1, source_target_pairs={{0,2},{1,3},{2,0},{3,1},{4,6},{5,7},{6,4},{7,5},{8,10},{9,11},{10,... | collective-permute-start | bytes 491528 | tf_op jit(solution)/shard_map/ppermute | solution.py:363
  77.6 7.6 %shard_map.100 = (bf16[64,128,128]{2,1,0:T(8,128)(2,1)}, f32[8,128]{1,0:T(8,128)}) custom-call(bf16[128,64,128]{2,1,0:T(8,128)(2,1)S(1)} %get-tuple-element.32.xt_ref, bf16[128,64,128]{2,1,0:T(8,128)(2,1)} %collective-permute-done.core_ref, bf16[64,64,128]{2,1,0:T(8,128)(2,1)} %collective-permute-done.1.early_ref, ...), custom_call_target="tpu_custom_call" | custom-call | flops 1048576 | bytes 1024 | tf_op jit(solution)/shard_map/pallas_call | solution.py:34
  85.2 3.3 %collective-permute-done.9.refs_2_ = bf16[10,64,128]{2,1,0:T(8,128)(2,1)S(1)} collective-permute-done((bf16[10,64,128]{2,1,0:T(8,128)(2,1)S(1)}, bf16[10,64,128]{2,1,0:T(8,128)(2,1)S(1)}, u32[]{:S(2)}, u32[]{:S(2)}) %collective-permute-start.9) | collective-permute-done | bytes 163872 | tf_op jit(solution)/shard_map/ppermute | solution.py:363
  89.1 2.7 %shard_map.101 = (bf16[9,256,128]{2,1,0:T(8,128)(2,1)S(1)}, bf16[4,256,128]{2,1,0:T(8,128)(2,1)}, bf16[2,256,128]{2,1,0:T(8,128)(2,1)S(1)}) custom-call(s32[2]{0:T(128)} %copy-done.4, bf16[128,64,128]{2,1,0:T(8,128)(2,1)S(1)} %get-tuple-element.32.xt_ref, bf16[8,64,128]{2,1,0:T(8,128)(2,1)S(1)} %get-tuple-element.45.whole_ref, ...), custom_call_target="tpu_custom_call" | custom-call | flops 1048576 | bytes 1024 | tf_op jit(solution)/shard_map/pallas_call | solution.py:34
  91.8 5.6 %collective-permute-start.11 = (bf16[4,256,128]{2,1,0:T(8,128)(2,1)}, bf16[4,256,128]{2,1,0:T(8,128)(2,1)S(1)}, u32[]{:S(2)}, u32[]{:S(2)}) collective-permute-start(bf16[4,256,128]{2,1,0:T(8,128)(2,1)} %get-tuple-element.51), channel_id=1, source_target_pairs={{4,8},{8,4},{5,9},{9,5},{6,10},{10,6},{7,11},{11,7},{20,24},{24,20... | collective-permute-start | bytes 786440 | tf_op jit(solution)/shard_map/ppermute | solution.py:492
  98.4 2.3 %shard_map.102.begun_ref = f32[2,256,256]{2,1,0:T(8,128)S(1)} custom-call(s32[2]{0:T(128)S(1)} %copy-done.5, bf16[25,256,128]{2,1,0:T(8,128)(2,1)S(1)} %get-tuple-element.43.unread.after_ref.all_ref, bf16[12,256,128]{2,1,0:T(8,128)(2,1)S(1)} %collective-permute-done.12.core_ref, bf16[12,256,128]{2,1,0:T(8,128)(2,1)} %copy-done.7, f32[128,128]{1,0:T(8,128)S(1)} %bitcast.10, ...), custom_call_target="tpu_custom_call" | custom-call | flops 1048576 | bytes 1024 | tf_op jit(solution)/shard_map/pallas_call | solution.py:34
  103.2 1.9 %collective-permute-start.15 = (bf16[256,128]{1,0:T(8,128)(2,1)S(1)}, bf16[256,128]{1,0:T(8,128)(2,1)S(1)}, u32[]{:S(2)}, u32[]{:S(2)}) collective-permute-start(bf16[256,128]{1,0:T(8,128)(2,1)S(1)} %get-tuple-element.56), channel_id=1, source_target_pairs={{0,8},{4,12},{8,0},{12,4},{1,9},{5,13},{9,1},{13,5},{2,10},{6,14},... | collective-permute-start | bytes 196616 | tf_op jit(solution)/shard_map/ppermute | solution.py:363
  105.4 1.8 %collective-permute-done.15.refs_1_ = bf16[256,128]{1,0:T(8,128)(2,1)S(1)} collective-permute-done((bf16[256,128]{1,0:T(8,128)(2,1)S(1)}, bf16[256,128]{1,0:T(8,128)(2,1)S(1)}, u32[]{:S(2)}, u32[]{:S(2)}) %collective-permute-start.15) | collective-permute-done | bytes 65568 | tf_op jit(solution)/shard_map/ppermute | solution.py:363
  107.2 1.9 %collective-permute-done.16.refs_2_ = bf16[256,128]{1,0:T(8,128)(2,1)S(1)} collective-permute-done((bf16[256,128]{1,0:T(8,128)(2,1)S(1)}, bf16[256,128]{1,0:T(8,128)(2,1)S(1)}, u32[]{:S(2)}, u32[]{:S(2)}) %collective-permute-start.16) | collective-permute-done | bytes 65568 | tf_op jit(solution)/shard_map/ppermute | solution.py:363
  110.0 3.0 %collective-permute-start.17 = (bf16[64,128]{1,0:T(8,128)(2,1)S(1)}, bf16[64,128]{1,0:T(8,128)(2,1)S(1)}, u32[]{:S(2)}, u32[]{:S(2)}) collective-permute-start(bf16[64,128]{1,0:T(8,128)(2,1)S(1)} %get-tuple-element.59), channel_id=1, source_target_pairs={{0,1},{1,0},{2,3},{3,2},{4,5},{5,4},{6,7},{7,6},{8,9},{9,8},{10,11... | collective-permute-start | bytes 49160 | tf_op jit(solution)/shard_map/ppermute | solution.py:363
  (65 shorter events, 17.9 us)
Async XLA Ops:
  5.6 59.9 %all-to-all-start = ((bf16[100,64,128]{2,1,0:T(8,128)(2,1)}), bf16[100,64,128]{2,1,0:T(8,128)(2,1)}, u32[]{:S(2)}, u32[]{:S(2)}) async-start(bf16[100,64,128]{2,1,0:T(8,128)(2,1)} %get-tuple-element.42), calls=%async_computation | async-start | bytes 3276800 | tf_op jit(solution)/shard_map/all_to_all | solution.py:393
  11.1 16.1 %copy-start.13 = (f32[256,16]{0,1:T(8,128)S(1)}, f32[256,16]{0,1:T(8,128)}, u32[]{:S(2)}) copy-start(f32[256,16]{0,1:T(8,128)} %param.14) | copy-start | bytes 49156
  11.1 66.3 %collective-permute-start = (bf16[128,64,128]{2,1,0:T(8,128)(2,1)}, bf16[128,64,128]{2,1,0:T(8,128)(2,1)}, u32[]{:S(2)}, u32[]{:S(2)}) collective-permute-start(bf16[128,64,128]{2,1,0:T(8,128)(2,1)} %get-tuple-element.33), channel_id=1, source_target_pairs={{0,4},{4,0},{8,12},{12,8},{1,5},{5,1},{9,13},{13,9},{2,6},{6,2},{1... | collective-permute-start | bytes 6291464 | tf_op jit(solution)/shard_map/ppermute | solution.py:395
  12.8 17.4 %copy-start.4 = (s32[2]{0:T(128)}, s32[2]{0:T(128)S(1)}, u32[]{:S(2)}) copy-start(s32[2]{0:T(128)S(1)} %pad_add_fusion.ids_ref) | copy-start | bytes 28
  21.6 5.9 %collective-permute-start.2 = (bf16[8,64,128]{2,1,0:T(8,128)(2,1)S(1)}, bf16[8,64,128]{2,1,0:T(8,128)(2,1)S(1)}, u32[]{:S(2)}, u32[]{:S(2)}) collective-permute-start(bf16[8,64,128]{2,1,0:T(8,128)(2,1)S(1)} %get-tuple-element.36), channel_id=1, source_target_pairs={{0,4},{4,0},{8,12},{12,8},{1,5},{5,1},{9,13},{13,9},{2,6},{6,2},{1... | collective-permute-start | bytes 393224 | tf_op jit(solution)/shard_map/ppermute | solution.py:412
  21.6 6.7 %collective-permute-start.3 = (bf16[8,64,128]{2,1,0:T(8,128)(2,1)S(1)}, bf16[8,64,128]{2,1,0:T(8,128)(2,1)S(1)}, u32[]{:S(2)}, u32[]{:S(2)}) collective-permute-start(bf16[8,64,128]{2,1,0:T(8,128)(2,1)S(1)} %get-tuple-element.37), channel_id=1, source_target_pairs={{4,8},{8,4},{5,9},{9,5},{6,10},{10,6},{7,11},{11,7},{20,24},{24,20... | collective-permute-start | bytes 393224 | tf_op jit(solution)/shard_map/ppermute | solution.py:411
  25.1 48.4 %collective-permute-start.1 = (bf16[64,64,128]{2,1,0:T(8,128)(2,1)}, bf16[64,64,128]{2,1,0:T(8,128)(2,1)}, u32[]{:S(2)}, u32[]{:S(2)}) collective-permute-start(bf16[64,64,128]{2,1,0:T(8,128)(2,1)} %copy-done.6), channel_id=1, source_target_pairs={{4,8},{8,4},{5,9},{9,5},{6,10},{10,6},{7,11},{11,7},{20,24},{24,20... | collective-permute-start | bytes 3145736 | tf_op jit(solution)/shard_map/ppermute | solution.py:394
  30.2 45.2 %collective-permute-start.4 = (bf16[64,64,128]{2,1,0:T(8,128)(2,1)}, bf16[64,64,128]{2,1,0:T(8,128)(2,1)}, u32[]{:S(2)}, u32[]{:S(2)}) collective-permute-start(bf16[64,64,128]{2,1,0:T(8,128)(2,1)} %get-tuple-element.39), channel_id=1, source_target_pairs={{4,8},{8,4},{5,9},{9,5},{6,10},{10,6},{7,11},{11,7},{20,24},{24,20... | collective-permute-start | bytes 3145736 | tf_op jit(solution)/shard_map/ppermute | solution.py:427
  33.3 20.8 %collective-permute-start.6 = (bf16[8,64,128]{2,1,0:T(8,128)(2,1)S(1)}, bf16[8,64,128]{2,1,0:T(8,128)(2,1)S(1)}, u32[]{:S(2)}, u32[]{:S(2)}) collective-permute-start(bf16[8,64,128]{2,1,0:T(8,128)(2,1)S(1)} %get-tuple-element.40), channel_id=1, source_target_pairs={{4,8},{8,4},{5,9},{9,5},{6,10},{10,6},{7,11},{11,7},{20,24},{24,20... | collective-permute-start | bytes 393224 | tf_op jit(solution)/shard_map/ppermute | solution.py:425
  35.8 18.4 %collective-permute-start.5 = (bf16[8,64,128]{2,1,0:T(8,128)(2,1)S(1)}, bf16[8,64,128]{2,1,0:T(8,128)(2,1)S(1)}, u32[]{:S(2)}, u32[]{:S(2)}) collective-permute-start(bf16[8,64,128]{2,1,0:T(8,128)(2,1)S(1)} %get-tuple-element.40), channel_id=1, source_target_pairs={{0,4},{4,0},{8,12},{12,8},{1,5},{5,1},{9,13},{13,9},{2,6},{6,2},{1... | collective-permute-start | bytes 393224 | tf_op jit(solution)/shard_map/ppermute | solution.py:426
  67.6 9.9 %copy-start.2 = (f32[129,64,128]{2,1,0:T(8,128)S(1)}, f32[129,64,128]{2,1,0:T(8,128)}, u32[]{:S(2)}) copy-start(f32[129,64,128]{2,1,0:T(8,128)} %copy-done) | copy-start | bytes 12681220
  71.2 26.3 %collective-permute-start.13 = (bf16[12,256,128]{2,1,0:T(8,128)(2,1)}, bf16[12,256,128]{2,1,0:T(8,128)(2,1)S(1)}, u32[]{:S(2)}, u32[]{:S(2)}) collective-permute-start(bf16[12,256,128]{2,1,0:T(8,128)(2,1)} %get-tuple-element.52), channel_id=1, source_target_pairs={{4,8},{8,4},{5,9},{9,5},{6,10},{10,6},{7,11},{11,7},{20,24},{24,20... | collective-permute-start | bytes 2359304 | tf_op jit(solution)/shard_map/ppermute | solution.py:455
  73.5 24.0 %collective-permute-start.12 = (bf16[12,256,128]{2,1,0:T(8,128)(2,1)}, bf16[12,256,128]{2,1,0:T(8,128)(2,1)S(1)}, u32[]{:S(2)}, u32[]{:S(2)}) collective-permute-start(bf16[12,256,128]{2,1,0:T(8,128)(2,1)} %get-tuple-element.52), channel_id=1, source_target_pairs={{0,4},{4,0},{8,12},{12,8},{1,5},{5,1},{9,13},{13,9},{2,6},{6,2},{1... | collective-permute-start | bytes 2359304 | tf_op jit(solution)/shard_map/ppermute | solution.py:456
  73.6 11.6 %collective-permute-start.7 = (bf16[10,64,128]{2,1,0:T(8,128)(2,1)S(1)}, bf16[10,64,128]{2,1,0:T(8,128)(2,1)S(1)}, u32[]{:S(2)}, u32[]{:S(2)}) collective-permute-start(bf16[10,64,128]{2,1,0:T(8,128)(2,1)S(1)} %get-tuple-element.47), channel_id=1, source_target_pairs={{0,1},{1,0},{2,3},{3,2},{4,5},{5,4},{6,7},{7,6},{8,9},{9,8},{10,11... | collective-permute-start | bytes 491528 | tf_op jit(solution)/shard_map/ppermute | solution.py:363
  75.4 9.8 %collective-permute-start.8 = (bf16[10,64,128]{2,1,0:T(8,128)(2,1)S(1)}, bf16[10,64,128]{2,1,0:T(8,128)(2,1)S(1)}, u32[]{:S(2)}, u32[]{:S(2)}) collective-permute-start(bf16[10,64,128]{2,1,0:T(8,128)(2,1)S(1)} %get-tuple-element.48), channel_id=1, source_target_pairs={{0,2},{1,3},{2,0},{3,1},{4,6},{5,7},{6,4},{7,5},{8,10},{9,11},{10,... | collective-permute-start | bytes 491528 | tf_op jit(solution)/shard_map/ppermute | solution.py:363
  77.5 10.9 %collective-permute-start.9 = (bf16[10,64,128]{2,1,0:T(8,128)(2,1)S(1)}, bf16[10,64,128]{2,1,0:T(8,128)(2,1)S(1)}, u32[]{:S(2)}, u32[]{:S(2)}) collective-permute-start(bf16[10,64,128]{2,1,0:T(8,128)(2,1)S(1)} %get-tuple-element.49), channel_id=1, source_target_pairs={{0,3},{1,2},{2,1},{3,0},{4,7},{5,6},{6,5},{7,4},{8,11},{9,10},{10,... | collective-permute-start | bytes 491528 | tf_op jit(solution)/shard_map/ppermute | solution.py:363
  91.8 9.9 %collective-permute-start.11 = (bf16[4,256,128]{2,1,0:T(8,128)(2,1)}, bf16[4,256,128]{2,1,0:T(8,128)(2,1)S(1)}, u32[]{:S(2)}, u32[]{:S(2)}) collective-permute-start(bf16[4,256,128]{2,1,0:T(8,128)(2,1)} %get-tuple-element.51), channel_id=1, source_target_pairs={{4,8},{8,4},{5,9},{9,5},{6,10},{10,6},{7,11},{11,7},{20,24},{24,20... | collective-permute-start | bytes 786440 | tf_op jit(solution)/shard_map/ppermute | solution.py:492
  97.4 4.3 %collective-permute-start.10 = (bf16[4,256,128]{2,1,0:T(8,128)(2,1)}, bf16[4,256,128]{2,1,0:T(8,128)(2,1)S(1)}, u32[]{:S(2)}, u32[]{:S(2)}) collective-permute-start(bf16[4,256,128]{2,1,0:T(8,128)(2,1)} %get-tuple-element.51), channel_id=1, source_target_pairs={{0,4},{4,0},{8,12},{12,8},{1,5},{5,1},{9,13},{13,9},{2,6},{6,2},{1... | collective-permute-start | bytes 786440 | tf_op jit(solution)/shard_map/ppermute | solution.py:493
  103.2 2.2 %collective-permute-start.14 = (bf16[256,128]{1,0:T(8,128)(2,1)S(1)}, bf16[256,128]{1,0:T(8,128)(2,1)S(1)}, u32[]{:S(2)}, u32[]{:S(2)}) collective-permute-start(bf16[256,128]{1,0:T(8,128)(2,1)S(1)} %get-tuple-element.55), channel_id=1, source_target_pairs={{0,4},{4,0},{8,12},{12,8},{1,5},{5,1},{9,13},{13,9},{2,6},{6,2},{1... | collective-permute-start | bytes 196616 | tf_op jit(solution)/shard_map/ppermute | solution.py:363
  103.2 4.0 %collective-permute-start.15 = (bf16[256,128]{1,0:T(8,128)(2,1)S(1)}, bf16[256,128]{1,0:T(8,128)(2,1)S(1)}, u32[]{:S(2)}, u32[]{:S(2)}) collective-permute-start(bf16[256,128]{1,0:T(8,128)(2,1)S(1)} %get-tuple-element.56), channel_id=1, source_target_pairs={{0,8},{4,12},{8,0},{12,4},{1,9},{5,13},{9,1},{13,5},{2,10},{6,14},... | collective-permute-start | bytes 196616 | tf_op jit(solution)/shard_map/ppermute | solution.py:363
  105.1 4.0 %collective-permute-start.16 = (bf16[256,128]{1,0:T(8,128)(2,1)S(1)}, bf16[256,128]{1,0:T(8,128)(2,1)S(1)}, u32[]{:S(2)}, u32[]{:S(2)}) collective-permute-start(bf16[256,128]{1,0:T(8,128)(2,1)S(1)} %get-tuple-element.57), channel_id=1, source_target_pairs={{0,12},{4,8},{8,4},{12,0},{1,13},{5,9},{9,5},{13,1},{2,14},{6,10},... | collective-permute-start | bytes 196616 | tf_op jit(solution)/shard_map/ppermute | solution.py:363
  110.0 5.2 %collective-permute-start.17 = (bf16[64,128]{1,0:T(8,128)(2,1)S(1)}, bf16[64,128]{1,0:T(8,128)(2,1)S(1)}, u32[]{:S(2)}, u32[]{:S(2)}) collective-permute-start(bf16[64,128]{1,0:T(8,128)(2,1)S(1)} %get-tuple-element.59), channel_id=1, source_target_pairs={{0,1},{1,0},{2,3},{3,2},{4,5},{5,4},{6,7},{7,6},{8,9},{9,8},{10,11... | collective-permute-start | bytes 49160 | tf_op jit(solution)/shard_map/ppermute | solution.py:363
  113.0 3.6 %collective-permute-start.18 = (bf16[64,128]{1,0:T(8,128)(2,1)S(1)}, bf16[64,128]{1,0:T(8,128)(2,1)S(1)}, u32[]{:S(2)}, u32[]{:S(2)}) collective-permute-start(bf16[64,128]{1,0:T(8,128)(2,1)S(1)} %get-tuple-element.60), channel_id=1, source_target_pairs={{0,2},{1,3},{2,0},{3,1},{4,6},{5,7},{6,4},{7,5},{8,10},{9,11},{10,... | collective-permute-start | bytes 49160 | tf_op jit(solution)/shard_map/ppermute | solution.py:363
  114.0 4.4 %collective-permute-start.19 = (bf16[64,128]{1,0:T(8,128)(2,1)S(1)}, bf16[64,128]{1,0:T(8,128)(2,1)S(1)}, u32[]{:S(2)}, u32[]{:S(2)}) collective-permute-start(bf16[64,128]{1,0:T(8,128)(2,1)S(1)} %get-tuple-element.61), channel_id=1, source_target_pairs={{0,3},{1,2},{2,1},{3,0},{4,7},{5,6},{6,5},{7,4},{8,11},{9,10},{10,... | collective-permute-start | bytes 49160 | tf_op jit(solution)/shard_map/ppermute | solution.py:363
  (13 other events, 47.8 us)

commit v5 on v4

--- a/solution.py
+++ b/solution.py
@@ -12,7 +12,6 @@
 BF16 = jnp.bfloat16
 LANES = 128
 ROWS = 16
-VMEM_BYTES = 50 * 1024 * 1024
 NT = (((1,), (1,)), ((), ()))
 WHOLE = pl.BlockSpec(memory_space=pltpu.VMEM)
 NEAR = pl.BlockSpec(memory_space=pltpu.VMEM)
@@ -22,7 +21,7 @@
 copies = pltpu.SemaphoreType.DMA
 
 
-def call(kernel, grid, in_specs, out_specs, outs, scratch, args, aliases=None):
+def call(room, kernel, grid, in_specs, out_specs, outs, scratch, args, aliases=None, micros=0.001):
     def place(spec):
         return pltpu.VMEM if spec is NEAR else None
 
@@ -39,8 +38,8 @@
         out_specs=out_specs,
         scratch_shapes=scratch,
         input_output_aliases=aliases or {},
-        compiler_params=pltpu.CompilerParams(vmem_limit_bytes=VMEM_BYTES),
-        cost_estimate=pl.CostEstimate(flops=1 << 20, bytes_accessed=1 << 10, transcendentals=0),
+        compiler_params=pltpu.CompilerParams(vmem_limit_bytes=room << 20),
+        cost_estimate=pl.CostEstimate(flops=int(micros * 1.1e9), bytes_accessed=1 << 10, transcendentals=0),
     )(*args)
 
 
@@ -125,9 +124,13 @@
         own_ref[g] = turned(groups + g)
 
 
-def owner_kernel(bands, first, ids_ref, xt_ref, own_ref, core_hbm, link_hbm, energy_ref, half_in, *refs):
-    half_out, scaled_ref, scaled_hbm, whole_ref = refs[:4]
-    messages, (core_ref, link_ref, in_sems, out_sems) = refs[4 : 3 + bands], refs[3 + bands :]
+def hand_on(value, unread, same):
+    pass
+
+
+def owner_kernel(bands, first, ids_ref, xt_ref, own_ref, core_hbm, link_hbm, energy_ref, unread, unread_too, *refs):
+    scaled_ref, scaled_hbm, whole_ref = refs[:3]
+    messages, (core_ref, link_ref, in_sems, out_sems) = refs[3 : 2 + bands], refs[2 + bands :]
     lines = xt_ref.shape[0]
     share = lines // bands
     band = ids_ref[1]
@@ -198,10 +201,9 @@
     lax.fori_loop(0, slots // unroll, body, 0)
 
 
-def stencil_kernel(xt_ref, core_ref, early_ref, late_ref, added_ref, pot_ref, ring_ref, unread, out_ref, done_ref):
+def stencil_kernel(xt_ref, core_ref, early_ref, late_ref, added_ref, pot_ref, ring_ref, unread, out_ref):
     states, here, _ = out_ref.shape
     lines = xt_ref.shape[0]
-    done_ref[...] = jnp.zeros_like(done_ref)
     step = pl.program_id(0)
     y0 = step * here
     early = step < pl.num_programs(0) // 2
@@ -228,7 +230,7 @@
     copy.wait()
 
 
-def later_kernel(bands, ids_ref, landed, unread, all_ref, pass_hbm, sems, pass_sem):
+def later_kernel(bands, ids_ref, landed, unread, unread_too, all_ref, pass_hbm, sems, pass_sem):
     count, states = all_ref.shape[0], landed.shape[1]
     loads = [
         start(
@@ -243,7 +245,7 @@
     pass_half(ids_ref, all_ref, pass_hbm, pass_sem)
 
 
-def early_kernel(bands, share, ids_ref, xt_ref, whole_ref, after_ref, unread, *refs):
+def early_kernel(bands, share, ids_ref, xt_ref, whole_ref, after_ref, *refs):
     pieces, (all_ref, pass_hbm, projs_ref, sems, pass_sem) = refs[: bands - 1], refs[bands - 1 :]
     states = xt_ref.shape[1]
     band = ids_ref[1]
@@ -295,9 +297,8 @@
 
 
 def final_kernel(
-    bands, share, ids_ref, all_ref, core_ref, link_ref, pot_ref, begun_ref, proj_ref, energy_ref, *refs
+    bands, share, ids_ref, all_ref, core_ref, link_ref, pot_ref, begun_ref, proj_ref, energy_ref, out_ref, acc
 ):
-    out_refs, (acc, blocks) = refs[:-2], refs[-2:]
     acc[...] = begun_ref[...]
     add_products(ids_ref[1] * share, ids_ref, all_ref, core_ref, link_ref, pot_ref, acc)
     groups = proj_ref.shape[0]
@@ -307,34 +308,17 @@
         scaled = (here.astype(F32) * energy_ref[pl.ds(first + g, 1), :]).astype(BF16)
         acc[1] += lax.dot_general(scaled, here, NT, preferred_element_type=F32)
     hamil = 0.5 * (acc[1] + acc[1].T)
-    cols = blocks.shape[2] // 2
-    for c in range(blocks.shape[0]):
-        blocks[c, :, :cols] = acc[0, :, c * cols : (c + 1) * cols].astype(BF16)
-        blocks[c, :, cols:] = hamil[:, c * cols : (c + 1) * cols].astype(BF16)
-    for k, out_ref in enumerate(out_refs):
-        out_ref[...] = blocks[ids_ref[0] ^ k]
-
-
-def load_all(sources, slots, sems):
-    copies_in = [start(pltpu.make_async_copy(far, slots.at[i], sems.at[i])) for i, far in enumerate(sources)]
-    for copy in copies_in:
-        copy.wait()
-
-
-def rows_kernel(domains, ids_ref, own_ref, *refs):
-    landed, (own_out, *outs, slots, total, sems) = refs[: domains - 1], refs[domains - 1 :]
-    load_all(landed, slots, sems)
-    rows = own_out.shape[0]
-    total[...] = own_ref[...].astype(F32) + jnp.sum(slots[...].astype(F32), axis=0)
-    for k, out_ref in enumerate((own_out, *outs)):
-        begin = pl.multiple_of((ids_ref[1] ^ k) * rows, rows)
-        out_ref[...] = total[pl.ds(begin, rows), :].astype(out_ref.dtype)
-
-
-def result_kernel(bands, scale, own_ref, *refs):
-    landed, (out_ref, slots, sems) = refs[: bands - 1], refs[bands - 1 :]
-    load_all(landed, slots, sems)
-    total = (own_ref[...] + jnp.sum(slots[...].astype(F32), axis=0)) * scale
+    domains = out_ref.shape[0] // bands
+    rows, cols = out_ref.shape[1], out_ref.shape[2] // 2
+    for c in range(domains):
+        for r in range(bands):
+            r0, c0 = r * rows, c * cols
+            out_ref[c * bands + r, :, :cols] = acc[0, r0 : r0 + rows, c0 : c0 + cols].astype(BF16)
+            out_ref[c * bands + r, :, cols:] = hamil[r0 : r0 + rows, c0 : c0 + cols].astype(BF16)
+
+
+def result_kernel(scale, parts_ref, out_ref):
+    total = jnp.sum(parts_ref[...].astype(F32), axis=0) * scale
     cols = out_ref.shape[2]
     out_ref[0] = total[:, :cols]
     out_ref[1] = total[:, cols:]
@@ -376,6 +360,7 @@
 
     line_shape, half_shape = (lines, states, cols_z), (lines // 2, states, cols_z)
     xt, xt_far, early_half, late_half, message = call(
+        58,
         functools.partial(pack_kernel, first),
         (),
         [FAR],
@@ -396,6 +381,7 @@
 
     group_shape = (groups, states, LANES)
     to_core, own, to_link = call(
+        50,
         project_kernel,
         (),
         [SCALARS, SCALARS, NEAR, FAR],
@@ -410,28 +396,31 @@
     )
     from_link = lax.ppermute(to_link, "domain", link_pairs)
     from_core = lax.ppermute(to_core, "domain", core_pairs)
-    late_half, scaled, scaled_far, whole, *messages = call(
+    scaled, scaled_far, whole, *messages = call(
+        59,
         functools.partial(owner_kernel, bands, first),
         (),
-        [SCALARS, NEAR, NEAR, FAR, FAR, WHOLE, FAR],
-        [FAR, NEAR, FAR, NEAR] + [FAR] * (bands - 1),
-        [(half_shape, BF16)]
-        + [(group_shape, BF16)] * 3
+        [SCALARS, NEAR, NEAR, FAR, FAR, WHOLE, UNREAD, UNREAD],
+        [NEAR, FAR, NEAR] + [FAR] * (bands - 1),
+        [(group_shape, BF16)] * 3
         + [((first + group_share, states, cols_z), BF16)] * (bands - 1),
         [pltpu.VMEM(group_shape, BF16), pltpu.VMEM(group_shape, BF16), copies((2,)), copies((2 * bands - 1,))],
-        (ids, xt, own, from_core, from_link, energy, late_half),
-        aliases={6: 0},
+        (ids, xt, own, from_core, from_link, energy, link_early, core_field),
     )
     link_scaled = lax.ppermute(scaled_far, "domain", link_pairs)
     core_scaled = lax.ppermute(scaled_far, "domain", core_pairs)
+    (late_half,) = call(
+        59, hand_on, (), [UNREAD, UNREAD], [UNREAD], [(half_shape, BF16)], [], (late_half, link_scaled), aliases={0: 0}
+    )
     link_late = lax.ppermute(late_half, "domain", link_pairs)
     early = swapped(messages, "band")
 
     (added,) = call(
+        40,
         nonlocal_kernel,
         (),
         [SCALARS, SCALARS, FAR, FAR, NEAR, FAR],
-        [NEAR],
+        [WHOLE],
         [((lines + 1, states, cols_z), F32)],
         [
             pltpu.VMEM((3 * atoms_here, states, proj_count), BF16),
@@ -444,20 +433,61 @@
     )
 
     later_all, later_pass = call(
+        40,
         functools.partial(later_kernel, bands),
         (),
-        [SCALARS, FAR, NEAR],
+        [SCALARS, FAR, UNREAD, UNREAD],
         [NEAR, FAR],
         [((rest + 1, total_states, cols_z), BF16), ((rest // 2, total_states, cols_z), BF16)],
         [copies((bands,)), copies],
-        (ids, landed, added),
+        (ids, landed, added, link_late),
     )
     later_link = lax.ppermute(later_pass, "domain", link_pairs)
     later_core = lax.ppermute(later_pass, "domain", core_pairs)
 
+    early_all, early_pass, projs = call(
+        40,
+        functools.partial(early_kernel, bands, share),
+        (),
+        [SCALARS, NEAR, NEAR, NEAR] + [FAR] * (bands - 1),
+        [NEAR, FAR, NEAR],
+        [
+            ((first + 1, total_states, cols_z), BF16),
+            ((first // 2, total_states, cols_z), BF16),
+            ((group_share, total_states, LANES), BF16),
+        ],
+        [copies((2 * bands + 1,)), copies],
+        (ids, xt, whole, later_all, *early),
+        micros=30,
+    )
+    early_link = lax.ppermute(early_pass, "domain", link_pairs)
+    early_core = lax.ppermute(early_pass, "domain", core_pairs)
+    (begun,) = call(
+        40,
+        functools.partial(gram_kernel, first, share),
+        (),
+        [SCALARS, NEAR, WHOLE, WHOLE, WHOLE, NEAR],
+        [NEAR],
+        [((2, total_states, total_states), F32)],
+        [],
+        (ids, later_all, later_core, later_link, pot, early_all),
+    )
+    parts = domains * bands
+    (blocks,) = call(
+        40,
+        functools.partial(final_kernel, bands, share),
+        (),
+        [SCALARS, NEAR, WHOLE, WHOLE, WHOLE, NEAR, NEAR, WHOLE],
+        [WHOLE],
+        [((parts, states, 2 * total_states // domains), BF16)],
+        [pltpu.VMEM((2, total_states, total_states), F32)],
+        (ids, early_all, early_core, early_link, pot, begun, projs, energy),
+    )
+    summed = lax.all_to_all(blocks, ("domain", "band"), split_axis=0, concat_axis=0, tiled=True)
     steps = lines // ROWS
     block = pl.BlockSpec((ROWS, states, cols_z), lambda i: (i, 0, 0))
-    applied, done = call(
+    (applied,) = call(
+        40,
         stencil_kernel,
         (steps,),
         [
@@ -465,69 +495,26 @@
             block,
             pl.BlockSpec((ROWS, states, cols_z), lambda i: (jnp.minimum(i, steps // 2 - 1), 0, 0)),
             pl.BlockSpec((ROWS, states, cols_z), lambda i: (jnp.maximum(i - steps // 2, 0), 0, 0)),
-            NEAR,
+            WHOLE,
             pl.BlockSpec((ROWS, cols_z), lambda i: (i, 0)),
             WHOLE,
-            NEAR,
+            UNREAD,
         ],
-        [pl.BlockSpec((states, ROWS, cols_z), lambda i: (0, i, 0)), WHOLE],
-        [((states, lines, cols_z), BF16), ((8, LANES), F32)],
+        [pl.BlockSpec((states, ROWS, cols_z), lambda i: (0, i, 0))],
+        [((states, lines, cols_z), BF16)],
         [],
-        (xt, core_field, link_early, link_late, added, pot, ring, later_all),
-    )
-
-    early_all, early_pass, projs = call(
-        functools.partial(early_kernel, bands, share),
-        (),
-        [SCALARS, NEAR, NEAR, NEAR, WHOLE] + [FAR] * (bands - 1),
-        [NEAR, FAR, NEAR],
-        [
-            ((first + 1, total_states, cols_z), BF16),
-            ((first // 2, total_states, cols_z), BF16),
-            ((group_share, total_states, LANES), BF16),
-        ],
-        [copies((2 * bands + 1,)), copies],
-        (ids, xt, whole, later_all, done, *early),
-    )
-    early_link = lax.ppermute(early_pass, "domain", link_pairs)
-    early_core = lax.ppermute(early_pass, "domain", core_pairs)
-    (begun,) = call(
-        functools.partial(gram_kernel, first, share),
-        (),
-        [SCALARS, NEAR, WHOLE, WHOLE, WHOLE, NEAR],
-        [NEAR],
-        [((2, total_states, total_states), F32)],
-        [],
-        (ids, later_all, later_core, later_link, pot, early_all),
-    )
-    columns = (total_states, 2 * total_states // domains)
-    own_columns, *far_columns = call(
-        functools.partial(final_kernel, bands, share),
-        (),
-        [SCALARS, NEAR, WHOLE, WHOLE, WHOLE, NEAR, NEAR, WHOLE],
-        [NEAR] + [WHOLE] * (domains - 1),
-        [(columns, BF16)] * domains,
-        [pltpu.VMEM((2, total_states, total_states), F32), pltpu.VMEM((domains, *columns), BF16)],
-        (ids, early_all, early_core, early_link, pot, begun, projs, energy),
-    )
-    piece = (states, columns[1])
-    own_rows, *far_rows = call(
-        functools.partial(rows_kernel, domains),
-        (),
-        [SCALARS, NEAR] + [FAR] * (domains - 1),
-        [NEAR] + [WHOLE] * (bands - 1),
-        [(piece, F32)] + [(piece, BF16)] * (bands - 1),
-        [pltpu.VMEM((domains - 1, *columns), BF16), pltpu.VMEM(columns, F32), copies((domains - 1,))],
-        (ids, own_columns, *swapped(far_columns, "domain")),
-    )
+        (xt, core_field, link_early, link_late, added, pot, ring, blocks),
+    )
+
     (subspace,) = call(
-        functools.partial(result_kernel, bands, 1.0 / (lines * cols_z * domains)),
-        (),
-        [NEAR] + [FAR] * (bands - 1),
+        40,
+        functools.partial(result_kernel, 1.0 / (lines * cols_z * domains)),
+        (),
+        [WHOLE],
         [WHOLE],
         [((2, states, total_states // domains), F32)],
-        [pltpu.VMEM((bands - 1, *piece), BF16), copies((bands - 1,))],
-        (own_rows, *swapped(far_rows, "band")),
+        [],
+        (summed,),
     )
     return applied.reshape(orbitals.shape), subspace
 

time: 122 us -> 102 us (0.84); the launches traced: 119 us -> 101 us
  waiting for transfers between devices: 30.4 us -> 17.7 us
  starting transfers between devices: 37.2 us -> 33.3 us
  Pallas kernels: 41.8 us -> 38.7 us
  local copies, waits for them, and re-layouts: 7.61 us -> 9.42 us
    ppermute x1, waiting for transfers between devices: 18.3 us -> 4.8 us  [local(): link_scaled = lax.ppermute(scaled_far, 'domain', link_pairs)]
    ppermute x9 -> x3, waiting for transfers between devices: 10.2 us -> 0.01 us  [swapped(): lax.ppermute(values[k - 1], axis, [(i, i ^ k) for i in range(size)])]
    ppermute x9 -> x3, starting transfers between devices: 11.3 us -> 3.98 us  [swapped(): lax.ppermute(values[k - 1], axis, [(i, i ^ k) for i in range(size)])]
    ppermute x1, waiting for transfers between devices: 0.01 us -> 6.65 us  [local(): later_link = lax.ppermute(later_pass, 'domain', link_pairs)]
    all_to_all x0 -> x1, starting transfers between devices: none -> 6.59 us  [local(): lax.all_to_all(blocks, ('domain', 'band'), split_axis=0, concat_axis=0, t...]
    ppermute x1, starting transfers between devices: 5.61 us -> 1.92 us  [local(): early_link = lax.ppermute(early_pass, 'domain', link_pairs)]
    pallas_call x11, Pallas kernels: 41.8 us -> 38.7 us  [call(): pl.pallas_call(kernel, grid=grid, out_shape=shapes, in_specs=in_specs, ou...]
    ppermute x1, waiting for transfers between devices: 0.88 us -> 3.6 us  [local(): from_link = lax.ppermute(to_link, 'domain', link_pairs)]
  transfers between devices with their start and end apart: 21 -> 16, of which waited for: 8 -> 5; matrix products, arithmetic and copies ran while one was open for 1% -> 1% of each run, Pallas kernels for 29% -> 32%
where the time goes in v5:
time: 102 us; the launch traced here: 101 us
  Pallas kernels  38.7 us (38%)
  starting transfers between devices  33.3 us (33%)
  waiting for transfers between devices  17.7 us (17%)
  local copies, waits for them, and re-layouts  9.42 us (9%)
  between operations  1.59 us (2%)
    pallas_call x11, Pallas kernels, call(): pl.pallas_call(kernel, grid=grid, out_shape=shapes, in_specs=in_specs, ou...  38.7 us
    unnamed x39, local copies, waits for them, and re-layouts  8.71 us
    ppermute x1, waiting for transfers between devices, local(): later_link = lax.ppermute(later_pass, 'domain', link_pairs)  6.65 us
    all_to_all x1, starting transfers between devices, local(): lax.all_to_all(blocks, ('domain', 'band'), split_axis=0, concat_axis=0, t...  6.59 us
    all_to_all x1, starting transfers between devices, local(): lax.all_to_all(message, 'band', split_axis=0, concat_axis=0, tiled=True)  6.04 us
    ppermute x1, waiting for transfers between devices, local(): link_scaled = lax.ppermute(scaled_far, 'domain', link_pairs)  4.8 us
    ppermute x1, starting transfers between devices, local(): later_link = lax.ppermute(later_pass, 'domain', link_pairs)  4.31 us
    ppermute x3, starting transfers between devices, swapped(): lax.ppermute(values[k - 1], axis, [(i, i ^ k) for i in range(size)])  3.98 us
  transfers between devices with their start and end apart: 16, of which 5 were waited for; matrix products, arithmetic and copies ran while one was open for 1% of the time, Pallas kernels for 32%

profile of v5, /device:TPU:1, one launch (start us, length us, event | category | flops | bytes accessed | tf_op | source)
XLA Modules:
  0.0 100.8 jit_solution(12011103190865046893)
XLA Ops:
  0.6 4.0 %shard_map.95 = (bf16[128,64,128]{2,1,0:T(8,128)(2,1)S(1)}, bf16[128,64,128]{2,1,0:T(8,128)(2,1)}, bf16[64,64,128]{2,1,0:T(8,128)(2,1)}, bf16[64,64,128]{2,1,0:T(8,128)(2,1)}, bf16[100,64,128]{2,1,0:T(8,128)(2,1)}) custom-call(bf16[64,128,128]{2,1,0:T(8,128)(2,1)} %bitcast.13), custom_call_target="tpu_custom_call" | custom-call | flops 1100000 | bytes 1024 | tf_op jit(solution)/shard_map/pallas_call | solution.py:33
  4.8 6.0 %all-to-all-start = ((bf16[100,64,128]{2,1,0:T(8,128)(2,1)}), bf16[100,64,128]{2,1,0:T(8,128)(2,1)}, u32[]{:S(2)}, u32[]{:S(2)}) async-start(bf16[100,64,128]{2,1,0:T(8,128)(2,1)} %get-tuple-element.31), calls=%async_computation | async-start | bytes 3276800 | tf_op jit(solution)/shard_map/all_to_all | solution.py:378
  10.9 3.5 %collective-permute-start.1 = (bf16[64,64,128]{2,1,0:T(8,128)(2,1)}, bf16[64,64,128]{2,1,0:T(8,128)(2,1)}, u32[]{:S(2)}, u32[]{:S(2)}) collective-permute-start(bf16[64,64,128]{2,1,0:T(8,128)(2,1)} %get-tuple-element.23), channel_id=1, source_target_pairs={{4,8},{8,4},{5,9},{9,5},{6,10},{10,6},{7,11},{11,7},{20,24},{24,20... | collective-permute-start | bytes 3145736 | tf_op jit(solution)/shard_map/ppermute | solution.py:379
  15.1 8.1 %shard_map.96 = (bf16[8,64,128]{2,1,0:T(8,128)(2,1)S(1)}, f32[8,64,128]{2,1,0:T(8,128)S(1)}, bf16[8,64,128]{2,1,0:T(8,128)(2,1)S(1)}) custom-call(s32[384]{0:T(512)S(1)} %get-tuple-element.45.words_ref, s32[2]{0:T(128)S(1)} %pad_add_fusion.ids_ref, bf16[128,64,128]{2,1,0:T(8,128)(2,1)S(1)} %get-tuple-element.21.xt_ref, bf16[384,16,128]{2,1,0:T(8,128)(2,1)} %p_hbm.3), custom_call_target="tpu_custom_call" | custom-call | flops 1100000 | bytes 1024 | tf_op jit(solution)/shard_map/pallas_call | solution.py:33
  23.3 2.3 %collective-permute-start.3 = (bf16[8,64,128]{2,1,0:T(8,128)(2,1)S(1)}, bf16[8,64,128]{2,1,0:T(8,128)(2,1)S(1)}, u32[]{:S(2)}, u32[]{:S(2)}) collective-permute-start(bf16[8,64,128]{2,1,0:T(8,128)(2,1)S(1)} %get-tuple-element.27), channel_id=1, source_target_pairs={{4,8},{8,4},{5,9},{9,5},{6,10},{10,6},{7,11},{11,7},{20,24},{24,20... | collective-permute-start | bytes 393224 | tf_op jit(solution)/shard_map/ppermute | solution.py:397
  26.4 3.6 %collective-permute-done.3.link_hbm = bf16[8,64,128]{2,1,0:T(8,128)(2,1)S(1)} collective-permute-done((bf16[8,64,128]{2,1,0:T(8,128)(2,1)S(1)}, bf16[8,64,128]{2,1,0:T(8,128)(2,1)S(1)}, u32[]{:S(2)}, u32[]{:S(2)}) %collective-permute-start.3) | collective-permute-done | bytes 131104 | tf_op jit(solution)/shard_map/ppermute | solution.py:397
  30.6 2.6 %shard_map.97 = (bf16[8,64,128]{2,1,0:T(8,128)(2,1)S(1)}, bf16[8,64,128]{2,1,0:T(8,128)(2,1)}, bf16[8,64,128]{2,1,0:T(8,128)(2,1)S(1)}, bf16[10,64,128]{2,1,0:T(...) custom-call(s32[2]{0:T(128)} %copy-done.9, bf16[128,64,128]{2,1,0:T(8,128)(2,1)S(1)} %get-tuple-element.21.xt_ref, ...), custom_call_target="tpu_custom_call" | custom-call | flops 1100000 | bytes 1024 | tf_op jit(solution)/shard_map/pallas_call | solution.py:33
  33.3 2.2 %collective-permute-start.4 = (bf16[8,64,128]{2,1,0:T(8,128)(2,1)}, bf16[8,64,128]{2,1,0:T(8,128)(2,1)S(1)}, u32[]{:S(2)}, u32[]{:S(2)}) collective-permute-start(bf16[8,64,128]{2,1,0:T(8,128)(2,1)} %get-tuple-element.28), channel_id=1, source_target_pairs={{4,8},{8,4},{5,9},{9,5},{6,10},{10,6},{7,11},{11,7},{20,24},{24,20... | collective-permute-start | bytes 393224 | tf_op jit(solution)/shard_map/ppermute | solution.py:410
  35.6 4.8 %collective-permute-done.4.unread.link_hbm = bf16[8,64,128]{2,1,0:T(8,128)(2,1)S(1)} collective-permute-done((bf16[8,64,128]{2,1,0:T(8,128)(2,1)}, bf16[8,64,128]{2,1,0:T(8,128)(2,1)S(1)}, u32[]{:S(2)}, u32[]{:S(2)}) %collective-permute-start.4) | collective-permute-done | bytes 131104 | tf_op jit(solution)/shard_map/ppermute | solution.py:410
  41.0 1.9 %collective-permute-start.5 = (bf16[64,64,128]{2,1,0:T(8,128)(2,1)}, bf16[64,64,128]{2,1,0:T(8,128)(2,1)}, u32[]{:S(2)}, u32[]{:S(2)}) collective-permute-start(bf16[64,64,128]{2,1,0:T(8,128)(2,1)} %shard_map.98), channel_id=1, source_target_pairs={{4,8},{8,4},{5,9},{9,5},{6,10},{10,6},{7,11},{11,7},{20,24},{24,20... | collective-permute-start | bytes 3145736 | tf_op jit(solution)/shard_map/ppermute | solution.py:415
  42.9 1.8 %collective-permute-start.7 = (bf16[10,64,128]{2,1,0:T(8,128)(2,1)S(1)}, bf16[10,64,128]{2,1,0:T(8,128)(2,1)S(1)}, u32[]{:S(2)}, u32[]{:S(2)}) collective-permute-start(bf16[10,64,128]{2,1,0:T(8,128)(2,1)S(1)} %copy-done.18), channel_id=1, source_target_pairs={{0,1},{1,0},{2,3},{3,2},{4,5},{5,4},{6,7},{7,6},{8,9},{9,8},{10,11... | collective-permute-start | bytes 491528 | tf_op jit(solution)/shard_map/ppermute | solution.py:347
  44.8 2.1 %collective-permute-start.8 = (bf16[10,64,128]{2,1,0:T(8,128)(2,1)S(1)}, bf16[10,64,128]{2,1,0:T(8,128)(2,1)S(1)}, u32[]{:S(2)}, u32[]{:S(2)}) collective-permute-start(bf16[10,64,128]{2,1,0:T(8,128)(2,1)S(1)} %copy-done.17), channel_id=1, source_target_pairs={{0,2},{1,3},{2,0},{3,1},{4,6},{5,7},{6,4},{7,5},{8,10},{9,11},{10,... | collective-permute-start | bytes 491528 | tf_op jit(solution)/shard_map/ppermute | solution.py:347
  49.4 8.8 %shard_map.99.unread.added_ref = f32[129,64,128]{2,1,0:T(8,128)S(1)} custom-call(s32[384]{0:T(512)S(1)} %get-tuple-element.44.words_ref, s32[2]{0:T(128)S(1)} %copy-done.10, bf16[384,16,128]{2,1,0:T(8,128)(2,1)S(1)} %copy-done.3, bf16[8,64,128]{2,1,0:T(8,128)(2,1)S(1)} %collective-permute-done.6.core_hbm, bf16[8,64,128]{2,1,0:T(8,128)(2,1)S(1)} %get-tuple-element.29.own_ref, ...), custom_call_target="tpu_custom_call" | custom-call | flops 1100000 | bytes 1024 | tf_op jit(solution)/shard_map/pallas_call | solution.py:33
  58.2 2.0 %copy-done = f32[129,64,128]{2,1,0:T(8,128)} copy-done((f32[129,64,128]{2,1,0:T(8,128)}, f32[129,64,128]{2,1,0:T(8,128)S(1)}, u32[]{:S(2)}) %copy-start) | copy-done | bytes 4227096
  60.2 2.2 %copy-done.1 = f32[129,64,128]{2,1,0:T(8,128)S(1)} copy-done((f32[129,64,128]{2,1,0:T(8,128)S(1)}, f32[129,64,128]{2,1,0:T(8,128)}, u32[]{:S(2)}) %copy-start.1) | copy-done | bytes 4227096
  62.4 2.0 %shard_map.100 = (bf16[25,256,128]{2,1,0:T(8,128)(2,1)S(1)}, bf16[12,256,128]{2,1,0:T(8,128)(2,1)S(1)}) custom-call(s32[2]{0:T(128)S(1)} %copy-done.10, bf16[100,64,128]{2,1,0:T(8,128)(2,1)} %all-to-all-done.landed, f32[129,64,128]{2,1,0:T(8,128)S(1)} %copy-done.1, bf16[64,64,128]{2,1,0:T(8,128)(2,1)} %collective-permute-done.5.unread_too.late_ref), custom_call_target="tpu_custom_call" | custom-call | flops 1100000 | bytes 1024 | tf_op jit(solution)/shard_map/pallas_call | solution.py:33
  64.7 4.3 %collective-permute-start.13 = (bf16[12,256,128]{2,1,0:T(8,128)(2,1)S(1)}, bf16[12,256,128]{2,1,0:T(8,128)(2,1)S(1)}, u32[]{:S(2)}, u32[]{:S(2)}) collective-permute-start(bf16[12,256,128]{2,1,0:T(8,128)(2,1)S(1)} %get-tuple-element.38), channel_id=1, source_target_pairs={{4,8},{8,4},{5,9},{9,5},{6,10},{10,6},{7,11},{11,7},{20,24},{24,20... | collective-permute-start | bytes 2359304 | tf_op jit(solution)/shard_map/ppermute | solution.py:445
  70.1 1.9 %collective-permute-start.11 = (bf16[4,256,128]{2,1,0:T(8,128)(2,1)S(1)}, bf16[4,256,128]{2,1,0:T(8,128)(2,1)S(1)}, u32[]{:S(2)}, u32[]{:S(2)}) collective-permute-start(bf16[4,256,128]{2,1,0:T(8,128)(2,1)S(1)} %get-tuple-element.37), channel_id=1, source_target_pairs={{4,8},{8,4},{5,9},{9,5},{6,10},{10,6},{7,11},{11,7},{20,24},{24,20... | collective-permute-start | bytes 786440 | tf_op jit(solution)/shard_map/ppermute | solution.py:463
  72.0 6.7 %collective-permute-done.13.link_ref = bf16[12,256,128]{2,1,0:T(8,128)(2,1)S(1)} collective-permute-done((bf16[12,256,128]{2,1,0:T(8,128)(2,1)S(1)}, bf16[12,256,128]{2,1,0:T(8,128)(2,1)S(1)}, u32[]{:S(2)}, u32[]{:S(2)}) %collective-permute-start.13) | collective-permute-done | bytes 786464 | tf_op jit(solution)/shard_map/ppermute | solution.py:445
  78.7 1.7 %shard_map.102.begun_ref = f32[2,256,256]{2,1,0:T(8,128)S(1)} custom-call(s32[2]{0:T(128)S(1)} %copy-done.10, bf16[25,256,128]{2,1,0:T(8,128)(2,1)S(1)} %get-tuple-element.32.after_ref.all_ref, bf16[12,256,128]{2,1,0:T(8,128)(2,1)S(1)} %collective-permute-done.12.core_ref, bf16[12,256,128]{2,1,0:T(8,128)(2,1)S(1)} %collective-permute-done.13.link_ref, ...), custom_call_target="tpu_custom_call" | custom-call | flops 1100000 | bytes 1024 | tf_op jit(solution)/shard_map/pallas_call | solution.py:33
  81.5 2.1 %shard_map.103.unread = bf16[16,64,128]{2,1,0:T(8,128)(2,1)} custom-call(s32[2]{0:T(128)S(1)} %copy-done.10, bf16[9,256,128]{2,1,0:T(8,128)(2,1)S(1)} %get-tuple-element.36.unread.all_ref, bf16[4,256,128]{2,1,0:T(8,128)(2,1)S(1)} %collective-permute-done.10.core_ref, bf16[4,256,128]{2,1,0:T(8,128)(2,1)S(1)} %collective-permute-done.11.link_ref, ...), custom_call_target="tpu_custom_call" | custom-call | flops 1100000 | bytes 1024 | tf_op jit(solution)/shard_map/pallas_call | solution.py:33
  83.6 6.6 %all-to-all-start.1 = ((bf16[16,64,128]{2,1,0:T(8,128)(2,1)}), bf16[16,64,128]{2,1,0:T(8,128)(2,1)S(1)}, u32[]{:S(2)}, u32[]{:S(2)}) async-start(bf16[16,64,128]{2,1,0:T(8,128)(2,1)} %shard_map.103.unread), calls=%async_computation.1 | async-start | bytes 524288 | tf_op jit(solution)/shard_map/all_to_all | solution.py:486
  90.3 2.2 %copy-done.2 = f32[129,64,128]{2,1,0:T(8,128)S(1)} copy-done((f32[129,64,128]{2,1,0:T(8,128)S(1)}, f32[129,64,128]{2,1,0:T(8,128)}, u32[]{:S(2)}) %copy-start.2) | copy-done | bytes 4227096
  92.4 7.6 %shard_map.104 = bf16[64,128,128]{2,1,0:T(8,128)(2,1)} custom-call(bf16[128,64,128]{2,1,0:T(8,128)(2,1)S(1)} %get-tuple-element.21.xt_ref, bf16[128,64,128]{2,1,0:T(8,128)(2,1)} %collective-permute-done.unread_too.core_ref, bf16[64,64,128]{2,1,0:T(8,128)(2,1)} %collective-permute-done.1.unread.early_ref, ...), custom_call_target="tpu_custom_call" | custom-call | flops 1100000 | bytes 1024 | tf_op jit(solution)/shard_map/pallas_call | solution.py:33
  (61 shorter events, 8.1 us)
Async XLA Ops:
  4.7 10.4 %copy-start.14 = (s32[384]{0:T(512)S(1)}, s32[384]{0:T(512)}, u32[]{:S(2)}) copy-start(s32[384]{0:T(512)} %param.12) | copy-start | bytes 4612
  4.7 10.4 %copy-start.15 = (s32[384]{0:T(512)S(1)}, s32[384]{0:T(512)}, u32[]{:S(2)}) copy-start(s32[384]{0:T(512)} %param.11) | copy-start | bytes 4612
  4.7 25.3 %collective-permute-start = (bf16[128,64,128]{2,1,0:T(8,128)(2,1)}, bf16[128,64,128]{2,1,0:T(8,128)(2,1)}, u32[]{:S(2)}, u32[]{:S(2)}) collective-permute-start(bf16[128,64,128]{2,1,0:T(8,128)(2,1)} %get-tuple-element.22), channel_id=1, source_target_pairs={{0,4},{4,0},{8,12},{12,8},{1,5},{5,1},{9,13},{13,9},{2,6},{6,2},{1... | collective-permute-start | bytes 6291464 | tf_op jit(solution)/shard_map/ppermute | solution.py:380
  4.8 55.3 %all-to-all-start = ((bf16[100,64,128]{2,1,0:T(8,128)(2,1)}), bf16[100,64,128]{2,1,0:T(8,128)(2,1)}, u32[]{:S(2)}, u32[]{:S(2)}) async-start(bf16[100,64,128]{2,1,0:T(8,128)(2,1)} %get-tuple-element.31), calls=%async_computation | async-start | bytes 3276800 | tf_op jit(solution)/shard_map/all_to_all | solution.py:378
  10.9 14.7 %copy-start.13 = (f32[256,16]{0,1:T(8,128)S(1)}, f32[256,16]{0,1:T(8,128)}, u32[]{:S(2)}) copy-start(f32[256,16]{0,1:T(8,128)} %param.14) | copy-start | bytes 49156
  10.9 19.1 %collective-permute-start.1 = (bf16[64,64,128]{2,1,0:T(8,128)(2,1)}, bf16[64,64,128]{2,1,0:T(8,128)(2,1)}, u32[]{:S(2)}, u32[]{:S(2)}) collective-permute-start(bf16[64,64,128]{2,1,0:T(8,128)(2,1)} %get-tuple-element.23), channel_id=1, source_target_pairs={{4,8},{8,4},{5,9},{9,5},{6,10},{10,6},{7,11},{11,7},{20,24},{24,20... | collective-permute-start | bytes 3145736 | tf_op jit(solution)/shard_map/ppermute | solution.py:379
  15.1 14.9 %copy-start.9 = (s32[2]{0:T(128)}, s32[2]{0:T(128)S(1)}, u32[]{:S(2)}) copy-start(s32[2]{0:T(128)S(1)} %pad_add_fusion.ids_ref) | copy-start | bytes 28
  23.2 3.2 %collective-permute-start.2 = (bf16[8,64,128]{2,1,0:T(8,128)(2,1)S(1)}, bf16[8,64,128]{2,1,0:T(8,128)(2,1)S(1)}, u32[]{:S(2)}, u32[]{:S(2)}) collective-permute-start(bf16[8,64,128]{2,1,0:T(8,128)(2,1)S(1)} %get-tuple-element.26), channel_id=1, source_target_pairs={{0,4},{4,0},{8,12},{12,8},{1,5},{5,1},{9,13},{13,9},{2,6},{6,2},{1... | collective-permute-start | bytes 393224 | tf_op jit(solution)/shard_map/ppermute | solution.py:398
  23.3 6.7 %collective-permute-start.3 = (bf16[8,64,128]{2,1,0:T(8,128)(2,1)S(1)}, bf16[8,64,128]{2,1,0:T(8,128)(2,1)S(1)}, u32[]{:S(2)}, u32[]{:S(2)}) collective-permute-start(bf16[8,64,128]{2,1,0:T(8,128)(2,1)S(1)} %get-tuple-element.27), channel_id=1, source_target_pairs={{4,8},{8,4},{5,9},{9,5},{6,10},{10,6},{7,11},{11,7},{20,24},{24,20... | collective-permute-start | bytes 393224 | tf_op jit(solution)/shard_map/ppermute | solution.py:397
  33.3 11.5 %copy-start.17 = (bf16[10,64,128]{2,1,0:T(8,128)(2,1)S(1)}, bf16[10,64,128]{2,1,0:T(8,128)(2,1)}, u32[]{:S(2)}) copy-start(bf16[10,64,128]{2,1,0:T(8,128)(2,1)} %get-tuple-element.34) | copy-start | bytes 491524
  33.3 13.5 %copy-start.16 = (bf16[10,64,128]{2,1,0:T(8,128)(2,1)S(1)}, bf16[10,64,128]{2,1,0:T(8,128)(2,1)}, u32[]{:S(2)}) copy-start(bf16[10,64,128]{2,1,0:T(8,128)(2,1)} %get-tuple-element.35) | copy-start | bytes 491524
  33.3 15.2 %copy-start.3 = (bf16[384,16,128]{2,1,0:T(8,128)(2,1)S(1)}, bf16[384,16,128]{2,1,0:T(8,128)(2,1)}, u32[]{:S(2)}) copy-start(bf16[384,16,128]{2,1,0:T(8,128)(2,1)} %p_hbm.3) | copy-start | bytes 4718596
  33.3 15.2 %copy-start.10 = (s32[2]{0:T(128)S(1)}, s32[2]{0:T(128)}, u32[]{:S(2)}) copy-start(s32[2]{0:T(128)} %copy-done.9) | copy-start | bytes 28
  33.3 7.0 %collective-permute-start.4 = (bf16[8,64,128]{2,1,0:T(8,128)(2,1)}, bf16[8,64,128]{2,1,0:T(8,128)(2,1)S(1)}, u32[]{:S(2)}, u32[]{:S(2)}) collective-permute-start(bf16[8,64,128]{2,1,0:T(8,128)(2,1)} %get-tuple-element.28), channel_id=1, source_target_pairs={{4,8},{8,4},{5,9},{9,5},{6,10},{10,6},{7,11},{11,7},{20,24},{24,20... | collective-permute-start | bytes 393224 | tf_op jit(solution)/shard_map/ppermute | solution.py:410
  41.0 19.2 %collective-permute-start.5 = (bf16[64,64,128]{2,1,0:T(8,128)(2,1)}, bf16[64,64,128]{2,1,0:T(8,128)(2,1)}, u32[]{:S(2)}, u32[]{:S(2)}) collective-permute-start(bf16[64,64,128]{2,1,0:T(8,128)(2,1)} %shard_map.98), channel_id=1, source_target_pairs={{4,8},{8,4},{5,9},{9,5},{6,10},{10,6},{7,11},{11,7},{20,24},{24,20... | collective-permute-start | bytes 3145736 | tf_op jit(solution)/shard_map/ppermute | solution.py:415
  42.9 26.1 %collective-permute-start.7 = (bf16[10,64,128]{2,1,0:T(8,128)(2,1)S(1)}, bf16[10,64,128]{2,1,0:T(8,128)(2,1)S(1)}, u32[]{:S(2)}, u32[]{:S(2)}) collective-permute-start(bf16[10,64,128]{2,1,0:T(8,128)(2,1)S(1)} %copy-done.18), channel_id=1, source_target_pairs={{0,1},{1,0},{2,3},{3,2},{4,5},{5,4},{6,7},{7,6},{8,9},{9,8},{10,11... | collective-permute-start | bytes 491528 | tf_op jit(solution)/shard_map/ppermute | solution.py:347
  44.8 24.3 %collective-permute-start.8 = (bf16[10,64,128]{2,1,0:T(8,128)(2,1)S(1)}, bf16[10,64,128]{2,1,0:T(8,128)(2,1)S(1)}, u32[]{:S(2)}, u32[]{:S(2)}) collective-permute-start(bf16[10,64,128]{2,1,0:T(8,128)(2,1)S(1)} %copy-done.17), channel_id=1, source_target_pairs={{0,2},{1,3},{2,0},{3,1},{4,6},{5,7},{6,4},{7,5},{8,10},{9,11},{10,... | collective-permute-start | bytes 491528 | tf_op jit(solution)/shard_map/ppermute | solution.py:347
  46.8 22.2 %collective-permute-start.9 = (bf16[10,64,128]{2,1,0:T(8,128)(2,1)S(1)}, bf16[10,64,128]{2,1,0:T(8,128)(2,1)S(1)}, u32[]{:S(2)}, u32[]{:S(2)}) collective-permute-start(bf16[10,64,128]{2,1,0:T(8,128)(2,1)S(1)} %copy-done.16), channel_id=1, source_target_pairs={{0,3},{1,2},{2,1},{3,0},{4,7},{5,6},{6,5},{7,4},{8,11},{9,10},{10,... | collective-permute-start | bytes 491528 | tf_op jit(solution)/shard_map/ppermute | solution.py:347
  46.9 1.6 %collective-permute-start.6 = (bf16[8,64,128]{2,1,0:T(8,128)(2,1)}, bf16[8,64,128]{2,1,0:T(8,128)(2,1)S(1)}, u32[]{:S(2)}, u32[]{:S(2)}) collective-permute-start(bf16[8,64,128]{2,1,0:T(8,128)(2,1)} %get-tuple-element.28), channel_id=1, source_target_pairs={{0,4},{4,0},{8,12},{12,8},{1,5},{5,1},{9,13},{13,9},{2,6},{6,2},{1... | collective-permute-start | bytes 393224 | tf_op jit(solution)/shard_map/ppermute | solution.py:411
  64.4 7.6 %collective-permute-start.12 = (bf16[12,256,128]{2,1,0:T(8,128)(2,1)S(1)}, bf16[12,256,128]{2,1,0:T(8,128)(2,1)S(1)}, u32[]{:S(2)}, u32[]{:S(2)}) collective-permute-start(bf16[12,256,128]{2,1,0:T(8,128)(2,1)S(1)} %get-tuple-element.38), channel_id=1, source_target_pairs={{0,4},{4,0},{8,12},{12,8},{1,5},{5,1},{9,13},{13,9},{2,6},{6,2},{1... | collective-permute-start | bytes 2359304 | tf_op jit(solution)/shard_map/ppermute | solution.py:446
  64.7 14.0 %collective-permute-start.13 = (bf16[12,256,128]{2,1,0:T(8,128)(2,1)S(1)}, bf16[12,256,128]{2,1,0:T(8,128)(2,1)S(1)}, u32[]{:S(2)}, u32[]{:S(2)}) collective-permute-start(bf16[12,256,128]{2,1,0:T(8,128)(2,1)S(1)} %get-tuple-element.38), channel_id=1, source_target_pairs={{4,8},{8,4},{5,9},{9,5},{6,10},{10,6},{7,11},{11,7},{20,24},{24,20... | collective-permute-start | bytes 2359304 | tf_op jit(solution)/shard_map/ppermute | solution.py:445
  70.0 10.4 %collective-permute-start.10 = (bf16[4,256,128]{2,1,0:T(8,128)(2,1)S(1)}, bf16[4,256,128]{2,1,0:T(8,128)(2,1)S(1)}, u32[]{:S(2)}, u32[]{:S(2)}) collective-permute-start(bf16[4,256,128]{2,1,0:T(8,128)(2,1)S(1)} %get-tuple-element.37), channel_id=1, source_target_pairs={{0,4},{4,0},{8,12},{12,8},{1,5},{5,1},{9,13},{13,9},{2,6},{6,2},{1... | collective-permute-start | bytes 786440 | tf_op jit(solution)/shard_map/ppermute | solution.py:464
  70.1 11.4 %collective-permute-start.11 = (bf16[4,256,128]{2,1,0:T(8,128)(2,1)S(1)}, bf16[4,256,128]{2,1,0:T(8,128)(2,1)S(1)}, u32[]{:S(2)}, u32[]{:S(2)}) collective-permute-start(bf16[4,256,128]{2,1,0:T(8,128)(2,1)S(1)} %get-tuple-element.37), channel_id=1, source_target_pairs={{4,8},{8,4},{5,9},{9,5},{6,10},{10,6},{7,11},{11,7},{20,24},{24,20... | collective-permute-start | bytes 786440 | tf_op jit(solution)/shard_map/ppermute | solution.py:463
  83.6 16.4 %all-to-all-start.1 = ((bf16[16,64,128]{2,1,0:T(8,128)(2,1)}), bf16[16,64,128]{2,1,0:T(8,128)(2,1)S(1)}, u32[]{:S(2)}, u32[]{:S(2)}) async-start(bf16[16,64,128]{2,1,0:T(8,128)(2,1)} %shard_map.103.unread), calls=%async_computation.1 | async-start | bytes 524288 | tf_op jit(solution)/shard_map/all_to_all | solution.py:486
  (11 other events, 44.2 us)

commit v6 on v5

--- a/solution.py
+++ b/solution.py
@@ -124,51 +124,36 @@
         own_ref[g] = turned(groups + g)
 
 
-def hand_on(value, unread, same):
+def hand_on(value, unread, unread_too, same):
     pass
 
 
-def owner_kernel(bands, first, ids_ref, xt_ref, own_ref, core_hbm, link_hbm, energy_ref, unread, unread_too, *refs):
-    scaled_ref, scaled_hbm, whole_ref = refs[:3]
-    messages, (core_ref, link_ref, in_sems, out_sems) = refs[3 : 2 + bands], refs[2 + bands :]
-    lines = xt_ref.shape[0]
-    share = lines // bands
-    band = ids_ref[1]
+def owner_kernel(
+    first, ids_ref, xt_ref, own_ref, core_ref, link_ref, energy_ref, unread, unread_too, scaled_ref, whole_ref, *messages
+):
+    share = xt_ref.shape[0] // (len(messages) + 1)
     groups = own_ref.shape[0]
-    group_share = groups // bands
-    loads = [
-        start(pltpu.make_async_copy(core_hbm, core_ref, in_sems.at[0])),
-        start(pltpu.make_async_copy(link_hbm, link_ref, in_sems.at[1])),
-    ]
-    sends = []
-
-    def send(source, target):
-        sends.append(start(pltpu.make_async_copy(source, target, out_sems.at[len(sends)])))
-
-    for k in range(1, bands):
-        send(xt_ref.at[pl.ds((band ^ k) * share, first)], messages[k - 1].at[pl.ds(0, first)])
-    for copy in loads:
-        copy.wait()
+    held = messages[0].shape[0] - first
     row = ids_ref[0] * groups
     for g in range(groups):
         whole = own_ref[g] + core_ref[g].astype(F32) + link_ref[g].astype(F32)
         scaled_ref[g] = (whole * energy_ref[pl.ds(row + g, 1), :]).astype(BF16)
         whole_ref[g] = whole.astype(BF16)
-    send(scaled_ref, scaled_hbm)
-    for k in range(1, bands):
-        send(whole_ref.at[pl.ds((band ^ k) * group_share, group_share)], messages[k - 1].at[pl.ds(first, group_share)])
-    for copy in sends:
-        copy.wait()
-
-
-def nonlocal_kernel(words_ref, ids_ref, p_hbm, core_hbm, own_ref, link_hbm, out_ref, atoms, p_ref, core_ref, link_ref, sems):
+    for k, message in enumerate(messages, 1):
+        to = ids_ref[1] ^ k
+        for i in range(first):
+            message[i] = xt_ref[to * share + i]
+        for i in range(held):
+            message[first + i] = whole_ref[to * held + i]
+
+
+def nonlocal_kernel(words_ref, ids_ref, p_hbm, core_ref, own_ref, link_ref, out_ref, atoms, p_ref, sem):
     slots, proj_count, _ = p_ref.shape
     groups, states, _ = own_ref.shape
     per_group = LANES // proj_count
     lines = out_ref.shape[0]
     unroll = 16
-    pairs = ((core_hbm, core_ref), (link_hbm, link_ref), (p_hbm, p_ref))
-    loads = [start(pltpu.make_async_copy(far, near, sems.at[i])) for i, (far, near) in enumerate(pairs)]
+    load = start(pltpu.make_async_copy(p_hbm, p_ref, sem))
 
     def clear(i, carry):
         out_ref[i] = jnp.zeros((states, LANES), F32)
@@ -177,18 +162,12 @@
     lax.fori_loop(0, lines, clear, 0)
     odd = ids_ref[0] & 1
 
-    def spread(first, ref):
+    for first, ref in (((1 - odd) * 2 * groups, core_ref), (groups, own_ref), (odd * 2 * groups, link_ref)):
         for g in range(groups):
             tile = ref[g]
             for u in range(per_group):
                 atoms[(first + g) * per_group + u] = tile[:, u * proj_count : (u + 1) * proj_count]
-
-    spread(groups, own_ref)
-    loads[0].wait()
-    spread((1 - odd) * 2 * groups, core_ref)
-    loads[1].wait()
-    spread(odd * 2 * groups, link_ref)
-    loads[2].wait()
+    load.wait()
 
     def body(i, carry):
         for u in range(unroll):
@@ -201,9 +180,10 @@
     lax.fori_loop(0, slots // unroll, body, 0)
 
 
-def stencil_kernel(xt_ref, core_ref, early_ref, late_ref, added_ref, pot_ref, ring_ref, unread, out_ref):
+def stencil_kernel(xt_ref, core_ref, early_ref, late_ref, added_ref, pot_ref, ring_ref, unread, out_ref, done_ref):
     states, here, _ = out_ref.shape
     lines = xt_ref.shape[0]
+    done_ref[...] = jnp.zeros_like(done_ref)
     step = pl.program_id(0)
     y0 = step * here
     early = step < pl.num_programs(0) // 2
@@ -245,7 +225,7 @@
     pass_half(ids_ref, all_ref, pass_hbm, pass_sem)
 
 
-def early_kernel(bands, share, ids_ref, xt_ref, whole_ref, after_ref, *refs):
+def early_kernel(bands, share, ids_ref, xt_ref, whole_ref, after_ref, unread, *refs):
     pieces, (all_ref, pass_hbm, projs_ref, sems, pass_sem) = refs[: bands - 1], refs[bands - 1 :]
     states = xt_ref.shape[1]
     band = ids_ref[1]
@@ -396,44 +376,49 @@
     )
     from_link = lax.ppermute(to_link, "domain", link_pairs)
     from_core = lax.ppermute(to_core, "domain", core_pairs)
-    scaled, scaled_far, whole, *messages = call(
+    scaled, whole, *messages = call(
         59,
-        functools.partial(owner_kernel, bands, first),
-        (),
-        [SCALARS, NEAR, NEAR, FAR, FAR, WHOLE, UNREAD, UNREAD],
-        [NEAR, FAR, NEAR] + [FAR] * (bands - 1),
-        [(group_shape, BF16)] * 3
-        + [((first + group_share, states, cols_z), BF16)] * (bands - 1),
-        [pltpu.VMEM(group_shape, BF16), pltpu.VMEM(group_shape, BF16), copies((2,)), copies((2 * bands - 1,))],
+        functools.partial(owner_kernel, first),
+        (),
+        [SCALARS, NEAR, NEAR, WHOLE, WHOLE, WHOLE, UNREAD, UNREAD],
+        [WHOLE, NEAR] + [WHOLE] * (bands - 1),
+        [(group_shape, BF16)] * 2 + [((first + group_share, states, cols_z), BF16)] * (bands - 1),
+        [],
         (ids, xt, own, from_core, from_link, energy, link_early, core_field),
     )
-    link_scaled = lax.ppermute(scaled_far, "domain", link_pairs)
-    core_scaled = lax.ppermute(scaled_far, "domain", core_pairs)
+    link_scaled = lax.ppermute(scaled, "domain", link_pairs)
+    core_scaled = lax.ppermute(scaled, "domain", core_pairs)
     (late_half,) = call(
-        59, hand_on, (), [UNREAD, UNREAD], [UNREAD], [(half_shape, BF16)], [], (late_half, link_scaled), aliases={0: 0}
+        59,
+        hand_on,
+        (),
+        [UNREAD] * 3,
+        [UNREAD],
+        [(half_shape, BF16)],
+        [],
+        (late_half, link_scaled, core_scaled),
+        aliases={0: 0},
     )
     link_late = lax.ppermute(late_half, "domain", link_pairs)
     early = swapped(messages, "band")
 
     (added,) = call(
-        40,
+        32,
         nonlocal_kernel,
         (),
-        [SCALARS, SCALARS, FAR, FAR, NEAR, FAR],
+        [SCALARS, SCALARS, FAR, WHOLE, WHOLE, WHOLE],
         [WHOLE],
         [((lines + 1, states, cols_z), F32)],
         [
             pltpu.VMEM((3 * atoms_here, states, proj_count), BF16),
             pltpu.VMEM(projectors.shape, BF16),
-            pltpu.VMEM(group_shape, BF16),
-            pltpu.VMEM(group_shape, BF16),
-            copies((3,)),
+            copies,
         ],
         (nonlocal_words, ids, projectors, core_scaled, scaled, link_scaled),
     )
 
     later_all, later_pass = call(
-        40,
+        32,
         functools.partial(later_kernel, bands),
         (),
         [SCALARS, FAR, UNREAD, UNREAD],
@@ -445,49 +430,10 @@
     later_link = lax.ppermute(later_pass, "domain", link_pairs)
     later_core = lax.ppermute(later_pass, "domain", core_pairs)
 
-    early_all, early_pass, projs = call(
-        40,
-        functools.partial(early_kernel, bands, share),
-        (),
-        [SCALARS, NEAR, NEAR, NEAR] + [FAR] * (bands - 1),
-        [NEAR, FAR, NEAR],
-        [
-            ((first + 1, total_states, cols_z), BF16),
-            ((first // 2, total_states, cols_z), BF16),
-            ((group_share, total_states, LANES), BF16),
-        ],
-        [copies((2 * bands + 1,)), copies],
-        (ids, xt, whole, later_all, *early),
-        micros=30,
-    )
-    early_link = lax.ppermute(early_pass, "domain", link_pairs)
-    early_core = lax.ppermute(early_pass, "domain", core_pairs)
-    (begun,) = call(
-        40,
-        functools.partial(gram_kernel, first, share),
-        (),
-        [SCALARS, NEAR, WHOLE, WHOLE, WHOLE, NEAR],
-        [NEAR],
-        [((2, total_states, total_states), F32)],
-        [],
-        (ids, later_all, later_core, later_link, pot, early_all),
-    )
-    parts = domains * bands
-    (blocks,) = call(
-        40,
-        functools.partial(final_kernel, bands, share),
-        (),
-        [SCALARS, NEAR, WHOLE, WHOLE, WHOLE, NEAR, NEAR, WHOLE],
-        [WHOLE],
-        [((parts, states, 2 * total_states // domains), BF16)],
-        [pltpu.VMEM((2, total_states, total_states), F32)],
-        (ids, early_all, early_core, early_link, pot, begun, projs, energy),
-    )
-    summed = lax.all_to_all(blocks, ("domain", "band"), split_axis=0, concat_axis=0, tiled=True)
     steps = lines // ROWS
     block = pl.BlockSpec((ROWS, states, cols_z), lambda i: (i, 0, 0))
-    (applied,) = call(
-        40,
+    applied, done = call(
+        32,
         stencil_kernel,
         (steps,),
         [
@@ -500,14 +446,53 @@
             WHOLE,
             UNREAD,
         ],
-        [pl.BlockSpec((states, ROWS, cols_z), lambda i: (0, i, 0))],
-        [((states, lines, cols_z), BF16)],
+        [pl.BlockSpec((states, ROWS, cols_z), lambda i: (0, i, 0)), WHOLE],
+        [((states, lines, cols_z), BF16), ((8, LANES), F32)],
         [],
-        (xt, core_field, link_early, link_late, added, pot, ring, blocks),
-    )
-
+        (xt, core_field, link_early, link_late, added, pot, ring, later_all),
+    )
+
+    early_all, early_pass, projs = call(
+        32,
+        functools.partial(early_kernel, bands, share),
+        (),
+        [SCALARS, NEAR, NEAR, NEAR, WHOLE] + [FAR] * (bands - 1),
+        [NEAR, FAR, NEAR],
+        [
+            ((first + 1, total_states, cols_z), BF16),
+            ((first // 2, total_states, cols_z), BF16),
+            ((group_share, total_states, LANES), BF16),
+        ],
+        [copies((2 * bands + 1,)), copies],
+        (ids, xt, whole, later_all, done, *early),
+        micros=30,
+    )
+    early_link = lax.ppermute(early_pass, "domain", link_pairs)
+    early_core = lax.ppermute(early_pass, "domain", core_pairs)
+    (begun,) = call(
+        32,
+        functools.partial(gram_kernel, first, share),
+        (),
+        [SCALARS, NEAR, WHOLE, WHOLE, WHOLE, NEAR],
+        [NEAR],
+        [((2, total_states, total_states), F32)],
+        [],
+        (ids, later_all, later_core, later_link, pot, early_all),
+    )
+    parts = domains * bands
+    (blocks,) = call(
+        32,
+        functools.partial(final_kernel, bands, share),
+        (),
+        [SCALARS, NEAR, WHOLE, WHOLE, WHOLE, NEAR, NEAR, WHOLE],
+        [WHOLE],
+        [((parts, states, 2 * total_states // domains), BF16)],
+        [pltpu.VMEM((2, total_states, total_states), F32)],
+        (ids, early_all, early_core, early_link, pot, begun, projs, energy),
+    )
+    summed = lax.all_to_all(blocks, ("domain", "band"), split_axis=0, concat_axis=0, tiled=True)
     (subspace,) = call(
-        40,
+        32,
         functools.partial(result_kernel, 1.0 / (lines * cols_z * domains)),
         (),
         [WHOLE],

time: 102 us -> 102 us (level)
  blocking collectives: 0 us -> 14.3 us
  starting transfers between devices: 33.3 us -> 26.5 us
  waiting for transfers between devices: 17.7 us -> 12.4 us
  Pallas kernels: 38.7 us -> 37.2 us
  local copies, waits for them, and re-layouts: 9.42 us -> 8.14 us
    all_to_all x0 -> x1, blocking collectives: none -> 14.3 us  [local(): lax.all_to_all(blocks, ('domain', 'band'), split_axis=0, concat_axis=0, t...]
    ppermute x1, waiting for transfers between devices: 6.65 us -> 0.01 us  [local(): later_link = lax.ppermute(later_pass, 'domain', link_pairs)]
    all_to_all x1 -> x0, starting transfers between devices: 6.59 us -> none  [local(): lax.all_to_all(blocks, ('domain', 'band'), split_axis=0, concat_axis=0, t...]
    ppermute x1, waiting for transfers between devices: 1.07 us -> 3.96 us  [local(): early_link = lax.ppermute(early_pass, 'domain', link_pairs)]
    pallas_call x11, Pallas kernels: 38.7 us -> 37.2 us  [call(): pl.pallas_call(kernel, grid=grid, out_shape=shapes, in_specs=in_specs, ou...]
    ppermute x2, waiting for transfers between devices: 6.35 us -> 4.82 us  [the longest x1 4.81 us: local(): link_scaled = lax.ppermute(scaled, 'domain', link_pairs)]
    unnamed x39 -> x45, local copies, waits for them, and re-layouts: 8.71 us -> 7.43 us
  transfers between devices with their start and end apart: 16 -> 15, of which waited for: 5 -> 3; matrix products, arithmetic and copies ran while one was open for 1% -> 1% of each run, Pallas kernels for 32% -> 31%
where the time goes in v6:
time: 102 us; the launch traced here: 100 us
  Pallas kernels  37.2 us (36%)
  starting transfers between devices  26.5 us (26%)
  blocking collectives  14.3 us (14%)
  waiting for transfers between devices  12.4 us (12%)
  local copies, waits for them, and re-layouts  8.14 us (8%)
  between operations  1.61 us (2%)
    pallas_call x11, Pallas kernels, call(): pl.pallas_call(kernel, grid=grid, out_shape=shapes, in_specs=in_specs, ou...  37.2 us
    all_to_all x1, blocking collectives, local(): lax.all_to_all(blocks, ('domain', 'band'), split_axis=0, concat_axis=0, t...  14.3 us
    unnamed x45, local copies, waits for them, and re-layouts  7.43 us
    all_to_all x1, starting transfers between devices, local(): lax.all_to_all(message, 'band', split_axis=0, concat_axis=0, tiled=True)  6.04 us
    ppermute x1, waiting for transfers between devices, local(): link_scaled = lax.ppermute(scaled, 'domain', link_pairs)  4.81 us
    ppermute x1, starting transfers between devices, local(): later_link = lax.ppermute(later_pass, 'domain', link_pairs)  4.34 us
    ppermute x3, starting transfers between devices, swapped(): lax.ppermute(values[k - 1], axis, [(i, i ^ k) for i in range(size)])  3.98 us
    ppermute x1, waiting for transfers between devices, local(): early_link = lax.ppermute(early_pass, 'domain', link_pairs)  3.96 us
  transfers between devices with their start and end apart: 15, of which 3 were waited for; matrix products, arithmetic and copies ran while one was open for 1% of the time, Pallas kernels for 31%

profile of v6, /device:TPU:1, one launch (start us, length us, event | category | flops | bytes accessed | tf_op | source)
XLA Modules:
  0.0 100.2 jit_solution(15682391552741285267)
XLA Ops:
  0.6 4.0 %shard_map.95 = (bf16[128,64,128]{2,1,0:T(8,128)(2,1)S(1)}, bf16[128,64,128]{2,1,0:T(8,128)(2,1)}, bf16[64,64,128]{2,1,0:T(8,128)(2,1)}, bf16[64,64,128]{2,1,0:T(8,128)(2,1)}, bf16[100,64,128]{2,1,0:T(8,128)(2,1)}) custom-call(bf16[64,128,128]{2,1,0:T(8,128)(2,1)} %bitcast.12), custom_call_target="tpu_custom_call" | custom-call | flops 1100000 | bytes 1024 | tf_op jit(solution)/shard_map/pallas_call | solution.py:33
  4.8 6.0 %all-to-all-start = ((bf16[100,64,128]{2,1,0:T(8,128)(2,1)}), bf16[100,64,128]{2,1,0:T(8,128)(2,1)}, u32[]{:S(2)}, u32[]{:S(2)}) async-start(bf16[100,64,128]{2,1,0:T(8,128)(2,1)} %get-tuple-element.30), calls=%async_computation | async-start | bytes 3276800 | tf_op jit(solution)/shard_map/all_to_all | solution.py:358
  10.9 3.5 %collective-permute-start.1 = (bf16[64,64,128]{2,1,0:T(8,128)(2,1)}, bf16[64,64,128]{2,1,0:T(8,128)(2,1)}, u32[]{:S(2)}, u32[]{:S(2)}) collective-permute-start(bf16[64,64,128]{2,1,0:T(8,128)(2,1)} %get-tuple-element.24), channel_id=1, source_target_pairs={{4,8},{8,4},{5,9},{9,5},{6,10},{10,6},{7,11},{11,7},{20,24},{24,20... | collective-permute-start | bytes 3145736 | tf_op jit(solution)/shard_map/ppermute | solution.py:359
  15.1 8.1 %shard_map.96 = (bf16[8,64,128]{2,1,0:T(8,128)(2,1)S(1)}, f32[8,64,128]{2,1,0:T(8,128)S(1)}, bf16[8,64,128]{2,1,0:T(8,128)(2,1)S(1)}) custom-call(s32[384]{0:T(512)S(1)} %get-tuple-element.47.words_ref, s32[2]{0:T(128)S(1)} %pad_add_fusion.ids_ref, bf16[128,64,128]{2,1,0:T(8,128)(2,1)S(1)} %get-tuple-element.22.xt_ref, bf16[384,16,128]{2,1,0:T(8,128)(2,1)} %p_hbm.3), custom_call_target="tpu_custom_call" | custom-call | flops 1100000 | bytes 1024 | tf_op jit(solution)/shard_map/pallas_call | solution.py:33
  23.3 2.3 %collective-permute-start.3 = (bf16[8,64,128]{2,1,0:T(8,128)(2,1)S(1)}, bf16[8,64,128]{2,1,0:T(8,128)(2,1)S(1)}, u32[]{:S(2)}, u32[]{:S(2)}) collective-permute-start(bf16[8,64,128]{2,1,0:T(8,128)(2,1)S(1)} %get-tuple-element.28), channel_id=1, source_target_pairs={{4,8},{8,4},{5,9},{9,5},{6,10},{10,6},{7,11},{11,7},{20,24},{24,20... | collective-permute-start | bytes 393224 | tf_op jit(solution)/shard_map/ppermute | solution.py:377
  26.4 3.6 %collective-permute-done.3.link_ref = bf16[8,64,128]{2,1,0:T(8,128)(2,1)S(1)} collective-permute-done((bf16[8,64,128]{2,1,0:T(8,128)(2,1)S(1)}, bf16[8,64,128]{2,1,0:T(8,128)(2,1)S(1)}, u32[]{:S(2)}, u32[]{:S(2)}) %collective-permute-start.3) | collective-permute-done | bytes 131104 | tf_op jit(solution)/shard_map/ppermute | solution.py:377
  30.7 1.9 %shard_map.97 = (bf16[8,64,128]{2,1,0:T(8,128)(2,1)}, bf16[8,64,128]{2,1,0:T(8,128)(2,1)S(1)}, bf16[10,64,128]{2,1,0:T(8,128)(2,1)}, bf16[10,64,128]{2,1,0:T(8,128)(2,1)}, bf16[10,64,128]{2,1,0:T(8,128)(2,1)}) custom-call(s32[2]{0:T(128)} %copy-done.12, bf16[128,64,128]{2,1,0:T(8,128)(2,1)S(1)} %get-tuple-element.22.xt_ref, ...), custom_call_target="tpu_custom_call" | custom-call | flops 1100000 | bytes 1024 | tf_op jit(solution)/shard_map/pallas_call | solution.py:33
  32.7 2.2 %collective-permute-start.4 = (bf16[8,64,128]{2,1,0:T(8,128)(2,1)}, bf16[8,64,128]{2,1,0:T(8,128)(2,1)S(1)}, u32[]{:S(2)}, u32[]{:S(2)}) collective-permute-start(bf16[8,64,128]{2,1,0:T(8,128)(2,1)} %get-tuple-element.29.own_ref), channel_id=1, source_target_pairs={{4,8},{8,4},{5,9},{9,5},{6,10},{10,6},{7,11},{11,7},{20,24},{24,20... | collective-permute-start | bytes 393224 | tf_op jit(solution)/shard_map/ppermute | solution.py:389
  34.9 4.8 %collective-permute-done.4.unread.link_ref = bf16[8,64,128]{2,1,0:T(8,128)(2,1)S(1)} collective-permute-done((bf16[8,64,128]{2,1,0:T(8,128)(2,1)}, bf16[8,64,128]{2,1,0:T(8,128)(2,1)S(1)}, u32[]{:S(2)}, u32[]{:S(2)}) %collective-permute-start.4) | collective-permute-done | bytes 131104 | tf_op jit(solution)/shard_map/ppermute | solution.py:389
  40.4 1.9 %collective-permute-start.6 = (bf16[64,64,128]{2,1,0:T(8,128)(2,1)}, bf16[64,64,128]{2,1,0:T(8,128)(2,1)}, u32[]{:S(2)}, u32[]{:S(2)}) collective-permute-start(bf16[64,64,128]{2,1,0:T(8,128)(2,1)} %shard_map.98), channel_id=1, source_target_pairs={{4,8},{8,4},{5,9},{9,5},{6,10},{10,6},{7,11},{11,7},{20,24},{24,20... | collective-permute-start | bytes 3145736 | tf_op jit(solution)/shard_map/ppermute | solution.py:402
  42.3 1.8 %collective-permute-start.7 = (bf16[10,64,128]{2,1,0:T(8,128)(2,1)S(1)}, bf16[10,64,128]{2,1,0:T(8,128)(2,1)S(1)}, u32[]{:S(2)}, u32[]{:S(2)}) collective-permute-start(bf16[10,64,128]{2,1,0:T(8,128)(2,1)S(1)} %copy-done.21), channel_id=1, source_target_pairs={{0,1},{1,0},{2,3},{3,2},{4,5},{5,4},{6,7},{7,6},{8,9},{9,8},{10,11... | collective-permute-start | bytes 491528 | tf_op jit(solution)/shard_map/ppermute | solution.py:327
  44.1 2.1 %collective-permute-start.8 = (bf16[10,64,128]{2,1,0:T(8,128)(2,1)S(1)}, bf16[10,64,128]{2,1,0:T(8,128)(2,1)S(1)}, u32[]{:S(2)}, u32[]{:S(2)}) collective-permute-start(bf16[10,64,128]{2,1,0:T(8,128)(2,1)S(1)} %copy-done.20), channel_id=1, source_target_pairs={{0,2},{1,3},{2,0},{3,1},{4,6},{5,7},{6,4},{7,5},{8,10},{9,11},{10,... | collective-permute-start | bytes 491528 | tf_op jit(solution)/shard_map/ppermute | solution.py:327
  48.1 8.5 %shard_map.99.unread.added_ref = f32[129,64,128]{2,1,0:T(8,128)S(1)} custom-call(s32[384]{0:T(512)S(1)} %get-tuple-element.46.words_ref, s32[2]{0:T(128)S(1)} %copy-done.13, bf16[384,16,128]{2,1,0:T(8,128)(2,1)S(1)} %copy-done.3, bf16[8,64,128]{2,1,0:T(8,128)(2,1)S(1)} %copy-done.6, bf16[8,64,128]{2,1,0:T(8,128)(2,1)S(1)} %copy-done.10, ...), custom_call_target="tpu_custom_call" | custom-call | flops 1100000 | bytes 1024 | tf_op jit(solution)/shard_map/pallas_call | solution.py:33
  56.6 2.0 %copy-done = f32[129,64,128]{2,1,0:T(8,128)} copy-done((f32[129,64,128]{2,1,0:T(8,128)}, f32[129,64,128]{2,1,0:T(8,128)S(1)}, u32[]{:S(2)}) %copy-start) | copy-done | bytes 4227096
  58.6 2.2 %copy-done.1 = f32[129,64,128]{2,1,0:T(8,128)S(1)} copy-done((f32[129,64,128]{2,1,0:T(8,128)S(1)}, f32[129,64,128]{2,1,0:T(8,128)}, u32[]{:S(2)}) %copy-start.1) | copy-done | bytes 4227096
  60.8 2.3 %shard_map.100 = (bf16[25,256,128]{2,1,0:T(8,128)(2,1)S(1)}, bf16[12,256,128]{2,1,0:T(8,128)(2,1)S(1)}) custom-call(s32[2]{0:T(128)S(1)} %copy-done.13, bf16[100,64,128]{2,1,0:T(8,128)(2,1)} %all-to-all-done.landed, f32[129,64,128]{2,1,0:T(8,128)S(1)} %copy-done.1, bf16[64,64,128]{2,1,0:T(8,128)(2,1)} %collective-permute-done.6.unread_too.late_ref), custom_call_target="tpu_custom_call" | custom-call | flops 1100000 | bytes 1024 | tf_op jit(solution)/shard_map/pallas_call | solution.py:33
  63.0 4.3 %collective-permute-start.13 = (bf16[12,256,128]{2,1,0:T(8,128)(2,1)S(1)}, bf16[12,256,128]{2,1,0:T(8,128)(2,1)S(1)}, u32[]{:S(2)}, u32[]{:S(2)}) collective-permute-start(bf16[12,256,128]{2,1,0:T(8,128)(2,1)S(1)} %get-tuple-element.40), channel_id=1, source_target_pairs={{4,8},{8,4},{5,9},{9,5},{6,10},{10,6},{7,11},{11,7},{20,24},{24,20... | collective-permute-start | bytes 2359304 | tf_op jit(solution)/shard_map/ppermute | solution.py:430
  67.5 7.6 %shard_map.101 = (bf16[64,128,128]{2,1,0:T(8,128)(2,1)}, f32[8,128]{1,0:T(8,128)S(1)}) custom-call(bf16[128,64,128]{2,1,0:T(8,128)(2,1)S(1)} %get-tuple-element.22.xt_ref, bf16[128,64,128]{2,1,0:T(8,128)(2,1)} %collective-permute-done.unread_too.core_ref, bf16[64,64,128]{2,1,0:T(8,128)(2,1)} %collective-permute-done.1.unread.early_ref, ...), custom_call_target="tpu_custom_call" | custom-call | flops 1100000 | bytes 1024 | tf_op jit(solution)/shard_map/pallas_call | solution.py:33
  75.1 0.9 shard_map.102
  76.0 1.9 %collective-permute-start.11 = (bf16[4,256,128]{2,1,0:T(8,128)(2,1)S(1)}, bf16[4,256,128]{2,1,0:T(8,128)(2,1)S(1)}, u32[]{:S(2)}, u32[]{:S(2)}) collective-permute-start(bf16[4,256,128]{2,1,0:T(8,128)(2,1)S(1)} %get-tuple-element.39), channel_id=1, source_target_pairs={{4,8},{8,4},{5,9},{9,5},{6,10},{10,6},{7,11},{11,7},{20,24},{24,20... | collective-permute-start | bytes 786440 | tf_op jit(solution)/shard_map/ppermute | solution.py:470
  78.1 1.7 %shard_map.103.begun_ref = f32[2,256,256]{2,1,0:T(8,128)S(1)} custom-call(s32[2]{0:T(128)S(1)} %copy-done.13, bf16[25,256,128]{2,1,0:T(8,128)(2,1)S(1)} %get-tuple-element.31.unread.after_ref.all_ref, bf16[12,256,128]{2,1,0:T(8,128)(2,1)S(1)} %collective-permute-done.12.core_ref, bf16[12,256,128]{2,1,0:T(8,128)(2,1)S(1)} %collective-permute-done.13.link_ref, ...), custom_call_target="tpu_custom_call" | custom-call | flops 1100000 | bytes 1024 | tf_op jit(solution)/shard_map/pallas_call | solution.py:33
  79.8 4.0 %collective-permute-done.11.link_ref = bf16[4,256,128]{2,1,0:T(8,128)(2,1)S(1)} collective-permute-done((bf16[4,256,128]{2,1,0:T(8,128)(2,1)S(1)}, bf16[4,256,128]{2,1,0:T(8,128)(2,1)S(1)}, u32[]{:S(2)}, u32[]{:S(2)}) %collective-permute-start.11) | collective-permute-done | bytes 262176 | tf_op jit(solution)/shard_map/ppermute | solution.py:470
  83.7 1.4 %shard_map.104 = bf16[16,64,128]{2,1,0:T(8,128)(2,1)S(1)} custom-call(s32[2]{0:T(128)S(1)} %copy-done.13, bf16[9,256,128]{2,1,0:T(8,128)(2,1)S(1)} %get-tuple-element.38.unread.all_ref, bf16[4,256,128]{2,1,0:T(8,128)(2,1)S(1)} %collective-permute-done.10.core_ref, bf16[4,256,128]{2,1,0:T(8,128)(2,1)S(1)} %collective-permute-done.11.link_ref, ...), custom_call_target="tpu_custom_call" | custom-call | flops 1100000 | bytes 1024 | tf_op jit(solution)/shard_map/pallas_call | solution.py:33
  85.2 14.3 %all_to_all.10.parts_ref = bf16[16,64,128]{2,1,0:T(8,128)(2,1)S(1)} all-to-all(bf16[16,64,128]{2,1,0:T(8,128)(2,1)S(1)} %shard_map.104), channel_id=1, replica_groups=mesh['groups'=2,'domain'=4,'band'=4] {'domain','band'}, dimensions={0} | all-to-all | bytes 524288 | tf_op jit(solution)/shard_map/all_to_all | solution.py:493
  (66 shorter events, 5.3 us)
Async XLA Ops:
  4.7 25.3 %collective-permute-start = (bf16[128,64,128]{2,1,0:T(8,128)(2,1)}, bf16[128,64,128]{2,1,0:T(8,128)(2,1)}, u32[]{:S(2)}, u32[]{:S(2)}) collective-permute-start(bf16[128,64,128]{2,1,0:T(8,128)(2,1)} %get-tuple-element.23), channel_id=1, source_target_pairs={{0,4},{4,0},{8,12},{12,8},{1,5},{5,1},{9,13},{13,9},{2,6},{6,2},{1... | collective-permute-start | bytes 6291464 | tf_op jit(solution)/shard_map/ppermute | solution.py:360
  4.8 53.7 %all-to-all-start = ((bf16[100,64,128]{2,1,0:T(8,128)(2,1)}), bf16[100,64,128]{2,1,0:T(8,128)(2,1)}, u32[]{:S(2)}, u32[]{:S(2)}) async-start(bf16[100,64,128]{2,1,0:T(8,128)(2,1)} %get-tuple-element.30), calls=%async_computation | async-start | bytes 3276800 | tf_op jit(solution)/shard_map/all_to_all | solution.py:358
  10.9 14.7 %copy-start.16 = (f32[256,16]{0,1:T(8,128)S(1)}, f32[256,16]{0,1:T(8,128)}, u32[]{:S(2)}) copy-start(f32[256,16]{0,1:T(8,128)} %param.14) | copy-start | bytes 49156
  10.9 19.1 %collective-permute-start.1 = (bf16[64,64,128]{2,1,0:T(8,128)(2,1)}, bf16[64,64,128]{2,1,0:T(8,128)(2,1)}, u32[]{:S(2)}, u32[]{:S(2)}) collective-permute-start(bf16[64,64,128]{2,1,0:T(8,128)(2,1)} %get-tuple-element.24), channel_id=1, source_target_pairs={{4,8},{8,4},{5,9},{9,5},{6,10},{10,6},{7,11},{11,7},{20,24},{24,20... | collective-permute-start | bytes 3145736 | tf_op jit(solution)/shard_map/ppermute | solution.py:359
  15.1 15.0 %copy-start.12 = (s32[2]{0:T(128)}, s32[2]{0:T(128)S(1)}, u32[]{:S(2)}) copy-start(s32[2]{0:T(128)S(1)} %pad_add_fusion.ids_ref) | copy-start | bytes 28
  23.2 3.2 %collective-permute-start.2 = (bf16[8,64,128]{2,1,0:T(8,128)(2,1)S(1)}, bf16[8,64,128]{2,1,0:T(8,128)(2,1)S(1)}, u32[]{:S(2)}, u32[]{:S(2)}) collective-permute-start(bf16[8,64,128]{2,1,0:T(8,128)(2,1)S(1)} %get-tuple-element.27), channel_id=1, source_target_pairs={{0,4},{4,0},{8,12},{12,8},{1,5},{5,1},{9,13},{13,9},{2,6},{6,2},{1... | collective-permute-start | bytes 393224 | tf_op jit(solution)/shard_map/ppermute | solution.py:378
  23.3 6.7 %collective-permute-start.3 = (bf16[8,64,128]{2,1,0:T(8,128)(2,1)S(1)}, bf16[8,64,128]{2,1,0:T(8,128)(2,1)S(1)}, u32[]{:S(2)}, u32[]{:S(2)}) collective-permute-start(bf16[8,64,128]{2,1,0:T(8,128)(2,1)S(1)} %get-tuple-element.28), channel_id=1, source_target_pairs={{4,8},{8,4},{5,9},{9,5},{6,10},{10,6},{7,11},{11,7},{20,24},{24,20... | collective-permute-start | bytes 393224 | tf_op jit(solution)/shard_map/ppermute | solution.py:377
  32.5 11.6 %copy-start.20 = (bf16[10,64,128]{2,1,0:T(8,128)(2,1)S(1)}, bf16[10,64,128]{2,1,0:T(8,128)(2,1)}, u32[]{:S(2)}) copy-start(bf16[10,64,128]{2,1,0:T(8,128)(2,1)} %get-tuple-element.36) | copy-start | bytes 491524
  32.5 13.6 %copy-start.19 = (bf16[10,64,128]{2,1,0:T(8,128)(2,1)S(1)}, bf16[10,64,128]{2,1,0:T(8,128)(2,1)}, u32[]{:S(2)}) copy-start(bf16[10,64,128]{2,1,0:T(8,128)(2,1)} %get-tuple-element.37) | copy-start | bytes 491524
  32.6 13.7 %copy-start.3 = (bf16[384,16,128]{2,1,0:T(8,128)(2,1)S(1)}, bf16[384,16,128]{2,1,0:T(8,128)(2,1)}, u32[]{:S(2)}) copy-start(bf16[384,16,128]{2,1,0:T(8,128)(2,1)} %p_hbm.3) | copy-start | bytes 4718596
  32.6 13.7 %copy-start.10 = (bf16[8,64,128]{2,1,0:T(8,128)(2,1)S(1)}, bf16[8,64,128]{2,1,0:T(8,128)(2,1)}, u32[]{:S(2)}) copy-start(bf16[8,64,128]{2,1,0:T(8,128)(2,1)} %get-tuple-element.29.own_ref) | copy-start | bytes 393220
  32.6 13.7 %copy-start.13 = (s32[2]{0:T(128)S(1)}, s32[2]{0:T(128)}, u32[]{:S(2)}) copy-start(s32[2]{0:T(128)} %copy-done.12) | copy-start | bytes 28
  32.6 2.3 %collective-permute-start.5 = (bf16[8,64,128]{2,1,0:T(8,128)(2,1)}, bf16[8,64,128]{2,1,0:T(8,128)(2,1)S(1)}, u32[]{:S(2)}, u32[]{:S(2)}) collective-permute-start(bf16[8,64,128]{2,1,0:T(8,128)(2,1)} %get-tuple-element.29.own_ref), channel_id=1, source_target_pairs={{0,4},{4,0},{8,12},{12,8},{1,5},{5,1},{9,13},{13,9},{2,6},{6,2},{1... | collective-permute-start | bytes 393224 | tf_op jit(solution)/shard_map/ppermute | solution.py:390
  32.7 7.0 %collective-permute-start.4 = (bf16[8,64,128]{2,1,0:T(8,128)(2,1)}, bf16[8,64,128]{2,1,0:T(8,128)(2,1)S(1)}, u32[]{:S(2)}, u32[]{:S(2)}) collective-permute-start(bf16[8,64,128]{2,1,0:T(8,128)(2,1)} %get-tuple-element.29.own_ref), channel_id=1, source_target_pairs={{4,8},{8,4},{5,9},{9,5},{6,10},{10,6},{7,11},{11,7},{20,24},{24,20... | collective-permute-start | bytes 393224 | tf_op jit(solution)/shard_map/ppermute | solution.py:389
  40.4 18.2 %collective-permute-start.6 = (bf16[64,64,128]{2,1,0:T(8,128)(2,1)}, bf16[64,64,128]{2,1,0:T(8,128)(2,1)}, u32[]{:S(2)}, u32[]{:S(2)}) collective-permute-start(bf16[64,64,128]{2,1,0:T(8,128)(2,1)} %shard_map.98), channel_id=1, source_target_pairs={{4,8},{8,4},{5,9},{9,5},{6,10},{10,6},{7,11},{11,7},{20,24},{24,20... | collective-permute-start | bytes 3145736 | tf_op jit(solution)/shard_map/ppermute | solution.py:402
  42.3 32.8 %collective-permute-start.7 = (bf16[10,64,128]{2,1,0:T(8,128)(2,1)S(1)}, bf16[10,64,128]{2,1,0:T(8,128)(2,1)S(1)}, u32[]{:S(2)}, u32[]{:S(2)}) collective-permute-start(bf16[10,64,128]{2,1,0:T(8,128)(2,1)S(1)} %copy-done.21), channel_id=1, source_target_pairs={{0,1},{1,0},{2,3},{3,2},{4,5},{5,4},{6,7},{7,6},{8,9},{9,8},{10,11... | collective-permute-start | bytes 491528 | tf_op jit(solution)/shard_map/ppermute | solution.py:327
  44.1 31.0 %collective-permute-start.8 = (bf16[10,64,128]{2,1,0:T(8,128)(2,1)S(1)}, bf16[10,64,128]{2,1,0:T(8,128)(2,1)S(1)}, u32[]{:S(2)}, u32[]{:S(2)}) collective-permute-start(bf16[10,64,128]{2,1,0:T(8,128)(2,1)S(1)} %copy-done.20), channel_id=1, source_target_pairs={{0,2},{1,3},{2,0},{3,1},{4,6},{5,7},{6,4},{7,5},{8,10},{9,11},{10,... | collective-permute-start | bytes 491528 | tf_op jit(solution)/shard_map/ppermute | solution.py:327
  46.2 28.9 %collective-permute-start.9 = (bf16[10,64,128]{2,1,0:T(8,128)(2,1)S(1)}, bf16[10,64,128]{2,1,0:T(8,128)(2,1)S(1)}, u32[]{:S(2)}, u32[]{:S(2)}) collective-permute-start(bf16[10,64,128]{2,1,0:T(8,128)(2,1)S(1)} %copy-done.19), channel_id=1, source_target_pairs={{0,3},{1,2},{2,1},{3,0},{4,7},{5,6},{6,5},{7,4},{8,11},{9,10},{10,... | collective-permute-start | bytes 491528 | tf_op jit(solution)/shard_map/ppermute | solution.py:327
  48.1 19.4 %copy-start.4 = (f32[1,128,128]{2,1,0:T(8,128)S(1)}, f32[1,128,128]{2,1,0:T(8,128)}, u32[]{:S(2)}) copy-start(f32[1,128,128]{2,1,0:T(8,128)} %param.9) | copy-start | bytes 196612
  48.1 19.4 %copy-start.11 = (bf16[128,128]{1,0:T(8,128)(2,1)S(1)}, bf16[128,128]{1,0:T(8,128)(2,1)}, u32[]{:S(2)}) copy-start(bf16[128,128]{1,0:T(8,128)(2,1)} %constant.24.clone.ring_ref) | copy-start | bytes 98308
  63.0 15.0 %collective-permute-start.13 = (bf16[12,256,128]{2,1,0:T(8,128)(2,1)S(1)}, bf16[12,256,128]{2,1,0:T(8,128)(2,1)S(1)}, u32[]{:S(2)}, u32[]{:S(2)}) collective-permute-start(bf16[12,256,128]{2,1,0:T(8,128)(2,1)S(1)} %get-tuple-element.40), channel_id=1, source_target_pairs={{4,8},{8,4},{5,9},{9,5},{6,10},{10,6},{7,11},{11,7},{20,24},{24,20... | collective-permute-start | bytes 2359304 | tf_op jit(solution)/shard_map/ppermute | solution.py:430
  67.4 10.7 %collective-permute-start.12 = (bf16[12,256,128]{2,1,0:T(8,128)(2,1)S(1)}, bf16[12,256,128]{2,1,0:T(8,128)(2,1)S(1)}, u32[]{:S(2)}, u32[]{:S(2)}) collective-permute-start(bf16[12,256,128]{2,1,0:T(8,128)(2,1)S(1)} %get-tuple-element.40), channel_id=1, source_target_pairs={{0,4},{4,0},{8,12},{12,8},{1,5},{5,1},{9,13},{13,9},{2,6},{6,2},{1... | collective-permute-start | bytes 2359304 | tf_op jit(solution)/shard_map/ppermute | solution.py:431
  76.0 7.7 %collective-permute-start.11 = (bf16[4,256,128]{2,1,0:T(8,128)(2,1)S(1)}, bf16[4,256,128]{2,1,0:T(8,128)(2,1)S(1)}, u32[]{:S(2)}, u32[]{:S(2)}) collective-permute-start(bf16[4,256,128]{2,1,0:T(8,128)(2,1)S(1)} %get-tuple-element.39), channel_id=1, source_target_pairs={{4,8},{8,4},{5,9},{9,5},{6,10},{10,6},{7,11},{11,7},{20,24},{24,20... | collective-permute-start | bytes 786440 | tf_op jit(solution)/shard_map/ppermute | solution.py:470
  78.0 5.8 %collective-permute-start.10 = (bf16[4,256,128]{2,1,0:T(8,128)(2,1)S(1)}, bf16[4,256,128]{2,1,0:T(8,128)(2,1)S(1)}, u32[]{:S(2)}, u32[]{:S(2)}) collective-permute-start(bf16[4,256,128]{2,1,0:T(8,128)(2,1)S(1)} %get-tuple-element.39), channel_id=1, source_target_pairs={{0,4},{4,0},{8,12},{12,8},{1,5},{5,1},{9,13},{13,9},{2,6},{6,2},{1... | collective-permute-start | bytes 786440 | tf_op jit(solution)/shard_map/ppermute | solution.py:471
  (13 other events, 58.7 us)

commit v7 on v6

--- a/solution.py
+++ b/solution.py
@@ -48,7 +48,7 @@
     return copy
 
 
-def pack_kernel(first, x_hbm, xt, xt_hbm, early_half, late_half, message, x, in_sems, out_sems):
+def pack_kernel(first, x_hbm, xt, xt_hbm, early, late, message, x, in_sems, out_sems):
     states, lines, _ = x.shape
     bands = in_sems.shape[0]
     share = lines // bands
@@ -73,17 +73,23 @@
                 xt[y0 : y0 + ROWS, s0 : s0 + ROWS, :] = turned
         send(c * share + first, count, message, c * (count + 1))
         send(c * share, 1, message, (c + bands - 1) % bands * (count + 1) + count)
-        if c == bands // 2 - 1:
-            send(0, lines // 2, early_half, 0)
-    send(lines // 2, lines // 2, late_half, 0)
+        if (c + 1) * share == early.shape[0]:
+            send(0, early.shape[0], early, 0)
+    send(early.shape[0], late.shape[0], late, 0)
     send(0, lines, xt_hbm, 0)
     for copy in sends:
         copy.wait()
 
 
-def project_kernel(words_ref, ids_ref, xt_ref, p_hbm, core_ref, own_ref, link_ref, total, p_ref, sems):
+def bases(ids_ref, groups):
+    odd, upper = ids_ref[0] & 1, (ids_ref[0] >> 1) & 1
+    return [2 * groups * side for side in (1 - odd, odd, 1 - upper, upper)]
+
+
+def project_kernel(words_ref, ids_ref, xt_ref, p_hbm, mine_ref, core_ref, link_ref, *refs):
+    far_refs, (total, p_ref, sems) = refs[:-3], refs[-3:]
     slots, proj_count, _ = p_ref.shape
-    groups, states, _ = own_ref.shape
+    groups, states = mine_ref.shape[0] // 3, mine_ref.shape[1]
     per_group = LANES // proj_count
     chunks = sems.shape[0]
     size = slots // chunks
@@ -111,62 +117,59 @@
     for c in range(chunks):
         loads[c].wait()
         lax.fori_loop(c * size // unroll, (c + 1) * size // unroll, body, 0)
-    odd = ids_ref[0] & 1
-    core_first, link_first = (1 - odd) * 2 * groups, odd * 2 * groups
-
-    def turned(group):
-        tiles = [total[group * per_group + u] for u in range(per_group)]
-        return jnp.concatenate(tiles, axis=0).T
-
+
+    for g in range(3 * groups):
+        tiles = [total[g * per_group + u] for u in range(per_group)]
+        mine_ref[g] = jnp.concatenate(tiles, axis=0).T
+    sides = bases(ids_ref, groups)
     for g in range(groups):
-        core_ref[g] = turned(core_first + g).astype(BF16)
-        link_ref[g] = turned(link_first + g).astype(BF16)
-        own_ref[g] = turned(groups + g)
-
-
-def hand_on(value, unread, unread_too, same):
-    pass
-
-
-def owner_kernel(
-    first, ids_ref, xt_ref, own_ref, core_ref, link_ref, energy_ref, unread, unread_too, scaled_ref, whole_ref, *messages
-):
+        own = mine_ref[groups + g].astype(BF16)
+        for side, ref in zip(sides[:2], (core_ref, link_ref)):
+            ref[g] = mine_ref[side + g].astype(BF16)
+            ref[groups + g] = own
+        for side, ref in zip(sides[2:], far_refs):
+            ref[g] = mine_ref[side + g].astype(BF16)
+
+
+def nonlocal_kernel(first, fars, words_ref, ids_ref, xt_ref, p_hbm, energy_ref, mine_ref, core_ref, link_ref, *refs):
+    far_refs, (_, _, _, out_ref, whole_ref, done_ref, _, *messages, total, atoms, p_ref, sem) = refs[:fars], refs[fars:]
+    slots, proj_count, _ = p_ref.shape
+    groups, states = mine_ref.shape[0] // 3, mine_ref.shape[1]
+    per_group = LANES // proj_count
+    lines = out_ref.shape[0]
+    unroll = 16
+    load = start(pltpu.make_async_copy(p_hbm, p_ref, sem))
+    done_ref[...] = jnp.zeros_like(done_ref)
+
+    def clear(i, carry):
+        out_ref[i] = jnp.zeros((states, LANES), F32)
+        return carry
+
+    lax.fori_loop(0, lines, clear, 0)
+    total[...] = mine_ref[...]
+    sides = bases(ids_ref, groups)
+    for g in range(groups):
+        total[groups + g] += core_ref[g].astype(F32) + link_ref[g].astype(F32)
+        for side, ref in zip(sides[:2], (core_ref, link_ref)):
+            total[side + g] += ref[groups + g].astype(F32)
+        for side, ref in zip(sides[2:], far_refs):
+            total[side + g] += ref[g].astype(F32)
+    last = energy_ref.shape[0] - 1
+    for g in range(3 * groups):
+        row = jnp.clip((ids_ref[0] - 1) * groups + g, 0, last)
+        tile = (total[g] * energy_ref[pl.ds(row, 1), :]).astype(BF16)
+        for u in range(per_group):
+            atoms[g * per_group + u] = tile[:, u * proj_count : (u + 1) * proj_count]
+    for g in range(groups):
+        whole_ref[g] = total[groups + g].astype(BF16)
     share = xt_ref.shape[0] // (len(messages) + 1)
-    groups = own_ref.shape[0]
-    held = messages[0].shape[0] - first
-    row = ids_ref[0] * groups
-    for g in range(groups):
-        whole = own_ref[g] + core_ref[g].astype(F32) + link_ref[g].astype(F32)
-        scaled_ref[g] = (whole * energy_ref[pl.ds(row + g, 1), :]).astype(BF16)
-        whole_ref[g] = whole.astype(BF16)
+    held = groups // (len(messages) + 1)
     for k, message in enumerate(messages, 1):
         to = ids_ref[1] ^ k
         for i in range(first):
             message[i] = xt_ref[to * share + i]
         for i in range(held):
             message[first + i] = whole_ref[to * held + i]
-
-
-def nonlocal_kernel(words_ref, ids_ref, p_hbm, core_ref, own_ref, link_ref, out_ref, atoms, p_ref, sem):
-    slots, proj_count, _ = p_ref.shape
-    groups, states, _ = own_ref.shape
-    per_group = LANES // proj_count
-    lines = out_ref.shape[0]
-    unroll = 16
-    load = start(pltpu.make_async_copy(p_hbm, p_ref, sem))
-
-    def clear(i, carry):
-        out_ref[i] = jnp.zeros((states, LANES), F32)
-        return carry
-
-    lax.fori_loop(0, lines, clear, 0)
-    odd = ids_ref[0] & 1
-
-    for first, ref in (((1 - odd) * 2 * groups, core_ref), (groups, own_ref), (odd * 2 * groups, link_ref)):
-        for g in range(groups):
-            tile = ref[g]
-            for u in range(per_group):
-                atoms[(first + g) * per_group + u] = tile[:, u * proj_count : (u + 1) * proj_count]
     load.wait()
 
     def body(i, carry):
@@ -180,13 +183,13 @@
     lax.fori_loop(0, slots // unroll, body, 0)
 
 
-def stencil_kernel(xt_ref, core_ref, early_ref, late_ref, added_ref, pot_ref, ring_ref, unread, out_ref, done_ref):
+def stencil_kernel(early_steps, xt_ref, core_ref, early_ref, late_ref, added_ref, pot_ref, ring_ref, unread, out_ref, done_ref):
     states, here, _ = out_ref.shape
     lines = xt_ref.shape[0]
     done_ref[...] = jnp.zeros_like(done_ref)
     step = pl.program_id(0)
     y0 = step * here
-    early = step < pl.num_programs(0) // 2
+    early = step < early_steps
     for s0 in range(0, states, ROWS):
         rows = slice(s0, s0 + ROWS)
         results = []
@@ -210,7 +213,7 @@
     copy.wait()
 
 
-def later_kernel(bands, ids_ref, landed, unread, unread_too, all_ref, pass_hbm, sems, pass_sem):
+def later_kernel(bands, ids_ref, landed, unread, all_ref, pass_hbm, sems, pass_sem):
     count, states = all_ref.shape[0], landed.shape[1]
     loads = [
         start(
@@ -321,6 +324,9 @@
 
     core_pairs = [(i, i ^ 1) for i in range(domains) if i ^ 1 < domains]
     link_pairs = [(i, ((i + 1) ^ 1) - 1) for i in range(1, domains) if ((i + 1) ^ 1) - 1 < domains]
+    near_far = [(i, i ^ 2) for i in range(domains) if i ^ 2 < domains]
+    next_far = [(i, ((i + 2) ^ 2) - 2) for i in range(2, domains) if ((i + 2) ^ 2) - 2 < domains]
+    far_pairs = [pairs for pairs in (near_far, next_far) if pairs]
 
     def swapped(values, axis):
         size = lax.axis_size(axis)
@@ -338,8 +344,9 @@
     eye = np.eye(cols_z, dtype=np.float32)
     ring = jnp.asarray(3.0 * eye - 0.5 * (np.roll(eye, 1, axis=0) + np.roll(eye, -1, axis=0)), dtype=BF16)
 
-    line_shape, half_shape = (lines, states, cols_z), (lines // 2, states, cols_z)
-    xt, xt_far, early_half, late_half, message = call(
+    late_lines = lines // 4
+    line_shape, late_shape = (lines, states, cols_z), (late_lines, states, cols_z)
+    xt, xt_far, early_part, late_part, message = call(
         58,
         functools.partial(pack_kernel, first),
         (),
@@ -348,25 +355,27 @@
         [
             (line_shape, BF16),
             (line_shape, BF16),
-            (half_shape, BF16),
-            (half_shape, BF16),
+            ((lines - late_lines, states, cols_z), BF16),
+            (late_shape, BF16),
             ((bands * (rest + 1), states, cols_z), BF16),
         ],
         [pltpu.VMEM((states, lines, cols_z), BF16), copies((bands,)), copies((2 * bands + 3,))],
         (field,),
     )
     landed = lax.all_to_all(message, "band", split_axis=0, concat_axis=0, tiled=True)
-    link_early = lax.ppermute(early_half, "domain", link_pairs)
+    link_early = lax.ppermute(early_part, "domain", link_pairs)
     core_field = lax.ppermute(xt_far, "domain", core_pairs)
 
     group_shape = (groups, states, LANES)
-    to_core, own, to_link = call(
+    mine, to_core, to_link, *to_far = call(
         50,
         project_kernel,
         (),
         [SCALARS, SCALARS, NEAR, FAR],
-        [WHOLE, NEAR, WHOLE],
-        [(group_shape, BF16), (group_shape, F32), (group_shape, BF16)],
+        [NEAR] + [WHOLE] * (2 + len(far_pairs)),
+        [((3 * groups, states, LANES), F32)]
+        + [((2 * groups, states, LANES), BF16)] * 2
+        + [(group_shape, BF16)] * len(far_pairs),
         [
             pltpu.VMEM((3 * atoms_here + 1, proj_count, states), F32),
             pltpu.VMEM(projectors.shape, BF16),
@@ -375,72 +384,57 @@
         (project_words, ids, xt, projectors),
     )
     from_link = lax.ppermute(to_link, "domain", link_pairs)
+    from_far = [lax.ppermute(value, "domain", pairs) for value, pairs in zip(to_far, far_pairs)]
     from_core = lax.ppermute(to_core, "domain", core_pairs)
-    scaled, whole, *messages = call(
-        59,
-        functools.partial(owner_kernel, first),
-        (),
-        [SCALARS, NEAR, NEAR, WHOLE, WHOLE, WHOLE, UNREAD, UNREAD],
-        [WHOLE, NEAR] + [WHOLE] * (bands - 1),
-        [(group_shape, BF16)] * 2 + [((first + group_share, states, cols_z), BF16)] * (bands - 1),
-        [],
-        (ids, xt, own, from_core, from_link, energy, link_early, core_field),
-    )
-    link_scaled = lax.ppermute(scaled, "domain", link_pairs)
-    core_scaled = lax.ppermute(scaled, "domain", core_pairs)
-    (late_half,) = call(
-        59,
-        hand_on,
-        (),
-        [UNREAD] * 3,
-        [UNREAD],
-        [(half_shape, BF16)],
-        [],
-        (late_half, link_scaled, core_scaled),
-        aliases={0: 0},
-    )
-    link_late = lax.ppermute(late_half, "domain", link_pairs)
-    early = swapped(messages, "band")
-
-    (added,) = call(
-        32,
-        nonlocal_kernel,
-        (),
-        [SCALARS, SCALARS, FAR, WHOLE, WHOLE, WHOLE],
-        [WHOLE],
-        [((lines + 1, states, cols_z), F32)],
+    added, whole, summed_up, late_part, *messages = call(
+        32,
+        functools.partial(nonlocal_kernel, first, len(far_pairs)),
+        (),
+        [SCALARS, SCALARS, NEAR, FAR, WHOLE, NEAR, WHOLE, WHOLE] + [WHOLE] * len(far_pairs) + [UNREAD] * 3,
+        [WHOLE, NEAR, WHOLE, UNREAD] + [WHOLE] * (bands - 1),
+        [((lines + 1, states, cols_z), F32), (group_shape, BF16), ((8, LANES), F32), (late_shape, BF16)]
+        + [((first + group_share, states, cols_z), BF16)] * (bands - 1),
         [
+            pltpu.VMEM((3 * groups, states, LANES), F32),
             pltpu.VMEM((3 * atoms_here, states, proj_count), BF16),
             pltpu.VMEM(projectors.shape, BF16),
             copies,
         ],
-        (nonlocal_words, ids, projectors, core_scaled, scaled, link_scaled),
-    )
+        (
+            nonlocal_words, ids, xt, projectors, energy, mine, from_core, from_link, *from_far,
+            link_early[0, :ROWS], core_field[0, :ROWS], late_part,
+        ),
+        aliases={10 + len(far_pairs): 3},
+        micros=30,
+    )
+    link_late = lax.ppermute(late_part, "domain", link_pairs)
+    early = swapped(messages, "band")
 
     later_all, later_pass = call(
         32,
         functools.partial(later_kernel, bands),
         (),
-        [SCALARS, FAR, UNREAD, UNREAD],
+        [SCALARS, FAR, UNREAD],
         [NEAR, FAR],
         [((rest + 1, total_states, cols_z), BF16), ((rest // 2, total_states, cols_z), BF16)],
         [copies((bands,)), copies],
-        (ids, landed, added, link_late),
+        (ids, landed, summed_up),
+        micros=10,
     )
     later_link = lax.ppermute(later_pass, "domain", link_pairs)
     later_core = lax.ppermute(later_pass, "domain", core_pairs)
 
-    steps = lines // ROWS
+    steps, early_steps = lines // ROWS, (lines - late_lines) // ROWS
     block = pl.BlockSpec((ROWS, states, cols_z), lambda i: (i, 0, 0))
     applied, done = call(
         32,
-        stencil_kernel,
+        functools.partial(stencil_kernel, early_steps),
         (steps,),
         [
             NEAR,
             block,
-            pl.BlockSpec((ROWS, states, cols_z), lambda i: (jnp.minimum(i, steps // 2 - 1), 0, 0)),
-            pl.BlockSpec((ROWS, states, cols_z), lambda i: (jnp.maximum(i - steps // 2, 0), 0, 0)),
+            pl.BlockSpec((ROWS, states, cols_z), lambda i: (jnp.minimum(i, early_steps - 1), 0, 0)),
+            pl.BlockSpec((ROWS, states, cols_z), lambda i: (jnp.maximum(i - early_steps, 0), 0, 0)),
             WHOLE,
             pl.BlockSpec((ROWS, cols_z), lambda i: (i, 0)),
             WHOLE,

time: 102 us -> 97.7 us (0.958)
  waiting for transfers between devices: 12.4 us -> 7.61 us
  local copies, waits for them, and re-layouts: 8.14 us -> 5.62 us
  starting transfers between devices: 26.5 us -> 28.1 us
    unnamed x45 -> x23, local copies, waits for them, and re-layouts: 7.43 us -> 4.17 us
    ppermute x4 -> x3, waiting for transfers between devices: 4.82 us -> 1.63 us  [the longest x1 0.96 us: local(): link_early = lax.ppermute(early_part, 'domain', link_pairs)]
    all_to_all x1, starting transfers between devices: 6.04 us -> 4.6 us  [local(): lax.all_to_all(message, 'band', split_axis=0, concat_axis=0, tiled=True)]
    squeeze x0 -> x2, local copies, waits for them, and re-layouts: none -> 1.35 us  [the longest x1 0.68 us: local(): core_field[0, :ROWS]]
    ppermute x1, waiting for transfers between devices: 3.96 us -> 2.69 us  [local(): early_link = lax.ppermute(early_pass, 'domain', link_pairs)]
    ppermute x1, starting transfers between devices: 1.92 us -> 3.18 us  [local(): early_link = lax.ppermute(early_pass, 'domain', link_pairs)]
    ppermute x1, starting transfers between devices: 0.07 us -> 1.15 us  [local(): from_core = lax.ppermute(to_core, 'domain', core_pairs)]
    pallas_call x11 -> x9, Pallas kernels: 37.2 us -> 38.1 us  [call(): pl.pallas_call(kernel, grid=grid, out_shape=shapes, in_specs=in_specs, ou...]
  transfers between devices with their start and end apart: 15 -> 14, of which waited for: 3 -> 4; matrix products, arithmetic and copies ran while one was open for 1% -> 2% of each run, Pallas kernels for 31% -> 33%
where the time goes in v7:
time: 97.7 us; the launch traced here: 96.3 us
  Pallas kernels  38.1 us (39%)
  starting transfers between devices  28.1 us (29%)
  blocking collectives  15.1 us (15%)
  waiting for transfers between devices  7.61 us (8%)
  local copies, waits for them, and re-layouts  5.62 us (6%)
  between operations  1.56 us (2%)
    pallas_call x9, Pallas kernels, call(): pl.pallas_call(kernel, grid=grid, out_shape=shapes, in_specs=in_specs, ou...  38.1 us
    all_to_all x1, blocking collectives, local(): lax.all_to_all(blocks, ('domain', 'band'), split_axis=0, concat_axis=0, t...  15.1 us
    all_to_all x1, starting transfers between devices, local(): lax.all_to_all(message, 'band', split_axis=0, concat_axis=0, tiled=True)  4.6 us
    ppermute x1, starting transfers between devices, local(): later_link = lax.ppermute(later_pass, 'domain', link_pairs)  4.5 us
    ppermute x1, starting transfers between devices, local(): link_early = lax.ppermute(early_part, 'domain', link_pairs)  4.5 us
    unnamed x23, local copies, waits for them, and re-layouts  4.17 us
    ppermute x3, starting transfers between devices, swapped(): lax.ppermute(values[k - 1], axis, [(i, i ^ k) for i in range(size)])  4.13 us
    ppermute x1, waiting for transfers between devices, local(): from_link = lax.ppermute(to_link, 'domain', link_pairs)  3.28 us
  transfers between devices with their start and end apart: 14, of which 4 were waited for; matrix products, arithmetic and copies ran while one was open for 2% of the time, Pallas kernels for 33%

profile of v7, /device:TPU:1, one launch (start us, length us, event | category | flops | bytes accessed | tf_op | source)
XLA Modules:
  0.0 96.3 jit_solution(9117641670176263328)
XLA Ops:
  0.6 4.1 %shard_map.95 = (bf16[128,64,128]{2,1,0:T(8,128)(2,1)S(1)}, bf16[128,64,128]{2,1,0:T(8,128)(2,1)}, bf16[96,64,128]{2,1,0:T(8,128)(2,1)}, bf16[32,64,128]{2,1,0:T(8,128)(2,1)}, bf16[100,64,128]{2,1,0:T(8,128)(2,1)}) custom-call(bf16[64,128,128]{2,1,0:T(8,128)(2,1)} %bitcast.18), custom_call_target="tpu_custom_call" | custom-call | flops 1100000 | bytes 1024 | tf_op jit(solution)/shard_map/pallas_call | solution.py:33
  4.9 4.5 %collective-permute-start.1 = (bf16[96,64,128]{2,1,0:T(8,128)(2,1)}, bf16[96,64,128]{2,1,0:T(8,128)(2,1)}, u32[]{:S(2)}, u32[]{:S(2)}) collective-permute-start(bf16[96,64,128]{2,1,0:T(8,128)(2,1)} %get-tuple-element.27), channel_id=1, source_target_pairs={{4,8},{8,4},{5,9},{9,5},{6,10},{10,6},{7,11},{11,7},{20,24},{24,20... | collective-permute-start | bytes 4718600 | tf_op jit(solution)/shard_map/ppermute | solution.py:366
  9.4 4.6 %all-to-all-start = ((bf16[100,64,128]{2,1,0:T(8,128)(2,1)}), bf16[100,64,128]{2,1,0:T(8,128)(2,1)}, u32[]{:S(2)}, u32[]{:S(2)}) async-start(bf16[100,64,128]{2,1,0:T(8,128)(2,1)} %get-tuple-element.35), calls=%async_computation | async-start | bytes 3276800 | tf_op jit(solution)/shard_map/all_to_all | solution.py:365
  14.8 9.2 %shard_map.96 = (f32[24,64,128]{2,1,0:T(8,128)S(1)}, bf16[16,64,128]{2,1,0:T(8,128)(2,1)}, bf16[16,64,128]{2,1,0:T(8,128)(2,1)}, bf16[8,64,128]{2,1,0:T(8,128)(2,1)}) custom-call(s32[384]{0:T(512)S(1)} %get-tuple-element.52.words_ref, s32[2]{0:T(128)S(1)} %pad_add_fusion.ids_ref, bf16[128,64,128]{2,1,0:T(8,128)(2,1)S(1)} %get-tuple-element.25.xt_ref, ...), custom_call_target="tpu_custom_call" | custom-call | flops 1100000 | bytes 1024 | tf_op jit(solution)/shard_map/pallas_call | solution.py:33
  24.1 1.1 %collective-permute-start.2 = (bf16[16,64,128]{2,1,0:T(8,128)(2,1)}, bf16[16,64,128]{2,1,0:T(8,128)(2,1)S(1)}, u32[]{:S(2)}, u32[]{:S(2)}) collective-permute-start(bf16[16,64,128]{2,1,0:T(8,128)(2,1)} %get-tuple-element.29), channel_id=1, source_target_pairs={{0,4},{4,0},{8,12},{12,8},{1,5},{5,1},{9,13},{13,9},{2,6},{6,2},{1... | collective-permute-start | bytes 786440 | tf_op jit(solution)/shard_map/ppermute | solution.py:388
  25.3 2.6 %collective-permute-start.3 = (bf16[16,64,128]{2,1,0:T(8,128)(2,1)}, bf16[16,64,128]{2,1,0:T(8,128)(2,1)}, u32[]{:S(2)}, u32[]{:S(2)}) collective-permute-start(bf16[16,64,128]{2,1,0:T(8,128)(2,1)} %get-tuple-element.30), channel_id=1, source_target_pairs={{4,8},{8,4},{5,9},{9,5},{6,10},{10,6},{7,11},{11,7},{20,24},{24,20... | collective-permute-start | bytes 786440 | tf_op jit(solution)/shard_map/ppermute | solution.py:386
  28.1 1.0 %collective-permute-done.1.early_ref = bf16[96,64,128]{2,1,0:T(8,128)(2,1)} collective-permute-done((bf16[96,64,128]{2,1,0:T(8,128)(2,1)}, bf16[96,64,128]{2,1,0:T(8,128)(2,1)}, u32[]{:S(2)}, u32[]{:S(2)}) %collective-permute-start.1) | collective-permute-done | bytes 1572896 | tf_op jit(solution)/shard_map/ppermute | solution.py:366
  30.4 3.3 %collective-permute-done.3.link_ref = bf16[16,64,128]{2,1,0:T(8,128)(2,1)} collective-permute-done((bf16[16,64,128]{2,1,0:T(8,128)(2,1)}, bf16[16,64,128]{2,1,0:T(8,128)(2,1)}, u32[]{:S(2)}, u32[]{:S(2)}) %collective-permute-start.3) | collective-permute-done | bytes 262176 | tf_op jit(solution)/shard_map/ppermute | solution.py:386
  33.7 1.4 %copy-done.1 = bf16[384,16,128]{2,1,0:T(8,128)(2,1)S(1)} copy-done((bf16[384,16,128]{2,1,0:T(8,128)(2,1)S(1)}, bf16[384,16,128]{2,1,0:T(8,128)(2,1)}, u32[]{:S(2)}) %copy-start.1) | copy-done | bytes 1572888
  35.1 10.0 %shard_map.97 = (f32[129,64,128]{2,1,0:T(8,128)S(1)}, bf16[8,64,128]{2,1,0:T(8,128)(2,1)S(1)}, f32[8,128]{1,0:T(8,128)S(1)}, bf16[32,64,128]{2,1,0:T(8,128)(2,1)...) custom-call(s32[384]{0:T(512)S(1)} %get-tuple-element.53.words_ref, ...), custom_call_target="tpu_custom_call", output_to_operand_aliasing={{3}: (11, {})} | custom-call | flops 32999999488 | bytes 1024 | tf_op jit(solution)/shard_map/pallas_call | solution.py:33
  45.2 2.0 %copy-done = f32[129,64,128]{2,1,0:T(8,128)} copy-done((f32[129,64,128]{2,1,0:T(8,128)}, f32[129,64,128]{2,1,0:T(8,128)S(1)}, u32[]{:S(2)}) %copy-start) | copy-done | bytes 4227096
  47.8 1.6 %collective-permute-start.6 = (bf16[10,64,128]{2,1,0:T(8,128)(2,1)}, bf16[10,64,128]{2,1,0:T(8,128)(2,1)S(1)}, u32[]{:S(2)}, u32[]{:S(2)}) collective-permute-start(bf16[10,64,128]{2,1,0:T(8,128)(2,1)} %get-tuple-element.41), channel_id=1, source_target_pairs={{0,1},{1,0},{2,3},{3,2},{4,5},{5,4},{6,7},{7,6},{8,9},{9,8},{10,11... | collective-permute-start | bytes 491528 | tf_op jit(solution)/shard_map/ppermute | solution.py:333
  49.4 2.3 %collective-permute-start.7 = (bf16[10,64,128]{2,1,0:T(8,128)(2,1)}, bf16[10,64,128]{2,1,0:T(8,128)(2,1)S(1)}, u32[]{:S(2)}, u32[]{:S(2)}) collective-permute-start(bf16[10,64,128]{2,1,0:T(8,128)(2,1)} %get-tuple-element.42), channel_id=1, source_target_pairs={{0,2},{1,3},{2,0},{3,1},{4,6},{5,7},{6,4},{7,5},{8,10},{9,11},{10,... | collective-permute-start | bytes 491528 | tf_op jit(solution)/shard_map/ppermute | solution.py:333
  51.9 3.2 %collective-permute-start.5 = (bf16[32,64,128]{2,1,0:T(8,128)(2,1)}, bf16[32,64,128]{2,1,0:T(8,128)(2,1)S(1)}, u32[]{:S(2)}, u32[]{:S(2)}) collective-permute-start(bf16[32,64,128]{2,1,0:T(8,128)(2,1)} %get-tuple-element.33), channel_id=1, source_target_pairs={{4,8},{8,4},{5,9},{9,5},{6,10},{10,6},{7,11},{11,7},{20,24},{24,20... | collective-permute-start | bytes 1572872 | tf_op jit(solution)/shard_map/ppermute | solution.py:410
  55.2 2.3 %shard_map.98 = (bf16[25,256,128]{2,1,0:T(8,128)(2,1)S(1)}, bf16[12,256,128]{2,1,0:T(8,128)(2,1)S(1)}) custom-call(s32[2]{0:T(128)S(1)} %pad_add_fusion.ids_ref, bf16[100,64,128]{2,1,0:T(8,128)(2,1)} %all-to-all-done.landed, f32[8,128]{1,0:T(8,128)S(1)} %get-tuple-element.36.unread), custom_call_target="tpu_custom_call" | custom-call | flops 11000000512 | bytes 1024 | tf_op jit(solution)/shard_map/pallas_call | solution.py:33
  57.5 4.5 %collective-permute-start.12 = (bf16[12,256,128]{2,1,0:T(8,128)(2,1)S(1)}, bf16[12,256,128]{2,1,0:T(8,128)(2,1)S(1)}, u32[]{:S(2)}, u32[]{:S(2)}) collective-permute-start(bf16[12,256,128]{2,1,0:T(8,128)(2,1)S(1)} %get-tuple-element.46), channel_id=1, source_target_pairs={{4,8},{8,4},{5,9},{9,5},{6,10},{10,6},{7,11},{11,7},{20,24},{24,20... | collective-permute-start | bytes 2359304 | tf_op jit(solution)/shard_map/ppermute | solution.py:424
  62.7 7.6 %shard_map.99 = (bf16[64,128,128]{2,1,0:T(8,128)(2,1)}, f32[8,128]{1,0:T(8,128)S(1)}) custom-call(bf16[128,64,128]{2,1,0:T(8,128)(2,1)S(1)} %get-tuple-element.25.xt_ref, bf16[128,64,128]{2,1,0:T(8,128)(2,1)} %collective-permute-done.core_ref, bf16[96,64,128]{2,1,0:T(8,128)(2,1)} %collective-permute-done.1.early_ref, ...), custom_call_target="tpu_custom_call" | custom-call | flops 1100000 | bytes 1024 | tf_op jit(solution)/shard_map/pallas_call | solution.py:33
  70.3 0.9 shard_map.100
  71.3 3.2 %collective-permute-start.10 = (bf16[4,256,128]{2,1,0:T(8,128)(2,1)S(1)}, bf16[4,256,128]{2,1,0:T(8,128)(2,1)S(1)}, u32[]{:S(2)}, u32[]{:S(2)}) collective-permute-start(bf16[4,256,128]{2,1,0:T(8,128)(2,1)S(1)} %get-tuple-element.45), channel_id=1, source_target_pairs={{4,8},{8,4},{5,9},{9,5},{6,10},{10,6},{7,11},{11,7},{20,24},{24,20... | collective-permute-start | bytes 786440 | tf_op jit(solution)/shard_map/ppermute | solution.py:464
  74.5 1.7 %shard_map.101.begun_ref = f32[2,256,256]{2,1,0:T(8,128)S(1)} custom-call(s32[2]{0:T(128)S(1)} %pad_add_fusion.ids_ref, bf16[25,256,128]{2,1,0:T(8,128)(2,1)S(1)} %get-tuple-element.37.unread.after_ref.all_ref, bf16[12,256,128]{2,1,0:T(8,128)(2,1)S(1)} %collective-permute-done.11.core_ref, bf16[12,256,128]{2,1,0:T(8,128)(2,1)S(1)} %collective-permute-done.12.link_ref, ...), custom_call_target="tpu_custom_call" | custom-call | flops 1100000 | bytes 1024 | tf_op jit(solution)/shard_map/pallas_call | solution.py:33
  76.3 2.7 %collective-permute-done.10.link_ref = bf16[4,256,128]{2,1,0:T(8,128)(2,1)S(1)} collective-permute-done((bf16[4,256,128]{2,1,0:T(8,128)(2,1)S(1)}, bf16[4,256,128]{2,1,0:T(8,128)(2,1)S(1)}, u32[]{:S(2)}, u32[]{:S(2)}) %collective-permute-start.10) | collective-permute-done | bytes 262176 | tf_op jit(solution)/shard_map/ppermute | solution.py:464
  79.0 1.4 %shard_map.102 = bf16[16,64,128]{2,1,0:T(8,128)(2,1)S(1)} custom-call(s32[2]{0:T(128)S(1)} %pad_add_fusion.ids_ref, bf16[9,256,128]{2,1,0:T(8,128)(2,1)S(1)} %get-tuple-element.44.unread.all_ref, bf16[4,256,128]{2,1,0:T(8,128)(2,1)S(1)} %collective-permute-done.9.core_ref, bf16[4,256,128]{2,1,0:T(8,128)(2,1)S(1)} %collective-permute-done.10.link_ref, ...), custom_call_target="tpu_custom_call" | custom-call | flops 1100000 | bytes 1024 | tf_op jit(solution)/shard_map/pallas_call | solution.py:33
  80.4 15.1 %all_to_all.10.parts_ref = bf16[16,64,128]{2,1,0:T(8,128)(2,1)S(1)} all-to-all(bf16[16,64,128]{2,1,0:T(8,128)(2,1)S(1)} %shard_map.102), channel_id=1, replica_groups=mesh['groups'=2,'domain'=4,'band'=4] {'domain','band'}, dimensions={0} | all-to-all | bytes 524288 | tf_op jit(solution)/shard_map/all_to_all | solution.py:487
  95.5 0.7 shard_map.103
  (43 shorter events, 3.5 us)
Async XLA Ops:
  4.8 10.0 %copy-start.7 = (s32[384]{0:T(512)S(1)}, s32[384]{0:T(512)}, u32[]{:S(2)}) copy-start(s32[384]{0:T(512)} %param.12) | copy-start | bytes 4612
  4.8 10.0 %copy-start.8 = (s32[384]{0:T(512)S(1)}, s32[384]{0:T(512)}, u32[]{:S(2)}) copy-start(s32[384]{0:T(512)} %param.11) | copy-start | bytes 4612
  4.8 24.9 %collective-permute-start = (bf16[128,64,128]{2,1,0:T(8,128)(2,1)}, bf16[128,64,128]{2,1,0:T(8,128)(2,1)}, u32[]{:S(2)}, u32[]{:S(2)}) collective-permute-start(bf16[128,64,128]{2,1,0:T(8,128)(2,1)} %get-tuple-element.26), channel_id=1, source_target_pairs={{0,4},{4,0},{8,12},{12,8},{1,5},{5,1},{9,13},{13,9},{2,6},{6,2},{1... | collective-permute-start | bytes 6291464 | tf_op jit(solution)/shard_map/ppermute | solution.py:367
  4.9 24.1 %collective-permute-start.1 = (bf16[96,64,128]{2,1,0:T(8,128)(2,1)}, bf16[96,64,128]{2,1,0:T(8,128)(2,1)}, u32[]{:S(2)}, u32[]{:S(2)}) collective-permute-start(bf16[96,64,128]{2,1,0:T(8,128)(2,1)} %get-tuple-element.27), channel_id=1, source_target_pairs={{4,8},{8,4},{5,9},{9,5},{6,10},{10,6},{7,11},{11,7},{20,24},{24,20... | collective-permute-start | bytes 4718600 | tf_op jit(solution)/shard_map/ppermute | solution.py:366
  9.4 45.7 %all-to-all-start = ((bf16[100,64,128]{2,1,0:T(8,128)(2,1)}), bf16[100,64,128]{2,1,0:T(8,128)(2,1)}, u32[]{:S(2)}, u32[]{:S(2)}) async-start(bf16[100,64,128]{2,1,0:T(8,128)(2,1)} %get-tuple-element.35), calls=%async_computation | async-start | bytes 3276800 | tf_op jit(solution)/shard_map/all_to_all | solution.py:365
  14.0 13.8 %copy-start.6 = (f32[256,16]{0,1:T(8,128)S(1)}, f32[256,16]{0,1:T(8,128)}, u32[]{:S(2)}) copy-start(f32[256,16]{0,1:T(8,128)} %param.14) | copy-start | bytes 49156
  24.0 6.4 %collective-permute-start.4 = (bf16[8,64,128]{2,1,0:T(8,128)(2,1)}, bf16[8,64,128]{2,1,0:T(8,128)(2,1)S(1)}, u32[]{:S(2)}, u32[]{:S(2)}) collective-permute-start(bf16[8,64,128]{2,1,0:T(8,128)(2,1)} %get-tuple-element.31), channel_id=1, source_target_pairs={{0,8},{4,12},{8,0},{12,4},{1,9},{5,13},{9,1},{13,5},{2,10},{6,14},... | collective-permute-start | bytes 393224 | tf_op jit(solution)/shard_map/ppermute | solution.py:387
  24.1 6.3 %collective-permute-start.2 = (bf16[16,64,128]{2,1,0:T(8,128)(2,1)}, bf16[16,64,128]{2,1,0:T(8,128)(2,1)S(1)}, u32[]{:S(2)}, u32[]{:S(2)}) collective-permute-start(bf16[16,64,128]{2,1,0:T(8,128)(2,1)} %get-tuple-element.29), channel_id=1, source_target_pairs={{0,4},{4,0},{8,12},{12,8},{1,5},{5,1},{9,13},{13,9},{2,6},{6,2},{1... | collective-permute-start | bytes 786440 | tf_op jit(solution)/shard_map/ppermute | solution.py:388
  25.3 8.4 %collective-permute-start.3 = (bf16[16,64,128]{2,1,0:T(8,128)(2,1)}, bf16[16,64,128]{2,1,0:T(8,128)(2,1)}, u32[]{:S(2)}, u32[]{:S(2)}) collective-permute-start(bf16[16,64,128]{2,1,0:T(8,128)(2,1)} %get-tuple-element.30), channel_id=1, source_target_pairs={{4,8},{8,4},{5,9},{9,5},{6,10},{10,6},{7,11},{11,7},{20,24},{24,20... | collective-permute-start | bytes 786440 | tf_op jit(solution)/shard_map/ppermute | solution.py:386
  33.7 1.4 %copy-start.1 = (bf16[384,16,128]{2,1,0:T(8,128)(2,1)S(1)}, bf16[384,16,128]{2,1,0:T(8,128)(2,1)}, u32[]{:S(2)}) copy-start(bf16[384,16,128]{2,1,0:T(8,128)(2,1)} %p_hbm.3) | copy-start | bytes 4718596
  45.1 2.0 %copy-start = (f32[129,64,128]{2,1,0:T(8,128)}, f32[129,64,128]{2,1,0:T(8,128)S(1)}, u32[]{:S(2)}) copy-start(f32[129,64,128]{2,1,0:T(8,128)S(1)} %get-tuple-element.34.added_ref) | copy-start | bytes 12681220
  47.8 22.5 %collective-permute-start.6 = (bf16[10,64,128]{2,1,0:T(8,128)(2,1)}, bf16[10,64,128]{2,1,0:T(8,128)(2,1)S(1)}, u32[]{:S(2)}, u32[]{:S(2)}) collective-permute-start(bf16[10,64,128]{2,1,0:T(8,128)(2,1)} %get-tuple-element.41), channel_id=1, source_target_pairs={{0,1},{1,0},{2,3},{3,2},{4,5},{5,4},{6,7},{7,6},{8,9},{9,8},{10,11... | collective-permute-start | bytes 491528 | tf_op jit(solution)/shard_map/ppermute | solution.py:333
  49.4 20.9 %collective-permute-start.7 = (bf16[10,64,128]{2,1,0:T(8,128)(2,1)}, bf16[10,64,128]{2,1,0:T(8,128)(2,1)S(1)}, u32[]{:S(2)}, u32[]{:S(2)}) collective-permute-start(bf16[10,64,128]{2,1,0:T(8,128)(2,1)} %get-tuple-element.42), channel_id=1, source_target_pairs={{0,2},{1,3},{2,0},{3,1},{4,6},{5,7},{6,4},{7,5},{8,10},{9,11},{10,... | collective-permute-start | bytes 491528 | tf_op jit(solution)/shard_map/ppermute | solution.py:333
  51.7 18.6 %collective-permute-start.8 = (bf16[10,64,128]{2,1,0:T(8,128)(2,1)}, bf16[10,64,128]{2,1,0:T(8,128)(2,1)S(1)}, u32[]{:S(2)}, u32[]{:S(2)}) collective-permute-start(bf16[10,64,128]{2,1,0:T(8,128)(2,1)} %get-tuple-element.43), channel_id=1, source_target_pairs={{0,3},{1,2},{2,1},{3,0},{4,7},{5,6},{6,5},{7,4},{8,11},{9,10},{10,... | collective-permute-start | bytes 491528 | tf_op jit(solution)/shard_map/ppermute | solution.py:333
  51.9 10.8 %collective-permute-start.5 = (bf16[32,64,128]{2,1,0:T(8,128)(2,1)}, bf16[32,64,128]{2,1,0:T(8,128)(2,1)S(1)}, u32[]{:S(2)}, u32[]{:S(2)}) collective-permute-start(bf16[32,64,128]{2,1,0:T(8,128)(2,1)} %get-tuple-element.33), channel_id=1, source_target_pairs={{4,8},{8,4},{5,9},{9,5},{6,10},{10,6},{7,11},{11,7},{20,24},{24,20... | collective-permute-start | bytes 1572872 | tf_op jit(solution)/shard_map/ppermute | solution.py:410
  55.1 7.5 %slice-start = ((s8[4227072]{0:T(1024)(128)(4,1)}), s8[4194304]{0:T(1024)(128)(4,1)S(1)}, s32[]{:S(2)}) async-start(s8[4227072]{0:T(1024)(128)(4,1)} %bitcast.13), calls=%async_computation.2 | async-start | bytes 8388608
  55.2 7.5 %slice-start.1 = ((s8[4227072]{0:T(1024)(128)(4,1)}), s8[32768]{0:T(1024)(128)(4,1)S(1)}, s32[]{:S(2)}) async-start(s8[4227072]{0:T(1024)(128)(4,1)} %bitcast.13), calls=%async_computation.3 | async-start | bytes 65536
  55.2 7.5 %copy-start.2 = (f32[1,128,128]{2,1,0:T(8,128)S(1)}, f32[1,128,128]{2,1,0:T(8,128)}, u32[]{:S(2)}) copy-start(f32[1,128,128]{2,1,0:T(8,128)} %param.9) | copy-start | bytes 196612
  55.2 7.5 %copy-start.3 = (bf16[128,128]{1,0:T(8,128)(2,1)S(1)}, bf16[128,128]{1,0:T(8,128)(2,1)}, u32[]{:S(2)}) copy-start(bf16[128,128]{1,0:T(8,128)(2,1)} %constant.24.clone.ring_ref) | copy-start | bytes 98308
  57.5 17.0 %collective-permute-start.12 = (bf16[12,256,128]{2,1,0:T(8,128)(2,1)S(1)}, bf16[12,256,128]{2,1,0:T(8,128)(2,1)S(1)}, u32[]{:S(2)}, u32[]{:S(2)}) collective-permute-start(bf16[12,256,128]{2,1,0:T(8,128)(2,1)S(1)} %get-tuple-element.46), channel_id=1, source_target_pairs={{4,8},{8,4},{5,9},{9,5},{6,10},{10,6},{7,11},{11,7},{20,24},{24,20... | collective-permute-start | bytes 2359304 | tf_op jit(solution)/shard_map/ppermute | solution.py:424
  62.7 11.9 %collective-permute-start.11 = (bf16[12,256,128]{2,1,0:T(8,128)(2,1)S(1)}, bf16[12,256,128]{2,1,0:T(8,128)(2,1)S(1)}, u32[]{:S(2)}, u32[]{:S(2)}) collective-permute-start(bf16[12,256,128]{2,1,0:T(8,128)(2,1)S(1)} %get-tuple-element.46), channel_id=1, source_target_pairs={{0,4},{4,0},{8,12},{12,8},{1,5},{5,1},{9,13},{13,9},{2,6},{6,2},{1... | collective-permute-start | bytes 2359304 | tf_op jit(solution)/shard_map/ppermute | solution.py:425
  62.7 7.6 %copy-start.5 = (bf16[8,64,128]{2,1,0:T(8,128)(2,1)S(1)}, bf16[8,64,128]{2,1,0:T(8,128)(2,1)}, u32[]{:S(2)}) copy-start(bf16[8,64,128]{2,1,0:T(8,128)(2,1)} %copy-done.4) | copy-start | bytes 393220
  71.3 7.7 %collective-permute-start.10 = (bf16[4,256,128]{2,1,0:T(8,128)(2,1)S(1)}, bf16[4,256,128]{2,1,0:T(8,128)(2,1)S(1)}, u32[]{:S(2)}, u32[]{:S(2)}) collective-permute-start(bf16[4,256,128]{2,1,0:T(8,128)(2,1)S(1)} %get-tuple-element.45), channel_id=1, source_target_pairs={{4,8},{8,4},{5,9},{9,5},{6,10},{10,6},{7,11},{11,7},{20,24},{24,20... | collective-permute-start | bytes 786440 | tf_op jit(solution)/shard_map/ppermute | solution.py:464
  74.4 4.5 %collective-permute-start.9 = (bf16[4,256,128]{2,1,0:T(8,128)(2,1)S(1)}, bf16[4,256,128]{2,1,0:T(8,128)(2,1)S(1)}, u32[]{:S(2)}, u32[]{:S(2)}) collective-permute-start(bf16[4,256,128]{2,1,0:T(8,128)(2,1)S(1)} %get-tuple-element.45), channel_id=1, source_target_pairs={{0,4},{4,0},{8,12},{12,8},{1,5},{5,1},{9,13},{13,9},{2,6},{6,2},{1... | collective-permute-start | bytes 786440 | tf_op jit(solution)/shard_map/ppermute | solution.py:465
  (1 other events, 0.7 us)

commit v8 on v7

--- a/solution.py
+++ b/solution.py
@@ -86,8 +86,8 @@
     return [2 * groups * side for side in (1 - odd, odd, 1 - upper, upper)]
 
 
-def project_kernel(words_ref, ids_ref, xt_ref, p_hbm, mine_ref, core_ref, link_ref, *refs):
-    far_refs, (total, p_ref, sems) = refs[:-3], refs[-3:]
+def project_kernel(words_ref, ids_ref, xt_ref, p_hbm, handed, p_ref, mine_ref, same, core_ref, link_ref, *refs):
+    far_refs, (total, sems) = refs[:-2], refs[-2:]
     slots, proj_count, _ = p_ref.shape
     groups, states = mine_ref.shape[0] // 3, mine_ref.shape[1]
     per_group = LANES // proj_count
@@ -131,15 +131,13 @@
             ref[g] = mine_ref[side + g].astype(BF16)
 
 
-def nonlocal_kernel(first, fars, words_ref, ids_ref, xt_ref, p_hbm, energy_ref, mine_ref, core_ref, link_ref, *refs):
-    far_refs, (_, _, _, out_ref, whole_ref, done_ref, _, *messages, total, atoms, p_ref, sem) = refs[:fars], refs[fars:]
+def nonlocal_kernel(first, fars, words_ref, ids_ref, xt_ref, p_ref, energy_ref, mine_ref, core_ref, link_ref, *refs):
+    far_refs, (_, _, out_ref, whole_ref, *messages, total, atoms) = refs[:fars], refs[fars:]
     slots, proj_count, _ = p_ref.shape
     groups, states = mine_ref.shape[0] // 3, mine_ref.shape[1]
     per_group = LANES // proj_count
     lines = out_ref.shape[0]
     unroll = 16
-    load = start(pltpu.make_async_copy(p_hbm, p_ref, sem))
-    done_ref[...] = jnp.zeros_like(done_ref)
 
     def clear(i, carry):
         out_ref[i] = jnp.zeros((states, LANES), F32)
@@ -170,7 +168,6 @@
             message[i] = xt_ref[to * share + i]
         for i in range(held):
             message[first + i] = whole_ref[to * held + i]
-    load.wait()
 
     def body(i, carry):
         for u in range(unroll):
@@ -183,7 +180,7 @@
     lax.fori_loop(0, slots // unroll, body, 0)
 
 
-def stencil_kernel(early_steps, xt_ref, core_ref, early_ref, late_ref, added_ref, pot_ref, ring_ref, unread, out_ref, done_ref):
+def stencil_kernel(early_steps, xt_ref, core_ref, early_ref, late_ref, added_ref, pot_ref, ring_ref, out_ref, done_ref):
     states, here, _ = out_ref.shape
     lines = xt_ref.shape[0]
     done_ref[...] = jnp.zeros_like(done_ref)
@@ -228,7 +225,7 @@
     pass_half(ids_ref, all_ref, pass_hbm, pass_sem)
 
 
-def early_kernel(bands, share, ids_ref, xt_ref, whole_ref, after_ref, unread, *refs):
+def early_kernel(bands, share, ids_ref, xt_ref, whole_ref, after_ref, *refs):
     pieces, (all_ref, pass_hbm, projs_ref, sems, pass_sem) = refs[: bands - 1], refs[bands - 1 :]
     states = xt_ref.shape[1]
     band = ids_ref[1]
@@ -344,7 +341,7 @@
     eye = np.eye(cols_z, dtype=np.float32)
     ring = jnp.asarray(3.0 * eye - 0.5 * (np.roll(eye, 1, axis=0) + np.roll(eye, -1, axis=0)), dtype=BF16)
 
-    late_lines = lines // 4
+    late_lines = lines // 2
     line_shape, late_shape = (lines, states, cols_z), (late_lines, states, cols_z)
     xt, xt_far, early_part, late_part, message = call(
         58,
@@ -367,62 +364,46 @@
     core_field = lax.ppermute(xt_far, "domain", core_pairs)
 
     group_shape = (groups, states, LANES)
-    mine, to_core, to_link, *to_far = call(
+    near_projectors, mine, late_part, to_core, to_link, *to_far = call(
         50,
         project_kernel,
         (),
-        [SCALARS, SCALARS, NEAR, FAR],
-        [NEAR] + [WHOLE] * (2 + len(far_pairs)),
-        [((3 * groups, states, LANES), F32)]
+        [SCALARS, SCALARS, NEAR, FAR, UNREAD],
+        [NEAR, NEAR, UNREAD] + [WHOLE] * (2 + len(far_pairs)),
+        [(projectors.shape, BF16), ((3 * groups, states, LANES), F32), (late_shape, BF16)]
         + [((2 * groups, states, LANES), BF16)] * 2
         + [(group_shape, BF16)] * len(far_pairs),
         [
             pltpu.VMEM((3 * atoms_here + 1, proj_count, states), F32),
-            pltpu.VMEM(projectors.shape, BF16),
             copies((4,)),
         ],
-        (project_words, ids, xt, projectors),
+        (project_words, ids, xt, projectors, late_part),
+        aliases={4: 2},
+        micros=10,
     )
     from_link = lax.ppermute(to_link, "domain", link_pairs)
     from_far = [lax.ppermute(value, "domain", pairs) for value, pairs in zip(to_far, far_pairs)]
     from_core = lax.ppermute(to_core, "domain", core_pairs)
-    added, whole, summed_up, late_part, *messages = call(
+    link_late = lax.ppermute(late_part, "domain", link_pairs)
+    added, whole, *messages = call(
         32,
         functools.partial(nonlocal_kernel, first, len(far_pairs)),
         (),
-        [SCALARS, SCALARS, NEAR, FAR, WHOLE, NEAR, WHOLE, WHOLE] + [WHOLE] * len(far_pairs) + [UNREAD] * 3,
-        [WHOLE, NEAR, WHOLE, UNREAD] + [WHOLE] * (bands - 1),
-        [((lines + 1, states, cols_z), F32), (group_shape, BF16), ((8, LANES), F32), (late_shape, BF16)]
+        [SCALARS, SCALARS, NEAR, NEAR, WHOLE, NEAR, WHOLE, WHOLE] + [WHOLE] * len(far_pairs) + [UNREAD] * 2,
+        [WHOLE, NEAR] + [WHOLE] * (bands - 1),
+        [((lines + 1, states, cols_z), F32), (group_shape, BF16)]
         + [((first + group_share, states, cols_z), BF16)] * (bands - 1),
         [
             pltpu.VMEM((3 * groups, states, LANES), F32),
             pltpu.VMEM((3 * atoms_here, states, proj_count), BF16),
-            pltpu.VMEM(projectors.shape, BF16),
-            copies,
         ],
         (
-            nonlocal_words, ids, xt, projectors, energy, mine, from_core, from_link, *from_far,
-            link_early[0, :ROWS], core_field[0, :ROWS], late_part,
+            nonlocal_words, ids, xt, near_projectors, energy, mine, from_core, from_link, *from_far,
+            link_early[0, :ROWS], core_field[0, :ROWS],
         ),
-        aliases={10 + len(far_pairs): 3},
         micros=30,
     )
-    link_late = lax.ppermute(late_part, "domain", link_pairs)
     early = swapped(messages, "band")
-
-    later_all, later_pass = call(
-        32,
-        functools.partial(later_kernel, bands),
-        (),
-        [SCALARS, FAR, UNREAD],
-        [NEAR, FAR],
-        [((rest + 1, total_states, cols_z), BF16), ((rest // 2, total_states, cols_z), BF16)],
-        [copies((bands,)), copies],
-        (ids, landed, summed_up),
-        micros=10,
-    )
-    later_link = lax.ppermute(later_pass, "domain", link_pairs)
-    later_core = lax.ppermute(later_pass, "domain", core_pairs)
 
     steps, early_steps = lines // ROWS, (lines - late_lines) // ROWS
     block = pl.BlockSpec((ROWS, states, cols_z), lambda i: (i, 0, 0))
@@ -438,19 +419,32 @@
             WHOLE,
             pl.BlockSpec((ROWS, cols_z), lambda i: (i, 0)),
             WHOLE,
-            UNREAD,
         ],
         [pl.BlockSpec((states, ROWS, cols_z), lambda i: (0, i, 0)), WHOLE],
         [((states, lines, cols_z), BF16), ((8, LANES), F32)],
         [],
-        (xt, core_field, link_early, link_late, added, pot, ring, later_all),
-    )
+        (xt, core_field, link_early, link_late, added, pot, ring),
+        micros=10,
+    )
+
+    later_all, later_pass = call(
+        32,
+        functools.partial(later_kernel, bands),
+        (),
+        [SCALARS, FAR, UNREAD],
+        [NEAR, FAR],
+        [((rest + 1, total_states, cols_z), BF16), ((rest // 2, total_states, cols_z), BF16)],
+        [copies((bands,)), copies],
+        (ids, landed, done),
+    )
+    later_link = lax.ppermute(later_pass, "domain", link_pairs)
+    later_core = lax.ppermute(later_pass, "domain", core_pairs)
 
     early_all, early_pass, projs = call(
         32,
         functools.partial(early_kernel, bands, share),
         (),
-        [SCALARS, NEAR, NEAR, NEAR, WHOLE] + [FAR] * (bands - 1),
+        [SCALARS, NEAR, NEAR, NEAR] + [FAR] * (bands - 1),
         [NEAR, FAR, NEAR],
         [
             ((first + 1, total_states, cols_z), BF16),
@@ -458,7 +452,7 @@
             ((group_share, total_states, LANES), BF16),
         ],
         [copies((2 * bands + 1,)), copies],
-        (ids, xt, whole, later_all, done, *early),
+        (ids, xt, whole, later_all, *early),
         micros=30,
     )
     early_link = lax.ppermute(early_pass, "domain", link_pairs)

time: 97.7 us -> 102 us (1.044)
  local copies, waits for them, and re-layouts: 5.62 us -> 16.3 us
  Pallas kernels: 38.1 us -> 35.1 us
  starting transfers between devices: 28.1 us -> 25.5 us
  waiting for transfers between devices: 7.61 us -> 5.22 us
  other arithmetic: 0.08 us -> 1.25 us
    unnamed x23 -> x37, local copies, waits for them, and re-layouts: 4.17 us -> 14.6 us
    ppermute x1, waiting for transfers between devices: 0.01 us -> 4.1 us  [local(): later_link = lax.ppermute(later_pass, 'domain', link_pairs)]
    ppermute x1, waiting for transfers between devices: 3.28 us -> 0.01 us  [local(): from_link = lax.ppermute(to_link, 'domain', link_pairs)]
    pallas_call x9, Pallas kernels: 38.1 us -> 35.1 us  [call(): pl.pallas_call(kernel, grid=grid, out_shape=shapes, in_specs=in_specs, ou...]
    ppermute x1, waiting for transfers between devices: 2.69 us -> 1.09 us  [local(): early_link = lax.ppermute(early_pass, 'domain', link_pairs)]
    all_to_all x1, starting transfers between devices: 4.6 us -> 6.04 us  [local(): lax.all_to_all(message, 'band', split_axis=0, concat_axis=0, tiled=True)]
    ppermute x1, starting transfers between devices: 3.18 us -> 1.92 us  [local(): early_link = lax.ppermute(early_pass, 'domain', link_pairs)]
    ppermute x1, starting transfers between devices: 4.5 us -> 3.45 us  [local(): link_early = lax.ppermute(early_part, 'domain', link_pairs)]
  transfers between devices with their start and end apart: 14 -> 14, of which waited for: 4 -> 2; matrix products, arithmetic and copies ran while one was open for 2% -> 4% of each run, Pallas kernels for 33% -> 29%
where the time goes in v8:
time: 102 us; the launch traced here: 101 us
  Pallas kernels  35.1 us (34%)
  starting transfers between devices  25.5 us (25%)
  local copies, waits for them, and re-layouts  16.3 us (16%)
  blocking collectives  15.8 us (15%)
  waiting for transfers between devices  5.22 us (5%)
  between operations  1.53 us (2%)
  other arithmetic  1.25 us (1%)
    pallas_call x9, Pallas kernels, call(): pl.pallas_call(kernel, grid=grid, out_shape=shapes, in_specs=in_specs, ou...  35.1 us
    all_to_all x1, blocking collectives, local(): lax.all_to_all(blocks, ('domain', 'band'), split_axis=0, concat_axis=0, t...  15.8 us
    unnamed x37, local copies, waits for them, and re-layouts  14.6 us
    all_to_all x1, starting transfers between devices, local(): lax.all_to_all(message, 'band', split_axis=0, concat_axis=0, tiled=True)  6.04 us
    ppermute x1, waiting for transfers between devices, local(): later_link = lax.ppermute(later_pass, 'domain', link_pairs)  4.1 us
    ppermute x1, starting transfers between devices, local(): later_link = lax.ppermute(later_pass, 'domain', link_pairs)  4.04 us
    ppermute x3, starting transfers between devices, swapped(): lax.ppermute(values[k - 1], axis, [(i, i ^ k) for i in range(size)])  3.65 us
    ppermute x1, starting transfers between devices, local(): link_early = lax.ppermute(early_part, 'domain', link_pairs)  3.45 us
  transfers between devices with their start and end apart: 14, of which 2 were waited for; matrix products, arithmetic and copies ran while one was open for 4% of the time, Pallas kernels for 29%

profile of v8, /device:TPU:1, one launch (start us, length us, event | category | flops | bytes accessed | tf_op | source)
XLA Modules:
  0.0 100.7 jit_solution(14713458566212882322)
XLA Ops:
  0.6 4.0 %shard_map.95 = (bf16[128,64,128]{2,1,0:T(8,128)(2,1)S(1)}, bf16[128,64,128]{2,1,0:T(8,128)(2,1)}, bf16[64,64,128]{2,1,0:T(8,128)(2,1)}, bf16[64,64,128]{2,1,0:T(8,128)(2,1)}, bf16[100,64,128]{2,1,0:T(8,128)(2,1)}) custom-call(bf16[64,128,128]{2,1,0:T(8,128)(2,1)} %bitcast.16), custom_call_target="tpu_custom_call" | custom-call | flops 1100000 | bytes 1024 | tf_op jit(solution)/shard_map/pallas_call | solution.py:33
  4.7 1.4 %copy-done.2 = bf16[128,64,128]{2,1,0:T(8,128)(2,1)} copy-done((bf16[128,64,128]{2,1,0:T(8,128)(2,1)}, bf16[128,64,128]{2,1,0:T(8,128)(2,1)S(1)}, u32[]{:S(2)}) %copy-start.2) | copy-done | bytes 2097176
  6.1 6.0 %all-to-all-start = ((bf16[100,64,128]{2,1,0:T(8,128)(2,1)}), bf16[100,64,128]{2,1,0:T(8,128)(2,1)S(1)}, u32[]{:S(2)}, u32[]{:S(2)}) async-start(bf16[100,64,128]{2,1,0:T(8,128)(2,1)} %get-tuple-element.38), calls=%async_computation | async-start | bytes 3276800 | tf_op jit(solution)/shard_map/all_to_all | solution.py:362
  12.1 3.4 %collective-permute-start.1 = (bf16[64,64,128]{2,1,0:T(8,128)(2,1)}, bf16[64,64,128]{2,1,0:T(8,128)(2,1)S(1)}, u32[]{:S(2)}, u32[]{:S(2)}) collective-permute-start(bf16[64,64,128]{2,1,0:T(8,128)(2,1)} %get-tuple-element.27), channel_id=1, source_target_pairs={{4,8},{8,4},{5,9},{9,5},{6,10},{10,6},{7,11},{11,7},{20,24},{24,20... | collective-permute-start | bytes 3145736 | tf_op jit(solution)/shard_map/ppermute | solution.py:363
  17.5 1.6 %copy-done.3 = bf16[128,64,128]{2,1,0:T(8,128)(2,1)S(1)} copy-done((bf16[128,64,128]{2,1,0:T(8,128)(2,1)S(1)}, bf16[128,64,128]{2,1,0:T(8,128)(2,1)}, u32[]{:S(2)}) %copy-start.3) | copy-done | bytes 2097176
  19.1 9.3 %shard_map.96 = (bf16[384,16,128]{2,1,0:T(8,128)(2,1)S(1)}, f32[24,64,128]{2,1,0:T(8,128)S(1)}, bf16[64,64,128]{2,1,0:T(8,128)(2,1)}, bf16[16,64,128]{2,1,0:T(8,...) custom-call(s32[384]{0:T(512)} %get-tuple-element.53.words_ref, ...), custom_call_target="tpu_custom_call", output_to_operand_aliasing={{2}: (4, {})} | custom-call | flops 11000000512 | bytes 1024 | tf_op jit(solution)/shard_map/pallas_call | solution.py:33
  28.5 1.2 %copy-done.9 = bf16[384,16,128]{2,1,0:T(8,128)(2,1)} copy-done((bf16[384,16,128]{2,1,0:T(8,128)(2,1)}, bf16[384,16,128]{2,1,0:T(8,128)(2,1)S(1)}, u32[]{:S(2)}) %copy-start.9) | copy-done | bytes 1572888
  31.2 3.1 %collective-permute-start.4 = (bf16[16,64,128]{2,1,0:T(8,128)(2,1)}, bf16[16,64,128]{2,1,0:T(8,128)(2,1)S(1)}, u32[]{:S(2)}, u32[]{:S(2)}) collective-permute-start(bf16[16,64,128]{2,1,0:T(8,128)(2,1)} %get-tuple-element.33), channel_id=1, source_target_pairs={{4,8},{8,4},{5,9},{9,5},{6,10},{10,6},{7,11},{11,7},{20,24},{24,20... | collective-permute-start | bytes 786440 | tf_op jit(solution)/shard_map/ppermute | solution.py:384
  36.1 2.4 %collective-permute-start.2 = (bf16[64,64,128]{2,1,0:T(8,128)(2,1)}, bf16[64,64,128]{2,1,0:T(8,128)(2,1)S(1)}, u32[]{:S(2)}, u32[]{:S(2)}) collective-permute-start(bf16[64,64,128]{2,1,0:T(8,128)(2,1)} %get-tuple-element.29), channel_id=1, source_target_pairs={{4,8},{8,4},{5,9},{9,5},{6,10},{10,6},{7,11},{11,7},{20,24},{24,20... | collective-permute-start | bytes 3145736 | tf_op jit(solution)/shard_map/ppermute | solution.py:387
  39.9 1.6 %copy-done.4 = bf16[128,64,128]{2,1,0:T(8,128)(2,1)S(1)} copy-done((bf16[128,64,128]{2,1,0:T(8,128)(2,1)S(1)}, bf16[128,64,128]{2,1,0:T(8,128)(2,1)}, u32[]{:S(2)}) %copy-start.4) | copy-done | bytes 2097176
  42.4 1.4 %copy-done.10 = bf16[384,16,128]{2,1,0:T(8,128)(2,1)S(1)} copy-done((bf16[384,16,128]{2,1,0:T(8,128)(2,1)S(1)}, bf16[384,16,128]{2,1,0:T(8,128)(2,1)}, u32[]{:S(2)}) %copy-start.10) | copy-done | bytes 1572888
  43.8 1.1 %copy-done.12 = f32[24,64,128]{2,1,0:T(8,128)S(1)} copy-done((f32[24,64,128]{2,1,0:T(8,128)S(1)}, f32[24,64,128]{2,1,0:T(8,128)}, u32[]{:S(2)}) %copy-start.12) | copy-done | bytes 786456
  44.9 9.0 %shard_map.97 = (f32[129,64,128]{2,1,0:T(8,128)S(1)}, bf16[8,64,128]{2,1,0:T(8,128)(2,1)S(1)}, bf16[10,64,128]{2,1,0:T(8,128)(2,1)}, bf16[10,64,128]{2,1,0:T(8,128)(2,1)}, bf16[10,64,128]{2,1,0:T(8,128)(2,1)S(1)}) custom-call(s32[384]{0:T(512)S(1)} %get-tuple-element.52.words_ref, s32[2]{0:T(128)S(1)} %copy-done.1, bf16[128,64,128]{2,1,0:T(8,128)(2,1)S(1)} %copy-done.4, ...), custom_call_target="tpu_custom_call" | custom-call | flops 32999999488 | bytes 1024 | tf_op jit(solution)/shard_map/pallas_call | solution.py:33
  54.5 1.6 %collective-permute-start.6 = (bf16[10,64,128]{2,1,0:T(8,128)(2,1)}, bf16[10,64,128]{2,1,0:T(8,128)(2,1)S(1)}, u32[]{:S(2)}, u32[]{:S(2)}) collective-permute-start(bf16[10,64,128]{2,1,0:T(8,128)(2,1)} %get-tuple-element.41), channel_id=1, source_target_pairs={{0,1},{1,0},{2,3},{3,2},{4,5},{5,4},{6,7},{7,6},{8,9},{9,8},{10,11... | collective-permute-start | bytes 491528 | tf_op jit(solution)/shard_map/ppermute | solution.py:330
  56.1 2.1 %collective-permute-start.7 = (bf16[10,64,128]{2,1,0:T(8,128)(2,1)}, bf16[10,64,128]{2,1,0:T(8,128)(2,1)S(1)}, u32[]{:S(2)}, u32[]{:S(2)}) collective-permute-start(bf16[10,64,128]{2,1,0:T(8,128)(2,1)} %get-tuple-element.42), channel_id=1, source_target_pairs={{0,2},{1,3},{2,0},{3,1},{4,6},{5,7},{6,4},{7,5},{8,10},{9,11},{10,... | collective-permute-start | bytes 491528 | tf_op jit(solution)/shard_map/ppermute | solution.py:330
  58.2 7.2 %shard_map.98 = (bf16[64,128,128]{2,1,0:T(8,128)(2,1)}, f32[8,128]{1,0:T(8,128)S(1)}) custom-call(bf16[128,64,128]{2,1,0:T(8,128)(2,1)S(1)} %copy-done.4, bf16[128,64,128]{2,1,0:T(8,128)(2,1)} %collective-permute-done.core_ref, bf16[64,64,128]{2,1,0:T(8,128)(2,1)S(1)} %collective-permute-done.1.early_ref, ...), custom_call_target="tpu_custom_call" | custom-call | flops 11000000512 | bytes 1024 | tf_op jit(solution)/shard_map/pallas_call | solution.py:33
  66.2 4.0 %collective-permute-start.12 = (bf16[12,256,128]{2,1,0:T(8,128)(2,1)S(1)}, bf16[12,256,128]{2,1,0:T(8,128)(2,1)S(1)}, u32[]{:S(2)}, u32[]{:S(2)}) collective-permute-start(bf16[12,256,128]{2,1,0:T(8,128)(2,1)S(1)} %get-tuple-element.46), channel_id=1, source_target_pairs={{4,8},{8,4},{5,9},{9,5},{6,10},{10,6},{7,11},{11,7},{20,24},{24,20... | collective-permute-start | bytes 2359304 | tf_op jit(solution)/shard_map/ppermute | solution.py:440
  70.4 1.6 %copy-done.5 = bf16[128,64,128]{2,1,0:T(8,128)(2,1)S(1)} copy-done((bf16[128,64,128]{2,1,0:T(8,128)(2,1)S(1)}, bf16[128,64,128]{2,1,0:T(8,128)(2,1)}, u32[]{:S(2)}) %copy-start.5) | copy-done | bytes 2097176
  73.8 1.9 %collective-permute-start.10 = (bf16[4,256,128]{2,1,0:T(8,128)(2,1)S(1)}, bf16[4,256,128]{2,1,0:T(8,128)(2,1)S(1)}, u32[]{:S(2)}, u32[]{:S(2)}) collective-permute-start(bf16[4,256,128]{2,1,0:T(8,128)(2,1)S(1)} %get-tuple-element.45), channel_id=1, source_target_pairs={{4,8},{8,4},{5,9},{9,5},{6,10},{10,6},{7,11},{11,7},{20,24},{24,20... | collective-permute-start | bytes 786440 | tf_op jit(solution)/shard_map/ppermute | solution.py:458
  75.8 4.1 %collective-permute-done.12.link_ref = bf16[12,256,128]{2,1,0:T(8,128)(2,1)S(1)} collective-permute-done((bf16[12,256,128]{2,1,0:T(8,128)(2,1)S(1)}, bf16[12,256,128]{2,1,0:T(8,128)(2,1)S(1)}, u32[]{:S(2)}, u32[]{:S(2)}) %collective-permute-start.12) | collective-permute-done | bytes 786464 | tf_op jit(solution)/shard_map/ppermute | solution.py:440
  79.9 1.7 %shard_map.101.begun_ref = f32[2,256,256]{2,1,0:T(8,128)S(1)} custom-call(s32[2]{0:T(128)S(1)} %copy-done.1, bf16[25,256,128]{2,1,0:T(8,128)(2,1)S(1)} %get-tuple-element.40.after_ref.all_ref, bf16[12,256,128]{2,1,0:T(8,128)(2,1)S(1)} %collective-permute-done.11.core_ref, bf16[12,256,128]{2,1,0:T(8,128)(2,1)S(1)} %collective-permute-done.12.link_ref, ...), custom_call_target="tpu_custom_call" | custom-call | flops 1100000 | bytes 1024 | tf_op jit(solution)/shard_map/pallas_call | solution.py:33
  81.6 1.1 %collective-permute-done.10.link_ref = bf16[4,256,128]{2,1,0:T(8,128)(2,1)S(1)} collective-permute-done((bf16[4,256,128]{2,1,0:T(8,128)(2,1)S(1)}, bf16[4,256,128]{2,1,0:T(8,128)(2,1)S(1)}, u32[]{:S(2)}, u32[]{:S(2)}) %collective-permute-start.10) | collective-permute-done | bytes 262176 | tf_op jit(solution)/shard_map/ppermute | solution.py:458
  82.7 1.4 %shard_map.102 = bf16[16,64,128]{2,1,0:T(8,128)(2,1)S(1)} custom-call(s32[2]{0:T(128)S(1)} %copy-done.1, bf16[9,256,128]{2,1,0:T(8,128)(2,1)S(1)} %get-tuple-element.44.unread.all_ref, bf16[4,256,128]{2,1,0:T(8,128)(2,1)S(1)} %collective-permute-done.9.core_ref, bf16[4,256,128]{2,1,0:T(8,128)(2,1)S(1)} %collective-permute-done.10.link_ref, ...), custom_call_target="tpu_custom_call" | custom-call | flops 1100000 | bytes 1024 | tf_op jit(solution)/shard_map/pallas_call | solution.py:33
  84.1 15.8 %all_to_all.10.parts_ref = bf16[16,64,128]{2,1,0:T(8,128)(2,1)S(1)} all-to-all(bf16[16,64,128]{2,1,0:T(8,128)(2,1)S(1)} %shard_map.102), channel_id=1, replica_groups=mesh['groups'=2,'domain'=4,'band'=4] {'domain','band'}, dimensions={0} | all-to-all | bytes 524288 | tf_op jit(solution)/shard_map/all_to_all | solution.py:481
  (56 shorter events, 11.0 us)
Async XLA Ops:
  6.0 10.2 %copy-start.16 = (s32[384]{0:T(512)S(1)}, s32[384]{0:T(512)}, u32[]{:S(2)}) copy-start(s32[384]{0:T(512)} %param.12) | copy-start | bytes 4612
  6.1 10.2 %copy-start.17 = (s32[384]{0:T(512)S(1)}, s32[384]{0:T(512)}, u32[]{:S(2)}) copy-start(s32[384]{0:T(512)} %param.11) | copy-start | bytes 4612
  6.1 32.5 %collective-permute-start = (bf16[128,64,128]{2,1,0:T(8,128)(2,1)}, bf16[128,64,128]{2,1,0:T(8,128)(2,1)}, u32[]{:S(2)}, u32[]{:S(2)}) collective-permute-start(bf16[128,64,128]{2,1,0:T(8,128)(2,1)} %get-tuple-element.26), channel_id=1, source_target_pairs={{0,4},{4,0},{8,12},{12,8},{1,5},{5,1},{9,13},{13,9},{2,6},{6,2},{1... | collective-permute-start | bytes 6291464 | tf_op jit(solution)/shard_map/ppermute | solution.py:364
  6.1 59.3 %all-to-all-start = ((bf16[100,64,128]{2,1,0:T(8,128)(2,1)}), bf16[100,64,128]{2,1,0:T(8,128)(2,1)S(1)}, u32[]{:S(2)}, u32[]{:S(2)}) async-start(bf16[100,64,128]{2,1,0:T(8,128)(2,1)} %get-tuple-element.38), calls=%async_computation | async-start | bytes 3276800 | tf_op jit(solution)/shard_map/all_to_all | solution.py:362
  12.1 23.9 %collective-permute-start.1 = (bf16[64,64,128]{2,1,0:T(8,128)(2,1)}, bf16[64,64,128]{2,1,0:T(8,128)(2,1)S(1)}, u32[]{:S(2)}, u32[]{:S(2)}) collective-permute-start(bf16[64,64,128]{2,1,0:T(8,128)(2,1)} %get-tuple-element.27), channel_id=1, source_target_pairs={{4,8},{8,4},{5,9},{9,5},{6,10},{10,6},{7,11},{11,7},{20,24},{24,20... | collective-permute-start | bytes 3145736 | tf_op jit(solution)/shard_map/ppermute | solution.py:363
  17.5 1.6 %copy-start.3 = (bf16[128,64,128]{2,1,0:T(8,128)(2,1)S(1)}, bf16[128,64,128]{2,1,0:T(8,128)(2,1)}, u32[]{:S(2)}) copy-start(bf16[128,64,128]{2,1,0:T(8,128)(2,1)} %copy-done.2) | copy-start | bytes 6291460
  19.1 15.2 %copy-start.15 = (f32[256,16]{0,1:T(8,128)S(1)}, f32[256,16]{0,1:T(8,128)}, u32[]{:S(2)}) copy-start(f32[256,16]{0,1:T(8,128)} %param.14) | copy-start | bytes 49156
  19.1 20.7 %copy-start.1 = (s32[2]{0:T(128)S(1)}, s32[2]{0:T(128)}, u32[]{:S(2)}) copy-start(s32[2]{0:T(128)} %pad_add_fusion.ids_ref) | copy-start | bytes 28
  30.5 8.7 %collective-permute-start.5 = (bf16[8,64,128]{2,1,0:T(8,128)(2,1)}, bf16[8,64,128]{2,1,0:T(8,128)(2,1)S(1)}, u32[]{:S(2)}, u32[]{:S(2)}) collective-permute-start(bf16[8,64,128]{2,1,0:T(8,128)(2,1)} %get-tuple-element.34), channel_id=1, source_target_pairs={{0,8},{4,12},{8,0},{12,4},{1,9},{5,13},{9,1},{13,5},{2,10},{6,14},... | collective-permute-start | bytes 393224 | tf_op jit(solution)/shard_map/ppermute | solution.py:385
  30.5 9.3 %collective-permute-start.3 = (bf16[16,64,128]{2,1,0:T(8,128)(2,1)}, bf16[16,64,128]{2,1,0:T(8,128)(2,1)S(1)}, u32[]{:S(2)}, u32[]{:S(2)}) collective-permute-start(bf16[16,64,128]{2,1,0:T(8,128)(2,1)} %get-tuple-element.32), channel_id=1, source_target_pairs={{0,4},{4,0},{8,12},{12,8},{1,5},{5,1},{9,13},{13,9},{2,6},{6,2},{1... | collective-permute-start | bytes 786440 | tf_op jit(solution)/shard_map/ppermute | solution.py:386
  31.2 8.7 %collective-permute-start.4 = (bf16[16,64,128]{2,1,0:T(8,128)(2,1)}, bf16[16,64,128]{2,1,0:T(8,128)(2,1)S(1)}, u32[]{:S(2)}, u32[]{:S(2)}) collective-permute-start(bf16[16,64,128]{2,1,0:T(8,128)(2,1)} %get-tuple-element.33), channel_id=1, source_target_pairs={{4,8},{8,4},{5,9},{9,5},{6,10},{10,6},{7,11},{11,7},{20,24},{24,20... | collective-permute-start | bytes 786440 | tf_op jit(solution)/shard_map/ppermute | solution.py:384
  36.1 22.1 %collective-permute-start.2 = (bf16[64,64,128]{2,1,0:T(8,128)(2,1)}, bf16[64,64,128]{2,1,0:T(8,128)(2,1)S(1)}, u32[]{:S(2)}, u32[]{:S(2)}) collective-permute-start(bf16[64,64,128]{2,1,0:T(8,128)(2,1)} %get-tuple-element.29), channel_id=1, source_target_pairs={{4,8},{8,4},{5,9},{9,5},{6,10},{10,6},{7,11},{11,7},{20,24},{24,20... | collective-permute-start | bytes 3145736 | tf_op jit(solution)/shard_map/ppermute | solution.py:387
  39.9 1.6 %copy-start.4 = (bf16[128,64,128]{2,1,0:T(8,128)(2,1)S(1)}, bf16[128,64,128]{2,1,0:T(8,128)(2,1)}, u32[]{:S(2)}) copy-start(bf16[128,64,128]{2,1,0:T(8,128)(2,1)} %copy-done.2) | copy-start | bytes 6291460
  42.4 1.4 %copy-start.10 = (bf16[384,16,128]{2,1,0:T(8,128)(2,1)S(1)}, bf16[384,16,128]{2,1,0:T(8,128)(2,1)}, u32[]{:S(2)}) copy-start(bf16[384,16,128]{2,1,0:T(8,128)(2,1)} %copy-done.9) | copy-start | bytes 4718596
  44.9 13.3 %copy-start = (f32[1,128,128]{2,1,0:T(8,128)S(1)}, f32[1,128,128]{2,1,0:T(8,128)}, u32[]{:S(2)}) copy-start(f32[1,128,128]{2,1,0:T(8,128)} %param.9) | copy-start | bytes 196612
  44.9 13.3 %copy-start.8 = (bf16[128,128]{1,0:T(8,128)(2,1)S(1)}, bf16[128,128]{1,0:T(8,128)(2,1)}, u32[]{:S(2)}) copy-start(bf16[128,128]{1,0:T(8,128)(2,1)} %constant.24.clone.ring_ref) | copy-start | bytes 98308
  54.5 15.8 %collective-permute-start.6 = (bf16[10,64,128]{2,1,0:T(8,128)(2,1)}, bf16[10,64,128]{2,1,0:T(8,128)(2,1)S(1)}, u32[]{:S(2)}, u32[]{:S(2)}) collective-permute-start(bf16[10,64,128]{2,1,0:T(8,128)(2,1)} %get-tuple-element.41), channel_id=1, source_target_pairs={{0,1},{1,0},{2,3},{3,2},{4,5},{5,4},{6,7},{7,6},{8,9},{9,8},{10,11... | collective-permute-start | bytes 491528 | tf_op jit(solution)/shard_map/ppermute | solution.py:330
  56.1 14.2 %collective-permute-start.7 = (bf16[10,64,128]{2,1,0:T(8,128)(2,1)}, bf16[10,64,128]{2,1,0:T(8,128)(2,1)S(1)}, u32[]{:S(2)}, u32[]{:S(2)}) collective-permute-start(bf16[10,64,128]{2,1,0:T(8,128)(2,1)} %get-tuple-element.42), channel_id=1, source_target_pairs={{0,2},{1,3},{2,0},{3,1},{4,6},{5,7},{6,4},{7,5},{8,10},{9,11},{10,... | collective-permute-start | bytes 491528 | tf_op jit(solution)/shard_map/ppermute | solution.py:330
  58.2 12.2 %collective-permute-start.8 = (bf16[10,64,128]{2,1,0:T(8,128)(2,1)S(1)}, bf16[10,64,128]{2,1,0:T(8,128)(2,1)S(1)}, u32[]{:S(2)}, u32[]{:S(2)}) collective-permute-start(bf16[10,64,128]{2,1,0:T(8,128)(2,1)S(1)} %get-tuple-element.43), channel_id=1, source_target_pairs={{0,3},{1,2},{2,1},{3,0},{4,7},{5,6},{6,5},{7,4},{8,11},{9,10},{10,... | collective-permute-start | bytes 491528 | tf_op jit(solution)/shard_map/ppermute | solution.py:330
  66.2 13.7 %collective-permute-start.12 = (bf16[12,256,128]{2,1,0:T(8,128)(2,1)S(1)}, bf16[12,256,128]{2,1,0:T(8,128)(2,1)S(1)}, u32[]{:S(2)}, u32[]{:S(2)}) collective-permute-start(bf16[12,256,128]{2,1,0:T(8,128)(2,1)S(1)} %get-tuple-element.46), channel_id=1, source_target_pairs={{4,8},{8,4},{5,9},{9,5},{6,10},{10,6},{7,11},{11,7},{20,24},{24,20... | collective-permute-start | bytes 2359304 | tf_op jit(solution)/shard_map/ppermute | solution.py:440
  70.2 9.7 %collective-permute-start.11 = (bf16[12,256,128]{2,1,0:T(8,128)(2,1)S(1)}, bf16[12,256,128]{2,1,0:T(8,128)(2,1)S(1)}, u32[]{:S(2)}, u32[]{:S(2)}) collective-permute-start(bf16[12,256,128]{2,1,0:T(8,128)(2,1)S(1)} %get-tuple-element.46), channel_id=1, source_target_pairs={{0,4},{4,0},{8,12},{12,8},{1,5},{5,1},{9,13},{13,9},{2,6},{6,2},{1... | collective-permute-start | bytes 2359304 | tf_op jit(solution)/shard_map/ppermute | solution.py:441
  70.3 1.6 %copy-start.5 = (bf16[128,64,128]{2,1,0:T(8,128)(2,1)S(1)}, bf16[128,64,128]{2,1,0:T(8,128)(2,1)}, u32[]{:S(2)}) copy-start(bf16[128,64,128]{2,1,0:T(8,128)(2,1)} %copy-done.2) | copy-start | bytes 6291460
  73.8 8.9 %collective-permute-start.10 = (bf16[4,256,128]{2,1,0:T(8,128)(2,1)S(1)}, bf16[4,256,128]{2,1,0:T(8,128)(2,1)S(1)}, u32[]{:S(2)}, u32[]{:S(2)}) collective-permute-start(bf16[4,256,128]{2,1,0:T(8,128)(2,1)S(1)} %get-tuple-element.45), channel_id=1, source_target_pairs={{4,8},{8,4},{5,9},{9,5},{6,10},{10,6},{7,11},{11,7},{20,24},{24,20... | collective-permute-start | bytes 786440 | tf_op jit(solution)/shard_map/ppermute | solution.py:458
  75.7 7.0 %collective-permute-start.9 = (bf16[4,256,128]{2,1,0:T(8,128)(2,1)S(1)}, bf16[4,256,128]{2,1,0:T(8,128)(2,1)S(1)}, u32[]{:S(2)}, u32[]{:S(2)}) collective-permute-start(bf16[4,256,128]{2,1,0:T(8,128)(2,1)S(1)} %get-tuple-element.45), channel_id=1, source_target_pairs={{0,4},{4,0},{8,12},{12,8},{1,5},{5,1},{9,13},{13,9},{2,6},{6,2},{1... | collective-permute-start | bytes 786440 | tf_op jit(solution)/shard_map/ppermute | solution.py:459
  (8 other events, 7.7 us)

commit v9 on v8

v9 whole, which is shorter than its diff:
```python
import functools

import jax
import jax.numpy as jnp
import numpy as np
from jax import lax
from jax.experimental import pallas as pl
from jax.experimental.pallas import tpu as pltpu
from jax.sharding import PartitionSpec as P

F32 = jnp.float32
BF16 = jnp.bfloat16
LANES = 128
VMEM_BYTES = 63 << 20
ROWS = 16
NT = (((1,), (1,)), ((), ()))
WHOLE = pl.BlockSpec(memory_space=pltpu.VMEM)
SCALARS = pl.BlockSpec(memory_space=pltpu.SMEM)
FAR = pl.BlockSpec(memory_space=pltpu.HBM)
UNREAD = pl.BlockSpec(memory_space=pl.ANY)
copies = pltpu.SemaphoreType.DMA


def call(kernel, grid, in_specs, out_specs, outs, scratch, args, aliases=None, micros=0.001):
    return pl.pallas_call(
        kernel,
        grid=grid,
        out_shape=[jax.ShapeDtypeStruct(shape, kind) for shape, kind in outs],
        in_specs=in_specs,
        out_specs=out_specs,
        scratch_shapes=scratch,
        input_output_aliases=aliases or {},
        compiler_params=pltpu.CompilerParams(vmem_limit_bytes=VMEM_BYTES),
        cost_estimate=pl.CostEstimate(flops=int(micros * 1.1e9), bytes_accessed=1 << 10, transcendentals=0),
    )(*args)


def start(copy):
    copy.start()
    return copy


def load_all(pairs, sems):
    return [start(pltpu.make_async_copy(far, near, sems.at[i])) for i, (far, near) in enumerate(pairs)]


def wait_all(started):
    for copy in started:
        copy.wait()


def pack_kernel(first, x_hbm, xt_hbm, early, late, message, x, xt, in_sems, out_sems):
    states, lines, _ = x.shape
    bands = in_sems.shape[0]
    share = lines // bands
    count = share - first
    loads, sends = [], []
    for c in range(bands):
        where = (slice(None), pl.ds(c * share, share), slice(None))
        loads.append(start(pltpu.make_async_copy(x_hbm.at[where], x.at[where], in_sems.at[c])))

    def send(line, number, target, at):
        copy = pltpu.make_async_copy(
            xt.at[pl.ds(line, number)], target.at[pl.ds(at, number)], out_sems.at[len(sends)]
        )
        sends.append(start(copy))

    for c in range(bands):
        loads[c].wait()
        for y0 in range(c * share, (c + 1) * share, ROWS):
            for s0 in range(0, states, ROWS):
                block = x[s0 : s0 + ROWS, y0 : y0 + ROWS, :].astype(F32)
                turned = jnp.swapaxes(block, 0, 1).astype(BF16)
                xt[y0 : y0 + ROWS, s0 : s0 + ROWS, :] = turned
        send(c * share + first, count, message, c * (count + 1))
        send(c * share, 1, message, (c + bands - 1) % bands * (count + 1) + count)
        if (c + 1) * share == early.shape[0]:
            send(0, early.shape[0], early, 0)
    send(early.shape[0], late.shape[0], late, 0)
    send(0, lines, xt_hbm, 0)
    wait_all(sends)


def bases(ids_ref, groups):
    odd, upper = ids_ref[0] & 1, (ids_ref[0] >> 1) & 1
    return [2 * groups * side for side in (1 - odd, odd, 1 - upper, upper)]


def project_kernel(words_ref, ids_ref, xt_hbm, p_hbm, handed, mine_hbm, same, core_ref, link_ref, *refs):
    far_refs, (total, mine, xt, p_ref, sems, mine_sem) = refs[:-6], refs[-6:]
    slots, proj_count, _ = p_ref.shape
    groups, states = mine.shape[0] // 3, mine.shape[1]
    per_group = LANES // proj_count
    chunks = sems.shape[0] - 1
    size = slots // chunks
    unroll = 16
    pairs = [(p_hbm.at[pl.ds(c * size, size)], p_ref.at[pl.ds(c * size, size)]) for c in range(chunks)]
    xt_load, *loads = load_all([(xt_hbm, xt), *pairs], sems)

    def clear(i, carry):
        for u in range(per_group):
            total[i * per_group + u] = jnp.zeros_like(total[0])
        return carry

    lax.fori_loop(0, 3 * groups, clear, 0)

    def body(i, carry):
        for u0 in range(0, unroll, 8):
            ts = [i * unroll + u0 + u for u in range(8)]
            words = [words_ref[t] for t in ts]
            parts = [
                lax.dot_general(p_ref[t], xt[word >> 16], NT, preferred_element_type=F32)
                for t, word in zip(ts, words)
            ]
            for word, part in zip(words, parts):
                total[word & 0xFFFF] += part
        return carry

    xt_load.wait()
    for c in range(chunks):
        loads[c].wait()
        lax.fori_loop(c * size // unroll, (c + 1) * size // unroll, body, 0)

    for g in range(3 * groups):
        tiles = [total[g * per_group + u] for u in range(per_group)]
        mine[g] = jnp.concatenate(tiles, axis=0).T
    send = start(pltpu.make_async_copy(mine, mine_hbm, mine_sem))
    sides = bases(ids_ref, groups)
    for g in range(groups):
        own = mine[groups + g].astype(BF16)
        for side, ref in zip(sides[:2], (core_ref, link_ref)):
            ref[g] = mine[side + g].astype(BF16)
            ref[groups + g] = own
        for side, ref in zip(sides[2:], far_refs):
            ref[g] = mine[side + g].astype(BF16)
    send.wait()


def nonlocal_kernel(
    first, fars, words_ref, ids_ref, xt_hbm, p_hbm, energy_ref, pot_ref, ring_ref, mine_hbm, core_hbm, link_hbm, *refs
):
    far_hbms, rest = refs[:fars], refs[fars:]
    _, _, out_hbm, whole_ref, *messages, lines_sum, total, atoms, p_ref, xt_ref, pair_refs, far_refs, sems, out_sems = rest
    slots, proj_count, _ = p_ref.shape
    groups, states = total.shape[0] // 3, total.shape[1]
    per_group = LANES // proj_count
    lines = xt_ref.shape[0]
    unroll = 16
    fars_here = [(far, far_refs.at[i]) for i, far in enumerate(far_hbms)]
    pairs = [(mine_hbm, total), (core_hbm, pair_refs.at[0]), (link_hbm, pair_refs.at[1]), *fars_here]
    loads = load_all([*pairs, (xt_hbm, xt_ref), (p_hbm, p_ref)], sems)

    def clear(i, carry):
        lines_sum[i] = jnp.zeros((states, LANES), F32)
        return carry

    lax.fori_loop(0, lines + 1, clear, 0)
    wait_all(loads[:-2])
    sides = bases(ids_ref, groups)
    for g in range(groups):
        total[groups + g] += pair_refs[0, g].astype(F32) + pair_refs[1, g].astype(F32)
        for i in range(2):
            total[sides[i] + g] += pair_refs[i, groups + g].astype(F32)
        for i in range(fars):
            total[sides[2 + i] + g] += far_refs[i, g].astype(F32)
    last = energy_ref.shape[0] - 1
    for g in range(3 * groups):
        row = jnp.clip((ids_ref[0] - 1) * groups + g, 0, last)
        tile = (total[g] * energy_ref[pl.ds(row, 1), :]).astype(BF16)
        for u in range(per_group):
            atoms[g * per_group + u] = tile[:, u * proj_count : (u + 1) * proj_count]
    for g in range(groups):
        whole_ref[g] = total[groups + g].astype(BF16)
    wait_all(loads[-2:])
    share = xt_ref.shape[0] // (len(messages) + 1)
    held = groups // (len(messages) + 1)
    for k, message in enumerate(messages, 1):
        to = ids_ref[1] ^ k
        for i in range(first):
            message[i] = xt_ref[to * share + i]
        for i in range(held):
            message[first + i] = whole_ref[to * held + i]

    def body(i, carry):
        for u0 in range(0, unroll, 4):
            ts = [i * unroll + u0 + u for u in range(4)]
            words = [words_ref[t] for t in ts]
            parts = [
                jnp.dot(atoms[word & 0xFFFF], p_ref[t], preferred_element_type=F32) for t, word in zip(ts, words)
            ]
            for word, part in zip(words, parts):
                lines_sum[word >> 16] += part
        return carry

    lax.fori_loop(0, slots // unroll, body, 0)
    blocks = out_sems.shape[0]
    size = lines // blocks
    step = 8

    def in_plane(i, carry):
        y0 = i * step
        cells = xt_ref[pl.ds(y0, step)].reshape(step * states, LANES)
        along = jnp.dot(cells, ring_ref[...], preferred_element_type=F32)
        before = xt_ref[lax.rem(y0 + lines - 1, lines)].astype(F32)
        x = xt_ref[y0].astype(F32)
        for j in range(step):
            after = xt_ref[lax.rem(y0 + j + 1, lines)].astype(F32)
            value = along[j * states : (j + 1) * states] + pot_ref[pl.ds(y0 + j, 1), :] * x
            lines_sum[y0 + j] += value - 0.5 * (before + after)
            before, x = x, after
        return carry

    sends = []
    for c in range(blocks):
        lax.fori_loop(c * size // step, (c + 1) * size // step, in_plane, 0)
        where = pl.ds(c * size, size)
        sends.append(start(pltpu.make_async_copy(lines_sum.at[where], out_hbm.at[where], out_sems.at[c])))
    wait_all(sends)


def beside_kernel(early_steps, sum_ref, core_ref, early_ref, late_ref, unread, out_ref, done_ref):
    states, here, _ = out_ref.shape
    done_ref[...] = jnp.zeros_like(done_ref)
    early = pl.program_id(0) < early_steps
    for s0 in range(0, states, ROWS):
        rows = slice(s0, s0 + ROWS)
        results = []
        for i in range(here):
            link = jnp.where(early, early_ref[i, rows, :], late_ref[i, rows, :]).astype(F32)
            results.append(sum_ref[i, rows, :] - 0.5 * (core_ref[i, rows, :].astype(F32) + link))
        out_ref[rows, :, :] = jnp.swapaxes(jnp.stack(results, axis=0), 0, 1).astype(BF16)


def later_kernel(bands, ids_ref, landed, unread, pass_hbm, done_ref, sems):
    done_ref[...] = jnp.zeros_like(done_ref)
    half, states = pass_hbm.shape[0], landed.shape[1]
    count = landed.shape[0] // bands
    begin = (1 - (ids_ref[0] & 1)) * half
    wait_all(
        load_all(
            [
                (landed.at[pl.ds(b * count + begin, half)], pass_hbm.at[:, pl.ds(b * states, states), :])
                for b in range(bands)
            ],
            sems,
        )
    )


def early_kernel(share, ids_ref, xt_hbm, unread, *refs):
    pieces, (pass_hbm, done_ref, sems) = refs[:-3], refs[-3:]
    done_ref[...] = jnp.zeros_like(done_ref)
    half, states = pass_hbm.shape[0], xt_hbm.shape[1]
    band = ids_ref[1]
    begin = (1 - (ids_ref[0] & 1)) * half
    pairs = []
    for k in range(len(pieces) + 1):
        at = pl.ds(pl.multiple_of((band ^ k) * states, states), states)
        source = xt_hbm.at[pl.ds(band * share + begin, half)] if k == 0 else pieces[k - 1].at[pl.ds(begin, half)]
        pairs.append((source, pass_hbm.at[:, at, :]))
    wait_all(load_all(pairs, sems))


def add_products(row, ids_ref, line, beside, pot_ref, acc):
    half = beside.shape[1]
    group = 4
    mine = (ids_ref[0] & 1) * half
    for part, base in ((0, mine), (1, half - mine)):
        for i0 in range(0, half, group):
            xs, ys = [], []
            for i in range(i0, min(i0 + group, half)):
                cell = line(base + i)
                x = cell.astype(F32)
                y = (3.0 + pot_ref[pl.ds(row + base + i, 1), :]) * x - pltpu.roll(x, x.shape[1] - 1, 1)
                y = y - line(base + i + 1).astype(F32)
                if part == 0:
                    y = y - beside[0, i].astype(F32) - beside[1, i].astype(F32)
                xs.append(cell)
                ys.append(y.astype(BF16))
            flat_x = jnp.concatenate(xs, axis=1)
            flat_y = jnp.concatenate(ys, axis=1)
            acc[0] += lax.dot_general(flat_x, flat_x, NT, preferred_element_type=F32)
            acc[1] += lax.dot_general(flat_y, flat_x, NT, preferred_element_type=F32)


def gram_kernel(bands, first, share, ids_ref, landed_hbm, core_hbm, link_hbm, pot_ref, unread, acc, landed, beside, sems):
    loads = load_all([(landed_hbm, landed), (core_hbm, beside.at[0]), (link_hbm, beside.at[1])], sems)
    acc[...] = jnp.zeros_like(acc)
    count = landed.shape[0] // bands
    wait_all(loads)

    def line(i):
        return jnp.concatenate([landed[b * count + i] for b in range(bands)], axis=0)

    add_products(ids_ref[1] * share + first, ids_ref, line, beside, pot_ref, acc)


def final_kernel(
    bands, share, ids_ref, xt_hbm, whole_ref, landed_hbm, core_hbm, link_hbm, begun_hbm, pot_ref, energy_ref, *refs
):
    pieces, (out_ref, lines_ref, projs, beside, acc, sems) = refs[: bands - 1], refs[bands - 1 :]
    states = xt_hbm.shape[1]
    band = ids_ref[1]
    first, held = lines_ref.shape[0] - 1, projs.shape[0]
    count = landed_hbm.shape[0] // bands
    pairs = [(begun_hbm, acc), (core_hbm, beside.at[0]), (link_hbm, beside.at[1])]
    for b in range(bands):
        at = pl.ds(b * states, states)
        pairs.append((landed_hbm.at[pl.ds(b * count, 1)], lines_ref.at[pl.ds(first, 1), at, :]))
    for k in range(bands):
        at = pl.ds(pl.multiple_of((band ^ k) * states, states), states)
        if k == 0:
            pairs.append((xt_hbm.at[pl.ds(band * share, first)], lines_ref.at[pl.ds(0, first), at, :]))
            for g in range(held):
                projs[g, at, :] = whole_ref[band * held + g]
        else:
            pairs.append((pieces[k - 1].at[pl.ds(0, first)], lines_ref.at[pl.ds(0, first), at, :]))
            pairs.append((pieces[k - 1].at[pl.ds(first, held)], projs.at[:, at, :]))
    wait_all(load_all(pairs, sems))
    add_products(band * share, ids_ref, lambda i: lines_ref[i], beside, pot_ref, acc)
    row = (ids_ref[0] * bands + band) * held
    for g in range(held):
        here = projs[g]
        scaled = (here.astype(F32) * energy_ref[pl.ds(row + g, 1), :]).astype(BF16)
        acc[1] += lax.dot_general(scaled, here, NT, preferred_element_type=F32)
    hamil = 0.5 * (acc[1] + acc[1].T)
    domains = out_ref.shape[0] // bands
    rows, cols = out_ref.shape[1], out_ref.shape[2] // 2
    for c in range(domains):
        for r in range(bands):
            r0, c0 = r * rows, c * cols
            out_ref[c * bands + r, :, :cols] = acc[0, r0 : r0 + rows, c0 : c0 + cols].astype(BF16)
            out_ref[c * bands + r, :, cols:] = hamil[r0 : r0 + rows, c0 : c0 + cols].astype(BF16)


def result_kernel(scale, parts_ref, out_ref):
    total = jnp.sum(parts_ref[...].astype(F32), axis=0) * scale
    cols = out_ref.shape[2]
    out_ref[0] = total[:, :cols]
    out_ref[1] = total[:, cols:]


def local(orbitals, potential, projectors, tile_atom, tile_line, tile_count, energies):
    states, _, lines, cols_z = orbitals.shape
    slots, proj_count, _ = projectors.shape
    atom_total = energies.shape[0]
    domains, bands = lax.axis_size("domain"), lax.axis_size("band")
    domain, band = lax.axis_index("domain"), lax.axis_index("band")
    total_states = states * bands
    atoms_here = atom_total // domains
    per_group = LANES // proj_count
    groups = atoms_here // per_group
    group_share = groups // bands
    share = lines // bands
    first = share // 4
    rest = share - first

    core_pairs = [(i, i ^ 1) for i in range(domains) if i ^ 1 < domains]
    link_pairs = [(i, ((i + 1) ^ 1) - 1) for i in range(1, domains) if ((i + 1) ^ 1) - 1 < domains]
    near_far = [(i, i ^ 2) for i in range(domains) if i ^ 2 < domains]
    next_far = [(i, ((i + 2) ^ 2) - 2) for i in range(2, domains) if ((i + 2) ^ 2) - 2 < domains]
    far_pairs = [pairs for pairs in (near_far, next_far) if pairs]

    def swapped(values, axis):
        size = lax.axis_size(axis)
        got = {k: lax.ppermute(values[k - 1], axis, [(i, i ^ k) for i in range(size)]) for k in range(size - 1, 0, -1)}
        return [got[k] for k in range(1, size)]

    ids = jnp.stack([domain, band]).astype(jnp.int32)
    near = jnp.clip(tile_atom - (domain - 1) * atoms_here, 0, 3 * atoms_here - 1)
    live = jnp.arange(slots, dtype=jnp.int32) < tile_count[0]
    project_words = (tile_line << 16) | jnp.where(live, near, 3 * atoms_here)
    nonlocal_words = (jnp.where(live, tile_line, lines) << 16) | near
    field = orbitals.reshape(states, lines, cols_z)
    pot = potential.reshape(lines, cols_z)
    energy = energies.reshape(atom_total // per_group, LANES)
    eye = np.eye(cols_z, dtype=np.float32)
    ring = jnp.asarray(3.0 * eye - 0.5 * (np.roll(eye, 1, axis=0) + np.roll(eye, -1, axis=0)), dtype=BF16)

    late_lines = lines // 2
    line_shape, late_shape = (lines, states, cols_z), (late_lines, states, cols_z)
    xt, early_part, late_part, message = call(
        functools.partial(pack_kernel, first),
        (),
        [FAR],
        [FAR] * 4,
        [
            (line_shape, BF16),
            ((lines - late_lines, states, cols_z), BF16),
            (late_shape, BF16),
            ((bands * (rest + 1), states, cols_z), BF16),
        ],
        [
            pltpu.VMEM((states, lines, cols_z), BF16),
            pltpu.VMEM(line_shape, BF16),
            copies((bands,)),
            copies((2 * bands + 3,)),
        ],
        (field,),
    )
    landed = lax.all_to_all(message, "band", split_axis=0, concat_axis=0, tiled=True)
    link_early = lax.ppermute(early_part, "domain", link_pairs)
    core_field = lax.ppermute(xt, "domain", core_pairs)

    group_shape = (groups, states, LANES)
    mine, late_part, to_core, to_link, *to_far = call(
        project_kernel,
        (),
        [SCALARS, SCALARS, FAR, FAR, UNREAD],
        [FAR, UNREAD] + [WHOLE] * (2 + len(far_pairs)),
        [((3 * groups, states, LANES), F32), (late_shape, BF16)]
        + [((2 * groups, states, LANES), BF16)] * 2
        + [(group_shape, BF16)] * len(far_pairs),
        [
            pltpu.VMEM((3 * atoms_here + 1, proj_count, states), F32),
            pltpu.VMEM((3 * groups, states, LANES), F32),
            pltpu.VMEM(line_shape, BF16),
            pltpu.VMEM(projectors.shape, BF16),
            copies((5,)),
            copies,
        ],
        (project_words, ids, xt, projectors, late_part),
        aliases={4: 1},
        micros=10,
    )
    from_link = lax.ppermute(to_link, "domain", link_pairs)
    from_far = [lax.ppermute(value, "domain", pairs) for value, pairs in zip(to_far, far_pairs)]
    from_core = lax.ppermute(to_core, "domain", core_pairs)
    link_late = lax.ppermute(late_part, "domain", link_pairs)
    added, whole, *messages = call(
        functools.partial(nonlocal_kernel, first, len(far_pairs)),
        (),
        [SCALARS, SCALARS, FAR, FAR, WHOLE, WHOLE, WHOLE] + [FAR] * (3 + len(far_pairs)) + [UNREAD] * 2,
        [FAR, WHOLE] + [WHOLE] * (bands - 1),
        [(line_shape, F32), (group_shape, BF16)]
        + [((first + group_share, states, cols_z), BF16)] * (bands - 1),
        [
            pltpu.VMEM((lines + 1, states, cols_z), F32),
            pltpu.VMEM((3 * groups, states, LANES), F32),
            pltpu.VMEM((3 * atoms_here, states, proj_count), BF16),
            pltpu.VMEM(projectors.shape, BF16),
            pltpu.VMEM(line_shape, BF16),
            pltpu.VMEM((2, 2 * groups, states, LANES), BF16),
            pltpu.VMEM((2, *group_shape), BF16),
            copies((5 + len(far_pairs),)),
            copies((4,)),
        ],
        (
            nonlocal_words, ids, xt, projectors, energy, pot, ring, mine, from_core, from_link, *from_far,
            link_early[0, :ROWS], core_field[0, :ROWS],
        ),
        micros=30,
    )
    early = swapped(messages, "band")

    later_pass, later_token = call(
        functools.partial(later_kernel, bands),
        (),
        [SCALARS, FAR, UNREAD],
        [FAR, WHOLE],
        [((rest // 2, total_states, cols_z), BF16), ((8, LANES), F32)],
        [copies((bands,))],
        (ids, landed, whole),
    )
    later_link = lax.ppermute(later_pass, "domain", link_pairs)
    later_core = lax.ppermute(later_pass, "domain", core_pairs)

    steps, early_steps = lines // ROWS, (lines - late_lines) // ROWS
    block = pl.BlockSpec((ROWS, states, cols_z), lambda i: (i, 0, 0))
    applied, beside_token = call(
        functools.partial(beside_kernel, early_steps),
        (steps,),
        [
            block,
            block,
            pl.BlockSpec((ROWS, states, cols_z), lambda i: (jnp.minimum(i, early_steps - 1), 0, 0)),
            pl.BlockSpec((ROWS, states, cols_z), lambda i: (jnp.maximum(i - early_steps, 0), 0, 0)),
            UNREAD,
        ],
        [pl.BlockSpec((states, ROWS, cols_z), lambda i: (0, i, 0)), WHOLE],
        [((states, lines, cols_z), BF16), ((8, LANES), F32)],
        [],
        (added, core_field, link_early, link_late, later_token),
    )

    early_pass, early_token = call(
        functools.partial(early_kernel, share),
        (),
        [SCALARS, FAR, UNREAD] + [FAR] * (bands - 1),
        [FAR, WHOLE],
        [((first // 2, total_states, cols_z), BF16), ((8, LANES), F32)],
        [copies((bands,))],
        (ids, xt, beside_token, *early),
        micros=30,
    )
    early_link = lax.ppermute(early_pass, "domain", link_pairs)
    early_core = lax.ppermute(early_pass, "domain", core_pairs)
    squares = (2, total_states, total_states)
    (begun,) = call(
        functools.partial(gram_kernel, bands, first, share),
        (),
        [SCALARS, FAR, FAR, FAR, WHOLE, UNREAD],
        [WHOLE],
        [(squares, F32)],
        [
            pltpu.VMEM((bands * (rest + 1), states, cols_z), BF16),
            pltpu.VMEM((2, rest // 2, total_states, cols_z), BF16),
            copies((3,)),
        ],
        (ids, landed, later_core, later_link, pot, early_token),
    )
    parts = domains * bands
    (blocks,) = call(
        functools.partial(final_kernel, bands, share),
        (),
        [SCALARS, FAR, WHOLE, FAR, FAR, FAR, FAR, WHOLE, WHOLE] + [FAR] * (bands - 1),
        [WHOLE],
        [((parts, states, 2 * total_states // domains), BF16)],
        [
            pltpu.VMEM((first + 1, total_states, cols_z), BF16),
            pltpu.VMEM((group_share, total_states, LANES), BF16),
            pltpu.VMEM((2, first // 2, total_states, cols_z), BF16),
            pltpu.VMEM(squares, F32),
            copies((3 * bands + 2,)),
        ],
        (ids, xt, whole, landed, early_core, early_link, begun, pot, energy, *early),
    )
    summed = lax.all_to_all(blocks, ("domain", "band"), split_axis=0, concat_axis=0, tiled=True)
    (subspace,) = call(
        functools.partial(result_kernel, 1.0 / (lines * cols_z * domains)),
        (),
        [WHOLE],
        [WHOLE],
        [((2, states, total_states // domains), F32)],
        [],
        (summed,),
    )
    return applied.reshape(orbitals.shape), subspace


def solution(mesh):
    in_specs = (
        P("band", ("groups", "domain"), None, None),
        P(("groups", "domain"), None, None),
        P(("groups", "domain"), None, None),
        P(("groups", "domain")),
        P(("groups", "domain")),
        P(("groups", "domain")),
        P("groups", None),
    )
    out_specs = (P("band", ("groups", "domain"), None, None), P(None, ("groups", "band"), "domain"))
    return jax.shard_map(local, mesh=mesh, in_specs=in_specs, out_specs=out_specs, check_vma=False)
```

time: 102 us -> 135 us (1.32)
  Pallas kernels: 35.1 us -> 84 us
  local copies, waits for them, and re-layouts: 16.3 us -> 5.69 us
  waiting for transfers between devices: 5.22 us -> 0.45 us
    pallas_call x9, Pallas kernels: 35.1 us -> 84 us  [call(): pl.pallas_call(kernel, grid=grid, out_shape=[jax.ShapeDtypeStruct(shape,...]
    unnamed x37 -> x17, local copies, waits for them, and re-layouts: 14.6 us -> 2.44 us
    ppermute x1, waiting for transfers between devices: 4.1 us -> 0.01 us  [local(): later_link = lax.ppermute(later_pass, 'domain', link_pairs)]
  transfers between devices with their start and end apart: 14 -> 14, of which waited for: 2 -> 1; matrix products, arithmetic and copies ran while one was open for 4% -> 3% of each run, Pallas kernels for 29% -> 55%
where the time goes in v9:
time: 135 us; the launch traced here: 134 us
  Pallas kernels  84 us (62%)
  starting transfers between devices  25.1 us (19%)
  blocking collectives  15.7 us (12%)
  local copies, waits for them, and re-layouts  5.69 us (4%)
  between operations  1.53 us (1%)
    pallas_call x9, Pallas kernels, call(): pl.pallas_call(kernel, grid=grid, out_shape=[jax.ShapeDtypeStruct(shape,...  84 us
    all_to_all x1, blocking collectives, local(): lax.all_to_all(blocks, ('domain', 'band'), split_axis=0, concat_axis=0, t...  15.7 us
    all_to_all x1, starting transfers between devices, local(): lax.all_to_all(message, 'band', split_axis=0, concat_axis=0, tiled=True)  6.04 us
    ppermute x3, starting transfers between devices, swapped(): lax.ppermute(values[k - 1], axis, [(i, i ^ k) for i in range(size)])  3.69 us
    ppermute x1, starting transfers between devices, local(): later_link = lax.ppermute(later_pass, 'domain', link_pairs)  3.61 us
    ppermute x1, starting transfers between devices, local(): link_early = lax.ppermute(early_part, 'domain', link_pairs)  3.33 us
    ppermute x1, starting transfers between devices, local(): from_link = lax.ppermute(to_link, 'domain', link_pairs)  3.14 us
  transfers between devices with their start and end apart: 14, of which 1 were waited for; matrix products, arithmetic and copies ran while one was open for 3% of the time, Pallas kernels for 55%

profile of v9, /device:TPU:1, one launch (start us, length us, event | category | flops | bytes accessed | tf_op | source)
XLA Modules:
  0.0 133.7 jit_solution(4185152130305961026)
XLA Ops:
  0.6 4.1 %shard_map.95 = (bf16[128,64,128]{2,1,0:T(8,128)(2,1)}, bf16[64,64,128]{2,1,0:T(8,128)(2,1)}, bf16[64,64,128]{2,1,0:T(8,128)(2,1)}, bf16[100,64,128]{2,1,0:T(8,128)(2,1)}) custom-call(bf16[64,128,128]{2,1,0:T(8,128)(2,1)} %bitcast.13), custom_call_target="tpu_custom_call" | custom-call | flops 1100000 | bytes 1024 | tf_op jit(solution)/shard_map/pallas_call | solution.py:25
  4.9 6.0 %all-to-all-start = ((bf16[100,64,128]{2,1,0:T(8,128)(2,1)}), bf16[100,64,128]{2,1,0:T(8,128)(2,1)}, u32[]{:S(2)}, u32[]{:S(2)}) async-start(bf16[100,64,128]{2,1,0:T(8,128)(2,1)} %get-tuple-element.31), calls=%async_computation | async-start | bytes 3276800 | tf_op jit(solution)/shard_map/all_to_all | solution.py:401
  10.9 3.3 %collective-permute-start.3 = (bf16[64,64,128]{2,1,0:T(8,128)(2,1)}, bf16[64,64,128]{2,1,0:T(8,128)(2,1)}, u32[]{:S(2)}, u32[]{:S(2)}) collective-permute-start(bf16[64,64,128]{2,1,0:T(8,128)(2,1)} %get-tuple-element.28), channel_id=1, source_target_pairs={{4,8},{8,4},{5,9},{9,5},{6,10},{10,6},{7,11},{11,7},{20,24},{24,20... | collective-permute-start | bytes 3145736 | tf_op jit(solution)/shard_map/ppermute | solution.py:402
  16.1 11.0 %shard_map.96 = (f32[24,64,128]{2,1,0:T(8,128)}, bf16[64,64,128]{2,1,0:T(8,128)(2,1)}, bf16[16,64,128]{2,1,0:T(8,128)(2,1)}, bf16[16,64,128]{2,1,0:T(8,128)(2,1)}, bf16[8,64,128]{2,1,0:T(8,128)(2,1)}) custom-call(s32[384]{0:T(512)} %get-tuple-element.46.words_ref, s32[2]{0:T(128)} %pad_add_fusion.ids_ref, ...), custom_call_target="tpu_custom_call", output_to_operand_aliasing={{1}: (4, {})} | custom-call | flops 11000000512 | bytes 1024 | tf_op jit(solution)/shard_map/pallas_call | solution.py:25
  27.8 3.1 %collective-permute-start.1 = (bf16[16,64,128]{2,1,0:T(8,128)(2,1)}, bf16[16,64,128]{2,1,0:T(8,128)(2,1)S(1)}, u32[]{:S(2)}, u32[]{:S(2)}) collective-permute-start(bf16[16,64,128]{2,1,0:T(8,128)(2,1)} %get-tuple-element.26), channel_id=1, source_target_pairs={{4,8},{8,4},{5,9},{9,5},{6,10},{10,6},{7,11},{11,7},{20,24},{24,20... | collective-permute-start | bytes 786440 | tf_op jit(solution)/shard_map/ppermute | solution.py:426
  31.1 0.7 reshape.17.energy_ref
  31.8 2.4 %collective-permute-start.5 = (bf16[64,64,128]{2,1,0:T(8,128)(2,1)}, bf16[64,64,128]{2,1,0:T(8,128)(2,1)}, u32[]{:S(2)}, u32[]{:S(2)}) collective-permute-start(bf16[64,64,128]{2,1,0:T(8,128)(2,1)} %get-tuple-element.30), channel_id=1, source_target_pairs={{4,8},{8,4},{5,9},{9,5},{6,10},{10,6},{7,11},{11,7},{20,24},{24,20... | collective-permute-start | bytes 3145736 | tf_op jit(solution)/shard_map/ppermute | solution.py:429
  34.2 1.3 slice_bitcast_fusion.1.refs_1_
  35.5 1.3 slice_bitcast_fusion.refs_2_
  36.8 0.6 copy-done.7
  37.6 14.3 %shard_map.97 = (f32[128,64,128]{2,1,0:T(8,128)}, bf16[8,64,128]{2,1,0:T(8,128)(2,1)}, bf16[10,64,128]{2,1,0:T(8,128)(2,1)}, bf16[10,64,128]{2,1,0:T(8,128)(2,1)}, bf16[10,64,128]{2,1,0:T(8,128)(2,1)}) custom-call(s32[384]{0:T(512)} %get-tuple-element.47.words_ref, s32[2]{0:T(128)} %pad_add_fusion.ids_ref, bf16[128,64,128]{2,1,0:T(8,128)(2,1)} %get-tuple-element.22.xt_hbm, ...), custom_call_target="tpu_custom_call" | custom-call | flops 32999999488 | bytes 1024 | tf_op jit(solution)/shard_map/pallas_call | solution.py:25
  51.9 1.5 %collective-permute-start.6 = (bf16[10,64,128]{2,1,0:T(8,128)(2,1)}, bf16[10,64,128]{2,1,0:T(8,128)(2,1)S(1)}, u32[]{:S(2)}, u32[]{:S(2)}) collective-permute-start(bf16[10,64,128]{2,1,0:T(8,128)(2,1)} %get-tuple-element.36), channel_id=1, source_target_pairs={{0,1},{1,0},{2,3},{3,2},{4,5},{5,4},{6,7},{7,6},{8,9},{9,8},{10,11... | collective-permute-start | bytes 491528 | tf_op jit(solution)/shard_map/ppermute | solution.py:366
  53.4 2.1 %collective-permute-start.7 = (bf16[10,64,128]{2,1,0:T(8,128)(2,1)}, bf16[10,64,128]{2,1,0:T(8,128)(2,1)}, u32[]{:S(2)}, u32[]{:S(2)}) collective-permute-start(bf16[10,64,128]{2,1,0:T(8,128)(2,1)} %get-tuple-element.37), channel_id=1, source_target_pairs={{0,2},{1,3},{2,0},{3,1},{4,6},{5,7},{6,4},{7,5},{8,10},{9,11},{10,... | collective-permute-start | bytes 491528 | tf_op jit(solution)/shard_map/ppermute | solution.py:366
  55.6 26.2 %shard_map.98 = (bf16[12,256,128]{2,1,0:T(8,128)(2,1)}, f32[8,128]{1,0:T(8,128)}) custom-call(s32[2]{0:T(128)} %pad_add_fusion.ids_ref, bf16[100,64,128]{2,1,0:T(8,128)(2,1)} %all-to-all-done.landed.landed_hbm, bf16[8,64,128]{2,1,0:T(8,128)(2,1)} %get-tuple-element.32.unread.whole_ref), custom_call_target="tpu_custom_call" | custom-call | flops 1100000 | bytes 1024 | tf_op jit(solution)/shard_map/pallas_call | solution.py:25
  81.8 3.6 %collective-permute-start.12 = (bf16[12,256,128]{2,1,0:T(8,128)(2,1)}, bf16[12,256,128]{2,1,0:T(8,128)(2,1)S(1)}, u32[]{:S(2)}, u32[]{:S(2)}) collective-permute-start(bf16[12,256,128]{2,1,0:T(8,128)(2,1)} %get-tuple-element.40), channel_id=1, source_target_pairs={{4,8},{8,4},{5,9},{9,5},{6,10},{10,6},{7,11},{11,7},{20,24},{24,20... | collective-permute-start | bytes 2359304 | tf_op jit(solution)/shard_map/ppermute | solution.py:465
  85.5 7.6 %shard_map.99 = (bf16[64,128,128]{2,1,0:T(8,128)(2,1)}, f32[8,128]{1,0:T(8,128)}) custom-call(f32[128,64,128]{2,1,0:T(8,128)} %get-tuple-element.29.sum_ref, bf16[128,64,128]{2,1,0:T(8,128)(2,1)} %collective-permute-done.4.core_ref, bf16[64,64,128]{2,1,0:T(8,128)(2,1)} %collective-permute-done.3.early_ref, ...), custom_call_target="tpu_custom_call" | custom-call | flops 1100000 | bytes 1024 | tf_op jit(solution)/shard_map/pallas_call | solution.py:25
  93.2 0.6 copy-done.1
  93.8 10.3 %shard_map.100 = (bf16[4,256,128]{2,1,0:T(8,128)(2,1)}, f32[8,128]{1,0:T(8,128)}) custom-call(s32[2]{0:T(128)} %pad_add_fusion.ids_ref, bf16[128,64,128]{2,1,0:T(8,128)(2,1)} %get-tuple-element.22.xt_hbm, f32[8,128]{1,0:T(8,128)} %get-tuple-element.35.unread, bf16[10,64,128]{2,1,0:T(8,128)(2,1)} %copy-done.1, ...), custom_call_target="tpu_custom_call" | custom-call | flops 32999999488 | bytes 1024 | tf_op jit(solution)/shard_map/pallas_call | solution.py:25
  104.1 2.0 %collective-permute-start.10 = (bf16[4,256,128]{2,1,0:T(8,128)(2,1)}, bf16[4,256,128]{2,1,0:T(8,128)(2,1)}, u32[]{:S(2)}, u32[]{:S(2)}) collective-permute-start(bf16[4,256,128]{2,1,0:T(8,128)(2,1)} %get-tuple-element.39), channel_id=1, source_target_pairs={{4,8},{8,4},{5,9},{9,5},{6,10},{10,6},{7,11},{11,7},{20,24},{24,20... | collective-permute-start | bytes 786440 | tf_op jit(solution)/shard_map/ppermute | solution.py:496
  106.2 0.9 copy-done
  107.1 4.6 %shard_map.101.begun_hbm = f32[2,256,256]{2,1,0:T(8,128)} custom-call(s32[2]{0:T(128)} %pad_add_fusion.ids_ref, bf16[100,64,128]{2,1,0:T(8,128)(2,1)} %all-to-all-done.landed.landed_hbm, bf16[12,256,128]{2,1,0:T(8,128)(2,1)} %collective-permute-done.11.core_hbm, bf16[12,256,128]{2,1,0:T(8,128)(2,1)} %copy-done, f32[128,128]{1,0:T(8,128)} %bitcast.15, ...), custom_call_target="tpu_custom_call" | custom-call | flops 1100000 | bytes 1024 | tf_op jit(solution)/shard_map/pallas_call | solution.py:25
  112.2 4.1 %shard_map.102 = bf16[16,64,128]{2,1,0:T(8,128)(2,1)} custom-call(s32[2]{0:T(128)} %pad_add_fusion.ids_ref, bf16[128,64,128]{2,1,0:T(8,128)(2,1)} %get-tuple-element.22.xt_hbm, bf16[8,64,128]{2,1,0:T(8,128)(2,1)} %get-tuple-element.32.unread.whole_ref, bf16[100,64,128]{2,1,0:T(8,128)(2,1)} %all-to-all-done.landed.landed_hbm, ...), custom_call_target="tpu_custom_call" | custom-call | flops 1100000 | bytes 1024 | tf_op jit(solution)/shard_map/pallas_call | solution.py:25
  116.3 15.7 %all_to_all.10.parts_ref = bf16[16,64,128]{2,1,0:T(8,128)(2,1)} all-to-all(bf16[16,64,128]{2,1,0:T(8,128)(2,1)} %shard_map.102), channel_id=1, replica_groups=mesh['groups'=2,'domain'=4,'band'=4] {'domain','band'}, dimensions={0} | all-to-all | bytes 524288 | tf_op jit(solution)/shard_map/all_to_all | solution.py:528
  132.0 1.7 %shard_map.103 = f32[2,64,64]{2,1,0:T(8,128)} custom-call(bf16[16,64,128]{2,1,0:T(8,128)(2,1)} %all_to_all.10.parts_ref), custom_call_target="tpu_custom_call" | custom-call | flops 1100000 | bytes 1024 | tf_op jit(solution)/shard_map/pallas_call | solution.py:25
  (36 shorter events, 3.0 us)
Async XLA Ops:
  4.7 10.2 %copy-start.3 = (s32[384]{0:T(512)S(1)}, s32[384]{0:T(512)}, u32[]{:S(2)}) copy-start(s32[384]{0:T(512)} %param.12) | copy-start | bytes 4612
  4.7 10.2 %copy-start.4 = (s32[384]{0:T(512)S(1)}, s32[384]{0:T(512)}, u32[]{:S(2)}) copy-start(s32[384]{0:T(512)} %param.11) | copy-start | bytes 4612
  4.8 30.7 %collective-permute-start.4 = (bf16[128,64,128]{2,1,0:T(8,128)(2,1)}, bf16[128,64,128]{2,1,0:T(8,128)(2,1)}, u32[]{:S(2)}, u32[]{:S(2)}) collective-permute-start(bf16[128,64,128]{2,1,0:T(8,128)(2,1)} %get-tuple-element.22.xt_hbm), channel_id=1, source_target_pairs={{0,4},{4,0},{8,12},{12,8},{1,5},{5,1},{9,13},{13,9},{2,6},{6,2},{1... | collective-permute-start | bytes 6291464 | tf_op jit(solution)/shard_map/ppermute | solution.py:403
  4.9 50.7 %all-to-all-start = ((bf16[100,64,128]{2,1,0:T(8,128)(2,1)}), bf16[100,64,128]{2,1,0:T(8,128)(2,1)}, u32[]{:S(2)}, u32[]{:S(2)}) async-start(bf16[100,64,128]{2,1,0:T(8,128)(2,1)} %get-tuple-element.31), calls=%async_computation | async-start | bytes 3276800 | tf_op jit(solution)/shard_map/all_to_all | solution.py:401
  10.9 20.9 %collective-permute-start.3 = (bf16[64,64,128]{2,1,0:T(8,128)(2,1)}, bf16[64,64,128]{2,1,0:T(8,128)(2,1)}, u32[]{:S(2)}, u32[]{:S(2)}) collective-permute-start(bf16[64,64,128]{2,1,0:T(8,128)(2,1)} %get-tuple-element.28), channel_id=1, source_target_pairs={{4,8},{8,4},{5,9},{9,5},{6,10},{10,6},{7,11},{11,7},{20,24},{24,20... | collective-permute-start | bytes 3145736 | tf_op jit(solution)/shard_map/ppermute | solution.py:402
  16.1 14.9 %copy-start.2 = (f32[256,16]{0,1:T(8,128)S(1)}, f32[256,16]{0,1:T(8,128)}, u32[]{:S(2)}) copy-start(f32[256,16]{0,1:T(8,128)} %param.14) | copy-start | bytes 49156
  27.1 9.6 %collective-permute-start.2 = (bf16[8,64,128]{2,1,0:T(8,128)(2,1)}, bf16[8,64,128]{2,1,0:T(8,128)(2,1)S(1)}, u32[]{:S(2)}, u32[]{:S(2)}) collective-permute-start(bf16[8,64,128]{2,1,0:T(8,128)(2,1)} %get-tuple-element.27), channel_id=1, source_target_pairs={{0,8},{4,12},{8,0},{12,4},{1,9},{5,13},{9,1},{13,5},{2,10},{6,14},... | collective-permute-start | bytes 393224 | tf_op jit(solution)/shard_map/ppermute | solution.py:427
  27.2 9.5 %collective-permute-start = (bf16[16,64,128]{2,1,0:T(8,128)(2,1)}, bf16[16,64,128]{2,1,0:T(8,128)(2,1)S(1)}, u32[]{:S(2)}, u32[]{:S(2)}) collective-permute-start(bf16[16,64,128]{2,1,0:T(8,128)(2,1)} %get-tuple-element.25), channel_id=1, source_target_pairs={{0,4},{4,0},{8,12},{12,8},{1,5},{5,1},{9,13},{13,9},{2,6},{6,2},{1... | collective-permute-start | bytes 786440 | tf_op jit(solution)/shard_map/ppermute | solution.py:428
  27.8 8.9 %collective-permute-start.1 = (bf16[16,64,128]{2,1,0:T(8,128)(2,1)}, bf16[16,64,128]{2,1,0:T(8,128)(2,1)S(1)}, u32[]{:S(2)}, u32[]{:S(2)}) collective-permute-start(bf16[16,64,128]{2,1,0:T(8,128)(2,1)} %get-tuple-element.26), channel_id=1, source_target_pairs={{4,8},{8,4},{5,9},{9,5},{6,10},{10,6},{7,11},{11,7},{20,24},{24,20... | collective-permute-start | bytes 786440 | tf_op jit(solution)/shard_map/ppermute | solution.py:426
  31.8 53.6 %collective-permute-start.5 = (bf16[64,64,128]{2,1,0:T(8,128)(2,1)}, bf16[64,64,128]{2,1,0:T(8,128)(2,1)}, u32[]{:S(2)}, u32[]{:S(2)}) collective-permute-start(bf16[64,64,128]{2,1,0:T(8,128)(2,1)} %get-tuple-element.30), channel_id=1, source_target_pairs={{4,8},{8,4},{5,9},{9,5},{6,10},{10,6},{7,11},{11,7},{20,24},{24,20... | collective-permute-start | bytes 3145736 | tf_op jit(solution)/shard_map/ppermute | solution.py:429
  36.7 0.7 copy-start.7
  36.8 0.8 copy-start.5
  36.8 0.8 copy-start.6
  51.9 41.3 %collective-permute-start.6 = (bf16[10,64,128]{2,1,0:T(8,128)(2,1)}, bf16[10,64,128]{2,1,0:T(8,128)(2,1)S(1)}, u32[]{:S(2)}, u32[]{:S(2)}) collective-permute-start(bf16[10,64,128]{2,1,0:T(8,128)(2,1)} %get-tuple-element.36), channel_id=1, source_target_pairs={{0,1},{1,0},{2,3},{3,2},{4,5},{5,4},{6,7},{7,6},{8,9},{9,8},{10,11... | collective-permute-start | bytes 491528 | tf_op jit(solution)/shard_map/ppermute | solution.py:366
  53.4 39.7 %collective-permute-start.7 = (bf16[10,64,128]{2,1,0:T(8,128)(2,1)}, bf16[10,64,128]{2,1,0:T(8,128)(2,1)}, u32[]{:S(2)}, u32[]{:S(2)}) collective-permute-start(bf16[10,64,128]{2,1,0:T(8,128)(2,1)} %get-tuple-element.37), channel_id=1, source_target_pairs={{0,2},{1,3},{2,0},{3,1},{4,6},{5,7},{6,4},{7,5},{8,10},{9,11},{10,... | collective-permute-start | bytes 491528 | tf_op jit(solution)/shard_map/ppermute | solution.py:366
  55.5 37.7 %collective-permute-start.8 = (bf16[10,64,128]{2,1,0:T(8,128)(2,1)}, bf16[10,64,128]{2,1,0:T(8,128)(2,1)}, u32[]{:S(2)}, u32[]{:S(2)}) collective-permute-start(bf16[10,64,128]{2,1,0:T(8,128)(2,1)} %get-tuple-element.38), channel_id=1, source_target_pairs={{0,3},{1,2},{2,1},{3,0},{4,7},{5,6},{6,5},{7,4},{8,11},{9,10},{10,... | collective-permute-start | bytes 491528 | tf_op jit(solution)/shard_map/ppermute | solution.py:366
  81.8 24.4 %collective-permute-start.12 = (bf16[12,256,128]{2,1,0:T(8,128)(2,1)}, bf16[12,256,128]{2,1,0:T(8,128)(2,1)S(1)}, u32[]{:S(2)}, u32[]{:S(2)}) collective-permute-start(bf16[12,256,128]{2,1,0:T(8,128)(2,1)} %get-tuple-element.40), channel_id=1, source_target_pairs={{4,8},{8,4},{5,9},{9,5},{6,10},{10,6},{7,11},{11,7},{20,24},{24,20... | collective-permute-start | bytes 2359304 | tf_op jit(solution)/shard_map/ppermute | solution.py:465
  85.4 20.8 %collective-permute-start.11 = (bf16[12,256,128]{2,1,0:T(8,128)(2,1)}, bf16[12,256,128]{2,1,0:T(8,128)(2,1)}, u32[]{:S(2)}, u32[]{:S(2)}) collective-permute-start(bf16[12,256,128]{2,1,0:T(8,128)(2,1)} %get-tuple-element.40), channel_id=1, source_target_pairs={{0,4},{4,0},{8,12},{12,8},{1,5},{5,1},{9,13},{13,9},{2,6},{6,2},{1... | collective-permute-start | bytes 2359304 | tf_op jit(solution)/shard_map/ppermute | solution.py:466
  93.1 0.7 copy-start.1
  104.1 8.0 %collective-permute-start.10 = (bf16[4,256,128]{2,1,0:T(8,128)(2,1)}, bf16[4,256,128]{2,1,0:T(8,128)(2,1)}, u32[]{:S(2)}, u32[]{:S(2)}) collective-permute-start(bf16[4,256,128]{2,1,0:T(8,128)(2,1)} %get-tuple-element.39), channel_id=1, source_target_pairs={{4,8},{8,4},{5,9},{9,5},{6,10},{10,6},{7,11},{11,7},{20,24},{24,20... | collective-permute-start | bytes 786440 | tf_op jit(solution)/shard_map/ppermute | solution.py:496
  106.1 6.1 %collective-permute-start.9 = (bf16[4,256,128]{2,1,0:T(8,128)(2,1)}, bf16[4,256,128]{2,1,0:T(8,128)(2,1)}, u32[]{:S(2)}, u32[]{:S(2)}) collective-permute-start(bf16[4,256,128]{2,1,0:T(8,128)(2,1)} %get-tuple-element.39), channel_id=1, source_target_pairs={{0,4},{4,0},{8,12},{12,8},{1,5},{5,1},{9,13},{13,9},{2,6},{6,2},{1... | collective-permute-start | bytes 786440 | tf_op jit(solution)/shard_map/ppermute | solution.py:497
  106.2 0.9 copy-start

commit v10 on v7

--- a/solution.py
+++ b/solution.py
@@ -17,13 +17,14 @@
 NEAR = pl.BlockSpec(memory_space=pltpu.VMEM)
 SCALARS = pl.BlockSpec(memory_space=pltpu.SMEM)
 FAR = pl.BlockSpec(memory_space=pltpu.HBM)
+PINNED = pl.BlockSpec(memory_space=pltpu.HBM)
 UNREAD = pl.BlockSpec(memory_space=pl.ANY)
 copies = pltpu.SemaphoreType.DMA
 
 
 def call(room, kernel, grid, in_specs, out_specs, outs, scratch, args, aliases=None, micros=0.001):
     def place(spec):
-        return pltpu.VMEM if spec is NEAR else None
+        return {id(NEAR): pltpu.VMEM, id(PINNED): pltpu.HBM}.get(id(spec))
 
     args = [
         pltpu.with_memory_space_constraint(arg, place(spec)) if place(spec) else arg
@@ -81,12 +82,19 @@
         copy.wait()
 
 
-def bases(ids_ref, groups):
-    odd, upper = ids_ref[0] & 1, (ids_ref[0] >> 1) & 1
+def bases(groups):
+    domain = lax.axis_index("domain")
+    odd, upper = domain & 1, (domain >> 1) & 1
     return [2 * groups * side for side in (1 - odd, odd, 1 - upper, upper)]
 
 
-def project_kernel(words_ref, ids_ref, xt_ref, p_hbm, mine_ref, core_ref, link_ref, *refs):
+def slot_at(t, atom_ref, line_ref, count_ref, atoms_here):
+    first = (lax.axis_index("domain") - 1) * atoms_here
+    atom = jnp.clip(atom_ref[t] - first, 0, 3 * atoms_here - 1)
+    return line_ref[t], atom, t < count_ref[0]
+
+
+def project_kernel(atom_ref, line_ref, count_ref, xt_ref, p_hbm, handed, mine_ref, same, core_ref, link_ref, *refs):
     far_refs, (total, p_ref, sems) = refs[:-3], refs[-3:]
     slots, proj_count, _ = p_ref.shape
     groups, states = mine_ref.shape[0] // 3, mine_ref.shape[1]
@@ -109,9 +117,9 @@
     def body(i, carry):
         for u in range(unroll):
             t = i * unroll + u
-            word = words_ref[t]
-            line, atom = word >> 16, word & 0xFFFF
-            total[atom] += lax.dot_general(p_ref[t], xt_ref[line], NT, preferred_element_type=F32)
+            line, atom, live = slot_at(t, atom_ref, line_ref, count_ref, groups * per_group)
+            part = lax.dot_general(p_ref[t], xt_ref[line], NT, preferred_element_type=F32)
+            total[jnp.where(live, atom, 3 * groups * per_group)] += part
         return carry
 
     for c in range(chunks):
@@ -121,7 +129,7 @@
     for g in range(3 * groups):
         tiles = [total[g * per_group + u] for u in range(per_group)]
         mine_ref[g] = jnp.concatenate(tiles, axis=0).T
-    sides = bases(ids_ref, groups)
+    sides = bases(groups)
     for g in range(groups):
         own = mine_ref[groups + g].astype(BF16)
         for side, ref in zip(sides[:2], (core_ref, link_ref)):
@@ -131,23 +139,28 @@
             ref[g] = mine_ref[side + g].astype(BF16)
 
 
-def nonlocal_kernel(first, fars, words_ref, ids_ref, xt_ref, p_hbm, energy_ref, mine_ref, core_ref, link_ref, *refs):
-    far_refs, (_, _, _, out_ref, whole_ref, done_ref, _, *messages, total, atoms, p_ref, sem) = refs[:fars], refs[fars:]
+def nonlocal_kernel(
+    first, fars, atom_ref, line_ref, count_ref, xt_ref, p_hbm, energy_ref, mine_ref, core_ref, link_ref, *refs
+):
+    far_refs, (_, _, out_hbm, whole_hbm, done_ref, *messages, lines_sum, whole_ref, total, atoms, p_ref, sems) = (
+        refs[:fars],
+        refs[fars:],
+    )
     slots, proj_count, _ = p_ref.shape
     groups, states = mine_ref.shape[0] // 3, mine_ref.shape[1]
     per_group = LANES // proj_count
-    lines = out_ref.shape[0]
+    lines = xt_ref.shape[0]
     unroll = 16
-    load = start(pltpu.make_async_copy(p_hbm, p_ref, sem))
+    load = start(pltpu.make_async_copy(p_hbm, p_ref, sems.at[0]))
     done_ref[...] = jnp.zeros_like(done_ref)
 
     def clear(i, carry):
-        out_ref[i] = jnp.zeros((states, LANES), F32)
+        lines_sum[i] = jnp.zeros((states, LANES), F32)
         return carry
 
-    lax.fori_loop(0, lines, clear, 0)
+    lax.fori_loop(0, lines + 1, clear, 0)
     total[...] = mine_ref[...]
-    sides = bases(ids_ref, groups)
+    sides = bases(groups)
     for g in range(groups):
         total[groups + g] += core_ref[g].astype(F32) + link_ref[g].astype(F32)
         for side, ref in zip(sides[:2], (core_ref, link_ref)):
@@ -156,16 +169,17 @@
             total[side + g] += ref[g].astype(F32)
     last = energy_ref.shape[0] - 1
     for g in range(3 * groups):
-        row = jnp.clip((ids_ref[0] - 1) * groups + g, 0, last)
+        row = jnp.clip((lax.axis_index("domain") - 1) * groups + g, 0, last)
         tile = (total[g] * energy_ref[pl.ds(row, 1), :]).astype(BF16)
         for u in range(per_group):
             atoms[g * per_group + u] = tile[:, u * proj_count : (u + 1) * proj_count]
     for g in range(groups):
         whole_ref[g] = total[groups + g].astype(BF16)
+    send_whole = start(pltpu.make_async_copy(whole_ref, whole_hbm, sems.at[1]))
     share = xt_ref.shape[0] // (len(messages) + 1)
     held = groups // (len(messages) + 1)
     for k, message in enumerate(messages, 1):
-        to = ids_ref[1] ^ k
+        to = lax.axis_index("band") ^ k
         for i in range(first):
             message[i] = xt_ref[to * share + i]
         for i in range(held):
@@ -175,12 +189,15 @@
     def body(i, carry):
         for u in range(unroll):
             t = i * unroll + u
-            word = words_ref[t]
-            line, atom = word >> 16, word & 0xFFFF
-            out_ref[line] += jnp.dot(atoms[atom], p_ref[t], preferred_element_type=F32)
+            line, atom, live = slot_at(t, atom_ref, line_ref, count_ref, groups * per_group)
+            part = jnp.dot(atoms[atom], p_ref[t], preferred_element_type=F32)
+            lines_sum[jnp.where(live, line, lines)] += part
         return carry
 
     lax.fori_loop(0, slots // unroll, body, 0)
+    send = start(pltpu.make_async_copy(lines_sum.at[pl.ds(0, lines)], out_hbm, sems.at[2]))
+    send_whole.wait()
+    send.wait()
 
 
 def stencil_kernel(early_steps, xt_ref, core_ref, early_ref, late_ref, added_ref, pot_ref, ring_ref, unread, out_ref, done_ref):
@@ -188,32 +205,35 @@
     lines = xt_ref.shape[0]
     done_ref[...] = jnp.zeros_like(done_ref)
     step = pl.program_id(0)
-    y0 = step * here
     early = step < early_steps
-    for s0 in range(0, states, ROWS):
-        rows = slice(s0, s0 + ROWS)
-        results = []
-        cells = jnp.concatenate([xt_ref[y0 + i, rows, :] for i in range(here)], axis=0)
-        along = jnp.dot(cells, ring_ref[...], preferred_element_type=F32)
-        before = xt_ref[lax.rem(y0 + lines - 1, lines), rows, :].astype(F32)
-        x = xt_ref[y0, rows, :].astype(F32)
-        for i in range(here):
-            after = xt_ref[lax.rem(y0 + i + 1, lines), rows, :].astype(F32)
-            link = jnp.where(early, early_ref[i, rows, :].astype(F32), late_ref[i, rows, :].astype(F32))
-            beside = (before + after) + (core_ref[i, rows, :].astype(F32) + link)
-            value = along[i * ROWS : (i + 1) * ROWS] + pot_ref[i : i + 1, :] * x
-            results.append(value + added_ref[y0 + i, rows, :] - 0.5 * beside)
-            before, x = x, after
-        out_ref[rows, :, :] = jnp.swapaxes(jnp.stack(results, axis=0), 0, 1).astype(BF16)
-
-
-def pass_half(ids_ref, all_ref, pass_hbm, sem):
+    for part in range(0, here, ROWS):
+        y0 = step * here + part
+        for s0 in range(0, states, ROWS):
+            rows = slice(s0, s0 + ROWS)
+            results = []
+            cells = jnp.concatenate([xt_ref[y0 + i, rows, :] for i in range(ROWS)], axis=0)
+            along = jnp.dot(cells, ring_ref[...], preferred_element_type=F32)
+            before = xt_ref[lax.rem(y0 + lines - 1, lines), rows, :].astype(F32)
+            x = xt_ref[y0, rows, :].astype(F32)
+            for i in range(ROWS):
+                after = xt_ref[lax.rem(y0 + i + 1, lines), rows, :].astype(F32)
+                link = jnp.where(early, early_ref[part + i, rows, :], late_ref[part + i, rows, :]).astype(F32)
+                beside = (before + after) + (core_ref[part + i, rows, :].astype(F32) + link)
+                value = along[i * ROWS : (i + 1) * ROWS] + pot_ref[part + i : part + i + 1, :] * x
+                results.append(value + added_ref[part + i, rows, :] - 0.5 * beside)
+                before, x = x, after
+            turned = jnp.swapaxes(jnp.stack(results, axis=0), 0, 1).astype(BF16)
+            out_ref[rows, part : part + ROWS, :] = turned
+
+
+def pass_half(all_ref, pass_hbm, sem):
     half = pass_hbm.shape[0]
-    copy = start(pltpu.make_async_copy(all_ref.at[pl.ds((1 - (ids_ref[0] & 1)) * half, half)], pass_hbm, sem))
+    copy = start(pltpu.make_async_copy(all_ref.at[pl.ds((1 - (lax.axis_index("domain") & 1)) * half, half)], pass_hbm, sem))
     copy.wait()
 
 
-def later_kernel(bands, ids_ref, landed, unread, all_ref, pass_hbm, sems, pass_sem):
+def later_kernel(bands, landed, unread, all_ref, pass_hbm, done_ref, sems, pass_sem):
+    done_ref[...] = jnp.zeros_like(done_ref)
     count, states = all_ref.shape[0], landed.shape[1]
     loads = [
         start(
@@ -225,13 +245,14 @@
     ]
     for copy in loads:
         copy.wait()
-    pass_half(ids_ref, all_ref, pass_hbm, pass_sem)
-
-
-def early_kernel(bands, share, ids_ref, xt_ref, whole_ref, after_ref, unread, *refs):
-    pieces, (all_ref, pass_hbm, projs_ref, sems, pass_sem) = refs[: bands - 1], refs[bands - 1 :]
+    pass_half(all_ref, pass_hbm, pass_sem)
+
+
+def early_kernel(bands, share, xt_ref, whole_ref, after_ref, unread, *refs):
+    pieces, (all_ref, pass_hbm, projs_ref, done_ref, sems, pass_sem) = refs[: bands - 1], refs[bands - 1 :]
+    done_ref[...] = jnp.zeros_like(done_ref)
     states = xt_ref.shape[1]
-    band = ids_ref[1]
+    band = lax.axis_index("band")
     count, held = all_ref.shape[0] - 1, projs_ref.shape[0]
     loads = []
 
@@ -249,13 +270,13 @@
     load(after_ref.at[pl.ds(0, 1)], all_ref.at[pl.ds(count, 1)])
     for copy in loads:
         copy.wait()
-    pass_half(ids_ref, all_ref, pass_hbm, pass_sem)
-
-
-def add_products(row, ids_ref, all_ref, core_ref, link_ref, pot_ref, acc):
+    pass_half(all_ref, pass_hbm, pass_sem)
+
+
+def add_products(row, all_ref, core_ref, link_ref, pot_ref, acc):
     half = core_ref.shape[0]
     group = 4
-    mine = (ids_ref[0] & 1) * half
+    mine = (lax.axis_index("domain") & 1) * half
     for part, base in ((0, mine), (1, half - mine)):
         for i0 in range(0, half, group):
             xs, ys = [], []
@@ -274,18 +295,18 @@
             acc[1] += lax.dot_general(flat_y, flat_x, NT, preferred_element_type=F32)
 
 
-def gram_kernel(first, share, ids_ref, all_ref, core_ref, link_ref, pot_ref, unread, acc):
+def gram_kernel(first, share, all_ref, core_ref, link_ref, pot_ref, unread, acc):
     acc[...] = jnp.zeros_like(acc)
-    add_products(ids_ref[1] * share + first, ids_ref, all_ref, core_ref, link_ref, pot_ref, acc)
+    add_products(lax.axis_index("band") * share + first, all_ref, core_ref, link_ref, pot_ref, acc)
 
 
 def final_kernel(
-    bands, share, ids_ref, all_ref, core_ref, link_ref, pot_ref, begun_ref, proj_ref, energy_ref, out_ref, acc
+    bands, share, all_ref, core_ref, link_ref, pot_ref, begun_ref, proj_ref, energy_ref, out_ref, acc
 ):
     acc[...] = begun_ref[...]
-    add_products(ids_ref[1] * share, ids_ref, all_ref, core_ref, link_ref, pot_ref, acc)
+    add_products(lax.axis_index("band") * share, all_ref, core_ref, link_ref, pot_ref, acc)
     groups = proj_ref.shape[0]
-    first = (ids_ref[0] * bands + ids_ref[1]) * groups
+    first = (lax.axis_index("domain") * bands + lax.axis_index("band")) * groups
     for g in range(groups):
         here = proj_ref[g]
         scaled = (here.astype(F32) * energy_ref[pl.ds(first + g, 1), :]).astype(BF16)
@@ -312,7 +333,6 @@
     slots, proj_count, _ = projectors.shape
     atom_total = energies.shape[0]
     domains, bands = lax.axis_size("domain"), lax.axis_size("band")
-    domain, band = lax.axis_index("domain"), lax.axis_index("band")
     total_states = states * bands
     atoms_here = atom_total // domains
     per_group = LANES // proj_count
@@ -333,18 +353,13 @@
         got = {k: lax.ppermute(values[k - 1], axis, [(i, i ^ k) for i in range(size)]) for k in range(size - 1, 0, -1)}
         return [got[k] for k in range(1, size)]
 
-    ids = jnp.stack([domain, band]).astype(jnp.int32)
-    near = jnp.clip(tile_atom - (domain - 1) * atoms_here, 0, 3 * atoms_here - 1)
-    live = jnp.arange(slots, dtype=jnp.int32) < tile_count[0]
-    project_words = (tile_line << 16) | jnp.where(live, near, 3 * atoms_here)
-    nonlocal_words = (jnp.where(live, tile_line, lines) << 16) | near
     field = orbitals.reshape(states, lines, cols_z)
     pot = potential.reshape(lines, cols_z)
     energy = energies.reshape(atom_total // per_group, LANES)
     eye = np.eye(cols_z, dtype=np.float32)
     ring = jnp.asarray(3.0 * eye - 0.5 * (np.roll(eye, 1, axis=0) + np.roll(eye, -1, axis=0)), dtype=BF16)
 
-    late_lines = lines // 4
+    late_lines = lines // 2
     line_shape, late_shape = (lines, states, cols_z), (late_lines, states, cols_z)
     xt, xt_far, early_part, late_part, message = call(
         58,
@@ -367,13 +382,13 @@
     core_field = lax.ppermute(xt_far, "domain", core_pairs)
 
     group_shape = (groups, states, LANES)
-    mine, to_core, to_link, *to_far = call(
+    mine, late_part, to_core, to_link, *to_far = call(
         50,
         project_kernel,
         (),
-        [SCALARS, SCALARS, NEAR, FAR],
-        [NEAR] + [WHOLE] * (2 + len(far_pairs)),
-        [((3 * groups, states, LANES), F32)]
+        [SCALARS] * 3 + [NEAR, PINNED, UNREAD],
+        [NEAR, UNREAD] + [WHOLE] * (2 + len(far_pairs)),
+        [((3 * groups, states, LANES), F32), (late_shape, BF16)]
         + [((2 * groups, states, LANES), BF16)] * 2
         + [(group_shape, BF16)] * len(far_pairs),
         [
@@ -381,51 +396,54 @@
             pltpu.VMEM(projectors.shape, BF16),
             copies((4,)),
         ],
-        (project_words, ids, xt, projectors),
+        (tile_atom, tile_line, tile_count, xt, projectors, late_part),
+        aliases={5: 1},
+        micros=10,
     )
     from_link = lax.ppermute(to_link, "domain", link_pairs)
     from_far = [lax.ppermute(value, "domain", pairs) for value, pairs in zip(to_far, far_pairs)]
     from_core = lax.ppermute(to_core, "domain", core_pairs)
-    added, whole, summed_up, late_part, *messages = call(
+    link_late = lax.ppermute(late_part, "domain", link_pairs)
+    added, whole, summed_up, *messages = call(
         32,
         functools.partial(nonlocal_kernel, first, len(far_pairs)),
         (),
-        [SCALARS, SCALARS, NEAR, FAR, WHOLE, NEAR, WHOLE, WHOLE] + [WHOLE] * len(far_pairs) + [UNREAD] * 3,
-        [WHOLE, NEAR, WHOLE, UNREAD] + [WHOLE] * (bands - 1),
-        [((lines + 1, states, cols_z), F32), (group_shape, BF16), ((8, LANES), F32), (late_shape, BF16)]
+        [SCALARS] * 3 + [NEAR, PINNED, WHOLE, NEAR, WHOLE, WHOLE] + [WHOLE] * len(far_pairs) + [UNREAD] * 2,
+        [PINNED, PINNED, WHOLE] + [WHOLE] * (bands - 1),
+        [(line_shape, F32), (group_shape, BF16), ((8, LANES), F32)]
         + [((first + group_share, states, cols_z), BF16)] * (bands - 1),
         [
+            pltpu.VMEM((lines + 1, states, cols_z), F32),
+            pltpu.VMEM(group_shape, BF16),
             pltpu.VMEM((3 * groups, states, LANES), F32),
             pltpu.VMEM((3 * atoms_here, states, proj_count), BF16),
             pltpu.VMEM(projectors.shape, BF16),
-            copies,
+            copies((3,)),
         ],
         (
-            nonlocal_words, ids, xt, projectors, energy, mine, from_core, from_link, *from_far,
-            link_early[0, :ROWS], core_field[0, :ROWS], late_part,
+            tile_atom, tile_line, tile_count, xt, projectors, energy, mine, from_core, from_link, *from_far,
+            link_early[0, :ROWS], core_field[0, :ROWS],
         ),
-        aliases={10 + len(far_pairs): 3},
         micros=30,
     )
-    link_late = lax.ppermute(late_part, "domain", link_pairs)
     early = swapped(messages, "band")
 
-    later_all, later_pass = call(
+    later_all, later_pass, later_token = call(
         32,
         functools.partial(later_kernel, bands),
         (),
-        [SCALARS, FAR, UNREAD],
-        [NEAR, FAR],
-        [((rest + 1, total_states, cols_z), BF16), ((rest // 2, total_states, cols_z), BF16)],
+        [FAR, UNREAD],
+        [NEAR, FAR, WHOLE],
+        [((rest + 1, total_states, cols_z), BF16), ((rest // 2, total_states, cols_z), BF16), ((8, LANES), F32)],
         [copies((bands,)), copies],
-        (ids, landed, summed_up),
-        micros=10,
+        (landed, summed_up),
     )
     later_link = lax.ppermute(later_pass, "domain", link_pairs)
     later_core = lax.ppermute(later_pass, "domain", core_pairs)
 
-    steps, early_steps = lines // ROWS, (lines - late_lines) // ROWS
-    block = pl.BlockSpec((ROWS, states, cols_z), lambda i: (i, 0, 0))
+    span = 2 * ROWS
+    steps, early_steps = lines // span, (lines - late_lines) // span
+    block = pl.BlockSpec((span, states, cols_z), lambda i: (i, 0, 0))
     applied, done = call(
         32,
         functools.partial(stencil_kernel, early_steps),
@@ -433,32 +451,36 @@
         [
             NEAR,
             block,
-            pl.BlockSpec((ROWS, states, cols_z), lambda i: (jnp.minimum(i, early_steps - 1), 0, 0)),
-            pl.BlockSpec((ROWS, states, cols_z), lambda i: (jnp.maximum(i - early_steps, 0), 0, 0)),
-            WHOLE,
-            pl.BlockSpec((ROWS, cols_z), lambda i: (i, 0)),
+            pl.BlockSpec((span, states, cols_z), lambda i: (jnp.minimum(i, early_steps - 1), 0, 0)),
+            pl.BlockSpec((span, states, cols_z), lambda i: (jnp.maximum(i - early_steps, 0), 0, 0)),
+            block,
+            pl.BlockSpec((span, cols_z), lambda i: (i, 0)),
             WHOLE,
             UNREAD,
         ],
-        [pl.BlockSpec((states, ROWS, cols_z), lambda i: (0, i, 0)), WHOLE],
+        [pl.BlockSpec((states, span, cols_z), lambda i: (0, i, 0)), WHOLE],
         [((states, lines, cols_z), BF16), ((8, LANES), F32)],
         [],
-        (xt, core_field, link_early, link_late, added, pot, ring, later_all),
-    )
-
-    early_all, early_pass, projs = call(
+        (
+            xt, core_field, link_early, link_late, pltpu.with_memory_space_constraint(added, pltpu.HBM), pot, ring,
+            later_token,
+        ),
+    )
+
+    early_all, early_pass, projs, early_token = call(
         32,
         functools.partial(early_kernel, bands, share),
         (),
-        [SCALARS, NEAR, NEAR, NEAR, WHOLE] + [FAR] * (bands - 1),
-        [NEAR, FAR, NEAR],
+        [NEAR, PINNED, NEAR, WHOLE] + [FAR] * (bands - 1),
+        [NEAR, FAR, NEAR, WHOLE],
         [
             ((first + 1, total_states, cols_z), BF16),
             ((first // 2, total_states, cols_z), BF16),
             ((group_share, total_states, LANES), BF16),
+            ((8, LANES), F32),
         ],
         [copies((2 * bands + 1,)), copies],
-        (ids, xt, whole, later_all, done, *early),
+        (xt, whole, later_all, done, *early),
         micros=30,
     )
     early_link = lax.ppermute(early_pass, "domain", link_pairs)
@@ -467,22 +489,22 @@
         32,
         functools.partial(gram_kernel, first, share),
         (),
-        [SCALARS, NEAR, WHOLE, WHOLE, WHOLE, NEAR],
+        [NEAR, WHOLE, WHOLE, WHOLE, UNREAD],
         [NEAR],
         [((2, total_states, total_states), F32)],
         [],
-        (ids, later_all, later_core, later_link, pot, early_all),
+        (later_all, later_core, later_link, pot, early_token),
     )
     parts = domains * bands
     (blocks,) = call(
         32,
         functools.partial(final_kernel, bands, share),
         (),
-        [SCALARS, NEAR, WHOLE, WHOLE, WHOLE, NEAR, NEAR, WHOLE],
+        [NEAR, WHOLE, WHOLE, WHOLE, NEAR, NEAR, WHOLE],
         [WHOLE],
         [((parts, states, 2 * total_states // domains), BF16)],
         [pltpu.VMEM((2, total_states, total_states), F32)],
-        (ids, early_all, early_core, early_link, pot, begun, projs, energy),
+        (early_all, early_core, early_link, pot, begun, projs, energy),
     )
     summed = lax.all_to_all(blocks, ("domain", "band"), split_axis=0, concat_axis=0, tiled=True)
     (subspace,) = call(

time: 97.7 us -> 92.7 us (0.949)
  local copies, waits for them, and re-layouts: 5.62 us -> 10.6 us
  waiting for transfers between devices: 7.61 us -> 4.09 us
  Pallas kernels: 38.1 us -> 35.1 us
  starting transfers between devices: 28.1 us -> 25.6 us
    unnamed x23, local copies, waits for them, and re-layouts: 4.17 us -> 8.9 us
    ppermute x1, waiting for transfers between devices: 3.28 us -> 0.01 us  [local(): from_link = lax.ppermute(to_link, 'domain', link_pairs)]
    pallas_call x9, Pallas kernels: 38.1 us -> 35.1 us  [call(): pl.pallas_call(kernel, grid=grid, out_shape=shapes, in_specs=in_specs, ou...]
    ppermute x1, starting transfers between devices: 4.5 us -> 3.05 us  [local(): later_link = lax.ppermute(later_pass, 'domain', link_pairs)]
    ppermute x1, waiting for transfers between devices: 2.69 us -> 3.95 us  [local(): early_link = lax.ppermute(early_pass, 'domain', link_pairs)]
  transfers between devices with their start and end apart: 14 -> 14, of which waited for: 4 -> 2; matrix products, arithmetic and copies ran while one was open for 2% -> 3% of each run, Pallas kernels for 33% -> 32%
where the time goes in v10:
time: 92.7 us; the launch traced here: 91.1 us
  Pallas kernels  35.1 us (38%)
  starting transfers between devices  25.6 us (28%)
  blocking collectives  14.3 us (15%)
  local copies, waits for them, and re-layouts  10.6 us (11%)
  waiting for transfers between devices  4.09 us (4%)
  between operations  1.54 us (2%)
    pallas_call x9, Pallas kernels, call(): pl.pallas_call(kernel, grid=grid, out_shape=shapes, in_specs=in_specs, ou...  35.1 us
    all_to_all x1, blocking collectives, local(): lax.all_to_all(blocks, ('domain', 'band'), split_axis=0, concat_axis=0, t...  14.3 us
    unnamed x23, local copies, waits for them, and re-layouts  8.9 us
    ppermute x1, starting transfers between devices, local(): link_early = lax.ppermute(early_part, 'domain', link_pairs)  4.6 us
    all_to_all x1, starting transfers between devices, local(): lax.all_to_all(message, 'band', split_axis=0, concat_axis=0, tiled=True)  4.6 us
    ppermute x3, starting transfers between devices, swapped(): lax.ppermute(values[k - 1], axis, [(i, i ^ k) for i in range(size)])  3.98 us
    ppermute x1, waiting for transfers between devices, local(): early_link = lax.ppermute(early_pass, 'domain', link_pairs)  3.95 us
    ppermute x1, starting transfers between devices, local(): later_link = lax.ppermute(later_pass, 'domain', link_pairs)  3.05 us
  transfers between devices with their start and end apart: 14, of which 2 were waited for; matrix products, arithmetic and copies ran while one was open for 3% of the time, Pallas kernels for 32%

profile of v10, /device:TPU:1, one launch (start us, length us, event | category | flops | bytes accessed | tf_op | source)
XLA Modules:
  0.0 91.1 jit_solution(4770915562768915396)
XLA Ops:
  0.6 4.0 %shard_map.95 = (bf16[128,64,128]{2,1,0:T(8,128)(2,1)S(1)}, bf16[128,64,128]{2,1,0:T(8,128)(2,1)}, bf16[64,64,128]{2,1,0:T(8,128)(2,1)}, bf16[64,64,128]{2,1,0:T(8,128)(2,1)}, bf16[100,64,128]{2,1,0:T(8,128)(2,1)}) custom-call(bf16[64,128,128]{2,1,0:T(8,128)(2,1)} %bitcast.12), custom_call_target="tpu_custom_call" | custom-call | flops 1100000 | bytes 1024 | tf_op jit(solution)/shard_map/pallas_call | solution.py:34
  4.7 1.4 %copy-done = bf16[128,64,128]{2,1,0:T(8,128)(2,1)} copy-done((bf16[128,64,128]{2,1,0:T(8,128)(2,1)}, bf16[128,64,128]{2,1,0:T(8,128)(2,1)S(1)}, u32[]{:S(2)}) %copy-start) | copy-done | bytes 2097176
  6.1 4.6 %collective-permute-start.1 = (bf16[64,64,128]{2,1,0:T(8,128)(2,1)}, bf16[64,64,128]{2,1,0:T(8,128)(2,1)S(1)}, u32[]{:S(2)}, u32[]{:S(2)}) collective-permute-start(bf16[64,64,128]{2,1,0:T(8,128)(2,1)} %get-tuple-element.29), channel_id=1, source_target_pairs={{4,8},{8,4},{5,9},{9,5},{6,10},{10,6},{7,11},{11,7},{20,24},{24,20... | collective-permute-start | bytes 3145736 | tf_op jit(solution)/shard_map/ppermute | solution.py:381
  10.7 4.6 %all-to-all-start = ((bf16[100,64,128]{2,1,0:T(8,128)(2,1)}), bf16[100,64,128]{2,1,0:T(8,128)(2,1)S(1)}, u32[]{:S(2)}, u32[]{:S(2)}) async-start(bf16[100,64,128]{2,1,0:T(8,128)(2,1)} %get-tuple-element.37), calls=%async_computation | async-start | bytes 3276800 | tf_op jit(solution)/shard_map/all_to_all | solution.py:380
  16.0 1.6 %copy-done.1 = bf16[128,64,128]{2,1,0:T(8,128)(2,1)S(1)} copy-done((bf16[128,64,128]{2,1,0:T(8,128)(2,1)S(1)}, bf16[128,64,128]{2,1,0:T(8,128)(2,1)}, u32[]{:S(2)}) %copy-start.1) | copy-done | bytes 2097176
  17.6 9.0 %shard_map.96 = (f32[24,64,128]{2,1,0:T(8,128)S(1)}, bf16[64,64,128]{2,1,0:T(8,128)(2,1)}, bf16[16,64,128]{2,1,0:T(8,128)(2,1)}, bf16[16,64,128]{2,1,0:T(8,128)(2,1)S(1)}, bf16[8,64,128]{2,1,0:T(8,128)(2,1)}) custom-call(s32[384]{0:T(512)S(1)} %copy-done.6, s32[384]{0:T(512)S(1)} %copy-done.7, ...), custom_call_target="tpu_custom_call", output_to_operand_aliasing={{1}: (5, {})} | custom-call | flops 11000000512 | bytes 1024 | tf_op jit(solution)/shard_map/pallas_call | solution.py:34
  27.6 1.1 %collective-permute-start.3 = (bf16[16,64,128]{2,1,0:T(8,128)(2,1)}, bf16[16,64,128]{2,1,0:T(8,128)(2,1)S(1)}, u32[]{:S(2)}, u32[]{:S(2)}) collective-permute-start(bf16[16,64,128]{2,1,0:T(8,128)(2,1)} %get-tuple-element.33), channel_id=1, source_target_pairs={{0,4},{4,0},{8,12},{12,8},{1,5},{5,1},{9,13},{13,9},{2,6},{6,2},{1... | collective-permute-start | bytes 786440 | tf_op jit(solution)/shard_map/ppermute | solution.py:405
  28.7 2.6 %collective-permute-start.4 = (bf16[16,64,128]{2,1,0:T(8,128)(2,1)S(1)}, bf16[16,64,128]{2,1,0:T(8,128)(2,1)}, u32[]{:S(2)}, u32[]{:S(2)}) collective-permute-start(bf16[16,64,128]{2,1,0:T(8,128)(2,1)S(1)} %get-tuple-element.34), channel_id=1, source_target_pairs={{4,8},{8,4},{5,9},{9,5},{6,10},{10,6},{7,11},{11,7},{20,24},{24,20... | collective-permute-start | bytes 786440 | tf_op jit(solution)/shard_map/ppermute | solution.py:403
  32.1 1.0 %reshape.17.energy_ref = f32[32,128]{1,0:T(8,128)S(1)} reshape(f32[256,16]{1,0:T(8,128)} %copy.13) | data formatting | bytes 32768 | tf_op jit(solution)/shard_map/reshape | solution.py:358
  33.1 2.9 %collective-permute-start.2 = (bf16[64,64,128]{2,1,0:T(8,128)(2,1)}, bf16[64,64,128]{2,1,0:T(8,128)(2,1)}, u32[]{:S(2)}, u32[]{:S(2)}) collective-permute-start(bf16[64,64,128]{2,1,0:T(8,128)(2,1)} %get-tuple-element.31), channel_id=1, source_target_pairs={{4,8},{8,4},{5,9},{9,5},{6,10},{10,6},{7,11},{11,7},{20,24},{24,20... | collective-permute-start | bytes 3145736 | tf_op jit(solution)/shard_map/ppermute | solution.py:406
  36.8 1.6 %copy-done.2 = bf16[128,64,128]{2,1,0:T(8,128)(2,1)S(1)} copy-done((bf16[128,64,128]{2,1,0:T(8,128)(2,1)S(1)}, bf16[128,64,128]{2,1,0:T(8,128)(2,1)}, u32[]{:S(2)}) %copy-start.2) | copy-done | bytes 2097176
  38.3 1.1 %copy-done.9 = f32[24,64,128]{2,1,0:T(8,128)S(1)} copy-done((f32[24,64,128]{2,1,0:T(8,128)S(1)}, f32[24,64,128]{2,1,0:T(8,128)}, u32[]{:S(2)}) %copy-start.9) | copy-done | bytes 786456
  39.5 11.4 %shard_map.97 = (f32[128,64,128]{2,1,0:T(8,128)}, bf16[8,64,128]{2,1,0:T(8,128)(2,1)}, f32[8,128]{1,0:T(8,128)S(1)}, bf16[10,64,128]{2,1,0:T(8,128)(2,1)}, bf16[...) custom-call(s32[384]{0:T(512)S(1)} %copy-done.6, s32[384]{0:T(512)S(1)} %copy-done.7, s32[1]{0:T(128)S(6)} %copy.16.count_ref, ...), custom_call_target="tpu_custom_call" | custom-call | flops 32999999488 | bytes 1024 | tf_op jit(solution)/shard_map/pallas_call | solution.py:34
  50.9 1.8 %collective-permute-start.6 = (bf16[10,64,128]{2,1,0:T(8,128)(2,1)}, bf16[10,64,128]{2,1,0:T(8,128)(2,1)S(1)}, u32[]{:S(2)}, u32[]{:S(2)}) collective-permute-start(bf16[10,64,128]{2,1,0:T(8,128)(2,1)} %get-tuple-element.44), channel_id=1, source_target_pairs={{0,1},{1,0},{2,3},{3,2},{4,5},{5,4},{6,7},{7,6},{8,9},{9,8},{10,11... | collective-permute-start | bytes 491528 | tf_op jit(solution)/shard_map/ppermute | solution.py:353
  52.7 2.1 %collective-permute-start.7 = (bf16[10,64,128]{2,1,0:T(8,128)(2,1)S(1)}, bf16[10,64,128]{2,1,0:T(8,128)(2,1)}, u32[]{:S(2)}, u32[]{:S(2)}) collective-permute-start(bf16[10,64,128]{2,1,0:T(8,128)(2,1)S(1)} %get-tuple-element.45), channel_id=1, source_target_pairs={{0,2},{1,3},{2,0},{3,1},{4,6},{5,7},{6,4},{7,5},{8,10},{9,11},{10,... | collective-permute-start | bytes 491528 | tf_op jit(solution)/shard_map/ppermute | solution.py:353
  55.1 3.0 %collective-permute-start.12 = (bf16[12,256,128]{2,1,0:T(8,128)(2,1)S(1)}, bf16[12,256,128]{2,1,0:T(8,128)(2,1)S(1)}, u32[]{:S(2)}, u32[]{:S(2)}) collective-permute-start(bf16[12,256,128]{2,1,0:T(8,128)(2,1)S(1)} %get-tuple-element.49), channel_id=1, source_target_pairs={{4,8},{8,4},{5,9},{9,5},{6,10},{10,6},{7,11},{11,7},{20,24},{24,20... | collective-permute-start | bytes 2359304 | tf_op jit(solution)/shard_map/ppermute | solution.py:441
  58.3 1.6 %copy-done.3 = bf16[128,64,128]{2,1,0:T(8,128)(2,1)S(1)} copy-done((bf16[128,64,128]{2,1,0:T(8,128)(2,1)S(1)}, bf16[128,64,128]{2,1,0:T(8,128)(2,1)}, u32[]{:S(2)}) %copy-start.3) | copy-done | bytes 2097176
  59.9 6.4 %shard_map.99 = (bf16[64,128,128]{2,1,0:T(8,128)(2,1)}, f32[8,128]{1,0:T(8,128)S(1)}) custom-call(bf16[128,64,128]{2,1,0:T(8,128)(2,1)S(1)} %copy-done.3, bf16[128,64,128]{2,1,0:T(8,128)(2,1)} %collective-permute-done.core_ref, bf16[64,64,128]{2,1,0:T(8,128)(2,1)S(1)} %collective-permute-done.1.early_ref, ...), custom_call_target="tpu_custom_call" | custom-call | flops 1100000 | bytes 1024 | tf_op jit(solution)/shard_map/pallas_call | solution.py:34
  66.3 1.2 %shard_map.100 = (bf16[9,256,128]{2,1,0:T(8,128)(2,1)S(1)}, bf16[4,256,128]{2,1,0:T(8,128)(2,1)S(1)}, bf16[2,256,128]{2,1,0:T(8,128)(2,1)S(1)}, f32[8,128]{1,0:T(8,128)S(1)}) custom-call(bf16[128,64,128]{2,1,0:T(8,128)(2,1)S(1)} %copy-done.3, bf16[8,64,128]{2,1,0:T(8,128)(2,1)} %get-tuple-element.41.whole_ref, ...), custom_call_target="tpu_custom_call" | custom-call | flops 32999999488 | bytes 1024 | tf_op jit(solution)/shard_map/pallas_call | solution.py:34
  67.5 2.5 %collective-permute-start.10 = (bf16[4,256,128]{2,1,0:T(8,128)(2,1)S(1)}, bf16[4,256,128]{2,1,0:T(8,128)(2,1)S(1)}, u32[]{:S(2)}, u32[]{:S(2)}) collective-permute-start(bf16[4,256,128]{2,1,0:T(8,128)(2,1)S(1)} %get-tuple-element.48), channel_id=1, source_target_pairs={{4,8},{8,4},{5,9},{9,5},{6,10},{10,6},{7,11},{11,7},{20,24},{24,20... | collective-permute-start | bytes 786440 | tf_op jit(solution)/shard_map/ppermute | solution.py:486
  70.1 1.2 %shard_map.101.begun_ref = f32[2,256,256]{2,1,0:T(8,128)S(1)} custom-call(bf16[25,256,128]{2,1,0:T(8,128)(2,1)S(1)} %get-tuple-element.42.after_ref.all_ref, bf16[12,256,128]{2,1,0:T(8,128)(2,1)S(1)} %collective-permute-done.11.core_ref, bf16[12,256,128]{2,1,0:T(8,128)(2,1)S(1)} %collective-permute-done.12.link_ref, f32[128,128]{1,0:T(8,128)S(1)} %bitcast.10, ...), custom_call_target="tpu_custom_call" | custom-call | flops 1100000 | bytes 1024 | tf_op jit(solution)/shard_map/pallas_call | solution.py:34
  71.3 4.0 %collective-permute-done.10.link_ref = bf16[4,256,128]{2,1,0:T(8,128)(2,1)S(1)} collective-permute-done((bf16[4,256,128]{2,1,0:T(8,128)(2,1)S(1)}, bf16[4,256,128]{2,1,0:T(8,128)(2,1)S(1)}, u32[]{:S(2)}, u32[]{:S(2)}) %collective-permute-start.10) | collective-permute-done | bytes 262176 | tf_op jit(solution)/shard_map/ppermute | solution.py:486
  75.2 0.9 shard_map.102
  76.1 14.3 %all_to_all.10.parts_ref = bf16[16,64,128]{2,1,0:T(8,128)(2,1)S(1)} all-to-all(bf16[16,64,128]{2,1,0:T(8,128)(2,1)S(1)} %shard_map.102), channel_id=1, replica_groups=mesh['groups'=2,'domain'=4,'band'=4] {'domain','band'}, dimensions={0} | all-to-all | bytes 524288 | tf_op jit(solution)/shard_map/all_to_all | solution.py:509
  (40 shorter events, 3.8 us)
Async XLA Ops:
  4.7 1.4 %copy-start = (bf16[128,64,128]{2,1,0:T(8,128)(2,1)}, bf16[128,64,128]{2,1,0:T(8,128)(2,1)S(1)}, u32[]{:S(2)}) copy-start(bf16[128,64,128]{2,1,0:T(8,128)(2,1)S(1)} %get-tuple-element.27.xt_ref) | copy-start | bytes 6291460
  6.1 9.9 %copy-start.6 = (s32[384]{0:T(512)S(1)}, s32[384]{0:T(512)}, u32[]{:S(2)}) copy-start(s32[384]{0:T(512)} %atom_ref.3) | copy-start | bytes 4612
  6.1 9.9 %copy-start.7 = (s32[384]{0:T(512)S(1)}, s32[384]{0:T(512)}, u32[]{:S(2)}) copy-start(s32[384]{0:T(512)} %line_ref.3) | copy-start | bytes 4612
  6.1 30.0 %collective-permute-start = (bf16[128,64,128]{2,1,0:T(8,128)(2,1)}, bf16[128,64,128]{2,1,0:T(8,128)(2,1)}, u32[]{:S(2)}, u32[]{:S(2)}) collective-permute-start(bf16[128,64,128]{2,1,0:T(8,128)(2,1)} %get-tuple-element.28), channel_id=1, source_target_pairs={{0,4},{4,0},{8,12},{12,8},{1,5},{5,1},{9,13},{13,9},{2,6},{6,2},{1... | collective-permute-start | bytes 6291464 | tf_op jit(solution)/shard_map/ppermute | solution.py:382
  6.1 27.0 %collective-permute-start.1 = (bf16[64,64,128]{2,1,0:T(8,128)(2,1)}, bf16[64,64,128]{2,1,0:T(8,128)(2,1)S(1)}, u32[]{:S(2)}, u32[]{:S(2)}) collective-permute-start(bf16[64,64,128]{2,1,0:T(8,128)(2,1)} %get-tuple-element.29), channel_id=1, source_target_pairs={{4,8},{8,4},{5,9},{9,5},{6,10},{10,6},{7,11},{11,7},{20,24},{24,20... | collective-permute-start | bytes 3145736 | tf_op jit(solution)/shard_map/ppermute | solution.py:381
  10.7 44.1 %all-to-all-start = ((bf16[100,64,128]{2,1,0:T(8,128)(2,1)}), bf16[100,64,128]{2,1,0:T(8,128)(2,1)S(1)}, u32[]{:S(2)}, u32[]{:S(2)}) async-start(bf16[100,64,128]{2,1,0:T(8,128)(2,1)} %get-tuple-element.37), calls=%async_computation | async-start | bytes 3276800 | tf_op jit(solution)/shard_map/all_to_all | solution.py:380
  16.0 1.6 %copy-start.1 = (bf16[128,64,128]{2,1,0:T(8,128)(2,1)S(1)}, bf16[128,64,128]{2,1,0:T(8,128)(2,1)}, u32[]{:S(2)}) copy-start(bf16[128,64,128]{2,1,0:T(8,128)(2,1)} %copy-done) | copy-start | bytes 6291460
  17.6 13.7 %copy-start.10 = (f32[256,16]{0,1:T(8,128)S(1)}, f32[256,16]{0,1:T(8,128)}, u32[]{:S(2)}) copy-start(f32[256,16]{0,1:T(8,128)} %param.14) | copy-start | bytes 49156
  27.5 9.2 %collective-permute-start.5 = (bf16[8,64,128]{2,1,0:T(8,128)(2,1)}, bf16[8,64,128]{2,1,0:T(8,128)(2,1)S(1)}, u32[]{:S(2)}, u32[]{:S(2)}) collective-permute-start(bf16[8,64,128]{2,1,0:T(8,128)(2,1)} %get-tuple-element.35), channel_id=1, source_target_pairs={{0,8},{4,12},{8,0},{12,4},{1,9},{5,13},{9,1},{13,5},{2,10},{6,14},... | collective-permute-start | bytes 393224 | tf_op jit(solution)/shard_map/ppermute | solution.py:404
  27.6 9.2 %collective-permute-start.3 = (bf16[16,64,128]{2,1,0:T(8,128)(2,1)}, bf16[16,64,128]{2,1,0:T(8,128)(2,1)S(1)}, u32[]{:S(2)}, u32[]{:S(2)}) collective-permute-start(bf16[16,64,128]{2,1,0:T(8,128)(2,1)} %get-tuple-element.33), channel_id=1, source_target_pairs={{0,4},{4,0},{8,12},{12,8},{1,5},{5,1},{9,13},{13,9},{2,6},{6,2},{1... | collective-permute-start | bytes 786440 | tf_op jit(solution)/shard_map/ppermute | solution.py:405
  28.7 8.1 %collective-permute-start.4 = (bf16[16,64,128]{2,1,0:T(8,128)(2,1)S(1)}, bf16[16,64,128]{2,1,0:T(8,128)(2,1)}, u32[]{:S(2)}, u32[]{:S(2)}) collective-permute-start(bf16[16,64,128]{2,1,0:T(8,128)(2,1)S(1)} %get-tuple-element.34), channel_id=1, source_target_pairs={{4,8},{8,4},{5,9},{9,5},{6,10},{10,6},{7,11},{11,7},{20,24},{24,20... | collective-permute-start | bytes 786440 | tf_op jit(solution)/shard_map/ppermute | solution.py:403
  33.1 25.1 %collective-permute-start.2 = (bf16[64,64,128]{2,1,0:T(8,128)(2,1)}, bf16[64,64,128]{2,1,0:T(8,128)(2,1)}, u32[]{:S(2)}, u32[]{:S(2)}) collective-permute-start(bf16[64,64,128]{2,1,0:T(8,128)(2,1)} %get-tuple-element.31), channel_id=1, source_target_pairs={{4,8},{8,4},{5,9},{9,5},{6,10},{10,6},{7,11},{11,7},{20,24},{24,20... | collective-permute-start | bytes 3145736 | tf_op jit(solution)/shard_map/ppermute | solution.py:406
  36.8 1.6 %copy-start.2 = (bf16[128,64,128]{2,1,0:T(8,128)(2,1)S(1)}, bf16[128,64,128]{2,1,0:T(8,128)(2,1)}, u32[]{:S(2)}) copy-start(bf16[128,64,128]{2,1,0:T(8,128)(2,1)} %copy-done) | copy-start | bytes 6291460
  38.3 1.1 %copy-start.9 = (f32[24,64,128]{2,1,0:T(8,128)S(1)}, f32[24,64,128]{2,1,0:T(8,128)}, u32[]{:S(2)}) copy-start(f32[24,64,128]{2,1,0:T(8,128)} %copy-done.8) | copy-start | bytes 2359300
  39.5 18.8 %copy-start.4 = (f32[1,128,128]{2,1,0:T(8,128)S(1)}, f32[1,128,128]{2,1,0:T(8,128)}, u32[]{:S(2)}) copy-start(f32[1,128,128]{2,1,0:T(8,128)} %param.9) | copy-start | bytes 196612
  39.5 18.8 %copy-start.5 = (bf16[128,128]{1,0:T(8,128)(2,1)S(1)}, bf16[128,128]{1,0:T(8,128)(2,1)}, u32[]{:S(2)}) copy-start(bf16[128,128]{1,0:T(8,128)(2,1)} %constant.2.clone.ring_ref) | copy-start | bytes 98308
  50.9 15.4 %collective-permute-start.6 = (bf16[10,64,128]{2,1,0:T(8,128)(2,1)}, bf16[10,64,128]{2,1,0:T(8,128)(2,1)S(1)}, u32[]{:S(2)}, u32[]{:S(2)}) collective-permute-start(bf16[10,64,128]{2,1,0:T(8,128)(2,1)} %get-tuple-element.44), channel_id=1, source_target_pairs={{0,1},{1,0},{2,3},{3,2},{4,5},{5,4},{6,7},{7,6},{8,9},{9,8},{10,11... | collective-permute-start | bytes 491528 | tf_op jit(solution)/shard_map/ppermute | solution.py:353
  52.7 13.7 %collective-permute-start.7 = (bf16[10,64,128]{2,1,0:T(8,128)(2,1)S(1)}, bf16[10,64,128]{2,1,0:T(8,128)(2,1)}, u32[]{:S(2)}, u32[]{:S(2)}) collective-permute-start(bf16[10,64,128]{2,1,0:T(8,128)(2,1)S(1)} %get-tuple-element.45), channel_id=1, source_target_pairs={{0,2},{1,3},{2,0},{3,1},{4,6},{5,7},{6,4},{7,5},{8,10},{9,11},{10,... | collective-permute-start | bytes 491528 | tf_op jit(solution)/shard_map/ppermute | solution.py:353
  54.8 11.6 %collective-permute-start.8 = (bf16[10,64,128]{2,1,0:T(8,128)(2,1)S(1)}, bf16[10,64,128]{2,1,0:T(8,128)(2,1)}, u32[]{:S(2)}, u32[]{:S(2)}) collective-permute-start(bf16[10,64,128]{2,1,0:T(8,128)(2,1)S(1)} %get-tuple-element.46), channel_id=1, source_target_pairs={{0,3},{1,2},{2,1},{3,0},{4,7},{5,6},{6,5},{7,4},{8,11},{9,10},{10,... | collective-permute-start | bytes 491528 | tf_op jit(solution)/shard_map/ppermute | solution.py:353
  55.1 15.0 %collective-permute-start.12 = (bf16[12,256,128]{2,1,0:T(8,128)(2,1)S(1)}, bf16[12,256,128]{2,1,0:T(8,128)(2,1)S(1)}, u32[]{:S(2)}, u32[]{:S(2)}) collective-permute-start(bf16[12,256,128]{2,1,0:T(8,128)(2,1)S(1)} %get-tuple-element.49), channel_id=1, source_target_pairs={{4,8},{8,4},{5,9},{9,5},{6,10},{10,6},{7,11},{11,7},{20,24},{24,20... | collective-permute-start | bytes 2359304 | tf_op jit(solution)/shard_map/ppermute | solution.py:441
  58.2 11.9 %collective-permute-start.11 = (bf16[12,256,128]{2,1,0:T(8,128)(2,1)S(1)}, bf16[12,256,128]{2,1,0:T(8,128)(2,1)S(1)}, u32[]{:S(2)}, u32[]{:S(2)}) collective-permute-start(bf16[12,256,128]{2,1,0:T(8,128)(2,1)S(1)} %get-tuple-element.49), channel_id=1, source_target_pairs={{0,4},{4,0},{8,12},{12,8},{1,5},{5,1},{9,13},{13,9},{2,6},{6,2},{1... | collective-permute-start | bytes 2359304 | tf_op jit(solution)/shard_map/ppermute | solution.py:442
  58.3 1.6 %copy-start.3 = (bf16[128,64,128]{2,1,0:T(8,128)(2,1)S(1)}, bf16[128,64,128]{2,1,0:T(8,128)(2,1)}, u32[]{:S(2)}) copy-start(bf16[128,64,128]{2,1,0:T(8,128)(2,1)} %copy-done) | copy-start | bytes 6291460
  67.5 7.7 %collective-permute-start.10 = (bf16[4,256,128]{2,1,0:T(8,128)(2,1)S(1)}, bf16[4,256,128]{2,1,0:T(8,128)(2,1)S(1)}, u32[]{:S(2)}, u32[]{:S(2)}) collective-permute-start(bf16[4,256,128]{2,1,0:T(8,128)(2,1)S(1)} %get-tuple-element.48), channel_id=1, source_target_pairs={{4,8},{8,4},{5,9},{9,5},{6,10},{10,6},{7,11},{11,7},{20,24},{24,20... | collective-permute-start | bytes 786440 | tf_op jit(solution)/shard_map/ppermute | solution.py:486
  70.0 5.2 %collective-permute-start.9 = (bf16[4,256,128]{2,1,0:T(8,128)(2,1)S(1)}, bf16[4,256,128]{2,1,0:T(8,128)(2,1)S(1)}, u32[]{:S(2)}, u32[]{:S(2)}) collective-permute-start(bf16[4,256,128]{2,1,0:T(8,128)(2,1)S(1)} %get-tuple-element.48), channel_id=1, source_target_pairs={{0,4},{4,0},{8,12},{12,8},{1,5},{5,1},{9,13},{13,9},{2,6},{6,2},{1... | collective-permute-start | bytes 786440 | tf_op jit(solution)/shard_map/ppermute | solution.py:487
  (1 other events, 0.9 us)

commit v11 on v10

--- a/solution.py
+++ b/solution.py
@@ -49,7 +49,20 @@
     return copy
 
 
-def pack_kernel(first, x_hbm, xt, xt_hbm, early, late, message, x, in_sems, out_sems):
+def start_all(pairs, sems):
+    return [start(pltpu.make_async_copy(source, target, sems.at[i])) for i, (source, target) in enumerate(pairs)]
+
+
+def wait_all(started):
+    for copy in started:
+        copy.wait()
+
+
+def hand_on(*refs):
+    pass
+
+
+def pack_kernel(first, x_hbm, xt_hbm, early, late, message, x, xt, in_sems, out_sems):
     states, lines, _ = x.shape
     bands = in_sems.shape[0]
     share = lines // bands
@@ -88,24 +101,26 @@
     return [2 * groups * side for side in (1 - odd, odd, 1 - upper, upper)]
 
 
-def slot_at(t, atom_ref, line_ref, count_ref, atoms_here):
+def slot_reader(atom_ref, line_ref, count_ref, atoms_here):
     first = (lax.axis_index("domain") - 1) * atoms_here
-    atom = jnp.clip(atom_ref[t] - first, 0, 3 * atoms_here - 1)
-    return line_ref[t], atom, t < count_ref[0]
-
-
-def project_kernel(atom_ref, line_ref, count_ref, xt_ref, p_hbm, handed, mine_ref, same, core_ref, link_ref, *refs):
-    far_refs, (total, p_ref, sems) = refs[:-3], refs[-3:]
+    live = count_ref[0]
+
+    def slot_at(t):
+        return line_ref[t], jnp.clip(atom_ref[t] - first, 0, 3 * atoms_here - 1), t < live
+
+    return slot_at
+
+
+def project_kernel(atom_ref, line_ref, count_ref, xt_hbm, p_hbm, handed, mine_hbm, same, core_ref, link_ref, *refs):
+    far_refs, (total, mine_ref, xt_ref, p_ref, sems, mine_sem) = refs[:-6], refs[-6:]
     slots, proj_count, _ = p_ref.shape
     groups, states = mine_ref.shape[0] // 3, mine_ref.shape[1]
     per_group = LANES // proj_count
-    chunks = sems.shape[0]
+    chunks = sems.shape[0] - 1
     size = slots // chunks
     unroll = 16
-    loads = []
-    for c in range(chunks):
-        where = pl.ds(c * size, size)
-        loads.append(start(pltpu.make_async_copy(p_hbm.at[where], p_ref.at[where], sems.at[c])))
+    pairs = [(p_hbm.at[pl.ds(c * size, size)], p_ref.at[pl.ds(c * size, size)]) for c in range(chunks)]
+    xt_load, *loads = start_all([(xt_hbm, xt_ref), *pairs], sems)
 
     def clear(i, carry):
         for u in range(per_group):
@@ -114,14 +129,17 @@
 
     lax.fori_loop(0, 3 * groups, clear, 0)
 
+    slot_at = slot_reader(atom_ref, line_ref, count_ref, groups * per_group)
+
     def body(i, carry):
         for u in range(unroll):
             t = i * unroll + u
-            line, atom, live = slot_at(t, atom_ref, line_ref, count_ref, groups * per_group)
+            line, atom, live = slot_at(t)
             part = lax.dot_general(p_ref[t], xt_ref[line], NT, preferred_element_type=F32)
             total[jnp.where(live, atom, 3 * groups * per_group)] += part
         return carry
 
+    xt_load.wait()
     for c in range(chunks):
         loads[c].wait()
         lax.fori_loop(c * size // unroll, (c + 1) * size // unroll, body, 0)
@@ -129,6 +147,7 @@
     for g in range(3 * groups):
         tiles = [total[g * per_group + u] for u in range(per_group)]
         mine_ref[g] = jnp.concatenate(tiles, axis=0).T
+    send = start(pltpu.make_async_copy(mine_ref, mine_hbm, mine_sem))
     sides = bases(groups)
     for g in range(groups):
         own = mine_ref[groups + g].astype(BF16)
@@ -137,21 +156,22 @@
             ref[groups + g] = own
         for side, ref in zip(sides[2:], far_refs):
             ref[g] = mine_ref[side + g].astype(BF16)
+    send.wait()
 
 
 def nonlocal_kernel(
-    first, fars, atom_ref, line_ref, count_ref, xt_ref, p_hbm, energy_ref, mine_ref, core_ref, link_ref, *refs
+    first, fars, atom_ref, line_ref, count_ref, xt_hbm, p_hbm, energy_ref, mine_hbm, core_ref, link_ref, *refs
 ):
-    far_refs, (_, _, out_hbm, whole_hbm, done_ref, *messages, lines_sum, whole_ref, total, atoms, p_ref, sems) = (
+    far_refs, (_, _, out_hbm, whole_hbm, done_ref, *messages, lines_sum, whole_ref, total, atoms, xt_ref, p_ref, sems) = (
         refs[:fars],
         refs[fars:],
     )
     slots, proj_count, _ = p_ref.shape
-    groups, states = mine_ref.shape[0] // 3, mine_ref.shape[1]
+    groups, states = total.shape[0] // 3, total.shape[1]
     per_group = LANES // proj_count
     lines = xt_ref.shape[0]
     unroll = 16
-    load = start(pltpu.make_async_copy(p_hbm, p_ref, sems.at[0]))
+    mine_load, *loads = start_all([(mine_hbm, total), (xt_hbm, xt_ref), (p_hbm, p_ref)], sems)
     done_ref[...] = jnp.zeros_like(done_ref)
 
     def clear(i, carry):
@@ -159,7 +179,7 @@
         return carry
 
     lax.fori_loop(0, lines + 1, clear, 0)
-    total[...] = mine_ref[...]
+    mine_load.wait()
     sides = bases(groups)
     for g in range(groups):
         total[groups + g] += core_ref[g].astype(F32) + link_ref[g].astype(F32)
@@ -175,7 +195,8 @@
             atoms[g * per_group + u] = tile[:, u * proj_count : (u + 1) * proj_count]
     for g in range(groups):
         whole_ref[g] = total[groups + g].astype(BF16)
-    send_whole = start(pltpu.make_async_copy(whole_ref, whole_hbm, sems.at[1]))
+    send_whole = start(pltpu.make_async_copy(whole_ref, whole_hbm, sems.at[3]))
+    wait_all(loads)
     share = xt_ref.shape[0] // (len(messages) + 1)
     held = groups // (len(messages) + 1)
     for k, message in enumerate(messages, 1):
@@ -184,46 +205,52 @@
             message[i] = xt_ref[to * share + i]
         for i in range(held):
             message[first + i] = whole_ref[to * held + i]
-    load.wait()
+
+    slot_at = slot_reader(atom_ref, line_ref, count_ref, groups * per_group)
 
     def body(i, carry):
         for u in range(unroll):
             t = i * unroll + u
-            line, atom, live = slot_at(t, atom_ref, line_ref, count_ref, groups * per_group)
+            line, atom, live = slot_at(t)
             part = jnp.dot(atoms[atom], p_ref[t], preferred_element_type=F32)
             lines_sum[jnp.where(live, line, lines)] += part
         return carry
 
     lax.fori_loop(0, slots // unroll, body, 0)
-    send = start(pltpu.make_async_copy(lines_sum.at[pl.ds(0, lines)], out_hbm, sems.at[2]))
+    send = start(pltpu.make_async_copy(lines_sum.at[pl.ds(0, lines)], out_hbm, sems.at[4]))
     send_whole.wait()
     send.wait()
 
 
-def stencil_kernel(early_steps, xt_ref, core_ref, early_ref, late_ref, added_ref, pot_ref, ring_ref, unread, out_ref, done_ref):
+def stencil_kernel(
+    early_steps, xt_ref, last_ref, next_ref, core_ref, early_link, late_link, added_ref, pot_ref, ring_ref,
+    unread, out_ref, done_ref,
+):
     states, here, _ = out_ref.shape
-    lines = xt_ref.shape[0]
     done_ref[...] = jnp.zeros_like(done_ref)
-    step = pl.program_id(0)
-    early = step < early_steps
-    for part in range(0, here, ROWS):
-        y0 = step * here + part
+    early = pl.program_id(0) < early_steps
+
+    def line(i, rows):
+        ref, at = (last_ref, 0) if i < 0 else (next_ref, 0) if i == here else (xt_ref, i)
+        return ref[at, rows, :]
+
+    for y0 in range(0, here, ROWS):
         for s0 in range(0, states, ROWS):
             rows = slice(s0, s0 + ROWS)
             results = []
-            cells = jnp.concatenate([xt_ref[y0 + i, rows, :] for i in range(ROWS)], axis=0)
+            cells = jnp.concatenate([line(y0 + i, rows) for i in range(ROWS)], axis=0)
             along = jnp.dot(cells, ring_ref[...], preferred_element_type=F32)
-            before = xt_ref[lax.rem(y0 + lines - 1, lines), rows, :].astype(F32)
-            x = xt_ref[y0, rows, :].astype(F32)
+            before, x = line(y0 - 1, rows).astype(F32), line(y0, rows).astype(F32)
             for i in range(ROWS):
-                after = xt_ref[lax.rem(y0 + i + 1, lines), rows, :].astype(F32)
-                link = jnp.where(early, early_ref[part + i, rows, :], late_ref[part + i, rows, :]).astype(F32)
-                beside = (before + after) + (core_ref[part + i, rows, :].astype(F32) + link)
-                value = along[i * ROWS : (i + 1) * ROWS] + pot_ref[part + i : part + i + 1, :] * x
-                results.append(value + added_ref[part + i, rows, :] - 0.5 * beside)
+                y = y0 + i
+                after = line(y + 1, rows).astype(F32)
+                core = core_ref[y, rows, :].astype(F32)
+                link = jnp.where(early, early_link[y, rows, :], late_link[y, rows, :]).astype(F32)
+                value = along[i * ROWS : (i + 1) * ROWS] + pot_ref[y : y + 1, :] * x + added_ref[y, rows, :]
+                results.append(value - 0.5 * ((before + after) + (core + link)))
                 before, x = x, after
             turned = jnp.swapaxes(jnp.stack(results, axis=0), 0, 1).astype(BF16)
-            out_ref[rows, part : part + ROWS, :] = turned
+            out_ref[rows, y0 : y0 + ROWS, :] = turned
 
 
 def pass_half(all_ref, pass_hbm, sem):
@@ -248,10 +275,10 @@
     pass_half(all_ref, pass_hbm, pass_sem)
 
 
-def early_kernel(bands, share, xt_ref, whole_ref, after_ref, unread, *refs):
+def early_kernel(bands, share, xt_hbm, whole_ref, after_ref, unread, *refs):
     pieces, (all_ref, pass_hbm, projs_ref, done_ref, sems, pass_sem) = refs[: bands - 1], refs[bands - 1 :]
     done_ref[...] = jnp.zeros_like(done_ref)
-    states = xt_ref.shape[1]
+    states = xt_hbm.shape[1]
     band = lax.axis_index("band")
     count, held = all_ref.shape[0] - 1, projs_ref.shape[0]
     loads = []
@@ -262,7 +289,7 @@
     for k in range(bands):
         at = pl.ds(pl.multiple_of((band ^ k) * states, states), states)
         if k == 0:
-            load(xt_ref.at[pl.ds(band * share, count)], all_ref.at[pl.ds(0, count), at, :])
+            load(xt_hbm.at[pl.ds(band * share, count)], all_ref.at[pl.ds(0, count), at, :])
             load(whole_ref.at[pl.ds(band * held, held)], projs_ref.at[:, at, :])
         else:
             load(pieces[k - 1].at[pl.ds(0, count)], all_ref.at[pl.ds(0, count), at, :])
@@ -361,40 +388,58 @@
 
     late_lines = lines // 2
     line_shape, late_shape = (lines, states, cols_z), (late_lines, states, cols_z)
-    xt, xt_far, early_part, late_part, message = call(
-        58,
+    xt, early_part, late_part, message = call(
+        63,
         functools.partial(pack_kernel, first),
         (),
         [FAR],
-        [NEAR, FAR, FAR, FAR, FAR],
+        [FAR] * 4,
         [
-            (line_shape, BF16),
             (line_shape, BF16),
             ((lines - late_lines, states, cols_z), BF16),
             (late_shape, BF16),
             ((bands * (rest + 1), states, cols_z), BF16),
         ],
-        [pltpu.VMEM((states, lines, cols_z), BF16), copies((bands,)), copies((2 * bands + 3,))],
+        [
+            pltpu.VMEM((states, lines, cols_z), BF16),
+            pltpu.VMEM(line_shape, BF16),
+            copies((bands,)),
+            copies((2 * bands + 3,)),
+        ],
         (field,),
     )
     landed = lax.all_to_all(message, "band", split_axis=0, concat_axis=0, tiled=True)
+    xt, early_part = call(
+        63,
+        hand_on,
+        (),
+        [UNREAD] * 2,
+        [UNREAD] * 2,
+        [(line_shape, BF16), (early_part.shape, BF16)],
+        [],
+        (xt, early_part),
+        aliases={0: 0, 1: 1},
+    )
     link_early = lax.ppermute(early_part, "domain", link_pairs)
-    core_field = lax.ppermute(xt_far, "domain", core_pairs)
+    core_field = lax.ppermute(xt, "domain", core_pairs)
 
     group_shape = (groups, states, LANES)
     mine, late_part, to_core, to_link, *to_far = call(
-        50,
+        63,
         project_kernel,
         (),
-        [SCALARS] * 3 + [NEAR, PINNED, UNREAD],
-        [NEAR, UNREAD] + [WHOLE] * (2 + len(far_pairs)),
+        [SCALARS] * 3 + [FAR, PINNED, UNREAD],
+        [PINNED, UNREAD] + [WHOLE] * (2 + len(far_pairs)),
         [((3 * groups, states, LANES), F32), (late_shape, BF16)]
         + [((2 * groups, states, LANES), BF16)] * 2
         + [(group_shape, BF16)] * len(far_pairs),
         [
             pltpu.VMEM((3 * atoms_here + 1, proj_count, states), F32),
+            pltpu.VMEM((3 * groups, states, LANES), F32),
+            pltpu.VMEM(line_shape, BF16),
             pltpu.VMEM(projectors.shape, BF16),
-            copies((4,)),
+            copies((5,)),
+            copies,
         ],
         (tile_atom, tile_line, tile_count, xt, projectors, late_part),
         aliases={5: 1},
@@ -405,10 +450,10 @@
     from_core = lax.ppermute(to_core, "domain", core_pairs)
     link_late = lax.ppermute(late_part, "domain", link_pairs)
     added, whole, summed_up, *messages = call(
-        32,
+        62,
         functools.partial(nonlocal_kernel, first, len(far_pairs)),
         (),
-        [SCALARS] * 3 + [NEAR, PINNED, WHOLE, NEAR, WHOLE, WHOLE] + [WHOLE] * len(far_pairs) + [UNREAD] * 2,
+        [SCALARS] * 3 + [FAR, PINNED, WHOLE, PINNED, WHOLE, WHOLE] + [WHOLE] * len(far_pairs) + [UNREAD] * 2,
         [PINNED, PINNED, WHOLE] + [WHOLE] * (bands - 1),
         [(line_shape, F32), (group_shape, BF16), ((8, LANES), F32)]
         + [((first + group_share, states, cols_z), BF16)] * (bands - 1),
@@ -417,8 +462,9 @@
             pltpu.VMEM(group_shape, BF16),
             pltpu.VMEM((3 * groups, states, LANES), F32),
             pltpu.VMEM((3 * atoms_here, states, proj_count), BF16),
+            pltpu.VMEM(line_shape, BF16),
             pltpu.VMEM(projectors.shape, BF16),
-            copies((3,)),
+            copies((5,)),
         ],
         (
             tile_atom, tile_line, tile_count, xt, projectors, energy, mine, from_core, from_link, *from_far,
@@ -444,15 +490,20 @@
     span = 2 * ROWS
     steps, early_steps = lines // span, (lines - late_lines) // span
     block = pl.BlockSpec((span, states, cols_z), lambda i: (i, 0, 0))
+    early_block = pl.BlockSpec((span, states, cols_z), lambda i: (jnp.minimum(i, early_steps - 1), 0, 0))
+    late_block = pl.BlockSpec((span, states, cols_z), lambda i: (jnp.maximum(i - early_steps, 0), 0, 0))
+    added_far = pltpu.with_memory_space_constraint(added, pltpu.HBM)
     applied, done = call(
-        32,
+        61,
         functools.partial(stencil_kernel, early_steps),
         (steps,),
         [
-            NEAR,
             block,
-            pl.BlockSpec((span, states, cols_z), lambda i: (jnp.minimum(i, early_steps - 1), 0, 0)),
-            pl.BlockSpec((span, states, cols_z), lambda i: (jnp.maximum(i - early_steps, 0), 0, 0)),
+            pl.BlockSpec((1, states, cols_z), lambda i: (lax.rem(i * span + lines - 1, lines), 0, 0)),
+            pl.BlockSpec((1, states, cols_z), lambda i: (lax.rem(i * span + span, lines), 0, 0)),
+            block,
+            early_block,
+            late_block,
             block,
             pl.BlockSpec((span, cols_z), lambda i: (i, 0)),
             WHOLE,
@@ -462,16 +513,15 @@
         [((states, lines, cols_z), BF16), ((8, LANES), F32)],
         [],
         (
-            xt, core_field, link_early, link_late, pltpu.with_memory_space_constraint(added, pltpu.HBM), pot, ring,
-            later_token,
+            xt, xt, xt, core_field, link_early, link_late, added_far, pot, ring, later_token,
         ),
     )
 
     early_all, early_pass, projs, early_token = call(
-        32,
+        60,
         functools.partial(early_kernel, bands, share),
         (),
-        [NEAR, PINNED, NEAR, WHOLE] + [FAR] * (bands - 1),
+        [FAR, PINNED, NEAR, WHOLE] + [FAR] * (bands - 1),
         [NEAR, FAR, NEAR, WHOLE],
         [
             ((first + 1, total_states, cols_z), BF16),

time: 92.7 us -> 95.7 us (1.032)
  Pallas kernels: 35.1 us -> 43.3 us
  local copies, waits for them, and re-layouts: 10.6 us -> 6.86 us
  blocking collectives: 14.3 us -> 10.9 us
  starting transfers between devices: 25.6 us -> 28.8 us
  waiting for transfers between devices: 4.09 us -> 2.71 us
    pallas_call x9 -> x10, Pallas kernels: 35.1 us -> 43.3 us  [call(): pl.pallas_call(kernel, grid=grid, out_shape=shapes, in_specs=in_specs, ou...]
    unnamed x23 -> x25, local copies, waits for them, and re-layouts: 8.9 us -> 3.62 us
    ppermute x1, starting transfers between devices: 3.05 us -> 6.77 us  [local(): later_link = lax.ppermute(later_pass, 'domain', link_pairs)]
    all_to_all x1, blocking collectives: 14.3 us -> 10.9 us  [local(): lax.all_to_all(blocks, ('domain', 'band'), split_axis=0, concat_axis=0, t...]
    ppermute x1, waiting for transfers between devices: 3.95 us -> 2.68 us  [local(): early_link = lax.ppermute(early_pass, 'domain', link_pairs)]
    squeeze x1, local copies, waits for them, and re-layouts: 0.01 us -> 1.27 us  [local(): link_early[0, :ROWS]]
  transfers between devices with their start and end apart: 14 -> 14, of which waited for: 2 -> 1; matrix products, arithmetic and copies ran while one was open for 3% -> 4% of each run, Pallas kernels for 32% -> 40%
where the time goes in v11:
time: 95.7 us; the launch traced here: 94.2 us
  Pallas kernels  43.3 us (45%)
  starting transfers between devices  28.8 us (30%)
  blocking collectives  10.9 us (11%)
  local copies, waits for them, and re-layouts  6.86 us (7%)
  waiting for transfers between devices  2.71 us (3%)
  between operations  1.56 us (2%)
    pallas_call x10, Pallas kernels, call(): pl.pallas_call(kernel, grid=grid, out_shape=shapes, in_specs=in_specs, ou...  43.3 us
    all_to_all x1, blocking collectives, local(): lax.all_to_all(blocks, ('domain', 'band'), split_axis=0, concat_axis=0, t...  10.9 us
    ppermute x1, starting transfers between devices, local(): later_link = lax.ppermute(later_pass, 'domain', link_pairs)  6.77 us
    all_to_all x1, starting transfers between devices, local(): lax.all_to_all(message, 'band', split_axis=0, concat_axis=0, tiled=True)  4.6 us
    ppermute x1, starting transfers between devices, local(): link_early = lax.ppermute(early_part, 'domain', link_pairs)  4.5 us
    ppermute x3, starting transfers between devices, swapped(): lax.ppermute(values[k - 1], axis, [(i, i ^ k) for i in range(size)])  3.97 us
    unnamed x25, local copies, waits for them, and re-layouts  3.62 us
    ppermute x1, starting transfers between devices, local(): link_late = lax.ppermute(late_part, 'domain', link_pairs)  3.01 us
  transfers between devices with their start and end apart: 14, of which 1 were waited for; matrix products, arithmetic and copies ran while one was open for 4% of the time, Pallas kernels for 40%

profile of v11, /device:TPU:1, one launch (start us, length us, event | category | flops | bytes accessed | tf_op | source)
XLA Modules:
  0.0 94.2 jit_solution(8816457700444431381)
XLA Ops:
  0.6 4.1 %shard_map.95 = (bf16[128,64,128]{2,1,0:T(8,128)(2,1)}, bf16[64,64,128]{2,1,0:T(8,128)(2,1)}, bf16[64,64,128]{2,1,0:T(8,128)(2,1)}, bf16[100,64,128]{2,1,0:T(8,128)(2,1)}) custom-call(bf16[64,128,128]{2,1,0:T(8,128)(2,1)} %bitcast.12), custom_call_target="tpu_custom_call" | custom-call | flops 1100000 | bytes 1024 | tf_op jit(solution)/shard_map/pallas_call | solution.py:34
  4.9 4.5 %collective-permute-start.1 = (bf16[64,64,128]{2,1,0:T(8,128)(2,1)}, bf16[64,64,128]{2,1,0:T(8,128)(2,1)}, u32[]{:S(2)}, u32[]{:S(2)}) collective-permute-start(bf16[64,64,128]{2,1,0:T(8,128)(2,1)} %get-tuple-element.31), channel_id=1, source_target_pairs={{4,8},{8,4},{5,9},{9,5},{6,10},{10,6},{7,11},{11,7},{20,24},{24,20... | collective-permute-start | bytes 3145736 | tf_op jit(solution)/shard_map/ppermute | solution.py:423
  9.4 4.6 %all-to-all-start = ((bf16[100,64,128]{2,1,0:T(8,128)(2,1)}), bf16[100,64,128]{2,1,0:T(8,128)(2,1)}, u32[]{:S(2)}, u32[]{:S(2)}) async-start(bf16[100,64,128]{2,1,0:T(8,128)(2,1)} %get-tuple-element.39), calls=%async_computation | async-start | bytes 3276800 | tf_op jit(solution)/shard_map/all_to_all | solution.py:411
  14.7 10.9 %shard_map.97 = (f32[24,64,128]{2,1,0:T(8,128)}, bf16[64,64,128]{2,1,0:T(8,128)(2,1)}, bf16[16,64,128]{2,1,0:T(8,128)(2,1)}, bf16[16,64,128]{2,1,0:T(8,128)(2,1)}, bf16[8,64,128]{2,1,0:T(8,128)(2,1)}) custom-call(s32[384]{0:T(512)} %atom_ref.3, s32[384]{0:T(512)} %line_ref.3, s32[1]{0:T(128)S(6)} %copy.20.count_ref, ...), custom_call_target="tpu_custom_call", output_to_operand_aliasing={{1}: (5, {})} | custom-call | flops 11000000512 | bytes 1024 | tf_op jit(solution)/shard_map/pallas_call | solution.py:34
  25.6 1.2 %collective-permute-start.3 = (bf16[16,64,128]{2,1,0:T(8,128)(2,1)}, bf16[16,64,128]{2,1,0:T(8,128)(2,1)S(1)}, u32[]{:S(2)}, u32[]{:S(2)}) collective-permute-start(bf16[16,64,128]{2,1,0:T(8,128)(2,1)} %get-tuple-element.35), channel_id=1, source_target_pairs={{0,4},{4,0},{8,12},{12,8},{1,5},{5,1},{9,13},{13,9},{2,6},{6,2},{1... | collective-permute-start | bytes 786440 | tf_op jit(solution)/shard_map/ppermute | solution.py:450
  26.8 2.5 %collective-permute-start.4 = (bf16[16,64,128]{2,1,0:T(8,128)(2,1)}, bf16[16,64,128]{2,1,0:T(8,128)(2,1)S(1)}, u32[]{:S(2)}, u32[]{:S(2)}) collective-permute-start(bf16[16,64,128]{2,1,0:T(8,128)(2,1)} %get-tuple-element.36), channel_id=1, source_target_pairs={{4,8},{8,4},{5,9},{9,5},{6,10},{10,6},{7,11},{11,7},{20,24},{24,20... | collective-permute-start | bytes 786440 | tf_op jit(solution)/shard_map/ppermute | solution.py:448
  29.5 0.7 reshape.17.energy_ref
  30.2 3.0 %collective-permute-start.2 = (bf16[64,64,128]{2,1,0:T(8,128)(2,1)}, bf16[64,64,128]{2,1,0:T(8,128)(2,1)}, u32[]{:S(2)}, u32[]{:S(2)}) collective-permute-start(bf16[64,64,128]{2,1,0:T(8,128)(2,1)} %get-tuple-element.33), channel_id=1, source_target_pairs={{4,8},{8,4},{5,9},{9,5},{6,10},{10,6},{7,11},{11,7},{20,24},{24,20... | collective-permute-start | bytes 3145736 | tf_op jit(solution)/shard_map/ppermute | solution.py:451
  33.2 1.3 %slice_bitcast_fusion.1.refs_1_ = bf16[16,128]{1,0:T(8,128)(2,1)} fusion(bf16[64,64,128]{2,1,0:T(8,128)(2,1)} %collective-permute-done.1.early_link), kind=kLoop, calls=%fused_computation.1 | loop fusion | bytes 8192 | tf_op jit(solution)/shard_map/squeeze | solution.py:471
  34.5 1.3 %slice_bitcast_fusion.refs_2_ = bf16[16,128]{1,0:T(8,128)(2,1)} fusion(bf16[128,64,128]{2,1,0:T(8,128)(2,1)} %collective-permute-done.core_ref), kind=kLoop, calls=%fused_computation | loop fusion | bytes 8192 | tf_op jit(solution)/shard_map/squeeze | solution.py:471
  36.6 12.2 %shard_map.98 = (f32[128,64,128]{2,1,0:T(8,128)}, bf16[8,64,128]{2,1,0:T(8,128)(2,1)}, f32[8,128]{1,0:T(8,128)}, bf16[10,64,128]{2,1,0:T(8,128)(2,1)}, bf16[10,6...) custom-call(s32[384]{0:T(512)} %atom_ref.3, s32[384]{0:T(512)} %line_ref.3, s32[1]{0:T(128)S(6)} %copy.20.count_ref, ...), custom_call_target="tpu_custom_call" | custom-call | flops 32999999488 | bytes 1024 | tf_op jit(solution)/shard_map/pallas_call | solution.py:34
  48.8 1.8 %collective-permute-start.6 = (bf16[10,64,128]{2,1,0:T(8,128)(2,1)}, bf16[10,64,128]{2,1,0:T(8,128)(2,1)S(1)}, u32[]{:S(2)}, u32[]{:S(2)}) collective-permute-start(bf16[10,64,128]{2,1,0:T(8,128)(2,1)} %get-tuple-element.46), channel_id=1, source_target_pairs={{0,1},{1,0},{2,3},{3,2},{4,5},{5,4},{6,7},{7,6},{8,9},{9,8},{10,11... | collective-permute-start | bytes 491528 | tf_op jit(solution)/shard_map/ppermute | solution.py:380
  50.7 2.1 %collective-permute-start.7 = (bf16[10,64,128]{2,1,0:T(8,128)(2,1)}, bf16[10,64,128]{2,1,0:T(8,128)(2,1)S(1)}, u32[]{:S(2)}, u32[]{:S(2)}) collective-permute-start(bf16[10,64,128]{2,1,0:T(8,128)(2,1)} %get-tuple-element.47), channel_id=1, source_target_pairs={{0,2},{1,3},{2,0},{3,1},{4,6},{5,7},{6,4},{7,5},{8,10},{9,11},{10,... | collective-permute-start | bytes 491528 | tf_op jit(solution)/shard_map/ppermute | solution.py:380
  52.8 0.7 copy-done.2
  53.5 1.5 %shard_map.99 = (bf16[25,256,128]{2,1,0:T(8,128)(2,1)S(1)}, bf16[12,256,128]{2,1,0:T(8,128)(2,1)S(1)}, f32[8,128]{1,0:T(8,128)S(1)}) custom-call(bf16[100,64,128]{2,1,0:T(8,128)(2,1)} %all-to-all-done.landed, f32[8,128]{1,0:T(8,128)S(1)} %copy-done.2), custom_call_target="tpu_custom_call" | custom-call | flops 1100000 | bytes 1024 | tf_op jit(solution)/shard_map/pallas_call | solution.py:34
  55.6 6.8 %collective-permute-start.12 = (bf16[12,256,128]{2,1,0:T(8,128)(2,1)S(1)}, bf16[12,256,128]{2,1,0:T(8,128)(2,1)}, u32[]{:S(2)}, u32[]{:S(2)}) collective-permute-start(bf16[12,256,128]{2,1,0:T(8,128)(2,1)S(1)} %get-tuple-element.51), channel_id=1, source_target_pairs={{4,8},{8,4},{5,9},{9,5},{6,10},{10,6},{7,11},{11,7},{20,24},{24,20... | collective-permute-start | bytes 2359304 | tf_op jit(solution)/shard_map/ppermute | solution.py:487
  62.4 7.3 %shard_map.100 = (bf16[64,128,128]{2,1,0:T(8,128)(2,1)}, f32[8,128]{1,0:T(8,128)}) custom-call(bf16[128,64,128]{2,1,0:T(8,128)(2,1)} %get-tuple-element.30.xt_hbm.xt_ref.last_ref.next_ref, bf16[128,64,128]{2,1,0:T(8,128)(2,1)} %get-tuple-element.30.xt_hbm.xt_ref.last_ref.next_ref, bf16[128,64,128]{2,1,0:T(8,128)(2,1)} %get-tuple-element.30.xt_hbm.xt_ref.last_ref.next_ref, ...), custom_call_target="tpu_custom_call" | custom-call | flops 1100000 | bytes 1024 | tf_op jit(solution)/shard_map/pallas_call | solution.py:34
  70.5 3.2 %shard_map.101 = (bf16[9,256,128]{2,1,0:T(8,128)(2,1)S(1)}, bf16[4,256,128]{2,1,0:T(8,128)(2,1)}, bf16[2,256,128]{2,1,0:T(8,128)(2,1)S(1)}, f32[8,128]{1,0:T(8,128)}) custom-call(bf16[128,64,128]{2,1,0:T(8,128)(2,1)} %get-tuple-element.30.xt_hbm.xt_ref.last_ref.next_ref, bf16[8,64,128]{2,1,0:T(8,128)(2,1)} %get-tuple-element.43.whole_ref, ...), custom_call_target="tpu_custom_call" | custom-call | flops 32999999488 | bytes 1024 | tf_op jit(solution)/shard_map/pallas_call | solution.py:34
  73.8 1.9 %collective-permute-start.10 = (bf16[4,256,128]{2,1,0:T(8,128)(2,1)}, bf16[4,256,128]{2,1,0:T(8,128)(2,1)S(1)}, u32[]{:S(2)}, u32[]{:S(2)}) collective-permute-start(bf16[4,256,128]{2,1,0:T(8,128)(2,1)} %get-tuple-element.50), channel_id=1, source_target_pairs={{4,8},{8,4},{5,9},{9,5},{6,10},{10,6},{7,11},{11,7},{20,24},{24,20... | collective-permute-start | bytes 786440 | tf_op jit(solution)/shard_map/ppermute | solution.py:536
  76.5 2.5 %shard_map.102.begun_ref = f32[2,256,256]{2,1,0:T(8,128)S(1)} custom-call(bf16[25,256,128]{2,1,0:T(8,128)(2,1)S(1)} %get-tuple-element.44.after_ref.all_ref, bf16[12,256,128]{2,1,0:T(8,128)(2,1)} %collective-permute-done.11.core_ref, bf16[12,256,128]{2,1,0:T(8,128)(2,1)} %collective-permute-done.12.link_ref, f32[128,128]{1,0:T(8,128)S(1)} %bitcast.10, ...), custom_call_target="tpu_custom_call" | custom-call | flops 1100000 | bytes 1024 | tf_op jit(solution)/shard_map/pallas_call | solution.py:34
  79.0 2.7 %collective-permute-done.10.link_ref = bf16[4,256,128]{2,1,0:T(8,128)(2,1)S(1)} collective-permute-done((bf16[4,256,128]{2,1,0:T(8,128)(2,1)}, bf16[4,256,128]{2,1,0:T(8,128)(2,1)S(1)}, u32[]{:S(2)}, u32[]{:S(2)}) %collective-permute-start.10) | collective-permute-done | bytes 262176 | tf_op jit(solution)/shard_map/ppermute | solution.py:536
  81.7 0.9 shard_map.103
  82.6 10.9 %all_to_all.10.parts_ref = bf16[16,64,128]{2,1,0:T(8,128)(2,1)S(1)} all-to-all(bf16[16,64,128]{2,1,0:T(8,128)(2,1)S(1)} %shard_map.103), channel_id=1, replica_groups=mesh['groups'=2,'domain'=4,'band'=4] {'domain','band'}, dimensions={0} | all-to-all | bytes 524288 | tf_op jit(solution)/shard_map/all_to_all | solution.py:559
  93.5 0.7 shard_map.104
  (43 shorter events, 3.4 us)
Async XLA Ops:
  4.8 29.7 %collective-permute-start = (bf16[128,64,128]{2,1,0:T(8,128)(2,1)}, bf16[128,64,128]{2,1,0:T(8,128)(2,1)}, u32[]{:S(2)}, u32[]{:S(2)}) collective-permute-start(bf16[128,64,128]{2,1,0:T(8,128)(2,1)} %get-tuple-element.30.xt_hbm.xt_ref.last_ref.next_ref), channel_id=1, source_target_pairs={{0,4},{4,0},{8,12},{12,8},{1,5},{5,1},{9,13},{13,9},{2,6},{6,2},{1... | collective-permute-start | bytes 6291464 | tf_op jit(solution)/shard_map/ppermute | solution.py:424
  4.9 25.3 %collective-permute-start.1 = (bf16[64,64,128]{2,1,0:T(8,128)(2,1)}, bf16[64,64,128]{2,1,0:T(8,128)(2,1)}, u32[]{:S(2)}, u32[]{:S(2)}) collective-permute-start(bf16[64,64,128]{2,1,0:T(8,128)(2,1)} %get-tuple-element.31), channel_id=1, source_target_pairs={{4,8},{8,4},{5,9},{9,5},{6,10},{10,6},{7,11},{11,7},{20,24},{24,20... | collective-permute-start | bytes 3145736 | tf_op jit(solution)/shard_map/ppermute | solution.py:423
  9.4 43.4 %all-to-all-start = ((bf16[100,64,128]{2,1,0:T(8,128)(2,1)}), bf16[100,64,128]{2,1,0:T(8,128)(2,1)}, u32[]{:S(2)}, u32[]{:S(2)}) async-start(bf16[100,64,128]{2,1,0:T(8,128)(2,1)} %get-tuple-element.39), calls=%async_computation | async-start | bytes 3276800 | tf_op jit(solution)/shard_map/all_to_all | solution.py:411
  14.7 14.7 %copy-start.5 = (f32[256,16]{0,1:T(8,128)S(1)}, f32[256,16]{0,1:T(8,128)}, u32[]{:S(2)}) copy-start(f32[256,16]{0,1:T(8,128)} %param.14) | copy-start | bytes 49156
  25.5 10.2 %collective-permute-start.5 = (bf16[8,64,128]{2,1,0:T(8,128)(2,1)}, bf16[8,64,128]{2,1,0:T(8,128)(2,1)S(1)}, u32[]{:S(2)}, u32[]{:S(2)}) collective-permute-start(bf16[8,64,128]{2,1,0:T(8,128)(2,1)} %get-tuple-element.37), channel_id=1, source_target_pairs={{0,8},{4,12},{8,0},{12,4},{1,9},{5,13},{9,1},{13,5},{2,10},{6,14},... | collective-permute-start | bytes 393224 | tf_op jit(solution)/shard_map/ppermute | solution.py:449
  25.6 10.1 %collective-permute-start.3 = (bf16[16,64,128]{2,1,0:T(8,128)(2,1)}, bf16[16,64,128]{2,1,0:T(8,128)(2,1)S(1)}, u32[]{:S(2)}, u32[]{:S(2)}) collective-permute-start(bf16[16,64,128]{2,1,0:T(8,128)(2,1)} %get-tuple-element.35), channel_id=1, source_target_pairs={{0,4},{4,0},{8,12},{12,8},{1,5},{5,1},{9,13},{13,9},{2,6},{6,2},{1... | collective-permute-start | bytes 786440 | tf_op jit(solution)/shard_map/ppermute | solution.py:450
  26.8 8.9 %collective-permute-start.4 = (bf16[16,64,128]{2,1,0:T(8,128)(2,1)}, bf16[16,64,128]{2,1,0:T(8,128)(2,1)S(1)}, u32[]{:S(2)}, u32[]{:S(2)}) collective-permute-start(bf16[16,64,128]{2,1,0:T(8,128)(2,1)} %get-tuple-element.36), channel_id=1, source_target_pairs={{4,8},{8,4},{5,9},{9,5},{6,10},{10,6},{7,11},{11,7},{20,24},{24,20... | collective-permute-start | bytes 786440 | tf_op jit(solution)/shard_map/ppermute | solution.py:448
  30.2 32.2 %collective-permute-start.2 = (bf16[64,64,128]{2,1,0:T(8,128)(2,1)}, bf16[64,64,128]{2,1,0:T(8,128)(2,1)}, u32[]{:S(2)}, u32[]{:S(2)}) collective-permute-start(bf16[64,64,128]{2,1,0:T(8,128)(2,1)} %get-tuple-element.33), channel_id=1, source_target_pairs={{4,8},{8,4},{5,9},{9,5},{6,10},{10,6},{7,11},{11,7},{20,24},{24,20... | collective-permute-start | bytes 3145736 | tf_op jit(solution)/shard_map/ppermute | solution.py:451
  35.8 0.7 copy-start.6
  35.8 0.8 copy-start.7
  48.8 20.9 %collective-permute-start.6 = (bf16[10,64,128]{2,1,0:T(8,128)(2,1)}, bf16[10,64,128]{2,1,0:T(8,128)(2,1)S(1)}, u32[]{:S(2)}, u32[]{:S(2)}) collective-permute-start(bf16[10,64,128]{2,1,0:T(8,128)(2,1)} %get-tuple-element.46), channel_id=1, source_target_pairs={{0,1},{1,0},{2,3},{3,2},{4,5},{5,4},{6,7},{7,6},{8,9},{9,8},{10,11... | collective-permute-start | bytes 491528 | tf_op jit(solution)/shard_map/ppermute | solution.py:380
  50.7 19.1 %collective-permute-start.7 = (bf16[10,64,128]{2,1,0:T(8,128)(2,1)}, bf16[10,64,128]{2,1,0:T(8,128)(2,1)S(1)}, u32[]{:S(2)}, u32[]{:S(2)}) collective-permute-start(bf16[10,64,128]{2,1,0:T(8,128)(2,1)} %get-tuple-element.47), channel_id=1, source_target_pairs={{0,2},{1,3},{2,0},{3,1},{4,6},{5,7},{6,4},{7,5},{8,10},{9,11},{10,... | collective-permute-start | bytes 491528 | tf_op jit(solution)/shard_map/ppermute | solution.py:380
  52.7 17.0 %collective-permute-start.8 = (bf16[10,64,128]{2,1,0:T(8,128)(2,1)}, bf16[10,64,128]{2,1,0:T(8,128)(2,1)S(1)}, u32[]{:S(2)}, u32[]{:S(2)}) collective-permute-start(bf16[10,64,128]{2,1,0:T(8,128)(2,1)} %get-tuple-element.48), channel_id=1, source_target_pairs={{0,3},{1,2},{2,1},{3,0},{4,7},{5,6},{6,5},{7,4},{8,11},{9,10},{10,... | collective-permute-start | bytes 491528 | tf_op jit(solution)/shard_map/ppermute | solution.py:380
  52.8 0.7 copy-start.2
  55.6 20.2 %collective-permute-start.12 = (bf16[12,256,128]{2,1,0:T(8,128)(2,1)S(1)}, bf16[12,256,128]{2,1,0:T(8,128)(2,1)}, u32[]{:S(2)}, u32[]{:S(2)}) collective-permute-start(bf16[12,256,128]{2,1,0:T(8,128)(2,1)S(1)} %get-tuple-element.51), channel_id=1, source_target_pairs={{4,8},{8,4},{5,9},{9,5},{6,10},{10,6},{7,11},{11,7},{20,24},{24,20... | collective-permute-start | bytes 2359304 | tf_op jit(solution)/shard_map/ppermute | solution.py:487
  62.4 13.5 %collective-permute-start.11 = (bf16[12,256,128]{2,1,0:T(8,128)(2,1)S(1)}, bf16[12,256,128]{2,1,0:T(8,128)(2,1)}, u32[]{:S(2)}, u32[]{:S(2)}) collective-permute-start(bf16[12,256,128]{2,1,0:T(8,128)(2,1)S(1)} %get-tuple-element.51), channel_id=1, source_target_pairs={{0,4},{4,0},{8,12},{12,8},{1,5},{5,1},{9,13},{13,9},{2,6},{6,2},{1... | collective-permute-start | bytes 2359304 | tf_op jit(solution)/shard_map/ppermute | solution.py:488
  69.7 0.7 copy-start.8
  69.8 0.7 copy-start.9
  69.8 0.8 copy-start.10
  70.5 5.3 %copy-start = (f32[1,128,128]{2,1,0:T(8,128)S(1)}, f32[1,128,128]{2,1,0:T(8,128)}, u32[]{:S(2)}) copy-start(f32[1,128,128]{2,1,0:T(8,128)} %param.9) | copy-start | bytes 196612
  73.8 7.9 %copy-start.1 = (f32[32,128]{1,0:T(8,128)S(1)}, f32[32,128]{1,0:T(8,128)}, u32[]{:S(2)}) copy-start(f32[32,128]{1,0:T(8,128)} %reshape.17.energy_ref) | copy-start | bytes 49156
  73.8 7.9 %collective-permute-start.10 = (bf16[4,256,128]{2,1,0:T(8,128)(2,1)}, bf16[4,256,128]{2,1,0:T(8,128)(2,1)S(1)}, u32[]{:S(2)}, u32[]{:S(2)}) collective-permute-start(bf16[4,256,128]{2,1,0:T(8,128)(2,1)} %get-tuple-element.50), channel_id=1, source_target_pairs={{4,8},{8,4},{5,9},{9,5},{6,10},{10,6},{7,11},{11,7},{20,24},{24,20... | collective-permute-start | bytes 786440 | tf_op jit(solution)/shard_map/ppermute | solution.py:536
  75.7 6.0 %collective-permute-start.9 = (bf16[4,256,128]{2,1,0:T(8,128)(2,1)}, bf16[4,256,128]{2,1,0:T(8,128)(2,1)S(1)}, u32[]{:S(2)}, u32[]{:S(2)}) collective-permute-start(bf16[4,256,128]{2,1,0:T(8,128)(2,1)} %get-tuple-element.50), channel_id=1, source_target_pairs={{0,4},{4,0},{8,12},{12,8},{1,5},{5,1},{9,13},{13,9},{2,6},{6,2},{1... | collective-permute-start | bytes 786440 | tf_op jit(solution)/shard_map/ppermute | solution.py:537
  75.8 0.7 copy-start.3
  (2 other events, 1.2 us)

commit v12 on v10

--- a/solution.py
+++ b/solution.py
@@ -88,10 +88,14 @@
     return [2 * groups * side for side in (1 - odd, odd, 1 - upper, upper)]
 
 
-def slot_at(t, atom_ref, line_ref, count_ref, atoms_here):
+def slot_reader(atom_ref, line_ref, count_ref, atoms_here):
     first = (lax.axis_index("domain") - 1) * atoms_here
-    atom = jnp.clip(atom_ref[t] - first, 0, 3 * atoms_here - 1)
-    return line_ref[t], atom, t < count_ref[0]
+    live = count_ref[0]
+
+    def slot_at(t):
+        return line_ref[t], jnp.clip(atom_ref[t] - first, 0, 3 * atoms_here - 1), t < live
+
+    return slot_at
 
 
 def project_kernel(atom_ref, line_ref, count_ref, xt_ref, p_hbm, handed, mine_ref, same, core_ref, link_ref, *refs):
@@ -114,10 +118,12 @@
 
     lax.fori_loop(0, 3 * groups, clear, 0)
 
+    slot_at = slot_reader(atom_ref, line_ref, count_ref, groups * per_group)
+
     def body(i, carry):
         for u in range(unroll):
             t = i * unroll + u
-            line, atom, live = slot_at(t, atom_ref, line_ref, count_ref, groups * per_group)
+            line, atom, live = slot_at(t)
             part = lax.dot_general(p_ref[t], xt_ref[line], NT, preferred_element_type=F32)
             total[jnp.where(live, atom, 3 * groups * per_group)] += part
         return carry
@@ -140,7 +146,7 @@
 
 
 def nonlocal_kernel(
-    first, fars, atom_ref, line_ref, count_ref, xt_ref, p_hbm, energy_ref, mine_ref, core_ref, link_ref, *refs
+    first, fars, atom_ref, line_ref, count_ref, xt_hbm, p_hbm, energy_ref, mine_ref, core_ref, link_ref, *refs
 ):
     far_refs, (_, _, out_hbm, whole_hbm, done_ref, *messages, lines_sum, whole_ref, total, atoms, p_ref, sems) = (
         refs[:fars],
@@ -149,7 +155,7 @@
     slots, proj_count, _ = p_ref.shape
     groups, states = mine_ref.shape[0] // 3, mine_ref.shape[1]
     per_group = LANES // proj_count
-    lines = xt_ref.shape[0]
+    lines = xt_hbm.shape[0]
     unroll = 16
     load = start(pltpu.make_async_copy(p_hbm, p_ref, sems.at[0]))
     done_ref[...] = jnp.zeros_like(done_ref)
@@ -176,54 +182,62 @@
     for g in range(groups):
         whole_ref[g] = total[groups + g].astype(BF16)
     send_whole = start(pltpu.make_async_copy(whole_ref, whole_hbm, sems.at[1]))
-    share = xt_ref.shape[0] // (len(messages) + 1)
+    share = lines // (len(messages) + 1)
     held = groups // (len(messages) + 1)
+    brought = []
     for k, message in enumerate(messages, 1):
         to = lax.axis_index("band") ^ k
-        for i in range(first):
-            message[i] = xt_ref[to * share + i]
+        target = message.at[pl.ds(0, first)]
+        brought.append(start(pltpu.make_async_copy(xt_hbm.at[pl.ds(to * share, first)], target, sems.at[2 + k])))
         for i in range(held):
             message[first + i] = whole_ref[to * held + i]
     load.wait()
 
+    slot_at = slot_reader(atom_ref, line_ref, count_ref, groups * per_group)
+
     def body(i, carry):
         for u in range(unroll):
             t = i * unroll + u
-            line, atom, live = slot_at(t, atom_ref, line_ref, count_ref, groups * per_group)
+            line, atom, live = slot_at(t)
             part = jnp.dot(atoms[atom], p_ref[t], preferred_element_type=F32)
             lines_sum[jnp.where(live, line, lines)] += part
         return carry
 
     lax.fori_loop(0, slots // unroll, body, 0)
     send = start(pltpu.make_async_copy(lines_sum.at[pl.ds(0, lines)], out_hbm, sems.at[2]))
-    send_whole.wait()
-    send.wait()
-
-
-def stencil_kernel(early_steps, xt_ref, core_ref, early_ref, late_ref, added_ref, pot_ref, ring_ref, unread, out_ref, done_ref):
+    for copy in (send_whole, send, *brought):
+        copy.wait()
+
+
+def stencil_kernel(
+    early_steps, xt_ref, last_ref, next_ref, core_ref, early_ref, late_ref, added_ref, pot_ref, ring_ref, unread,
+    out_ref, done_ref,
+):
     states, here, _ = out_ref.shape
-    lines = xt_ref.shape[0]
     done_ref[...] = jnp.zeros_like(done_ref)
-    step = pl.program_id(0)
-    early = step < early_steps
-    for part in range(0, here, ROWS):
-        y0 = step * here + part
+    early = pl.program_id(0) < early_steps
+
+    def line(i, rows):
+        ref, at = (last_ref, 0) if i < 0 else (next_ref, 0) if i == here else (xt_ref, i)
+        return ref[at, rows, :]
+
+    for y0 in range(0, here, ROWS):
         for s0 in range(0, states, ROWS):
             rows = slice(s0, s0 + ROWS)
             results = []
-            cells = jnp.concatenate([xt_ref[y0 + i, rows, :] for i in range(ROWS)], axis=0)
+            cells = jnp.concatenate([line(y0 + i, rows) for i in range(ROWS)], axis=0)
             along = jnp.dot(cells, ring_ref[...], preferred_element_type=F32)
-            before = xt_ref[lax.rem(y0 + lines - 1, lines), rows, :].astype(F32)
-            x = xt_ref[y0, rows, :].astype(F32)
+            before, x = line(y0 - 1, rows).astype(F32), line(y0, rows).astype(F32)
             for i in range(ROWS):
-                after = xt_ref[lax.rem(y0 + i + 1, lines), rows, :].astype(F32)
-                link = jnp.where(early, early_ref[part + i, rows, :], late_ref[part + i, rows, :]).astype(F32)
-                beside = (before + after) + (core_ref[part + i, rows, :].astype(F32) + link)
-                value = along[i * ROWS : (i + 1) * ROWS] + pot_ref[part + i : part + i + 1, :] * x
-                results.append(value + added_ref[part + i, rows, :] - 0.5 * beside)
+                y = y0 + i
+                after = line(y + 1, rows).astype(F32)
+                link = jnp.where(early, early_ref[y, rows, :], late_ref[y, rows, :]).astype(F32)
+                beside = (before + after) + (core_ref[y, rows, :].astype(F32) + link)
+                value = along[i * ROWS : (i + 1) * ROWS] + pot_ref[y : y + 1, :] * x
+                results.append(value + added_ref[y, rows, :] - 0.5 * beside)
                 before, x = x, after
             turned = jnp.swapaxes(jnp.stack(results, axis=0), 0, 1).astype(BF16)
-            out_ref[rows, part : part + ROWS, :] = turned
+            out_ref[rows, y0 : y0 + ROWS, :] = turned
 
 
 def pass_half(all_ref, pass_hbm, sem):
@@ -248,10 +262,10 @@
     pass_half(all_ref, pass_hbm, pass_sem)
 
 
-def early_kernel(bands, share, xt_ref, whole_ref, after_ref, unread, *refs):
+def early_kernel(bands, share, xt_hbm, whole_ref, after_ref, unread, *refs):
     pieces, (all_ref, pass_hbm, projs_ref, done_ref, sems, pass_sem) = refs[: bands - 1], refs[bands - 1 :]
     done_ref[...] = jnp.zeros_like(done_ref)
-    states = xt_ref.shape[1]
+    states = xt_hbm.shape[1]
     band = lax.axis_index("band")
     count, held = all_ref.shape[0] - 1, projs_ref.shape[0]
     loads = []
@@ -262,7 +276,7 @@
     for k in range(bands):
         at = pl.ds(pl.multiple_of((band ^ k) * states, states), states)
         if k == 0:
-            load(xt_ref.at[pl.ds(band * share, count)], all_ref.at[pl.ds(0, count), at, :])
+            load(xt_hbm.at[pl.ds(band * share, count)], all_ref.at[pl.ds(0, count), at, :])
             load(whole_ref.at[pl.ds(band * held, held)], projs_ref.at[:, at, :])
         else:
             load(pieces[k - 1].at[pl.ds(0, count)], all_ref.at[pl.ds(0, count), at, :])
@@ -398,17 +412,16 @@
         ],
         (tile_atom, tile_line, tile_count, xt, projectors, late_part),
         aliases={5: 1},
-        micros=10,
     )
     from_link = lax.ppermute(to_link, "domain", link_pairs)
     from_far = [lax.ppermute(value, "domain", pairs) for value, pairs in zip(to_far, far_pairs)]
     from_core = lax.ppermute(to_core, "domain", core_pairs)
     link_late = lax.ppermute(late_part, "domain", link_pairs)
     added, whole, summed_up, *messages = call(
-        32,
+        61,
         functools.partial(nonlocal_kernel, first, len(far_pairs)),
         (),
-        [SCALARS] * 3 + [NEAR, PINNED, WHOLE, NEAR, WHOLE, WHOLE] + [WHOLE] * len(far_pairs) + [UNREAD] * 2,
+        [SCALARS] * 3 + [FAR, PINNED, WHOLE, NEAR, WHOLE, WHOLE] + [WHOLE] * len(far_pairs) + [UNREAD] * 2,
         [PINNED, PINNED, WHOLE] + [WHOLE] * (bands - 1),
         [(line_shape, F32), (group_shape, BF16), ((8, LANES), F32)]
         + [((first + group_share, states, cols_z), BF16)] * (bands - 1),
@@ -418,13 +431,12 @@
             pltpu.VMEM((3 * groups, states, LANES), F32),
             pltpu.VMEM((3 * atoms_here, states, proj_count), BF16),
             pltpu.VMEM(projectors.shape, BF16),
-            copies((3,)),
+            copies((2 + bands,)),
         ],
         (
-            tile_atom, tile_line, tile_count, xt, projectors, energy, mine, from_core, from_link, *from_far,
+            tile_atom, tile_line, tile_count, xt_far, projectors, energy, mine, from_core, from_link, *from_far,
             link_early[0, :ROWS], core_field[0, :ROWS],
         ),
-        micros=30,
     )
     early = swapped(messages, "band")
 
@@ -437,6 +449,7 @@
         [((rest + 1, total_states, cols_z), BF16), ((rest // 2, total_states, cols_z), BF16), ((8, LANES), F32)],
         [copies((bands,)), copies],
         (landed, summed_up),
+        micros=20,
     )
     later_link = lax.ppermute(later_pass, "domain", link_pairs)
     later_core = lax.ppermute(later_pass, "domain", core_pairs)
@@ -449,7 +462,9 @@
         functools.partial(stencil_kernel, early_steps),
         (steps,),
         [
-            NEAR,
+            block,
+            pl.BlockSpec((1, states, cols_z), lambda i: (lax.rem(i * span + lines - 1, lines), 0, 0)),
+            pl.BlockSpec((1, states, cols_z), lambda i: (lax.rem(i * span + span, lines), 0, 0)),
             block,
             pl.BlockSpec((span, states, cols_z), lambda i: (jnp.minimum(i, early_steps - 1), 0, 0)),
             pl.BlockSpec((span, states, cols_z), lambda i: (jnp.maximum(i - early_steps, 0), 0, 0)),
@@ -462,7 +477,7 @@
         [((states, lines, cols_z), BF16), ((8, LANES), F32)],
         [],
         (
-            xt, core_field, link_early, link_late, pltpu.with_memory_space_constraint(added, pltpu.HBM), pot, ring,
+            xt_far, xt_far, xt_far, core_field, link_early, link_late, pltpu.with_memory_space_constraint(added, pltpu.HBM), pot, ring,
             later_token,
         ),
     )
@@ -471,7 +486,7 @@
         32,
         functools.partial(early_kernel, bands, share),
         (),
-        [NEAR, PINNED, NEAR, WHOLE] + [FAR] * (bands - 1),
+        [FAR, PINNED, NEAR, WHOLE] + [FAR] * (bands - 1),
         [NEAR, FAR, NEAR, WHOLE],
         [
             ((first + 1, total_states, cols_z), BF16),
@@ -480,7 +495,7 @@
             ((8, LANES), F32),
         ],
         [copies((2 * bands + 1,)), copies],
-        (xt, whole, later_all, done, *early),
+        (xt_far, whole, later_all, done, *early),
         micros=30,
     )
     early_link = lax.ppermute(early_pass, "domain", link_pairs)

time: 92.7 us -> 93.1 us (level)
  Pallas kernels: 35.1 us -> 36.7 us
  local copies, waits for them, and re-layouts: 10.6 us -> 9.25 us
    unnamed x23 -> x31, local copies, waits for them, and re-layouts: 8.9 us -> 6.7 us
    pallas_call x9, Pallas kernels: 35.1 us -> 36.7 us  [call(): pl.pallas_call(kernel, grid=grid, out_shape=shapes, in_specs=in_specs, ou...]
    ppermute x1, starting transfers between devices: 4.6 us -> 3.04 us  [local(): link_early = lax.ppermute(early_part, 'domain', link_pairs)]
    all_to_all x1, starting transfers between devices: 4.6 us -> 5.55 us  [local(): lax.all_to_all(message, 'band', split_axis=0, concat_axis=0, tiled=True)]
  transfers between devices with their start and end apart: 14 -> 14, of which waited for: 2 -> 2; matrix products, arithmetic and copies ran while one was open for 3% -> 3% of each run, Pallas kernels for 32% -> 34%
where the time goes in v12:
time: 93.1 us; the launch traced here: 91.7 us
  Pallas kernels  36.7 us (39%)
  starting transfers between devices  25.7 us (28%)
  blocking collectives  14.3 us (15%)
  local copies, waits for them, and re-layouts  9.25 us (10%)
  waiting for transfers between devices  4.26 us (5%)
  between operations  1.52 us (2%)
    pallas_call x9, Pallas kernels, call(): pl.pallas_call(kernel, grid=grid, out_shape=shapes, in_specs=in_specs, ou...  36.7 us
    all_to_all x1, blocking collectives, local(): lax.all_to_all(blocks, ('domain', 'band'), split_axis=0, concat_axis=0, t...  14.3 us
    unnamed x31, local copies, waits for them, and re-layouts  6.7 us
    all_to_all x1, starting transfers between devices, local(): lax.all_to_all(message, 'band', split_axis=0, concat_axis=0, tiled=True)  5.55 us
    ppermute x1, waiting for transfers between devices, local(): early_link = lax.ppermute(early_pass, 'domain', link_pairs)  4.07 us
    ppermute x3, starting transfers between devices, swapped(): lax.ppermute(values[k - 1], axis, [(i, i ^ k) for i in range(size)])  3.94 us
    ppermute x1, starting transfers between devices, local(): later_link = lax.ppermute(later_pass, 'domain', link_pairs)  3.32 us
    ppermute x1, starting transfers between devices, local(): link_early = lax.ppermute(early_part, 'domain', link_pairs)  3.04 us
  transfers between devices with their start and end apart: 14, of which 2 were waited for; matrix products, arithmetic and copies ran while one was open for 3% of the time, Pallas kernels for 34%

profile of v12, /device:TPU:1, one launch (start us, length us, event | category | flops | bytes accessed | tf_op | source)
XLA Modules:
  0.0 91.7 jit_solution(5782200784382194556)
XLA Ops:
  0.6 4.0 %shard_map.95 = (bf16[128,64,128]{2,1,0:T(8,128)(2,1)S(1)}, bf16[128,64,128]{2,1,0:T(8,128)(2,1)}, bf16[64,64,128]{2,1,0:T(8,128)(2,1)}, bf16[64,64,128]{2,1,0:T(8,128)(2,1)}, bf16[100,64,128]{2,1,0:T(8,128)(2,1)}) custom-call(bf16[64,128,128]{2,1,0:T(8,128)(2,1)} %bitcast.12), custom_call_target="tpu_custom_call" | custom-call | flops 1100000 | bytes 1024 | tf_op jit(solution)/shard_map/pallas_call | solution.py:34
  4.7 1.3 %copy-done.2 = bf16[128,64,128]{2,1,0:T(8,128)(2,1)} copy-done((bf16[128,64,128]{2,1,0:T(8,128)(2,1)}, bf16[128,64,128]{2,1,0:T(8,128)(2,1)S(1)}, u32[]{:S(2)}) %copy-start.2) | copy-done | bytes 2097176
  6.0 5.6 %all-to-all-start = ((bf16[100,64,128]{2,1,0:T(8,128)(2,1)}), bf16[100,64,128]{2,1,0:T(8,128)(2,1)}, u32[]{:S(2)}, u32[]{:S(2)}) async-start(bf16[100,64,128]{2,1,0:T(8,128)(2,1)} %get-tuple-element.37), calls=%async_computation | async-start | bytes 3276800 | tf_op jit(solution)/shard_map/all_to_all | solution.py:394
  11.6 1.0 %collective-permute-start = (bf16[128,64,128]{2,1,0:T(8,128)(2,1)S(1)}, bf16[128,64,128]{2,1,0:T(8,128)(2,1)}, u32[]{:S(2)}, u32[]{:S(2)}) collective-permute-start(bf16[128,64,128]{2,1,0:T(8,128)(2,1)S(1)} %copy-done), channel_id=1, source_target_pairs={{0,4},{4,0},{8,12},{12,8},{1,5},{5,1},{9,13},{13,9},{2,6},{6,2},{1... | collective-permute-start | bytes 6291464 | tf_op jit(solution)/shard_map/ppermute | solution.py:396
  12.5 3.0 %collective-permute-start.1 = (bf16[64,64,128]{2,1,0:T(8,128)(2,1)}, bf16[64,64,128]{2,1,0:T(8,128)(2,1)S(1)}, u32[]{:S(2)}, u32[]{:S(2)}) collective-permute-start(bf16[64,64,128]{2,1,0:T(8,128)(2,1)} %get-tuple-element.28), channel_id=1, source_target_pairs={{4,8},{8,4},{5,9},{9,5},{6,10},{10,6},{7,11},{11,7},{20,24},{24,20... | collective-permute-start | bytes 3145736 | tf_op jit(solution)/shard_map/ppermute | solution.py:395
  16.3 1.6 %copy-done.3 = bf16[128,64,128]{2,1,0:T(8,128)(2,1)S(1)} copy-done((bf16[128,64,128]{2,1,0:T(8,128)(2,1)S(1)}, bf16[128,64,128]{2,1,0:T(8,128)(2,1)}, u32[]{:S(2)}) %copy-start.3) | copy-done | bytes 2097176
  17.9 9.1 %shard_map.96 = (f32[24,64,128]{2,1,0:T(8,128)S(1)}, bf16[64,64,128]{2,1,0:T(8,128)(2,1)}, bf16[16,64,128]{2,1,0:T(8,128)(2,1)}, bf16[16,64,128]{2,1,0:T(8,128)(2,1)}, bf16[8,64,128]{2,1,0:T(8,128)(2,1)S(1)}) custom-call(s32[384]{0:T(512)S(1)} %copy-done.11, s32[384]{0:T(512)S(1)} %copy-done.12, ...), custom_call_target="tpu_custom_call", output_to_operand_aliasing={{1}: (5, {})} | custom-call | flops 1100000 | bytes 1024 | tf_op jit(solution)/shard_map/pallas_call | solution.py:34
  27.9 1.0 %collective-permute-start.3 = (bf16[16,64,128]{2,1,0:T(8,128)(2,1)}, bf16[16,64,128]{2,1,0:T(8,128)(2,1)}, u32[]{:S(2)}, u32[]{:S(2)}) collective-permute-start(bf16[16,64,128]{2,1,0:T(8,128)(2,1)} %get-tuple-element.33), channel_id=1, source_target_pairs={{0,4},{4,0},{8,12},{12,8},{1,5},{5,1},{9,13},{13,9},{2,6},{6,2},{1... | collective-permute-start | bytes 786440 | tf_op jit(solution)/shard_map/ppermute | solution.py:418
  28.9 2.8 %collective-permute-start.4 = (bf16[16,64,128]{2,1,0:T(8,128)(2,1)}, bf16[16,64,128]{2,1,0:T(8,128)(2,1)}, u32[]{:S(2)}, u32[]{:S(2)}) collective-permute-start(bf16[16,64,128]{2,1,0:T(8,128)(2,1)} %get-tuple-element.34), channel_id=1, source_target_pairs={{4,8},{8,4},{5,9},{9,5},{6,10},{10,6},{7,11},{11,7},{20,24},{24,20... | collective-permute-start | bytes 786440 | tf_op jit(solution)/shard_map/ppermute | solution.py:416
  32.5 2.8 %collective-permute-start.2 = (bf16[64,64,128]{2,1,0:T(8,128)(2,1)}, bf16[64,64,128]{2,1,0:T(8,128)(2,1)}, u32[]{:S(2)}, u32[]{:S(2)}) collective-permute-start(bf16[64,64,128]{2,1,0:T(8,128)(2,1)} %get-tuple-element.31), channel_id=1, source_target_pairs={{4,8},{8,4},{5,9},{9,5},{6,10},{10,6},{7,11},{11,7},{20,24},{24,20... | collective-permute-start | bytes 3145736 | tf_op jit(solution)/shard_map/ppermute | solution.py:419
  35.8 1.0 %copy-done.4 = bf16[64,64,128]{2,1,0:T(8,128)(2,1)} copy-done((bf16[64,64,128]{2,1,0:T(8,128)(2,1)}, bf16[64,64,128]{2,1,0:T(8,128)(2,1)S(1)}, u32[]{:S(2)}) %copy-start.4) | copy-done | bytes 1048600
  36.8 1.3 %slice_bitcast_fusion.refs_2_ = bf16[16,128]{1,0:T(8,128)(2,1)} fusion(bf16[128,64,128]{2,1,0:T(8,128)(2,1)} %collective-permute-done.core_ref), kind=kLoop, calls=%fused_computation | loop fusion | bytes 8192 | tf_op jit(solution)/shard_map/squeeze | solution.py:438
  38.1 1.1 %copy-done.7 = f32[24,64,128]{2,1,0:T(8,128)S(1)} copy-done((f32[24,64,128]{2,1,0:T(8,128)S(1)}, f32[24,64,128]{2,1,0:T(8,128)}, u32[]{:S(2)}) %copy-start.7) | copy-done | bytes 786456
  39.2 11.8 %shard_map.97 = (f32[128,64,128]{2,1,0:T(8,128)}, bf16[8,64,128]{2,1,0:T(8,128)(2,1)}, f32[8,128]{1,0:T(8,128)}, bf16[10,64,128]{2,1,0:T(8,128)(2,1)}, bf16[10,6...) custom-call(s32[384]{0:T(512)} %atom_ref.3, s32[384]{0:T(512)} %line_ref.3, s32[1]{0:T(128)S(6)} %copy.16.count_ref, ...), custom_call_target="tpu_custom_call" | custom-call | flops 1100000 | bytes 1024 | tf_op jit(solution)/shard_map/pallas_call | solution.py:34
  51.0 1.8 %collective-permute-start.6 = (bf16[10,64,128]{2,1,0:T(8,128)(2,1)}, bf16[10,64,128]{2,1,0:T(8,128)(2,1)S(1)}, u32[]{:S(2)}, u32[]{:S(2)}) collective-permute-start(bf16[10,64,128]{2,1,0:T(8,128)(2,1)} %get-tuple-element.44), channel_id=1, source_target_pairs={{0,1},{1,0},{2,3},{3,2},{4,5},{5,4},{6,7},{7,6},{8,9},{9,8},{10,11... | collective-permute-start | bytes 491528 | tf_op jit(solution)/shard_map/ppermute | solution.py:367
  52.8 2.1 %collective-permute-start.7 = (bf16[10,64,128]{2,1,0:T(8,128)(2,1)}, bf16[10,64,128]{2,1,0:T(8,128)(2,1)S(1)}, u32[]{:S(2)}, u32[]{:S(2)}) collective-permute-start(bf16[10,64,128]{2,1,0:T(8,128)(2,1)} %get-tuple-element.45), channel_id=1, source_target_pairs={{0,2},{1,3},{2,0},{3,1},{4,6},{5,7},{6,4},{7,5},{8,10},{9,11},{10,... | collective-permute-start | bytes 491528 | tf_op jit(solution)/shard_map/ppermute | solution.py:367
  55.7 1.6 %shard_map.98 = (bf16[25,256,128]{2,1,0:T(8,128)(2,1)S(1)}, bf16[12,256,128]{2,1,0:T(8,128)(2,1)S(1)}, f32[8,128]{1,0:T(8,128)S(1)}) custom-call(bf16[100,64,128]{2,1,0:T(8,128)(2,1)} %all-to-all-done.landed, f32[8,128]{1,0:T(8,128)S(1)} %copy-done.13), custom_call_target="tpu_custom_call" | custom-call | flops 22000001024 | bytes 1024 | tf_op jit(solution)/shard_map/pallas_call | solution.py:34
  57.3 3.3 %collective-permute-start.12 = (bf16[12,256,128]{2,1,0:T(8,128)(2,1)S(1)}, bf16[12,256,128]{2,1,0:T(8,128)(2,1)S(1)}, u32[]{:S(2)}, u32[]{:S(2)}) collective-permute-start(bf16[12,256,128]{2,1,0:T(8,128)(2,1)S(1)} %get-tuple-element.49), channel_id=1, source_target_pairs={{4,8},{8,4},{5,9},{9,5},{6,10},{10,6},{7,11},{11,7},{20,24},{24,20... | collective-permute-start | bytes 2359304 | tf_op jit(solution)/shard_map/ppermute | solution.py:454
  60.8 6.4 %shard_map.99 = (bf16[64,128,128]{2,1,0:T(8,128)(2,1)}, f32[8,128]{1,0:T(8,128)S(1)}) custom-call(bf16[128,64,128]{2,1,0:T(8,128)(2,1)S(1)} %copy-done.1, bf16[128,64,128]{2,1,0:T(8,128)(2,1)S(1)} %copy-done.1, bf16[128,64,128]{2,1,0:T(8,128)(2,1)S(1)} %copy-done.1, bf16[128,64,128]{2,1,0:T(8,128)(2,1)} %collective-permute-done.core_ref, ...), custom_call_target="tpu_custom_call" | custom-call | flops 1100000 | bytes 1024 | tf_op jit(solution)/shard_map/pallas_call | solution.py:34
  67.2 0.9 shard_map.100
  68.1 2.2 %collective-permute-start.10 = (bf16[4,256,128]{2,1,0:T(8,128)(2,1)S(1)}, bf16[4,256,128]{2,1,0:T(8,128)(2,1)S(1)}, u32[]{:S(2)}, u32[]{:S(2)}) collective-permute-start(bf16[4,256,128]{2,1,0:T(8,128)(2,1)S(1)} %get-tuple-element.48), channel_id=1, source_target_pairs={{4,8},{8,4},{5,9},{9,5},{6,10},{10,6},{7,11},{11,7},{20,24},{24,20... | collective-permute-start | bytes 786440 | tf_op jit(solution)/shard_map/ppermute | solution.py:501
  70.6 1.1 %shard_map.101.begun_ref = f32[2,256,256]{2,1,0:T(8,128)S(1)} custom-call(bf16[25,256,128]{2,1,0:T(8,128)(2,1)S(1)} %get-tuple-element.42.after_ref.all_ref, bf16[12,256,128]{2,1,0:T(8,128)(2,1)S(1)} %collective-permute-done.11.core_ref, bf16[12,256,128]{2,1,0:T(8,128)(2,1)S(1)} %collective-permute-done.12.link_ref, f32[128,128]{1,0:T(8,128)S(1)} %bitcast.10, ...), custom_call_target="tpu_custom_call" | custom-call | flops 1100000 | bytes 1024 | tf_op jit(solution)/shard_map/pallas_call | solution.py:34
  71.8 4.1 %collective-permute-done.10.link_ref = bf16[4,256,128]{2,1,0:T(8,128)(2,1)S(1)} collective-permute-done((bf16[4,256,128]{2,1,0:T(8,128)(2,1)S(1)}, bf16[4,256,128]{2,1,0:T(8,128)(2,1)S(1)}, u32[]{:S(2)}, u32[]{:S(2)}) %collective-permute-start.10) | collective-permute-done | bytes 262176 | tf_op jit(solution)/shard_map/ppermute | solution.py:501
  76.7 14.3 %all_to_all.10.parts_ref = bf16[16,64,128]{2,1,0:T(8,128)(2,1)S(1)} all-to-all(bf16[16,64,128]{2,1,0:T(8,128)(2,1)S(1)} %shard_map.102), channel_id=1, replica_groups=mesh['groups'=2,'domain'=4,'band'=4] {'domain','band'}, dimensions={0} | all-to-all | bytes 524288 | tf_op jit(solution)/shard_map/all_to_all | solution.py:524
  (48 shorter events, 5.0 us)
Async XLA Ops:
  6.0 5.6 %copy-start = (bf16[128,64,128]{2,1,0:T(8,128)(2,1)S(1)}, bf16[128,64,128]{2,1,0:T(8,128)(2,1)}, u32[]{:S(2)}) copy-start(bf16[128,64,128]{2,1,0:T(8,128)(2,1)} %get-tuple-element.27.xt_hbm.xt_ref.last_ref.next_ref) | copy-start | bytes 6291460
  6.0 10.2 %copy-start.11 = (s32[384]{0:T(512)S(1)}, s32[384]{0:T(512)}, u32[]{:S(2)}) copy-start(s32[384]{0:T(512)} %atom_ref.3) | copy-start | bytes 4612
  6.0 10.2 %copy-start.12 = (s32[384]{0:T(512)S(1)}, s32[384]{0:T(512)}, u32[]{:S(2)}) copy-start(s32[384]{0:T(512)} %line_ref.3) | copy-start | bytes 4612
  6.0 49.0 %all-to-all-start = ((bf16[100,64,128]{2,1,0:T(8,128)(2,1)}), bf16[100,64,128]{2,1,0:T(8,128)(2,1)}, u32[]{:S(2)}, u32[]{:S(2)}) async-start(bf16[100,64,128]{2,1,0:T(8,128)(2,1)} %get-tuple-element.37), calls=%async_computation | async-start | bytes 3276800 | tf_op jit(solution)/shard_map/all_to_all | solution.py:394
  11.6 25.2 %collective-permute-start = (bf16[128,64,128]{2,1,0:T(8,128)(2,1)S(1)}, bf16[128,64,128]{2,1,0:T(8,128)(2,1)}, u32[]{:S(2)}, u32[]{:S(2)}) collective-permute-start(bf16[128,64,128]{2,1,0:T(8,128)(2,1)S(1)} %copy-done), channel_id=1, source_target_pairs={{0,4},{4,0},{8,12},{12,8},{1,5},{5,1},{9,13},{13,9},{2,6},{6,2},{1... | collective-permute-start | bytes 6291464 | tf_op jit(solution)/shard_map/ppermute | solution.py:396
  12.5 19.9 %collective-permute-start.1 = (bf16[64,64,128]{2,1,0:T(8,128)(2,1)}, bf16[64,64,128]{2,1,0:T(8,128)(2,1)S(1)}, u32[]{:S(2)}, u32[]{:S(2)}) collective-permute-start(bf16[64,64,128]{2,1,0:T(8,128)(2,1)} %get-tuple-element.28), channel_id=1, source_target_pairs={{4,8},{8,4},{5,9},{9,5},{6,10},{10,6},{7,11},{11,7},{20,24},{24,20... | collective-permute-start | bytes 3145736 | tf_op jit(solution)/shard_map/ppermute | solution.py:395
  16.3 1.6 %copy-start.3 = (bf16[128,64,128]{2,1,0:T(8,128)(2,1)S(1)}, bf16[128,64,128]{2,1,0:T(8,128)(2,1)}, u32[]{:S(2)}) copy-start(bf16[128,64,128]{2,1,0:T(8,128)(2,1)} %copy-done.2) | copy-start | bytes 6291460
  17.9 13.8 %copy-start.14 = (f32[256,16]{0,1:T(8,128)S(1)}, f32[256,16]{0,1:T(8,128)}, u32[]{:S(2)}) copy-start(f32[256,16]{0,1:T(8,128)} %param.14) | copy-start | bytes 49156
  27.9 10.2 %collective-permute-start.5 = (bf16[8,64,128]{2,1,0:T(8,128)(2,1)S(1)}, bf16[8,64,128]{2,1,0:T(8,128)(2,1)}, u32[]{:S(2)}, u32[]{:S(2)}) collective-permute-start(bf16[8,64,128]{2,1,0:T(8,128)(2,1)S(1)} %get-tuple-element.35), channel_id=1, source_target_pairs={{0,8},{4,12},{8,0},{12,4},{1,9},{5,13},{9,1},{13,5},{2,10},{6,14},... | collective-permute-start | bytes 393224 | tf_op jit(solution)/shard_map/ppermute | solution.py:417
  27.9 10.2 %collective-permute-start.3 = (bf16[16,64,128]{2,1,0:T(8,128)(2,1)}, bf16[16,64,128]{2,1,0:T(8,128)(2,1)}, u32[]{:S(2)}, u32[]{:S(2)}) collective-permute-start(bf16[16,64,128]{2,1,0:T(8,128)(2,1)} %get-tuple-element.33), channel_id=1, source_target_pairs={{0,4},{4,0},{8,12},{12,8},{1,5},{5,1},{9,13},{13,9},{2,6},{6,2},{1... | collective-permute-start | bytes 786440 | tf_op jit(solution)/shard_map/ppermute | solution.py:418
  28.9 9.2 %collective-permute-start.4 = (bf16[16,64,128]{2,1,0:T(8,128)(2,1)}, bf16[16,64,128]{2,1,0:T(8,128)(2,1)}, u32[]{:S(2)}, u32[]{:S(2)}) collective-permute-start(bf16[16,64,128]{2,1,0:T(8,128)(2,1)} %get-tuple-element.34), channel_id=1, source_target_pairs={{4,8},{8,4},{5,9},{9,5},{6,10},{10,6},{7,11},{11,7},{20,24},{24,20... | collective-permute-start | bytes 786440 | tf_op jit(solution)/shard_map/ppermute | solution.py:416
  32.5 28.2 %collective-permute-start.2 = (bf16[64,64,128]{2,1,0:T(8,128)(2,1)}, bf16[64,64,128]{2,1,0:T(8,128)(2,1)}, u32[]{:S(2)}, u32[]{:S(2)}) collective-permute-start(bf16[64,64,128]{2,1,0:T(8,128)(2,1)} %get-tuple-element.31), channel_id=1, source_target_pairs={{4,8},{8,4},{5,9},{9,5},{6,10},{10,6},{7,11},{11,7},{20,24},{24,20... | collective-permute-start | bytes 3145736 | tf_op jit(solution)/shard_map/ppermute | solution.py:419
  51.0 16.1 %collective-permute-start.6 = (bf16[10,64,128]{2,1,0:T(8,128)(2,1)}, bf16[10,64,128]{2,1,0:T(8,128)(2,1)S(1)}, u32[]{:S(2)}, u32[]{:S(2)}) collective-permute-start(bf16[10,64,128]{2,1,0:T(8,128)(2,1)} %get-tuple-element.44), channel_id=1, source_target_pairs={{0,1},{1,0},{2,3},{3,2},{4,5},{5,4},{6,7},{7,6},{8,9},{9,8},{10,11... | collective-permute-start | bytes 491528 | tf_op jit(solution)/shard_map/ppermute | solution.py:367
  52.8 14.4 %collective-permute-start.7 = (bf16[10,64,128]{2,1,0:T(8,128)(2,1)}, bf16[10,64,128]{2,1,0:T(8,128)(2,1)S(1)}, u32[]{:S(2)}, u32[]{:S(2)}) collective-permute-start(bf16[10,64,128]{2,1,0:T(8,128)(2,1)} %get-tuple-element.45), channel_id=1, source_target_pairs={{0,2},{1,3},{2,0},{3,1},{4,6},{5,7},{6,4},{7,5},{8,10},{9,11},{10,... | collective-permute-start | bytes 491528 | tf_op jit(solution)/shard_map/ppermute | solution.py:367
  54.9 12.3 %collective-permute-start.8 = (bf16[10,64,128]{2,1,0:T(8,128)(2,1)}, bf16[10,64,128]{2,1,0:T(8,128)(2,1)S(1)}, u32[]{:S(2)}, u32[]{:S(2)}) collective-permute-start(bf16[10,64,128]{2,1,0:T(8,128)(2,1)} %get-tuple-element.46), channel_id=1, source_target_pairs={{0,3},{1,2},{2,1},{3,0},{4,7},{5,6},{6,5},{7,4},{8,11},{9,10},{10,... | collective-permute-start | bytes 491528 | tf_op jit(solution)/shard_map/ppermute | solution.py:367
  55.7 5.1 %copy-start.1 = (bf16[128,64,128]{2,1,0:T(8,128)(2,1)S(1)}, bf16[128,64,128]{2,1,0:T(8,128)(2,1)}, u32[]{:S(2)}) copy-start(bf16[128,64,128]{2,1,0:T(8,128)(2,1)} %get-tuple-element.27.xt_hbm.xt_ref.last_ref.next_ref) | copy-start | bytes 6291460
  55.7 5.1 %copy-start.5 = (bf16[64,64,128]{2,1,0:T(8,128)(2,1)S(1)}, bf16[64,64,128]{2,1,0:T(8,128)(2,1)}, u32[]{:S(2)}) copy-start(bf16[64,64,128]{2,1,0:T(8,128)(2,1)} %copy-done.4) | copy-start | bytes 3145732
  55.7 5.1 %copy-start.8 = (f32[1,128,128]{2,1,0:T(8,128)S(1)}, f32[1,128,128]{2,1,0:T(8,128)}, u32[]{:S(2)}) copy-start(f32[1,128,128]{2,1,0:T(8,128)} %param.9) | copy-start | bytes 196612
  55.7 5.1 %copy-start.10 = (bf16[128,128]{1,0:T(8,128)(2,1)S(1)}, bf16[128,128]{1,0:T(8,128)(2,1)}, u32[]{:S(2)}) copy-start(bf16[128,128]{1,0:T(8,128)(2,1)} %constant.2.clone.ring_ref) | copy-start | bytes 98308
  57.3 13.3 %collective-permute-start.12 = (bf16[12,256,128]{2,1,0:T(8,128)(2,1)S(1)}, bf16[12,256,128]{2,1,0:T(8,128)(2,1)S(1)}, u32[]{:S(2)}, u32[]{:S(2)}) collective-permute-start(bf16[12,256,128]{2,1,0:T(8,128)(2,1)S(1)} %get-tuple-element.49), channel_id=1, source_target_pairs={{4,8},{8,4},{5,9},{9,5},{6,10},{10,6},{7,11},{11,7},{20,24},{24,20... | collective-permute-start | bytes 2359304 | tf_op jit(solution)/shard_map/ppermute | solution.py:454
  60.6 10.0 %collective-permute-start.11 = (bf16[12,256,128]{2,1,0:T(8,128)(2,1)S(1)}, bf16[12,256,128]{2,1,0:T(8,128)(2,1)S(1)}, u32[]{:S(2)}, u32[]{:S(2)}) collective-permute-start(bf16[12,256,128]{2,1,0:T(8,128)(2,1)S(1)} %get-tuple-element.49), channel_id=1, source_target_pairs={{0,4},{4,0},{8,12},{12,8},{1,5},{5,1},{9,13},{13,9},{2,6},{6,2},{1... | collective-permute-start | bytes 2359304 | tf_op jit(solution)/shard_map/ppermute | solution.py:455
  68.1 7.7 %copy-start.9 = (f32[32,128]{1,0:T(8,128)S(1)}, f32[32,128]{1,0:T(8,128)}, u32[]{:S(2)}) copy-start(f32[32,128]{1,0:T(8,128)} %reshape.17.energy_ref) | copy-start | bytes 49156
  68.1 7.7 %collective-permute-start.10 = (bf16[4,256,128]{2,1,0:T(8,128)(2,1)S(1)}, bf16[4,256,128]{2,1,0:T(8,128)(2,1)S(1)}, u32[]{:S(2)}, u32[]{:S(2)}) collective-permute-start(bf16[4,256,128]{2,1,0:T(8,128)(2,1)S(1)} %get-tuple-element.48), channel_id=1, source_target_pairs={{4,8},{8,4},{5,9},{9,5},{6,10},{10,6},{7,11},{11,7},{20,24},{24,20... | collective-permute-start | bytes 786440 | tf_op jit(solution)/shard_map/ppermute | solution.py:501
  70.4 5.4 %collective-permute-start.9 = (bf16[4,256,128]{2,1,0:T(8,128)(2,1)S(1)}, bf16[4,256,128]{2,1,0:T(8,128)(2,1)S(1)}, u32[]{:S(2)}, u32[]{:S(2)}) collective-permute-start(bf16[4,256,128]{2,1,0:T(8,128)(2,1)S(1)} %get-tuple-element.48), channel_id=1, source_target_pairs={{0,4},{4,0},{8,12},{12,8},{1,5},{5,1},{9,13},{13,9},{2,6},{6,2},{1... | collective-permute-start | bytes 786440 | tf_op jit(solution)/shard_map/ppermute | solution.py:502
  (5 other events, 5.0 us)

commit v13 on v11

--- a/solution.py
+++ b/solution.py
@@ -58,10 +58,6 @@
         copy.wait()
 
 
-def hand_on(*refs):
-    pass
-
-
 def pack_kernel(first, x_hbm, xt_hbm, early, late, message, x, xt, in_sems, out_sems):
     states, lines, _ = x.shape
     bands = in_sems.shape[0]
@@ -112,7 +108,7 @@
 
 
 def project_kernel(atom_ref, line_ref, count_ref, xt_hbm, p_hbm, handed, mine_hbm, same, core_ref, link_ref, *refs):
-    far_refs, (total, mine_ref, xt_ref, p_ref, sems, mine_sem) = refs[:-6], refs[-6:]
+    far_refs, (total, mine_ref, xt_ref, p_ref, sems, out_sems) = refs[:-6], refs[-6:]
     slots, proj_count, _ = p_ref.shape
     groups, states = mine_ref.shape[0] // 3, mine_ref.shape[1]
     per_group = LANES // proj_count
@@ -144,35 +140,42 @@
         loads[c].wait()
         lax.fori_loop(c * size // unroll, (c + 1) * size // unroll, body, 0)
 
-    for g in range(3 * groups):
-        tiles = [total[g * per_group + u] for u in range(per_group)]
-        mine_ref[g] = jnp.concatenate(tiles, axis=0).T
-    send = start(pltpu.make_async_copy(mine_ref, mine_hbm, mine_sem))
+    sends = []
+    for part in range(3):
+        for g in range(part * groups, (part + 1) * groups):
+            tiles = [total[g * per_group + u] for u in range(per_group)]
+            mine_ref[g] = jnp.concatenate(tiles, axis=0).T.astype(BF16)
+        where = pl.ds(part * groups, groups)
+        sends.append(start(pltpu.make_async_copy(mine_ref.at[where], mine_hbm.at[where], out_sems.at[part])))
     sides = bases(groups)
     for g in range(groups):
-        own = mine_ref[groups + g].astype(BF16)
+        own = mine_ref[groups + g]
         for side, ref in zip(sides[:2], (core_ref, link_ref)):
-            ref[g] = mine_ref[side + g].astype(BF16)
+            ref[g] = mine_ref[side + g]
             ref[groups + g] = own
         for side, ref in zip(sides[2:], far_refs):
-            ref[g] = mine_ref[side + g].astype(BF16)
-    send.wait()
+            ref[g] = mine_ref[side + g]
+    wait_all(sends)
 
 
 def nonlocal_kernel(
     first, fars, atom_ref, line_ref, count_ref, xt_hbm, p_hbm, energy_ref, mine_hbm, core_ref, link_ref, *refs
 ):
-    far_refs, (_, _, out_hbm, whole_hbm, done_ref, *messages, lines_sum, whole_ref, total, atoms, xt_ref, p_ref, sems) = (
+    far_refs, (_, _, out_hbm, whole_hbm, *messages, lines_sum, whole_ref, mine_ref, total, atoms, p_ref, sems) = (
         refs[:fars],
         refs[fars:],
     )
     slots, proj_count, _ = p_ref.shape
     groups, states = total.shape[0] // 3, total.shape[1]
     per_group = LANES // proj_count
-    lines = xt_ref.shape[0]
+    lines = xt_hbm.shape[0]
     unroll = 16
-    mine_load, *loads = start_all([(mine_hbm, total), (xt_hbm, xt_ref), (p_hbm, p_ref)], sems)
-    done_ref[...] = jnp.zeros_like(done_ref)
+    mine_load, load = start_all([(mine_hbm, mine_ref), (p_hbm, p_ref)], sems)
+    share = lines // (len(messages) + 1)
+    sends = []
+    for k, message in enumerate(messages, 1):
+        where = pl.ds((lax.axis_index("band") ^ k) * share, first)
+        sends.append(start(pltpu.make_async_copy(xt_hbm.at[where], message, sems.at[3 + k])))
 
     def clear(i, carry):
         lines_sum[i] = jnp.zeros((states, LANES), F32)
@@ -180,6 +183,7 @@
 
     lax.fori_loop(0, lines + 1, clear, 0)
     mine_load.wait()
+    total[...] = mine_ref[...].astype(F32)
     sides = bases(groups)
     for g in range(groups):
         total[groups + g] += core_ref[g].astype(F32) + link_ref[g].astype(F32)
@@ -195,16 +199,8 @@
             atoms[g * per_group + u] = tile[:, u * proj_count : (u + 1) * proj_count]
     for g in range(groups):
         whole_ref[g] = total[groups + g].astype(BF16)
-    send_whole = start(pltpu.make_async_copy(whole_ref, whole_hbm, sems.at[3]))
-    wait_all(loads)
-    share = xt_ref.shape[0] // (len(messages) + 1)
-    held = groups // (len(messages) + 1)
-    for k, message in enumerate(messages, 1):
-        to = lax.axis_index("band") ^ k
-        for i in range(first):
-            message[i] = xt_ref[to * share + i]
-        for i in range(held):
-            message[first + i] = whole_ref[to * held + i]
+    sends.append(start(pltpu.make_async_copy(whole_ref, whole_hbm, sems.at[2])))
+    load.wait()
 
     slot_at = slot_reader(atom_ref, line_ref, count_ref, groups * per_group)
 
@@ -217,17 +213,15 @@
         return carry
 
     lax.fori_loop(0, slots // unroll, body, 0)
-    send = start(pltpu.make_async_copy(lines_sum.at[pl.ds(0, lines)], out_hbm, sems.at[4]))
-    send_whole.wait()
-    send.wait()
+    sends.append(start(pltpu.make_async_copy(lines_sum.at[pl.ds(0, lines)], out_hbm, sems.at[3])))
+    wait_all(sends)
 
 
 def stencil_kernel(
-    early_steps, xt_ref, last_ref, next_ref, core_ref, early_link, late_link, added_ref, pot_ref, ring_ref,
-    unread, out_ref, done_ref,
+    early_steps, xt_ref, last_ref, next_ref, core_ref, early_ref, late_ref, added_ref, pot_ref, ring_ref, unread,
+    out_ref,
 ):
     states, here, _ = out_ref.shape
-    done_ref[...] = jnp.zeros_like(done_ref)
     early = pl.program_id(0) < early_steps
 
     def line(i, rows):
@@ -244,10 +238,10 @@
             for i in range(ROWS):
                 y = y0 + i
                 after = line(y + 1, rows).astype(F32)
-                core = core_ref[y, rows, :].astype(F32)
-                link = jnp.where(early, early_link[y, rows, :], late_link[y, rows, :]).astype(F32)
-                value = along[i * ROWS : (i + 1) * ROWS] + pot_ref[y : y + 1, :] * x + added_ref[y, rows, :]
-                results.append(value - 0.5 * ((before + after) + (core + link)))
+                link = jnp.where(early, early_ref[y, rows, :], late_ref[y, rows, :]).astype(F32)
+                beside = (before + after) + (core_ref[y, rows, :].astype(F32) + link)
+                value = along[i * ROWS : (i + 1) * ROWS] + pot_ref[y : y + 1, :] * x
+                results.append(value + added_ref[y, rows, :] - 0.5 * beside)
                 before, x = x, after
             turned = jnp.swapaxes(jnp.stack(results, axis=0), 0, 1).astype(BF16)
             out_ref[rows, y0 : y0 + ROWS, :] = turned
@@ -259,8 +253,7 @@
     copy.wait()
 
 
-def later_kernel(bands, landed, unread, all_ref, pass_hbm, done_ref, sems, pass_sem):
-    done_ref[...] = jnp.zeros_like(done_ref)
+def later_kernel(bands, landed, handed, unread, all_ref, pass_hbm, same, sems, pass_sem):
     count, states = all_ref.shape[0], landed.shape[1]
     loads = [
         start(
@@ -275,28 +268,20 @@
     pass_half(all_ref, pass_hbm, pass_sem)
 
 
-def early_kernel(bands, share, xt_hbm, whole_ref, after_ref, unread, *refs):
-    pieces, (all_ref, pass_hbm, projs_ref, done_ref, sems, pass_sem) = refs[: bands - 1], refs[bands - 1 :]
+def early_kernel(share, xt_hbm, after_ref, *refs):
+    pieces, (all_ref, pass_hbm, done_ref, sems, pass_sem) = refs[:-5], refs[-5:]
     done_ref[...] = jnp.zeros_like(done_ref)
     states = xt_hbm.shape[1]
     band = lax.axis_index("band")
-    count, held = all_ref.shape[0] - 1, projs_ref.shape[0]
-    loads = []
-
-    def load(source, target):
-        loads.append(start(pltpu.make_async_copy(source, target, sems.at[len(loads)])))
-
-    for k in range(bands):
+    count = all_ref.shape[0] - 1
+    pairs = []
+    for k in range(len(pieces) + 1):
         at = pl.ds(pl.multiple_of((band ^ k) * states, states), states)
-        if k == 0:
-            load(xt_hbm.at[pl.ds(band * share, count)], all_ref.at[pl.ds(0, count), at, :])
-            load(whole_ref.at[pl.ds(band * held, held)], projs_ref.at[:, at, :])
-        else:
-            load(pieces[k - 1].at[pl.ds(0, count)], all_ref.at[pl.ds(0, count), at, :])
-            load(pieces[k - 1].at[pl.ds(count, held)], projs_ref.at[:, at, :])
-    load(after_ref.at[pl.ds(0, 1)], all_ref.at[pl.ds(count, 1)])
-    for copy in loads:
-        copy.wait()
+        source = pieces[k - 1] if k else xt_hbm.at[pl.ds(band * share, count)]
+        pairs.append((source, all_ref.at[pl.ds(0, count), at, :]))
+    loads = start_all(pairs, sems)
+    all_ref[count] = after_ref[0]
+    wait_all(loads)
     pass_half(all_ref, pass_hbm, pass_sem)
 
 
@@ -328,14 +313,15 @@
 
 
 def final_kernel(
-    bands, share, all_ref, core_ref, link_ref, pot_ref, begun_ref, proj_ref, energy_ref, out_ref, acc
+    bands, share, all_ref, core_ref, link_ref, pot_ref, begun_ref, shares_ref, energy_ref, out_ref, done_ref, acc
 ):
+    done_ref[...] = jnp.zeros_like(done_ref)
     acc[...] = begun_ref[...]
     add_products(lax.axis_index("band") * share, all_ref, core_ref, link_ref, pot_ref, acc)
-    groups = proj_ref.shape[0]
+    groups = shares_ref.shape[0] // bands
     first = (lax.axis_index("domain") * bands + lax.axis_index("band")) * groups
     for g in range(groups):
-        here = proj_ref[g]
+        here = jnp.concatenate([shares_ref[b * groups + g] for b in range(bands)], axis=0)
         scaled = (here.astype(F32) * energy_ref[pl.ds(first + g, 1), :]).astype(BF16)
         acc[1] += lax.dot_general(scaled, here, NT, preferred_element_type=F32)
     hamil = 0.5 * (acc[1] + acc[1].T)
@@ -364,7 +350,6 @@
     atoms_here = atom_total // domains
     per_group = LANES // proj_count
     groups = atoms_here // per_group
-    group_share = groups // bands
     share = lines // bands
     first = share // 4
     rest = share - first
@@ -372,8 +357,8 @@
     core_pairs = [(i, i ^ 1) for i in range(domains) if i ^ 1 < domains]
     link_pairs = [(i, ((i + 1) ^ 1) - 1) for i in range(1, domains) if ((i + 1) ^ 1) - 1 < domains]
     near_far = [(i, i ^ 2) for i in range(domains) if i ^ 2 < domains]
-    next_far = [(i, ((i + 2) ^ 2) - 2) for i in range(2, domains) if ((i + 2) ^ 2) - 2 < domains]
-    far_pairs = [pairs for pairs in (near_far, next_far) if pairs]
+    next = [(i, ((i + 2) ^ 2) - 2) for i in range(2, domains) if ((i + 2) ^ 2) - 2 < domains]
+    far_pairs = [pairs for pairs in (near_far, next) if pairs]
 
     def swapped(values, axis):
         size = lax.axis_size(axis)
@@ -409,17 +394,6 @@
         (field,),
     )
     landed = lax.all_to_all(message, "band", split_axis=0, concat_axis=0, tiled=True)
-    xt, early_part = call(
-        63,
-        hand_on,
-        (),
-        [UNREAD] * 2,
-        [UNREAD] * 2,
-        [(line_shape, BF16), (early_part.shape, BF16)],
-        [],
-        (xt, early_part),
-        aliases={0: 0, 1: 1},
-    )
     link_early = lax.ppermute(early_part, "domain", link_pairs)
     core_field = lax.ppermute(xt, "domain", core_pairs)
 
@@ -430,107 +404,80 @@
         (),
         [SCALARS] * 3 + [FAR, PINNED, UNREAD],
         [PINNED, UNREAD] + [WHOLE] * (2 + len(far_pairs)),
-        [((3 * groups, states, LANES), F32), (late_shape, BF16)]
+        [((3 * groups, states, LANES), BF16), (late_shape, BF16)]
         + [((2 * groups, states, LANES), BF16)] * 2
         + [(group_shape, BF16)] * len(far_pairs),
         [
             pltpu.VMEM((3 * atoms_here + 1, proj_count, states), F32),
-            pltpu.VMEM((3 * groups, states, LANES), F32),
+            pltpu.VMEM((3 * groups, states, LANES), BF16),
             pltpu.VMEM(line_shape, BF16),
             pltpu.VMEM(projectors.shape, BF16),
             copies((5,)),
-            copies,
+            copies((3,)),
         ],
         (tile_atom, tile_line, tile_count, xt, projectors, late_part),
         aliases={5: 1},
-        micros=10,
     )
     from_link = lax.ppermute(to_link, "domain", link_pairs)
     from_far = [lax.ppermute(value, "domain", pairs) for value, pairs in zip(to_far, far_pairs)]
     from_core = lax.ppermute(to_core, "domain", core_pairs)
     link_late = lax.ppermute(late_part, "domain", link_pairs)
-    added, whole, summed_up, *messages = call(
+    added, whole, *messages = call(
         62,
         functools.partial(nonlocal_kernel, first, len(far_pairs)),
         (),
         [SCALARS] * 3 + [FAR, PINNED, WHOLE, PINNED, WHOLE, WHOLE] + [WHOLE] * len(far_pairs) + [UNREAD] * 2,
-        [PINNED, PINNED, WHOLE] + [WHOLE] * (bands - 1),
-        [(line_shape, F32), (group_shape, BF16), ((8, LANES), F32)]
-        + [((first + group_share, states, cols_z), BF16)] * (bands - 1),
+        [PINNED, FAR] + [FAR] * (bands - 1),
+        [(line_shape, F32), (group_shape, BF16)] + [((first, states, cols_z), BF16)] * (bands - 1),
         [
             pltpu.VMEM((lines + 1, states, cols_z), F32),
             pltpu.VMEM(group_shape, BF16),
+            pltpu.VMEM((3 * groups, states, LANES), BF16),
             pltpu.VMEM((3 * groups, states, LANES), F32),
             pltpu.VMEM((3 * atoms_here, states, proj_count), BF16),
-            pltpu.VMEM(line_shape, BF16),
             pltpu.VMEM(projectors.shape, BF16),
-            copies((5,)),
+            copies((3 + bands,)),
         ],
         (
             tile_atom, tile_line, tile_count, xt, projectors, energy, mine, from_core, from_link, *from_far,
-            link_early[0, :ROWS], core_field[0, :ROWS],
+            link_early, core_field,
         ),
-        micros=30,
     )
     early = swapped(messages, "band")
 
-    later_all, later_pass, later_token = call(
-        32,
+    later_all, later_pass, whole = call(
+        62,
         functools.partial(later_kernel, bands),
         (),
-        [FAR, UNREAD],
-        [NEAR, FAR, WHOLE],
-        [((rest + 1, total_states, cols_z), BF16), ((rest // 2, total_states, cols_z), BF16), ((8, LANES), F32)],
+        [FAR, UNREAD, UNREAD],
+        [NEAR, FAR, UNREAD],
+        [
+            ((rest + 1, total_states, cols_z), BF16),
+            ((rest // 2, total_states, cols_z), BF16),
+            (group_shape, BF16),
+        ],
         [copies((bands,)), copies],
-        (landed, summed_up),
+        (landed, whole, link_late),
+        aliases={1: 2},
+        micros=20,
     )
     later_link = lax.ppermute(later_pass, "domain", link_pairs)
     later_core = lax.ppermute(later_pass, "domain", core_pairs)
-
-    span = 2 * ROWS
-    steps, early_steps = lines // span, (lines - late_lines) // span
-    block = pl.BlockSpec((span, states, cols_z), lambda i: (i, 0, 0))
-    early_block = pl.BlockSpec((span, states, cols_z), lambda i: (jnp.minimum(i, early_steps - 1), 0, 0))
-    late_block = pl.BlockSpec((span, states, cols_z), lambda i: (jnp.maximum(i - early_steps, 0), 0, 0))
-    added_far = pltpu.with_memory_space_constraint(added, pltpu.HBM)
-    applied, done = call(
-        61,
-        functools.partial(stencil_kernel, early_steps),
-        (steps,),
-        [
-            block,
-            pl.BlockSpec((1, states, cols_z), lambda i: (lax.rem(i * span + lines - 1, lines), 0, 0)),
-            pl.BlockSpec((1, states, cols_z), lambda i: (lax.rem(i * span + span, lines), 0, 0)),
-            block,
-            early_block,
-            late_block,
-            block,
-            pl.BlockSpec((span, cols_z), lambda i: (i, 0)),
-            WHOLE,
-            UNREAD,
-        ],
-        [pl.BlockSpec((states, span, cols_z), lambda i: (0, i, 0)), WHOLE],
-        [((states, lines, cols_z), BF16), ((8, LANES), F32)],
-        [],
-        (
-            xt, xt, xt, core_field, link_early, link_late, added_far, pot, ring, later_token,
-        ),
-    )
-
-    early_all, early_pass, projs, early_token = call(
-        60,
-        functools.partial(early_kernel, bands, share),
-        (),
-        [FAR, PINNED, NEAR, WHOLE] + [FAR] * (bands - 1),
-        [NEAR, FAR, NEAR, WHOLE],
+    shares = lax.all_to_all(whole, "band", split_axis=0, concat_axis=0, tiled=True)
+
+    early_all, early_pass, early_token = call(
+        32,
+        functools.partial(early_kernel, share),
+        (),
+        [FAR, NEAR] + [FAR] * (bands - 1),
+        [NEAR, FAR, WHOLE],
         [
             ((first + 1, total_states, cols_z), BF16),
             ((first // 2, total_states, cols_z), BF16),
-            ((group_share, total_states, LANES), BF16),
             ((8, LANES), F32),
         ],
-        [copies((2 * bands + 1,)), copies],
-        (xt, whole, later_all, done, *early),
+        [copies((bands,)), copies],
+        (xt, later_all, *early),
         micros=30,
     )
     early_link = lax.ppermute(early_pass, "domain", link_pairs)
@@ -546,17 +493,45 @@
         (later_all, later_core, later_link, pot, early_token),
     )
     parts = domains * bands
-    (blocks,) = call(
+    blocks, final_token = call(
         32,
         functools.partial(final_kernel, bands, share),
         (),
-        [NEAR, WHOLE, WHOLE, WHOLE, NEAR, NEAR, WHOLE],
-        [WHOLE],
-        [((parts, states, 2 * total_states // domains), BF16)],
+        [NEAR, WHOLE, WHOLE, WHOLE, NEAR, WHOLE, WHOLE],
+        [WHOLE, WHOLE],
+        [((parts, states, 2 * total_states // domains), BF16), ((8, LANES), F32)],
         [pltpu.VMEM((2, total_states, total_states), F32)],
-        (early_all, early_core, early_link, pot, begun, projs, energy),
+        (early_all, early_core, early_link, pot, begun, shares, energy),
     )
     summed = lax.all_to_all(blocks, ("domain", "band"), split_axis=0, concat_axis=0, tiled=True)
+    span = 2 * ROWS
+    steps, early_steps = lines // span, (lines - late_lines) // span
+    block = pl.BlockSpec((span, states, cols_z), lambda i: (i, 0, 0))
+    (applied,) = call(
+        32,
+        functools.partial(stencil_kernel, early_steps),
+        (steps,),
+        [
+            block,
+            pl.BlockSpec((1, states, cols_z), lambda i: (lax.rem(i * span + lines - 1, lines), 0, 0)),
+            pl.BlockSpec((1, states, cols_z), lambda i: (lax.rem(i * span + span, lines), 0, 0)),
+            block,
+            pl.BlockSpec((span, states, cols_z), lambda i: (jnp.minimum(i, early_steps - 1), 0, 0)),
+            pl.BlockSpec((span, states, cols_z), lambda i: (jnp.maximum(i - early_steps, 0), 0, 0)),
+            block,
+            pl.BlockSpec((span, cols_z), lambda i: (i, 0)),
+            WHOLE,
+            UNREAD,
+        ],
+        [pl.BlockSpec((states, span, cols_z), lambda i: (0, i, 0))],
+        [((states, lines, cols_z), BF16)],
+        [],
+        (
+            xt, xt, xt, core_field, link_early, link_late, pltpu.with_memory_space_constraint(added, pltpu.HBM), pot, ring,
+            final_token,
+        ),
+    )
+
     (subspace,) = call(
         32,
         functools.partial(result_kernel, 1.0 / (lines * cols_z * domains)),

time: 95.7 us -> 113 us (1.18)
  waiting for transfers between devices: 2.71 us -> 22.2 us
  blocking collectives: 10.9 us -> 0 us
  starting transfers between devices: 28.8 us -> 38.3 us
  local copies, waits for them, and re-layouts: 6.86 us -> 4.38 us
  Pallas kernels: 43.3 us -> 45.2 us
    ppermute x1, waiting for transfers between devices: 0.01 us -> 13.2 us  [local(): lax.ppermute(value, 'domain', pairs)]
    all_to_all x1 -> x0, blocking collectives: 10.9 us -> none  [local(): lax.all_to_all(blocks, ('domain', 'band'), split_axis=0, concat_axis=0, t...]
    all_to_all x0 -> x2, starting transfers between devices: none -> 9.53 us  [the longest x1 6.19 us: local(): lax.all_to_all(blocks, ('domain', 'band'), split_axis=0, concat_axis=0, t...]
    all_to_all x0 -> x2, waiting for transfers between devices: none -> 4.91 us  [the longest x1 2.55 us: local(): lax.all_to_all(blocks, ('domain', 'band'), split_axis=0, concat_axis=0, t...]
    ppermute x1, waiting for transfers between devices: 0.01 us -> 3.43 us  [local(): from_link = lax.ppermute(to_link, 'domain', link_pairs)]
    ppermute x1, waiting for transfers between devices: 2.68 us -> 0.01 us  [local(): early_link = lax.ppermute(early_pass, 'domain', link_pairs)]
    ppermute x1, starting transfers between devices: 6.77 us -> 4.2 us  [local(): later_link = lax.ppermute(later_pass, 'domain', link_pairs)]
    squeeze x2 -> x0, local copies, waits for them, and re-layouts: 2.53 us -> none  [the longest x1 1.27 us: local(): link_early[0, :ROWS]]
  transfers between devices with their start and end apart: 14 -> 16, of which waited for: 1 -> 6; matrix products, arithmetic and copies ran while one was open for 4% -> 1% of each run, Pallas kernels for 40% -> 34%
where the time goes in v13:
time: 113 us; the launch traced here: 112 us
  Pallas kernels  45.2 us (40%)
  starting transfers between devices  38.3 us (34%)
  waiting for transfers between devices  22.2 us (20%)
  local copies, waits for them, and re-layouts  4.38 us (4%)
  between operations  1.5 us (1%)
    pallas_call x9, Pallas kernels, call(): pl.pallas_call(kernel, grid=grid, out_shape=shapes, in_specs=in_specs, ou...  45.2 us
    ppermute x1, waiting for transfers between devices, local(): lax.ppermute(value, 'domain', pairs)  13.2 us
    all_to_all x1, starting transfers between devices, local(): lax.all_to_all(blocks, ('domain', 'band'), split_axis=0, concat_axis=0, t...  6.19 us
    all_to_all x1, starting transfers between devices, local(): lax.all_to_all(message, 'band', split_axis=0, concat_axis=0, tiled=True)  5.43 us
    ppermute x1, starting transfers between devices, local(): later_link = lax.ppermute(later_pass, 'domain', link_pairs)  4.2 us
    ppermute x3, starting transfers between devices, swapped(): lax.ppermute(values[k - 1], axis, [(i, i ^ k) for i in range(size)])  3.97 us
    unnamed x23, local copies, waits for them, and re-layouts  3.67 us
    ppermute x1, starting transfers between devices, local(): from_link = lax.ppermute(to_link, 'domain', link_pairs)  3.64 us
  transfers between devices with their start and end apart: 16, of which 6 were waited for; matrix products, arithmetic and copies ran while one was open for 1% of the time, Pallas kernels for 34%

profile of v13, /device:TPU:1, one launch (start us, length us, event | category | flops | bytes accessed | tf_op | source)
XLA Modules:
  0.0 111.6 jit_solution(12751877548198437637)
XLA Ops:
  0.6 4.1 %shard_map.95 = (bf16[128,64,128]{2,1,0:T(8,128)(2,1)}, bf16[64,64,128]{2,1,0:T(8,128)(2,1)}, bf16[64,64,128]{2,1,0:T(8,128)(2,1)}, bf16[100,64,128]{2,1,0:T(8,128)(2,1)}) custom-call(bf16[64,128,128]{2,1,0:T(8,128)(2,1)} %bitcast.9), custom_call_target="tpu_custom_call" | custom-call | flops 1100000 | bytes 1024 | tf_op jit(solution)/shard_map/pallas_call | solution.py:34
  4.7 5.4 %all-to-all-start = ((bf16[100,64,128]{2,1,0:T(8,128)(2,1)}), bf16[100,64,128]{2,1,0:T(8,128)(2,1)}, u32[]{:S(2)}, u32[]{:S(2)}) async-start(bf16[100,64,128]{2,1,0:T(8,128)(2,1)} %get-tuple-element.33), calls=%async_computation | async-start | bytes 3276800 | tf_op jit(solution)/shard_map/all_to_all | solution.py:396
  11.1 3.0 %collective-permute-start.1 = (bf16[64,64,128]{2,1,0:T(8,128)(2,1)}, bf16[64,64,128]{2,1,0:T(8,128)(2,1)}, u32[]{:S(2)}, u32[]{:S(2)}) collective-permute-start(bf16[64,64,128]{2,1,0:T(8,128)(2,1)} %get-tuple-element.25), channel_id=1, source_target_pairs={{4,8},{8,4},{5,9},{9,5},{6,10},{10,6},{7,11},{11,7},{20,24},{24,20... | collective-permute-start | bytes 3145736 | tf_op jit(solution)/shard_map/ppermute | solution.py:397
  14.8 10.5 %shard_map.96 = (bf16[24,64,128]{2,1,0:T(8,128)(2,1)}, bf16[64,64,128]{2,1,0:T(8,128)(2,1)}, bf16[16,64,128]{2,1,0:T(8,128)(2,1)}, bf16[16,64,128]{2,1,0:T(8,128)(2,1)}, bf16[8,64,128]{2,1,0:T(8,128)(2,1)}) custom-call(s32[384]{0:T(512)} %atom_ref.3, s32[384]{0:T(512)} %line_ref.3, s32[1]{0:T(128)S(6)} %copy.18.count_ref, ...), custom_call_target="tpu_custom_call", output_to_operand_aliasing={{1}: (5, {})} | custom-call | flops 1100000 | bytes 1024 | tf_op jit(solution)/shard_map/pallas_call | solution.py:34
  25.3 2.5 %collective-permute-start.2 = (bf16[64,64,128]{2,1,0:T(8,128)(2,1)}, bf16[64,64,128]{2,1,0:T(8,128)(2,1)S(1)}, u32[]{:S(2)}, u32[]{:S(2)}) collective-permute-start(bf16[64,64,128]{2,1,0:T(8,128)(2,1)} %get-tuple-element.27), channel_id=1, source_target_pairs={{4,8},{8,4},{5,9},{9,5},{6,10},{10,6},{7,11},{11,7},{20,24},{24,20... | collective-permute-start | bytes 3145736 | tf_op jit(solution)/shard_map/ppermute | solution.py:424
  27.9 1.6 %collective-permute-start.3 = (bf16[16,64,128]{2,1,0:T(8,128)(2,1)}, bf16[16,64,128]{2,1,0:T(8,128)(2,1)S(1)}, u32[]{:S(2)}, u32[]{:S(2)}) collective-permute-start(bf16[16,64,128]{2,1,0:T(8,128)(2,1)} %get-tuple-element.29), channel_id=1, source_target_pairs={{0,4},{4,0},{8,12},{12,8},{1,5},{5,1},{9,13},{13,9},{2,6},{6,2},{1... | collective-permute-start | bytes 786440 | tf_op jit(solution)/shard_map/ppermute | solution.py:423
  29.4 13.2 %collective-permute-done.5.refs_0_ = bf16[8,64,128]{2,1,0:T(8,128)(2,1)S(1)} collective-permute-done((bf16[8,64,128]{2,1,0:T(8,128)(2,1)}, bf16[8,64,128]{2,1,0:T(8,128)(2,1)S(1)}, u32[]{:S(2)}, u32[]{:S(2)}) %collective-permute-start.5) | collective-permute-done | bytes 131104 | tf_op jit(solution)/shard_map/ppermute | solution.py:422
  42.7 3.6 %collective-permute-start.4 = (bf16[16,64,128]{2,1,0:T(8,128)(2,1)}, bf16[16,64,128]{2,1,0:T(8,128)(2,1)S(1)}, u32[]{:S(2)}, u32[]{:S(2)}) collective-permute-start(bf16[16,64,128]{2,1,0:T(8,128)(2,1)} %get-tuple-element.30), channel_id=1, source_target_pairs={{4,8},{8,4},{5,9},{9,5},{6,10},{10,6},{7,11},{11,7},{20,24},{24,20... | collective-permute-start | bytes 786440 | tf_op jit(solution)/shard_map/ppermute | solution.py:421
  47.1 3.4 %collective-permute-done.4.link_ref = bf16[16,64,128]{2,1,0:T(8,128)(2,1)S(1)} collective-permute-done((bf16[16,64,128]{2,1,0:T(8,128)(2,1)}, bf16[16,64,128]{2,1,0:T(8,128)(2,1)S(1)}, u32[]{:S(2)}, u32[]{:S(2)}) %collective-permute-start.4) | collective-permute-done | bytes 262176 | tf_op jit(solution)/shard_map/ppermute | solution.py:421
  51.3 14.2 %shard_map.97 = (f32[128,64,128]{2,1,0:T(8,128)}, bf16[8,64,128]{2,1,0:T(8,128)(2,1)}, bf16[8,64,128]{2,1,0:T(8,128)(2,1)}, bf16[8,64,128]{2,1,0:T(8,128)(2,1)}, bf16[8,64,128]{2,1,0:T(8,128)(2,1)}) custom-call(s32[384]{0:T(512)} %atom_ref.3, s32[384]{0:T(512)} %line_ref.3, s32[1]{0:T(128)S(6)} %copy.18.count_ref, ...), custom_call_target="tpu_custom_call" | custom-call | flops 1100000 | bytes 1024 | tf_op jit(solution)/shard_map/pallas_call | solution.py:34
  65.4 1.8 %collective-permute-start.6 = (bf16[8,64,128]{2,1,0:T(8,128)(2,1)}, bf16[8,64,128]{2,1,0:T(8,128)(2,1)S(1)}, u32[]{:S(2)}, u32[]{:S(2)}) collective-permute-start(bf16[8,64,128]{2,1,0:T(8,128)(2,1)} %get-tuple-element.36), channel_id=1, source_target_pairs={{0,1},{1,0},{2,3},{3,2},{4,5},{5,4},{6,7},{7,6},{8,9},{9,8},{10,11... | collective-permute-start | bytes 393224 | tf_op jit(solution)/shard_map/ppermute | solution.py:365
  67.3 2.1 %collective-permute-start.7 = (bf16[8,64,128]{2,1,0:T(8,128)(2,1)}, bf16[8,64,128]{2,1,0:T(8,128)(2,1)S(1)}, u32[]{:S(2)}, u32[]{:S(2)}) collective-permute-start(bf16[8,64,128]{2,1,0:T(8,128)(2,1)} %get-tuple-element.37), channel_id=1, source_target_pairs={{0,2},{1,3},{2,0},{3,1},{4,6},{5,7},{6,4},{7,5},{8,10},{9,11},{10,... | collective-permute-start | bytes 393224 | tf_op jit(solution)/shard_map/ppermute | solution.py:365
  70.4 2.3 %shard_map.98 = (bf16[25,256,128]{2,1,0:T(8,128)(2,1)S(1)}, bf16[12,256,128]{2,1,0:T(8,128)(2,1)}, bf16[8,64,128]{2,1,0:T(8,128)(2,1)}) custom-call(bf16[100,64,128]{2,1,0:T(8,128)(2,1)} %all-to-all-done.landed, bf16[8,64,128]{2,1,0:T(8,128)(2,1)} %get-tuple-element.34.handed, bf16[64,64,128]{2,1,0:T(8,128)(2,1)} %copy-done), custom_call_target="tpu_custom_call", output_to_operand_aliasing={{2}: (1, {})} | custom-call | flops 22000001024 | bytes 1024 | tf_op jit(solution)/shard_map/pallas_call | solution.py:34
  72.8 4.2 %collective-permute-start.12 = (bf16[12,256,128]{2,1,0:T(8,128)(2,1)}, bf16[12,256,128]{2,1,0:T(8,128)(2,1)}, u32[]{:S(2)}, u32[]{:S(2)}) collective-permute-start(bf16[12,256,128]{2,1,0:T(8,128)(2,1)} %get-tuple-element.41), channel_id=1, source_target_pairs={{4,8},{8,4},{5,9},{9,5},{6,10},{10,6},{7,11},{11,7},{20,24},{24,20... | collective-permute-start | bytes 2359304 | tf_op jit(solution)/shard_map/ppermute | solution.py:464
  77.6 1.7 %shard_map.99 = (bf16[9,256,128]{2,1,0:T(8,128)(2,1)S(1)}, bf16[4,256,128]{2,1,0:T(8,128)(2,1)}, f32[8,128]{1,0:T(8,128)S(1)}) custom-call(bf16[128,64,128]{2,1,0:T(8,128)(2,1)} %get-tuple-element.24.xt_hbm.xt_ref.last_ref.next_ref, bf16[25,256,128]{2,1,0:T(8,128)(2,1)S(1)} %get-tuple-element.35.after_ref.all_ref, ...), custom_call_target="tpu_custom_call" | custom-call | flops 32999999488 | bytes 1024 | tf_op jit(solution)/shard_map/pallas_call | solution.py:34
  80.2 3.3 %collective-permute-start.10 = (bf16[4,256,128]{2,1,0:T(8,128)(2,1)}, bf16[4,256,128]{2,1,0:T(8,128)(2,1)}, u32[]{:S(2)}, u32[]{:S(2)}) collective-permute-start(bf16[4,256,128]{2,1,0:T(8,128)(2,1)} %get-tuple-element.40), channel_id=1, source_target_pairs={{4,8},{8,4},{5,9},{9,5},{6,10},{10,6},{7,11},{11,7},{20,24},{24,20... | collective-permute-start | bytes 786440 | tf_op jit(solution)/shard_map/ppermute | solution.py:483
  83.5 3.3 %all-to-all-start.1 = ((bf16[8,64,128]{2,1,0:T(8,128)(2,1)}), bf16[8,64,128]{2,1,0:T(8,128)(2,1)S(1)}, u32[]{:S(2)}, u32[]{:S(2)}) async-start(bf16[8,64,128]{2,1,0:T(8,128)(2,1)} %get-tuple-element.43), calls=%async_computation.1 | async-start | bytes 262144 | tf_op jit(solution)/shard_map/all_to_all | solution.py:466
  87.0 2.3 %shard_map.100.begun_ref = f32[2,256,256]{2,1,0:T(8,128)S(1)} custom-call(bf16[25,256,128]{2,1,0:T(8,128)(2,1)S(1)} %get-tuple-element.35.after_ref.all_ref, bf16[12,256,128]{2,1,0:T(8,128)(2,1)S(1)} %collective-permute-done.11.core_ref, bf16[12,256,128]{2,1,0:T(8,128)(2,1)} %collective-permute-done.12.link_ref, f32[128,128]{1,0:T(8,128)S(1)} %bitcast.5, ...), custom_call_target="tpu_custom_call" | custom-call | flops 1100000 | bytes 1024 | tf_op jit(solution)/shard_map/pallas_call | solution.py:34
  89.3 2.4 %all-to-all-done.1.shares_ref = bf16[8,64,128]{2,1,0:T(8,128)(2,1)S(1)} async-done(((bf16[8,64,128]{2,1,0:T(8,128)(2,1)}), bf16[8,64,128]{2,1,0:T(8,128)(2,1)S(1)}, u32[]{:S(2)}, u32[]{:S(2)}) %all-to-all-start.1) | async-done | bytes 131104 | tf_op jit(solution)/shard_map/all_to_all | solution.py:466
  91.6 1.1 copy-done.4
  92.7 2.6 %shard_map.101 = (bf16[16,64,128]{2,1,0:T(8,128)(2,1)}, f32[8,128]{1,0:T(8,128)S(1)}) custom-call(bf16[9,256,128]{2,1,0:T(8,128)(2,1)S(1)} %copy-done.4, bf16[4,256,128]{2,1,0:T(8,128)(2,1)} %collective-permute-done.9.core_ref, bf16[4,256,128]{2,1,0:T(8,128)(2,1)} %collective-permute-done.10.link_ref, f32[128,128]{1,0:T(8,128)S(1)} %bitcast.6, ...), custom_call_target="tpu_custom_call" | custom-call | flops 1100000 | bytes 1024 | tf_op jit(solution)/shard_map/pallas_call | solution.py:34
  95.3 6.2 %all-to-all-start.2 = ((bf16[16,64,128]{2,1,0:T(8,128)(2,1)}), bf16[16,64,128]{2,1,0:T(8,128)(2,1)S(1)}, u32[]{:S(2)}, u32[]{:S(2)}) async-start(bf16[16,64,128]{2,1,0:T(8,128)(2,1)} %get-tuple-element.45), calls=%async_computation.2 | async-start | bytes 524288 | tf_op jit(solution)/shard_map/all_to_all | solution.py:506
  101.5 6.8 %shard_map.102 = bf16[64,128,128]{2,1,0:T(8,128)(2,1)} custom-call(bf16[128,64,128]{2,1,0:T(8,128)(2,1)} %get-tuple-element.24.xt_hbm.xt_ref.last_ref.next_ref, bf16[128,64,128]{2,1,0:T(8,128)(2,1)} %get-tuple-element.24.xt_hbm.xt_ref.last_ref.next_ref, bf16[128,64,128]{2,1,0:T(8,128)(2,1)} %get-tuple-element.24.xt_hbm.xt_ref.last_ref.next_ref, ...), custom_call_target="tpu_custom_call" | custom-call | flops 1100000 | bytes 1024 | tf_op jit(solution)/shard_map/pallas_call | solution.py:34
  108.3 2.6 %all-to-all-done.2.parts_ref = bf16[16,64,128]{2,1,0:T(8,128)(2,1)S(1)} async-done(((bf16[16,64,128]{2,1,0:T(8,128)(2,1)}), bf16[16,64,128]{2,1,0:T(8,128)(2,1)S(1)}, u32[]{:S(2)}, u32[]{:S(2)}) %all-to-all-start.2) | async-done | bytes 262176 | tf_op jit(solution)/shard_map/all_to_all | solution.py:506
  (41 shorter events, 6.0 us)
Async XLA Ops:
  4.7 64.7 %all-to-all-start = ((bf16[100,64,128]{2,1,0:T(8,128)(2,1)}), bf16[100,64,128]{2,1,0:T(8,128)(2,1)}, u32[]{:S(2)}, u32[]{:S(2)}) async-start(bf16[100,64,128]{2,1,0:T(8,128)(2,1)} %get-tuple-element.33), calls=%async_computation | async-start | bytes 3276800 | tf_op jit(solution)/shard_map/all_to_all | solution.py:396
  10.2 40.4 %collective-permute-start = (bf16[128,64,128]{2,1,0:T(8,128)(2,1)}, bf16[128,64,128]{2,1,0:T(8,128)(2,1)}, u32[]{:S(2)}, u32[]{:S(2)}) collective-permute-start(bf16[128,64,128]{2,1,0:T(8,128)(2,1)} %get-tuple-element.24.xt_hbm.xt_ref.last_ref.next_ref), channel_id=1, source_target_pairs={{0,4},{4,0},{8,12},{12,8},{1,5},{5,1},{9,13},{13,9},{2,6},{6,2},{1... | collective-permute-start | bytes 6291464 | tf_op jit(solution)/shard_map/ppermute | solution.py:398
  11.1 39.4 %collective-permute-start.1 = (bf16[64,64,128]{2,1,0:T(8,128)(2,1)}, bf16[64,64,128]{2,1,0:T(8,128)(2,1)}, u32[]{:S(2)}, u32[]{:S(2)}) collective-permute-start(bf16[64,64,128]{2,1,0:T(8,128)(2,1)} %get-tuple-element.25), channel_id=1, source_target_pairs={{4,8},{8,4},{5,9},{9,5},{6,10},{10,6},{7,11},{11,7},{20,24},{24,20... | collective-permute-start | bytes 3145736 | tf_op jit(solution)/shard_map/ppermute | solution.py:397
  14.8 31.5 %copy-start.10 = (f32[256,16]{0,1:T(8,128)S(1)}, f32[256,16]{0,1:T(8,128)}, u32[]{:S(2)}) copy-start(f32[256,16]{0,1:T(8,128)} %param.14) | copy-start | bytes 49156
  25.3 44.1 %collective-permute-start.2 = (bf16[64,64,128]{2,1,0:T(8,128)(2,1)}, bf16[64,64,128]{2,1,0:T(8,128)(2,1)S(1)}, u32[]{:S(2)}, u32[]{:S(2)}) collective-permute-start(bf16[64,64,128]{2,1,0:T(8,128)(2,1)} %get-tuple-element.27), channel_id=1, source_target_pairs={{4,8},{8,4},{5,9},{9,5},{6,10},{10,6},{7,11},{11,7},{20,24},{24,20... | collective-permute-start | bytes 3145736 | tf_op jit(solution)/shard_map/ppermute | solution.py:424
  27.8 14.8 %collective-permute-start.5 = (bf16[8,64,128]{2,1,0:T(8,128)(2,1)}, bf16[8,64,128]{2,1,0:T(8,128)(2,1)S(1)}, u32[]{:S(2)}, u32[]{:S(2)}) collective-permute-start(bf16[8,64,128]{2,1,0:T(8,128)(2,1)} %get-tuple-element.31), channel_id=1, source_target_pairs={{0,8},{4,12},{8,0},{12,4},{1,9},{5,13},{9,1},{13,5},{2,10},{6,14},... | collective-permute-start | bytes 393224 | tf_op jit(solution)/shard_map/ppermute | solution.py:422
  27.9 19.2 %collective-permute-start.3 = (bf16[16,64,128]{2,1,0:T(8,128)(2,1)}, bf16[16,64,128]{2,1,0:T(8,128)(2,1)S(1)}, u32[]{:S(2)}, u32[]{:S(2)}) collective-permute-start(bf16[16,64,128]{2,1,0:T(8,128)(2,1)} %get-tuple-element.29), channel_id=1, source_target_pairs={{0,4},{4,0},{8,12},{12,8},{1,5},{5,1},{9,13},{13,9},{2,6},{6,2},{1... | collective-permute-start | bytes 786440 | tf_op jit(solution)/shard_map/ppermute | solution.py:423
  42.6 7.9 %copy-start.9 = (bf16[8,64,128]{2,1,0:T(8,128)(2,1)}, bf16[8,64,128]{2,1,0:T(8,128)(2,1)S(1)}, u32[]{:S(2)}) copy-start(bf16[8,64,128]{2,1,0:T(8,128)(2,1)S(1)} %collective-permute-done.5.refs_0_) | copy-start | bytes 393220
  42.7 7.9 %collective-permute-start.4 = (bf16[16,64,128]{2,1,0:T(8,128)(2,1)}, bf16[16,64,128]{2,1,0:T(8,128)(2,1)S(1)}, u32[]{:S(2)}, u32[]{:S(2)}) collective-permute-start(bf16[16,64,128]{2,1,0:T(8,128)(2,1)} %get-tuple-element.30), channel_id=1, source_target_pairs={{4,8},{8,4},{5,9},{9,5},{6,10},{10,6},{7,11},{11,7},{20,24},{24,20... | collective-permute-start | bytes 786440 | tf_op jit(solution)/shard_map/ppermute | solution.py:421
  47.1 3.5 %copy-start.7 = (bf16[16,64,128]{2,1,0:T(8,128)(2,1)}, bf16[16,64,128]{2,1,0:T(8,128)(2,1)S(1)}, u32[]{:S(2)}) copy-start(bf16[16,64,128]{2,1,0:T(8,128)(2,1)S(1)} %collective-permute-done.3.core_ref) | copy-start | bytes 786436
  65.4 11.6 %collective-permute-start.6 = (bf16[8,64,128]{2,1,0:T(8,128)(2,1)}, bf16[8,64,128]{2,1,0:T(8,128)(2,1)S(1)}, u32[]{:S(2)}, u32[]{:S(2)}) collective-permute-start(bf16[8,64,128]{2,1,0:T(8,128)(2,1)} %get-tuple-element.36), channel_id=1, source_target_pairs={{0,1},{1,0},{2,3},{3,2},{4,5},{5,4},{6,7},{7,6},{8,9},{9,8},{10,11... | collective-permute-start | bytes 393224 | tf_op jit(solution)/shard_map/ppermute | solution.py:365
  67.3 10.3 %collective-permute-start.7 = (bf16[8,64,128]{2,1,0:T(8,128)(2,1)}, bf16[8,64,128]{2,1,0:T(8,128)(2,1)S(1)}, u32[]{:S(2)}, u32[]{:S(2)}) collective-permute-start(bf16[8,64,128]{2,1,0:T(8,128)(2,1)} %get-tuple-element.37), channel_id=1, source_target_pairs={{0,2},{1,3},{2,0},{3,1},{4,6},{5,7},{6,4},{7,5},{8,10},{9,11},{10,... | collective-permute-start | bytes 393224 | tf_op jit(solution)/shard_map/ppermute | solution.py:365
  69.3 8.2 %collective-permute-start.8 = (bf16[8,64,128]{2,1,0:T(8,128)(2,1)}, bf16[8,64,128]{2,1,0:T(8,128)(2,1)}, u32[]{:S(2)}, u32[]{:S(2)}) collective-permute-start(bf16[8,64,128]{2,1,0:T(8,128)(2,1)} %get-tuple-element.38), channel_id=1, source_target_pairs={{0,3},{1,2},{2,1},{3,0},{4,7},{5,6},{6,5},{7,4},{8,11},{9,10},{10,... | collective-permute-start | bytes 393224 | tf_op jit(solution)/shard_map/ppermute | solution.py:365
  72.7 14.1 %collective-permute-start.11 = (bf16[12,256,128]{2,1,0:T(8,128)(2,1)}, bf16[12,256,128]{2,1,0:T(8,128)(2,1)S(1)}, u32[]{:S(2)}, u32[]{:S(2)}) collective-permute-start(bf16[12,256,128]{2,1,0:T(8,128)(2,1)} %get-tuple-element.41), channel_id=1, source_target_pairs={{0,4},{4,0},{8,12},{12,8},{1,5},{5,1},{9,13},{13,9},{2,6},{6,2},{1... | collective-permute-start | bytes 2359304 | tf_op jit(solution)/shard_map/ppermute | solution.py:465
  72.8 14.2 %collective-permute-start.12 = (bf16[12,256,128]{2,1,0:T(8,128)(2,1)}, bf16[12,256,128]{2,1,0:T(8,128)(2,1)}, u32[]{:S(2)}, u32[]{:S(2)}) collective-permute-start(bf16[12,256,128]{2,1,0:T(8,128)(2,1)} %get-tuple-element.41), channel_id=1, source_target_pairs={{4,8},{8,4},{5,9},{9,5},{6,10},{10,6},{7,11},{11,7},{20,24},{24,20... | collective-permute-start | bytes 2359304 | tf_op jit(solution)/shard_map/ppermute | solution.py:464
  77.6 9.4 %copy-start.2 = (f32[1,128,128]{2,1,0:T(8,128)S(1)}, f32[1,128,128]{2,1,0:T(8,128)}, u32[]{:S(2)}) copy-start(f32[1,128,128]{2,1,0:T(8,128)} %param.9) | copy-start | bytes 196612
  80.1 11.5 %copy-start.5 = (f32[32,128]{1,0:T(8,128)S(1)}, f32[32,128]{1,0:T(8,128)}, u32[]{:S(2)}) copy-start(f32[32,128]{1,0:T(8,128)} %reshape.17.energy_ref) | copy-start | bytes 49156
  80.2 11.5 %collective-permute-start.10 = (bf16[4,256,128]{2,1,0:T(8,128)(2,1)}, bf16[4,256,128]{2,1,0:T(8,128)(2,1)}, u32[]{:S(2)}, u32[]{:S(2)}) collective-permute-start(bf16[4,256,128]{2,1,0:T(8,128)(2,1)} %get-tuple-element.40), channel_id=1, source_target_pairs={{4,8},{8,4},{5,9},{9,5},{6,10},{10,6},{7,11},{11,7},{20,24},{24,20... | collective-permute-start | bytes 786440 | tf_op jit(solution)/shard_map/ppermute | solution.py:483
  83.4 8.2 %collective-permute-start.9 = (bf16[4,256,128]{2,1,0:T(8,128)(2,1)}, bf16[4,256,128]{2,1,0:T(8,128)(2,1)}, u32[]{:S(2)}, u32[]{:S(2)}) collective-permute-start(bf16[4,256,128]{2,1,0:T(8,128)(2,1)} %get-tuple-element.40), channel_id=1, source_target_pairs={{0,4},{4,0},{8,12},{12,8},{1,5},{5,1},{9,13},{13,9},{2,6},{6,2},{1... | collective-permute-start | bytes 786440 | tf_op jit(solution)/shard_map/ppermute | solution.py:484
  83.5 8.1 %all-to-all-start.1 = ((bf16[8,64,128]{2,1,0:T(8,128)(2,1)}), bf16[8,64,128]{2,1,0:T(8,128)(2,1)S(1)}, u32[]{:S(2)}, u32[]{:S(2)}) async-start(bf16[8,64,128]{2,1,0:T(8,128)(2,1)} %get-tuple-element.43), calls=%async_computation.1 | async-start | bytes 262144 | tf_op jit(solution)/shard_map/all_to_all | solution.py:466
  87.0 14.5 %copy-start.6 = (bf16[128,128]{1,0:T(8,128)(2,1)S(1)}, bf16[128,128]{1,0:T(8,128)(2,1)}, u32[]{:S(2)}) copy-start(bf16[128,128]{1,0:T(8,128)(2,1)} %constant.2.clone.ring_ref) | copy-start | bytes 98308
  89.3 12.3 %copy-start.1 = (bf16[64,64,128]{2,1,0:T(8,128)(2,1)S(1)}, bf16[64,64,128]{2,1,0:T(8,128)(2,1)}, u32[]{:S(2)}) copy-start(bf16[64,64,128]{2,1,0:T(8,128)(2,1)} %copy-done) | copy-start | bytes 3145732
  91.6 1.1 copy-start.4
  95.3 15.5 %all-to-all-start.2 = ((bf16[16,64,128]{2,1,0:T(8,128)(2,1)}), bf16[16,64,128]{2,1,0:T(8,128)(2,1)S(1)}, u32[]{:S(2)}, u32[]{:S(2)}) async-start(bf16[16,64,128]{2,1,0:T(8,128)(2,1)} %get-tuple-element.45), calls=%async_computation.2 | async-start | bytes 524288 | tf_op jit(solution)/shard_map/all_to_all | solution.py:506
  (3 other events, 2.5 us)

commit v14 on v13

--- a/solution.py
+++ b/solution.py
@@ -58,6 +58,10 @@
         copy.wait()
 
 
+def hand_on(*refs):
+    pass
+
+
 def pack_kernel(first, x_hbm, xt_hbm, early, late, message, x, xt, in_sems, out_sems):
     states, lines, _ = x.shape
     bands = in_sems.shape[0]
@@ -107,7 +111,7 @@
     return slot_at
 
 
-def project_kernel(atom_ref, line_ref, count_ref, xt_hbm, p_hbm, handed, mine_hbm, same, core_ref, link_ref, *refs):
+def project_kernel(atom_ref, line_ref, count_ref, xt_hbm, p_hbm, mine_hbm, core_ref, link_ref, *refs):
     far_refs, (total, mine_ref, xt_ref, p_ref, sems, out_sems) = refs[:-6], refs[-6:]
     slots, proj_count, _ = p_ref.shape
     groups, states = mine_ref.shape[0] // 3, mine_ref.shape[1]
@@ -159,23 +163,18 @@
 
 
 def nonlocal_kernel(
-    first, fars, atom_ref, line_ref, count_ref, xt_hbm, p_hbm, energy_ref, mine_hbm, core_ref, link_ref, *refs
+    lines, fars, atom_ref, line_ref, count_ref, p_hbm, energy_ref, mine_hbm, core_ref, link_ref, *refs
 ):
-    far_refs, (_, _, out_hbm, whole_hbm, *messages, lines_sum, whole_ref, mine_ref, total, atoms, p_ref, sems) = (
+    far_refs, (_, _, out_hbm, whole_hbm, lines_sum, whole_ref, mine_ref, total, atoms, p_ref, sems) = (
         refs[:fars],
         refs[fars:],
     )
     slots, proj_count, _ = p_ref.shape
     groups, states = total.shape[0] // 3, total.shape[1]
     per_group = LANES // proj_count
-    lines = xt_hbm.shape[0]
     unroll = 16
     mine_load, load = start_all([(mine_hbm, mine_ref), (p_hbm, p_ref)], sems)
-    share = lines // (len(messages) + 1)
     sends = []
-    for k, message in enumerate(messages, 1):
-        where = pl.ds((lax.axis_index("band") ^ k) * share, first)
-        sends.append(start(pltpu.make_async_copy(xt_hbm.at[where], message, sems.at[3 + k])))
 
     def clear(i, carry):
         lines_sum[i] = jnp.zeros((states, LANES), F32)
@@ -217,11 +216,51 @@
     wait_all(sends)
 
 
+def second_kernel(share, xt_hbm, core_hbm, early_hbm, late_hbm, whole_hbm, *refs):
+    messages, (built, cores, links, in_sems, out_sems) = refs[:-5], refs[-5:]
+    bands = len(messages)
+    half = cores.shape[1]
+    first = 2 * half
+    held = built.shape[1] - first - half
+    early_lines = early_hbm.shape[0]
+    mine = (lax.axis_index("domain") & 1) * half
+    loads = []
+
+    def load(source, target):
+        loads.append(start(pltpu.make_async_copy(source, target, in_sems.at[len(loads)])))
+
+    for k in range(bands):
+        to = lax.axis_index("band") ^ k
+        begin = to * share
+        load(xt_hbm.at[pl.ds(begin, first)], built.at[k, pl.ds(0, first)])
+        load(whole_hbm.at[pl.ds(to * held, held)], built.at[k, pl.ds(first + half, held)])
+        load(core_hbm.at[pl.ds(begin + mine, half)], cores.at[k])
+        sem = in_sems.at[len(loads)]
+
+        @pl.when(begin < early_lines)
+        def _():
+            pltpu.make_async_copy(early_hbm.at[pl.ds(begin + mine, half)], links.at[k], sem).start()
+
+        @pl.when(begin >= early_lines)
+        def _():
+            pltpu.make_async_copy(late_hbm.at[pl.ds(begin + mine - early_lines, half)], links.at[k], sem).start()
+
+        loads.append(pltpu.make_async_copy(early_hbm.at[pl.ds(0, half)], links.at[k], sem))
+    wait_all(loads)
+    sends = []
+    for k, message in enumerate(messages):
+        for i in range(half):
+            built[k, first + i] = (cores[k, i].astype(F32) + links[k, i].astype(F32)).astype(BF16)
+        sends.append(start(pltpu.make_async_copy(built.at[k], message, out_sems.at[k])))
+    wait_all(sends)
+
+
 def stencil_kernel(
     early_steps, xt_ref, last_ref, next_ref, core_ref, early_ref, late_ref, added_ref, pot_ref, ring_ref, unread,
-    out_ref,
+    out_ref, done_ref,
 ):
     states, here, _ = out_ref.shape
+    done_ref[...] = jnp.zeros_like(done_ref)
     early = pl.program_id(0) < early_steps
 
     def line(i, rows):
@@ -253,7 +292,8 @@
     copy.wait()
 
 
-def later_kernel(bands, landed, handed, unread, all_ref, pass_hbm, same, sems, pass_sem):
+def later_kernel(bands, landed, unread, all_ref, pass_hbm, done_ref, sems, pass_sem):
+    done_ref[...] = jnp.zeros_like(done_ref)
     count, states = all_ref.shape[0], landed.shape[1]
     loads = [
         start(
@@ -268,25 +308,24 @@
     pass_half(all_ref, pass_hbm, pass_sem)
 
 
-def early_kernel(share, xt_hbm, after_ref, *refs):
-    pieces, (all_ref, pass_hbm, done_ref, sems, pass_sem) = refs[:-5], refs[-5:]
+def early_kernel(after_ref, unread, *refs):
+    pieces, (all_ref, beside_ref, projs_ref, done_ref, sems) = refs[:-5], refs[-5:]
     done_ref[...] = jnp.zeros_like(done_ref)
-    states = xt_hbm.shape[1]
-    band = lax.axis_index("band")
-    count = all_ref.shape[0] - 1
+    states = pieces[0].shape[1]
+    count, half, held = all_ref.shape[0] - 1, beside_ref.shape[0], projs_ref.shape[0]
     pairs = []
-    for k in range(len(pieces) + 1):
-        at = pl.ds(pl.multiple_of((band ^ k) * states, states), states)
-        source = pieces[k - 1] if k else xt_hbm.at[pl.ds(band * share, count)]
-        pairs.append((source, all_ref.at[pl.ds(0, count), at, :]))
+    for k, piece in enumerate(pieces):
+        at = pl.ds(pl.multiple_of((lax.axis_index("band") ^ k) * states, states), states)
+        pairs.append((piece.at[pl.ds(0, count)], all_ref.at[pl.ds(0, count), at, :]))
+        pairs.append((piece.at[pl.ds(count, half)], beside_ref.at[:, at, :]))
+        pairs.append((piece.at[pl.ds(count + half, held)], projs_ref.at[:, at, :]))
     loads = start_all(pairs, sems)
     all_ref[count] = after_ref[0]
     wait_all(loads)
-    pass_half(all_ref, pass_hbm, pass_sem)
-
-
-def add_products(row, all_ref, core_ref, link_ref, pot_ref, acc):
-    half = core_ref.shape[0]
+
+
+def add_products(row, all_ref, beside_refs, pot_ref, acc):
+    half = beside_refs[0].shape[0]
     group = 4
     mine = (lax.axis_index("domain") & 1) * half
     for part, base in ((0, mine), (1, half - mine)):
@@ -298,7 +337,8 @@
                 y = (3.0 + pot_ref[pl.ds(row + base + i, 1), :]) * x - pltpu.roll(x, x.shape[1] - 1, 1)
                 y = y - all_ref[base + i + 1].astype(F32)
                 if part == 0:
-                    y = y - core_ref[i].astype(F32) - link_ref[i].astype(F32)
+                    for ref in beside_refs:
+                        y = y - ref[i].astype(F32)
                 xs.append(cell)
                 ys.append(y.astype(BF16))
             flat_x = jnp.concatenate(xs, axis=1)
@@ -309,19 +349,16 @@
 
 def gram_kernel(first, share, all_ref, core_ref, link_ref, pot_ref, unread, acc):
     acc[...] = jnp.zeros_like(acc)
-    add_products(lax.axis_index("band") * share + first, all_ref, core_ref, link_ref, pot_ref, acc)
-
-
-def final_kernel(
-    bands, share, all_ref, core_ref, link_ref, pot_ref, begun_ref, shares_ref, energy_ref, out_ref, done_ref, acc
-):
-    done_ref[...] = jnp.zeros_like(done_ref)
+    add_products(lax.axis_index("band") * share + first, all_ref, (core_ref, link_ref), pot_ref, acc)
+
+
+def final_kernel(bands, share, all_ref, beside_ref, pot_ref, begun_ref, proj_ref, energy_ref, out_ref, acc):
     acc[...] = begun_ref[...]
-    add_products(lax.axis_index("band") * share, all_ref, core_ref, link_ref, pot_ref, acc)
-    groups = shares_ref.shape[0] // bands
+    add_products(lax.axis_index("band") * share, all_ref, (beside_ref,), pot_ref, acc)
+    groups = proj_ref.shape[0]
     first = (lax.axis_index("domain") * bands + lax.axis_index("band")) * groups
     for g in range(groups):
-        here = jnp.concatenate([shares_ref[b * groups + g] for b in range(bands)], axis=0)
+        here = proj_ref[g]
         scaled = (here.astype(F32) * energy_ref[pl.ds(first + g, 1), :]).astype(BF16)
         acc[1] += lax.dot_general(scaled, here, NT, preferred_element_type=F32)
     hamil = 0.5 * (acc[1] + acc[1].T)
@@ -351,7 +388,7 @@
     per_group = LANES // proj_count
     groups = atoms_here // per_group
     share = lines // bands
-    first = share // 4
+    first = 2 * (share * 3 // 32)
     rest = share - first
 
     core_pairs = [(i, i ^ 1) for i in range(domains) if i ^ 1 < domains]
@@ -398,13 +435,13 @@
     core_field = lax.ppermute(xt, "domain", core_pairs)
 
     group_shape = (groups, states, LANES)
-    mine, late_part, to_core, to_link, *to_far = call(
+    mine, to_core, to_link, *to_far = call(
         63,
         project_kernel,
         (),
-        [SCALARS] * 3 + [FAR, PINNED, UNREAD],
-        [PINNED, UNREAD] + [WHOLE] * (2 + len(far_pairs)),
-        [((3 * groups, states, LANES), BF16), (late_shape, BF16)]
+        [SCALARS] * 3 + [FAR, PINNED],
+        [PINNED] + [WHOLE] * (2 + len(far_pairs)),
+        [((3 * groups, states, LANES), BF16)]
         + [((2 * groups, states, LANES), BF16)] * 2
         + [(group_shape, BF16)] * len(far_pairs),
         [
@@ -415,20 +452,30 @@
             copies((5,)),
             copies((3,)),
         ],
-        (tile_atom, tile_line, tile_count, xt, projectors, late_part),
-        aliases={5: 1},
+        (tile_atom, tile_line, tile_count, xt, projectors),
     )
     from_link = lax.ppermute(to_link, "domain", link_pairs)
     from_far = [lax.ppermute(value, "domain", pairs) for value, pairs in zip(to_far, far_pairs)]
     from_core = lax.ppermute(to_core, "domain", core_pairs)
+    (late_part,) = call(
+        63,
+        hand_on,
+        (),
+        [UNREAD] * (3 + len(far_pairs)),
+        [UNREAD],
+        [(late_shape, BF16)],
+        [],
+        (late_part, from_core, from_link, *from_far),
+        aliases={0: 0},
+    )
     link_late = lax.ppermute(late_part, "domain", link_pairs)
-    added, whole, *messages = call(
+    added, whole = call(
         62,
-        functools.partial(nonlocal_kernel, first, len(far_pairs)),
-        (),
-        [SCALARS] * 3 + [FAR, PINNED, WHOLE, PINNED, WHOLE, WHOLE] + [WHOLE] * len(far_pairs) + [UNREAD] * 2,
-        [PINNED, FAR] + [FAR] * (bands - 1),
-        [(line_shape, F32), (group_shape, BF16)] + [((first, states, cols_z), BF16)] * (bands - 1),
+        functools.partial(nonlocal_kernel, lines, len(far_pairs)),
+        (),
+        [SCALARS] * 3 + [PINNED, WHOLE, PINNED, WHOLE, WHOLE] + [WHOLE] * len(far_pairs) + [UNREAD] * 2,
+        [PINNED, PINNED],
+        [(line_shape, F32), (group_shape, BF16)],
         [
             pltpu.VMEM((lines + 1, states, cols_z), F32),
             pltpu.VMEM(group_shape, BF16),
@@ -436,78 +483,50 @@
             pltpu.VMEM((3 * groups, states, LANES), F32),
             pltpu.VMEM((3 * atoms_here, states, proj_count), BF16),
             pltpu.VMEM(projectors.shape, BF16),
-            copies((3 + bands,)),
+            copies((4,)),
         ],
         (
-            tile_atom, tile_line, tile_count, xt, projectors, energy, mine, from_core, from_link, *from_far,
+            tile_atom, tile_line, tile_count, projectors, energy, mine, from_core, from_link, *from_far,
             link_early, core_field,
         ),
     )
+    held = groups // bands
+    built_shape = (first + first // 2 + held, states, cols_z)
+    own_message, *messages = call(
+        62,
+        functools.partial(second_kernel, share),
+        (),
+        [FAR] * 4 + [PINNED],
+        [PINNED] + [FAR] * (bands - 1),
+        [(built_shape, BF16)] * bands,
+        [
+            pltpu.VMEM((bands, *built_shape), BF16),
+            pltpu.VMEM((bands, first // 2, states, cols_z), BF16),
+            pltpu.VMEM((bands, first // 2, states, cols_z), BF16),
+            copies((4 * bands,)),
+            copies((bands,)),
+        ],
+        (xt, core_field, link_early, link_late, whole),
+    )
     early = swapped(messages, "band")
 
-    later_all, later_pass, whole = call(
-        62,
+    later_all, later_pass, later_token = call(
+        32,
         functools.partial(later_kernel, bands),
         (),
-        [FAR, UNREAD, UNREAD],
-        [NEAR, FAR, UNREAD],
-        [
-            ((rest + 1, total_states, cols_z), BF16),
-            ((rest // 2, total_states, cols_z), BF16),
-            (group_shape, BF16),
-        ],
+        [FAR, PINNED],
+        [NEAR, FAR, WHOLE],
+        [((rest + 1, total_states, cols_z), BF16), ((rest // 2, total_states, cols_z), BF16), ((8, LANES), F32)],
         [copies((bands,)), copies],
-        (landed, whole, link_late),
-        aliases={1: 2},
-        micros=20,
+        (landed, own_message),
     )
     later_link = lax.ppermute(later_pass, "domain", link_pairs)
     later_core = lax.ppermute(later_pass, "domain", core_pairs)
-    shares = lax.all_to_all(whole, "band", split_axis=0, concat_axis=0, tiled=True)
-
-    early_all, early_pass, early_token = call(
-        32,
-        functools.partial(early_kernel, share),
-        (),
-        [FAR, NEAR] + [FAR] * (bands - 1),
-        [NEAR, FAR, WHOLE],
-        [
-            ((first + 1, total_states, cols_z), BF16),
-            ((first // 2, total_states, cols_z), BF16),
-            ((8, LANES), F32),
-        ],
-        [copies((bands,)), copies],
-        (xt, later_all, *early),
-        micros=30,
-    )
-    early_link = lax.ppermute(early_pass, "domain", link_pairs)
-    early_core = lax.ppermute(early_pass, "domain", core_pairs)
-    (begun,) = call(
-        32,
-        functools.partial(gram_kernel, first, share),
-        (),
-        [NEAR, WHOLE, WHOLE, WHOLE, UNREAD],
-        [NEAR],
-        [((2, total_states, total_states), F32)],
-        [],
-        (later_all, later_core, later_link, pot, early_token),
-    )
-    parts = domains * bands
-    blocks, final_token = call(
-        32,
-        functools.partial(final_kernel, bands, share),
-        (),
-        [NEAR, WHOLE, WHOLE, WHOLE, NEAR, WHOLE, WHOLE],
-        [WHOLE, WHOLE],
-        [((parts, states, 2 * total_states // domains), BF16), ((8, LANES), F32)],
-        [pltpu.VMEM((2, total_states, total_states), F32)],
-        (early_all, early_core, early_link, pot, begun, shares, energy),
-    )
-    summed = lax.all_to_all(blocks, ("domain", "band"), split_axis=0, concat_axis=0, tiled=True)
+
     span = 2 * ROWS
     steps, early_steps = lines // span, (lines - late_lines) // span
     block = pl.BlockSpec((span, states, cols_z), lambda i: (i, 0, 0))
-    (applied,) = call(
+    applied, done = call(
         32,
         functools.partial(stencil_kernel, early_steps),
         (steps,),
@@ -523,15 +542,53 @@
             WHOLE,
             UNREAD,
         ],
-        [pl.BlockSpec((states, span, cols_z), lambda i: (0, i, 0))],
-        [((states, lines, cols_z), BF16)],
+        [pl.BlockSpec((states, span, cols_z), lambda i: (0, i, 0)), WHOLE],
+        [((states, lines, cols_z), BF16), ((8, LANES), F32)],
         [],
         (
             xt, xt, xt, core_field, link_early, link_late, pltpu.with_memory_space_constraint(added, pltpu.HBM), pot, ring,
-            final_token,
+            later_token,
         ),
     )
 
+    early_all, early_beside, projs, early_token = call(
+        32,
+        early_kernel,
+        (),
+        [NEAR, WHOLE, PINNED] + [FAR] * (bands - 1),
+        [NEAR, NEAR, NEAR, WHOLE],
+        [
+            ((first + 1, total_states, cols_z), BF16),
+            ((first // 2, total_states, cols_z), BF16),
+            ((held, total_states, LANES), BF16),
+            ((8, LANES), F32),
+        ],
+        [copies((3 * bands,))],
+        (later_all, done, own_message, *early),
+        micros=30,
+    )
+    (begun,) = call(
+        32,
+        functools.partial(gram_kernel, first, share),
+        (),
+        [NEAR, WHOLE, WHOLE, WHOLE, UNREAD],
+        [NEAR],
+        [((2, total_states, total_states), F32)],
+        [],
+        (later_all, later_core, later_link, pot, early_token),
+    )
+    parts = domains * bands
+    (blocks,) = call(
+        32,
+        functools.partial(final_kernel, bands, share),
+        (),
+        [NEAR, NEAR, WHOLE, NEAR, NEAR, WHOLE],
+        [WHOLE],
+        [((parts, states, 2 * total_states // domains), BF16)],
+        [pltpu.VMEM((2, total_states, total_states), F32)],
+        (early_all, early_beside, pot, begun, projs, energy),
+    )
+    summed = lax.all_to_all(blocks, ("domain", "band"), split_axis=0, concat_axis=0, tiled=True)
     (subspace,) = call(
         32,
         functools.partial(result_kernel, 1.0 / (lines * cols_z * domains)),

time: 113 us -> 98.8 us (0.87)
  starting transfers between devices: 38.3 us -> 22.4 us
  blocking collectives: 0 us -> 15.7 us
  waiting for transfers between devices: 22.2 us -> 14.7 us
  Pallas kernels: 45.2 us -> 40.4 us
  local copies, waits for them, and re-layouts: 4.38 us -> 2.68 us
    all_to_all x0 -> x1, blocking collectives: none -> 15.7 us  [local(): lax.all_to_all(blocks, ('domain', 'band'), split_axis=0, concat_axis=0, t...]
    all_to_all x2 -> x0, starting transfers between devices: 9.53 us -> none  [the longest x1 6.19 us: local(): lax.all_to_all(blocks, ('domain', 'band'), split_axis=0, concat_axis=0, t...]
    ppermute x1, waiting for transfers between devices: 13.2 us -> 4.27 us  [local(): lax.ppermute(value, 'domain', pairs)]
    ppermute x1, waiting for transfers between devices: 0.01 us -> 8.02 us  [local(): link_early = lax.ppermute(early_part, 'domain', link_pairs)]
    all_to_all x2 -> x0, waiting for transfers between devices: 4.91 us -> none  [the longest x1 2.55 us: local(): lax.all_to_all(blocks, ('domain', 'band'), split_axis=0, concat_axis=0, t...]
    pallas_call x9 -> x11, Pallas kernels: 45.2 us -> 40.4 us  [call(): pl.pallas_call(kernel, grid=grid, out_shape=shapes, in_specs=in_specs, ou...]
    ppermute x1, waiting for transfers between devices: 3.43 us -> 0.01 us  [local(): from_link = lax.ppermute(to_link, 'domain', link_pairs)]
    ppermute x2 -> x0, starting transfers between devices: 3.34 us -> none  [the longest x1 3.27 us: local(): early_link = lax.ppermute(early_pass, 'domain', link_pairs)]
  transfers between devices with their start and end apart: 16 -> 12, of which waited for: 6 -> 3; matrix products, arithmetic and copies ran while one was open for 1% -> 1% of each run, Pallas kernels for 34% -> 34%
where the time goes in v14:
time: 98.8 us; the launch traced here: 97.4 us
  Pallas kernels  40.4 us (41%)
  starting transfers between devices  22.4 us (23%)
  blocking collectives  15.7 us (16%)
  waiting for transfers between devices  14.7 us (15%)
  local copies, waits for them, and re-layouts  2.68 us (3%)
  between operations  1.5 us (2%)
    pallas_call x11, Pallas kernels, call(): pl.pallas_call(kernel, grid=grid, out_shape=shapes, in_specs=in_specs, ou...  40.4 us
    all_to_all x1, blocking collectives, local(): lax.all_to_all(blocks, ('domain', 'band'), split_axis=0, concat_axis=0, t...  15.7 us
    ppermute x1, waiting for transfers between devices, local(): link_early = lax.ppermute(early_part, 'domain', link_pairs)  8.02 us
    all_to_all x1, starting transfers between devices, local(): lax.all_to_all(message, 'band', split_axis=0, concat_axis=0, tiled=True)  5.43 us
    ppermute x1, waiting for transfers between devices, local(): lax.ppermute(value, 'domain', pairs)  4.27 us
    ppermute x3, starting transfers between devices, swapped(): lax.ppermute(values[k - 1], axis, [(i, i ^ k) for i in range(size)])  3.9 us
    ppermute x1, starting transfers between devices, local(): later_link = lax.ppermute(later_pass, 'domain', link_pairs)  3.69 us
    ppermute x1, starting transfers between devices, local(): from_link = lax.ppermute(to_link, 'domain', link_pairs)  3.5 us
  transfers between devices with their start and end apart: 12, of which 3 were waited for; matrix products, arithmetic and copies ran while one was open for 1% of the time, Pallas kernels for 34%

profile of v14, /device:TPU:1, one launch (start us, length us, event | category | flops | bytes accessed | tf_op | source)
XLA Modules:
  0.0 97.4 jit_solution(6383323571454045253)
XLA Ops:
  0.6 4.1 %shard_map.95 = (bf16[128,64,128]{2,1,0:T(8,128)(2,1)}, bf16[64,64,128]{2,1,0:T(8,128)(2,1)}, bf16[64,64,128]{2,1,0:T(8,128)(2,1)}, bf16[108,64,128]{2,1,0:T(8,128)(2,1)}) custom-call(bf16[64,128,128]{2,1,0:T(8,128)(2,1)} %bitcast.8), custom_call_target="tpu_custom_call" | custom-call | flops 1100000 | bytes 1024 | tf_op jit(solution)/shard_map/pallas_call | solution.py:34
  4.7 5.4 %all-to-all-start = ((bf16[108,64,128]{2,1,0:T(8,128)(2,1)}), bf16[108,64,128]{2,1,0:T(8,128)(2,1)}, u32[]{:S(2)}, u32[]{:S(2)}) async-start(bf16[108,64,128]{2,1,0:T(8,128)(2,1)} %get-tuple-element.33), calls=%async_computation | async-start | bytes 3538944 | tf_op jit(solution)/shard_map/all_to_all | solution.py:433
  10.2 1.0 collective-permute-start
  11.8 10.4 %shard_map.96 = (bf16[24,64,128]{2,1,0:T(8,128)(2,1)}, bf16[16,64,128]{2,1,0:T(8,128)(2,1)}, bf16[16,64,128]{2,1,0:T(8,128)(2,1)}, bf16[8,64,128]{2,1,0:T(8,128)(2,1)}) custom-call(s32[384]{0:T(512)} %atom_ref.3, s32[384]{0:T(512)} %line_ref.3, s32[1]{0:T(128)S(6)} %copy.16.count_ref, ...), custom_call_target="tpu_custom_call" | custom-call | flops 1100000 | bytes 1024 | tf_op jit(solution)/shard_map/pallas_call | solution.py:34
  22.3 3.5 %collective-permute-start.3 = (bf16[16,64,128]{2,1,0:T(8,128)(2,1)}, bf16[16,64,128]{2,1,0:T(8,128)(2,1)S(1)}, u32[]{:S(2)}, u32[]{:S(2)}) collective-permute-start(bf16[16,64,128]{2,1,0:T(8,128)(2,1)} %get-tuple-element.29), channel_id=1, source_target_pairs={{4,8},{8,4},{5,9},{9,5},{6,10},{10,6},{7,11},{11,7},{20,24},{24,20... | collective-permute-start | bytes 786440 | tf_op jit(solution)/shard_map/ppermute | solution.py:457
  25.9 2.1 %collective-permute-start.1 = (bf16[64,64,128]{2,1,0:T(8,128)(2,1)}, bf16[64,64,128]{2,1,0:T(8,128)(2,1)}, u32[]{:S(2)}, u32[]{:S(2)}) collective-permute-start(bf16[64,64,128]{2,1,0:T(8,128)(2,1)} %get-tuple-element.26), channel_id=1, source_target_pairs={{4,8},{8,4},{5,9},{9,5},{6,10},{10,6},{7,11},{11,7},{20,24},{24,20... | collective-permute-start | bytes 3145736 | tf_op jit(solution)/shard_map/ppermute | solution.py:434
  28.0 4.3 %collective-permute-done.4.refs_3_.refs_0_ = bf16[8,64,128]{2,1,0:T(8,128)(2,1)S(1)} collective-permute-done((bf16[8,64,128]{2,1,0:T(8,128)(2,1)}, bf16[8,64,128]{2,1,0:T(8,128)(2,1)S(1)}, u32[]{:S(2)}, u32[]{:S(2)}) %collective-permute-start.4) | collective-permute-done | bytes 131104 | tf_op jit(solution)/shard_map/ppermute | solution.py:458
  33.1 2.7 %collective-permute-start.5 = (bf16[64,64,128]{2,1,0:T(8,128)(2,1)}, bf16[64,64,128]{2,1,0:T(8,128)(2,1)S(1)}, u32[]{:S(2)}, u32[]{:S(2)}) collective-permute-start(bf16[64,64,128]{2,1,0:T(8,128)(2,1)} %shard_map.97), channel_id=1, source_target_pairs={{4,8},{8,4},{5,9},{9,5},{6,10},{10,6},{7,11},{11,7},{20,24},{24,20... | collective-permute-start | bytes 3145736 | tf_op jit(solution)/shard_map/ppermute | solution.py:471
  35.9 0.7 reshape.17.energy_ref
  36.7 8.0 %collective-permute-done.1.refs_1_.early_hbm.early_ref = bf16[64,64,128]{2,1,0:T(8,128)(2,1)} collective-permute-done((bf16[64,64,128]{2,1,0:T(8,128)(2,1)}, bf16[64,64,128]{2,1,0:T(8,128)(2,1)}, u32[]{:S(2)}, u32[]{:S(2)}) %collective-permute-start.1) | collective-permute-done | bytes 1048608 | tf_op jit(solution)/shard_map/ppermute | solution.py:434
  44.7 11.3 %shard_map.98 = (f32[128,64,128]{2,1,0:T(8,128)}, bf16[8,64,128]{2,1,0:T(8,128)(2,1)}) custom-call(s32[384]{0:T(512)} %atom_ref.3, s32[384]{0:T(512)} %line_ref.3, s32[1]{0:T(128)S(6)} %copy.16.count_ref, bf16[384,16,128]{2,1,0:T(8,128)(2,1)} %p_hbm.3, f32[32,128]{1,0:T(8,128)} %reshape.17.energy_ref, bf16[24,64,128]{2,1,0:T(8,128)(2,1)} %get-tuple-element.31.mine_hbm, ...), custom_call_target="tpu_custom_call" | custom-call | flops 1100000 | bytes 1024 | tf_op jit(solution)/shard_map/pallas_call | solution.py:34
  56.0 1.0 %copy-done = bf16[64,64,128]{2,1,0:T(8,128)(2,1)} copy-done((bf16[64,64,128]{2,1,0:T(8,128)(2,1)}, bf16[64,64,128]{2,1,0:T(8,128)(2,1)S(1)}, u32[]{:S(2)}) %copy-start) | copy-done | bytes 1048600
  56.9 2.3 %shard_map.99 = (bf16[11,64,128]{2,1,0:T(8,128)(2,1)}, bf16[11,64,128]{2,1,0:T(8,128)(2,1)}, bf16[11,64,128]{2,1,0:T(8,128)(2,1)}, bf16[11,64,128]{2,1,0:T(8,128)(2,1)}) custom-call(bf16[128,64,128]{2,1,0:T(8,128)(2,1)} %get-tuple-element.25.xt_hbm.xt_ref.last_ref.next_ref, bf16[128,64,128]{2,1,0:T(8,128)(2,1)} %collective-permute-done.refs_2_.core_hbm.core_ref, ...), custom_call_target="tpu_custom_call" | custom-call | flops 1100000 | bytes 1024 | tf_op jit(solution)/shard_map/pallas_call | solution.py:34
  59.3 1.7 %collective-permute-start.6 = (bf16[11,64,128]{2,1,0:T(8,128)(2,1)}, bf16[11,64,128]{2,1,0:T(8,128)(2,1)S(1)}, u32[]{:S(2)}, u32[]{:S(2)}) collective-permute-start(bf16[11,64,128]{2,1,0:T(8,128)(2,1)} %get-tuple-element.40), channel_id=1, source_target_pairs={{0,1},{1,0},{2,3},{3,2},{4,5},{5,4},{6,7},{7,6},{8,9},{9,8},{10,11... | collective-permute-start | bytes 540680 | tf_op jit(solution)/shard_map/ppermute | solution.py:402
  61.0 2.2 %collective-permute-start.7 = (bf16[11,64,128]{2,1,0:T(8,128)(2,1)}, bf16[11,64,128]{2,1,0:T(8,128)(2,1)S(1)}, u32[]{:S(2)}, u32[]{:S(2)}) collective-permute-start(bf16[11,64,128]{2,1,0:T(8,128)(2,1)} %get-tuple-element.41), channel_id=1, source_target_pairs={{0,2},{1,3},{2,0},{3,1},{4,6},{5,7},{6,4},{7,5},{8,10},{9,11},{10,... | collective-permute-start | bytes 540680 | tf_op jit(solution)/shard_map/ppermute | solution.py:402
  63.2 1.6 %shard_map.100 = (bf16[27,256,128]{2,1,0:T(8,128)(2,1)S(1)}, bf16[13,256,128]{2,1,0:T(8,128)(2,1)S(1)}, f32[8,128]{1,0:T(8,128)S(1)}) custom-call(bf16[108,64,128]{2,1,0:T(8,128)(2,1)} %all-to-all-done.landed, bf16[11,64,128]{2,1,0:T(8,128)(2,1)} %get-tuple-element.35.unread.refs_0_), custom_call_target="tpu_custom_call" | custom-call | flops 1100000 | bytes 1024 | tf_op jit(solution)/shard_map/pallas_call | solution.py:34
  64.8 3.7 %collective-permute-start.10 = (bf16[13,256,128]{2,1,0:T(8,128)(2,1)S(1)}, bf16[13,256,128]{2,1,0:T(8,128)(2,1)S(1)}, u32[]{:S(2)}, u32[]{:S(2)}) collective-permute-start(bf16[13,256,128]{2,1,0:T(8,128)(2,1)S(1)} %get-tuple-element.45), channel_id=1, source_target_pairs={{4,8},{8,4},{5,9},{9,5},{6,10},{10,6},{7,11},{11,7},{20,24},{24,20... | collective-permute-start | bytes 2555912 | tf_op jit(solution)/shard_map/ppermute | solution.py:523
  68.6 6.8 %shard_map.101 = (bf16[64,128,128]{2,1,0:T(8,128)(2,1)}, f32[8,128]{1,0:T(8,128)S(1)}) custom-call(bf16[128,64,128]{2,1,0:T(8,128)(2,1)} %get-tuple-element.25.xt_hbm.xt_ref.last_ref.next_ref, bf16[128,64,128]{2,1,0:T(8,128)(2,1)} %get-tuple-element.25.xt_hbm.xt_ref.last_ref.next_ref, ...), custom_call_target="tpu_custom_call" | custom-call | flops 1100000 | bytes 1024 | tf_op jit(solution)/shard_map/pallas_call | solution.py:34
  75.4 1.0 %shard_map.102 = (bf16[7,256,128]{2,1,0:T(8,128)(2,1)S(1)}, bf16[3,256,128]{2,1,0:T(8,128)(2,1)S(1)}, bf16[2,256,128]{2,1,0:T(8,128)(2,1)S(1)}, f32[8,128]{1,0:T(8,128)S(1)}) custom-call(bf16[27,256,128]{2,1,0:T(8,128)(2,1)S(1)} %get-tuple-element.38.after_ref.all_ref, f32[8,128]{1,0:T(8,128)S(1)} %get-tuple-element.39.unread, ...), custom_call_target="tpu_custom_call" | custom-call | flops 32999999488 | bytes 1024 | tf_op jit(solution)/shard_map/pallas_call | solution.py:34
  76.4 2.4 %collective-permute-done.10.link_ref = bf16[13,256,128]{2,1,0:T(8,128)(2,1)S(1)} collective-permute-done((bf16[13,256,128]{2,1,0:T(8,128)(2,1)S(1)}, bf16[13,256,128]{2,1,0:T(8,128)(2,1)S(1)}, u32[]{:S(2)}, u32[]{:S(2)}) %collective-permute-start.10) | collective-permute-done | bytes 852000 | tf_op jit(solution)/shard_map/ppermute | solution.py:523
  78.9 1.3 %shard_map.103.begun_ref = f32[2,256,256]{2,1,0:T(8,128)S(1)} custom-call(bf16[27,256,128]{2,1,0:T(8,128)(2,1)S(1)} %get-tuple-element.38.after_ref.all_ref, bf16[13,256,128]{2,1,0:T(8,128)(2,1)S(1)} %collective-permute-done.9.core_ref, bf16[13,256,128]{2,1,0:T(8,128)(2,1)S(1)} %collective-permute-done.10.link_ref, f32[128,128]{1,0:T(8,128)S(1)} %bitcast.6, ...), custom_call_target="tpu_custom_call" | custom-call | flops 1100000 | bytes 1024 | tf_op jit(solution)/shard_map/pallas_call | solution.py:34
  80.1 0.8 shard_map.104
  81.0 15.7 %all_to_all.10.parts_ref = bf16[16,64,128]{2,1,0:T(8,128)(2,1)S(1)} all-to-all(bf16[16,64,128]{2,1,0:T(8,128)(2,1)S(1)} %shard_map.104), channel_id=1, replica_groups=mesh['groups'=2,'domain'=4,'band'=4] {'domain','band'}, dimensions={0} | all-to-all | bytes 524288 | tf_op jit(solution)/shard_map/all_to_all | solution.py:591
  96.7 0.7 shard_map.105
  (32 shorter events, 1.2 us)
Async XLA Ops:
  4.7 58.4 %all-to-all-start = ((bf16[108,64,128]{2,1,0:T(8,128)(2,1)}), bf16[108,64,128]{2,1,0:T(8,128)(2,1)}, u32[]{:S(2)}, u32[]{:S(2)}) async-start(bf16[108,64,128]{2,1,0:T(8,128)(2,1)} %get-tuple-element.33), calls=%async_computation | async-start | bytes 3538944 | tf_op jit(solution)/shard_map/all_to_all | solution.py:433
  10.2 34.5 %collective-permute-start = (bf16[128,64,128]{2,1,0:T(8,128)(2,1)}, bf16[128,64,128]{2,1,0:T(8,128)(2,1)}, u32[]{:S(2)}, u32[]{:S(2)}) collective-permute-start(bf16[128,64,128]{2,1,0:T(8,128)(2,1)} %get-tuple-element.25.xt_hbm.xt_ref.last_ref.next_ref), channel_id=1, source_target_pairs={{0,4},{4,0},{8,12},{12,8},{1,5},{5,1},{9,13},{13,9},{2,6},{6,2},{1... | collective-permute-start | bytes 6291464 | tf_op jit(solution)/shard_map/ppermute | solution.py:435
  22.2 13.6 %copy-start.8 = (f32[256,16]{0,1:T(8,128)S(1)}, f32[256,16]{0,1:T(8,128)}, u32[]{:S(2)}) copy-start(f32[256,16]{0,1:T(8,128)} %param.14) | copy-start | bytes 49156
  22.2 10.0 %collective-permute-start.2 = (bf16[16,64,128]{2,1,0:T(8,128)(2,1)}, bf16[16,64,128]{2,1,0:T(8,128)(2,1)S(1)}, u32[]{:S(2)}, u32[]{:S(2)}) collective-permute-start(bf16[16,64,128]{2,1,0:T(8,128)(2,1)} %get-tuple-element.28), channel_id=1, source_target_pairs={{0,4},{4,0},{8,12},{12,8},{1,5},{5,1},{9,13},{13,9},{2,6},{6,2},{1... | collective-permute-start | bytes 786440 | tf_op jit(solution)/shard_map/ppermute | solution.py:459
  22.3 9.9 %collective-permute-start.3 = (bf16[16,64,128]{2,1,0:T(8,128)(2,1)}, bf16[16,64,128]{2,1,0:T(8,128)(2,1)S(1)}, u32[]{:S(2)}, u32[]{:S(2)}) collective-permute-start(bf16[16,64,128]{2,1,0:T(8,128)(2,1)} %get-tuple-element.29), channel_id=1, source_target_pairs={{4,8},{8,4},{5,9},{9,5},{6,10},{10,6},{7,11},{11,7},{20,24},{24,20... | collective-permute-start | bytes 786440 | tf_op jit(solution)/shard_map/ppermute | solution.py:457
  25.8 6.4 %collective-permute-start.4 = (bf16[8,64,128]{2,1,0:T(8,128)(2,1)}, bf16[8,64,128]{2,1,0:T(8,128)(2,1)S(1)}, u32[]{:S(2)}, u32[]{:S(2)}) collective-permute-start(bf16[8,64,128]{2,1,0:T(8,128)(2,1)} %get-tuple-element.30), channel_id=1, source_target_pairs={{0,8},{4,12},{8,0},{12,4},{1,9},{5,13},{9,1},{13,5},{2,10},{6,14},... | collective-permute-start | bytes 393224 | tf_op jit(solution)/shard_map/ppermute | solution.py:458
  25.9 18.8 %collective-permute-start.1 = (bf16[64,64,128]{2,1,0:T(8,128)(2,1)}, bf16[64,64,128]{2,1,0:T(8,128)(2,1)}, u32[]{:S(2)}, u32[]{:S(2)}) collective-permute-start(bf16[64,64,128]{2,1,0:T(8,128)(2,1)} %get-tuple-element.26), channel_id=1, source_target_pairs={{4,8},{8,4},{5,9},{9,5},{6,10},{10,6},{7,11},{11,7},{20,24},{24,20... | collective-permute-start | bytes 3145736 | tf_op jit(solution)/shard_map/ppermute | solution.py:434
  32.3 0.7 copy-start.7
  32.3 0.8 copy-start.5
  32.3 0.9 copy-start.6
  33.1 22.8 %collective-permute-start.5 = (bf16[64,64,128]{2,1,0:T(8,128)(2,1)}, bf16[64,64,128]{2,1,0:T(8,128)(2,1)S(1)}, u32[]{:S(2)}, u32[]{:S(2)}) collective-permute-start(bf16[64,64,128]{2,1,0:T(8,128)(2,1)} %shard_map.97), channel_id=1, source_target_pairs={{4,8},{8,4},{5,9},{9,5},{6,10},{10,6},{7,11},{11,7},{20,24},{24,20... | collective-permute-start | bytes 3145736 | tf_op jit(solution)/shard_map/ppermute | solution.py:471
  55.9 1.0 %copy-start = (bf16[64,64,128]{2,1,0:T(8,128)(2,1)}, bf16[64,64,128]{2,1,0:T(8,128)(2,1)S(1)}, u32[]{:S(2)}) copy-start(bf16[64,64,128]{2,1,0:T(8,128)(2,1)S(1)} %collective-permute-done.5.late_hbm.late_ref) | copy-start | bytes 3145732
  56.9 11.6 %copy-start.2 = (f32[1,128,128]{2,1,0:T(8,128)S(1)}, f32[1,128,128]{2,1,0:T(8,128)}, u32[]{:S(2)}) copy-start(f32[1,128,128]{2,1,0:T(8,128)} %param.9) | copy-start | bytes 196612
  56.9 11.6 %copy-start.4 = (bf16[128,128]{1,0:T(8,128)(2,1)S(1)}, bf16[128,128]{1,0:T(8,128)(2,1)}, u32[]{:S(2)}) copy-start(bf16[128,128]{1,0:T(8,128)(2,1)} %constant.2.clone.ring_ref) | copy-start | bytes 98308
  59.3 9.3 %copy-start.1 = (bf16[64,64,128]{2,1,0:T(8,128)(2,1)S(1)}, bf16[64,64,128]{2,1,0:T(8,128)(2,1)}, u32[]{:S(2)}) copy-start(bf16[64,64,128]{2,1,0:T(8,128)(2,1)} %copy-done) | copy-start | bytes 3145732
  59.3 16.1 %collective-permute-start.6 = (bf16[11,64,128]{2,1,0:T(8,128)(2,1)}, bf16[11,64,128]{2,1,0:T(8,128)(2,1)S(1)}, u32[]{:S(2)}, u32[]{:S(2)}) collective-permute-start(bf16[11,64,128]{2,1,0:T(8,128)(2,1)} %get-tuple-element.40), channel_id=1, source_target_pairs={{0,1},{1,0},{2,3},{3,2},{4,5},{5,4},{6,7},{7,6},{8,9},{9,8},{10,11... | collective-permute-start | bytes 540680 | tf_op jit(solution)/shard_map/ppermute | solution.py:402
  61.0 14.4 %collective-permute-start.7 = (bf16[11,64,128]{2,1,0:T(8,128)(2,1)}, bf16[11,64,128]{2,1,0:T(8,128)(2,1)S(1)}, u32[]{:S(2)}, u32[]{:S(2)}) collective-permute-start(bf16[11,64,128]{2,1,0:T(8,128)(2,1)} %get-tuple-element.41), channel_id=1, source_target_pairs={{0,2},{1,3},{2,0},{3,1},{4,6},{5,7},{6,4},{7,5},{8,10},{9,11},{10,... | collective-permute-start | bytes 540680 | tf_op jit(solution)/shard_map/ppermute | solution.py:402
  63.2 12.2 %collective-permute-start.8 = (bf16[11,64,128]{2,1,0:T(8,128)(2,1)}, bf16[11,64,128]{2,1,0:T(8,128)(2,1)S(1)}, u32[]{:S(2)}, u32[]{:S(2)}) collective-permute-start(bf16[11,64,128]{2,1,0:T(8,128)(2,1)} %get-tuple-element.42), channel_id=1, source_target_pairs={{0,3},{1,2},{2,1},{3,0},{4,7},{5,6},{6,5},{7,4},{8,11},{9,10},{10,... | collective-permute-start | bytes 540680 | tf_op jit(solution)/shard_map/ppermute | solution.py:402
  64.8 14.1 %collective-permute-start.10 = (bf16[13,256,128]{2,1,0:T(8,128)(2,1)S(1)}, bf16[13,256,128]{2,1,0:T(8,128)(2,1)S(1)}, u32[]{:S(2)}, u32[]{:S(2)}) collective-permute-start(bf16[13,256,128]{2,1,0:T(8,128)(2,1)S(1)} %get-tuple-element.45), channel_id=1, source_target_pairs={{4,8},{8,4},{5,9},{9,5},{6,10},{10,6},{7,11},{11,7},{20,24},{24,20... | collective-permute-start | bytes 2555912 | tf_op jit(solution)/shard_map/ppermute | solution.py:523
  68.5 10.4 %collective-permute-start.9 = (bf16[13,256,128]{2,1,0:T(8,128)(2,1)S(1)}, bf16[13,256,128]{2,1,0:T(8,128)(2,1)S(1)}, u32[]{:S(2)}, u32[]{:S(2)}) collective-permute-start(bf16[13,256,128]{2,1,0:T(8,128)(2,1)S(1)} %get-tuple-element.45), channel_id=1, source_target_pairs={{0,4},{4,0},{8,12},{12,8},{1,5},{5,1},{9,13},{13,9},{2,6},{6,2},{1... | collective-permute-start | bytes 2555912 | tf_op jit(solution)/shard_map/ppermute | solution.py:524
  76.4 3.7 %copy-start.3 = (f32[32,128]{1,0:T(8,128)S(1)}, f32[32,128]{1,0:T(8,128)}, u32[]{:S(2)}) copy-start(f32[32,128]{1,0:T(8,128)} %reshape.17.energy_ref) | copy-start | bytes 49156

commit v15 on v14

--- a/solution.py
+++ b/solution.py
@@ -165,7 +165,7 @@
 def nonlocal_kernel(
     lines, fars, atom_ref, line_ref, count_ref, p_hbm, energy_ref, mine_hbm, core_ref, link_ref, *refs
 ):
-    far_refs, (_, _, out_hbm, whole_hbm, lines_sum, whole_ref, mine_ref, total, atoms, p_ref, sems) = (
+    far_refs, (out_hbm, whole_hbm, lines_sum, whole_ref, mine_ref, total, atoms, p_ref, sems) = (
         refs[:fars],
         refs[fars:],
     )
@@ -461,11 +461,11 @@
         63,
         hand_on,
         (),
-        [UNREAD] * (3 + len(far_pairs)),
+        [UNREAD] * (5 + len(far_pairs)),
         [UNREAD],
         [(late_shape, BF16)],
         [],
-        (late_part, from_core, from_link, *from_far),
+        (late_part, from_core, from_link, *from_far, link_early, core_field),
         aliases={0: 0},
     )
     link_late = lax.ppermute(late_part, "domain", link_pairs)
@@ -473,7 +473,7 @@
         62,
         functools.partial(nonlocal_kernel, lines, len(far_pairs)),
         (),
-        [SCALARS] * 3 + [PINNED, WHOLE, PINNED, WHOLE, WHOLE] + [WHOLE] * len(far_pairs) + [UNREAD] * 2,
+        [SCALARS] * 3 + [PINNED, WHOLE, PINNED, WHOLE, WHOLE] + [WHOLE] * len(far_pairs),
         [PINNED, PINNED],
         [(line_shape, F32), (group_shape, BF16)],
         [
@@ -485,10 +485,7 @@
             pltpu.VMEM(projectors.shape, BF16),
             copies((4,)),
         ],
-        (
-            tile_atom, tile_line, tile_count, projectors, energy, mine, from_core, from_link, *from_far,
-            link_early, core_field,
-        ),
+        (tile_atom, tile_line, tile_count, projectors, energy, mine, from_core, from_link, *from_far),
     )
     held = groups // bands
     built_shape = (first + first // 2 + held, states, cols_z)

time: 98.8 us -> 94.7 us (0.959)
  waiting for transfers between devices: 14.7 us -> 9.36 us
  local copies, waits for them, and re-layouts: 2.68 us -> 4.09 us
    ppermute x1, waiting for transfers between devices: 8.02 us -> 0.01 us  [local(): link_early = lax.ppermute(early_part, 'domain', link_pairs)]
    ppermute x1, waiting for transfers between devices: 4.27 us -> 6.34 us  [local(): lax.ppermute(value, 'domain', pairs)]
    unnamed x19 -> x21, local copies, waits for them, and re-layouts: 1.97 us -> 3.38 us
    ppermute x1, starting transfers between devices: 2.07 us -> 3.33 us  [local(): link_early = lax.ppermute(early_part, 'domain', link_pairs)]
    ppermute x1, starting transfers between devices: 3.5 us -> 2.26 us  [local(): from_link = lax.ppermute(to_link, 'domain', link_pairs)]
    ppermute x1, waiting for transfers between devices: 0.01 us -> 1.19 us  [local(): link_late = lax.ppermute(late_part, 'domain', link_pairs)]
    ppermute x1, waiting for transfers between devices: 2.4 us -> 1.33 us  [local(): later_link = lax.ppermute(later_pass, 'domain', link_pairs)]
  transfers between devices with their start and end apart: 12 -> 12, of which waited for: 3 -> 4; matrix products, arithmetic and copies ran while one was open for 1% -> 1% of each run, Pallas kernels for 34% -> 35%
where the time goes in v15:
time: 94.7 us; the launch traced here: 93.4 us
  Pallas kernels  39.9 us (42%)
  starting transfers between devices  22.9 us (24%)
  blocking collectives  15.7 us (17%)
  waiting for transfers between devices  9.36 us (10%)
  local copies, waits for them, and re-layouts  4.09 us (4%)
  between operations  1.48 us (2%)
    pallas_call x11, Pallas kernels, call(): pl.pallas_call(kernel, grid=grid, out_shape=shapes, in_specs=in_specs, ou...  39.9 us
    all_to_all x1, blocking collectives, local(): lax.all_to_all(blocks, ('domain', 'band'), split_axis=0, concat_axis=0, t...  15.7 us
    ppermute x1, waiting for transfers between devices, local(): lax.ppermute(value, 'domain', pairs)  6.34 us
    all_to_all x1, starting transfers between devices, local(): lax.all_to_all(message, 'band', split_axis=0, concat_axis=0, tiled=True)  6.04 us
    ppermute x1, starting transfers between devices, local(): later_link = lax.ppermute(later_pass, 'domain', link_pairs)  3.76 us
    ppermute x3, starting transfers between devices, swapped(): lax.ppermute(values[k - 1], axis, [(i, i ^ k) for i in range(size)])  3.69 us
    ppermute x1, starting transfers between devices, local(): link_late = lax.ppermute(late_part, 'domain', link_pairs)  3.51 us
    unnamed x21, local copies, waits for them, and re-layouts  3.38 us
  transfers between devices with their start and end apart: 12, of which 4 were waited for; matrix products, arithmetic and copies ran while one was open for 1% of the time, Pallas kernels for 35%

profile of v15, /device:TPU:1, one launch (start us, length us, event | category | flops | bytes accessed | tf_op | source)
XLA Modules:
  0.0 93.4 jit_solution(988925689522549664)
XLA Ops:
  0.6 4.1 %shard_map.95 = (bf16[128,64,128]{2,1,0:T(8,128)(2,1)}, bf16[64,64,128]{2,1,0:T(8,128)(2,1)}, bf16[64,64,128]{2,1,0:T(8,128)(2,1)}, bf16[108,64,128]{2,1,0:T(8,128)(2,1)}) custom-call(bf16[64,128,128]{2,1,0:T(8,128)(2,1)} %bitcast.8), custom_call_target="tpu_custom_call" | custom-call | flops 1100000 | bytes 1024 | tf_op jit(solution)/shard_map/pallas_call | solution.py:34
  4.8 6.0 %all-to-all-start = ((bf16[108,64,128]{2,1,0:T(8,128)(2,1)}), bf16[108,64,128]{2,1,0:T(8,128)(2,1)}, u32[]{:S(2)}, u32[]{:S(2)}) async-start(bf16[108,64,128]{2,1,0:T(8,128)(2,1)} %get-tuple-element.33), calls=%async_computation | async-start | bytes 3538944 | tf_op jit(solution)/shard_map/all_to_all | solution.py:433
  10.9 3.3 %collective-permute-start.1 = (bf16[64,64,128]{2,1,0:T(8,128)(2,1)}, bf16[64,64,128]{2,1,0:T(8,128)(2,1)}, u32[]{:S(2)}, u32[]{:S(2)}) collective-permute-start(bf16[64,64,128]{2,1,0:T(8,128)(2,1)} %get-tuple-element.26), channel_id=1, source_target_pairs={{4,8},{8,4},{5,9},{9,5},{6,10},{10,6},{7,11},{11,7},{20,24},{24,20... | collective-permute-start | bytes 3145736 | tf_op jit(solution)/shard_map/ppermute | solution.py:434
  14.9 10.5 %shard_map.96 = (bf16[24,64,128]{2,1,0:T(8,128)(2,1)}, bf16[16,64,128]{2,1,0:T(8,128)(2,1)}, bf16[16,64,128]{2,1,0:T(8,128)(2,1)}, bf16[8,64,128]{2,1,0:T(8,128)(2,1)}) custom-call(s32[384]{0:T(512)} %atom_ref.3, s32[384]{0:T(512)} %line_ref.3, s32[1]{0:T(128)S(6)} %copy.16.count_ref, ...), custom_call_target="tpu_custom_call" | custom-call | flops 1100000 | bytes 1024 | tf_op jit(solution)/shard_map/pallas_call | solution.py:34
  25.4 2.3 %collective-permute-start.3 = (bf16[16,64,128]{2,1,0:T(8,128)(2,1)}, bf16[16,64,128]{2,1,0:T(8,128)(2,1)S(1)}, u32[]{:S(2)}, u32[]{:S(2)}) collective-permute-start(bf16[16,64,128]{2,1,0:T(8,128)(2,1)} %get-tuple-element.29), channel_id=1, source_target_pairs={{4,8},{8,4},{5,9},{9,5},{6,10},{10,6},{7,11},{11,7},{20,24},{24,20... | collective-permute-start | bytes 786440 | tf_op jit(solution)/shard_map/ppermute | solution.py:457
  27.7 6.3 %collective-permute-done.4.refs_3_.refs_0_ = bf16[8,64,128]{2,1,0:T(8,128)(2,1)S(1)} collective-permute-done((bf16[8,64,128]{2,1,0:T(8,128)(2,1)}, bf16[8,64,128]{2,1,0:T(8,128)(2,1)S(1)}, u32[]{:S(2)}, u32[]{:S(2)}) %collective-permute-start.4) | collective-permute-done | bytes 131104 | tf_op jit(solution)/shard_map/ppermute | solution.py:458
  35.3 3.5 %collective-permute-start.5 = (bf16[64,64,128]{2,1,0:T(8,128)(2,1)}, bf16[64,64,128]{2,1,0:T(8,128)(2,1)S(1)}, u32[]{:S(2)}, u32[]{:S(2)}) collective-permute-start(bf16[64,64,128]{2,1,0:T(8,128)(2,1)} %shard_map.97), channel_id=1, source_target_pairs={{4,8},{8,4},{5,9},{9,5},{6,10},{10,6},{7,11},{11,7},{20,24},{24,20... | collective-permute-start | bytes 3145736 | tf_op jit(solution)/shard_map/ppermute | solution.py:471
  38.9 0.7 reshape.17.energy_ref
  39.6 11.3 %shard_map.98 = (f32[128,64,128]{2,1,0:T(8,128)}, bf16[8,64,128]{2,1,0:T(8,128)(2,1)}) custom-call(s32[384]{0:T(512)} %atom_ref.3, s32[384]{0:T(512)} %line_ref.3, s32[1]{0:T(128)S(6)} %copy.16.count_ref, bf16[384,16,128]{2,1,0:T(8,128)(2,1)} %p_hbm.3, f32[32,128]{1,0:T(8,128)} %reshape.17.energy_ref, bf16[24,64,128]{2,1,0:T(8,128)(2,1)} %get-tuple-element.31.mine_hbm, ...), custom_call_target="tpu_custom_call" | custom-call | flops 1100000 | bytes 1024 | tf_op jit(solution)/shard_map/pallas_call | solution.py:34
  50.9 1.2 %collective-permute-done.5.late_hbm.late_ref = bf16[64,64,128]{2,1,0:T(8,128)(2,1)S(1)} collective-permute-done((bf16[64,64,128]{2,1,0:T(8,128)(2,1)}, bf16[64,64,128]{2,1,0:T(8,128)(2,1)S(1)}, u32[]{:S(2)}, u32[]{:S(2)}) %collective-permute-start.5) | collective-permute-done | bytes 1048608 | tf_op jit(solution)/shard_map/ppermute | solution.py:471
  52.1 1.0 %copy-done.1 = bf16[64,64,128]{2,1,0:T(8,128)(2,1)} copy-done((bf16[64,64,128]{2,1,0:T(8,128)(2,1)}, bf16[64,64,128]{2,1,0:T(8,128)(2,1)S(1)}, u32[]{:S(2)}) %copy-start.1) | copy-done | bytes 1048600
  53.1 2.3 %shard_map.99 = (bf16[11,64,128]{2,1,0:T(8,128)(2,1)}, bf16[11,64,128]{2,1,0:T(8,128)(2,1)}, bf16[11,64,128]{2,1,0:T(8,128)(2,1)}, bf16[11,64,128]{2,1,0:T(8,128)(2,1)}) custom-call(bf16[128,64,128]{2,1,0:T(8,128)(2,1)} %get-tuple-element.25.xt_hbm.xt_ref.last_ref.next_ref, bf16[128,64,128]{2,1,0:T(8,128)(2,1)} %collective-permute-done.refs_5_.core_hbm.core_ref, ...), custom_call_target="tpu_custom_call" | custom-call | flops 1100000 | bytes 1024 | tf_op jit(solution)/shard_map/pallas_call | solution.py:34
  55.4 1.5 %collective-permute-start.6 = (bf16[11,64,128]{2,1,0:T(8,128)(2,1)}, bf16[11,64,128]{2,1,0:T(8,128)(2,1)S(1)}, u32[]{:S(2)}, u32[]{:S(2)}) collective-permute-start(bf16[11,64,128]{2,1,0:T(8,128)(2,1)} %get-tuple-element.40), channel_id=1, source_target_pairs={{0,1},{1,0},{2,3},{3,2},{4,5},{5,4},{6,7},{7,6},{8,9},{9,8},{10,11... | collective-permute-start | bytes 540680 | tf_op jit(solution)/shard_map/ppermute | solution.py:402
  57.0 1.7 %collective-permute-start.7 = (bf16[11,64,128]{2,1,0:T(8,128)(2,1)}, bf16[11,64,128]{2,1,0:T(8,128)(2,1)S(1)}, u32[]{:S(2)}, u32[]{:S(2)}) collective-permute-start(bf16[11,64,128]{2,1,0:T(8,128)(2,1)} %get-tuple-element.41), channel_id=1, source_target_pairs={{0,2},{1,3},{2,0},{3,1},{4,6},{5,7},{6,4},{7,5},{8,10},{9,11},{10,... | collective-permute-start | bytes 540680 | tf_op jit(solution)/shard_map/ppermute | solution.py:402
  59.1 1.6 %shard_map.100 = (bf16[27,256,128]{2,1,0:T(8,128)(2,1)S(1)}, bf16[13,256,128]{2,1,0:T(8,128)(2,1)S(1)}, f32[8,128]{1,0:T(8,128)S(1)}) custom-call(bf16[108,64,128]{2,1,0:T(8,128)(2,1)} %all-to-all-done.landed, bf16[11,64,128]{2,1,0:T(8,128)(2,1)} %get-tuple-element.35.unread.refs_0_), custom_call_target="tpu_custom_call" | custom-call | flops 1100000 | bytes 1024 | tf_op jit(solution)/shard_map/pallas_call | solution.py:34
  60.7 3.8 %collective-permute-start.10 = (bf16[13,256,128]{2,1,0:T(8,128)(2,1)S(1)}, bf16[13,256,128]{2,1,0:T(8,128)(2,1)S(1)}, u32[]{:S(2)}, u32[]{:S(2)}) collective-permute-start(bf16[13,256,128]{2,1,0:T(8,128)(2,1)S(1)} %get-tuple-element.45), channel_id=1, source_target_pairs={{4,8},{8,4},{5,9},{9,5},{6,10},{10,6},{7,11},{11,7},{20,24},{24,20... | collective-permute-start | bytes 2555912 | tf_op jit(solution)/shard_map/ppermute | solution.py:520
  64.6 1.6 %copy-done = bf16[128,64,128]{2,1,0:T(8,128)(2,1)S(1)} copy-done((bf16[128,64,128]{2,1,0:T(8,128)(2,1)S(1)}, bf16[128,64,128]{2,1,0:T(8,128)(2,1)}, u32[]{:S(2)}) %copy-start) | copy-done | bytes 2097176
  66.2 6.3 %shard_map.101 = (bf16[64,128,128]{2,1,0:T(8,128)(2,1)}, f32[8,128]{1,0:T(8,128)S(1)}) custom-call(bf16[128,64,128]{2,1,0:T(8,128)(2,1)S(1)} %copy-done, bf16[128,64,128]{2,1,0:T(8,128)(2,1)S(1)} %copy-done, bf16[128,64,128]{2,1,0:T(8,128)(2,1)S(1)} %copy-done, bf16[128,64,128]{2,1,0:T(8,128)(2,1)} %collective-permute-done.refs_5_.core_hbm.core_ref, ...), custom_call_target="tpu_custom_call" | custom-call | flops 1100000 | bytes 1024 | tf_op jit(solution)/shard_map/pallas_call | solution.py:34
  72.5 1.0 %shard_map.102 = (bf16[7,256,128]{2,1,0:T(8,128)(2,1)S(1)}, bf16[3,256,128]{2,1,0:T(8,128)(2,1)S(1)}, bf16[2,256,128]{2,1,0:T(8,128)(2,1)S(1)}, f32[8,128]{1,0:T(8,128)S(1)}) custom-call(bf16[27,256,128]{2,1,0:T(8,128)(2,1)S(1)} %get-tuple-element.38.after_ref.all_ref, f32[8,128]{1,0:T(8,128)S(1)} %get-tuple-element.39.unread, ...), custom_call_target="tpu_custom_call" | custom-call | flops 32999999488 | bytes 1024 | tf_op jit(solution)/shard_map/pallas_call | solution.py:34
  73.5 1.3 %collective-permute-done.10.link_ref = bf16[13,256,128]{2,1,0:T(8,128)(2,1)S(1)} collective-permute-done((bf16[13,256,128]{2,1,0:T(8,128)(2,1)S(1)}, bf16[13,256,128]{2,1,0:T(8,128)(2,1)S(1)}, u32[]{:S(2)}, u32[]{:S(2)}) %collective-permute-start.10) | collective-permute-done | bytes 852000 | tf_op jit(solution)/shard_map/ppermute | solution.py:520
  74.9 1.3 %shard_map.103.begun_ref = f32[2,256,256]{2,1,0:T(8,128)S(1)} custom-call(bf16[27,256,128]{2,1,0:T(8,128)(2,1)S(1)} %get-tuple-element.38.after_ref.all_ref, bf16[13,256,128]{2,1,0:T(8,128)(2,1)S(1)} %collective-permute-done.9.core_ref, bf16[13,256,128]{2,1,0:T(8,128)(2,1)S(1)} %collective-permute-done.10.link_ref, f32[128,128]{1,0:T(8,128)S(1)} %bitcast.6, ...), custom_call_target="tpu_custom_call" | custom-call | flops 1100000 | bytes 1024 | tf_op jit(solution)/shard_map/pallas_call | solution.py:34
  76.1 0.8 shard_map.104
  77.0 15.7 %all_to_all.10.parts_ref = bf16[16,64,128]{2,1,0:T(8,128)(2,1)S(1)} all-to-all(bf16[16,64,128]{2,1,0:T(8,128)(2,1)S(1)} %shard_map.104), channel_id=1, replica_groups=mesh['groups'=2,'domain'=4,'band'=4] {'domain','band'}, dimensions={0} | all-to-all | bytes 524288 | tf_op jit(solution)/shard_map/all_to_all | solution.py:588
  92.6 0.7 shard_map.105
  (34 shorter events, 2.1 us)
Async XLA Ops:
  4.7 29.9 %collective-permute-start = (bf16[128,64,128]{2,1,0:T(8,128)(2,1)}, bf16[128,64,128]{2,1,0:T(8,128)(2,1)}, u32[]{:S(2)}, u32[]{:S(2)}) collective-permute-start(bf16[128,64,128]{2,1,0:T(8,128)(2,1)} %get-tuple-element.25.xt_hbm.xt_ref.last_ref.next_ref), channel_id=1, source_target_pairs={{0,4},{4,0},{8,12},{12,8},{1,5},{5,1},{9,13},{13,9},{2,6},{6,2},{1... | collective-permute-start | bytes 6291464 | tf_op jit(solution)/shard_map/ppermute | solution.py:435
  4.8 54.3 %all-to-all-start = ((bf16[108,64,128]{2,1,0:T(8,128)(2,1)}), bf16[108,64,128]{2,1,0:T(8,128)(2,1)}, u32[]{:S(2)}, u32[]{:S(2)}) async-start(bf16[108,64,128]{2,1,0:T(8,128)(2,1)} %get-tuple-element.33), calls=%async_computation | async-start | bytes 3538944 | tf_op jit(solution)/shard_map/all_to_all | solution.py:433
  10.9 23.7 %collective-permute-start.1 = (bf16[64,64,128]{2,1,0:T(8,128)(2,1)}, bf16[64,64,128]{2,1,0:T(8,128)(2,1)}, u32[]{:S(2)}, u32[]{:S(2)}) collective-permute-start(bf16[64,64,128]{2,1,0:T(8,128)(2,1)} %get-tuple-element.26), channel_id=1, source_target_pairs={{4,8},{8,4},{5,9},{9,5},{6,10},{10,6},{7,11},{11,7},{20,24},{24,20... | collective-permute-start | bytes 3145736 | tf_op jit(solution)/shard_map/ppermute | solution.py:434
  25.3 8.8 %collective-permute-start.2 = (bf16[16,64,128]{2,1,0:T(8,128)(2,1)}, bf16[16,64,128]{2,1,0:T(8,128)(2,1)S(1)}, u32[]{:S(2)}, u32[]{:S(2)}) collective-permute-start(bf16[16,64,128]{2,1,0:T(8,128)(2,1)} %get-tuple-element.28), channel_id=1, source_target_pairs={{0,4},{4,0},{8,12},{12,8},{1,5},{5,1},{9,13},{13,9},{2,6},{6,2},{1... | collective-permute-start | bytes 786440 | tf_op jit(solution)/shard_map/ppermute | solution.py:459
  25.4 9.2 %collective-permute-start.3 = (bf16[16,64,128]{2,1,0:T(8,128)(2,1)}, bf16[16,64,128]{2,1,0:T(8,128)(2,1)S(1)}, u32[]{:S(2)}, u32[]{:S(2)}) collective-permute-start(bf16[16,64,128]{2,1,0:T(8,128)(2,1)} %get-tuple-element.29), channel_id=1, source_target_pairs={{4,8},{8,4},{5,9},{9,5},{6,10},{10,6},{7,11},{11,7},{20,24},{24,20... | collective-permute-start | bytes 786440 | tf_op jit(solution)/shard_map/ppermute | solution.py:457
  27.7 6.4 %collective-permute-start.4 = (bf16[8,64,128]{2,1,0:T(8,128)(2,1)}, bf16[8,64,128]{2,1,0:T(8,128)(2,1)S(1)}, u32[]{:S(2)}, u32[]{:S(2)}) collective-permute-start(bf16[8,64,128]{2,1,0:T(8,128)(2,1)} %get-tuple-element.30), channel_id=1, source_target_pairs={{0,8},{4,12},{8,0},{12,4},{1,9},{5,13},{9,1},{13,5},{2,10},{6,14},... | collective-permute-start | bytes 393224 | tf_op jit(solution)/shard_map/ppermute | solution.py:458
  34.1 0.6 copy-start.8
  34.1 0.8 copy-start.6
  34.6 0.7 copy-start.7
  35.3 3.5 %copy-start.9 = (f32[256,16]{0,1:T(8,128)S(1)}, f32[256,16]{0,1:T(8,128)}, u32[]{:S(2)}) copy-start(f32[256,16]{0,1:T(8,128)} %param.14) | copy-start | bytes 49156
  35.3 16.8 %collective-permute-start.5 = (bf16[64,64,128]{2,1,0:T(8,128)(2,1)}, bf16[64,64,128]{2,1,0:T(8,128)(2,1)S(1)}, u32[]{:S(2)}, u32[]{:S(2)}) collective-permute-start(bf16[64,64,128]{2,1,0:T(8,128)(2,1)} %shard_map.97), channel_id=1, source_target_pairs={{4,8},{8,4},{5,9},{9,5},{6,10},{10,6},{7,11},{11,7},{20,24},{24,20... | collective-permute-start | bytes 3145736 | tf_op jit(solution)/shard_map/ppermute | solution.py:471
  52.1 1.0 %copy-start.1 = (bf16[64,64,128]{2,1,0:T(8,128)(2,1)}, bf16[64,64,128]{2,1,0:T(8,128)(2,1)S(1)}, u32[]{:S(2)}) copy-start(bf16[64,64,128]{2,1,0:T(8,128)(2,1)S(1)} %collective-permute-done.5.late_hbm.late_ref) | copy-start | bytes 3145732
  53.1 11.5 %copy-start.3 = (f32[1,128,128]{2,1,0:T(8,128)S(1)}, f32[1,128,128]{2,1,0:T(8,128)}, u32[]{:S(2)}) copy-start(f32[1,128,128]{2,1,0:T(8,128)} %param.9) | copy-start | bytes 196612
  53.1 11.5 %copy-start.5 = (bf16[128,128]{1,0:T(8,128)(2,1)S(1)}, bf16[128,128]{1,0:T(8,128)(2,1)}, u32[]{:S(2)}) copy-start(bf16[128,128]{1,0:T(8,128)(2,1)} %constant.2.clone.ring_ref) | copy-start | bytes 98308
  55.4 9.2 %copy-start.2 = (bf16[64,64,128]{2,1,0:T(8,128)(2,1)S(1)}, bf16[64,64,128]{2,1,0:T(8,128)(2,1)}, u32[]{:S(2)}) copy-start(bf16[64,64,128]{2,1,0:T(8,128)(2,1)} %copy-done.1) | copy-start | bytes 3145732
  55.4 17.0 %collective-permute-start.6 = (bf16[11,64,128]{2,1,0:T(8,128)(2,1)}, bf16[11,64,128]{2,1,0:T(8,128)(2,1)S(1)}, u32[]{:S(2)}, u32[]{:S(2)}) collective-permute-start(bf16[11,64,128]{2,1,0:T(8,128)(2,1)} %get-tuple-element.40), channel_id=1, source_target_pairs={{0,1},{1,0},{2,3},{3,2},{4,5},{5,4},{6,7},{7,6},{8,9},{9,8},{10,11... | collective-permute-start | bytes 540680 | tf_op jit(solution)/shard_map/ppermute | solution.py:402
  57.0 15.5 %collective-permute-start.7 = (bf16[11,64,128]{2,1,0:T(8,128)(2,1)}, bf16[11,64,128]{2,1,0:T(8,128)(2,1)S(1)}, u32[]{:S(2)}, u32[]{:S(2)}) collective-permute-start(bf16[11,64,128]{2,1,0:T(8,128)(2,1)} %get-tuple-element.41), channel_id=1, source_target_pairs={{0,2},{1,3},{2,0},{3,1},{4,6},{5,7},{6,4},{7,5},{8,10},{9,11},{10,... | collective-permute-start | bytes 540680 | tf_op jit(solution)/shard_map/ppermute | solution.py:402
  58.7 13.8 %collective-permute-start.8 = (bf16[11,64,128]{2,1,0:T(8,128)(2,1)}, bf16[11,64,128]{2,1,0:T(8,128)(2,1)S(1)}, u32[]{:S(2)}, u32[]{:S(2)}) collective-permute-start(bf16[11,64,128]{2,1,0:T(8,128)(2,1)} %get-tuple-element.42), channel_id=1, source_target_pairs={{0,3},{1,2},{2,1},{3,0},{4,7},{5,6},{6,5},{7,4},{8,11},{9,10},{10,... | collective-permute-start | bytes 540680 | tf_op jit(solution)/shard_map/ppermute | solution.py:402
  60.7 14.1 %collective-permute-start.10 = (bf16[13,256,128]{2,1,0:T(8,128)(2,1)S(1)}, bf16[13,256,128]{2,1,0:T(8,128)(2,1)S(1)}, u32[]{:S(2)}, u32[]{:S(2)}) collective-permute-start(bf16[13,256,128]{2,1,0:T(8,128)(2,1)S(1)} %get-tuple-element.45), channel_id=1, source_target_pairs={{4,8},{8,4},{5,9},{9,5},{6,10},{10,6},{7,11},{11,7},{20,24},{24,20... | collective-permute-start | bytes 2555912 | tf_op jit(solution)/shard_map/ppermute | solution.py:520
  64.5 10.4 %collective-permute-start.9 = (bf16[13,256,128]{2,1,0:T(8,128)(2,1)S(1)}, bf16[13,256,128]{2,1,0:T(8,128)(2,1)S(1)}, u32[]{:S(2)}, u32[]{:S(2)}) collective-permute-start(bf16[13,256,128]{2,1,0:T(8,128)(2,1)S(1)} %get-tuple-element.45), channel_id=1, source_target_pairs={{0,4},{4,0},{8,12},{12,8},{1,5},{5,1},{9,13},{13,9},{2,6},{6,2},{1... | collective-permute-start | bytes 2555912 | tf_op jit(solution)/shard_map/ppermute | solution.py:521
  64.6 1.6 %copy-start = (bf16[128,64,128]{2,1,0:T(8,128)(2,1)S(1)}, bf16[128,64,128]{2,1,0:T(8,128)(2,1)}, u32[]{:S(2)}) copy-start(bf16[128,64,128]{2,1,0:T(8,128)(2,1)} %get-tuple-element.25.xt_hbm.xt_ref.last_ref.next_ref) | copy-start | bytes 6291460
  73.5 2.6 %copy-start.4 = (f32[32,128]{1,0:T(8,128)S(1)}, f32[32,128]{1,0:T(8,128)}, u32[]{:S(2)}) copy-start(f32[32,128]{1,0:T(8,128)} %reshape.17.energy_ref) | copy-start | bytes 49156

commit v16 on v15

--- a/solution.py
+++ b/solution.py
@@ -111,8 +111,21 @@
     return slot_at
 
 
-def project_kernel(atom_ref, line_ref, count_ref, xt_hbm, p_hbm, mine_hbm, core_ref, link_ref, *refs):
-    far_refs, (total, mine_ref, xt_ref, p_ref, sems, out_sems) = refs[:-6], refs[-6:]
+def energy_table(energy_ref):
+    proj_count, atoms = energy_ref.shape
+    per_group = LANES // proj_count
+    lane = lax.broadcasted_iota(jnp.int32, (proj_count, LANES), 1)
+    row = lax.broadcasted_iota(jnp.int32, (proj_count, LANES), 0)
+    pick = jnp.where(lane % proj_count == row, 1.0, 0.0).astype(F32)
+    spread = jnp.dot(energy_ref[...].T, pick, precision=lax.Precision.HIGHEST, preferred_element_type=F32)
+    spread = spread.reshape(atoms // per_group, per_group, LANES)
+    lane = lax.broadcasted_iota(jnp.int32, spread.shape, 2)
+    atom = lax.broadcasted_iota(jnp.int32, spread.shape, 1)
+    return jnp.sum(jnp.where(lane // proj_count == atom, spread, 0.0), axis=1)
+
+
+def project_kernel(atom_ref, line_ref, count_ref, xt_hbm, p_hbm, mine_hbm, core_hbm, link_hbm, *refs):
+    far_hbms, (total, mine_ref, xt_ref, p_ref, sems, out_sems) = refs[:-6], refs[-6:]
     slots, proj_count, _ = p_ref.shape
     groups, states = mine_ref.shape[0] // 3, mine_ref.shape[1]
     per_group = LANES // proj_count
@@ -144,28 +157,23 @@
         loads[c].wait()
         lax.fori_loop(c * size // unroll, (c + 1) * size // unroll, body, 0)
 
-    sends = []
-    for part in range(3):
-        for g in range(part * groups, (part + 1) * groups):
-            tiles = [total[g * per_group + u] for u in range(per_group)]
-            mine_ref[g] = jnp.concatenate(tiles, axis=0).T.astype(BF16)
-        where = pl.ds(part * groups, groups)
-        sends.append(start(pltpu.make_async_copy(mine_ref.at[where], mine_hbm.at[where], out_sems.at[part])))
+    for g in range(3 * groups):
+        tiles = [total[g * per_group + u] for u in range(per_group)]
+        mine_ref[g] = jnp.concatenate(tiles, axis=0).T.astype(BF16)
     sides = bases(groups)
-    for g in range(groups):
-        own = mine_ref[groups + g]
-        for side, ref in zip(sides[:2], (core_ref, link_ref)):
-            ref[g] = mine_ref[side + g]
-            ref[groups + g] = own
-        for side, ref in zip(sides[2:], far_refs):
-            ref[g] = mine_ref[side + g]
-    wait_all(sends)
+    pairs = [(mine_ref, mine_hbm)]
+    for side, far in zip(sides[:2], (core_hbm, link_hbm)):
+        pairs.append((mine_ref.at[pl.ds(side, groups)], far.at[pl.ds(0, groups)]))
+        pairs.append((mine_ref.at[pl.ds(groups, groups)], far.at[pl.ds(groups, groups)]))
+    for side, far in zip(sides[2:], far_hbms):
+        pairs.append((mine_ref.at[pl.ds(side, groups)], far))
+    wait_all(start_all(pairs, out_sems))
 
 
 def nonlocal_kernel(
     lines, fars, atom_ref, line_ref, count_ref, p_hbm, energy_ref, mine_hbm, core_ref, link_ref, *refs
 ):
-    far_refs, (out_hbm, whole_hbm, lines_sum, whole_ref, mine_ref, total, atoms, p_ref, sems) = (
+    far_refs, (out_hbm, whole_hbm, lines_sum, whole_ref, mine_ref, total, table, atoms, p_ref, sems) = (
         refs[:fars],
         refs[fars:],
     )
@@ -190,10 +198,11 @@
             total[side + g] += ref[groups + g].astype(F32)
         for side, ref in zip(sides[2:], far_refs):
             total[side + g] += ref[g].astype(F32)
-    last = energy_ref.shape[0] - 1
+    table[...] = energy_table(energy_ref)
+    last = table.shape[0] - 1
     for g in range(3 * groups):
         row = jnp.clip((lax.axis_index("domain") - 1) * groups + g, 0, last)
-        tile = (total[g] * energy_ref[pl.ds(row, 1), :]).astype(BF16)
+        tile = (total[g] * table[pl.ds(row, 1), :]).astype(BF16)
         for u in range(per_group):
             atoms[g * per_group + u] = tile[:, u * proj_count : (u + 1) * proj_count]
     for g in range(groups):
@@ -257,10 +266,9 @@
 
 def stencil_kernel(
     early_steps, xt_ref, last_ref, next_ref, core_ref, early_ref, late_ref, added_ref, pot_ref, ring_ref, unread,
-    out_ref, done_ref,
+    out_ref, token,
 ):
     states, here, _ = out_ref.shape
-    done_ref[...] = jnp.zeros_like(done_ref)
     early = pl.program_id(0) < early_steps
 
     def line(i, rows):
@@ -292,8 +300,7 @@
     copy.wait()
 
 
-def later_kernel(bands, landed, unread, all_ref, pass_hbm, done_ref, sems, pass_sem):
-    done_ref[...] = jnp.zeros_like(done_ref)
+def later_kernel(bands, landed, unread, all_ref, pass_hbm, token, sems, pass_sem):
     count, states = all_ref.shape[0], landed.shape[1]
     loads = [
         start(
@@ -308,9 +315,8 @@
     pass_half(all_ref, pass_hbm, pass_sem)
 
 
-def early_kernel(after_ref, unread, *refs):
-    pieces, (all_ref, beside_ref, projs_ref, done_ref, sems) = refs[:-5], refs[-5:]
-    done_ref[...] = jnp.zeros_like(done_ref)
+def early_kernel(after_ref, energy_ref, unread, *refs):
+    pieces, (all_ref, beside_ref, projs_ref, table_ref, token, sems) = refs[:-6], refs[-6:]
     states = pieces[0].shape[1]
     count, half, held = all_ref.shape[0] - 1, beside_ref.shape[0], projs_ref.shape[0]
     pairs = []
@@ -321,6 +327,7 @@
         pairs.append((piece.at[pl.ds(count + half, held)], projs_ref.at[:, at, :]))
     loads = start_all(pairs, sems)
     all_ref[count] = after_ref[0]
+    table_ref[...] = energy_table(energy_ref)
     wait_all(loads)
 
 
@@ -404,7 +411,9 @@
 
     field = orbitals.reshape(states, lines, cols_z)
     pot = potential.reshape(lines, cols_z)
-    energy = energies.reshape(atom_total // per_group, LANES)
+    energy = energies.T
+    energy_rows = (atom_total // per_group, LANES)
+    token = ((8, LANES), F32)
     eye = np.eye(cols_z, dtype=np.float32)
     ring = jnp.asarray(3.0 * eye - 0.5 * (np.roll(eye, 1, axis=0) + np.roll(eye, -1, axis=0)), dtype=BF16)
 
@@ -440,7 +449,7 @@
         project_kernel,
         (),
         [SCALARS] * 3 + [FAR, PINNED],
-        [PINNED] + [WHOLE] * (2 + len(far_pairs)),
+        [PINNED] + [FAR] * (2 + len(far_pairs)),
         [((3 * groups, states, LANES), BF16)]
         + [((2 * groups, states, LANES), BF16)] * 2
         + [(group_shape, BF16)] * len(far_pairs),
@@ -450,7 +459,7 @@
             pltpu.VMEM(line_shape, BF16),
             pltpu.VMEM(projectors.shape, BF16),
             copies((5,)),
-            copies((3,)),
+            copies((5 + len(far_pairs),)),
         ],
         (tile_atom, tile_line, tile_count, xt, projectors),
     )
@@ -481,6 +490,7 @@
             pltpu.VMEM(group_shape, BF16),
             pltpu.VMEM((3 * groups, states, LANES), BF16),
             pltpu.VMEM((3 * groups, states, LANES), F32),
+            pltpu.VMEM(energy_rows, F32),
             pltpu.VMEM((3 * atoms_here, states, proj_count), BF16),
             pltpu.VMEM(projectors.shape, BF16),
             copies((4,)),
@@ -490,7 +500,7 @@
     held = groups // bands
     built_shape = (first + first // 2 + held, states, cols_z)
     own_message, *messages = call(
-        62,
+        63,
         functools.partial(second_kernel, share),
         (),
         [FAR] * 4 + [PINNED],
@@ -512,8 +522,8 @@
         functools.partial(later_kernel, bands),
         (),
         [FAR, PINNED],
-        [NEAR, FAR, WHOLE],
-        [((rest + 1, total_states, cols_z), BF16), ((rest // 2, total_states, cols_z), BF16), ((8, LANES), F32)],
+        [NEAR, FAR, PINNED],
+        [((rest + 1, total_states, cols_z), BF16), ((rest // 2, total_states, cols_z), BF16), token],
         [copies((bands,)), copies],
         (landed, own_message),
     )
@@ -524,7 +534,7 @@
     steps, early_steps = lines // span, (lines - late_lines) // span
     block = pl.BlockSpec((span, states, cols_z), lambda i: (i, 0, 0))
     applied, done = call(
-        32,
+        62,
         functools.partial(stencil_kernel, early_steps),
         (steps,),
         [
@@ -537,10 +547,10 @@
             block,
             pl.BlockSpec((span, cols_z), lambda i: (i, 0)),
             WHOLE,
-            UNREAD,
+            PINNED,
         ],
-        [pl.BlockSpec((states, span, cols_z), lambda i: (0, i, 0)), WHOLE],
-        [((states, lines, cols_z), BF16), ((8, LANES), F32)],
+        [pl.BlockSpec((states, span, cols_z), lambda i: (0, i, 0)), PINNED],
+        [((states, lines, cols_z), BF16), token],
         [],
         (
             xt, xt, xt, core_field, link_early, link_late, pltpu.with_memory_space_constraint(added, pltpu.HBM), pot, ring,
@@ -548,27 +558,28 @@
         ),
     )
 
-    early_all, early_beside, projs, early_token = call(
+    early_all, early_beside, projs, energy_table_here, early_token = call(
         32,
         early_kernel,
         (),
-        [NEAR, WHOLE, PINNED] + [FAR] * (bands - 1),
-        [NEAR, NEAR, NEAR, WHOLE],
+        [NEAR, WHOLE, PINNED, PINNED] + [FAR] * (bands - 1),
+        [NEAR, NEAR, NEAR, NEAR, PINNED],
         [
             ((first + 1, total_states, cols_z), BF16),
             ((first // 2, total_states, cols_z), BF16),
             ((held, total_states, LANES), BF16),
-            ((8, LANES), F32),
+            (energy_rows, F32),
+            token,
         ],
         [copies((3 * bands,))],
-        (later_all, done, own_message, *early),
+        (later_all, energy, done, own_message, *early),
         micros=30,
     )
     (begun,) = call(
         32,
         functools.partial(gram_kernel, first, share),
         (),
-        [NEAR, WHOLE, WHOLE, WHOLE, UNREAD],
+        [NEAR, WHOLE, WHOLE, WHOLE, PINNED],
         [NEAR],
         [((2, total_states, total_states), F32)],
         [],
@@ -579,11 +590,11 @@
         32,
         functools.partial(final_kernel, bands, share),
         (),
-        [NEAR, NEAR, WHOLE, NEAR, NEAR, WHOLE],
+        [NEAR, NEAR, WHOLE, NEAR, NEAR, NEAR],
         [WHOLE],
         [((parts, states, 2 * total_states // domains), BF16)],
         [pltpu.VMEM((2, total_states, total_states), F32)],
-        (early_all, early_beside, pot, begun, projs, energy),
+        (early_all, early_beside, pot, begun, projs, energy_table_here),
     )
     summed = lax.all_to_all(blocks, ("domain", "band"), split_axis=0, concat_axis=0, tiled=True)
     (subspace,) = call(

time: 94.7 us -> 95.7 us (1.011)
  local copies, waits for them, and re-layouts: 4.09 us -> 0.72 us
  Pallas kernels: 39.9 us -> 43.1 us
  waiting for transfers between devices: 9.36 us -> 10.5 us
    pallas_call x11, Pallas kernels: 39.9 us -> 43.1 us  [call(): pl.pallas_call(kernel, grid=grid, out_shape=shapes, in_specs=in_specs, ou...]
    unnamed x21 -> x10, local copies, waits for them, and re-layouts: 3.38 us -> 0.72 us
  transfers between devices with their start and end apart: 12 -> 12, of which waited for: 4 -> 4; matrix products, arithmetic and copies ran while one was open for 1% -> 0% of each run, Pallas kernels for 35% -> 37%
where the time goes in v16:
time: 95.7 us; the launch traced here: 94.4 us
  Pallas kernels  43.1 us (45%)
  starting transfers between devices  22.9 us (24%)
  blocking collectives  15.7 us (16%)
  waiting for transfers between devices  10.5 us (11%)
  between operations  1.45 us (2%)
    pallas_call x11, Pallas kernels, call(): pl.pallas_call(kernel, grid=grid, out_shape=shapes, in_specs=in_specs, ou...  43.1 us
    all_to_all x1, blocking collectives, local(): lax.all_to_all(blocks, ('domain', 'band'), split_axis=0, concat_axis=0, t...  15.7 us
    ppermute x1, waiting for transfers between devices, local(): lax.ppermute(value, 'domain', pairs)  6.34 us
    all_to_all x1, starting transfers between devices, local(): lax.all_to_all(message, 'band', split_axis=0, concat_axis=0, tiled=True)  6.04 us
    ppermute x3, starting transfers between devices, swapped(): lax.ppermute(values[k - 1], axis, [(i, i ^ k) for i in range(size)])  3.79 us
    ppermute x1, starting transfers between devices, local(): later_link = lax.ppermute(later_pass, 'domain', link_pairs)  3.76 us
    ppermute x1, starting transfers between devices, local(): link_late = lax.ppermute(late_part, 'domain', link_pairs)  3.38 us
    ppermute x1, starting transfers between devices, local(): link_early = lax.ppermute(early_part, 'domain', link_pairs)  3.33 us
  transfers between devices with their start and end apart: 12, of which 4 were waited for; matrix products, arithmetic and copies ran while one was open for 0% of the time, Pallas kernels for 37%

profile of v16, /device:TPU:1, one launch (start us, length us, event | category | flops | bytes accessed | tf_op | source)
XLA Modules:
  0.0 94.4 jit_solution(1391688855730475820)
XLA Ops:
  0.6 4.1 %shard_map.95 = (bf16[128,64,128]{2,1,0:T(8,128)(2,1)}, bf16[64,64,128]{2,1,0:T(8,128)(2,1)}, bf16[64,64,128]{2,1,0:T(8,128)(2,1)}, bf16[108,64,128]{2,1,0:T(8,128)(2,1)}) custom-call(bf16[64,128,128]{2,1,0:T(8,128)(2,1)} %bitcast.11), custom_call_target="tpu_custom_call" | custom-call | flops 1100000 | bytes 1024 | tf_op jit(solution)/shard_map/pallas_call | solution.py:34
  4.9 6.0 %all-to-all-start = ((bf16[108,64,128]{2,1,0:T(8,128)(2,1)}), bf16[108,64,128]{2,1,0:T(8,128)(2,1)}, u32[]{:S(2)}, u32[]{:S(2)}) async-start(bf16[108,64,128]{2,1,0:T(8,128)(2,1)} %get-tuple-element.34), calls=%async_computation | async-start | bytes 3538944 | tf_op jit(solution)/shard_map/all_to_all | solution.py:442
  10.9 3.3 %collective-permute-start.1 = (bf16[64,64,128]{2,1,0:T(8,128)(2,1)}, bf16[64,64,128]{2,1,0:T(8,128)(2,1)}, u32[]{:S(2)}, u32[]{:S(2)}) collective-permute-start(bf16[64,64,128]{2,1,0:T(8,128)(2,1)} %get-tuple-element.27), channel_id=1, source_target_pairs={{4,8},{8,4},{5,9},{9,5},{6,10},{10,6},{7,11},{11,7},{20,24},{24,20... | collective-permute-start | bytes 3145736 | tf_op jit(solution)/shard_map/ppermute | solution.py:443
  14.9 9.9 %shard_map.96 = (bf16[24,64,128]{2,1,0:T(8,128)(2,1)}, bf16[16,64,128]{2,1,0:T(8,128)(2,1)}, bf16[16,64,128]{2,1,0:T(8,128)(2,1)}, bf16[8,64,128]{2,1,0:T(8,128)(2,1)}) custom-call(s32[384]{0:T(512)} %atom_ref.3, s32[384]{0:T(512)} %line_ref.3, s32[1]{0:T(128)S(6)} %copy.13.count_ref, ...), custom_call_target="tpu_custom_call" | custom-call | flops 1100000 | bytes 1024 | tf_op jit(solution)/shard_map/pallas_call | solution.py:34
  24.9 2.3 %collective-permute-start.3 = (bf16[16,64,128]{2,1,0:T(8,128)(2,1)}, bf16[16,64,128]{2,1,0:T(8,128)(2,1)S(1)}, u32[]{:S(2)}, u32[]{:S(2)}) collective-permute-start(bf16[16,64,128]{2,1,0:T(8,128)(2,1)} %get-tuple-element.30), channel_id=1, source_target_pairs={{4,8},{8,4},{5,9},{9,5},{6,10},{10,6},{7,11},{11,7},{20,24},{24,20... | collective-permute-start | bytes 786440 | tf_op jit(solution)/shard_map/ppermute | solution.py:466
  27.3 6.3 %collective-permute-done.4.refs_3_.refs_0_ = bf16[8,64,128]{2,1,0:T(8,128)(2,1)S(1)} collective-permute-done((bf16[8,64,128]{2,1,0:T(8,128)(2,1)}, bf16[8,64,128]{2,1,0:T(8,128)(2,1)S(1)}, u32[]{:S(2)}, u32[]{:S(2)}) %collective-permute-start.4) | collective-permute-done | bytes 131104 | tf_op jit(solution)/shard_map/ppermute | solution.py:467
  33.6 0.5 collective-permute-done.3.refs_2_.link_ref
  34.4 0.5 copy-done.3
  34.8 3.4 %collective-permute-start.5 = (bf16[64,64,128]{2,1,0:T(8,128)(2,1)}, bf16[64,64,128]{2,1,0:T(8,128)(2,1)}, u32[]{:S(2)}, u32[]{:S(2)}) collective-permute-start(bf16[64,64,128]{2,1,0:T(8,128)(2,1)} %shard_map.97), channel_id=1, source_target_pairs={{4,8},{8,4},{5,9},{9,5},{6,10},{10,6},{7,11},{11,7},{20,24},{24,20... | collective-permute-start | bytes 3145736 | tf_op jit(solution)/shard_map/ppermute | solution.py:480
  38.2 11.6 %shard_map.98 = (f32[128,64,128]{2,1,0:T(8,128)}, bf16[8,64,128]{2,1,0:T(8,128)(2,1)}) custom-call(s32[384]{0:T(512)} %atom_ref.3, s32[384]{0:T(512)} %line_ref.3, s32[1]{0:T(128)S(6)} %copy.13.count_ref, bf16[384,16,128]{2,1,0:T(8,128)(2,1)} %p_hbm.3, f32[16,256]{1,0:T(8,128)} %bitcast.9, bf16[24,64,128]{2,1,0:T(8,128)(2,1)} %get-tuple-element.32.mine_hbm, ...), custom_call_target="tpu_custom_call" | custom-call | flops 1100000 | bytes 1024 | tf_op jit(solution)/shard_map/pallas_call | solution.py:34
  49.8 1.7 %collective-permute-done.5.late_hbm.late_ref = bf16[64,64,128]{2,1,0:T(8,128)(2,1)} collective-permute-done((bf16[64,64,128]{2,1,0:T(8,128)(2,1)}, bf16[64,64,128]{2,1,0:T(8,128)(2,1)}, u32[]{:S(2)}, u32[]{:S(2)}) %collective-permute-start.5) | collective-permute-done | bytes 1048608 | tf_op jit(solution)/shard_map/ppermute | solution.py:480
  51.5 2.2 %shard_map.99 = (bf16[11,64,128]{2,1,0:T(8,128)(2,1)}, bf16[11,64,128]{2,1,0:T(8,128)(2,1)}, bf16[11,64,128]{2,1,0:T(8,128)(2,1)}, bf16[11,64,128]{2,1,0:T(8,128)(2,1)}) custom-call(bf16[128,64,128]{2,1,0:T(8,128)(2,1)} %get-tuple-element.26.xt_hbm.xt_ref.last_ref.next_ref, bf16[128,64,128]{2,1,0:T(8,128)(2,1)} %collective-permute-done.refs_5_.core_hbm.core_ref, ...), custom_call_target="tpu_custom_call" | custom-call | flops 1100000 | bytes 1024 | tf_op jit(solution)/shard_map/pallas_call | solution.py:34
  53.8 1.6 %collective-permute-start.6 = (bf16[11,64,128]{2,1,0:T(8,128)(2,1)}, bf16[11,64,128]{2,1,0:T(8,128)(2,1)S(1)}, u32[]{:S(2)}, u32[]{:S(2)}) collective-permute-start(bf16[11,64,128]{2,1,0:T(8,128)(2,1)} %get-tuple-element.41), channel_id=1, source_target_pairs={{0,1},{1,0},{2,3},{3,2},{4,5},{5,4},{6,7},{7,6},{8,9},{9,8},{10,11... | collective-permute-start | bytes 540680 | tf_op jit(solution)/shard_map/ppermute | solution.py:409
  55.4 1.7 %collective-permute-start.7 = (bf16[11,64,128]{2,1,0:T(8,128)(2,1)}, bf16[11,64,128]{2,1,0:T(8,128)(2,1)}, u32[]{:S(2)}, u32[]{:S(2)}) collective-permute-start(bf16[11,64,128]{2,1,0:T(8,128)(2,1)} %get-tuple-element.42), channel_id=1, source_target_pairs={{0,2},{1,3},{2,0},{3,1},{4,6},{5,7},{6,4},{7,5},{8,10},{9,11},{10,... | collective-permute-start | bytes 540680 | tf_op jit(solution)/shard_map/ppermute | solution.py:409
  57.1 0.5 collective-permute-start.8
  57.6 2.4 %shard_map.100 = (bf16[27,256,128]{2,1,0:T(8,128)(2,1)S(1)}, bf16[13,256,128]{2,1,0:T(8,128)(2,1)}, f32[8,128]{1,0:T(8,128)}) custom-call(bf16[108,64,128]{2,1,0:T(8,128)(2,1)} %all-to-all-done.landed, bf16[11,64,128]{2,1,0:T(8,128)(2,1)} %get-tuple-element.36.unread.refs_0_), custom_call_target="tpu_custom_call" | custom-call | flops 1100000 | bytes 1024 | tf_op jit(solution)/shard_map/pallas_call | solution.py:34
  60.0 3.8 %collective-permute-start.10 = (bf16[13,256,128]{2,1,0:T(8,128)(2,1)}, bf16[13,256,128]{2,1,0:T(8,128)(2,1)}, u32[]{:S(2)}, u32[]{:S(2)}) collective-permute-start(bf16[13,256,128]{2,1,0:T(8,128)(2,1)} %get-tuple-element.46), channel_id=1, source_target_pairs={{4,8},{8,4},{5,9},{9,5},{6,10},{10,6},{7,11},{11,7},{20,24},{24,20... | collective-permute-start | bytes 2555912 | tf_op jit(solution)/shard_map/ppermute | solution.py:530
  63.9 7.3 %shard_map.101 = (bf16[64,128,128]{2,1,0:T(8,128)(2,1)}, f32[8,128]{1,0:T(8,128)}) custom-call(bf16[128,64,128]{2,1,0:T(8,128)(2,1)} %get-tuple-element.26.xt_hbm.xt_ref.last_ref.next_ref, bf16[128,64,128]{2,1,0:T(8,128)(2,1)} %get-tuple-element.26.xt_hbm.xt_ref.last_ref.next_ref, bf16[128,64,128]{2,1,0:T(8,128)(2,1)} %get-tuple-element.26.xt_hbm.xt_ref.last_ref.next_ref, ...), custom_call_target="tpu_custom_call" | custom-call | flops 1100000 | bytes 1024 | tf_op jit(solution)/shard_map/pallas_call | solution.py:34
  71.2 1.2 %shard_map.102 = (bf16[7,256,128]{2,1,0:T(8,128)(2,1)S(1)}, bf16[3,256,128]{2,1,0:T(8,128)(2,1)S(1)}, bf16[2,256,128]{2,1,0:T(8,128)(2,1)S(1)}, f32[32,128]{1,0:T(8,128)S(1)}, f32[8,128]{1,0:T(8,128)}) custom-call(bf16[27,256,128]{2,1,0:T(8,128)(2,1)S(1)} %get-tuple-element.39.after_ref.all_ref, f32[16,256]{1,0:T(8,128)S(1)} %bitcast.10, ...), custom_call_target="tpu_custom_call" | custom-call | flops 32999999488 | bytes 1024 | tf_op jit(solution)/shard_map/pallas_call | solution.py:34
  72.4 2.0 %collective-permute-done.10.link_ref = bf16[13,256,128]{2,1,0:T(8,128)(2,1)} collective-permute-done((bf16[13,256,128]{2,1,0:T(8,128)(2,1)}, bf16[13,256,128]{2,1,0:T(8,128)(2,1)}, u32[]{:S(2)}, u32[]{:S(2)}) %collective-permute-start.10) | collective-permute-done | bytes 852000 | tf_op jit(solution)/shard_map/ppermute | solution.py:530
  74.4 2.7 %shard_map.103.begun_ref = f32[2,256,256]{2,1,0:T(8,128)S(1)} custom-call(bf16[27,256,128]{2,1,0:T(8,128)(2,1)S(1)} %get-tuple-element.39.after_ref.all_ref, bf16[13,256,128]{2,1,0:T(8,128)(2,1)} %collective-permute-done.9.core_ref, bf16[13,256,128]{2,1,0:T(8,128)(2,1)} %collective-permute-done.10.link_ref, f32[128,128]{1,0:T(8,128)S(1)} %bitcast.7, ...), custom_call_target="tpu_custom_call" | custom-call | flops 1100000 | bytes 1024 | tf_op jit(solution)/shard_map/pallas_call | solution.py:34
  77.1 0.8 shard_map.104
  78.0 15.7 %all_to_all.10.parts_ref = bf16[16,64,128]{2,1,0:T(8,128)(2,1)S(1)} all-to-all(bf16[16,64,128]{2,1,0:T(8,128)(2,1)S(1)} %shard_map.104), channel_id=1, replica_groups=mesh['groups'=2,'domain'=4,'band'=4] {'domain','band'}, dimensions={0} | all-to-all | bytes 524288 | tf_op jit(solution)/shard_map/all_to_all | solution.py:599
  93.6 0.7 shard_map.105
  (22 shorter events, 0.6 us)
Async XLA Ops:
  4.7 29.4 %collective-permute-start = (bf16[128,64,128]{2,1,0:T(8,128)(2,1)}, bf16[128,64,128]{2,1,0:T(8,128)(2,1)}, u32[]{:S(2)}, u32[]{:S(2)}) collective-permute-start(bf16[128,64,128]{2,1,0:T(8,128)(2,1)} %get-tuple-element.26.xt_hbm.xt_ref.last_ref.next_ref), channel_id=1, source_target_pairs={{0,4},{4,0},{8,12},{12,8},{1,5},{5,1},{9,13},{13,9},{2,6},{6,2},{1... | collective-permute-start | bytes 6291464 | tf_op jit(solution)/shard_map/ppermute | solution.py:444
  4.9 52.7 %all-to-all-start = ((bf16[108,64,128]{2,1,0:T(8,128)(2,1)}), bf16[108,64,128]{2,1,0:T(8,128)(2,1)}, u32[]{:S(2)}, u32[]{:S(2)}) async-start(bf16[108,64,128]{2,1,0:T(8,128)(2,1)} %get-tuple-element.34), calls=%async_computation | async-start | bytes 3538944 | tf_op jit(solution)/shard_map/all_to_all | solution.py:442
  10.9 23.2 %collective-permute-start.1 = (bf16[64,64,128]{2,1,0:T(8,128)(2,1)}, bf16[64,64,128]{2,1,0:T(8,128)(2,1)}, u32[]{:S(2)}, u32[]{:S(2)}) collective-permute-start(bf16[64,64,128]{2,1,0:T(8,128)(2,1)} %get-tuple-element.27), channel_id=1, source_target_pairs={{4,8},{8,4},{5,9},{9,5},{6,10},{10,6},{7,11},{11,7},{20,24},{24,20... | collective-permute-start | bytes 3145736 | tf_op jit(solution)/shard_map/ppermute | solution.py:443
  24.8 8.8 %collective-permute-start.2 = (bf16[16,64,128]{2,1,0:T(8,128)(2,1)}, bf16[16,64,128]{2,1,0:T(8,128)(2,1)S(1)}, u32[]{:S(2)}, u32[]{:S(2)}) collective-permute-start(bf16[16,64,128]{2,1,0:T(8,128)(2,1)} %get-tuple-element.29), channel_id=1, source_target_pairs={{0,4},{4,0},{8,12},{12,8},{1,5},{5,1},{9,13},{13,9},{2,6},{6,2},{1... | collective-permute-start | bytes 786440 | tf_op jit(solution)/shard_map/ppermute | solution.py:468
  24.9 9.2 %collective-permute-start.3 = (bf16[16,64,128]{2,1,0:T(8,128)(2,1)}, bf16[16,64,128]{2,1,0:T(8,128)(2,1)S(1)}, u32[]{:S(2)}, u32[]{:S(2)}) collective-permute-start(bf16[16,64,128]{2,1,0:T(8,128)(2,1)} %get-tuple-element.30), channel_id=1, source_target_pairs={{4,8},{8,4},{5,9},{9,5},{6,10},{10,6},{7,11},{11,7},{20,24},{24,20... | collective-permute-start | bytes 786440 | tf_op jit(solution)/shard_map/ppermute | solution.py:466
  27.2 6.4 %collective-permute-start.4 = (bf16[8,64,128]{2,1,0:T(8,128)(2,1)}, bf16[8,64,128]{2,1,0:T(8,128)(2,1)S(1)}, u32[]{:S(2)}, u32[]{:S(2)}) collective-permute-start(bf16[8,64,128]{2,1,0:T(8,128)(2,1)} %get-tuple-element.31), channel_id=1, source_target_pairs={{0,8},{4,12},{8,0},{12,4},{1,9},{5,13},{9,1},{13,5},{2,10},{6,14},... | collective-permute-start | bytes 393224 | tf_op jit(solution)/shard_map/ppermute | solution.py:467
  33.6 0.6 copy-start.4
  33.6 0.7 copy-start.2
  34.1 0.7 copy-start.3
  34.8 16.7 %collective-permute-start.5 = (bf16[64,64,128]{2,1,0:T(8,128)(2,1)}, bf16[64,64,128]{2,1,0:T(8,128)(2,1)}, u32[]{:S(2)}, u32[]{:S(2)}) collective-permute-start(bf16[64,64,128]{2,1,0:T(8,128)(2,1)} %shard_map.97), channel_id=1, source_target_pairs={{4,8},{8,4},{5,9},{9,5},{6,10},{10,6},{7,11},{11,7},{20,24},{24,20... | collective-permute-start | bytes 3145736 | tf_op jit(solution)/shard_map/ppermute | solution.py:480
  53.8 17.3 %collective-permute-start.6 = (bf16[11,64,128]{2,1,0:T(8,128)(2,1)}, bf16[11,64,128]{2,1,0:T(8,128)(2,1)S(1)}, u32[]{:S(2)}, u32[]{:S(2)}) collective-permute-start(bf16[11,64,128]{2,1,0:T(8,128)(2,1)} %get-tuple-element.41), channel_id=1, source_target_pairs={{0,1},{1,0},{2,3},{3,2},{4,5},{5,4},{6,7},{7,6},{8,9},{9,8},{10,11... | collective-permute-start | bytes 540680 | tf_op jit(solution)/shard_map/ppermute | solution.py:409
  55.4 15.7 %collective-permute-start.7 = (bf16[11,64,128]{2,1,0:T(8,128)(2,1)}, bf16[11,64,128]{2,1,0:T(8,128)(2,1)}, u32[]{:S(2)}, u32[]{:S(2)}) collective-permute-start(bf16[11,64,128]{2,1,0:T(8,128)(2,1)} %get-tuple-element.42), channel_id=1, source_target_pairs={{0,2},{1,3},{2,0},{3,1},{4,6},{5,7},{6,4},{7,5},{8,10},{9,11},{10,... | collective-permute-start | bytes 540680 | tf_op jit(solution)/shard_map/ppermute | solution.py:409
  57.1 14.0 %collective-permute-start.8 = (bf16[11,64,128]{2,1,0:T(8,128)(2,1)}, bf16[11,64,128]{2,1,0:T(8,128)(2,1)}, u32[]{:S(2)}, u32[]{:S(2)}) collective-permute-start(bf16[11,64,128]{2,1,0:T(8,128)(2,1)} %get-tuple-element.43), channel_id=1, source_target_pairs={{0,3},{1,2},{2,1},{3,0},{4,7},{5,6},{6,5},{7,4},{8,11},{9,10},{10,... | collective-permute-start | bytes 540680 | tf_op jit(solution)/shard_map/ppermute | solution.py:409
  60.0 14.4 %collective-permute-start.10 = (bf16[13,256,128]{2,1,0:T(8,128)(2,1)}, bf16[13,256,128]{2,1,0:T(8,128)(2,1)}, u32[]{:S(2)}, u32[]{:S(2)}) collective-permute-start(bf16[13,256,128]{2,1,0:T(8,128)(2,1)} %get-tuple-element.46), channel_id=1, source_target_pairs={{4,8},{8,4},{5,9},{9,5},{6,10},{10,6},{7,11},{11,7},{20,24},{24,20... | collective-permute-start | bytes 2555912 | tf_op jit(solution)/shard_map/ppermute | solution.py:530
  63.8 10.7 %collective-permute-start.9 = (bf16[13,256,128]{2,1,0:T(8,128)(2,1)}, bf16[13,256,128]{2,1,0:T(8,128)(2,1)}, u32[]{:S(2)}, u32[]{:S(2)}) collective-permute-start(bf16[13,256,128]{2,1,0:T(8,128)(2,1)} %get-tuple-element.46), channel_id=1, source_target_pairs={{0,4},{4,0},{8,12},{12,8},{1,5},{5,1},{9,13},{13,9},{2,6},{6,2},{1... | collective-permute-start | bytes 2555912 | tf_op jit(solution)/shard_map/ppermute | solution.py:531
  63.8 7.3 %copy-start.1 = (f32[256,16]{0,1:T(8,128)S(1)}, f32[256,16]{0,1:T(8,128)}, u32[]{:S(2)}) copy-start(f32[256,16]{0,1:T(8,128)} %param.14) | copy-start | bytes 49156
  71.2 3.3 %copy-start = (f32[1,128,128]{2,1,0:T(8,128)S(1)}, f32[1,128,128]{2,1,0:T(8,128)}, u32[]{:S(2)}) copy-start(f32[1,128,128]{2,1,0:T(8,128)} %param.9) | copy-start | bytes 196612

commit v17 on v16

--- a/solution.py
+++ b/solution.py
@@ -85,12 +85,10 @@
                 block = x[s0 : s0 + ROWS, y0 : y0 + ROWS, :].astype(F32)
                 turned = jnp.swapaxes(block, 0, 1).astype(BF16)
                 xt[y0 : y0 + ROWS, s0 : s0 + ROWS, :] = turned
+        send(c * share, share, early if c < bands // 2 else late, c % (bands // 2) * share)
         send(c * share + first, count, message, c * (count + 1))
         send(c * share, 1, message, (c + bands - 1) % bands * (count + 1) + count)
-        if (c + 1) * share == early.shape[0]:
-            send(0, early.shape[0], early, 0)
-    send(early.shape[0], late.shape[0], late, 0)
-    send(0, lines, xt_hbm, 0)
+        send(c * share, share, xt_hbm, c * share)
     for copy in sends:
         copy.wait()
 
@@ -266,7 +264,7 @@
 
 def stencil_kernel(
     early_steps, xt_ref, last_ref, next_ref, core_ref, early_ref, late_ref, added_ref, pot_ref, ring_ref, unread,
-    out_ref, token,
+    out_ref,
 ):
     states, here, _ = out_ref.shape
     early = pl.program_id(0) < early_steps
@@ -300,7 +298,7 @@
     copy.wait()
 
 
-def later_kernel(bands, landed, unread, all_ref, pass_hbm, token, sems, pass_sem):
+def later_kernel(bands, landed, unread, all_ref, pass_hbm, sems, pass_sem):
     count, states = all_ref.shape[0], landed.shape[1]
     loads = [
         start(
@@ -315,7 +313,7 @@
     pass_half(all_ref, pass_hbm, pass_sem)
 
 
-def early_kernel(after_ref, energy_ref, unread, *refs):
+def early_kernel(after_ref, energy_ref, *refs):
     pieces, (all_ref, beside_ref, projs_ref, table_ref, token, sems) = refs[:-6], refs[-6:]
     states = pieces[0].shape[1]
     count, half, held = all_ref.shape[0] - 1, beside_ref.shape[0], projs_ref.shape[0]
@@ -359,7 +357,7 @@
     add_products(lax.axis_index("band") * share + first, all_ref, (core_ref, link_ref), pot_ref, acc)
 
 
-def final_kernel(bands, share, all_ref, beside_ref, pot_ref, begun_ref, proj_ref, energy_ref, out_ref, acc):
+def final_kernel(bands, share, all_ref, beside_ref, pot_ref, begun_ref, proj_ref, energy_ref, out_ref, token, acc):
     acc[...] = begun_ref[...]
     add_products(lax.axis_index("band") * share, all_ref, (beside_ref,), pot_ref, acc)
     groups = proj_ref.shape[0]
@@ -435,7 +433,7 @@
             pltpu.VMEM((states, lines, cols_z), BF16),
             pltpu.VMEM(line_shape, BF16),
             copies((bands,)),
-            copies((2 * bands + 3,)),
+            copies((4 * bands,)),
         ],
         (field,),
     )
@@ -496,6 +494,7 @@
             copies((4,)),
         ],
         (tile_atom, tile_line, tile_count, projectors, energy, mine, from_core, from_link, *from_far),
+        micros=30,
     )
     held = groups // bands
     built_shape = (first + first // 2 + held, states, cols_z)
@@ -517,24 +516,63 @@
     )
     early = swapped(messages, "band")
 
-    later_all, later_pass, later_token = call(
+    later_all, later_pass = call(
         32,
         functools.partial(later_kernel, bands),
         (),
         [FAR, PINNED],
-        [NEAR, FAR, PINNED],
-        [((rest + 1, total_states, cols_z), BF16), ((rest // 2, total_states, cols_z), BF16), token],
+        [NEAR, FAR],
+        [((rest + 1, total_states, cols_z), BF16), ((rest // 2, total_states, cols_z), BF16)],
         [copies((bands,)), copies],
         (landed, own_message),
     )
     later_link = lax.ppermute(later_pass, "domain", link_pairs)
     later_core = lax.ppermute(later_pass, "domain", core_pairs)
 
+    early_all, early_beside, projs, energy_table_here, early_token = call(
+        32,
+        early_kernel,
+        (),
+        [NEAR, WHOLE, PINNED] + [FAR] * (bands - 1),
+        [NEAR, NEAR, NEAR, NEAR, PINNED],
+        [
+            ((first + 1, total_states, cols_z), BF16),
+            ((first // 2, total_states, cols_z), BF16),
+            ((held, total_states, LANES), BF16),
+            (energy_rows, F32),
+            token,
+        ],
+        [copies((3 * bands,))],
+        (later_all, energy, own_message, *early),
+        micros=30,
+    )
+    (begun,) = call(
+        32,
+        functools.partial(gram_kernel, first, share),
+        (),
+        [NEAR, WHOLE, WHOLE, WHOLE, PINNED],
+        [NEAR],
+        [((2, total_states, total_states), F32)],
+        [],
+        (later_all, later_core, later_link, pot, early_token),
+    )
+    parts = domains * bands
+    blocks, final_token = call(
+        32,
+        functools.partial(final_kernel, bands, share),
+        (),
+        [NEAR, NEAR, WHOLE, NEAR, NEAR, NEAR],
+        [WHOLE, PINNED],
+        [((parts, states, 2 * total_states // domains), BF16), token],
+        [pltpu.VMEM((2, total_states, total_states), F32)],
+        (early_all, early_beside, pot, begun, projs, energy_table_here),
+    )
+    summed = lax.all_to_all(blocks, ("domain", "band"), split_axis=0, concat_axis=0, tiled=True)
     span = 2 * ROWS
     steps, early_steps = lines // span, (lines - late_lines) // span
     block = pl.BlockSpec((span, states, cols_z), lambda i: (i, 0, 0))
-    applied, done = call(
-        62,
+    (applied,) = call(
+        60,
         functools.partial(stencil_kernel, early_steps),
         (steps,),
         [
@@ -549,54 +587,15 @@
             WHOLE,
             PINNED,
         ],
-        [pl.BlockSpec((states, span, cols_z), lambda i: (0, i, 0)), PINNED],
-        [((states, lines, cols_z), BF16), token],
+        [pl.BlockSpec((states, span, cols_z), lambda i: (0, i, 0))],
+        [((states, lines, cols_z), BF16)],
         [],
         (
             xt, xt, xt, core_field, link_early, link_late, pltpu.with_memory_space_constraint(added, pltpu.HBM), pot, ring,
-            later_token,
+            final_token,
         ),
     )
 
-    early_all, early_beside, projs, energy_table_here, early_token = call(
-        32,
-        early_kernel,
-        (),
-        [NEAR, WHOLE, PINNED, PINNED] + [FAR] * (bands - 1),
-        [NEAR, NEAR, NEAR, NEAR, PINNED],
-        [
-            ((first + 1, total_states, cols_z), BF16),
-            ((first // 2, total_states, cols_z), BF16),
-            ((held, total_states, LANES), BF16),
-            (energy_rows, F32),
-            token,
-        ],
-        [copies((3 * bands,))],
-        (later_all, energy, done, own_message, *early),
-        micros=30,
-    )
-    (begun,) = call(
-        32,
-        functools.partial(gram_kernel, first, share),
-        (),
-        [NEAR, WHOLE, WHOLE, WHOLE, PINNED],
-        [NEAR],
-        [((2, total_states, total_states), F32)],
-        [],
-        (later_all, later_core, later_link, pot, early_token),
-    )
-    parts = domains * bands
-    (blocks,) = call(
-        32,
-        functools.partial(final_kernel, bands, share),
-        (),
-        [NEAR, NEAR, WHOLE, NEAR, NEAR, NEAR],
-        [WHOLE],
-        [((parts, states, 2 * total_states // domains), BF16)],
-        [pltpu.VMEM((2, total_states, total_states), F32)],
-        (early_all, early_beside, pot, begun, projs, energy_table_here),
-    )
-    summed = lax.all_to_all(blocks, ("domain", "band"), split_axis=0, concat_axis=0, tiled=True)
     (subspace,) = call(
         32,
         functools.partial(result_kernel, 1.0 / (lines * cols_z * domains)),

time: 95.7 us -> 111 us (1.16)
  waiting for transfers between devices: 10.5 us -> 36.5 us
  blocking collectives: 15.7 us -> 0 us
  starting transfers between devices: 22.9 us -> 28.9 us
  Pallas kernels: 43.1 us -> 41.6 us
    all_to_all x1, waiting for transfers between devices: 0.01 us -> 21.9 us  [local(): lax.all_to_all(message, 'band', split_axis=0, concat_axis=0, tiled=True)]
    all_to_all x1 -> x0, blocking collectives: 15.7 us -> none  [local(): lax.all_to_all(blocks, ('domain', 'band'), split_axis=0, concat_axis=0, t...]
    ppermute x1, waiting for transfers between devices: 2.02 us -> 9.16 us  [local(): later_link = lax.ppermute(later_pass, 'domain', link_pairs)]
    ppermute x1, waiting for transfers between devices: 6.34 us -> 1.45 us  [local(): lax.ppermute(value, 'domain', pairs)]
    all_to_all x0 -> x1, starting transfers between devices: none -> 4.32 us  [local(): lax.all_to_all(blocks, ('domain', 'band'), split_axis=0, concat_axis=0, t...]
    all_to_all x0 -> x1, waiting for transfers between devices: none -> 2.09 us  [local(): lax.all_to_all(blocks, ('domain', 'band'), split_axis=0, concat_axis=0, t...]
    ppermute x1, starting transfers between devices: 3.76 us -> 5.3 us  [local(): later_link = lax.ppermute(later_pass, 'domain', link_pairs)]
    pallas_call x11, Pallas kernels: 43.1 us -> 41.6 us  [call(): pl.pallas_call(kernel, grid=grid, out_shape=shapes, in_specs=in_specs, ou...]
  transfers between devices with their start and end apart: 12 -> 13, of which waited for: 4 -> 6; matrix products, arithmetic and copies ran while one was open for 0% -> 0% of each run, Pallas kernels for 37% -> 31%
where the time goes in v17:
time: 111 us; the launch traced here: 110 us
  Pallas kernels  41.6 us (37%)
  waiting for transfers between devices  36.5 us (33%)
  starting transfers between devices  28.9 us (26%)
  local copies, waits for them, and re-layouts  1.71 us (2%)
  between operations  1.44 us (1%)
    pallas_call x11, Pallas kernels, call(): pl.pallas_call(kernel, grid=grid, out_shape=shapes, in_specs=in_specs, ou...  41.6 us
    all_to_all x1, waiting for transfers between devices, local(): lax.all_to_all(message, 'band', split_axis=0, concat_axis=0, tiled=True)  21.9 us
    ppermute x1, waiting for transfers between devices, local(): later_link = lax.ppermute(later_pass, 'domain', link_pairs)  9.16 us
    ppermute x1, starting transfers between devices, local(): later_link = lax.ppermute(later_pass, 'domain', link_pairs)  5.3 us
    all_to_all x1, starting transfers between devices, local(): lax.all_to_all(message, 'band', split_axis=0, concat_axis=0, tiled=True)  4.9 us
    ppermute x1, starting transfers between devices, local(): link_early = lax.ppermute(early_part, 'domain', link_pairs)  4.5 us
    all_to_all x1, starting transfers between devices, local(): lax.all_to_all(blocks, ('domain', 'band'), split_axis=0, concat_axis=0, t...  4.32 us
    ppermute x3, starting transfers between devices, swapped(): lax.ppermute(values[k - 1], axis, [(i, i ^ k) for i in range(size)])  3.95 us
  transfers between devices with their start and end apart: 13, of which 6 were waited for; matrix products, arithmetic and copies ran while one was open for 0% of the time, Pallas kernels for 31%

profile of v17, /device:TPU:1, one launch (start us, length us, event | category | flops | bytes accessed | tf_op | source)
XLA Modules:
  0.0 110.1 jit_solution(434324043878302266)
XLA Ops:
  0.6 4.0 %shard_map.95 = (bf16[128,64,128]{2,1,0:T(8,128)(2,1)}, bf16[64,64,128]{2,1,0:T(8,128)(2,1)}, bf16[64,64,128]{2,1,0:T(8,128)(2,1)}, bf16[108,64,128]{2,1,0:T(8,128)(2,1)}) custom-call(bf16[64,128,128]{2,1,0:T(8,128)(2,1)} %bitcast.12), custom_call_target="tpu_custom_call" | custom-call | flops 1100000 | bytes 1024 | tf_op jit(solution)/shard_map/pallas_call | solution.py:34
  4.8 4.5 %collective-permute-start.1 = (bf16[64,64,128]{2,1,0:T(8,128)(2,1)}, bf16[64,64,128]{2,1,0:T(8,128)(2,1)}, u32[]{:S(2)}, u32[]{:S(2)}) collective-permute-start(bf16[64,64,128]{2,1,0:T(8,128)(2,1)} %get-tuple-element.26), channel_id=1, source_target_pairs={{4,8},{8,4},{5,9},{9,5},{6,10},{10,6},{7,11},{11,7},{20,24},{24,20... | collective-permute-start | bytes 3145736 | tf_op jit(solution)/shard_map/ppermute | solution.py:441
  9.9 10.0 %shard_map.96 = (bf16[24,64,128]{2,1,0:T(8,128)(2,1)}, bf16[16,64,128]{2,1,0:T(8,128)(2,1)}, bf16[16,64,128]{2,1,0:T(8,128)(2,1)}, bf16[8,64,128]{2,1,0:T(8,128)(2,1)}) custom-call(s32[384]{0:T(512)} %atom_ref.3, s32[384]{0:T(512)} %line_ref.3, s32[1]{0:T(128)S(6)} %copy.13.count_ref, ...), custom_call_target="tpu_custom_call" | custom-call | flops 1100000 | bytes 1024 | tf_op jit(solution)/shard_map/pallas_call | solution.py:34
  20.0 2.1 %collective-permute-start.3 = (bf16[16,64,128]{2,1,0:T(8,128)(2,1)}, bf16[16,64,128]{2,1,0:T(8,128)(2,1)S(1)}, u32[]{:S(2)}, u32[]{:S(2)}) collective-permute-start(bf16[16,64,128]{2,1,0:T(8,128)(2,1)} %get-tuple-element.29), channel_id=1, source_target_pairs={{4,8},{8,4},{5,9},{9,5},{6,10},{10,6},{7,11},{11,7},{20,24},{24,20... | collective-permute-start | bytes 786440 | tf_op jit(solution)/shard_map/ppermute | solution.py:464
  22.2 4.9 %all-to-all-start = ((bf16[108,64,128]{2,1,0:T(8,128)(2,1)}), bf16[108,64,128]{2,1,0:T(8,128)(2,1)}, u32[]{:S(2)}, u32[]{:S(2)}) async-start(bf16[108,64,128]{2,1,0:T(8,128)(2,1)} %get-tuple-element.33), calls=%async_computation | async-start | bytes 3538944 | tf_op jit(solution)/shard_map/all_to_all | solution.py:440
  27.1 1.4 %collective-permute-done.4.refs_3_.refs_0_ = bf16[8,64,128]{2,1,0:T(8,128)(2,1)S(1)} collective-permute-done((bf16[8,64,128]{2,1,0:T(8,128)(2,1)}, bf16[8,64,128]{2,1,0:T(8,128)(2,1)S(1)}, u32[]{:S(2)}, u32[]{:S(2)}) %collective-permute-start.4) | collective-permute-done | bytes 131104 | tf_op jit(solution)/shard_map/ppermute | solution.py:465
  29.7 3.4 %collective-permute-start.5 = (bf16[64,64,128]{2,1,0:T(8,128)(2,1)}, bf16[64,64,128]{2,1,0:T(8,128)(2,1)S(1)}, u32[]{:S(2)}, u32[]{:S(2)}) collective-permute-start(bf16[64,64,128]{2,1,0:T(8,128)(2,1)} %shard_map.97), channel_id=1, source_target_pairs={{4,8},{8,4},{5,9},{9,5},{6,10},{10,6},{7,11},{11,7},{20,24},{24,20... | collective-permute-start | bytes 3145736 | tf_op jit(solution)/shard_map/ppermute | solution.py:478
  33.2 11.9 %shard_map.98 = (f32[128,64,128]{2,1,0:T(8,128)}, bf16[8,64,128]{2,1,0:T(8,128)(2,1)}) custom-call(s32[384]{0:T(512)} %atom_ref.3, s32[384]{0:T(512)} %line_ref.3, s32[1]{0:T(128)S(6)} %copy.13.count_ref, bf16[384,16,128]{2,1,0:T(8,128)(2,1)} %p_hbm.3, f32[16,256]{1,0:T(8,128)} %bitcast.9, bf16[24,64,128]{2,1,0:T(8,128)(2,1)} %get-tuple-element.31.mine_hbm, ...), custom_call_target="tpu_custom_call" | custom-call | flops 32999999488 | bytes 1024 | tf_op jit(solution)/shard_map/pallas_call | solution.py:34
  45.0 1.4 %collective-permute-done.5.late_hbm.late_ref = bf16[64,64,128]{2,1,0:T(8,128)(2,1)S(1)} collective-permute-done((bf16[64,64,128]{2,1,0:T(8,128)(2,1)}, bf16[64,64,128]{2,1,0:T(8,128)(2,1)S(1)}, u32[]{:S(2)}, u32[]{:S(2)}) %collective-permute-start.5) | collective-permute-done | bytes 1048608 | tf_op jit(solution)/shard_map/ppermute | solution.py:478
  46.4 1.0 copy-done.2
  47.4 2.3 %shard_map.99 = (bf16[11,64,128]{2,1,0:T(8,128)(2,1)}, bf16[11,64,128]{2,1,0:T(8,128)(2,1)}, bf16[11,64,128]{2,1,0:T(8,128)(2,1)}, bf16[11,64,128]{2,1,0:T(8,128)(2,1)}) custom-call(bf16[128,64,128]{2,1,0:T(8,128)(2,1)} %get-tuple-element.25.xt_hbm.xt_ref.last_ref.next_ref, bf16[128,64,128]{2,1,0:T(8,128)(2,1)} %collective-permute-done.refs_5_.core_hbm.core_ref, ...), custom_call_target="tpu_custom_call" | custom-call | flops 1100000 | bytes 1024 | tf_op jit(solution)/shard_map/pallas_call | solution.py:34
  49.7 1.6 %collective-permute-start.6 = (bf16[11,64,128]{2,1,0:T(8,128)(2,1)}, bf16[11,64,128]{2,1,0:T(8,128)(2,1)S(1)}, u32[]{:S(2)}, u32[]{:S(2)}) collective-permute-start(bf16[11,64,128]{2,1,0:T(8,128)(2,1)} %get-tuple-element.37), channel_id=1, source_target_pairs={{0,1},{1,0},{2,3},{3,2},{4,5},{5,4},{6,7},{7,6},{8,9},{9,8},{10,11... | collective-permute-start | bytes 540680 | tf_op jit(solution)/shard_map/ppermute | solution.py:407
  51.4 2.3 %collective-permute-start.7 = (bf16[11,64,128]{2,1,0:T(8,128)(2,1)}, bf16[11,64,128]{2,1,0:T(8,128)(2,1)S(1)}, u32[]{:S(2)}, u32[]{:S(2)}) collective-permute-start(bf16[11,64,128]{2,1,0:T(8,128)(2,1)} %get-tuple-element.38), channel_id=1, source_target_pairs={{0,2},{1,3},{2,0},{3,1},{4,6},{5,7},{6,4},{7,5},{8,10},{9,11},{10,... | collective-permute-start | bytes 540680 | tf_op jit(solution)/shard_map/ppermute | solution.py:407
  53.7 21.9 %all-to-all-done.landed = bf16[108,64,128]{2,1,0:T(8,128)(2,1)} async-done(((bf16[108,64,128]{2,1,0:T(8,128)(2,1)}), bf16[108,64,128]{2,1,0:T(8,128)(2,1)}, u32[]{:S(2)}, u32[]{:S(2)}) %all-to-all-start) | async-done | bytes 1769504 | tf_op jit(solution)/shard_map/all_to_all | solution.py:440
  75.6 1.6 %shard_map.100 = (bf16[27,256,128]{2,1,0:T(8,128)(2,1)S(1)}, bf16[13,256,128]{2,1,0:T(8,128)(2,1)S(1)}) custom-call(bf16[108,64,128]{2,1,0:T(8,128)(2,1)} %all-to-all-done.landed, bf16[11,64,128]{2,1,0:T(8,128)(2,1)} %get-tuple-element.35.unread.refs_0_), custom_call_target="tpu_custom_call" | custom-call | flops 1100000 | bytes 1024 | tf_op jit(solution)/shard_map/pallas_call | solution.py:34
  77.2 5.3 %collective-permute-start.10 = (bf16[13,256,128]{2,1,0:T(8,128)(2,1)S(1)}, bf16[13,256,128]{2,1,0:T(8,128)(2,1)S(1)}, u32[]{:S(2)}, u32[]{:S(2)}) collective-permute-start(bf16[13,256,128]{2,1,0:T(8,128)(2,1)S(1)} %get-tuple-element.42), channel_id=1, source_target_pairs={{4,8},{8,4},{5,9},{9,5},{6,10},{10,6},{7,11},{11,7},{20,24},{24,20... | collective-permute-start | bytes 2555912 | tf_op jit(solution)/shard_map/ppermute | solution.py:529
  82.6 1.1 shard_map.101
  83.7 9.2 %collective-permute-done.10.link_ref = bf16[13,256,128]{2,1,0:T(8,128)(2,1)S(1)} collective-permute-done((bf16[13,256,128]{2,1,0:T(8,128)(2,1)S(1)}, bf16[13,256,128]{2,1,0:T(8,128)(2,1)S(1)}, u32[]{:S(2)}, u32[]{:S(2)}) %collective-permute-start.10) | collective-permute-done | bytes 852000 | tf_op jit(solution)/shard_map/ppermute | solution.py:529
  92.8 1.3 %shard_map.102.begun_ref = f32[2,256,256]{2,1,0:T(8,128)S(1)} custom-call(bf16[27,256,128]{2,1,0:T(8,128)(2,1)S(1)} %get-tuple-element.36.after_ref.all_ref, bf16[13,256,128]{2,1,0:T(8,128)(2,1)S(1)} %collective-permute-done.9.core_ref, bf16[13,256,128]{2,1,0:T(8,128)(2,1)S(1)} %collective-permute-done.10.link_ref, f32[128,128]{1,0:T(8,128)S(1)} %bitcast.7, ...), custom_call_target="tpu_custom_call" | custom-call | flops 1100000 | bytes 1024 | tf_op jit(solution)/shard_map/pallas_call | solution.py:34
  94.1 1.6 %shard_map.103 = (bf16[16,64,128]{2,1,0:T(8,128)(2,1)}, f32[8,128]{1,0:T(8,128)}) custom-call(bf16[7,256,128]{2,1,0:T(8,128)(2,1)S(1)} %get-tuple-element.40.all_ref, bf16[3,256,128]{2,1,0:T(8,128)(2,1)S(1)} %get-tuple-element.41.beside_ref, f32[128,128]{1,0:T(8,128)S(1)} %bitcast.8, f32[2,256,256]{2,1,0:T(8,128)S(1)} %shard_map.102.begun_ref, ...), custom_call_target="tpu_custom_call" | custom-call | flops 1100000 | bytes 1024 | tf_op jit(solution)/shard_map/pallas_call | solution.py:34
  95.7 4.3 %all-to-all-start.1 = ((bf16[16,64,128]{2,1,0:T(8,128)(2,1)}), bf16[16,64,128]{2,1,0:T(8,128)(2,1)S(1)}, u32[]{:S(2)}, u32[]{:S(2)}) async-start(bf16[16,64,128]{2,1,0:T(8,128)(2,1)} %get-tuple-element.47), calls=%async_computation.1 | async-start | bytes 524288 | tf_op jit(solution)/shard_map/all_to_all | solution.py:570
  100.0 7.3 %shard_map.104 = bf16[64,128,128]{2,1,0:T(8,128)(2,1)} custom-call(bf16[128,64,128]{2,1,0:T(8,128)(2,1)} %get-tuple-element.25.xt_hbm.xt_ref.last_ref.next_ref, bf16[128,64,128]{2,1,0:T(8,128)(2,1)} %get-tuple-element.25.xt_hbm.xt_ref.last_ref.next_ref, bf16[128,64,128]{2,1,0:T(8,128)(2,1)} %get-tuple-element.25.xt_hbm.xt_ref.last_ref.next_ref, ...), custom_call_target="tpu_custom_call" | custom-call | flops 1100000 | bytes 1024 | tf_op jit(solution)/shard_map/pallas_call | solution.py:34
  107.2 2.1 %all-to-all-done.1.parts_ref = bf16[16,64,128]{2,1,0:T(8,128)(2,1)S(1)} async-done(((bf16[16,64,128]{2,1,0:T(8,128)(2,1)}), bf16[16,64,128]{2,1,0:T(8,128)(2,1)S(1)}, u32[]{:S(2)}, u32[]{:S(2)}) %all-to-all-start.1) | async-done | bytes 262176 | tf_op jit(solution)/shard_map/all_to_all | solution.py:570
  109.3 0.7 shard_map.105
  (25 shorter events, 1.5 us)
Async XLA Ops:
  4.6 24.4 %collective-permute-start = (bf16[128,64,128]{2,1,0:T(8,128)(2,1)}, bf16[128,64,128]{2,1,0:T(8,128)(2,1)}, u32[]{:S(2)}, u32[]{:S(2)}) collective-permute-start(bf16[128,64,128]{2,1,0:T(8,128)(2,1)} %get-tuple-element.25.xt_hbm.xt_ref.last_ref.next_ref), channel_id=1, source_target_pairs={{0,4},{4,0},{8,12},{12,8},{1,5},{5,1},{9,13},{13,9},{2,6},{6,2},{1... | collective-permute-start | bytes 6291464 | tf_op jit(solution)/shard_map/ppermute | solution.py:442
  4.8 24.2 %collective-permute-start.1 = (bf16[64,64,128]{2,1,0:T(8,128)(2,1)}, bf16[64,64,128]{2,1,0:T(8,128)(2,1)}, u32[]{:S(2)}, u32[]{:S(2)}) collective-permute-start(bf16[64,64,128]{2,1,0:T(8,128)(2,1)} %get-tuple-element.26), channel_id=1, source_target_pairs={{4,8},{8,4},{5,9},{9,5},{6,10},{10,6},{7,11},{11,7},{20,24},{24,20... | collective-permute-start | bytes 3145736 | tf_op jit(solution)/shard_map/ppermute | solution.py:441
  19.9 8.6 %collective-permute-start.2 = (bf16[16,64,128]{2,1,0:T(8,128)(2,1)}, bf16[16,64,128]{2,1,0:T(8,128)(2,1)S(1)}, u32[]{:S(2)}, u32[]{:S(2)}) collective-permute-start(bf16[16,64,128]{2,1,0:T(8,128)(2,1)} %get-tuple-element.28), channel_id=1, source_target_pairs={{0,4},{4,0},{8,12},{12,8},{1,5},{5,1},{9,13},{13,9},{2,6},{6,2},{1... | collective-permute-start | bytes 786440 | tf_op jit(solution)/shard_map/ppermute | solution.py:466
  20.0 9.0 %collective-permute-start.3 = (bf16[16,64,128]{2,1,0:T(8,128)(2,1)}, bf16[16,64,128]{2,1,0:T(8,128)(2,1)S(1)}, u32[]{:S(2)}, u32[]{:S(2)}) collective-permute-start(bf16[16,64,128]{2,1,0:T(8,128)(2,1)} %get-tuple-element.29), channel_id=1, source_target_pairs={{4,8},{8,4},{5,9},{9,5},{6,10},{10,6},{7,11},{11,7},{20,24},{24,20... | collective-permute-start | bytes 786440 | tf_op jit(solution)/shard_map/ppermute | solution.py:464
  22.1 6.4 %collective-permute-start.4 = (bf16[8,64,128]{2,1,0:T(8,128)(2,1)}, bf16[8,64,128]{2,1,0:T(8,128)(2,1)S(1)}, u32[]{:S(2)}, u32[]{:S(2)}) collective-permute-start(bf16[8,64,128]{2,1,0:T(8,128)(2,1)} %get-tuple-element.30), channel_id=1, source_target_pairs={{0,8},{4,12},{8,0},{12,4},{1,9},{5,13},{9,1},{13,5},{2,10},{6,14},... | collective-permute-start | bytes 393224 | tf_op jit(solution)/shard_map/ppermute | solution.py:465
  22.2 53.4 %all-to-all-start = ((bf16[108,64,128]{2,1,0:T(8,128)(2,1)}), bf16[108,64,128]{2,1,0:T(8,128)(2,1)}, u32[]{:S(2)}, u32[]{:S(2)}) async-start(bf16[108,64,128]{2,1,0:T(8,128)(2,1)} %get-tuple-element.33), calls=%async_computation | async-start | bytes 3538944 | tf_op jit(solution)/shard_map/all_to_all | solution.py:440
  28.5 0.7 copy-start.5
  28.5 0.8 copy-start.3
  29.0 0.7 copy-start.4
  29.7 16.7 %collective-permute-start.5 = (bf16[64,64,128]{2,1,0:T(8,128)(2,1)}, bf16[64,64,128]{2,1,0:T(8,128)(2,1)S(1)}, u32[]{:S(2)}, u32[]{:S(2)}) collective-permute-start(bf16[64,64,128]{2,1,0:T(8,128)(2,1)} %shard_map.97), channel_id=1, source_target_pairs={{4,8},{8,4},{5,9},{9,5},{6,10},{10,6},{7,11},{11,7},{20,24},{24,20... | collective-permute-start | bytes 3145736 | tf_op jit(solution)/shard_map/ppermute | solution.py:478
  46.4 1.0 copy-start.2
  47.4 35.2 %copy-start.1 = (f32[256,16]{0,1:T(8,128)S(1)}, f32[256,16]{0,1:T(8,128)}, u32[]{:S(2)}) copy-start(f32[256,16]{0,1:T(8,128)} %param.14) | copy-start | bytes 49156
  49.7 32.8 %collective-permute-start.6 = (bf16[11,64,128]{2,1,0:T(8,128)(2,1)}, bf16[11,64,128]{2,1,0:T(8,128)(2,1)S(1)}, u32[]{:S(2)}, u32[]{:S(2)}) collective-permute-start(bf16[11,64,128]{2,1,0:T(8,128)(2,1)} %get-tuple-element.37), channel_id=1, source_target_pairs={{0,1},{1,0},{2,3},{3,2},{4,5},{5,4},{6,7},{7,6},{8,9},{9,8},{10,11... | collective-permute-start | bytes 540680 | tf_op jit(solution)/shard_map/ppermute | solution.py:407
  51.4 31.2 %collective-permute-start.7 = (bf16[11,64,128]{2,1,0:T(8,128)(2,1)}, bf16[11,64,128]{2,1,0:T(8,128)(2,1)S(1)}, u32[]{:S(2)}, u32[]{:S(2)}) collective-permute-start(bf16[11,64,128]{2,1,0:T(8,128)(2,1)} %get-tuple-element.38), channel_id=1, source_target_pairs={{0,2},{1,3},{2,0},{3,1},{4,6},{5,7},{6,4},{7,5},{8,10},{9,11},{10,... | collective-permute-start | bytes 540680 | tf_op jit(solution)/shard_map/ppermute | solution.py:407
  53.7 28.9 %collective-permute-start.8 = (bf16[11,64,128]{2,1,0:T(8,128)(2,1)}, bf16[11,64,128]{2,1,0:T(8,128)(2,1)S(1)}, u32[]{:S(2)}, u32[]{:S(2)}) collective-permute-start(bf16[11,64,128]{2,1,0:T(8,128)(2,1)} %get-tuple-element.39), channel_id=1, source_target_pairs={{0,3},{1,2},{2,1},{3,0},{4,7},{5,6},{6,5},{7,4},{8,11},{9,10},{10,... | collective-permute-start | bytes 540680 | tf_op jit(solution)/shard_map/ppermute | solution.py:407
  77.2 15.7 %collective-permute-start.10 = (bf16[13,256,128]{2,1,0:T(8,128)(2,1)S(1)}, bf16[13,256,128]{2,1,0:T(8,128)(2,1)S(1)}, u32[]{:S(2)}, u32[]{:S(2)}) collective-permute-start(bf16[13,256,128]{2,1,0:T(8,128)(2,1)S(1)} %get-tuple-element.42), channel_id=1, source_target_pairs={{4,8},{8,4},{5,9},{9,5},{6,10},{10,6},{7,11},{11,7},{20,24},{24,20... | collective-permute-start | bytes 2555912 | tf_op jit(solution)/shard_map/ppermute | solution.py:529
  82.5 10.4 %collective-permute-start.9 = (bf16[13,256,128]{2,1,0:T(8,128)(2,1)S(1)}, bf16[13,256,128]{2,1,0:T(8,128)(2,1)S(1)}, u32[]{:S(2)}, u32[]{:S(2)}) collective-permute-start(bf16[13,256,128]{2,1,0:T(8,128)(2,1)S(1)} %get-tuple-element.42), channel_id=1, source_target_pairs={{0,4},{4,0},{8,12},{12,8},{1,5},{5,1},{9,13},{13,9},{2,6},{6,2},{1... | collective-permute-start | bytes 2555912 | tf_op jit(solution)/shard_map/ppermute | solution.py:530
  82.6 10.2 %copy-start = (f32[1,128,128]{2,1,0:T(8,128)S(1)}, f32[1,128,128]{2,1,0:T(8,128)}, u32[]{:S(2)}) copy-start(f32[1,128,128]{2,1,0:T(8,128)} %param.9) | copy-start | bytes 196612
  95.7 13.7 %all-to-all-start.1 = ((bf16[16,64,128]{2,1,0:T(8,128)(2,1)}), bf16[16,64,128]{2,1,0:T(8,128)(2,1)S(1)}, u32[]{:S(2)}, u32[]{:S(2)}) async-start(bf16[16,64,128]{2,1,0:T(8,128)(2,1)} %get-tuple-element.47), calls=%async_computation.1 | async-start | bytes 524288 | tf_op jit(solution)/shard_map/all_to_all | solution.py:570

commit v18 on v17

--- a/solution.py
+++ b/solution.py
@@ -494,7 +494,7 @@
             copies((4,)),
         ],
         (tile_atom, tile_line, tile_count, projectors, energy, mine, from_core, from_link, *from_far),
-        micros=30,
+        micros=8,
     )
     held = groups // bands
     built_shape = (first + first // 2 + held, states, cols_z)

time: 111 us -> 95 us (0.86)
  waiting for transfers between devices: 36.5 us -> 19.9 us
    all_to_all x1, waiting for transfers between devices: 21.9 us -> 0.01 us  [local(): lax.all_to_all(message, 'band', split_axis=0, concat_axis=0, tiled=True)]
    ppermute x3, waiting for transfers between devices: 0.01 us -> 7.5 us  [swapped(): lax.ppermute(values[k - 1], axis, [(i, i ^ k) for i in range(size)])]
    ppermute x1, waiting for transfers between devices: 9.16 us -> 1.69 us  [local(): later_link = lax.ppermute(later_pass, 'domain', link_pairs)]
    ppermute x1, waiting for transfers between devices: 1.45 us -> 6.34 us  [local(): lax.ppermute(value, 'domain', pairs)]
    all_to_all x1, starting transfers between devices: 4.32 us -> 6.56 us  [local(): lax.all_to_all(blocks, ('domain', 'band'), split_axis=0, concat_axis=0, t...]
    ppermute x1, starting transfers between devices: 5.3 us -> 3.82 us  [local(): later_link = lax.ppermute(later_pass, 'domain', link_pairs)]
    ppermute x1, starting transfers between devices: 4.5 us -> 3.33 us  [local(): link_early = lax.ppermute(early_part, 'domain', link_pairs)]
    all_to_all x1, starting transfers between devices: 4.9 us -> 6.04 us  [local(): lax.all_to_all(message, 'band', split_axis=0, concat_axis=0, tiled=True)]
  transfers between devices with their start and end apart: 13 -> 13, of which waited for: 6 -> 6; matrix products, arithmetic and copies ran while one was open for 0% -> 0% of each run, Pallas kernels for 31% -> 36%
where the time goes in v18:
time: 95 us; the launch traced here: 93.6 us
  Pallas kernels  41.2 us (43%)
  starting transfers between devices  29.4 us (31%)
  waiting for transfers between devices  19.9 us (21%)
  local copies, waits for them, and re-layouts  1.7 us (2%)
  between operations  1.41 us (1%)
    pallas_call x11, Pallas kernels, call(): pl.pallas_call(kernel, grid=grid, out_shape=shapes, in_specs=in_specs, ou...  41.2 us
    ppermute x3, waiting for transfers between devices, swapped(): lax.ppermute(values[k - 1], axis, [(i, i ^ k) for i in range(size)])  7.5 us
    all_to_all x1, starting transfers between devices, local(): lax.all_to_all(blocks, ('domain', 'band'), split_axis=0, concat_axis=0, t...  6.56 us
    ppermute x1, waiting for transfers between devices, local(): lax.ppermute(value, 'domain', pairs)  6.34 us
    all_to_all x1, starting transfers between devices, local(): lax.all_to_all(message, 'band', split_axis=0, concat_axis=0, tiled=True)  6.04 us
    ppermute x1, starting transfers between devices, local(): later_link = lax.ppermute(later_pass, 'domain', link_pairs)  3.82 us
    ppermute x3, starting transfers between devices, swapped(): lax.ppermute(values[k - 1], axis, [(i, i ^ k) for i in range(size)])  3.69 us
    ppermute x1, starting transfers between devices, local(): link_late = lax.ppermute(late_part, 'domain', link_pairs)  3.44 us
  transfers between devices with their start and end apart: 13, of which 6 were waited for; matrix products, arithmetic and copies ran while one was open for 0% of the time, Pallas kernels for 36%

profile of v18, /device:TPU:1, one launch (start us, length us, event | category | flops | bytes accessed | tf_op | source)
XLA Modules:
  0.0 93.6 jit_solution(15915474854196058400)
XLA Ops:
  0.6 4.0 %shard_map.95 = (bf16[128,64,128]{2,1,0:T(8,128)(2,1)}, bf16[64,64,128]{2,1,0:T(8,128)(2,1)}, bf16[64,64,128]{2,1,0:T(8,128)(2,1)}, bf16[108,64,128]{2,1,0:T(8,128)(2,1)}) custom-call(bf16[64,128,128]{2,1,0:T(8,128)(2,1)} %bitcast.12), custom_call_target="tpu_custom_call" | custom-call | flops 1100000 | bytes 1024 | tf_op jit(solution)/shard_map/pallas_call | solution.py:34
  4.8 6.0 %all-to-all-start = ((bf16[108,64,128]{2,1,0:T(8,128)(2,1)}), bf16[108,64,128]{2,1,0:T(8,128)(2,1)}, u32[]{:S(2)}, u32[]{:S(2)}) async-start(bf16[108,64,128]{2,1,0:T(8,128)(2,1)} %get-tuple-element.33), calls=%async_computation | async-start | bytes 3538944 | tf_op jit(solution)/shard_map/all_to_all | solution.py:440
  10.8 3.3 %collective-permute-start.1 = (bf16[64,64,128]{2,1,0:T(8,128)(2,1)}, bf16[64,64,128]{2,1,0:T(8,128)(2,1)}, u32[]{:S(2)}, u32[]{:S(2)}) collective-permute-start(bf16[64,64,128]{2,1,0:T(8,128)(2,1)} %get-tuple-element.26), channel_id=1, source_target_pairs={{4,8},{8,4},{5,9},{9,5},{6,10},{10,6},{7,11},{11,7},{20,24},{24,20... | collective-permute-start | bytes 3145736 | tf_op jit(solution)/shard_map/ppermute | solution.py:441
  14.8 9.9 %shard_map.96 = (bf16[24,64,128]{2,1,0:T(8,128)(2,1)}, bf16[16,64,128]{2,1,0:T(8,128)(2,1)}, bf16[16,64,128]{2,1,0:T(8,128)(2,1)}, bf16[8,64,128]{2,1,0:T(8,128)(2,1)}) custom-call(s32[384]{0:T(512)} %atom_ref.3, s32[384]{0:T(512)} %line_ref.3, s32[1]{0:T(128)S(6)} %copy.13.count_ref, ...), custom_call_target="tpu_custom_call" | custom-call | flops 1100000 | bytes 1024 | tf_op jit(solution)/shard_map/pallas_call | solution.py:34
  24.7 2.2 %collective-permute-start.3 = (bf16[16,64,128]{2,1,0:T(8,128)(2,1)}, bf16[16,64,128]{2,1,0:T(8,128)(2,1)S(1)}, u32[]{:S(2)}, u32[]{:S(2)}) collective-permute-start(bf16[16,64,128]{2,1,0:T(8,128)(2,1)} %get-tuple-element.29), channel_id=1, source_target_pairs={{4,8},{8,4},{5,9},{9,5},{6,10},{10,6},{7,11},{11,7},{20,24},{24,20... | collective-permute-start | bytes 786440 | tf_op jit(solution)/shard_map/ppermute | solution.py:464
  27.1 6.3 %collective-permute-done.4.refs_3_.refs_0_ = bf16[8,64,128]{2,1,0:T(8,128)(2,1)S(1)} collective-permute-done((bf16[8,64,128]{2,1,0:T(8,128)(2,1)}, bf16[8,64,128]{2,1,0:T(8,128)(2,1)S(1)}, u32[]{:S(2)}, u32[]{:S(2)}) %collective-permute-start.4) | collective-permute-done | bytes 131104 | tf_op jit(solution)/shard_map/ppermute | solution.py:465
  34.6 3.4 %collective-permute-start.5 = (bf16[64,64,128]{2,1,0:T(8,128)(2,1)}, bf16[64,64,128]{2,1,0:T(8,128)(2,1)S(1)}, u32[]{:S(2)}, u32[]{:S(2)}) collective-permute-start(bf16[64,64,128]{2,1,0:T(8,128)(2,1)} %shard_map.97), channel_id=1, source_target_pairs={{4,8},{8,4},{5,9},{9,5},{6,10},{10,6},{7,11},{11,7},{20,24},{24,20... | collective-permute-start | bytes 3145736 | tf_op jit(solution)/shard_map/ppermute | solution.py:478
  38.1 11.5 %shard_map.98 = (f32[128,64,128]{2,1,0:T(8,128)}, bf16[8,64,128]{2,1,0:T(8,128)(2,1)}) custom-call(s32[384]{0:T(512)} %atom_ref.3, s32[384]{0:T(512)} %line_ref.3, s32[1]{0:T(128)S(6)} %copy.13.count_ref, bf16[384,16,128]{2,1,0:T(8,128)(2,1)} %p_hbm.3, f32[16,256]{1,0:T(8,128)} %bitcast.9, bf16[24,64,128]{2,1,0:T(8,128)(2,1)} %get-tuple-element.31.mine_hbm, ...), custom_call_target="tpu_custom_call" | custom-call | flops 8800000000 | bytes 1024 | tf_op jit(solution)/shard_map/pallas_call | solution.py:34
  49.6 1.8 %collective-permute-done.5.late_hbm.late_ref = bf16[64,64,128]{2,1,0:T(8,128)(2,1)S(1)} collective-permute-done((bf16[64,64,128]{2,1,0:T(8,128)(2,1)}, bf16[64,64,128]{2,1,0:T(8,128)(2,1)S(1)}, u32[]{:S(2)}, u32[]{:S(2)}) %collective-permute-start.5) | collective-permute-done | bytes 1048608 | tf_op jit(solution)/shard_map/ppermute | solution.py:478
  51.3 1.0 %copy-done.2 = bf16[64,64,128]{2,1,0:T(8,128)(2,1)} copy-done((bf16[64,64,128]{2,1,0:T(8,128)(2,1)}, bf16[64,64,128]{2,1,0:T(8,128)(2,1)S(1)}, u32[]{:S(2)}) %copy-start.2) | copy-done | bytes 1048600
  52.3 2.3 %shard_map.99 = (bf16[11,64,128]{2,1,0:T(8,128)(2,1)}, bf16[11,64,128]{2,1,0:T(8,128)(2,1)}, bf16[11,64,128]{2,1,0:T(8,128)(2,1)}, bf16[11,64,128]{2,1,0:T(8,128)(2,1)}) custom-call(bf16[128,64,128]{2,1,0:T(8,128)(2,1)} %get-tuple-element.25.xt_hbm.xt_ref.last_ref.next_ref, bf16[128,64,128]{2,1,0:T(8,128)(2,1)} %collective-permute-done.refs_5_.core_hbm.core_ref, ...), custom_call_target="tpu_custom_call" | custom-call | flops 1100000 | bytes 1024 | tf_op jit(solution)/shard_map/pallas_call | solution.py:34
  54.6 1.5 %collective-permute-start.6 = (bf16[11,64,128]{2,1,0:T(8,128)(2,1)}, bf16[11,64,128]{2,1,0:T(8,128)(2,1)S(1)}, u32[]{:S(2)}, u32[]{:S(2)}) collective-permute-start(bf16[11,64,128]{2,1,0:T(8,128)(2,1)} %get-tuple-element.37), channel_id=1, source_target_pairs={{0,1},{1,0},{2,3},{3,2},{4,5},{5,4},{6,7},{7,6},{8,9},{9,8},{10,11... | collective-permute-start | bytes 540680 | tf_op jit(solution)/shard_map/ppermute | solution.py:407
  56.2 1.7 %collective-permute-start.7 = (bf16[11,64,128]{2,1,0:T(8,128)(2,1)}, bf16[11,64,128]{2,1,0:T(8,128)(2,1)S(1)}, u32[]{:S(2)}, u32[]{:S(2)}) collective-permute-start(bf16[11,64,128]{2,1,0:T(8,128)(2,1)} %get-tuple-element.38), channel_id=1, source_target_pairs={{0,2},{1,3},{2,0},{3,1},{4,6},{5,7},{6,4},{7,5},{8,10},{9,11},{10,... | collective-permute-start | bytes 540680 | tf_op jit(solution)/shard_map/ppermute | solution.py:407
  58.3 1.6 %shard_map.100 = (bf16[27,256,128]{2,1,0:T(8,128)(2,1)S(1)}, bf16[13,256,128]{2,1,0:T(8,128)(2,1)S(1)}) custom-call(bf16[108,64,128]{2,1,0:T(8,128)(2,1)} %all-to-all-done.landed, bf16[11,64,128]{2,1,0:T(8,128)(2,1)} %get-tuple-element.35.unread.refs_0_), custom_call_target="tpu_custom_call" | custom-call | flops 1100000 | bytes 1024 | tf_op jit(solution)/shard_map/pallas_call | solution.py:34
  59.9 3.8 %collective-permute-start.10 = (bf16[13,256,128]{2,1,0:T(8,128)(2,1)S(1)}, bf16[13,256,128]{2,1,0:T(8,128)(2,1)S(1)}, u32[]{:S(2)}, u32[]{:S(2)}) collective-permute-start(bf16[13,256,128]{2,1,0:T(8,128)(2,1)S(1)} %get-tuple-element.42), channel_id=1, source_target_pairs={{4,8},{8,4},{5,9},{9,5},{6,10},{10,6},{7,11},{11,7},{20,24},{24,20... | collective-permute-start | bytes 2555912 | tf_op jit(solution)/shard_map/ppermute | solution.py:529
  63.9 7.5 %collective-permute-done.7.refs_2_ = bf16[11,64,128]{2,1,0:T(8,128)(2,1)S(1)} collective-permute-done((bf16[11,64,128]{2,1,0:T(8,128)(2,1)}, bf16[11,64,128]{2,1,0:T(8,128)(2,1)S(1)}, u32[]{:S(2)}, u32[]{:S(2)}) %collective-permute-start.7) | collective-permute-done | bytes 180256 | tf_op jit(solution)/shard_map/ppermute | solution.py:407
  71.4 1.1 %shard_map.101 = (bf16[7,256,128]{2,1,0:T(8,128)(2,1)S(1)}, bf16[3,256,128]{2,1,0:T(8,128)(2,1)S(1)}, bf16[2,256,128]{2,1,0:T(8,128)(2,1)S(1)}, f32[32,128]{1,0:T(8,128)S(1)}, f32[8,128]{1,0:T(8,128)}) custom-call(bf16[27,256,128]{2,1,0:T(8,128)(2,1)S(1)} %get-tuple-element.36.after_ref.all_ref, f32[16,256]{1,0:T(8,128)S(1)} %bitcast.10, ...), custom_call_target="tpu_custom_call" | custom-call | flops 32999999488 | bytes 1024 | tf_op jit(solution)/shard_map/pallas_call | solution.py:34
  72.4 1.7 %collective-permute-done.10.link_ref = bf16[13,256,128]{2,1,0:T(8,128)(2,1)S(1)} collective-permute-done((bf16[13,256,128]{2,1,0:T(8,128)(2,1)S(1)}, bf16[13,256,128]{2,1,0:T(8,128)(2,1)S(1)}, u32[]{:S(2)}, u32[]{:S(2)}) %collective-permute-start.10) | collective-permute-done | bytes 852000 | tf_op jit(solution)/shard_map/ppermute | solution.py:529
  74.1 1.3 %shard_map.102.begun_ref = f32[2,256,256]{2,1,0:T(8,128)S(1)} custom-call(bf16[27,256,128]{2,1,0:T(8,128)(2,1)S(1)} %get-tuple-element.36.after_ref.all_ref, bf16[13,256,128]{2,1,0:T(8,128)(2,1)S(1)} %collective-permute-done.9.core_ref, bf16[13,256,128]{2,1,0:T(8,128)(2,1)S(1)} %collective-permute-done.10.link_ref, f32[128,128]{1,0:T(8,128)S(1)} %bitcast.7, ...), custom_call_target="tpu_custom_call" | custom-call | flops 1100000 | bytes 1024 | tf_op jit(solution)/shard_map/pallas_call | solution.py:34
  75.4 1.6 %shard_map.103 = (bf16[16,64,128]{2,1,0:T(8,128)(2,1)}, f32[8,128]{1,0:T(8,128)}) custom-call(bf16[7,256,128]{2,1,0:T(8,128)(2,1)S(1)} %get-tuple-element.40.all_ref, bf16[3,256,128]{2,1,0:T(8,128)(2,1)S(1)} %get-tuple-element.41.beside_ref, f32[128,128]{1,0:T(8,128)S(1)} %bitcast.8, f32[2,256,256]{2,1,0:T(8,128)S(1)} %shard_map.102.begun_ref, ...), custom_call_target="tpu_custom_call" | custom-call | flops 1100000 | bytes 1024 | tf_op jit(solution)/shard_map/pallas_call | solution.py:34
  76.9 6.6 %all-to-all-start.1 = ((bf16[16,64,128]{2,1,0:T(8,128)(2,1)}), bf16[16,64,128]{2,1,0:T(8,128)(2,1)S(1)}, u32[]{:S(2)}, u32[]{:S(2)}) async-start(bf16[16,64,128]{2,1,0:T(8,128)(2,1)} %get-tuple-element.47), calls=%async_computation.1 | async-start | bytes 524288 | tf_op jit(solution)/shard_map/all_to_all | solution.py:570
  83.5 7.3 %shard_map.104 = bf16[64,128,128]{2,1,0:T(8,128)(2,1)} custom-call(bf16[128,64,128]{2,1,0:T(8,128)(2,1)} %get-tuple-element.25.xt_hbm.xt_ref.last_ref.next_ref, bf16[128,64,128]{2,1,0:T(8,128)(2,1)} %get-tuple-element.25.xt_hbm.xt_ref.last_ref.next_ref, bf16[128,64,128]{2,1,0:T(8,128)(2,1)} %get-tuple-element.25.xt_hbm.xt_ref.last_ref.next_ref, ...), custom_call_target="tpu_custom_call" | custom-call | flops 1100000 | bytes 1024 | tf_op jit(solution)/shard_map/pallas_call | solution.py:34
  90.8 2.1 %all-to-all-done.1.parts_ref = bf16[16,64,128]{2,1,0:T(8,128)(2,1)S(1)} async-done(((bf16[16,64,128]{2,1,0:T(8,128)(2,1)}), bf16[16,64,128]{2,1,0:T(8,128)(2,1)S(1)}, u32[]{:S(2)}, u32[]{:S(2)}) %all-to-all-start.1) | async-done | bytes 262176 | tf_op jit(solution)/shard_map/all_to_all | solution.py:570
  92.8 0.7 shard_map.105
  (25 shorter events, 2.0 us)
Async XLA Ops:
  4.6 29.3 %collective-permute-start = (bf16[128,64,128]{2,1,0:T(8,128)(2,1)}, bf16[128,64,128]{2,1,0:T(8,128)(2,1)}, u32[]{:S(2)}, u32[]{:S(2)}) collective-permute-start(bf16[128,64,128]{2,1,0:T(8,128)(2,1)} %get-tuple-element.25.xt_hbm.xt_ref.last_ref.next_ref), channel_id=1, source_target_pairs={{0,4},{4,0},{8,12},{12,8},{1,5},{5,1},{9,13},{13,9},{2,6},{6,2},{1... | collective-permute-start | bytes 6291464 | tf_op jit(solution)/shard_map/ppermute | solution.py:442
  4.8 53.6 %all-to-all-start = ((bf16[108,64,128]{2,1,0:T(8,128)(2,1)}), bf16[108,64,128]{2,1,0:T(8,128)(2,1)}, u32[]{:S(2)}, u32[]{:S(2)}) async-start(bf16[108,64,128]{2,1,0:T(8,128)(2,1)} %get-tuple-element.33), calls=%async_computation | async-start | bytes 3538944 | tf_op jit(solution)/shard_map/all_to_all | solution.py:440
  10.8 23.1 %collective-permute-start.1 = (bf16[64,64,128]{2,1,0:T(8,128)(2,1)}, bf16[64,64,128]{2,1,0:T(8,128)(2,1)}, u32[]{:S(2)}, u32[]{:S(2)}) collective-permute-start(bf16[64,64,128]{2,1,0:T(8,128)(2,1)} %get-tuple-element.26), channel_id=1, source_target_pairs={{4,8},{8,4},{5,9},{9,5},{6,10},{10,6},{7,11},{11,7},{20,24},{24,20... | collective-permute-start | bytes 3145736 | tf_op jit(solution)/shard_map/ppermute | solution.py:441
  24.7 8.8 %collective-permute-start.2 = (bf16[16,64,128]{2,1,0:T(8,128)(2,1)}, bf16[16,64,128]{2,1,0:T(8,128)(2,1)S(1)}, u32[]{:S(2)}, u32[]{:S(2)}) collective-permute-start(bf16[16,64,128]{2,1,0:T(8,128)(2,1)} %get-tuple-element.28), channel_id=1, source_target_pairs={{0,4},{4,0},{8,12},{12,8},{1,5},{5,1},{9,13},{13,9},{2,6},{6,2},{1... | collective-permute-start | bytes 786440 | tf_op jit(solution)/shard_map/ppermute | solution.py:466
  24.7 9.2 %collective-permute-start.3 = (bf16[16,64,128]{2,1,0:T(8,128)(2,1)}, bf16[16,64,128]{2,1,0:T(8,128)(2,1)S(1)}, u32[]{:S(2)}, u32[]{:S(2)}) collective-permute-start(bf16[16,64,128]{2,1,0:T(8,128)(2,1)} %get-tuple-element.29), channel_id=1, source_target_pairs={{4,8},{8,4},{5,9},{9,5},{6,10},{10,6},{7,11},{11,7},{20,24},{24,20... | collective-permute-start | bytes 786440 | tf_op jit(solution)/shard_map/ppermute | solution.py:464
  27.0 6.4 %collective-permute-start.4 = (bf16[8,64,128]{2,1,0:T(8,128)(2,1)}, bf16[8,64,128]{2,1,0:T(8,128)(2,1)S(1)}, u32[]{:S(2)}, u32[]{:S(2)}) collective-permute-start(bf16[8,64,128]{2,1,0:T(8,128)(2,1)} %get-tuple-element.30), channel_id=1, source_target_pairs={{0,8},{4,12},{8,0},{12,4},{1,9},{5,13},{9,1},{13,5},{2,10},{6,14},... | collective-permute-start | bytes 393224 | tf_op jit(solution)/shard_map/ppermute | solution.py:465
  33.4 0.7 copy-start.5
  33.4 0.8 copy-start.3
  33.9 0.7 copy-start.4
  34.6 16.7 %collective-permute-start.5 = (bf16[64,64,128]{2,1,0:T(8,128)(2,1)}, bf16[64,64,128]{2,1,0:T(8,128)(2,1)S(1)}, u32[]{:S(2)}, u32[]{:S(2)}) collective-permute-start(bf16[64,64,128]{2,1,0:T(8,128)(2,1)} %shard_map.97), channel_id=1, source_target_pairs={{4,8},{8,4},{5,9},{9,5},{6,10},{10,6},{7,11},{11,7},{20,24},{24,20... | collective-permute-start | bytes 3145736 | tf_op jit(solution)/shard_map/ppermute | solution.py:478
  51.3 1.0 %copy-start.2 = (bf16[64,64,128]{2,1,0:T(8,128)(2,1)}, bf16[64,64,128]{2,1,0:T(8,128)(2,1)S(1)}, u32[]{:S(2)}) copy-start(bf16[64,64,128]{2,1,0:T(8,128)(2,1)S(1)} %collective-permute-done.5.late_hbm.late_ref) | copy-start | bytes 3145732
  52.3 19.0 %copy-start.1 = (f32[256,16]{0,1:T(8,128)S(1)}, f32[256,16]{0,1:T(8,128)}, u32[]{:S(2)}) copy-start(f32[256,16]{0,1:T(8,128)} %param.14) | copy-start | bytes 49156
  54.6 9.2 %collective-permute-start.6 = (bf16[11,64,128]{2,1,0:T(8,128)(2,1)}, bf16[11,64,128]{2,1,0:T(8,128)(2,1)S(1)}, u32[]{:S(2)}, u32[]{:S(2)}) collective-permute-start(bf16[11,64,128]{2,1,0:T(8,128)(2,1)} %get-tuple-element.37), channel_id=1, source_target_pairs={{0,1},{1,0},{2,3},{3,2},{4,5},{5,4},{6,7},{7,6},{8,9},{9,8},{10,11... | collective-permute-start | bytes 540680 | tf_op jit(solution)/shard_map/ppermute | solution.py:407
  56.2 15.2 %collective-permute-start.7 = (bf16[11,64,128]{2,1,0:T(8,128)(2,1)}, bf16[11,64,128]{2,1,0:T(8,128)(2,1)S(1)}, u32[]{:S(2)}, u32[]{:S(2)}) collective-permute-start(bf16[11,64,128]{2,1,0:T(8,128)(2,1)} %get-tuple-element.38), channel_id=1, source_target_pairs={{0,2},{1,3},{2,0},{3,1},{4,6},{5,7},{6,4},{7,5},{8,10},{9,11},{10,... | collective-permute-start | bytes 540680 | tf_op jit(solution)/shard_map/ppermute | solution.py:407
  57.9 13.5 %collective-permute-start.8 = (bf16[11,64,128]{2,1,0:T(8,128)(2,1)}, bf16[11,64,128]{2,1,0:T(8,128)(2,1)S(1)}, u32[]{:S(2)}, u32[]{:S(2)}) collective-permute-start(bf16[11,64,128]{2,1,0:T(8,128)(2,1)} %get-tuple-element.39), channel_id=1, source_target_pairs={{0,3},{1,2},{2,1},{3,0},{4,7},{5,6},{6,5},{7,4},{8,11},{9,10},{10,... | collective-permute-start | bytes 540680 | tf_op jit(solution)/shard_map/ppermute | solution.py:407
  59.9 14.2 %collective-permute-start.10 = (bf16[13,256,128]{2,1,0:T(8,128)(2,1)S(1)}, bf16[13,256,128]{2,1,0:T(8,128)(2,1)S(1)}, u32[]{:S(2)}, u32[]{:S(2)}) collective-permute-start(bf16[13,256,128]{2,1,0:T(8,128)(2,1)S(1)} %get-tuple-element.42), channel_id=1, source_target_pairs={{4,8},{8,4},{5,9},{9,5},{6,10},{10,6},{7,11},{11,7},{20,24},{24,20... | collective-permute-start | bytes 2555912 | tf_op jit(solution)/shard_map/ppermute | solution.py:529
  63.8 10.4 %collective-permute-start.9 = (bf16[13,256,128]{2,1,0:T(8,128)(2,1)S(1)}, bf16[13,256,128]{2,1,0:T(8,128)(2,1)S(1)}, u32[]{:S(2)}, u32[]{:S(2)}) collective-permute-start(bf16[13,256,128]{2,1,0:T(8,128)(2,1)S(1)} %get-tuple-element.42), channel_id=1, source_target_pairs={{0,4},{4,0},{8,12},{12,8},{1,5},{5,1},{9,13},{13,9},{2,6},{6,2},{1... | collective-permute-start | bytes 2555912 | tf_op jit(solution)/shard_map/ppermute | solution.py:530
  71.4 2.8 %copy-start = (f32[1,128,128]{2,1,0:T(8,128)S(1)}, f32[1,128,128]{2,1,0:T(8,128)}, u32[]{:S(2)}) copy-start(f32[1,128,128]{2,1,0:T(8,128)} %param.9) | copy-start | bytes 196612
  76.9 15.9 %all-to-all-start.1 = ((bf16[16,64,128]{2,1,0:T(8,128)(2,1)}), bf16[16,64,128]{2,1,0:T(8,128)(2,1)S(1)}, u32[]{:S(2)}, u32[]{:S(2)}) async-start(bf16[16,64,128]{2,1,0:T(8,128)(2,1)} %get-tuple-element.47), calls=%async_computation.1 | async-start | bytes 524288 | tf_op jit(solution)/shard_map/all_to_all | solution.py:570

commit v19 on v18

--- a/solution.py
+++ b/solution.py
@@ -262,12 +262,9 @@
     wait_all(sends)
 
 
-def stencil_kernel(
-    early_steps, xt_ref, last_ref, next_ref, core_ref, early_ref, late_ref, added_ref, pot_ref, ring_ref, unread,
-    out_ref,
-):
+def stencil_kernel(xt_ref, last_ref, next_ref, core_ref, link_ref, added_ref, pot_ref, ring_ref, *refs):
+    out_ref = refs[-2]
     states, here, _ = out_ref.shape
-    early = pl.program_id(0) < early_steps
 
     def line(i, rows):
         ref, at = (last_ref, 0) if i < 0 else (next_ref, 0) if i == here else (xt_ref, i)
@@ -283,8 +280,7 @@
             for i in range(ROWS):
                 y = y0 + i
                 after = line(y + 1, rows).astype(F32)
-                link = jnp.where(early, early_ref[y, rows, :], late_ref[y, rows, :]).astype(F32)
-                beside = (before + after) + (core_ref[y, rows, :].astype(F32) + link)
+                beside = (before + after) + (core_ref[y, rows, :].astype(F32) + link_ref[y, rows, :].astype(F32))
                 value = along[i * ROWS : (i + 1) * ROWS] + pot_ref[y : y + 1, :] * x
                 results.append(value + added_ref[y, rows, :] - 0.5 * beside)
                 before, x = x, after
@@ -298,7 +294,7 @@
     copy.wait()
 
 
-def later_kernel(bands, landed, unread, all_ref, pass_hbm, sems, pass_sem):
+def later_kernel(bands, landed, unread, all_ref, pass_hbm, token, sems, pass_sem):
     count, states = all_ref.shape[0], landed.shape[1]
     loads = [
         start(
@@ -313,7 +309,7 @@
     pass_half(all_ref, pass_hbm, pass_sem)
 
 
-def early_kernel(after_ref, energy_ref, *refs):
+def early_kernel(after_ref, energy_ref, unread, *refs):
     pieces, (all_ref, beside_ref, projs_ref, table_ref, token, sems) = refs[:-6], refs[-6:]
     states = pieces[0].shape[1]
     count, half, held = all_ref.shape[0] - 1, beside_ref.shape[0], projs_ref.shape[0]
@@ -494,7 +490,7 @@
             copies((4,)),
         ],
         (tile_atom, tile_line, tile_count, projectors, energy, mine, from_core, from_link, *from_far),
-        micros=8,
+        micros=18,
     )
     held = groups // bands
     built_shape = (first + first // 2 + held, states, cols_z)
@@ -516,24 +512,54 @@
     )
     early = swapped(messages, "band")
 
-    later_all, later_pass = call(
+    later_all, later_pass, later_token = call(
         32,
         functools.partial(later_kernel, bands),
         (),
         [FAR, PINNED],
-        [NEAR, FAR],
-        [((rest + 1, total_states, cols_z), BF16), ((rest // 2, total_states, cols_z), BF16)],
+        [NEAR, FAR, PINNED],
+        [((rest + 1, total_states, cols_z), BF16), ((rest // 2, total_states, cols_z), BF16), token],
         [copies((bands,)), copies],
         (landed, own_message),
     )
     later_link = lax.ppermute(later_pass, "domain", link_pairs)
     later_core = lax.ppermute(later_pass, "domain", core_pairs)
 
+    span = 2 * ROWS
+    added_far = pltpu.with_memory_space_constraint(added, pltpu.HBM)
+
+    def stencil(link_half, begin, extra):
+        steps, skip = link_half.shape[0] // span, begin // span
+        block = pl.BlockSpec((span, states, cols_z), lambda i: (i + skip, 0, 0))
+        return call(
+            62,
+            stencil_kernel,
+            (steps,),
+            [
+                block,
+                pl.BlockSpec((1, states, cols_z), lambda i: (lax.rem((i + skip) * span + lines - 1, lines), 0, 0)),
+                pl.BlockSpec((1, states, cols_z), lambda i: (lax.rem((i + skip) * span + span, lines), 0, 0)),
+                block,
+                pl.BlockSpec((span, states, cols_z), lambda i: (i, 0, 0)),
+                block,
+                pl.BlockSpec((span, cols_z), lambda i: (i + skip, 0)),
+                WHOLE,
+                PINNED,
+            ]
+            + [UNREAD] * (len(extra) - 1),
+            [pl.BlockSpec((states, span, cols_z), lambda i: (0, i + skip, 0)), PINNED],
+            [((states, lines, cols_z), BF16), token],
+            [],
+            (xt, xt, xt, core_field, link_half, added_far, pot, ring, *extra),
+            aliases={9: 0} if len(extra) > 1 else None,
+        )
+
+    applied, applied_token = stencil(link_early, 0, (later_token,))
     early_all, early_beside, projs, energy_table_here, early_token = call(
         32,
         early_kernel,
         (),
-        [NEAR, WHOLE, PINNED] + [FAR] * (bands - 1),
+        [NEAR, WHOLE, PINNED, PINNED] + [FAR] * (bands - 1),
         [NEAR, NEAR, NEAR, NEAR, PINNED],
         [
             ((first + 1, total_states, cols_z), BF16),
@@ -543,7 +569,7 @@
             token,
         ],
         [copies((3 * bands,))],
-        (later_all, energy, own_message, *early),
+        (later_all, energy, applied_token, own_message, *early),
         micros=30,
     )
     (begun,) = call(
@@ -568,34 +594,7 @@
         (early_all, early_beside, pot, begun, projs, energy_table_here),
     )
     summed = lax.all_to_all(blocks, ("domain", "band"), split_axis=0, concat_axis=0, tiled=True)
-    span = 2 * ROWS
-    steps, early_steps = lines // span, (lines - late_lines) // span
-    block = pl.BlockSpec((span, states, cols_z), lambda i: (i, 0, 0))
-    (applied,) = call(
-        60,
-        functools.partial(stencil_kernel, early_steps),
-        (steps,),
-        [
-            block,
-            pl.BlockSpec((1, states, cols_z), lambda i: (lax.rem(i * span + lines - 1, lines), 0, 0)),
-            pl.BlockSpec((1, states, cols_z), lambda i: (lax.rem(i * span + span, lines), 0, 0)),
-            block,
-            pl.BlockSpec((span, states, cols_z), lambda i: (jnp.minimum(i, early_steps - 1), 0, 0)),
-            pl.BlockSpec((span, states, cols_z), lambda i: (jnp.maximum(i - early_steps, 0), 0, 0)),
-            block,
-            pl.BlockSpec((span, cols_z), lambda i: (i, 0)),
-            WHOLE,
-            PINNED,
-        ],
-        [pl.BlockSpec((states, span, cols_z), lambda i: (0, i, 0))],
-        [((states, lines, cols_z), BF16)],
-        [],
-        (
-            xt, xt, xt, core_field, link_early, link_late, pltpu.with_memory_space_constraint(added, pltpu.HBM), pot, ring,
-            final_token,
-        ),
-    )
-
+    applied, _ = stencil(link_late, lines - late_lines, (final_token, applied))
     (subspace,) = call(
         32,
         functools.partial(result_kernel, 1.0 / (lines * cols_z * domains)),

time: 95 us -> 96.3 us (1.014)
  Pallas kernels: 41.2 us -> 45.1 us
  local copies, waits for them, and re-layouts: 1.7 us -> 0.72 us
    ppermute x3, waiting for transfers between devices: 7.5 us -> 2.28 us  [swapped(): lax.ppermute(values[k - 1], axis, [(i, i ^ k) for i in range(size)])]
    pallas_call x11 -> x12, Pallas kernels: 41.2 us -> 45.1 us  [call(): pl.pallas_call(kernel, grid=grid, out_shape=shapes, in_specs=in_specs, ou...]
    all_to_all x1, waiting for transfers between devices: 2.09 us -> 5.03 us  [local(): lax.all_to_all(blocks, ('domain', 'band'), split_axis=0, concat_axis=0, t...]
    all_to_all x1, starting transfers between devices: 6.04 us -> 4.6 us  [local(): lax.all_to_all(message, 'band', split_axis=0, concat_axis=0, tiled=True)]
    ppermute x1, starting transfers between devices: 3.33 us -> 4.5 us  [local(): link_early = lax.ppermute(early_part, 'domain', link_pairs)]
    ppermute x1, waiting for transfers between devices: 1.69 us -> 2.69 us  [local(): later_link = lax.ppermute(later_pass, 'domain', link_pairs)]
    unnamed x12 -> x10, local copies, waits for them, and re-layouts: 1.7 us -> 0.72 us
  transfers between devices with their start and end apart: 13 -> 13, of which waited for: 6 -> 6; matrix products, arithmetic and copies ran while one was open for 0% -> 0% of each run, Pallas kernels for 36% -> 38%
where the time goes in v19:
time: 96.3 us; the launch traced here: 95 us
  Pallas kernels  45.1 us (47%)
  starting transfers between devices  28.7 us (30%)
  waiting for transfers between devices  19 us (20%)
  between operations  1.42 us (1%)
    pallas_call x12, Pallas kernels, call(): pl.pallas_call(kernel, grid=grid, out_shape=shapes, in_specs=in_specs, ou...  45.1 us
    ppermute x1, waiting for transfers between devices, local(): lax.ppermute(value, 'domain', pairs)  6.34 us
    all_to_all x1, starting transfers between devices, local(): lax.all_to_all(blocks, ('domain', 'band'), split_axis=0, concat_axis=0, t...  6.29 us
    all_to_all x1, waiting for transfers between devices, local(): lax.all_to_all(blocks, ('domain', 'band'), split_axis=0, concat_axis=0, t...  5.03 us
    all_to_all x1, starting transfers between devices, local(): lax.all_to_all(message, 'band', split_axis=0, concat_axis=0, tiled=True)  4.6 us
    ppermute x1, starting transfers between devices, local(): link_early = lax.ppermute(early_part, 'domain', link_pairs)  4.5 us
    ppermute x3, starting transfers between devices, swapped(): lax.ppermute(values[k - 1], axis, [(i, i ^ k) for i in range(size)])  3.61 us
    ppermute x1, starting transfers between devices, local(): later_link = lax.ppermute(later_pass, 'domain', link_pairs)  3.53 us
  transfers between devices with their start and end apart: 13, of which 6 were waited for; matrix products, arithmetic and copies ran while one was open for 0% of the time, Pallas kernels for 38%

profile of v19, /device:TPU:1, one launch (start us, length us, event | category | flops | bytes accessed | tf_op | source)
XLA Modules:
  0.0 95.0 jit_solution(13498140062553582126)
XLA Ops:
  0.6 4.0 %shard_map.95 = (bf16[128,64,128]{2,1,0:T(8,128)(2,1)}, bf16[64,64,128]{2,1,0:T(8,128)(2,1)}, bf16[64,64,128]{2,1,0:T(8,128)(2,1)}, bf16[108,64,128]{2,1,0:T(8,128)(2,1)}) custom-call(bf16[64,128,128]{2,1,0:T(8,128)(2,1)} %bitcast.13), custom_call_target="tpu_custom_call" | custom-call | flops 1100000 | bytes 1024 | tf_op jit(solution)/shard_map/pallas_call | solution.py:34
  4.8 4.5 %collective-permute-start.4 = (bf16[64,64,128]{2,1,0:T(8,128)(2,1)}, bf16[64,64,128]{2,1,0:T(8,128)(2,1)}, u32[]{:S(2)}, u32[]{:S(2)}) collective-permute-start(bf16[64,64,128]{2,1,0:T(8,128)(2,1)} %get-tuple-element.34), channel_id=1, source_target_pairs={{4,8},{8,4},{5,9},{9,5},{6,10},{10,6},{7,11},{11,7},{20,24},{24,20... | collective-permute-start | bytes 3145736 | tf_op jit(solution)/shard_map/ppermute | solution.py:437
  9.3 4.6 %all-to-all-start = ((bf16[108,64,128]{2,1,0:T(8,128)(2,1)}), bf16[108,64,128]{2,1,0:T(8,128)(2,1)}, u32[]{:S(2)}, u32[]{:S(2)}) async-start(bf16[108,64,128]{2,1,0:T(8,128)(2,1)} %get-tuple-element.37), calls=%async_computation | async-start | bytes 3538944 | tf_op jit(solution)/shard_map/all_to_all | solution.py:436
  14.5 9.9 %shard_map.96 = (bf16[24,64,128]{2,1,0:T(8,128)(2,1)}, bf16[16,64,128]{2,1,0:T(8,128)(2,1)}, bf16[16,64,128]{2,1,0:T(8,128)(2,1)}, bf16[8,64,128]{2,1,0:T(8,128)(2,1)}) custom-call(s32[384]{0:T(512)} %atom_ref.3, s32[384]{0:T(512)} %line_ref.3, s32[1]{0:T(128)S(6)} %copy.15.count_ref, ...), custom_call_target="tpu_custom_call" | custom-call | flops 1100000 | bytes 1024 | tf_op jit(solution)/shard_map/pallas_call | solution.py:34
  24.5 2.9 %collective-permute-start.2 = (bf16[16,64,128]{2,1,0:T(8,128)(2,1)}, bf16[16,64,128]{2,1,0:T(8,128)(2,1)S(1)}, u32[]{:S(2)}, u32[]{:S(2)}) collective-permute-start(bf16[16,64,128]{2,1,0:T(8,128)(2,1)} %get-tuple-element.32), channel_id=1, source_target_pairs={{4,8},{8,4},{5,9},{9,5},{6,10},{10,6},{7,11},{11,7},{20,24},{24,20... | collective-permute-start | bytes 786440 | tf_op jit(solution)/shard_map/ppermute | solution.py:460
  27.5 6.3 %collective-permute-done.3.refs_3_.refs_0_ = bf16[8,64,128]{2,1,0:T(8,128)(2,1)S(1)} collective-permute-done((bf16[8,64,128]{2,1,0:T(8,128)(2,1)}, bf16[8,64,128]{2,1,0:T(8,128)(2,1)S(1)}, u32[]{:S(2)}, u32[]{:S(2)}) %collective-permute-start.3) | collective-permute-done | bytes 131104 | tf_op jit(solution)/shard_map/ppermute | solution.py:461
  34.9 3.0 %collective-permute-start.5 = (bf16[64,64,128]{2,1,0:T(8,128)(2,1)}, bf16[64,64,128]{2,1,0:T(8,128)(2,1)}, u32[]{:S(2)}, u32[]{:S(2)}) collective-permute-start(bf16[64,64,128]{2,1,0:T(8,128)(2,1)} %shard_map.97), channel_id=1, source_target_pairs={{4,8},{8,4},{5,9},{9,5},{6,10},{10,6},{7,11},{11,7},{20,24},{24,20... | collective-permute-start | bytes 3145736 | tf_op jit(solution)/shard_map/ppermute | solution.py:474
  37.9 11.5 %shard_map.98 = (f32[128,64,128]{2,1,0:T(8,128)}, bf16[8,64,128]{2,1,0:T(8,128)(2,1)}) custom-call(s32[384]{0:T(512)} %atom_ref.3, s32[384]{0:T(512)} %line_ref.3, s32[1]{0:T(128)S(6)} %copy.15.count_ref, bf16[384,16,128]{2,1,0:T(8,128)(2,1)} %p_hbm.3, f32[16,256]{1,0:T(8,128)} %bitcast.10, bf16[24,64,128]{2,1,0:T(8,128)(2,1)} %get-tuple-element.35.mine_hbm, ...), custom_call_target="tpu_custom_call" | custom-call | flops 19800000512 | bytes 1024 | tf_op jit(solution)/shard_map/pallas_call | solution.py:34
  49.4 2.3 %collective-permute-done.5.late_hbm.link_ref = bf16[64,64,128]{2,1,0:T(8,128)(2,1)} collective-permute-done((bf16[64,64,128]{2,1,0:T(8,128)(2,1)}, bf16[64,64,128]{2,1,0:T(8,128)(2,1)}, u32[]{:S(2)}, u32[]{:S(2)}) %collective-permute-start.5) | collective-permute-done | bytes 1048608 | tf_op jit(solution)/shard_map/ppermute | solution.py:474
  51.7 2.3 %shard_map.99 = (bf16[11,64,128]{2,1,0:T(8,128)(2,1)}, bf16[11,64,128]{2,1,0:T(8,128)(2,1)}, bf16[11,64,128]{2,1,0:T(8,128)(2,1)}, bf16[11,64,128]{2,1,0:T(8,128)(2,1)}) custom-call(bf16[128,64,128]{2,1,0:T(8,128)(2,1)} %get-tuple-element.29.xt_hbm.xt_ref.last_ref.next_ref, bf16[128,64,128]{2,1,0:T(8,128)(2,1)} %collective-permute-done.refs_5_.core_hbm.core_ref, ...), custom_call_target="tpu_custom_call" | custom-call | flops 1100000 | bytes 1024 | tf_op jit(solution)/shard_map/pallas_call | solution.py:34
  53.9 1.2 %collective-permute-start.6 = (bf16[11,64,128]{2,1,0:T(8,128)(2,1)}, bf16[11,64,128]{2,1,0:T(8,128)(2,1)S(1)}, u32[]{:S(2)}, u32[]{:S(2)}) collective-permute-start(bf16[11,64,128]{2,1,0:T(8,128)(2,1)} %get-tuple-element.43), channel_id=1, source_target_pairs={{0,1},{1,0},{2,3},{3,2},{4,5},{5,4},{6,7},{7,6},{8,9},{9,8},{10,11... | collective-permute-start | bytes 540680 | tf_op jit(solution)/shard_map/ppermute | solution.py:403
  55.2 2.4 %collective-permute-start.7 = (bf16[11,64,128]{2,1,0:T(8,128)(2,1)}, bf16[11,64,128]{2,1,0:T(8,128)(2,1)}, u32[]{:S(2)}, u32[]{:S(2)}) collective-permute-start(bf16[11,64,128]{2,1,0:T(8,128)(2,1)} %get-tuple-element.44), channel_id=1, source_target_pairs={{0,2},{1,3},{2,0},{3,1},{4,6},{5,7},{6,4},{7,5},{8,10},{9,11},{10,... | collective-permute-start | bytes 540680 | tf_op jit(solution)/shard_map/ppermute | solution.py:403
  57.6 2.4 %shard_map.100 = (bf16[27,256,128]{2,1,0:T(8,128)(2,1)S(1)}, bf16[13,256,128]{2,1,0:T(8,128)(2,1)}, f32[8,128]{1,0:T(8,128)}) custom-call(bf16[108,64,128]{2,1,0:T(8,128)(2,1)} %all-to-all-done.landed, bf16[11,64,128]{2,1,0:T(8,128)(2,1)} %get-tuple-element.39.unread.refs_0_), custom_call_target="tpu_custom_call" | custom-call | flops 1100000 | bytes 1024 | tf_op jit(solution)/shard_map/pallas_call | solution.py:34
  60.0 3.5 %collective-permute-start.10 = (bf16[13,256,128]{2,1,0:T(8,128)(2,1)}, bf16[13,256,128]{2,1,0:T(8,128)(2,1)}, u32[]{:S(2)}, u32[]{:S(2)}) collective-permute-start(bf16[13,256,128]{2,1,0:T(8,128)(2,1)} %get-tuple-element.48), channel_id=1, source_target_pairs={{4,8},{8,4},{5,9},{9,5},{6,10},{10,6},{7,11},{11,7},{20,24},{24,20... | collective-permute-start | bytes 2555912 | tf_op jit(solution)/shard_map/ppermute | solution.py:525
  63.6 4.5 %shard_map.101 = (bf16[64,128,128]{2,1,0:T(8,128)(2,1)}, f32[8,128]{1,0:T(8,128)}) custom-call(bf16[128,64,128]{2,1,0:T(8,128)(2,1)} %get-tuple-element.29.xt_hbm.xt_ref.last_ref.next_ref, bf16[128,64,128]{2,1,0:T(8,128)(2,1)} %get-tuple-element.29.xt_hbm.xt_ref.last_ref.next_ref, bf16[128,64,128]{2,1,0:T(8,128)(2,1)} %get-tuple-element.29.xt_hbm.xt_ref.last_ref.next_ref, ...), custom_call_target="tpu_custom_call" | custom-call | flops 1100000 | bytes 1024 | tf_op jit(solution)/shard_map/pallas_call | solution.py:34
  68.1 2.3 %collective-permute-done.7.refs_2_ = bf16[11,64,128]{2,1,0:T(8,128)(2,1)} collective-permute-done((bf16[11,64,128]{2,1,0:T(8,128)(2,1)}, bf16[11,64,128]{2,1,0:T(8,128)(2,1)}, u32[]{:S(2)}, u32[]{:S(2)}) %collective-permute-start.7) | collective-permute-done | bytes 180256 | tf_op jit(solution)/shard_map/ppermute | solution.py:403
  70.4 1.2 %shard_map.102 = (bf16[7,256,128]{2,1,0:T(8,128)(2,1)S(1)}, bf16[3,256,128]{2,1,0:T(8,128)(2,1)S(1)}, bf16[2,256,128]{2,1,0:T(8,128)(2,1)S(1)}, f32[32,128]{1,0:T(8,128)S(1)}, f32[8,128]{1,0:T(8,128)}) custom-call(bf16[27,256,128]{2,1,0:T(8,128)(2,1)S(1)} %get-tuple-element.40.after_ref.all_ref, f32[16,256]{1,0:T(8,128)S(1)} %bitcast.11, ...), custom_call_target="tpu_custom_call" | custom-call | flops 32999999488 | bytes 1024 | tf_op jit(solution)/shard_map/pallas_call | solution.py:34
  71.6 2.7 %collective-permute-done.10.link_ref = bf16[13,256,128]{2,1,0:T(8,128)(2,1)} collective-permute-done((bf16[13,256,128]{2,1,0:T(8,128)(2,1)}, bf16[13,256,128]{2,1,0:T(8,128)(2,1)}, u32[]{:S(2)}, u32[]{:S(2)}) %collective-permute-start.10) | collective-permute-done | bytes 852000 | tf_op jit(solution)/shard_map/ppermute | solution.py:525
  74.3 2.7 %shard_map.103.begun_ref = f32[2,256,256]{2,1,0:T(8,128)S(1)} custom-call(bf16[27,256,128]{2,1,0:T(8,128)(2,1)S(1)} %get-tuple-element.40.after_ref.all_ref, bf16[13,256,128]{2,1,0:T(8,128)(2,1)} %collective-permute-done.9.core_ref, bf16[13,256,128]{2,1,0:T(8,128)(2,1)} %collective-permute-done.10.link_ref, f32[128,128]{1,0:T(8,128)S(1)} %bitcast.8, ...), custom_call_target="tpu_custom_call" | custom-call | flops 1100000 | bytes 1024 | tf_op jit(solution)/shard_map/pallas_call | solution.py:34
  77.0 1.6 %shard_map.104 = (bf16[16,64,128]{2,1,0:T(8,128)(2,1)}, f32[8,128]{1,0:T(8,128)}) custom-call(bf16[7,256,128]{2,1,0:T(8,128)(2,1)S(1)} %get-tuple-element.46.all_ref, bf16[3,256,128]{2,1,0:T(8,128)(2,1)S(1)} %get-tuple-element.47.beside_ref, f32[128,128]{1,0:T(8,128)S(1)} %bitcast.9, f32[2,256,256]{2,1,0:T(8,128)S(1)} %shard_map.103.begun_ref, ...), custom_call_target="tpu_custom_call" | custom-call | flops 1100000 | bytes 1024 | tf_op jit(solution)/shard_map/pallas_call | solution.py:34
  78.6 6.3 %all-to-all-start.1 = ((bf16[16,64,128]{2,1,0:T(8,128)(2,1)}), bf16[16,64,128]{2,1,0:T(8,128)(2,1)S(1)}, u32[]{:S(2)}, u32[]{:S(2)}) async-start(bf16[16,64,128]{2,1,0:T(8,128)(2,1)} %get-tuple-element.55), calls=%async_computation.1 | async-start | bytes 524288 | tf_op jit(solution)/shard_map/all_to_all | solution.py:596
  84.9 4.3 %shard_map.105 = (bf16[64,128,128]{2,1,0:T(8,128)(2,1)}, f32[8,128]{1,0:T(8,128)}) custom-call(bf16[128,64,128]{2,1,0:T(8,128)(2,1)} %get-tuple-element.29.xt_hbm.xt_ref.last_ref.next_ref, bf16[128,64,128]{2,1,0:T(8,128)(2,1)} %get-tuple-element.29.xt_hbm.xt_ref.last_ref.next_ref, ...), custom_call_target="tpu_custom_call", output_to_operand_aliasing={{0}: (9, {})} | custom-call | flops 1100000 | bytes 1024 | tf_op jit(solution)/shard_map/pallas_call | solution.py:34
  89.2 5.0 %all-to-all-done.1.parts_ref = bf16[16,64,128]{2,1,0:T(8,128)(2,1)S(1)} async-done(((bf16[16,64,128]{2,1,0:T(8,128)(2,1)}), bf16[16,64,128]{2,1,0:T(8,128)(2,1)S(1)}, u32[]{:S(2)}, u32[]{:S(2)}) %all-to-all-start.1) | async-done | bytes 262176 | tf_op jit(solution)/shard_map/all_to_all | solution.py:596
  94.2 0.7 shard_map.106
  (24 shorter events, 1.5 us)
Async XLA Ops:
  4.7 29.6 %collective-permute-start = (bf16[128,64,128]{2,1,0:T(8,128)(2,1)}, bf16[128,64,128]{2,1,0:T(8,128)(2,1)}, u32[]{:S(2)}, u32[]{:S(2)}) collective-permute-start(bf16[128,64,128]{2,1,0:T(8,128)(2,1)} %get-tuple-element.29.xt_hbm.xt_ref.last_ref.next_ref), channel_id=1, source_target_pairs={{0,4},{4,0},{8,12},{12,8},{1,5},{5,1},{9,13},{13,9},{2,6},{6,2},{1... | collective-permute-start | bytes 6291464 | tf_op jit(solution)/shard_map/ppermute | solution.py:438
  4.8 29.4 %collective-permute-start.4 = (bf16[64,64,128]{2,1,0:T(8,128)(2,1)}, bf16[64,64,128]{2,1,0:T(8,128)(2,1)}, u32[]{:S(2)}, u32[]{:S(2)}) collective-permute-start(bf16[64,64,128]{2,1,0:T(8,128)(2,1)} %get-tuple-element.34), channel_id=1, source_target_pairs={{4,8},{8,4},{5,9},{9,5},{6,10},{10,6},{7,11},{11,7},{20,24},{24,20... | collective-permute-start | bytes 3145736 | tf_op jit(solution)/shard_map/ppermute | solution.py:437
  9.3 48.3 %all-to-all-start = ((bf16[108,64,128]{2,1,0:T(8,128)(2,1)}), bf16[108,64,128]{2,1,0:T(8,128)(2,1)}, u32[]{:S(2)}, u32[]{:S(2)}) async-start(bf16[108,64,128]{2,1,0:T(8,128)(2,1)} %get-tuple-element.37), calls=%async_computation | async-start | bytes 3538944 | tf_op jit(solution)/shard_map/all_to_all | solution.py:436
  24.4 9.4 %collective-permute-start.1 = (bf16[16,64,128]{2,1,0:T(8,128)(2,1)}, bf16[16,64,128]{2,1,0:T(8,128)(2,1)S(1)}, u32[]{:S(2)}, u32[]{:S(2)}) collective-permute-start(bf16[16,64,128]{2,1,0:T(8,128)(2,1)} %get-tuple-element.31), channel_id=1, source_target_pairs={{0,4},{4,0},{8,12},{12,8},{1,5},{5,1},{9,13},{13,9},{2,6},{6,2},{1... | collective-permute-start | bytes 786440 | tf_op jit(solution)/shard_map/ppermute | solution.py:462
  24.5 9.7 %collective-permute-start.2 = (bf16[16,64,128]{2,1,0:T(8,128)(2,1)}, bf16[16,64,128]{2,1,0:T(8,128)(2,1)S(1)}, u32[]{:S(2)}, u32[]{:S(2)}) collective-permute-start(bf16[16,64,128]{2,1,0:T(8,128)(2,1)} %get-tuple-element.32), channel_id=1, source_target_pairs={{4,8},{8,4},{5,9},{9,5},{6,10},{10,6},{7,11},{11,7},{20,24},{24,20... | collective-permute-start | bytes 786440 | tf_op jit(solution)/shard_map/ppermute | solution.py:460
  27.4 6.4 %collective-permute-start.3 = (bf16[8,64,128]{2,1,0:T(8,128)(2,1)}, bf16[8,64,128]{2,1,0:T(8,128)(2,1)S(1)}, u32[]{:S(2)}, u32[]{:S(2)}) collective-permute-start(bf16[8,64,128]{2,1,0:T(8,128)(2,1)} %get-tuple-element.33), channel_id=1, source_target_pairs={{0,8},{4,12},{8,0},{12,4},{1,9},{5,13},{9,1},{13,5},{2,10},{6,14},... | collective-permute-start | bytes 393224 | tf_op jit(solution)/shard_map/ppermute | solution.py:461
  33.8 0.6 copy-start.4
  33.8 0.8 copy-start.2
  34.2 0.7 copy-start.3
  34.9 16.7 %collective-permute-start.5 = (bf16[64,64,128]{2,1,0:T(8,128)(2,1)}, bf16[64,64,128]{2,1,0:T(8,128)(2,1)}, u32[]{:S(2)}, u32[]{:S(2)}) collective-permute-start(bf16[64,64,128]{2,1,0:T(8,128)(2,1)} %shard_map.97), channel_id=1, source_target_pairs={{4,8},{8,4},{5,9},{9,5},{6,10},{10,6},{7,11},{11,7},{20,24},{24,20... | collective-permute-start | bytes 3145736 | tf_op jit(solution)/shard_map/ppermute | solution.py:474
  53.9 14.2 %collective-permute-start.6 = (bf16[11,64,128]{2,1,0:T(8,128)(2,1)}, bf16[11,64,128]{2,1,0:T(8,128)(2,1)S(1)}, u32[]{:S(2)}, u32[]{:S(2)}) collective-permute-start(bf16[11,64,128]{2,1,0:T(8,128)(2,1)} %get-tuple-element.43), channel_id=1, source_target_pairs={{0,1},{1,0},{2,3},{3,2},{4,5},{5,4},{6,7},{7,6},{8,9},{9,8},{10,11... | collective-permute-start | bytes 540680 | tf_op jit(solution)/shard_map/ppermute | solution.py:403
  55.2 15.2 %collective-permute-start.7 = (bf16[11,64,128]{2,1,0:T(8,128)(2,1)}, bf16[11,64,128]{2,1,0:T(8,128)(2,1)}, u32[]{:S(2)}, u32[]{:S(2)}) collective-permute-start(bf16[11,64,128]{2,1,0:T(8,128)(2,1)} %get-tuple-element.44), channel_id=1, source_target_pairs={{0,2},{1,3},{2,0},{3,1},{4,6},{5,7},{6,4},{7,5},{8,10},{9,11},{10,... | collective-permute-start | bytes 540680 | tf_op jit(solution)/shard_map/ppermute | solution.py:403
  57.5 12.8 %collective-permute-start.8 = (bf16[11,64,128]{2,1,0:T(8,128)(2,1)}, bf16[11,64,128]{2,1,0:T(8,128)(2,1)}, u32[]{:S(2)}, u32[]{:S(2)}) collective-permute-start(bf16[11,64,128]{2,1,0:T(8,128)(2,1)} %get-tuple-element.45), channel_id=1, source_target_pairs={{0,3},{1,2},{2,1},{3,0},{4,7},{5,6},{6,5},{7,4},{8,11},{9,10},{10,... | collective-permute-start | bytes 540680 | tf_op jit(solution)/shard_map/ppermute | solution.py:403
  60.0 14.3 %collective-permute-start.10 = (bf16[13,256,128]{2,1,0:T(8,128)(2,1)}, bf16[13,256,128]{2,1,0:T(8,128)(2,1)}, u32[]{:S(2)}, u32[]{:S(2)}) collective-permute-start(bf16[13,256,128]{2,1,0:T(8,128)(2,1)} %get-tuple-element.48), channel_id=1, source_target_pairs={{4,8},{8,4},{5,9},{9,5},{6,10},{10,6},{7,11},{11,7},{20,24},{24,20... | collective-permute-start | bytes 2555912 | tf_op jit(solution)/shard_map/ppermute | solution.py:525
  63.5 10.8 %collective-permute-start.9 = (bf16[13,256,128]{2,1,0:T(8,128)(2,1)}, bf16[13,256,128]{2,1,0:T(8,128)(2,1)}, u32[]{:S(2)}, u32[]{:S(2)}) collective-permute-start(bf16[13,256,128]{2,1,0:T(8,128)(2,1)} %get-tuple-element.48), channel_id=1, source_target_pairs={{0,4},{4,0},{8,12},{12,8},{1,5},{5,1},{9,13},{13,9},{2,6},{6,2},{1... | collective-permute-start | bytes 2555912 | tf_op jit(solution)/shard_map/ppermute | solution.py:526
  63.6 6.8 %copy-start.1 = (f32[256,16]{0,1:T(8,128)S(1)}, f32[256,16]{0,1:T(8,128)}, u32[]{:S(2)}) copy-start(f32[256,16]{0,1:T(8,128)} %param.14) | copy-start | bytes 49156
  70.4 4.0 %copy-start = (f32[1,128,128]{2,1,0:T(8,128)S(1)}, f32[1,128,128]{2,1,0:T(8,128)}, u32[]{:S(2)}) copy-start(f32[1,128,128]{2,1,0:T(8,128)} %param.9) | copy-start | bytes 196612
  78.6 15.6 %all-to-all-start.1 = ((bf16[16,64,128]{2,1,0:T(8,128)(2,1)}), bf16[16,64,128]{2,1,0:T(8,128)(2,1)S(1)}, u32[]{:S(2)}, u32[]{:S(2)}) async-start(bf16[16,64,128]{2,1,0:T(8,128)(2,1)} %get-tuple-element.55), calls=%async_computation.1 | async-start | bytes 524288 | tf_op jit(solution)/shard_map/all_to_all | solution.py:596

commit v20 on v18

--- a/solution.py
+++ b/solution.py
@@ -85,7 +85,8 @@
                 block = x[s0 : s0 + ROWS, y0 : y0 + ROWS, :].astype(F32)
                 turned = jnp.swapaxes(block, 0, 1).astype(BF16)
                 xt[y0 : y0 + ROWS, s0 : s0 + ROWS, :] = turned
-        send(c * share, share, early if c < bands // 2 else late, c % (bands // 2) * share)
+        send(c * share, share // 2, early, c * (share // 2))
+        send(c * share + share // 2, share // 2, late, c * (share // 2))
         send(c * share + first, count, message, c * (count + 1))
         send(c * share, 1, message, (c + bands - 1) % bands * (count + 1) + count)
         send(c * share, share, xt_hbm, c * share)
@@ -169,12 +170,22 @@
 
 
 def nonlocal_kernel(
-    lines, fars, atom_ref, line_ref, count_ref, p_hbm, energy_ref, mine_hbm, core_ref, link_ref, *refs
+    fars, atom_ref, line_ref, count_ref, xt_hbm, beside_hbm, early_hbm, p_hbm, energy_ref, mine_hbm, core_ref, link_ref, *refs
 ):
-    far_refs, (out_hbm, whole_hbm, lines_sum, whole_ref, mine_ref, total, table, atoms, p_ref, sems) = (
-        refs[:fars],
-        refs[fars:],
-    )
+    far_refs, out_hbm, messages, scratch = refs[:fars], refs[fars], refs[fars + 1 : -13], refs[-13:]
+    lines_sum, whole_ref, mine_ref, total, table, atoms, p_ref, built, cores, links, sems, in_sems, out_sems = scratch
+    lines = xt_hbm.shape[0]
+    bands, half = cores.shape[:2]
+    share, first = lines // bands, 2 * half
+    held = built.shape[1] - first - half
+    mine = (lax.axis_index("domain") & 1) * half
+    pairs = []
+    for k in range(bands):
+        to = lax.axis_index("band") ^ k
+        pairs.append((xt_hbm.at[pl.ds(to * share, first)], built.at[k, pl.ds(0, first)]))
+        pairs.append((beside_hbm.at[pl.ds(to * share + mine, half)], cores.at[k]))
+        pairs.append((early_hbm.at[pl.ds(to * (share // 2) + mine, half)], links.at[k]))
+    brought = start_all(pairs, in_sems)
     slots, proj_count, _ = p_ref.shape
     groups, states = total.shape[0] // 3, total.shape[1]
     per_group = LANES // proj_count
@@ -205,7 +216,14 @@
             atoms[g * per_group + u] = tile[:, u * proj_count : (u + 1) * proj_count]
     for g in range(groups):
         whole_ref[g] = total[groups + g].astype(BF16)
-    sends.append(start(pltpu.make_async_copy(whole_ref, whole_hbm, sems.at[2])))
+    wait_all(brought)
+    for k, message in enumerate(messages):
+        to = lax.axis_index("band") ^ k
+        for i in range(half):
+            built[k, first + i] = (cores[k, i].astype(F32) + links[k, i].astype(F32)).astype(BF16)
+        for i in range(held):
+            built[k, first + half + i] = whole_ref[to * held + i]
+        sends.append(start(pltpu.make_async_copy(built.at[k], message, out_sems.at[k])))
     load.wait()
 
     slot_at = slot_reader(atom_ref, line_ref, count_ref, groups * per_group)
@@ -223,51 +241,16 @@
     wait_all(sends)
 
 
-def second_kernel(share, xt_hbm, core_hbm, early_hbm, late_hbm, whole_hbm, *refs):
-    messages, (built, cores, links, in_sems, out_sems) = refs[:-5], refs[-5:]
-    bands = len(messages)
-    half = cores.shape[1]
-    first = 2 * half
-    held = built.shape[1] - first - half
-    early_lines = early_hbm.shape[0]
-    mine = (lax.axis_index("domain") & 1) * half
-    loads = []
-
-    def load(source, target):
-        loads.append(start(pltpu.make_async_copy(source, target, in_sems.at[len(loads)])))
-
-    for k in range(bands):
-        to = lax.axis_index("band") ^ k
-        begin = to * share
-        load(xt_hbm.at[pl.ds(begin, first)], built.at[k, pl.ds(0, first)])
-        load(whole_hbm.at[pl.ds(to * held, held)], built.at[k, pl.ds(first + half, held)])
-        load(core_hbm.at[pl.ds(begin + mine, half)], cores.at[k])
-        sem = in_sems.at[len(loads)]
-
-        @pl.when(begin < early_lines)
-        def _():
-            pltpu.make_async_copy(early_hbm.at[pl.ds(begin + mine, half)], links.at[k], sem).start()
-
-        @pl.when(begin >= early_lines)
-        def _():
-            pltpu.make_async_copy(late_hbm.at[pl.ds(begin + mine - early_lines, half)], links.at[k], sem).start()
-
-        loads.append(pltpu.make_async_copy(early_hbm.at[pl.ds(0, half)], links.at[k], sem))
-    wait_all(loads)
-    sends = []
-    for k, message in enumerate(messages):
-        for i in range(half):
-            built[k, first + i] = (cores[k, i].astype(F32) + links[k, i].astype(F32)).astype(BF16)
-        sends.append(start(pltpu.make_async_copy(built.at[k], message, out_sems.at[k])))
-    wait_all(sends)
-
-
 def stencil_kernel(
-    early_steps, xt_ref, last_ref, next_ref, core_ref, early_ref, late_ref, added_ref, pot_ref, ring_ref, unread,
+    share, xt_ref, last_ref, next_ref, core_ref, early_ref, late_ref, added_ref, pot_ref, ring_ref, unread,
     out_ref,
 ):
     states, here, _ = out_ref.shape
-    early = pl.program_id(0) < early_steps
+
+    def link(i, rows):
+        chunk, at = divmod(i, share)
+        ref = early_ref if at < share // 2 else late_ref
+        return ref[chunk * (share // 2) + at % (share // 2), rows, :]
 
     def line(i, rows):
         ref, at = (last_ref, 0) if i < 0 else (next_ref, 0) if i == here else (xt_ref, i)
@@ -283,8 +266,7 @@
             for i in range(ROWS):
                 y = y0 + i
                 after = line(y + 1, rows).astype(F32)
-                link = jnp.where(early, early_ref[y, rows, :], late_ref[y, rows, :]).astype(F32)
-                beside = (before + after) + (core_ref[y, rows, :].astype(F32) + link)
+                beside = (before + after) + (core_ref[y, rows, :].astype(F32) + link(y, rows).astype(F32))
                 value = along[i * ROWS : (i + 1) * ROWS] + pot_ref[y : y + 1, :] * x
                 results.append(value + added_ref[y, rows, :] - 0.5 * beside)
                 before, x = x, after
@@ -433,7 +415,7 @@
             pltpu.VMEM((states, lines, cols_z), BF16),
             pltpu.VMEM(line_shape, BF16),
             copies((bands,)),
-            copies((4 * bands,)),
+            copies((5 * bands,)),
         ],
         (field,),
     )
@@ -465,7 +447,7 @@
     from_far = [lax.ppermute(value, "domain", pairs) for value, pairs in zip(to_far, far_pairs)]
     from_core = lax.ppermute(to_core, "domain", core_pairs)
     (late_part,) = call(
-        63,
+        56,
         hand_on,
         (),
         [UNREAD] * (5 + len(far_pairs)),
@@ -476,13 +458,16 @@
         aliases={0: 0},
     )
     link_late = lax.ppermute(late_part, "domain", link_pairs)
-    added, whole = call(
+    held = groups // bands
+    built_shape = (first + first // 2 + held, states, cols_z)
+    beside_shape = (bands, first // 2, states, cols_z)
+    added, own_message, *messages = call(
         62,
-        functools.partial(nonlocal_kernel, lines, len(far_pairs)),
-        (),
-        [SCALARS] * 3 + [PINNED, WHOLE, PINNED, WHOLE, WHOLE] + [WHOLE] * len(far_pairs),
-        [PINNED, PINNED],
-        [(line_shape, F32), (group_shape, BF16)],
+        functools.partial(nonlocal_kernel, len(far_pairs)),
+        (),
+        [SCALARS] * 3 + [FAR] * 3 + [PINNED, WHOLE, PINNED, WHOLE, WHOLE] + [WHOLE] * len(far_pairs),
+        [PINNED, PINNED] + [FAR] * (bands - 1),
+        [(line_shape, F32)] + [(built_shape, BF16)] * bands,
         [
             pltpu.VMEM((lines + 1, states, cols_z), F32),
             pltpu.VMEM(group_shape, BF16),
@@ -491,28 +476,18 @@
             pltpu.VMEM(energy_rows, F32),
             pltpu.VMEM((3 * atoms_here, states, proj_count), BF16),
             pltpu.VMEM(projectors.shape, BF16),
+            pltpu.VMEM((bands, *built_shape), BF16),
+            pltpu.VMEM(beside_shape, BF16),
+            pltpu.VMEM(beside_shape, BF16),
             copies((4,)),
-        ],
-        (tile_atom, tile_line, tile_count, projectors, energy, mine, from_core, from_link, *from_far),
-        micros=8,
-    )
-    held = groups // bands
-    built_shape = (first + first // 2 + held, states, cols_z)
-    own_message, *messages = call(
-        63,
-        functools.partial(second_kernel, share),
-        (),
-        [FAR] * 4 + [PINNED],
-        [PINNED] + [FAR] * (bands - 1),
-        [(built_shape, BF16)] * bands,
-        [
-            pltpu.VMEM((bands, *built_shape), BF16),
-            pltpu.VMEM((bands, first // 2, states, cols_z), BF16),
-            pltpu.VMEM((bands, first // 2, states, cols_z), BF16),
-            copies((4 * bands,)),
+            copies((3 * bands,)),
             copies((bands,)),
         ],
-        (xt, core_field, link_early, link_late, whole),
+        (
+            tile_atom, tile_line, tile_count, xt, core_field, link_early, projectors, energy, mine, from_core,
+            from_link, *from_far,
+        ),
+        micros=8,
     )
     early = swapped(messages, "band")
 
@@ -569,19 +544,19 @@
     )
     summed = lax.all_to_all(blocks, ("domain", "band"), split_axis=0, concat_axis=0, tiled=True)
     span = 2 * ROWS
-    steps, early_steps = lines // span, (lines - late_lines) // span
+    steps = lines // span
     block = pl.BlockSpec((span, states, cols_z), lambda i: (i, 0, 0))
     (applied,) = call(
         60,
-        functools.partial(stencil_kernel, early_steps),
+        functools.partial(stencil_kernel, share),
         (steps,),
         [
             block,
             pl.BlockSpec((1, states, cols_z), lambda i: (lax.rem(i * span + lines - 1, lines), 0, 0)),
             pl.BlockSpec((1, states, cols_z), lambda i: (lax.rem(i * span + span, lines), 0, 0)),
             block,
-            pl.BlockSpec((span, states, cols_z), lambda i: (jnp.minimum(i, early_steps - 1), 0, 0)),
-            pl.BlockSpec((span, states, cols_z), lambda i: (jnp.maximum(i - early_steps, 0), 0, 0)),
+            pl.BlockSpec((span // 2, states, cols_z), lambda i: (i, 0, 0)),
+            pl.BlockSpec((span // 2, states, cols_z), lambda i: (i, 0, 0)),
             block,
             pl.BlockSpec((span, cols_z), lambda i: (i, 0)),
             WHOLE,

time: 95 us -> 97.6 us (1.027)
  waiting for transfers between devices: 19.9 us -> 24.5 us
  Pallas kernels: 41.2 us -> 39.3 us
    ppermute x1, waiting for transfers between devices: 1.69 us -> 14.3 us  [local(): later_link = lax.ppermute(later_pass, 'domain', link_pairs)]
    ppermute x3, waiting for transfers between devices: 7.5 us -> 2.28 us  [swapped(): lax.ppermute(values[k - 1], axis, [(i, i ^ k) for i in range(size)])]
    ppermute x1, starting transfers between devices: 3.82 us -> 1.92 us  [local(): later_link = lax.ppermute(later_pass, 'domain', link_pairs)]
    pallas_call x11 -> x10, Pallas kernels: 41.2 us -> 39.3 us  [call(): pl.pallas_call(kernel, grid=grid, out_shape=shapes, in_specs=in_specs, ou...]
    ppermute x1, waiting for transfers between devices: 1.75 us -> 0.01 us  [local(): link_late = lax.ppermute(late_part, 'domain', link_pairs)]
    all_to_all x1, waiting for transfers between devices: 2.09 us -> 1.05 us  [local(): lax.all_to_all(blocks, ('domain', 'band'), split_axis=0, concat_axis=0, t...]
  transfers between devices with their start and end apart: 13 -> 13, of which waited for: 6 -> 5; matrix products, arithmetic and copies ran while one was open for 0% -> 0% of each run, Pallas kernels for 36% -> 36%
where the time goes in v20:
time: 97.6 us; the launch traced here: 96.3 us
  Pallas kernels  39.3 us (40%)
  starting transfers between devices  29.2 us (30%)
  waiting for transfers between devices  24.5 us (25%)
  local copies, waits for them, and re-layouts  1.79 us (2%)
  between operations  1.41 us (1%)
    pallas_call x10, Pallas kernels, call(): pl.pallas_call(kernel, grid=grid, out_shape=shapes, in_specs=in_specs, ou...  39.3 us
    ppermute x1, waiting for transfers between devices, local(): later_link = lax.ppermute(later_pass, 'domain', link_pairs)  14.3 us
    all_to_all x1, starting transfers between devices, local(): lax.all_to_all(blocks, ('domain', 'band'), split_axis=0, concat_axis=0, t...  6.49 us
    ppermute x1, waiting for transfers between devices, local(): lax.ppermute(value, 'domain', pairs)  6.34 us
    all_to_all x1, starting transfers between devices, local(): lax.all_to_all(message, 'band', split_axis=0, concat_axis=0, tiled=True)  6.04 us
    ppermute x1, starting transfers between devices, local(): link_late = lax.ppermute(late_part, 'domain', link_pairs)  4.25 us
    ppermute x3, starting transfers between devices, swapped(): lax.ppermute(values[k - 1], axis, [(i, i ^ k) for i in range(size)])  4.08 us
    ppermute x1, starting transfers between devices, local(): link_early = lax.ppermute(early_part, 'domain', link_pairs)  3.33 us
  transfers between devices with their start and end apart: 13, of which 5 were waited for; matrix products, arithmetic and copies ran while one was open for 0% of the time, Pallas kernels for 36%

profile of v20, /device:TPU:1, one launch (start us, length us, event | category | flops | bytes accessed | tf_op | source)
XLA Modules:
  0.0 96.3 jit_solution(17182819991443085671)
XLA Ops:
  0.6 4.0 %shard_map.95 = (bf16[128,64,128]{2,1,0:T(8,128)(2,1)}, bf16[64,64,128]{2,1,0:T(8,128)(2,1)}, bf16[64,64,128]{2,1,0:T(8,128)(2,1)}, bf16[108,64,128]{2,1,0:T(8,128)(2,1)}) custom-call(bf16[64,128,128]{2,1,0:T(8,128)(2,1)} %bitcast.12), custom_call_target="tpu_custom_call" | custom-call | flops 1100000 | bytes 1024 | tf_op jit(solution)/shard_map/pallas_call | solution.py:34
  4.8 6.0 %all-to-all-start = ((bf16[108,64,128]{2,1,0:T(8,128)(2,1)}), bf16[108,64,128]{2,1,0:T(8,128)(2,1)}, u32[]{:S(2)}, u32[]{:S(2)}) async-start(bf16[108,64,128]{2,1,0:T(8,128)(2,1)} %get-tuple-element.32), calls=%async_computation | async-start | bytes 3538944 | tf_op jit(solution)/shard_map/all_to_all | solution.py:422
  10.8 3.3 %collective-permute-start.1 = (bf16[64,64,128]{2,1,0:T(8,128)(2,1)}, bf16[64,64,128]{2,1,0:T(8,128)(2,1)}, u32[]{:S(2)}, u32[]{:S(2)}) collective-permute-start(bf16[64,64,128]{2,1,0:T(8,128)(2,1)} %get-tuple-element.25), channel_id=1, source_target_pairs={{4,8},{8,4},{5,9},{9,5},{6,10},{10,6},{7,11},{11,7},{20,24},{24,20... | collective-permute-start | bytes 3145736 | tf_op jit(solution)/shard_map/ppermute | solution.py:423
  14.8 9.9 %shard_map.96 = (bf16[24,64,128]{2,1,0:T(8,128)(2,1)}, bf16[16,64,128]{2,1,0:T(8,128)(2,1)}, bf16[16,64,128]{2,1,0:T(8,128)(2,1)}, bf16[8,64,128]{2,1,0:T(8,128)(2,1)}) custom-call(s32[384]{0:T(512)} %atom_ref.3, s32[384]{0:T(512)} %line_ref.3, s32[1]{0:T(128)S(6)} %copy.13.count_ref, ...), custom_call_target="tpu_custom_call" | custom-call | flops 1100000 | bytes 1024 | tf_op jit(solution)/shard_map/pallas_call | solution.py:34
  24.8 2.3 %collective-permute-start.3 = (bf16[16,64,128]{2,1,0:T(8,128)(2,1)}, bf16[16,64,128]{2,1,0:T(8,128)(2,1)S(1)}, u32[]{:S(2)}, u32[]{:S(2)}) collective-permute-start(bf16[16,64,128]{2,1,0:T(8,128)(2,1)} %get-tuple-element.28), channel_id=1, source_target_pairs={{4,8},{8,4},{5,9},{9,5},{6,10},{10,6},{7,11},{11,7},{20,24},{24,20... | collective-permute-start | bytes 786440 | tf_op jit(solution)/shard_map/ppermute | solution.py:446
  27.2 6.3 %collective-permute-done.4.refs_3_.refs_0_ = bf16[8,64,128]{2,1,0:T(8,128)(2,1)S(1)} collective-permute-done((bf16[8,64,128]{2,1,0:T(8,128)(2,1)}, bf16[8,64,128]{2,1,0:T(8,128)(2,1)S(1)}, u32[]{:S(2)}, u32[]{:S(2)}) %collective-permute-start.4) | collective-permute-done | bytes 131104 | tf_op jit(solution)/shard_map/ppermute | solution.py:447
  34.7 12.0 %shard_map.98 = (f32[128,64,128]{2,1,0:T(8,128)}, bf16[11,64,128]{2,1,0:T(8,128)(2,1)}, bf16[11,64,128]{2,1,0:T(8,128)(2,1)}, bf16[11,64,128]{2,1,0:T(8,128)(2,1)}, bf16[11,64,128]{2,1,0:T(8,128)(2,1)}) custom-call(s32[384]{0:T(512)} %atom_ref.3, s32[384]{0:T(512)} %line_ref.3, s32[1]{0:T(128)S(6)} %copy.13.count_ref, ...), custom_call_target="tpu_custom_call" | custom-call | flops 8800000000 | bytes 1024 | tf_op jit(solution)/shard_map/pallas_call | solution.py:34
  46.7 1.9 %collective-permute-start.6 = (bf16[11,64,128]{2,1,0:T(8,128)(2,1)}, bf16[11,64,128]{2,1,0:T(8,128)(2,1)S(1)}, u32[]{:S(2)}, u32[]{:S(2)}) collective-permute-start(bf16[11,64,128]{2,1,0:T(8,128)(2,1)} %get-tuple-element.35), channel_id=1, source_target_pairs={{0,1},{1,0},{2,3},{3,2},{4,5},{5,4},{6,7},{7,6},{8,9},{9,8},{10,11... | collective-permute-start | bytes 540680 | tf_op jit(solution)/shard_map/ppermute | solution.py:389
  48.6 1.7 %collective-permute-start.7 = (bf16[11,64,128]{2,1,0:T(8,128)(2,1)}, bf16[11,64,128]{2,1,0:T(8,128)(2,1)S(1)}, u32[]{:S(2)}, u32[]{:S(2)}) collective-permute-start(bf16[11,64,128]{2,1,0:T(8,128)(2,1)} %get-tuple-element.36), channel_id=1, source_target_pairs={{0,2},{1,3},{2,0},{3,1},{4,6},{5,7},{6,4},{7,5},{8,10},{9,11},{10,... | collective-permute-start | bytes 540680 | tf_op jit(solution)/shard_map/ppermute | solution.py:389
  50.3 0.5 collective-permute-start.8
  50.8 4.3 %collective-permute-start.5 = (bf16[64,64,128]{2,1,0:T(8,128)(2,1)}, bf16[64,64,128]{2,1,0:T(8,128)(2,1)S(1)}, u32[]{:S(2)}, u32[]{:S(2)}) collective-permute-start(bf16[64,64,128]{2,1,0:T(8,128)(2,1)} %shard_map.97), channel_id=1, source_target_pairs={{4,8},{8,4},{5,9},{9,5},{6,10},{10,6},{7,11},{11,7},{20,24},{24,20... | collective-permute-start | bytes 3145736 | tf_op jit(solution)/shard_map/ppermute | solution.py:460
  55.1 1.6 %shard_map.99 = (bf16[27,256,128]{2,1,0:T(8,128)(2,1)S(1)}, bf16[13,256,128]{2,1,0:T(8,128)(2,1)S(1)}) custom-call(bf16[108,64,128]{2,1,0:T(8,128)(2,1)} %all-to-all-done.landed, bf16[11,64,128]{2,1,0:T(8,128)(2,1)} %get-tuple-element.33.unread.refs_0_), custom_call_target="tpu_custom_call" | custom-call | flops 1100000 | bytes 1024 | tf_op jit(solution)/shard_map/pallas_call | solution.py:34
  56.7 1.9 %collective-permute-start.10 = (bf16[13,256,128]{2,1,0:T(8,128)(2,1)S(1)}, bf16[13,256,128]{2,1,0:T(8,128)(2,1)S(1)}, u32[]{:S(2)}, u32[]{:S(2)}) collective-permute-start(bf16[13,256,128]{2,1,0:T(8,128)(2,1)S(1)} %get-tuple-element.40), channel_id=1, source_target_pairs={{4,8},{8,4},{5,9},{9,5},{6,10},{10,6},{7,11},{11,7},{20,24},{24,20... | collective-permute-start | bytes 2555912 | tf_op jit(solution)/shard_map/ppermute | solution.py:504
  58.6 2.3 %collective-permute-done.6.refs_1_ = bf16[11,64,128]{2,1,0:T(8,128)(2,1)S(1)} collective-permute-done((bf16[11,64,128]{2,1,0:T(8,128)(2,1)}, bf16[11,64,128]{2,1,0:T(8,128)(2,1)S(1)}, u32[]{:S(2)}, u32[]{:S(2)}) %collective-permute-start.6) | collective-permute-done | bytes 180256 | tf_op jit(solution)/shard_map/ppermute | solution.py:389
  60.9 0.6 collective-permute-start.9
  61.5 1.1 %shard_map.100 = (bf16[7,256,128]{2,1,0:T(8,128)(2,1)S(1)}, bf16[3,256,128]{2,1,0:T(8,128)(2,1)S(1)}, bf16[2,256,128]{2,1,0:T(8,128)(2,1)S(1)}, f32[32,128]{1,0:T(8,128)S(1)}, f32[8,128]{1,0:T(8,128)}) custom-call(bf16[27,256,128]{2,1,0:T(8,128)(2,1)S(1)} %get-tuple-element.34.after_ref.all_ref, f32[16,256]{1,0:T(8,128)S(1)} %bitcast.10, ...), custom_call_target="tpu_custom_call" | custom-call | flops 32999999488 | bytes 1024 | tf_op jit(solution)/shard_map/pallas_call | solution.py:34
  62.6 14.3 %collective-permute-done.10.link_ref = bf16[13,256,128]{2,1,0:T(8,128)(2,1)S(1)} collective-permute-done((bf16[13,256,128]{2,1,0:T(8,128)(2,1)S(1)}, bf16[13,256,128]{2,1,0:T(8,128)(2,1)S(1)}, u32[]{:S(2)}, u32[]{:S(2)}) %collective-permute-start.10) | collective-permute-done | bytes 852000 | tf_op jit(solution)/shard_map/ppermute | solution.py:504
  76.9 1.3 %shard_map.101.begun_ref = f32[2,256,256]{2,1,0:T(8,128)S(1)} custom-call(bf16[27,256,128]{2,1,0:T(8,128)(2,1)S(1)} %get-tuple-element.34.after_ref.all_ref, bf16[13,256,128]{2,1,0:T(8,128)(2,1)S(1)} %collective-permute-done.9.core_ref, bf16[13,256,128]{2,1,0:T(8,128)(2,1)S(1)} %collective-permute-done.10.link_ref, f32[128,128]{1,0:T(8,128)S(1)} %bitcast.7, ...), custom_call_target="tpu_custom_call" | custom-call | flops 1100000 | bytes 1024 | tf_op jit(solution)/shard_map/pallas_call | solution.py:34
  78.1 1.5 %shard_map.102 = (bf16[16,64,128]{2,1,0:T(8,128)(2,1)}, f32[8,128]{1,0:T(8,128)}) custom-call(bf16[7,256,128]{2,1,0:T(8,128)(2,1)S(1)} %get-tuple-element.38.all_ref, bf16[3,256,128]{2,1,0:T(8,128)(2,1)S(1)} %get-tuple-element.39.beside_ref, f32[128,128]{1,0:T(8,128)S(1)} %bitcast.8, f32[2,256,256]{2,1,0:T(8,128)S(1)} %shard_map.101.begun_ref, ...), custom_call_target="tpu_custom_call" | custom-call | flops 1100000 | bytes 1024 | tf_op jit(solution)/shard_map/pallas_call | solution.py:34
  79.7 6.5 %all-to-all-start.1 = ((bf16[16,64,128]{2,1,0:T(8,128)(2,1)}), bf16[16,64,128]{2,1,0:T(8,128)(2,1)S(1)}, u32[]{:S(2)}, u32[]{:S(2)}) async-start(bf16[16,64,128]{2,1,0:T(8,128)(2,1)} %get-tuple-element.45), calls=%async_computation.1 | async-start | bytes 524288 | tf_op jit(solution)/shard_map/all_to_all | solution.py:545
  86.2 1.1 %copy-done.2 = bf16[64,64,128]{2,1,0:T(8,128)(2,1)} copy-done((bf16[64,64,128]{2,1,0:T(8,128)(2,1)}, bf16[64,64,128]{2,1,0:T(8,128)(2,1)S(1)}, u32[]{:S(2)}) %copy-start.2) | copy-done | bytes 1048600
  87.2 7.2 %shard_map.103 = bf16[64,128,128]{2,1,0:T(8,128)(2,1)} custom-call(bf16[128,64,128]{2,1,0:T(8,128)(2,1)} %get-tuple-element.24.xt_hbm.xt_ref.last_ref.next_ref, bf16[128,64,128]{2,1,0:T(8,128)(2,1)} %get-tuple-element.24.xt_hbm.xt_ref.last_ref.next_ref, bf16[128,64,128]{2,1,0:T(8,128)(2,1)} %get-tuple-element.24.xt_hbm.xt_ref.last_ref.next_ref, ...), custom_call_target="tpu_custom_call" | custom-call | flops 1100000 | bytes 1024 | tf_op jit(solution)/shard_map/pallas_call | solution.py:34
  94.5 1.1 %all-to-all-done.1.parts_ref = bf16[16,64,128]{2,1,0:T(8,128)(2,1)S(1)} async-done(((bf16[16,64,128]{2,1,0:T(8,128)(2,1)}), bf16[16,64,128]{2,1,0:T(8,128)(2,1)S(1)}, u32[]{:S(2)}, u32[]{:S(2)}) %all-to-all-start.1) | async-done | bytes 262176 | tf_op jit(solution)/shard_map/all_to_all | solution.py:545
  95.5 0.7 shard_map.104
  (24 shorter events, 1.5 us)
Async XLA Ops:
  4.7 29.3 %collective-permute-start = (bf16[128,64,128]{2,1,0:T(8,128)(2,1)}, bf16[128,64,128]{2,1,0:T(8,128)(2,1)}, u32[]{:S(2)}, u32[]{:S(2)}) collective-permute-start(bf16[128,64,128]{2,1,0:T(8,128)(2,1)} %get-tuple-element.24.xt_hbm.xt_ref.last_ref.next_ref), channel_id=1, source_target_pairs={{0,4},{4,0},{8,12},{12,8},{1,5},{5,1},{9,13},{13,9},{2,6},{6,2},{1... | collective-permute-start | bytes 6291464 | tf_op jit(solution)/shard_map/ppermute | solution.py:424
  4.8 50.3 %all-to-all-start = ((bf16[108,64,128]{2,1,0:T(8,128)(2,1)}), bf16[108,64,128]{2,1,0:T(8,128)(2,1)}, u32[]{:S(2)}, u32[]{:S(2)}) async-start(bf16[108,64,128]{2,1,0:T(8,128)(2,1)} %get-tuple-element.32), calls=%async_computation | async-start | bytes 3538944 | tf_op jit(solution)/shard_map/all_to_all | solution.py:422
  10.8 23.2 %collective-permute-start.1 = (bf16[64,64,128]{2,1,0:T(8,128)(2,1)}, bf16[64,64,128]{2,1,0:T(8,128)(2,1)}, u32[]{:S(2)}, u32[]{:S(2)}) collective-permute-start(bf16[64,64,128]{2,1,0:T(8,128)(2,1)} %get-tuple-element.25), channel_id=1, source_target_pairs={{4,8},{8,4},{5,9},{9,5},{6,10},{10,6},{7,11},{11,7},{20,24},{24,20... | collective-permute-start | bytes 3145736 | tf_op jit(solution)/shard_map/ppermute | solution.py:423
  24.7 8.8 %collective-permute-start.2 = (bf16[16,64,128]{2,1,0:T(8,128)(2,1)}, bf16[16,64,128]{2,1,0:T(8,128)(2,1)S(1)}, u32[]{:S(2)}, u32[]{:S(2)}) collective-permute-start(bf16[16,64,128]{2,1,0:T(8,128)(2,1)} %get-tuple-element.27), channel_id=1, source_target_pairs={{0,4},{4,0},{8,12},{12,8},{1,5},{5,1},{9,13},{13,9},{2,6},{6,2},{1... | collective-permute-start | bytes 786440 | tf_op jit(solution)/shard_map/ppermute | solution.py:448
  24.8 9.2 %collective-permute-start.3 = (bf16[16,64,128]{2,1,0:T(8,128)(2,1)}, bf16[16,64,128]{2,1,0:T(8,128)(2,1)S(1)}, u32[]{:S(2)}, u32[]{:S(2)}) collective-permute-start(bf16[16,64,128]{2,1,0:T(8,128)(2,1)} %get-tuple-element.28), channel_id=1, source_target_pairs={{4,8},{8,4},{5,9},{9,5},{6,10},{10,6},{7,11},{11,7},{20,24},{24,20... | collective-permute-start | bytes 786440 | tf_op jit(solution)/shard_map/ppermute | solution.py:446
  27.1 6.4 %collective-permute-start.4 = (bf16[8,64,128]{2,1,0:T(8,128)(2,1)}, bf16[8,64,128]{2,1,0:T(8,128)(2,1)S(1)}, u32[]{:S(2)}, u32[]{:S(2)}) collective-permute-start(bf16[8,64,128]{2,1,0:T(8,128)(2,1)} %get-tuple-element.29), channel_id=1, source_target_pairs={{0,8},{4,12},{8,0},{12,4},{1,9},{5,13},{9,1},{13,5},{2,10},{6,14},... | collective-permute-start | bytes 393224 | tf_op jit(solution)/shard_map/ppermute | solution.py:447
  33.5 0.7 copy-start.5
  33.5 0.8 copy-start.3
  34.0 0.7 copy-start.4
  46.7 14.2 %collective-permute-start.6 = (bf16[11,64,128]{2,1,0:T(8,128)(2,1)}, bf16[11,64,128]{2,1,0:T(8,128)(2,1)S(1)}, u32[]{:S(2)}, u32[]{:S(2)}) collective-permute-start(bf16[11,64,128]{2,1,0:T(8,128)(2,1)} %get-tuple-element.35), channel_id=1, source_target_pairs={{0,1},{1,0},{2,3},{3,2},{4,5},{5,4},{6,7},{7,6},{8,9},{9,8},{10,11... | collective-permute-start | bytes 540680 | tf_op jit(solution)/shard_map/ppermute | solution.py:389
  48.6 12.8 %collective-permute-start.7 = (bf16[11,64,128]{2,1,0:T(8,128)(2,1)}, bf16[11,64,128]{2,1,0:T(8,128)(2,1)S(1)}, u32[]{:S(2)}, u32[]{:S(2)}) collective-permute-start(bf16[11,64,128]{2,1,0:T(8,128)(2,1)} %get-tuple-element.36), channel_id=1, source_target_pairs={{0,2},{1,3},{2,0},{3,1},{4,6},{5,7},{6,4},{7,5},{8,10},{9,11},{10,... | collective-permute-start | bytes 540680 | tf_op jit(solution)/shard_map/ppermute | solution.py:389
  50.3 11.2 %collective-permute-start.8 = (bf16[11,64,128]{2,1,0:T(8,128)(2,1)}, bf16[11,64,128]{2,1,0:T(8,128)(2,1)S(1)}, u32[]{:S(2)}, u32[]{:S(2)}) collective-permute-start(bf16[11,64,128]{2,1,0:T(8,128)(2,1)} %get-tuple-element.37), channel_id=1, source_target_pairs={{0,3},{1,2},{2,1},{3,0},{4,7},{5,6},{6,5},{7,4},{8,11},{9,10},{10,... | collective-permute-start | bytes 540680 | tf_op jit(solution)/shard_map/ppermute | solution.py:389
  50.8 10.7 %copy-start.1 = (f32[256,16]{0,1:T(8,128)S(1)}, f32[256,16]{0,1:T(8,128)}, u32[]{:S(2)}) copy-start(f32[256,16]{0,1:T(8,128)} %param.14) | copy-start | bytes 49156
  50.8 35.4 %collective-permute-start.5 = (bf16[64,64,128]{2,1,0:T(8,128)(2,1)}, bf16[64,64,128]{2,1,0:T(8,128)(2,1)S(1)}, u32[]{:S(2)}, u32[]{:S(2)}) collective-permute-start(bf16[64,64,128]{2,1,0:T(8,128)(2,1)} %shard_map.97), channel_id=1, source_target_pairs={{4,8},{8,4},{5,9},{9,5},{6,10},{10,6},{7,11},{11,7},{20,24},{24,20... | collective-permute-start | bytes 3145736 | tf_op jit(solution)/shard_map/ppermute | solution.py:460
  56.7 20.2 %collective-permute-start.10 = (bf16[13,256,128]{2,1,0:T(8,128)(2,1)S(1)}, bf16[13,256,128]{2,1,0:T(8,128)(2,1)S(1)}, u32[]{:S(2)}, u32[]{:S(2)}) collective-permute-start(bf16[13,256,128]{2,1,0:T(8,128)(2,1)S(1)} %get-tuple-element.40), channel_id=1, source_target_pairs={{4,8},{8,4},{5,9},{9,5},{6,10},{10,6},{7,11},{11,7},{20,24},{24,20... | collective-permute-start | bytes 2555912 | tf_op jit(solution)/shard_map/ppermute | solution.py:504
  60.9 16.0 %collective-permute-start.9 = (bf16[13,256,128]{2,1,0:T(8,128)(2,1)S(1)}, bf16[13,256,128]{2,1,0:T(8,128)(2,1)S(1)}, u32[]{:S(2)}, u32[]{:S(2)}) collective-permute-start(bf16[13,256,128]{2,1,0:T(8,128)(2,1)S(1)} %get-tuple-element.40), channel_id=1, source_target_pairs={{0,4},{4,0},{8,12},{12,8},{1,5},{5,1},{9,13},{13,9},{2,6},{6,2},{1... | collective-permute-start | bytes 2555912 | tf_op jit(solution)/shard_map/ppermute | solution.py:505
  61.5 15.4 %copy-start = (f32[1,128,128]{2,1,0:T(8,128)S(1)}, f32[1,128,128]{2,1,0:T(8,128)}, u32[]{:S(2)}) copy-start(f32[1,128,128]{2,1,0:T(8,128)} %param.9) | copy-start | bytes 196612
  79.7 15.8 %all-to-all-start.1 = ((bf16[16,64,128]{2,1,0:T(8,128)(2,1)}), bf16[16,64,128]{2,1,0:T(8,128)(2,1)S(1)}, u32[]{:S(2)}, u32[]{:S(2)}) async-start(bf16[16,64,128]{2,1,0:T(8,128)(2,1)} %get-tuple-element.45), calls=%async_computation.1 | async-start | bytes 524288 | tf_op jit(solution)/shard_map/all_to_all | solution.py:545
  86.2 1.1 %copy-start.2 = (bf16[64,64,128]{2,1,0:T(8,128)(2,1)}, bf16[64,64,128]{2,1,0:T(8,128)(2,1)S(1)}, u32[]{:S(2)}) copy-start(bf16[64,64,128]{2,1,0:T(8,128)(2,1)S(1)} %collective-permute-done.5.late_ref) | copy-start | bytes 3145732

commit v21 on v20

--- a/solution.py
+++ b/solution.py
@@ -58,7 +58,7 @@
         copy.wait()
 
 
-def hand_on(*refs):
+def wait_for(*refs):
     pass
 
 
@@ -172,7 +172,7 @@
 def nonlocal_kernel(
     fars, atom_ref, line_ref, count_ref, xt_hbm, beside_hbm, early_hbm, p_hbm, energy_ref, mine_hbm, core_ref, link_ref, *refs
 ):
-    far_refs, out_hbm, messages, scratch = refs[:fars], refs[fars], refs[fars + 1 : -13], refs[-13:]
+    far_refs, out_hbm, messages, scratch = refs[:fars], refs[fars + 1], refs[fars + 2 : -13], refs[-13:]
     lines_sum, whole_ref, mine_ref, total, table, atoms, p_ref, built, cores, links, sems, in_sems, out_sems = scratch
     lines = xt_hbm.shape[0]
     bands, half = cores.shape[:2]
@@ -280,7 +280,7 @@
     copy.wait()
 
 
-def later_kernel(bands, landed, unread, all_ref, pass_hbm, sems, pass_sem):
+def later_kernel(bands, landed, unread, handed, all_ref, pass_hbm, same, sems, pass_sem):
     count, states = all_ref.shape[0], landed.shape[1]
     loads = [
         start(
@@ -446,18 +446,16 @@
     from_link = lax.ppermute(to_link, "domain", link_pairs)
     from_far = [lax.ppermute(value, "domain", pairs) for value, pairs in zip(to_far, far_pairs)]
     from_core = lax.ppermute(to_core, "domain", core_pairs)
-    (late_part,) = call(
-        56,
-        hand_on,
-        (),
-        [UNREAD] * (5 + len(far_pairs)),
-        [UNREAD],
-        [(late_shape, BF16)],
+    (gate,) = call(
+        63,
+        wait_for,
+        (),
+        [UNREAD] * (4 + len(far_pairs)),
+        [PINNED],
+        [token],
         [],
-        (late_part, from_core, from_link, *from_far, link_early, core_field),
-        aliases={0: 0},
-    )
-    link_late = lax.ppermute(late_part, "domain", link_pairs)
+        (from_core, from_link, *from_far, link_early, core_field),
+    )
     held = groups // bands
     built_shape = (first + first // 2 + held, states, cols_z)
     beside_shape = (bands, first // 2, states, cols_z)
@@ -465,7 +463,7 @@
         62,
         functools.partial(nonlocal_kernel, len(far_pairs)),
         (),
-        [SCALARS] * 3 + [FAR] * 3 + [PINNED, WHOLE, PINNED, WHOLE, WHOLE] + [WHOLE] * len(far_pairs),
+        [SCALARS] * 3 + [FAR] * 3 + [PINNED, WHOLE, PINNED, WHOLE, WHOLE] + [WHOLE] * len(far_pairs) + [PINNED],
         [PINNED, PINNED] + [FAR] * (bands - 1),
         [(line_shape, F32)] + [(built_shape, BF16)] * bands,
         [
@@ -485,24 +483,30 @@
         ],
         (
             tile_atom, tile_line, tile_count, xt, core_field, link_early, projectors, energy, mine, from_core,
-            from_link, *from_far,
+            from_link, *from_far, gate,
         ),
         micros=8,
     )
     early = swapped(messages, "band")
 
-    later_all, later_pass = call(
+    later_all, later_pass, late_part = call(
         32,
         functools.partial(later_kernel, bands),
         (),
-        [FAR, PINNED],
-        [NEAR, FAR],
-        [((rest + 1, total_states, cols_z), BF16), ((rest // 2, total_states, cols_z), BF16)],
+        [FAR, PINNED, UNREAD],
+        [NEAR, FAR, UNREAD],
+        [
+            ((rest + 1, total_states, cols_z), BF16),
+            ((rest // 2, total_states, cols_z), BF16),
+            (late_shape, BF16),
+        ],
         [copies((bands,)), copies],
-        (landed, own_message),
+        (landed, own_message, late_part),
+        aliases={2: 2},
     )
     later_link = lax.ppermute(later_pass, "domain", link_pairs)
     later_core = lax.ppermute(later_pass, "domain", core_pairs)
+    link_late = lax.ppermute(late_part, "domain", link_pairs)
 
     early_all, early_beside, projs, energy_table_here, early_token = call(
         32,

time: 97.6 us -> 88.6 us (0.908)
  waiting for transfers between devices: 24.5 us -> 17 us
  local copies, waits for them, and re-layouts: 1.79 us -> 0.73 us
    ppermute x1, waiting for transfers between devices: 14.3 us -> 3.75 us  [local(): later_link = lax.ppermute(later_pass, 'domain', link_pairs)]
    ppermute x1, waiting for transfers between devices: 0.01 us -> 3.7 us  [local(): link_late = lax.ppermute(late_part, 'domain', link_pairs)]
    ppermute x1, starting transfers between devices: 1.92 us -> 4.27 us  [local(): later_link = lax.ppermute(later_pass, 'domain', link_pairs)]
    all_to_all x1, starting transfers between devices: 6.49 us -> 5.37 us  [local(): lax.all_to_all(blocks, ('domain', 'band'), split_axis=0, concat_axis=0, t...]
    unnamed x12, local copies, waits for them, and re-layouts: 1.79 us -> 0.73 us
    all_to_all x1, waiting for transfers between devices: 1.05 us -> 0.01 us  [local(): lax.all_to_all(blocks, ('domain', 'band'), split_axis=0, concat_axis=0, t...]
  transfers between devices with their start and end apart: 13 -> 13, of which waited for: 5 -> 6; matrix products, arithmetic and copies ran while one was open for 0% -> 0% of each run, Pallas kernels for 36% -> 40%
where the time goes in v21:
time: 88.6 us; the launch traced here: 88 us
  Pallas kernels  39.9 us (45%)
  starting transfers between devices  29 us (33%)
  waiting for transfers between devices  17 us (19%)
  between operations  1.43 us (2%)
    pallas_call x10, Pallas kernels, call(): pl.pallas_call(kernel, grid=grid, out_shape=shapes, in_specs=in_specs, ou...  39.9 us
    ppermute x1, waiting for transfers between devices, local(): lax.ppermute(value, 'domain', pairs)  6.34 us
    all_to_all x1, starting transfers between devices, local(): lax.all_to_all(message, 'band', split_axis=0, concat_axis=0, tiled=True)  6.04 us
    all_to_all x1, starting transfers between devices, local(): lax.all_to_all(blocks, ('domain', 'band'), split_axis=0, concat_axis=0, t...  5.37 us
    ppermute x1, starting transfers between devices, local(): later_link = lax.ppermute(later_pass, 'domain', link_pairs)  4.27 us
    ppermute x3, starting transfers between devices, swapped(): lax.ppermute(values[k - 1], axis, [(i, i ^ k) for i in range(size)])  4.15 us
    ppermute x1, waiting for transfers between devices, local(): later_link = lax.ppermute(later_pass, 'domain', link_pairs)  3.75 us
    ppermute x1, waiting for transfers between devices, local(): link_late = lax.ppermute(late_part, 'domain', link_pairs)  3.7 us
  transfers between devices with their start and end apart: 13, of which 6 were waited for; matrix products, arithmetic and copies ran while one was open for 0% of the time, Pallas kernels for 40%

profile of v21, /device:TPU:1, one launch (start us, length us, event | category | flops | bytes accessed | tf_op | source)
XLA Modules:
  0.0 88.0 jit_solution(14088381698415309769)
XLA Ops:
  0.6 4.0 %shard_map.95 = (bf16[128,64,128]{2,1,0:T(8,128)(2,1)}, bf16[64,64,128]{2,1,0:T(8,128)(2,1)}, bf16[64,64,128]{2,1,0:T(8,128)(2,1)}, bf16[108,64,128]{2,1,0:T(8,128)(2,1)}) custom-call(bf16[64,128,128]{2,1,0:T(8,128)(2,1)} %bitcast.12), custom_call_target="tpu_custom_call" | custom-call | flops 1100000 | bytes 1024 | tf_op jit(solution)/shard_map/pallas_call | solution.py:34
  4.8 6.0 %all-to-all-start = ((bf16[108,64,128]{2,1,0:T(8,128)(2,1)}), bf16[108,64,128]{2,1,0:T(8,128)(2,1)}, u32[]{:S(2)}, u32[]{:S(2)}) async-start(bf16[108,64,128]{2,1,0:T(8,128)(2,1)} %get-tuple-element.27), calls=%async_computation | async-start | bytes 3538944 | tf_op jit(solution)/shard_map/all_to_all | solution.py:422
  10.8 3.3 %collective-permute-start.1 = (bf16[64,64,128]{2,1,0:T(8,128)(2,1)}, bf16[64,64,128]{2,1,0:T(8,128)(2,1)}, u32[]{:S(2)}, u32[]{:S(2)}) collective-permute-start(bf16[64,64,128]{2,1,0:T(8,128)(2,1)} %get-tuple-element.26), channel_id=1, source_target_pairs={{4,8},{8,4},{5,9},{9,5},{6,10},{10,6},{7,11},{11,7},{20,24},{24,20... | collective-permute-start | bytes 3145736 | tf_op jit(solution)/shard_map/ppermute | solution.py:423
  14.8 10.0 %shard_map.96 = (bf16[24,64,128]{2,1,0:T(8,128)(2,1)}, bf16[16,64,128]{2,1,0:T(8,128)(2,1)}, bf16[16,64,128]{2,1,0:T(8,128)(2,1)}, bf16[8,64,128]{2,1,0:T(8,128)(2,1)}) custom-call(s32[384]{0:T(512)} %atom_ref.3, s32[384]{0:T(512)} %line_ref.3, s32[1]{0:T(128)S(6)} %copy.13.count_ref, ...), custom_call_target="tpu_custom_call" | custom-call | flops 1100000 | bytes 1024 | tf_op jit(solution)/shard_map/pallas_call | solution.py:34
  24.9 2.1 %collective-permute-start.3 = (bf16[16,64,128]{2,1,0:T(8,128)(2,1)}, bf16[16,64,128]{2,1,0:T(8,128)(2,1)S(1)}, u32[]{:S(2)}, u32[]{:S(2)}) collective-permute-start(bf16[16,64,128]{2,1,0:T(8,128)(2,1)} %get-tuple-element.30), channel_id=1, source_target_pairs={{4,8},{8,4},{5,9},{9,5},{6,10},{10,6},{7,11},{11,7},{20,24},{24,20... | collective-permute-start | bytes 786440 | tf_op jit(solution)/shard_map/ppermute | solution.py:446
  27.1 6.3 %collective-permute-done.4.refs_2_.refs_0_ = bf16[8,64,128]{2,1,0:T(8,128)(2,1)S(1)} collective-permute-done((bf16[8,64,128]{2,1,0:T(8,128)(2,1)}, bf16[8,64,128]{2,1,0:T(8,128)(2,1)S(1)}, u32[]{:S(2)}, u32[]{:S(2)}) %collective-permute-start.4) | collective-permute-done | bytes 131104 | tf_op jit(solution)/shard_map/ppermute | solution.py:447
  33.5 0.5 collective-permute-done.3.refs_1_.link_ref
  34.7 12.5 %shard_map.98 = (f32[128,64,128]{2,1,0:T(8,128)}, bf16[11,64,128]{2,1,0:T(8,128)(2,1)}, bf16[11,64,128]{2,1,0:T(8,128)(2,1)}, bf16[11,64,128]{2,1,0:T(8,128)(2,1)}, bf16[11,64,128]{2,1,0:T(8,128)(2,1)}) custom-call(s32[384]{0:T(512)} %atom_ref.3, s32[384]{0:T(512)} %line_ref.3, s32[1]{0:T(128)S(6)} %copy.13.count_ref, ...), custom_call_target="tpu_custom_call" | custom-call | flops 8800000000 | bytes 1024 | tf_op jit(solution)/shard_map/pallas_call | solution.py:34
  47.1 2.0 %collective-permute-start.6 = (bf16[11,64,128]{2,1,0:T(8,128)(2,1)}, bf16[11,64,128]{2,1,0:T(8,128)(2,1)S(1)}, u32[]{:S(2)}, u32[]{:S(2)}) collective-permute-start(bf16[11,64,128]{2,1,0:T(8,128)(2,1)} %get-tuple-element.37), channel_id=1, source_target_pairs={{0,1},{1,0},{2,3},{3,2},{4,5},{5,4},{6,7},{7,6},{8,9},{9,8},{10,11... | collective-permute-start | bytes 540680 | tf_op jit(solution)/shard_map/ppermute | solution.py:389
  49.1 1.7 %collective-permute-start.7 = (bf16[11,64,128]{2,1,0:T(8,128)(2,1)}, bf16[11,64,128]{2,1,0:T(8,128)(2,1)S(1)}, u32[]{:S(2)}, u32[]{:S(2)}) collective-permute-start(bf16[11,64,128]{2,1,0:T(8,128)(2,1)} %get-tuple-element.38), channel_id=1, source_target_pairs={{0,2},{1,3},{2,0},{3,1},{4,6},{5,7},{6,4},{7,5},{8,10},{9,11},{10,... | collective-permute-start | bytes 540680 | tf_op jit(solution)/shard_map/ppermute | solution.py:389
  50.8 0.5 collective-permute-start.8
  51.3 0.7 all-to-all-done.landed
  52.0 1.6 %shard_map.99 = (bf16[27,256,128]{2,1,0:T(8,128)(2,1)S(1)}, bf16[13,256,128]{2,1,0:T(8,128)(2,1)S(1)}, bf16[64,64,128]{2,1,0:T(8,128)(2,1)S(1)}) custom-call(bf16[108,64,128]{2,1,0:T(8,128)(2,1)} %all-to-all-done.landed, bf16[11,64,128]{2,1,0:T(8,128)(2,1)} %get-tuple-element.32.unread.refs_0_, ...), custom_call_target="tpu_custom_call", output_to_operand_aliasing={{2}: (2, {})} | custom-call | flops 1100000 | bytes 1024 | tf_op jit(solution)/shard_map/pallas_call | solution.py:34
  53.5 4.3 %collective-permute-start.10 = (bf16[13,256,128]{2,1,0:T(8,128)(2,1)S(1)}, bf16[13,256,128]{2,1,0:T(8,128)(2,1)S(1)}, u32[]{:S(2)}, u32[]{:S(2)}) collective-permute-start(bf16[13,256,128]{2,1,0:T(8,128)(2,1)S(1)} %get-tuple-element.42), channel_id=1, source_target_pairs={{4,8},{8,4},{5,9},{9,5},{6,10},{10,6},{7,11},{11,7},{20,24},{24,20... | collective-permute-start | bytes 2555912 | tf_op jit(solution)/shard_map/ppermute | solution.py:507
  57.9 2.1 %collective-permute-done.6.refs_1_ = bf16[11,64,128]{2,1,0:T(8,128)(2,1)S(1)} collective-permute-done((bf16[11,64,128]{2,1,0:T(8,128)(2,1)}, bf16[11,64,128]{2,1,0:T(8,128)(2,1)S(1)}, u32[]{:S(2)}, u32[]{:S(2)}) %collective-permute-start.6) | collective-permute-done | bytes 180256 | tf_op jit(solution)/shard_map/ppermute | solution.py:389
  60.0 3.4 %collective-permute-start.5 = (bf16[64,64,128]{2,1,0:T(8,128)(2,1)S(1)}, bf16[64,64,128]{2,1,0:T(8,128)(2,1)}, u32[]{:S(2)}, u32[]{:S(2)}) collective-permute-start(bf16[64,64,128]{2,1,0:T(8,128)(2,1)S(1)} %get-tuple-element.34), channel_id=1, source_target_pairs={{4,8},{8,4},{5,9},{9,5},{6,10},{10,6},{7,11},{11,7},{20,24},{24,20... | collective-permute-start | bytes 3145736 | tf_op jit(solution)/shard_map/ppermute | solution.py:509
  63.4 1.1 %shard_map.100 = (bf16[7,256,128]{2,1,0:T(8,128)(2,1)S(1)}, bf16[3,256,128]{2,1,0:T(8,128)(2,1)S(1)}, bf16[2,256,128]{2,1,0:T(8,128)(2,1)S(1)}, f32[32,128]{1,0:T(8,128)S(1)}, f32[8,128]{1,0:T(8,128)}) custom-call(bf16[27,256,128]{2,1,0:T(8,128)(2,1)S(1)} %get-tuple-element.36.after_ref.all_ref, f32[16,256]{1,0:T(8,128)S(1)} %bitcast.10, ...), custom_call_target="tpu_custom_call" | custom-call | flops 32999999488 | bytes 1024 | tf_op jit(solution)/shard_map/pallas_call | solution.py:34
  64.4 3.8 %collective-permute-done.10.link_ref = bf16[13,256,128]{2,1,0:T(8,128)(2,1)S(1)} collective-permute-done((bf16[13,256,128]{2,1,0:T(8,128)(2,1)S(1)}, bf16[13,256,128]{2,1,0:T(8,128)(2,1)S(1)}, u32[]{:S(2)}, u32[]{:S(2)}) %collective-permute-start.10) | collective-permute-done | bytes 852000 | tf_op jit(solution)/shard_map/ppermute | solution.py:507
  68.2 1.3 %shard_map.101.begun_ref = f32[2,256,256]{2,1,0:T(8,128)S(1)} custom-call(bf16[27,256,128]{2,1,0:T(8,128)(2,1)S(1)} %get-tuple-element.36.after_ref.all_ref, bf16[13,256,128]{2,1,0:T(8,128)(2,1)S(1)} %collective-permute-done.9.core_ref, bf16[13,256,128]{2,1,0:T(8,128)(2,1)S(1)} %collective-permute-done.10.link_ref, f32[128,128]{1,0:T(8,128)S(1)} %bitcast.7, ...), custom_call_target="tpu_custom_call" | custom-call | flops 1100000 | bytes 1024 | tf_op jit(solution)/shard_map/pallas_call | solution.py:34
  69.4 1.5 %shard_map.102 = (bf16[16,64,128]{2,1,0:T(8,128)(2,1)}, f32[8,128]{1,0:T(8,128)}) custom-call(bf16[7,256,128]{2,1,0:T(8,128)(2,1)S(1)} %get-tuple-element.40.all_ref, bf16[3,256,128]{2,1,0:T(8,128)(2,1)S(1)} %get-tuple-element.41.beside_ref, f32[128,128]{1,0:T(8,128)S(1)} %bitcast.8, f32[2,256,256]{2,1,0:T(8,128)S(1)} %shard_map.101.begun_ref, ...), custom_call_target="tpu_custom_call" | custom-call | flops 1100000 | bytes 1024 | tf_op jit(solution)/shard_map/pallas_call | solution.py:34
  71.0 5.4 %all-to-all-start.1 = ((bf16[16,64,128]{2,1,0:T(8,128)(2,1)}), bf16[16,64,128]{2,1,0:T(8,128)(2,1)S(1)}, u32[]{:S(2)}, u32[]{:S(2)}) async-start(bf16[16,64,128]{2,1,0:T(8,128)(2,1)} %get-tuple-element.47), calls=%async_computation.1 | async-start | bytes 524288 | tf_op jit(solution)/shard_map/all_to_all | solution.py:549
  76.4 3.7 %collective-permute-done.5.late_ref = bf16[64,64,128]{2,1,0:T(8,128)(2,1)} collective-permute-done((bf16[64,64,128]{2,1,0:T(8,128)(2,1)S(1)}, bf16[64,64,128]{2,1,0:T(8,128)(2,1)}, u32[]{:S(2)}, u32[]{:S(2)}) %collective-permute-start.5) | collective-permute-done | bytes 1048608 | tf_op jit(solution)/shard_map/ppermute | solution.py:509
  80.1 7.2 %shard_map.103 = bf16[64,128,128]{2,1,0:T(8,128)(2,1)} custom-call(bf16[128,64,128]{2,1,0:T(8,128)(2,1)} %get-tuple-element.25.xt_hbm.xt_ref.last_ref.next_ref, bf16[128,64,128]{2,1,0:T(8,128)(2,1)} %get-tuple-element.25.xt_hbm.xt_ref.last_ref.next_ref, bf16[128,64,128]{2,1,0:T(8,128)(2,1)} %get-tuple-element.25.xt_hbm.xt_ref.last_ref.next_ref, ...), custom_call_target="tpu_custom_call" | custom-call | flops 1100000 | bytes 1024 | tf_op jit(solution)/shard_map/pallas_call | solution.py:34
  87.3 0.7 shard_map.104
  (24 shorter events, 1.1 us)
Async XLA Ops:
  4.7 29.3 %collective-permute-start = (bf16[128,64,128]{2,1,0:T(8,128)(2,1)}, bf16[128,64,128]{2,1,0:T(8,128)(2,1)}, u32[]{:S(2)}, u32[]{:S(2)}) collective-permute-start(bf16[128,64,128]{2,1,0:T(8,128)(2,1)} %get-tuple-element.25.xt_hbm.xt_ref.last_ref.next_ref), channel_id=1, source_target_pairs={{0,4},{4,0},{8,12},{12,8},{1,5},{5,1},{9,13},{13,9},{2,6},{6,2},{1... | collective-permute-start | bytes 6291464 | tf_op jit(solution)/shard_map/ppermute | solution.py:424
  4.8 47.1 %all-to-all-start = ((bf16[108,64,128]{2,1,0:T(8,128)(2,1)}), bf16[108,64,128]{2,1,0:T(8,128)(2,1)}, u32[]{:S(2)}, u32[]{:S(2)}) async-start(bf16[108,64,128]{2,1,0:T(8,128)(2,1)} %get-tuple-element.27), calls=%async_computation | async-start | bytes 3538944 | tf_op jit(solution)/shard_map/all_to_all | solution.py:422
  10.8 23.1 %collective-permute-start.1 = (bf16[64,64,128]{2,1,0:T(8,128)(2,1)}, bf16[64,64,128]{2,1,0:T(8,128)(2,1)}, u32[]{:S(2)}, u32[]{:S(2)}) collective-permute-start(bf16[64,64,128]{2,1,0:T(8,128)(2,1)} %get-tuple-element.26), channel_id=1, source_target_pairs={{4,8},{8,4},{5,9},{9,5},{6,10},{10,6},{7,11},{11,7},{20,24},{24,20... | collective-permute-start | bytes 3145736 | tf_op jit(solution)/shard_map/ppermute | solution.py:423
  24.8 8.6 %collective-permute-start.2 = (bf16[16,64,128]{2,1,0:T(8,128)(2,1)}, bf16[16,64,128]{2,1,0:T(8,128)(2,1)S(1)}, u32[]{:S(2)}, u32[]{:S(2)}) collective-permute-start(bf16[16,64,128]{2,1,0:T(8,128)(2,1)} %get-tuple-element.29), channel_id=1, source_target_pairs={{0,4},{4,0},{8,12},{12,8},{1,5},{5,1},{9,13},{13,9},{2,6},{6,2},{1... | collective-permute-start | bytes 786440 | tf_op jit(solution)/shard_map/ppermute | solution.py:448
  24.9 9.0 %collective-permute-start.3 = (bf16[16,64,128]{2,1,0:T(8,128)(2,1)}, bf16[16,64,128]{2,1,0:T(8,128)(2,1)S(1)}, u32[]{:S(2)}, u32[]{:S(2)}) collective-permute-start(bf16[16,64,128]{2,1,0:T(8,128)(2,1)} %get-tuple-element.30), channel_id=1, source_target_pairs={{4,8},{8,4},{5,9},{9,5},{6,10},{10,6},{7,11},{11,7},{20,24},{24,20... | collective-permute-start | bytes 786440 | tf_op jit(solution)/shard_map/ppermute | solution.py:446
  27.0 6.4 %collective-permute-start.4 = (bf16[8,64,128]{2,1,0:T(8,128)(2,1)}, bf16[8,64,128]{2,1,0:T(8,128)(2,1)S(1)}, u32[]{:S(2)}, u32[]{:S(2)}) collective-permute-start(bf16[8,64,128]{2,1,0:T(8,128)(2,1)} %get-tuple-element.31), channel_id=1, source_target_pairs={{0,8},{4,12},{8,0},{12,4},{1,9},{5,13},{9,1},{13,5},{2,10},{6,14},... | collective-permute-start | bytes 393224 | tf_op jit(solution)/shard_map/ppermute | solution.py:447
  33.5 0.7 copy-start.5
  33.5 0.8 copy-start.3
  33.9 0.7 copy-start.4
  34.7 17.3 %copy-start = (bf16[64,64,128]{2,1,0:T(8,128)(2,1)S(1)}, bf16[64,64,128]{2,1,0:T(8,128)(2,1)}, u32[]{:S(2)}) copy-start(bf16[64,64,128]{2,1,0:T(8,128)(2,1)} %get-tuple-element.33.handed) | copy-start | bytes 3145732
  47.1 16.2 %copy-start.2 = (f32[256,16]{0,1:T(8,128)S(1)}, f32[256,16]{0,1:T(8,128)}, u32[]{:S(2)}) copy-start(f32[256,16]{0,1:T(8,128)} %param.14) | copy-start | bytes 49156
  47.1 12.8 %collective-permute-start.6 = (bf16[11,64,128]{2,1,0:T(8,128)(2,1)}, bf16[11,64,128]{2,1,0:T(8,128)(2,1)S(1)}, u32[]{:S(2)}, u32[]{:S(2)}) collective-permute-start(bf16[11,64,128]{2,1,0:T(8,128)(2,1)} %get-tuple-element.37), channel_id=1, source_target_pairs={{0,1},{1,0},{2,3},{3,2},{4,5},{5,4},{6,7},{7,6},{8,9},{9,8},{10,11... | collective-permute-start | bytes 540680 | tf_op jit(solution)/shard_map/ppermute | solution.py:389
  49.1 14.2 %collective-permute-start.7 = (bf16[11,64,128]{2,1,0:T(8,128)(2,1)}, bf16[11,64,128]{2,1,0:T(8,128)(2,1)S(1)}, u32[]{:S(2)}, u32[]{:S(2)}) collective-permute-start(bf16[11,64,128]{2,1,0:T(8,128)(2,1)} %get-tuple-element.38), channel_id=1, source_target_pairs={{0,2},{1,3},{2,0},{3,1},{4,6},{5,7},{6,4},{7,5},{8,10},{9,11},{10,... | collective-permute-start | bytes 540680 | tf_op jit(solution)/shard_map/ppermute | solution.py:389
  50.8 12.5 %collective-permute-start.8 = (bf16[11,64,128]{2,1,0:T(8,128)(2,1)}, bf16[11,64,128]{2,1,0:T(8,128)(2,1)S(1)}, u32[]{:S(2)}, u32[]{:S(2)}) collective-permute-start(bf16[11,64,128]{2,1,0:T(8,128)(2,1)} %get-tuple-element.39), channel_id=1, source_target_pairs={{0,3},{1,2},{2,1},{3,0},{4,7},{5,6},{6,5},{7,4},{8,11},{9,10},{10,... | collective-permute-start | bytes 540680 | tf_op jit(solution)/shard_map/ppermute | solution.py:389
  53.5 14.6 %collective-permute-start.10 = (bf16[13,256,128]{2,1,0:T(8,128)(2,1)S(1)}, bf16[13,256,128]{2,1,0:T(8,128)(2,1)S(1)}, u32[]{:S(2)}, u32[]{:S(2)}) collective-permute-start(bf16[13,256,128]{2,1,0:T(8,128)(2,1)S(1)} %get-tuple-element.42), channel_id=1, source_target_pairs={{4,8},{8,4},{5,9},{9,5},{6,10},{10,6},{7,11},{11,7},{20,24},{24,20... | collective-permute-start | bytes 2555912 | tf_op jit(solution)/shard_map/ppermute | solution.py:507
  57.8 10.4 %collective-permute-start.9 = (bf16[13,256,128]{2,1,0:T(8,128)(2,1)S(1)}, bf16[13,256,128]{2,1,0:T(8,128)(2,1)S(1)}, u32[]{:S(2)}, u32[]{:S(2)}) collective-permute-start(bf16[13,256,128]{2,1,0:T(8,128)(2,1)S(1)} %get-tuple-element.42), channel_id=1, source_target_pairs={{0,4},{4,0},{8,12},{12,8},{1,5},{5,1},{9,13},{13,9},{2,6},{6,2},{1... | collective-permute-start | bytes 2555912 | tf_op jit(solution)/shard_map/ppermute | solution.py:508
  60.0 20.1 %collective-permute-start.5 = (bf16[64,64,128]{2,1,0:T(8,128)(2,1)S(1)}, bf16[64,64,128]{2,1,0:T(8,128)(2,1)}, u32[]{:S(2)}, u32[]{:S(2)}) collective-permute-start(bf16[64,64,128]{2,1,0:T(8,128)(2,1)S(1)} %get-tuple-element.34), channel_id=1, source_target_pairs={{4,8},{8,4},{5,9},{9,5},{6,10},{10,6},{7,11},{11,7},{20,24},{24,20... | collective-permute-start | bytes 3145736 | tf_op jit(solution)/shard_map/ppermute | solution.py:509
  63.4 4.8 %copy-start.1 = (f32[1,128,128]{2,1,0:T(8,128)S(1)}, f32[1,128,128]{2,1,0:T(8,128)}, u32[]{:S(2)}) copy-start(f32[1,128,128]{2,1,0:T(8,128)} %param.9) | copy-start | bytes 196612
  71.0 16.3 %all-to-all-start.1 = ((bf16[16,64,128]{2,1,0:T(8,128)(2,1)}), bf16[16,64,128]{2,1,0:T(8,128)(2,1)S(1)}, u32[]{:S(2)}, u32[]{:S(2)}) async-start(bf16[16,64,128]{2,1,0:T(8,128)(2,1)} %get-tuple-element.47), calls=%async_computation.1 | async-start | bytes 524288 | tf_op jit(solution)/shard_map/all_to_all | solution.py:549

commit v22 on v21

--- a/solution.py
+++ b/solution.py
@@ -242,9 +242,9 @@
 
 
 def stencil_kernel(
-    share, xt_ref, last_ref, next_ref, core_ref, early_ref, late_ref, added_ref, pot_ref, ring_ref, unread,
-    out_ref,
+    share, xt_ref, last_ref, next_ref, core_ref, early_ref, late_ref, added_ref, pot_ref, ring_ref, *refs
 ):
+    out_ref = refs[-2]
     states, here, _ = out_ref.shape
 
     def link(i, rows):
@@ -280,7 +280,7 @@
     copy.wait()
 
 
-def later_kernel(bands, landed, unread, handed, all_ref, pass_hbm, same, sems, pass_sem):
+def later_kernel(bands, landed, unread, handed, all_ref, pass_hbm, same, token, sems, pass_sem):
     count, states = all_ref.shape[0], landed.shape[1]
     loads = [
         start(
@@ -295,7 +295,7 @@
     pass_half(all_ref, pass_hbm, pass_sem)
 
 
-def early_kernel(after_ref, energy_ref, *refs):
+def early_kernel(after_ref, energy_ref, unread, *refs):
     pieces, (all_ref, beside_ref, projs_ref, table_ref, token, sems) = refs[:-6], refs[-6:]
     states = pieces[0].shape[1]
     count, half, held = all_ref.shape[0] - 1, beside_ref.shape[0], projs_ref.shape[0]
@@ -489,16 +489,17 @@
     )
     early = swapped(messages, "band")
 
-    later_all, later_pass, late_part = call(
+    later_all, later_pass, late_part, later_token = call(
         32,
         functools.partial(later_kernel, bands),
         (),
         [FAR, PINNED, UNREAD],
-        [NEAR, FAR, UNREAD],
+        [NEAR, FAR, UNREAD, PINNED],
         [
             ((rest + 1, total_states, cols_z), BF16),
             ((rest // 2, total_states, cols_z), BF16),
             (late_shape, BF16),
+            token,
         ],
         [copies((bands,)), copies],
         (landed, own_message, late_part),
@@ -508,11 +509,48 @@
     later_core = lax.ppermute(later_pass, "domain", core_pairs)
     link_late = lax.ppermute(late_part, "domain", link_pairs)
 
+    added_far = pltpu.with_memory_space_constraint(added, pltpu.HBM)
+
+    def stencil(room, part, extra):
+        span, every, skip, links = part
+        steps = lines // (span * every)
+
+        def place(i):
+            return i * every + skip
+
+        def line_of(offset):
+            return pl.BlockSpec(
+                (1, states, cols_z), lambda i: (lax.rem(place(i) * span + offset + lines, lines), 0, 0)
+            )
+
+        block = pl.BlockSpec((span, states, cols_z), lambda i: (place(i), 0, 0))
+        link_block = pl.BlockSpec((span * every // 2, states, cols_z), lambda i: (i, 0, 0))
+        return call(
+            room,
+            functools.partial(stencil_kernel, share if every == 1 else 2 * span),
+            (steps,),
+            [block, line_of(-1), line_of(span), block, link_block, link_block, block]
+            + [pl.BlockSpec((span, cols_z), lambda i: (place(i), 0)), WHOLE, PINNED]
+            + [UNREAD] * (len(extra) - 1),
+            [pl.BlockSpec((states, span, cols_z), lambda i: (0, place(i), 0)), PINNED],
+            [((states, lines, cols_z), BF16), token],
+            [],
+            (xt, xt, xt, core_field, *links, added_far, pot, ring, *extra),
+            aliases={10: 0} if len(extra) > 1 else None,
+        )
+
+    applied, applied_token = [], later_token
+    late_parts = (2 * ROWS, 1, 0, (link_early, link_late))
+    if share // 2 % ROWS == 0:
+        early_parts = (share // 2, 2, 0, (link_early, link_early))
+        late_parts = (share // 2, 2, 1, (link_late, link_late))
+        *applied, applied_token = stencil(32, early_parts, (later_token,))
+
     early_all, early_beside, projs, energy_table_here, early_token = call(
         32,
         early_kernel,
         (),
-        [NEAR, WHOLE, PINNED] + [FAR] * (bands - 1),
+        [NEAR, WHOLE, PINNED, PINNED] + [FAR] * (bands - 1),
         [NEAR, NEAR, NEAR, NEAR, PINNED],
         [
             ((first + 1, total_states, cols_z), BF16),
@@ -522,7 +560,7 @@
             token,
         ],
         [copies((3 * bands,))],
-        (later_all, energy, own_message, *early),
+        (later_all, energy, applied_token, own_message, *early),
         micros=30,
     )
     (begun,) = call(
@@ -547,34 +585,7 @@
         (early_all, early_beside, pot, begun, projs, energy_table_here),
     )
     summed = lax.all_to_all(blocks, ("domain", "band"), split_axis=0, concat_axis=0, tiled=True)
-    span = 2 * ROWS
-    steps = lines // span
-    block = pl.BlockSpec((span, states, cols_z), lambda i: (i, 0, 0))
-    (applied,) = call(
-        60,
-        functools.partial(stencil_kernel, share),
-        (steps,),
-        [
-            block,
-            pl.BlockSpec((1, states, cols_z), lambda i: (lax.rem(i * span + lines - 1, lines), 0, 0)),
-            pl.BlockSpec((1, states, cols_z), lambda i: (lax.rem(i * span + span, lines), 0, 0)),
-            block,
-            pl.BlockSpec((span // 2, states, cols_z), lambda i: (i, 0, 0)),
-            pl.BlockSpec((span // 2, states, cols_z), lambda i: (i, 0, 0)),
-            block,
-            pl.BlockSpec((span, cols_z), lambda i: (i, 0)),
-            WHOLE,
-            PINNED,
-        ],
-        [pl.BlockSpec((states, span, cols_z), lambda i: (0, i, 0))],
-        [((states, lines, cols_z), BF16)],
-        [],
-        (
-            xt, xt, xt, core_field, link_early, link_late, pltpu.with_memory_space_constraint(added, pltpu.HBM), pot, ring,
-            final_token,
-        ),
-    )
-
+    applied, _ = stencil(60, late_parts, (final_token, *applied))
     (subspace,) = call(
         32,
         functools.partial(result_kernel, 1.0 / (lines * cols_z * domains)),

time: 88.6 us -> 89.7 us (1.012)
  waiting for transfers between devices: 17 us -> 14.3 us
  Pallas kernels: 39.9 us -> 42.5 us
  local copies, waits for them, and re-layouts: 0.73 us -> 1.77 us
    pallas_call x10 -> x11, Pallas kernels: 39.9 us -> 42.5 us  [call(): pl.pallas_call(kernel, grid=grid, out_shape=shapes, in_specs=in_specs, ou...]
    ppermute x3, waiting for transfers between devices: 2.06 us -> 0.01 us  [swapped(): lax.ppermute(values[k - 1], axis, [(i, i ^ k) for i in range(size)])]
    ppermute x1, starting transfers between devices: 4.27 us -> 2.36 us  [local(): later_link = lax.ppermute(later_pass, 'domain', link_pairs)]
    ppermute x1, starting transfers between devices: 0.07 us -> 1.97 us  [local(): later_core = lax.ppermute(later_pass, 'domain', core_pairs)]
    ppermute x1, waiting for transfers between devices: 3.75 us -> 2.31 us  [local(): later_link = lax.ppermute(later_pass, 'domain', link_pairs)]
    unnamed x12 -> x18, local copies, waits for them, and re-layouts: 0.73 us -> 1.77 us
  transfers between devices with their start and end apart: 13 -> 13, of which waited for: 6 -> 5; matrix products, arithmetic and copies ran while one was open for 0% -> 0% of each run, Pallas kernels for 40% -> 43%
where the time goes in v22:
time: 89.7 us; the launch traced here: 88.5 us
  Pallas kernels  42.5 us (47%)
  starting transfers between devices  28.4 us (32%)
  waiting for transfers between devices  14.3 us (16%)
  local copies, waits for them, and re-layouts  1.77 us (2%)
  between operations  1.47 us (2%)
    pallas_call x11, Pallas kernels, call(): pl.pallas_call(kernel, grid=grid, out_shape=shapes, in_specs=in_specs, ou...  42.5 us
    ppermute x1, waiting for transfers between devices, local(): lax.ppermute(value, 'domain', pairs)  6.34 us
    all_to_all x1, starting transfers between devices, local(): lax.all_to_all(message, 'band', split_axis=0, concat_axis=0, tiled=True)  6.04 us
    all_to_all x1, starting transfers between devices, local(): lax.all_to_all(blocks, ('domain', 'band'), split_axis=0, concat_axis=0, t...  4.95 us
    ppermute x1, waiting for transfers between devices, local(): link_late = lax.ppermute(late_part, 'domain', link_pairs)  4.18 us
    ppermute x3, starting transfers between devices, swapped(): lax.ppermute(values[k - 1], axis, [(i, i ^ k) for i in range(size)])  4.08 us
    ppermute x1, starting transfers between devices, local(): link_early = lax.ppermute(early_part, 'domain', link_pairs)  3.33 us
    ppermute x1, starting transfers between devices, local(): link_late = lax.ppermute(late_part, 'domain', link_pairs)  3.18 us
  transfers between devices with their start and end apart: 13, of which 5 were waited for; matrix products, arithmetic and copies ran while one was open for 0% of the time, Pallas kernels for 43%

profile of v22, /device:TPU:1, one launch (start us, length us, event | category | flops | bytes accessed | tf_op | source)
XLA Modules:
  0.0 88.5 jit_solution(6876340670998231651)
XLA Ops:
  0.6 4.0 %shard_map.95 = (bf16[128,64,128]{2,1,0:T(8,128)(2,1)}, bf16[64,64,128]{2,1,0:T(8,128)(2,1)}, bf16[64,64,128]{2,1,0:T(8,128)(2,1)}, bf16[108,64,128]{2,1,0:T(8,128)(2,1)}) custom-call(bf16[64,128,128]{2,1,0:T(8,128)(2,1)} %bitcast.13), custom_call_target="tpu_custom_call" | custom-call | flops 1100000 | bytes 1024 | tf_op jit(solution)/shard_map/pallas_call | solution.py:34
  4.8 6.0 %all-to-all-start = ((bf16[108,64,128]{2,1,0:T(8,128)(2,1)}), bf16[108,64,128]{2,1,0:T(8,128)(2,1)}, u32[]{:S(2)}, u32[]{:S(2)}) async-start(bf16[108,64,128]{2,1,0:T(8,128)(2,1)} %get-tuple-element.30), calls=%async_computation | async-start | bytes 3538944 | tf_op jit(solution)/shard_map/all_to_all | solution.py:422
  10.8 3.3 %collective-permute-start.1 = (bf16[64,64,128]{2,1,0:T(8,128)(2,1)}, bf16[64,64,128]{2,1,0:T(8,128)(2,1)}, u32[]{:S(2)}, u32[]{:S(2)}) collective-permute-start(bf16[64,64,128]{2,1,0:T(8,128)(2,1)} %get-tuple-element.31), channel_id=1, source_target_pairs={{4,8},{8,4},{5,9},{9,5},{6,10},{10,6},{7,11},{11,7},{20,24},{24,20... | collective-permute-start | bytes 3145736 | tf_op jit(solution)/shard_map/ppermute | solution.py:423
  14.8 9.9 %shard_map.96 = (bf16[24,64,128]{2,1,0:T(8,128)(2,1)}, bf16[16,64,128]{2,1,0:T(8,128)(2,1)}, bf16[16,64,128]{2,1,0:T(8,128)(2,1)}, bf16[8,64,128]{2,1,0:T(8,128)(2,1)}) custom-call(s32[384]{0:T(512)} %atom_ref.3, s32[384]{0:T(512)} %line_ref.3, s32[1]{0:T(128)S(6)} %copy.15.count_ref, ...), custom_call_target="tpu_custom_call" | custom-call | flops 1100000 | bytes 1024 | tf_op jit(solution)/shard_map/pallas_call | solution.py:34
  24.8 2.2 %collective-permute-start.3 = (bf16[16,64,128]{2,1,0:T(8,128)(2,1)}, bf16[16,64,128]{2,1,0:T(8,128)(2,1)S(1)}, u32[]{:S(2)}, u32[]{:S(2)}) collective-permute-start(bf16[16,64,128]{2,1,0:T(8,128)(2,1)} %get-tuple-element.34), channel_id=1, source_target_pairs={{4,8},{8,4},{5,9},{9,5},{6,10},{10,6},{7,11},{11,7},{20,24},{24,20... | collective-permute-start | bytes 786440 | tf_op jit(solution)/shard_map/ppermute | solution.py:446
  27.1 6.3 %collective-permute-done.4.refs_2_.refs_0_ = bf16[8,64,128]{2,1,0:T(8,128)(2,1)S(1)} collective-permute-done((bf16[8,64,128]{2,1,0:T(8,128)(2,1)}, bf16[8,64,128]{2,1,0:T(8,128)(2,1)S(1)}, u32[]{:S(2)}, u32[]{:S(2)}) %collective-permute-start.4) | collective-permute-done | bytes 131104 | tf_op jit(solution)/shard_map/ppermute | solution.py:447
  34.6 12.2 %shard_map.98 = (f32[128,64,128]{2,1,0:T(8,128)}, bf16[11,64,128]{2,1,0:T(8,128)(2,1)}, bf16[11,64,128]{2,1,0:T(8,128)(2,1)}, bf16[11,64,128]{2,1,0:T(8,128)(2,1)}, bf16[11,64,128]{2,1,0:T(8,128)(2,1)}) custom-call(s32[384]{0:T(512)} %atom_ref.3, s32[384]{0:T(512)} %line_ref.3, s32[1]{0:T(128)S(6)} %copy.15.count_ref, ...), custom_call_target="tpu_custom_call" | custom-call | flops 8800000000 | bytes 1024 | tf_op jit(solution)/shard_map/pallas_call | solution.py:34
  46.9 1.9 %collective-permute-start.6 = (bf16[11,64,128]{2,1,0:T(8,128)(2,1)}, bf16[11,64,128]{2,1,0:T(8,128)(2,1)S(1)}, u32[]{:S(2)}, u32[]{:S(2)}) collective-permute-start(bf16[11,64,128]{2,1,0:T(8,128)(2,1)} %get-tuple-element.43), channel_id=1, source_target_pairs={{0,1},{1,0},{2,3},{3,2},{4,5},{5,4},{6,7},{7,6},{8,9},{9,8},{10,11... | collective-permute-start | bytes 540680 | tf_op jit(solution)/shard_map/ppermute | solution.py:389
  48.8 1.7 %collective-permute-start.7 = (bf16[11,64,128]{2,1,0:T(8,128)(2,1)}, bf16[11,64,128]{2,1,0:T(8,128)(2,1)}, u32[]{:S(2)}, u32[]{:S(2)}) collective-permute-start(bf16[11,64,128]{2,1,0:T(8,128)(2,1)} %get-tuple-element.44), channel_id=1, source_target_pairs={{0,2},{1,3},{2,0},{3,1},{4,6},{5,7},{6,4},{7,5},{8,10},{9,11},{10,... | collective-permute-start | bytes 540680 | tf_op jit(solution)/shard_map/ppermute | solution.py:389
  51.0 1.0 %all-to-all-done.landed = bf16[108,64,128]{2,1,0:T(8,128)(2,1)} async-done(((bf16[108,64,128]{2,1,0:T(8,128)(2,1)}), bf16[108,64,128]{2,1,0:T(8,128)(2,1)}, u32[]{:S(2)}, u32[]{:S(2)}) %all-to-all-start) | async-done | bytes 1769504 | tf_op jit(solution)/shard_map/all_to_all | solution.py:422
  52.0 1.6 %shard_map.99 = (bf16[27,256,128]{2,1,0:T(8,128)(2,1)S(1)}, bf16[13,256,128]{2,1,0:T(8,128)(2,1)S(1)}, bf16[64,64,128]{2,1,0:T(8,128)(2,1)S(1)}, f32[8,128]{1,0:T(8,128)}) custom-call(bf16[108,64,128]{2,1,0:T(8,128)(2,1)} %all-to-all-done.landed, bf16[11,64,128]{2,1,0:T(8,128)(2,1)} %get-tuple-element.36.unread.refs_0_, ...), custom_call_target="tpu_custom_call", output_to_operand_aliasing={{2}: (2, {})} | custom-call | flops 1100000 | bytes 1024 | tf_op jit(solution)/shard_map/pallas_call | solution.py:34
  53.6 2.0 %collective-permute-start.9 = (bf16[13,256,128]{2,1,0:T(8,128)(2,1)S(1)}, bf16[13,256,128]{2,1,0:T(8,128)(2,1)S(1)}, u32[]{:S(2)}, u32[]{:S(2)}) collective-permute-start(bf16[13,256,128]{2,1,0:T(8,128)(2,1)S(1)} %get-tuple-element.48), channel_id=1, source_target_pairs={{0,4},{4,0},{8,12},{12,8},{1,5},{5,1},{9,13},{13,9},{2,6},{6,2},{1... | collective-permute-start | bytes 2555912 | tf_op jit(solution)/shard_map/ppermute | solution.py:509
  55.5 2.4 %collective-permute-start.10 = (bf16[13,256,128]{2,1,0:T(8,128)(2,1)S(1)}, bf16[13,256,128]{2,1,0:T(8,128)(2,1)S(1)}, u32[]{:S(2)}, u32[]{:S(2)}) collective-permute-start(bf16[13,256,128]{2,1,0:T(8,128)(2,1)S(1)} %get-tuple-element.48), channel_id=1, source_target_pairs={{4,8},{8,4},{5,9},{9,5},{6,10},{10,6},{7,11},{11,7},{20,24},{24,20... | collective-permute-start | bytes 2555912 | tf_op jit(solution)/shard_map/ppermute | solution.py:508
  57.9 4.8 %shard_map.100 = (bf16[64,128,128]{2,1,0:T(8,128)(2,1)}, f32[8,128]{1,0:T(8,128)}) custom-call(bf16[128,64,128]{2,1,0:T(8,128)(2,1)S(1)} %copy-done, bf16[128,64,128]{2,1,0:T(8,128)(2,1)S(1)} %copy-done, bf16[128,64,128]{2,1,0:T(8,128)(2,1)S(1)} %copy-done, bf16[128,64,128]{2,1,0:T(8,128)(2,1)} %collective-permute-done.refs_4_.beside_hbm.core_ref, ...), custom_call_target="tpu_custom_call" | custom-call | flops 1100000 | bytes 1024 | tf_op jit(solution)/shard_map/pallas_call | solution.py:34
  62.8 3.2 %collective-permute-start.5 = (bf16[64,64,128]{2,1,0:T(8,128)(2,1)S(1)}, bf16[64,64,128]{2,1,0:T(8,128)(2,1)S(1)}, u32[]{:S(2)}, u32[]{:S(2)}) collective-permute-start(bf16[64,64,128]{2,1,0:T(8,128)(2,1)S(1)} %get-tuple-element.38), channel_id=1, source_target_pairs={{4,8},{8,4},{5,9},{9,5},{6,10},{10,6},{7,11},{11,7},{20,24},{24,20... | collective-permute-start | bytes 3145736 | tf_op jit(solution)/shard_map/ppermute | solution.py:510
  66.0 1.2 %shard_map.101 = (bf16[7,256,128]{2,1,0:T(8,128)(2,1)S(1)}, bf16[3,256,128]{2,1,0:T(8,128)(2,1)S(1)}, bf16[2,256,128]{2,1,0:T(8,128)(2,1)S(1)}, f32[32,128]{1,0:T(8,128)S(1)}, f32[8,128]{1,0:T(8,128)}) custom-call(bf16[27,256,128]{2,1,0:T(8,128)(2,1)S(1)} %get-tuple-element.40.after_ref.all_ref, f32[16,256]{1,0:T(8,128)S(1)} %bitcast.11, ...), custom_call_target="tpu_custom_call" | custom-call | flops 32999999488 | bytes 1024 | tf_op jit(solution)/shard_map/pallas_call | solution.py:34
  67.2 2.3 %collective-permute-done.10.link_ref = bf16[13,256,128]{2,1,0:T(8,128)(2,1)S(1)} collective-permute-done((bf16[13,256,128]{2,1,0:T(8,128)(2,1)S(1)}, bf16[13,256,128]{2,1,0:T(8,128)(2,1)S(1)}, u32[]{:S(2)}, u32[]{:S(2)}) %collective-permute-start.10) | collective-permute-done | bytes 852000 | tf_op jit(solution)/shard_map/ppermute | solution.py:508
  69.5 1.3 %shard_map.102.begun_ref = f32[2,256,256]{2,1,0:T(8,128)S(1)} custom-call(bf16[27,256,128]{2,1,0:T(8,128)(2,1)S(1)} %get-tuple-element.40.after_ref.all_ref, bf16[13,256,128]{2,1,0:T(8,128)(2,1)S(1)} %collective-permute-done.9.core_ref, bf16[13,256,128]{2,1,0:T(8,128)(2,1)S(1)} %collective-permute-done.10.link_ref, f32[128,128]{1,0:T(8,128)S(1)} %bitcast.8, ...), custom_call_target="tpu_custom_call" | custom-call | flops 1100000 | bytes 1024 | tf_op jit(solution)/shard_map/pallas_call | solution.py:34
  70.8 1.5 %shard_map.103 = (bf16[16,64,128]{2,1,0:T(8,128)(2,1)}, f32[8,128]{1,0:T(8,128)}) custom-call(bf16[7,256,128]{2,1,0:T(8,128)(2,1)S(1)} %get-tuple-element.46.all_ref, bf16[3,256,128]{2,1,0:T(8,128)(2,1)S(1)} %get-tuple-element.47.beside_ref, f32[128,128]{1,0:T(8,128)S(1)} %bitcast.9, f32[2,256,256]{2,1,0:T(8,128)S(1)} %shard_map.102.begun_ref, ...), custom_call_target="tpu_custom_call" | custom-call | flops 1100000 | bytes 1024 | tf_op jit(solution)/shard_map/pallas_call | solution.py:34
  72.3 5.0 %all-to-all-start.1 = ((bf16[16,64,128]{2,1,0:T(8,128)(2,1)}), bf16[16,64,128]{2,1,0:T(8,128)(2,1)S(1)}, u32[]{:S(2)}, u32[]{:S(2)}) async-start(bf16[16,64,128]{2,1,0:T(8,128)(2,1)} %get-tuple-element.55), calls=%async_computation.1 | async-start | bytes 524288 | tf_op jit(solution)/shard_map/all_to_all | solution.py:587
  77.3 4.2 %collective-permute-done.5.early_ref.late_ref = bf16[64,64,128]{2,1,0:T(8,128)(2,1)S(1)} collective-permute-done((bf16[64,64,128]{2,1,0:T(8,128)(2,1)S(1)}, bf16[64,64,128]{2,1,0:T(8,128)(2,1)S(1)}, u32[]{:S(2)}, u32[]{:S(2)}) %collective-permute-start.5) | collective-permute-done | bytes 1048608 | tf_op jit(solution)/shard_map/ppermute | solution.py:510
  81.5 1.0 %copy-done.5 = bf16[64,64,128]{2,1,0:T(8,128)(2,1)} copy-done((bf16[64,64,128]{2,1,0:T(8,128)(2,1)}, bf16[64,64,128]{2,1,0:T(8,128)(2,1)S(1)}, u32[]{:S(2)}) %copy-start.5) | copy-done | bytes 1048600
  82.5 5.2 %shard_map.104 = (bf16[64,128,128]{2,1,0:T(8,128)(2,1)}, f32[8,128]{1,0:T(8,128)}) custom-call(bf16[128,64,128]{2,1,0:T(8,128)(2,1)} %get-tuple-element.29.xt_hbm.xt_ref.last_ref.next_ref, bf16[128,64,128]{2,1,0:T(8,128)(2,1)} %get-tuple-element.29.xt_hbm.xt_ref.last_ref.next_ref, ...), custom_call_target="tpu_custom_call", output_to_operand_aliasing={{0}: (10, {})} | custom-call | flops 1100000 | bytes 1024 | tf_op jit(solution)/shard_map/pallas_call | solution.py:34
  87.8 0.7 shard_map.105
  (31 shorter events, 2.0 us)
Async XLA Ops:
  4.7 29.2 %collective-permute-start = (bf16[128,64,128]{2,1,0:T(8,128)(2,1)}, bf16[128,64,128]{2,1,0:T(8,128)(2,1)}, u32[]{:S(2)}, u32[]{:S(2)}) collective-permute-start(bf16[128,64,128]{2,1,0:T(8,128)(2,1)} %get-tuple-element.29.xt_hbm.xt_ref.last_ref.next_ref), channel_id=1, source_target_pairs={{0,4},{4,0},{8,12},{12,8},{1,5},{5,1},{9,13},{13,9},{2,6},{6,2},{1... | collective-permute-start | bytes 6291464 | tf_op jit(solution)/shard_map/ppermute | solution.py:424
  4.8 47.2 %all-to-all-start = ((bf16[108,64,128]{2,1,0:T(8,128)(2,1)}), bf16[108,64,128]{2,1,0:T(8,128)(2,1)}, u32[]{:S(2)}, u32[]{:S(2)}) async-start(bf16[108,64,128]{2,1,0:T(8,128)(2,1)} %get-tuple-element.30), calls=%async_computation | async-start | bytes 3538944 | tf_op jit(solution)/shard_map/all_to_all | solution.py:422
  10.8 23.1 %collective-permute-start.1 = (bf16[64,64,128]{2,1,0:T(8,128)(2,1)}, bf16[64,64,128]{2,1,0:T(8,128)(2,1)}, u32[]{:S(2)}, u32[]{:S(2)}) collective-permute-start(bf16[64,64,128]{2,1,0:T(8,128)(2,1)} %get-tuple-element.31), channel_id=1, source_target_pairs={{4,8},{8,4},{5,9},{9,5},{6,10},{10,6},{7,11},{11,7},{20,24},{24,20... | collective-permute-start | bytes 3145736 | tf_op jit(solution)/shard_map/ppermute | solution.py:423
  24.7 8.7 %collective-permute-start.2 = (bf16[16,64,128]{2,1,0:T(8,128)(2,1)}, bf16[16,64,128]{2,1,0:T(8,128)(2,1)S(1)}, u32[]{:S(2)}, u32[]{:S(2)}) collective-permute-start(bf16[16,64,128]{2,1,0:T(8,128)(2,1)} %get-tuple-element.33), channel_id=1, source_target_pairs={{0,4},{4,0},{8,12},{12,8},{1,5},{5,1},{9,13},{13,9},{2,6},{6,2},{1... | collective-permute-start | bytes 786440 | tf_op jit(solution)/shard_map/ppermute | solution.py:448
  24.8 9.1 %collective-permute-start.3 = (bf16[16,64,128]{2,1,0:T(8,128)(2,1)}, bf16[16,64,128]{2,1,0:T(8,128)(2,1)S(1)}, u32[]{:S(2)}, u32[]{:S(2)}) collective-permute-start(bf16[16,64,128]{2,1,0:T(8,128)(2,1)} %get-tuple-element.34), channel_id=1, source_target_pairs={{4,8},{8,4},{5,9},{9,5},{6,10},{10,6},{7,11},{11,7},{20,24},{24,20... | collective-permute-start | bytes 786440 | tf_op jit(solution)/shard_map/ppermute | solution.py:446
  27.0 6.4 %collective-permute-start.4 = (bf16[8,64,128]{2,1,0:T(8,128)(2,1)}, bf16[8,64,128]{2,1,0:T(8,128)(2,1)S(1)}, u32[]{:S(2)}, u32[]{:S(2)}) collective-permute-start(bf16[8,64,128]{2,1,0:T(8,128)(2,1)} %get-tuple-element.35), channel_id=1, source_target_pairs={{0,8},{4,12},{8,0},{12,4},{1,9},{5,13},{9,1},{13,5},{2,10},{6,14},... | collective-permute-start | bytes 393224 | tf_op jit(solution)/shard_map/ppermute | solution.py:447
  33.4 0.6 copy-start.8
  33.4 0.8 copy-start.6
  33.9 0.7 copy-start.7
  34.6 17.3 %copy-start.2 = (bf16[64,64,128]{2,1,0:T(8,128)(2,1)S(1)}, bf16[64,64,128]{2,1,0:T(8,128)(2,1)}, u32[]{:S(2)}) copy-start(bf16[64,64,128]{2,1,0:T(8,128)(2,1)} %get-tuple-element.37.handed) | copy-start | bytes 3145732
  46.8 11.1 %copy-start = (bf16[128,64,128]{2,1,0:T(8,128)(2,1)S(1)}, bf16[128,64,128]{2,1,0:T(8,128)(2,1)}, u32[]{:S(2)}) copy-start(bf16[128,64,128]{2,1,0:T(8,128)(2,1)} %get-tuple-element.29.xt_hbm.xt_ref.last_ref.next_ref) | copy-start | bytes 6291460
  46.8 11.1 %copy-start.1 = (f32[1,128,128]{2,1,0:T(8,128)S(1)}, f32[1,128,128]{2,1,0:T(8,128)}, u32[]{:S(2)}) copy-start(f32[1,128,128]{2,1,0:T(8,128)} %param.9) | copy-start | bytes 196612
  46.9 11.1 %copy-start.3 = (bf16[128,128]{1,0:T(8,128)(2,1)S(1)}, bf16[128,128]{1,0:T(8,128)(2,1)}, u32[]{:S(2)}) copy-start(bf16[128,128]{1,0:T(8,128)(2,1)} %constant.2.clone.ring_ref) | copy-start | bytes 98308
  46.9 15.9 %collective-permute-start.6 = (bf16[11,64,128]{2,1,0:T(8,128)(2,1)}, bf16[11,64,128]{2,1,0:T(8,128)(2,1)S(1)}, u32[]{:S(2)}, u32[]{:S(2)}) collective-permute-start(bf16[11,64,128]{2,1,0:T(8,128)(2,1)} %get-tuple-element.43), channel_id=1, source_target_pairs={{0,1},{1,0},{2,3},{3,2},{4,5},{5,4},{6,7},{7,6},{8,9},{9,8},{10,11... | collective-permute-start | bytes 540680 | tf_op jit(solution)/shard_map/ppermute | solution.py:389
  48.8 17.2 %collective-permute-start.7 = (bf16[11,64,128]{2,1,0:T(8,128)(2,1)}, bf16[11,64,128]{2,1,0:T(8,128)(2,1)}, u32[]{:S(2)}, u32[]{:S(2)}) collective-permute-start(bf16[11,64,128]{2,1,0:T(8,128)(2,1)} %get-tuple-element.44), channel_id=1, source_target_pairs={{0,2},{1,3},{2,0},{3,1},{4,6},{5,7},{6,4},{7,5},{8,10},{9,11},{10,... | collective-permute-start | bytes 540680 | tf_op jit(solution)/shard_map/ppermute | solution.py:389
  50.5 15.5 %collective-permute-start.8 = (bf16[11,64,128]{2,1,0:T(8,128)(2,1)}, bf16[11,64,128]{2,1,0:T(8,128)(2,1)}, u32[]{:S(2)}, u32[]{:S(2)}) collective-permute-start(bf16[11,64,128]{2,1,0:T(8,128)(2,1)} %get-tuple-element.45), channel_id=1, source_target_pairs={{0,3},{1,2},{2,1},{3,0},{4,7},{5,6},{6,5},{7,4},{8,11},{9,10},{10,... | collective-permute-start | bytes 540680 | tf_op jit(solution)/shard_map/ppermute | solution.py:389
  53.6 13.7 %collective-permute-start.9 = (bf16[13,256,128]{2,1,0:T(8,128)(2,1)S(1)}, bf16[13,256,128]{2,1,0:T(8,128)(2,1)S(1)}, u32[]{:S(2)}, u32[]{:S(2)}) collective-permute-start(bf16[13,256,128]{2,1,0:T(8,128)(2,1)S(1)} %get-tuple-element.48), channel_id=1, source_target_pairs={{0,4},{4,0},{8,12},{12,8},{1,5},{5,1},{9,13},{13,9},{2,6},{6,2},{1... | collective-permute-start | bytes 2555912 | tf_op jit(solution)/shard_map/ppermute | solution.py:509
  55.5 14.0 %collective-permute-start.10 = (bf16[13,256,128]{2,1,0:T(8,128)(2,1)S(1)}, bf16[13,256,128]{2,1,0:T(8,128)(2,1)S(1)}, u32[]{:S(2)}, u32[]{:S(2)}) collective-permute-start(bf16[13,256,128]{2,1,0:T(8,128)(2,1)S(1)} %get-tuple-element.48), channel_id=1, source_target_pairs={{4,8},{8,4},{5,9},{9,5},{6,10},{10,6},{7,11},{11,7},{20,24},{24,20... | collective-permute-start | bytes 2555912 | tf_op jit(solution)/shard_map/ppermute | solution.py:508
  57.9 8.1 %copy-start.4 = (f32[256,16]{0,1:T(8,128)S(1)}, f32[256,16]{0,1:T(8,128)}, u32[]{:S(2)}) copy-start(f32[256,16]{0,1:T(8,128)} %param.14) | copy-start | bytes 49156
  62.8 18.7 %collective-permute-start.5 = (bf16[64,64,128]{2,1,0:T(8,128)(2,1)S(1)}, bf16[64,64,128]{2,1,0:T(8,128)(2,1)S(1)}, u32[]{:S(2)}, u32[]{:S(2)}) collective-permute-start(bf16[64,64,128]{2,1,0:T(8,128)(2,1)S(1)} %get-tuple-element.38), channel_id=1, source_target_pairs={{4,8},{8,4},{5,9},{9,5},{6,10},{10,6},{7,11},{11,7},{20,24},{24,20... | collective-permute-start | bytes 3145736 | tf_op jit(solution)/shard_map/ppermute | solution.py:510
  72.3 15.4 %all-to-all-start.1 = ((bf16[16,64,128]{2,1,0:T(8,128)(2,1)}), bf16[16,64,128]{2,1,0:T(8,128)(2,1)S(1)}, u32[]{:S(2)}, u32[]{:S(2)}) async-start(bf16[16,64,128]{2,1,0:T(8,128)(2,1)} %get-tuple-element.55), calls=%async_computation.1 | async-start | bytes 524288 | tf_op jit(solution)/shard_map/all_to_all | solution.py:587
  81.5 1.0 %copy-start.5 = (bf16[64,64,128]{2,1,0:T(8,128)(2,1)}, bf16[64,64,128]{2,1,0:T(8,128)(2,1)S(1)}, u32[]{:S(2)}) copy-start(bf16[64,64,128]{2,1,0:T(8,128)(2,1)S(1)} %collective-permute-done.5.early_ref.late_ref) | copy-start | bytes 3145732

commit v23 on v21

--- a/solution.py
+++ b/solution.py
@@ -67,6 +67,7 @@
     bands = in_sems.shape[0]
     share = lines // bands
     count = share - first
+    ahead = early.shape[0] // bands
     loads, sends = [], []
     for c in range(bands):
         where = (slice(None), pl.ds(c * share, share), slice(None))
@@ -85,8 +86,8 @@
                 block = x[s0 : s0 + ROWS, y0 : y0 + ROWS, :].astype(F32)
                 turned = jnp.swapaxes(block, 0, 1).astype(BF16)
                 xt[y0 : y0 + ROWS, s0 : s0 + ROWS, :] = turned
-        send(c * share, share // 2, early, c * (share // 2))
-        send(c * share + share // 2, share // 2, late, c * (share // 2))
+        send(c * share, ahead, early, c * ahead)
+        send(c * share + ahead, share - ahead, late, c * (share - ahead))
         send(c * share + first, count, message, c * (count + 1))
         send(c * share, 1, message, (c + bands - 1) % bands * (count + 1) + count)
         send(c * share, share, xt_hbm, c * share)
@@ -178,13 +179,14 @@
     bands, half = cores.shape[:2]
     share, first = lines // bands, 2 * half
     held = built.shape[1] - first - half
+    ahead = early_hbm.shape[0] // bands
     mine = (lax.axis_index("domain") & 1) * half
     pairs = []
     for k in range(bands):
         to = lax.axis_index("band") ^ k
         pairs.append((xt_hbm.at[pl.ds(to * share, first)], built.at[k, pl.ds(0, first)]))
         pairs.append((beside_hbm.at[pl.ds(to * share + mine, half)], cores.at[k]))
-        pairs.append((early_hbm.at[pl.ds(to * (share // 2) + mine, half)], links.at[k]))
+        pairs.append((early_hbm.at[pl.ds(to * ahead + mine, half)], links.at[k]))
     brought = start_all(pairs, in_sems)
     slots, proj_count, _ = p_ref.shape
     groups, states = total.shape[0] // 3, total.shape[1]
@@ -247,10 +249,13 @@
 ):
     states, here, _ = out_ref.shape
 
+    ahead = early_ref.shape[0] * share // here
+
     def link(i, rows):
         chunk, at = divmod(i, share)
-        ref = early_ref if at < share // 2 else late_ref
-        return ref[chunk * (share // 2) + at % (share // 2), rows, :]
+        if at < ahead:
+            return early_ref[chunk * ahead + at, rows, :]
+        return late_ref[chunk * (share - ahead) + at - ahead, rows, :]
 
     def line(i, rows):
         ref, at = (last_ref, 0) if i < 0 else (next_ref, 0) if i == here else (xt_ref, i)
@@ -397,7 +402,8 @@
     eye = np.eye(cols_z, dtype=np.float32)
     ring = jnp.asarray(3.0 * eye - 0.5 * (np.roll(eye, 1, axis=0) + np.roll(eye, -1, axis=0)), dtype=BF16)
 
-    late_lines = lines // 2
+    ahead = share * 5 // 8
+    late_lines = lines - ahead * bands
     line_shape, late_shape = (lines, states, cols_z), (late_lines, states, cols_z)
     xt, early_part, late_part, message = call(
         63,
@@ -559,8 +565,8 @@
             pl.BlockSpec((1, states, cols_z), lambda i: (lax.rem(i * span + lines - 1, lines), 0, 0)),
             pl.BlockSpec((1, states, cols_z), lambda i: (lax.rem(i * span + span, lines), 0, 0)),
             block,
-            pl.BlockSpec((span // 2, states, cols_z), lambda i: (i, 0, 0)),
-            pl.BlockSpec((span // 2, states, cols_z), lambda i: (i, 0, 0)),
+            pl.BlockSpec((ahead * bands // steps, states, cols_z), lambda i: (i, 0, 0)),
+            pl.BlockSpec((late_lines // steps, states, cols_z), lambda i: (i, 0, 0)),
             block,
             pl.BlockSpec((span, cols_z), lambda i: (i, 0)),
             WHOLE,

time: 88.6 us -> 88.3 us (level)
  waiting for transfers between devices: 17 us -> 13.6 us
  starting transfers between devices: 29 us -> 30.3 us
  local copies, waits for them, and re-layouts: 0.73 us -> 1.86 us
    ppermute x1, waiting for transfers between devices: 3.7 us -> 0.01 us  [local(): link_late = lax.ppermute(late_part, 'domain', link_pairs)]
    ppermute x1, waiting for transfers between devices: 6.34 us -> 7.55 us  [local(): lax.ppermute(value, 'domain', pairs)]
    ppermute x3, waiting for transfers between devices: 2.06 us -> 0.88 us  [swapped(): lax.ppermute(values[k - 1], axis, [(i, i ^ k) for i in range(size)])]
    all_to_all x1, waiting for transfers between devices: 0.01 us -> 1.17 us  [local(): lax.all_to_all(blocks, ('domain', 'band'), split_axis=0, concat_axis=0, t...]
    unnamed x12 -> x14, local copies, waits for them, and re-layouts: 0.73 us -> 1.86 us
    ppermute x1, starting transfers between devices: 3.36 us -> 4.34 us  [local(): link_late = lax.ppermute(late_part, 'domain', link_pairs)]
  transfers between devices with their start and end apart: 13 -> 13, of which waited for: 6 -> 5; matrix products, arithmetic and copies ran while one was open for 0% -> 0% of each run, Pallas kernels for 40% -> 40%
where the time goes in v23:
time: 88.3 us; the launch traced here: 86.9 us
  Pallas kernels  39.7 us (45%)
  starting transfers between devices  30.3 us (34%)
  waiting for transfers between devices  13.6 us (15%)
  local copies, waits for them, and re-layouts  1.86 us (2%)
  between operations  1.44 us (2%)
    pallas_call x10, Pallas kernels, call(): pl.pallas_call(kernel, grid=grid, out_shape=shapes, in_specs=in_specs, ou...  39.7 us
    ppermute x1, waiting for transfers between devices, local(): lax.ppermute(value, 'domain', pairs)  7.55 us
    all_to_all x1, starting transfers between devices, local(): lax.all_to_all(message, 'band', split_axis=0, concat_axis=0, tiled=True)  6.04 us
    all_to_all x1, starting transfers between devices, local(): lax.all_to_all(blocks, ('domain', 'band'), split_axis=0, concat_axis=0, t...  5.88 us
    ppermute x1, starting transfers between devices, local(): link_late = lax.ppermute(late_part, 'domain', link_pairs)  4.34 us
    ppermute x1, starting transfers between devices, local(): later_link = lax.ppermute(later_pass, 'domain', link_pairs)  4.27 us
    ppermute x1, waiting for transfers between devices, local(): later_link = lax.ppermute(later_pass, 'domain', link_pairs)  3.98 us
    ppermute x3, starting transfers between devices, swapped(): lax.ppermute(values[k - 1], axis, [(i, i ^ k) for i in range(size)])  3.97 us
  transfers between devices with their start and end apart: 13, of which 5 were waited for; matrix products, arithmetic and copies ran while one was open for 0% of the time, Pallas kernels for 40%

profile of v23, /device:TPU:1, one launch (start us, length us, event | category | flops | bytes accessed | tf_op | source)
XLA Modules:
  0.0 86.9 jit_solution(2200906725132872120)
XLA Ops:
  0.6 4.0 %shard_map.95 = (bf16[128,64,128]{2,1,0:T(8,128)(2,1)}, bf16[80,64,128]{2,1,0:T(8,128)(2,1)}, bf16[48,64,128]{2,1,0:T(8,128)(2,1)}, bf16[108,64,128]{2,1,0:T(8,128)(2,1)}) custom-call(bf16[64,128,128]{2,1,0:T(8,128)(2,1)} %bitcast.12), custom_call_target="tpu_custom_call" | custom-call | flops 1100000 | bytes 1024 | tf_op jit(solution)/shard_map/pallas_call | solution.py:34
  4.8 6.0 %all-to-all-start = ((bf16[108,64,128]{2,1,0:T(8,128)(2,1)}), bf16[108,64,128]{2,1,0:T(8,128)(2,1)}, u32[]{:S(2)}, u32[]{:S(2)}) async-start(bf16[108,64,128]{2,1,0:T(8,128)(2,1)} %get-tuple-element.27), calls=%async_computation | async-start | bytes 3538944 | tf_op jit(solution)/shard_map/all_to_all | solution.py:428
  10.8 3.3 %collective-permute-start.1 = (bf16[80,64,128]{2,1,0:T(8,128)(2,1)}, bf16[80,64,128]{2,1,0:T(8,128)(2,1)}, u32[]{:S(2)}, u32[]{:S(2)}) collective-permute-start(bf16[80,64,128]{2,1,0:T(8,128)(2,1)} %get-tuple-element.26), channel_id=1, source_target_pairs={{4,8},{8,4},{5,9},{9,5},{6,10},{10,6},{7,11},{11,7},{20,24},{24,20... | collective-permute-start | bytes 3932168 | tf_op jit(solution)/shard_map/ppermute | solution.py:429
  14.8 10.0 %shard_map.96 = (bf16[24,64,128]{2,1,0:T(8,128)(2,1)}, bf16[16,64,128]{2,1,0:T(8,128)(2,1)}, bf16[16,64,128]{2,1,0:T(8,128)(2,1)}, bf16[8,64,128]{2,1,0:T(8,128)(2,1)}) custom-call(s32[384]{0:T(512)} %atom_ref.3, s32[384]{0:T(512)} %line_ref.3, s32[1]{0:T(128)S(6)} %copy.13.count_ref, ...), custom_call_target="tpu_custom_call" | custom-call | flops 1100000 | bytes 1024 | tf_op jit(solution)/shard_map/pallas_call | solution.py:34
  24.9 2.1 %collective-permute-start.3 = (bf16[16,64,128]{2,1,0:T(8,128)(2,1)}, bf16[16,64,128]{2,1,0:T(8,128)(2,1)S(1)}, u32[]{:S(2)}, u32[]{:S(2)}) collective-permute-start(bf16[16,64,128]{2,1,0:T(8,128)(2,1)} %get-tuple-element.30), channel_id=1, source_target_pairs={{4,8},{8,4},{5,9},{9,5},{6,10},{10,6},{7,11},{11,7},{20,24},{24,20... | collective-permute-start | bytes 786440 | tf_op jit(solution)/shard_map/ppermute | solution.py:452
  27.1 7.5 %collective-permute-done.4.refs_2_.refs_0_ = bf16[8,64,128]{2,1,0:T(8,128)(2,1)S(1)} collective-permute-done((bf16[8,64,128]{2,1,0:T(8,128)(2,1)}, bf16[8,64,128]{2,1,0:T(8,128)(2,1)S(1)}, u32[]{:S(2)}, u32[]{:S(2)}) %collective-permute-start.4) | collective-permute-done | bytes 131104 | tf_op jit(solution)/shard_map/ppermute | solution.py:453
  34.7 0.6 copy-done.6
  35.3 0.1 copy-done.4
  35.6 12.4 %shard_map.98 = (f32[128,64,128]{2,1,0:T(8,128)}, bf16[11,64,128]{2,1,0:T(8,128)(2,1)}, bf16[11,64,128]{2,1,0:T(8,128)(2,1)}, bf16[11,64,128]{2,1,0:T(8,128)(2,1)}, bf16[11,64,128]{2,1,0:T(8,128)(2,1)}) custom-call(s32[384]{0:T(512)} %atom_ref.3, s32[384]{0:T(512)} %line_ref.3, s32[1]{0:T(128)S(6)} %copy.13.count_ref, ...), custom_call_target="tpu_custom_call" | custom-call | flops 8800000000 | bytes 1024 | tf_op jit(solution)/shard_map/pallas_call | solution.py:34
  48.0 1.8 %collective-permute-start.6 = (bf16[11,64,128]{2,1,0:T(8,128)(2,1)}, bf16[11,64,128]{2,1,0:T(8,128)(2,1)S(1)}, u32[]{:S(2)}, u32[]{:S(2)}) collective-permute-start(bf16[11,64,128]{2,1,0:T(8,128)(2,1)} %get-tuple-element.37), channel_id=1, source_target_pairs={{0,1},{1,0},{2,3},{3,2},{4,5},{5,4},{6,7},{7,6},{8,9},{9,8},{10,11... | collective-permute-start | bytes 540680 | tf_op jit(solution)/shard_map/ppermute | solution.py:394
  49.8 2.1 %collective-permute-start.7 = (bf16[11,64,128]{2,1,0:T(8,128)(2,1)}, bf16[11,64,128]{2,1,0:T(8,128)(2,1)S(1)}, u32[]{:S(2)}, u32[]{:S(2)}) collective-permute-start(bf16[11,64,128]{2,1,0:T(8,128)(2,1)} %get-tuple-element.38), channel_id=1, source_target_pairs={{0,2},{1,3},{2,0},{3,1},{4,6},{5,7},{6,4},{7,5},{8,10},{9,11},{10,... | collective-permute-start | bytes 540680 | tf_op jit(solution)/shard_map/ppermute | solution.py:394
  51.9 1.6 %shard_map.99 = (bf16[27,256,128]{2,1,0:T(8,128)(2,1)S(1)}, bf16[13,256,128]{2,1,0:T(8,128)(2,1)S(1)}, bf16[48,64,128]{2,1,0:T(8,128)(2,1)S(1)}) custom-call(bf16[108,64,128]{2,1,0:T(8,128)(2,1)} %all-to-all-done.landed, bf16[11,64,128]{2,1,0:T(8,128)(2,1)} %get-tuple-element.32.unread.refs_0_, ...), custom_call_target="tpu_custom_call", output_to_operand_aliasing={{2}: (2, {})} | custom-call | flops 1100000 | bytes 1024 | tf_op jit(solution)/shard_map/pallas_call | solution.py:34
  53.5 4.3 %collective-permute-start.10 = (bf16[13,256,128]{2,1,0:T(8,128)(2,1)S(1)}, bf16[13,256,128]{2,1,0:T(8,128)(2,1)S(1)}, u32[]{:S(2)}, u32[]{:S(2)}) collective-permute-start(bf16[13,256,128]{2,1,0:T(8,128)(2,1)S(1)} %get-tuple-element.42), channel_id=1, source_target_pairs={{4,8},{8,4},{5,9},{9,5},{6,10},{10,6},{7,11},{11,7},{20,24},{24,20... | collective-permute-start | bytes 2555912 | tf_op jit(solution)/shard_map/ppermute | solution.py:513
  57.9 0.8 collective-permute-done.6.refs_1_
  58.7 4.3 %collective-permute-start.5 = (bf16[48,64,128]{2,1,0:T(8,128)(2,1)S(1)}, bf16[48,64,128]{2,1,0:T(8,128)(2,1)S(1)}, u32[]{:S(2)}, u32[]{:S(2)}) collective-permute-start(bf16[48,64,128]{2,1,0:T(8,128)(2,1)S(1)} %get-tuple-element.34), channel_id=1, source_target_pairs={{4,8},{8,4},{5,9},{9,5},{6,10},{10,6},{7,11},{11,7},{20,24},{24,20... | collective-permute-start | bytes 2359304 | tf_op jit(solution)/shard_map/ppermute | solution.py:515
  63.1 1.0 %shard_map.100 = (bf16[7,256,128]{2,1,0:T(8,128)(2,1)S(1)}, bf16[3,256,128]{2,1,0:T(8,128)(2,1)S(1)}, bf16[2,256,128]{2,1,0:T(8,128)(2,1)S(1)}, f32[32,128]{1,0:T(8,128)S(1)}, f32[8,128]{1,0:T(8,128)}) custom-call(bf16[27,256,128]{2,1,0:T(8,128)(2,1)S(1)} %get-tuple-element.36.after_ref.all_ref, f32[16,256]{1,0:T(8,128)S(1)} %bitcast.10, ...), custom_call_target="tpu_custom_call" | custom-call | flops 32999999488 | bytes 1024 | tf_op jit(solution)/shard_map/pallas_call | solution.py:34
  64.2 4.0 %collective-permute-done.10.link_ref = bf16[13,256,128]{2,1,0:T(8,128)(2,1)S(1)} collective-permute-done((bf16[13,256,128]{2,1,0:T(8,128)(2,1)S(1)}, bf16[13,256,128]{2,1,0:T(8,128)(2,1)S(1)}, u32[]{:S(2)}, u32[]{:S(2)}) %collective-permute-start.10) | collective-permute-done | bytes 852000 | tf_op jit(solution)/shard_map/ppermute | solution.py:513
  68.2 1.3 %shard_map.101.begun_ref = f32[2,256,256]{2,1,0:T(8,128)S(1)} custom-call(bf16[27,256,128]{2,1,0:T(8,128)(2,1)S(1)} %get-tuple-element.36.after_ref.all_ref, bf16[13,256,128]{2,1,0:T(8,128)(2,1)S(1)} %collective-permute-done.9.core_ref, bf16[13,256,128]{2,1,0:T(8,128)(2,1)S(1)} %collective-permute-done.10.link_ref, f32[128,128]{1,0:T(8,128)S(1)} %bitcast.7, ...), custom_call_target="tpu_custom_call" | custom-call | flops 1100000 | bytes 1024 | tf_op jit(solution)/shard_map/pallas_call | solution.py:34
  69.4 1.5 %shard_map.102 = (bf16[16,64,128]{2,1,0:T(8,128)(2,1)}, f32[8,128]{1,0:T(8,128)}) custom-call(bf16[7,256,128]{2,1,0:T(8,128)(2,1)S(1)} %get-tuple-element.40.all_ref, bf16[3,256,128]{2,1,0:T(8,128)(2,1)S(1)} %get-tuple-element.41.beside_ref, f32[128,128]{1,0:T(8,128)S(1)} %bitcast.8, f32[2,256,256]{2,1,0:T(8,128)S(1)} %shard_map.101.begun_ref, ...), custom_call_target="tpu_custom_call" | custom-call | flops 1100000 | bytes 1024 | tf_op jit(solution)/shard_map/pallas_call | solution.py:34
  71.0 5.9 %all-to-all-start.1 = ((bf16[16,64,128]{2,1,0:T(8,128)(2,1)}), bf16[16,64,128]{2,1,0:T(8,128)(2,1)S(1)}, u32[]{:S(2)}, u32[]{:S(2)}) async-start(bf16[16,64,128]{2,1,0:T(8,128)(2,1)} %get-tuple-element.47), calls=%async_computation.1 | async-start | bytes 524288 | tf_op jit(solution)/shard_map/all_to_all | solution.py:555
  76.9 1.0 %copy-done.3 = bf16[48,64,128]{2,1,0:T(8,128)(2,1)} copy-done((bf16[48,64,128]{2,1,0:T(8,128)(2,1)}, bf16[48,64,128]{2,1,0:T(8,128)(2,1)S(1)}, u32[]{:S(2)}) %copy-start.3) | copy-done | bytes 786456
  77.8 7.2 %shard_map.103 = bf16[64,128,128]{2,1,0:T(8,128)(2,1)} custom-call(bf16[128,64,128]{2,1,0:T(8,128)(2,1)} %get-tuple-element.25.xt_hbm.xt_ref.last_ref.next_ref, bf16[128,64,128]{2,1,0:T(8,128)(2,1)} %get-tuple-element.25.xt_hbm.xt_ref.last_ref.next_ref, bf16[128,64,128]{2,1,0:T(8,128)(2,1)} %get-tuple-element.25.xt_hbm.xt_ref.last_ref.next_ref, ...), custom_call_target="tpu_custom_call" | custom-call | flops 1100000 | bytes 1024 | tf_op jit(solution)/shard_map/pallas_call | solution.py:34
  85.0 1.2 %all-to-all-done.1.parts_ref = bf16[16,64,128]{2,1,0:T(8,128)(2,1)S(1)} async-done(((bf16[16,64,128]{2,1,0:T(8,128)(2,1)}), bf16[16,64,128]{2,1,0:T(8,128)(2,1)S(1)}, u32[]{:S(2)}, u32[]{:S(2)}) %all-to-all-start.1) | async-done | bytes 262176 | tf_op jit(solution)/shard_map/all_to_all | solution.py:555
  86.2 0.7 shard_map.104
  (26 shorter events, 0.7 us)
Async XLA Ops:
  4.7 30.0 %collective-permute-start = (bf16[128,64,128]{2,1,0:T(8,128)(2,1)}, bf16[128,64,128]{2,1,0:T(8,128)(2,1)}, u32[]{:S(2)}, u32[]{:S(2)}) collective-permute-start(bf16[128,64,128]{2,1,0:T(8,128)(2,1)} %get-tuple-element.25.xt_hbm.xt_ref.last_ref.next_ref), channel_id=1, source_target_pairs={{0,4},{4,0},{8,12},{12,8},{1,5},{5,1},{9,13},{13,9},{2,6},{6,2},{1... | collective-permute-start | bytes 6291464 | tf_op jit(solution)/shard_map/ppermute | solution.py:430
  4.8 47.1 %all-to-all-start = ((bf16[108,64,128]{2,1,0:T(8,128)(2,1)}), bf16[108,64,128]{2,1,0:T(8,128)(2,1)}, u32[]{:S(2)}, u32[]{:S(2)}) async-start(bf16[108,64,128]{2,1,0:T(8,128)(2,1)} %get-tuple-element.27), calls=%async_computation | async-start | bytes 3538944 | tf_op jit(solution)/shard_map/all_to_all | solution.py:428
  10.8 23.8 %collective-permute-start.1 = (bf16[80,64,128]{2,1,0:T(8,128)(2,1)}, bf16[80,64,128]{2,1,0:T(8,128)(2,1)}, u32[]{:S(2)}, u32[]{:S(2)}) collective-permute-start(bf16[80,64,128]{2,1,0:T(8,128)(2,1)} %get-tuple-element.26), channel_id=1, source_target_pairs={{4,8},{8,4},{5,9},{9,5},{6,10},{10,6},{7,11},{11,7},{20,24},{24,20... | collective-permute-start | bytes 3932168 | tf_op jit(solution)/shard_map/ppermute | solution.py:429
  24.8 9.9 %collective-permute-start.2 = (bf16[16,64,128]{2,1,0:T(8,128)(2,1)}, bf16[16,64,128]{2,1,0:T(8,128)(2,1)S(1)}, u32[]{:S(2)}, u32[]{:S(2)}) collective-permute-start(bf16[16,64,128]{2,1,0:T(8,128)(2,1)} %get-tuple-element.29), channel_id=1, source_target_pairs={{0,4},{4,0},{8,12},{12,8},{1,5},{5,1},{9,13},{13,9},{2,6},{6,2},{1... | collective-permute-start | bytes 786440 | tf_op jit(solution)/shard_map/ppermute | solution.py:454
  24.9 9.8 %collective-permute-start.3 = (bf16[16,64,128]{2,1,0:T(8,128)(2,1)}, bf16[16,64,128]{2,1,0:T(8,128)(2,1)S(1)}, u32[]{:S(2)}, u32[]{:S(2)}) collective-permute-start(bf16[16,64,128]{2,1,0:T(8,128)(2,1)} %get-tuple-element.30), channel_id=1, source_target_pairs={{4,8},{8,4},{5,9},{9,5},{6,10},{10,6},{7,11},{11,7},{20,24},{24,20... | collective-permute-start | bytes 786440 | tf_op jit(solution)/shard_map/ppermute | solution.py:452
  27.0 7.6 %collective-permute-start.4 = (bf16[8,64,128]{2,1,0:T(8,128)(2,1)}, bf16[8,64,128]{2,1,0:T(8,128)(2,1)S(1)}, u32[]{:S(2)}, u32[]{:S(2)}) collective-permute-start(bf16[8,64,128]{2,1,0:T(8,128)(2,1)} %get-tuple-element.31), channel_id=1, source_target_pairs={{0,8},{4,12},{8,0},{12,4},{1,9},{5,13},{9,1},{13,5},{2,10},{6,14},... | collective-permute-start | bytes 393224 | tf_op jit(solution)/shard_map/ppermute | solution.py:453
  34.6 0.7 copy-start.6
  34.6 0.8 copy-start.4
  34.7 0.9 %copy-start.5 = (bf16[16,64,128]{2,1,0:T(8,128)(2,1)}, bf16[16,64,128]{2,1,0:T(8,128)(2,1)S(1)}, u32[]{:S(2)}) copy-start(bf16[16,64,128]{2,1,0:T(8,128)(2,1)S(1)} %collective-permute-done.3.refs_1_.link_ref) | copy-start | bytes 786436
  35.6 16.4 %copy-start = (bf16[48,64,128]{2,1,0:T(8,128)(2,1)S(1)}, bf16[48,64,128]{2,1,0:T(8,128)(2,1)}, u32[]{:S(2)}) copy-start(bf16[48,64,128]{2,1,0:T(8,128)(2,1)} %get-tuple-element.33.handed) | copy-start | bytes 2359300
  47.9 15.2 %copy-start.2 = (f32[256,16]{0,1:T(8,128)S(1)}, f32[256,16]{0,1:T(8,128)}, u32[]{:S(2)}) copy-start(f32[256,16]{0,1:T(8,128)} %param.14) | copy-start | bytes 49156
  48.0 10.7 %collective-permute-start.6 = (bf16[11,64,128]{2,1,0:T(8,128)(2,1)}, bf16[11,64,128]{2,1,0:T(8,128)(2,1)S(1)}, u32[]{:S(2)}, u32[]{:S(2)}) collective-permute-start(bf16[11,64,128]{2,1,0:T(8,128)(2,1)} %get-tuple-element.37), channel_id=1, source_target_pairs={{0,1},{1,0},{2,3},{3,2},{4,5},{5,4},{6,7},{7,6},{8,9},{9,8},{10,11... | collective-permute-start | bytes 540680 | tf_op jit(solution)/shard_map/ppermute | solution.py:394
  49.8 13.3 %collective-permute-start.7 = (bf16[11,64,128]{2,1,0:T(8,128)(2,1)}, bf16[11,64,128]{2,1,0:T(8,128)(2,1)S(1)}, u32[]{:S(2)}, u32[]{:S(2)}) collective-permute-start(bf16[11,64,128]{2,1,0:T(8,128)(2,1)} %get-tuple-element.38), channel_id=1, source_target_pairs={{0,2},{1,3},{2,0},{3,1},{4,6},{5,7},{6,4},{7,5},{8,10},{9,11},{10,... | collective-permute-start | bytes 540680 | tf_op jit(solution)/shard_map/ppermute | solution.py:394
  51.8 11.3 %collective-permute-start.8 = (bf16[11,64,128]{2,1,0:T(8,128)(2,1)}, bf16[11,64,128]{2,1,0:T(8,128)(2,1)S(1)}, u32[]{:S(2)}, u32[]{:S(2)}) collective-permute-start(bf16[11,64,128]{2,1,0:T(8,128)(2,1)} %get-tuple-element.39), channel_id=1, source_target_pairs={{0,3},{1,2},{2,1},{3,0},{4,7},{5,6},{6,5},{7,4},{8,11},{9,10},{10,... | collective-permute-start | bytes 540680 | tf_op jit(solution)/shard_map/ppermute | solution.py:394
  53.5 14.6 %collective-permute-start.10 = (bf16[13,256,128]{2,1,0:T(8,128)(2,1)S(1)}, bf16[13,256,128]{2,1,0:T(8,128)(2,1)S(1)}, u32[]{:S(2)}, u32[]{:S(2)}) collective-permute-start(bf16[13,256,128]{2,1,0:T(8,128)(2,1)S(1)} %get-tuple-element.42), channel_id=1, source_target_pairs={{4,8},{8,4},{5,9},{9,5},{6,10},{10,6},{7,11},{11,7},{20,24},{24,20... | collective-permute-start | bytes 2555912 | tf_op jit(solution)/shard_map/ppermute | solution.py:513
  57.8 10.4 %collective-permute-start.9 = (bf16[13,256,128]{2,1,0:T(8,128)(2,1)S(1)}, bf16[13,256,128]{2,1,0:T(8,128)(2,1)S(1)}, u32[]{:S(2)}, u32[]{:S(2)}) collective-permute-start(bf16[13,256,128]{2,1,0:T(8,128)(2,1)S(1)} %get-tuple-element.42), channel_id=1, source_target_pairs={{0,4},{4,0},{8,12},{12,8},{1,5},{5,1},{9,13},{13,9},{2,6},{6,2},{1... | collective-permute-start | bytes 2555912 | tf_op jit(solution)/shard_map/ppermute | solution.py:514
  58.7 18.2 %collective-permute-start.5 = (bf16[48,64,128]{2,1,0:T(8,128)(2,1)S(1)}, bf16[48,64,128]{2,1,0:T(8,128)(2,1)S(1)}, u32[]{:S(2)}, u32[]{:S(2)}) collective-permute-start(bf16[48,64,128]{2,1,0:T(8,128)(2,1)S(1)} %get-tuple-element.34), channel_id=1, source_target_pairs={{4,8},{8,4},{5,9},{9,5},{6,10},{10,6},{7,11},{11,7},{20,24},{24,20... | collective-permute-start | bytes 2359304 | tf_op jit(solution)/shard_map/ppermute | solution.py:515
  63.1 5.0 %copy-start.1 = (f32[1,128,128]{2,1,0:T(8,128)S(1)}, f32[1,128,128]{2,1,0:T(8,128)}, u32[]{:S(2)}) copy-start(f32[1,128,128]{2,1,0:T(8,128)} %param.9) | copy-start | bytes 196612
  71.0 15.2 %all-to-all-start.1 = ((bf16[16,64,128]{2,1,0:T(8,128)(2,1)}), bf16[16,64,128]{2,1,0:T(8,128)(2,1)S(1)}, u32[]{:S(2)}, u32[]{:S(2)}) async-start(bf16[16,64,128]{2,1,0:T(8,128)(2,1)} %get-tuple-element.47), calls=%async_computation.1 | async-start | bytes 524288 | tf_op jit(solution)/shard_map/all_to_all | solution.py:555
  76.9 1.0 %copy-start.3 = (bf16[48,64,128]{2,1,0:T(8,128)(2,1)}, bf16[48,64,128]{2,1,0:T(8,128)(2,1)S(1)}, u32[]{:S(2)}) copy-start(bf16[48,64,128]{2,1,0:T(8,128)(2,1)S(1)} %collective-permute-done.5.late_ref) | copy-start | bytes 2359300

commit v24 on v23

--- a/solution.py
+++ b/solution.py
@@ -83,9 +83,8 @@
         loads[c].wait()
         for y0 in range(c * share, (c + 1) * share, ROWS):
             for s0 in range(0, states, ROWS):
-                block = x[s0 : s0 + ROWS, y0 : y0 + ROWS, :].astype(F32)
-                turned = jnp.swapaxes(block, 0, 1).astype(BF16)
-                xt[y0 : y0 + ROWS, s0 : s0 + ROWS, :] = turned
+                block = x[s0 : s0 + ROWS, y0 : y0 + ROWS, :]
+                xt[y0 : y0 + ROWS, s0 : s0 + ROWS, :] = jnp.swapaxes(block, 0, 1)
         send(c * share, ahead, early, c * ahead)
         send(c * share + ahead, share - ahead, late, c * (share - ahead))
         send(c * share + first, count, message, c * (count + 1))
@@ -131,7 +130,7 @@
     per_group = LANES // proj_count
     chunks = sems.shape[0] - 1
     size = slots // chunks
-    unroll = 16
+    unroll = 32
     pairs = [(p_hbm.at[pl.ds(c * size, size)], p_ref.at[pl.ds(c * size, size)]) for c in range(chunks)]
     xt_load, *loads = start_all([(xt_hbm, xt_ref), *pairs], sems)
 
@@ -191,7 +190,7 @@
     slots, proj_count, _ = p_ref.shape
     groups, states = total.shape[0] // 3, total.shape[1]
     per_group = LANES // proj_count
-    unroll = 16
+    unroll = 32
     mine_load, load = start_all([(mine_hbm, mine_ref), (p_hbm, p_ref)], sems)
     sends = []
 
@@ -273,10 +272,9 @@
                 after = line(y + 1, rows).astype(F32)
                 beside = (before + after) + (core_ref[y, rows, :].astype(F32) + link(y, rows).astype(F32))
                 value = along[i * ROWS : (i + 1) * ROWS] + pot_ref[y : y + 1, :] * x
-                results.append(value + added_ref[y, rows, :] - 0.5 * beside)
+                results.append((value + added_ref[y, rows, :] - 0.5 * beside).astype(BF16))
                 before, x = x, after
-            turned = jnp.swapaxes(jnp.stack(results, axis=0), 0, 1).astype(BF16)
-            out_ref[rows, y0 : y0 + ROWS, :] = turned
+            out_ref[rows, y0 : y0 + ROWS, :] = jnp.swapaxes(jnp.stack(results, axis=0), 0, 1)
 
 
 def pass_half(all_ref, pass_hbm, sem):
@@ -402,7 +400,7 @@
     eye = np.eye(cols_z, dtype=np.float32)
     ring = jnp.asarray(3.0 * eye - 0.5 * (np.roll(eye, 1, axis=0) + np.roll(eye, -1, axis=0)), dtype=BF16)
 
-    ahead = share * 5 // 8
+    ahead = share * 9 // 16
     late_lines = lines - ahead * bands
     line_shape, late_shape = (lines, states, cols_z), (late_lines, states, cols_z)
     xt, early_part, late_part, message = call(
@@ -557,7 +555,7 @@
     steps = lines // span
     block = pl.BlockSpec((span, states, cols_z), lambda i: (i, 0, 0))
     (applied,) = call(
-        60,
+        62,
         functools.partial(stencil_kernel, share),
         (steps,),
         [

time: 88.3 us -> 88.3 us (level)
  waiting for transfers between devices: 13.6 us -> 21.8 us
  Pallas kernels: 39.7 us -> 36.4 us
  starting transfers between devices: 30.3 us -> 27.1 us
  local copies, waits for them, and re-layouts: 1.86 us -> 0.9 us
    ppermute x1, waiting for transfers between devices: 0.01 us -> 4.26 us  [local(): link_late = lax.ppermute(late_part, 'domain', link_pairs)]
    pallas_call x10, Pallas kernels: 39.7 us -> 36.4 us  [call(): pl.pallas_call(kernel, grid=grid, out_shape=shapes, in_specs=in_specs, ou...]
    all_to_all x1, waiting for transfers between devices: 0.02 us -> 3.22 us  [local(): lax.all_to_all(message, 'band', split_axis=0, concat_axis=0, tiled=True)]
    all_to_all x1, starting transfers between devices: 5.88 us -> 3.57 us  [local(): lax.all_to_all(blocks, ('domain', 'band'), split_axis=0, concat_axis=0, t...]
    ppermute x1, starting transfers between devices: 4.34 us -> 2.5 us  [local(): link_late = lax.ppermute(late_part, 'domain', link_pairs)]
    ppermute x3, waiting for transfers between devices: 0.88 us -> 2.17 us  [swapped(): lax.ppermute(values[k - 1], axis, [(i, i ^ k) for i in range(size)])]
    all_to_all x1, waiting for transfers between devices: 1.17 us -> 0.01 us  [local(): lax.all_to_all(blocks, ('domain', 'band'), split_axis=0, concat_axis=0, t...]
    unnamed x14 -> x12, local copies, waits for them, and re-layouts: 1.86 us -> 0.9 us
  transfers between devices with their start and end apart: 13 -> 13, of which waited for: 5 -> 6; matrix products, arithmetic and copies ran while one was open for 0% -> 0% of each run, Pallas kernels for 40% -> 36%
where the time goes in v24:
time: 88.3 us; the launch traced here: 87.6 us
  Pallas kernels  36.4 us (41%)
  starting transfers between devices  27.1 us (31%)
  waiting for transfers between devices  21.8 us (25%)
  between operations  1.43 us (2%)
  local copies, waits for them, and re-layouts  0.9 us (1%)
    pallas_call x10, Pallas kernels, call(): pl.pallas_call(kernel, grid=grid, out_shape=shapes, in_specs=in_specs, ou...  36.4 us
    ppermute x1, waiting for transfers between devices, local(): lax.ppermute(value, 'domain', pairs)  7.59 us
    all_to_all x1, starting transfers between devices, local(): lax.all_to_all(message, 'band', split_axis=0, concat_axis=0, tiled=True)  6.04 us
    ppermute x1, starting transfers between devices, local(): later_link = lax.ppermute(later_pass, 'domain', link_pairs)  5.12 us
    ppermute x1, waiting for transfers between devices, local(): later_link = lax.ppermute(later_pass, 'domain', link_pairs)  4.53 us
    ppermute x1, waiting for transfers between devices, local(): link_late = lax.ppermute(late_part, 'domain', link_pairs)  4.26 us
    ppermute x3, starting transfers between devices, swapped(): lax.ppermute(values[k - 1], axis, [(i, i ^ k) for i in range(size)])  3.98 us
    all_to_all x1, starting transfers between devices, local(): lax.all_to_all(blocks, ('domain', 'band'), split_axis=0, concat_axis=0, t...  3.57 us
  transfers between devices with their start and end apart: 13, of which 6 were waited for; matrix products, arithmetic and copies ran while one was open for 0% of the time, Pallas kernels for 36%

profile of v24, /device:TPU:1, one launch (start us, length us, event | category | flops | bytes accessed | tf_op | source)
XLA Modules:
  0.0 87.6 jit_solution(3614801131455991682)
XLA Ops:
  0.6 4.0 %shard_map.95 = (bf16[128,64,128]{2,1,0:T(8,128)(2,1)}, bf16[72,64,128]{2,1,0:T(8,128)(2,1)}, bf16[56,64,128]{2,1,0:T(8,128)(2,1)}, bf16[108,64,128]{2,1,0:T(8,128)(2,1)}) custom-call(bf16[64,128,128]{2,1,0:T(8,128)(2,1)} %bitcast.12), custom_call_target="tpu_custom_call" | custom-call | flops 1100000 | bytes 1024 | tf_op jit(solution)/shard_map/pallas_call | solution.py:34
  4.7 6.0 %all-to-all-start = ((bf16[108,64,128]{2,1,0:T(8,128)(2,1)}), bf16[108,64,128]{2,1,0:T(8,128)(2,1)}, u32[]{:S(2)}, u32[]{:S(2)}) async-start(bf16[108,64,128]{2,1,0:T(8,128)(2,1)} %get-tuple-element.27), calls=%async_computation | async-start | bytes 3538944 | tf_op jit(solution)/shard_map/all_to_all | solution.py:426
  10.8 3.3 %collective-permute-start.1 = (bf16[72,64,128]{2,1,0:T(8,128)(2,1)}, bf16[72,64,128]{2,1,0:T(8,128)(2,1)}, u32[]{:S(2)}, u32[]{:S(2)}) collective-permute-start(bf16[72,64,128]{2,1,0:T(8,128)(2,1)} %get-tuple-element.26), channel_id=1, source_target_pairs={{4,8},{8,4},{5,9},{9,5},{6,10},{10,6},{7,11},{11,7},{20,24},{24,20... | collective-permute-start | bytes 3538952 | tf_op jit(solution)/shard_map/ppermute | solution.py:427
  14.8 8.4 %shard_map.96 = (bf16[24,64,128]{2,1,0:T(8,128)(2,1)}, bf16[16,64,128]{2,1,0:T(8,128)(2,1)}, bf16[16,64,128]{2,1,0:T(8,128)(2,1)}, bf16[8,64,128]{2,1,0:T(8,128)(2,1)}) custom-call(s32[384]{0:T(512)} %atom_ref.3, s32[384]{0:T(512)} %line_ref.3, s32[1]{0:T(128)S(6)} %copy.13.count_ref, ...), custom_call_target="tpu_custom_call" | custom-call | flops 1100000 | bytes 1024 | tf_op jit(solution)/shard_map/pallas_call | solution.py:34
  23.3 2.2 %collective-permute-start.3 = (bf16[16,64,128]{2,1,0:T(8,128)(2,1)}, bf16[16,64,128]{2,1,0:T(8,128)(2,1)S(1)}, u32[]{:S(2)}, u32[]{:S(2)}) collective-permute-start(bf16[16,64,128]{2,1,0:T(8,128)(2,1)} %get-tuple-element.30), channel_id=1, source_target_pairs={{4,8},{8,4},{5,9},{9,5},{6,10},{10,6},{7,11},{11,7},{20,24},{24,20... | collective-permute-start | bytes 786440 | tf_op jit(solution)/shard_map/ppermute | solution.py:450
  25.6 7.6 %collective-permute-done.4.refs_2_.refs_0_ = bf16[8,64,128]{2,1,0:T(8,128)(2,1)S(1)} collective-permute-done((bf16[8,64,128]{2,1,0:T(8,128)(2,1)}, bf16[8,64,128]{2,1,0:T(8,128)(2,1)S(1)}, u32[]{:S(2)}, u32[]{:S(2)}) %collective-permute-start.4) | collective-permute-done | bytes 131104 | tf_op jit(solution)/shard_map/ppermute | solution.py:451
  33.2 0.6 copy-done.5
  34.1 10.6 %shard_map.98 = (f32[128,64,128]{2,1,0:T(8,128)}, bf16[11,64,128]{2,1,0:T(8,128)(2,1)}, bf16[11,64,128]{2,1,0:T(8,128)(2,1)}, bf16[11,64,128]{2,1,0:T(8,128)(2,1)}, bf16[11,64,128]{2,1,0:T(8,128)(2,1)}) custom-call(s32[384]{0:T(512)} %atom_ref.3, s32[384]{0:T(512)} %line_ref.3, s32[1]{0:T(128)S(6)} %copy.13.count_ref, ...), custom_call_target="tpu_custom_call" | custom-call | flops 8800000000 | bytes 1024 | tf_op jit(solution)/shard_map/pallas_call | solution.py:34
  44.7 1.8 %collective-permute-start.6 = (bf16[11,64,128]{2,1,0:T(8,128)(2,1)}, bf16[11,64,128]{2,1,0:T(8,128)(2,1)S(1)}, u32[]{:S(2)}, u32[]{:S(2)}) collective-permute-start(bf16[11,64,128]{2,1,0:T(8,128)(2,1)} %get-tuple-element.37), channel_id=1, source_target_pairs={{0,1},{1,0},{2,3},{3,2},{4,5},{5,4},{6,7},{7,6},{8,9},{9,8},{10,11... | collective-permute-start | bytes 540680 | tf_op jit(solution)/shard_map/ppermute | solution.py:392
  46.6 2.1 %collective-permute-start.7 = (bf16[11,64,128]{2,1,0:T(8,128)(2,1)}, bf16[11,64,128]{2,1,0:T(8,128)(2,1)S(1)}, u32[]{:S(2)}, u32[]{:S(2)}) collective-permute-start(bf16[11,64,128]{2,1,0:T(8,128)(2,1)} %get-tuple-element.38), channel_id=1, source_target_pairs={{0,2},{1,3},{2,0},{3,1},{4,6},{5,7},{6,4},{7,5},{8,10},{9,11},{10,... | collective-permute-start | bytes 540680 | tf_op jit(solution)/shard_map/ppermute | solution.py:392
  48.7 3.2 %all-to-all-done.landed = bf16[108,64,128]{2,1,0:T(8,128)(2,1)} async-done(((bf16[108,64,128]{2,1,0:T(8,128)(2,1)}), bf16[108,64,128]{2,1,0:T(8,128)(2,1)}, u32[]{:S(2)}, u32[]{:S(2)}) %all-to-all-start) | async-done | bytes 1769504 | tf_op jit(solution)/shard_map/all_to_all | solution.py:426
  51.9 1.6 %shard_map.99 = (bf16[27,256,128]{2,1,0:T(8,128)(2,1)S(1)}, bf16[13,256,128]{2,1,0:T(8,128)(2,1)S(1)}, bf16[56,64,128]{2,1,0:T(8,128)(2,1)S(1)}) custom-call(bf16[108,64,128]{2,1,0:T(8,128)(2,1)} %all-to-all-done.landed, bf16[11,64,128]{2,1,0:T(8,128)(2,1)} %get-tuple-element.32.unread.refs_0_, ...), custom_call_target="tpu_custom_call", output_to_operand_aliasing={{2}: (2, {})} | custom-call | flops 1100000 | bytes 1024 | tf_op jit(solution)/shard_map/pallas_call | solution.py:34
  53.5 5.1 %collective-permute-start.10 = (bf16[13,256,128]{2,1,0:T(8,128)(2,1)S(1)}, bf16[13,256,128]{2,1,0:T(8,128)(2,1)S(1)}, u32[]{:S(2)}, u32[]{:S(2)}) collective-permute-start(bf16[13,256,128]{2,1,0:T(8,128)(2,1)S(1)} %get-tuple-element.42), channel_id=1, source_target_pairs={{4,8},{8,4},{5,9},{9,5},{6,10},{10,6},{7,11},{11,7},{20,24},{24,20... | collective-permute-start | bytes 2555912 | tf_op jit(solution)/shard_map/ppermute | solution.py:511
  58.7 0.9 collective-permute-done.6.refs_1_
  59.6 2.5 %collective-permute-start.5 = (bf16[56,64,128]{2,1,0:T(8,128)(2,1)S(1)}, bf16[56,64,128]{2,1,0:T(8,128)(2,1)}, u32[]{:S(2)}, u32[]{:S(2)}) collective-permute-start(bf16[56,64,128]{2,1,0:T(8,128)(2,1)S(1)} %get-tuple-element.34), channel_id=1, source_target_pairs={{4,8},{8,4},{5,9},{9,5},{6,10},{10,6},{7,11},{11,7},{20,24},{24,20... | collective-permute-start | bytes 2752520 | tf_op jit(solution)/shard_map/ppermute | solution.py:513
  62.1 1.3 %collective-permute-done.7.refs_2_ = bf16[11,64,128]{2,1,0:T(8,128)(2,1)S(1)} collective-permute-done((bf16[11,64,128]{2,1,0:T(8,128)(2,1)}, bf16[11,64,128]{2,1,0:T(8,128)(2,1)S(1)}, u32[]{:S(2)}, u32[]{:S(2)}) %collective-permute-start.7) | collective-permute-done | bytes 180256 | tf_op jit(solution)/shard_map/ppermute | solution.py:392
  63.4 1.1 %shard_map.100 = (bf16[7,256,128]{2,1,0:T(8,128)(2,1)S(1)}, bf16[3,256,128]{2,1,0:T(8,128)(2,1)S(1)}, bf16[2,256,128]{2,1,0:T(8,128)(2,1)S(1)}, f32[32,128]{1,0:T(8,128)S(1)}, f32[8,128]{1,0:T(8,128)}) custom-call(bf16[27,256,128]{2,1,0:T(8,128)(2,1)S(1)} %get-tuple-element.36.after_ref.all_ref, f32[16,256]{1,0:T(8,128)S(1)} %bitcast.10, ...), custom_call_target="tpu_custom_call" | custom-call | flops 32999999488 | bytes 1024 | tf_op jit(solution)/shard_map/pallas_call | solution.py:34
  64.5 4.5 %collective-permute-done.10.link_ref = bf16[13,256,128]{2,1,0:T(8,128)(2,1)S(1)} collective-permute-done((bf16[13,256,128]{2,1,0:T(8,128)(2,1)S(1)}, bf16[13,256,128]{2,1,0:T(8,128)(2,1)S(1)}, u32[]{:S(2)}, u32[]{:S(2)}) %collective-permute-start.10) | collective-permute-done | bytes 852000 | tf_op jit(solution)/shard_map/ppermute | solution.py:511
  69.0 1.3 %shard_map.101.begun_ref = f32[2,256,256]{2,1,0:T(8,128)S(1)} custom-call(bf16[27,256,128]{2,1,0:T(8,128)(2,1)S(1)} %get-tuple-element.36.after_ref.all_ref, bf16[13,256,128]{2,1,0:T(8,128)(2,1)S(1)} %collective-permute-done.9.core_ref, bf16[13,256,128]{2,1,0:T(8,128)(2,1)S(1)} %collective-permute-done.10.link_ref, f32[128,128]{1,0:T(8,128)S(1)} %bitcast.7, ...), custom_call_target="tpu_custom_call" | custom-call | flops 1100000 | bytes 1024 | tf_op jit(solution)/shard_map/pallas_call | solution.py:34
  70.3 1.5 %shard_map.102 = (bf16[16,64,128]{2,1,0:T(8,128)(2,1)}, f32[8,128]{1,0:T(8,128)}) custom-call(bf16[7,256,128]{2,1,0:T(8,128)(2,1)S(1)} %get-tuple-element.40.all_ref, bf16[3,256,128]{2,1,0:T(8,128)(2,1)S(1)} %get-tuple-element.41.beside_ref, f32[128,128]{1,0:T(8,128)S(1)} %bitcast.8, f32[2,256,256]{2,1,0:T(8,128)S(1)} %shard_map.101.begun_ref, ...), custom_call_target="tpu_custom_call" | custom-call | flops 1100000 | bytes 1024 | tf_op jit(solution)/shard_map/pallas_call | solution.py:34
  71.8 3.6 %all-to-all-start.1 = ((bf16[16,64,128]{2,1,0:T(8,128)(2,1)}), bf16[16,64,128]{2,1,0:T(8,128)(2,1)S(1)}, u32[]{:S(2)}, u32[]{:S(2)}) async-start(bf16[16,64,128]{2,1,0:T(8,128)(2,1)} %get-tuple-element.47), calls=%async_computation.1 | async-start | bytes 524288 | tf_op jit(solution)/shard_map/all_to_all | solution.py:553
  75.4 4.3 %collective-permute-done.5.late_ref = bf16[56,64,128]{2,1,0:T(8,128)(2,1)} collective-permute-done((bf16[56,64,128]{2,1,0:T(8,128)(2,1)S(1)}, bf16[56,64,128]{2,1,0:T(8,128)(2,1)}, u32[]{:S(2)}, u32[]{:S(2)}) %collective-permute-start.5) | collective-permute-done | bytes 917536 | tf_op jit(solution)/shard_map/ppermute | solution.py:513
  79.7 7.2 %shard_map.103 = bf16[64,128,128]{2,1,0:T(8,128)(2,1)} custom-call(bf16[128,64,128]{2,1,0:T(8,128)(2,1)} %get-tuple-element.25.xt_hbm.xt_ref.last_ref.next_ref, bf16[128,64,128]{2,1,0:T(8,128)(2,1)} %get-tuple-element.25.xt_hbm.xt_ref.last_ref.next_ref, bf16[128,64,128]{2,1,0:T(8,128)(2,1)} %get-tuple-element.25.xt_hbm.xt_ref.last_ref.next_ref, ...), custom_call_target="tpu_custom_call" | custom-call | flops 1100000 | bytes 1024 | tf_op jit(solution)/shard_map/pallas_call | solution.py:34
  86.8 0.7 shard_map.104
  (24 shorter events, 0.7 us)
Async XLA Ops:
  4.6 28.6 %collective-permute-start = (bf16[128,64,128]{2,1,0:T(8,128)(2,1)}, bf16[128,64,128]{2,1,0:T(8,128)(2,1)}, u32[]{:S(2)}, u32[]{:S(2)}) collective-permute-start(bf16[128,64,128]{2,1,0:T(8,128)(2,1)} %get-tuple-element.25.xt_hbm.xt_ref.last_ref.next_ref), channel_id=1, source_target_pairs={{0,4},{4,0},{8,12},{12,8},{1,5},{5,1},{9,13},{13,9},{2,6},{6,2},{1... | collective-permute-start | bytes 6291464 | tf_op jit(solution)/shard_map/ppermute | solution.py:428
  4.7 47.2 %all-to-all-start = ((bf16[108,64,128]{2,1,0:T(8,128)(2,1)}), bf16[108,64,128]{2,1,0:T(8,128)(2,1)}, u32[]{:S(2)}, u32[]{:S(2)}) async-start(bf16[108,64,128]{2,1,0:T(8,128)(2,1)} %get-tuple-element.27), calls=%async_computation | async-start | bytes 3538944 | tf_op jit(solution)/shard_map/all_to_all | solution.py:426
  10.8 22.4 %collective-permute-start.1 = (bf16[72,64,128]{2,1,0:T(8,128)(2,1)}, bf16[72,64,128]{2,1,0:T(8,128)(2,1)}, u32[]{:S(2)}, u32[]{:S(2)}) collective-permute-start(bf16[72,64,128]{2,1,0:T(8,128)(2,1)} %get-tuple-element.26), channel_id=1, source_target_pairs={{4,8},{8,4},{5,9},{9,5},{6,10},{10,6},{7,11},{11,7},{20,24},{24,20... | collective-permute-start | bytes 3538952 | tf_op jit(solution)/shard_map/ppermute | solution.py:427
  23.2 10.0 %collective-permute-start.2 = (bf16[16,64,128]{2,1,0:T(8,128)(2,1)}, bf16[16,64,128]{2,1,0:T(8,128)(2,1)S(1)}, u32[]{:S(2)}, u32[]{:S(2)}) collective-permute-start(bf16[16,64,128]{2,1,0:T(8,128)(2,1)} %get-tuple-element.29), channel_id=1, source_target_pairs={{0,4},{4,0},{8,12},{12,8},{1,5},{5,1},{9,13},{13,9},{2,6},{6,2},{1... | collective-permute-start | bytes 786440 | tf_op jit(solution)/shard_map/ppermute | solution.py:452
  23.3 9.9 %collective-permute-start.3 = (bf16[16,64,128]{2,1,0:T(8,128)(2,1)}, bf16[16,64,128]{2,1,0:T(8,128)(2,1)S(1)}, u32[]{:S(2)}, u32[]{:S(2)}) collective-permute-start(bf16[16,64,128]{2,1,0:T(8,128)(2,1)} %get-tuple-element.30), channel_id=1, source_target_pairs={{4,8},{8,4},{5,9},{9,5},{6,10},{10,6},{7,11},{11,7},{20,24},{24,20... | collective-permute-start | bytes 786440 | tf_op jit(solution)/shard_map/ppermute | solution.py:450
  25.5 7.7 %collective-permute-start.4 = (bf16[8,64,128]{2,1,0:T(8,128)(2,1)}, bf16[8,64,128]{2,1,0:T(8,128)(2,1)S(1)}, u32[]{:S(2)}, u32[]{:S(2)}) collective-permute-start(bf16[8,64,128]{2,1,0:T(8,128)(2,1)} %get-tuple-element.31), channel_id=1, source_target_pairs={{0,8},{4,12},{8,0},{12,4},{1,9},{5,13},{9,1},{13,5},{2,10},{6,14},... | collective-permute-start | bytes 393224 | tf_op jit(solution)/shard_map/ppermute | solution.py:451
  33.2 0.7 copy-start.5
  33.2 0.8 copy-start.3
  33.2 0.9 %copy-start.4 = (bf16[16,64,128]{2,1,0:T(8,128)(2,1)}, bf16[16,64,128]{2,1,0:T(8,128)(2,1)S(1)}, u32[]{:S(2)}) copy-start(bf16[16,64,128]{2,1,0:T(8,128)(2,1)S(1)} %collective-permute-done.3.refs_1_.link_ref) | copy-start | bytes 786436
  34.1 17.8 %copy-start = (bf16[56,64,128]{2,1,0:T(8,128)(2,1)S(1)}, bf16[56,64,128]{2,1,0:T(8,128)(2,1)}, u32[]{:S(2)}) copy-start(bf16[56,64,128]{2,1,0:T(8,128)(2,1)} %get-tuple-element.33.handed) | copy-start | bytes 2752516
  44.7 18.7 %copy-start.2 = (f32[256,16]{0,1:T(8,128)S(1)}, f32[256,16]{0,1:T(8,128)}, u32[]{:S(2)}) copy-start(f32[256,16]{0,1:T(8,128)} %param.14) | copy-start | bytes 49156
  44.7 14.9 %collective-permute-start.6 = (bf16[11,64,128]{2,1,0:T(8,128)(2,1)}, bf16[11,64,128]{2,1,0:T(8,128)(2,1)S(1)}, u32[]{:S(2)}, u32[]{:S(2)}) collective-permute-start(bf16[11,64,128]{2,1,0:T(8,128)(2,1)} %get-tuple-element.37), channel_id=1, source_target_pairs={{0,1},{1,0},{2,3},{3,2},{4,5},{5,4},{6,7},{7,6},{8,9},{9,8},{10,11... | collective-permute-start | bytes 540680 | tf_op jit(solution)/shard_map/ppermute | solution.py:392
  46.6 16.9 %collective-permute-start.7 = (bf16[11,64,128]{2,1,0:T(8,128)(2,1)}, bf16[11,64,128]{2,1,0:T(8,128)(2,1)S(1)}, u32[]{:S(2)}, u32[]{:S(2)}) collective-permute-start(bf16[11,64,128]{2,1,0:T(8,128)(2,1)} %get-tuple-element.38), channel_id=1, source_target_pairs={{0,2},{1,3},{2,0},{3,1},{4,6},{5,7},{6,4},{7,5},{8,10},{9,11},{10,... | collective-permute-start | bytes 540680 | tf_op jit(solution)/shard_map/ppermute | solution.py:392
  48.6 14.8 %collective-permute-start.8 = (bf16[11,64,128]{2,1,0:T(8,128)(2,1)}, bf16[11,64,128]{2,1,0:T(8,128)(2,1)S(1)}, u32[]{:S(2)}, u32[]{:S(2)}) collective-permute-start(bf16[11,64,128]{2,1,0:T(8,128)(2,1)} %get-tuple-element.39), channel_id=1, source_target_pairs={{0,3},{1,2},{2,1},{3,0},{4,7},{5,6},{6,5},{7,4},{8,11},{9,10},{10,... | collective-permute-start | bytes 540680 | tf_op jit(solution)/shard_map/ppermute | solution.py:392
  53.5 15.5 %collective-permute-start.10 = (bf16[13,256,128]{2,1,0:T(8,128)(2,1)S(1)}, bf16[13,256,128]{2,1,0:T(8,128)(2,1)S(1)}, u32[]{:S(2)}, u32[]{:S(2)}) collective-permute-start(bf16[13,256,128]{2,1,0:T(8,128)(2,1)S(1)} %get-tuple-element.42), channel_id=1, source_target_pairs={{4,8},{8,4},{5,9},{9,5},{6,10},{10,6},{7,11},{11,7},{20,24},{24,20... | collective-permute-start | bytes 2555912 | tf_op jit(solution)/shard_map/ppermute | solution.py:511
  58.7 10.4 %collective-permute-start.9 = (bf16[13,256,128]{2,1,0:T(8,128)(2,1)S(1)}, bf16[13,256,128]{2,1,0:T(8,128)(2,1)S(1)}, u32[]{:S(2)}, u32[]{:S(2)}) collective-permute-start(bf16[13,256,128]{2,1,0:T(8,128)(2,1)S(1)} %get-tuple-element.42), channel_id=1, source_target_pairs={{0,4},{4,0},{8,12},{12,8},{1,5},{5,1},{9,13},{13,9},{2,6},{6,2},{1... | collective-permute-start | bytes 2555912 | tf_op jit(solution)/shard_map/ppermute | solution.py:512
  59.6 20.1 %collective-permute-start.5 = (bf16[56,64,128]{2,1,0:T(8,128)(2,1)S(1)}, bf16[56,64,128]{2,1,0:T(8,128)(2,1)}, u32[]{:S(2)}, u32[]{:S(2)}) collective-permute-start(bf16[56,64,128]{2,1,0:T(8,128)(2,1)S(1)} %get-tuple-element.34), channel_id=1, source_target_pairs={{4,8},{8,4},{5,9},{9,5},{6,10},{10,6},{7,11},{11,7},{20,24},{24,20... | collective-permute-start | bytes 2752520 | tf_op jit(solution)/shard_map/ppermute | solution.py:513
  63.4 5.6 %copy-start.1 = (f32[1,128,128]{2,1,0:T(8,128)S(1)}, f32[1,128,128]{2,1,0:T(8,128)}, u32[]{:S(2)}) copy-start(f32[1,128,128]{2,1,0:T(8,128)} %param.9) | copy-start | bytes 196612
  71.8 15.0 %all-to-all-start.1 = ((bf16[16,64,128]{2,1,0:T(8,128)(2,1)}), bf16[16,64,128]{2,1,0:T(8,128)(2,1)S(1)}, u32[]{:S(2)}, u32[]{:S(2)}) async-start(bf16[16,64,128]{2,1,0:T(8,128)(2,1)} %get-tuple-element.47), calls=%async_computation.1 | async-start | bytes 524288 | tf_op jit(solution)/shard_map/all_to_all | solution.py:553

commit v25 on v24

--- a/solution.py
+++ b/solution.py
@@ -130,7 +130,7 @@
     per_group = LANES // proj_count
     chunks = sems.shape[0] - 1
     size = slots // chunks
-    unroll = 32
+    unroll = 48
     pairs = [(p_hbm.at[pl.ds(c * size, size)], p_ref.at[pl.ds(c * size, size)]) for c in range(chunks)]
     xt_load, *loads = start_all([(xt_hbm, xt_ref), *pairs], sems)
 
@@ -190,7 +190,7 @@
     slots, proj_count, _ = p_ref.shape
     groups, states = total.shape[0] // 3, total.shape[1]
     per_group = LANES // proj_count
-    unroll = 32
+    unroll = 48
     mine_load, load = start_all([(mine_hbm, mine_ref), (p_hbm, p_ref)], sems)
     sends = []
 
@@ -400,7 +400,7 @@
     eye = np.eye(cols_z, dtype=np.float32)
     ring = jnp.asarray(3.0 * eye - 0.5 * (np.roll(eye, 1, axis=0) + np.roll(eye, -1, axis=0)), dtype=BF16)
 
-    ahead = share * 9 // 16
+    ahead = share * 3 // 4
     late_lines = lines - ahead * bands
     line_shape, late_shape = (lines, states, cols_z), (late_lines, states, cols_z)
     xt, early_part, late_part, message = call(

time: 88.3 us -> 89.1 us (level)
  starting transfers between devices: 27.1 us -> 31.3 us
  waiting for transfers between devices: 21.8 us -> 17.8 us
  Pallas kernels: 36.4 us -> 35.4 us
    ppermute x1, waiting for transfers between devices: 7.59 us -> 12.3 us  [local(): lax.ppermute(value, 'domain', pairs)]
    ppermute x1, waiting for transfers between devices: 4.26 us -> 0.01 us  [local(): link_late = lax.ppermute(late_part, 'domain', link_pairs)]
    all_to_all x1, waiting for transfers between devices: 3.22 us -> 0.01 us  [local(): lax.all_to_all(message, 'band', split_axis=0, concat_axis=0, tiled=True)]
    all_to_all x1, starting transfers between devices: 3.57 us -> 6.71 us  [local(): lax.all_to_all(blocks, ('domain', 'band'), split_axis=0, concat_axis=0, t...]
    ppermute x1, starting transfers between devices: 2.5 us -> 5.12 us  [local(): link_late = lax.ppermute(late_part, 'domain', link_pairs)]
    ppermute x3, waiting for transfers between devices: 2.17 us -> 0.58 us  [swapped(): lax.ppermute(values[k - 1], axis, [(i, i ^ k) for i in range(size)])]
    ppermute x1, starting transfers between devices: 5.12 us -> 3.68 us  [local(): later_link = lax.ppermute(later_pass, 'domain', link_pairs)]
    all_to_all x1, waiting for transfers between devices: 0.01 us -> 1.35 us  [local(): lax.all_to_all(blocks, ('domain', 'band'), split_axis=0, concat_axis=0, t...]
  transfers between devices with their start and end apart: 13 -> 13, of which waited for: 6 -> 4; matrix products, arithmetic and copies ran while one was open for 0% -> 0% of each run, Pallas kernels for 36% -> 35%
where the time goes in v25:
time: 89.1 us; the launch traced here: 87.7 us
  Pallas kernels  35.4 us (40%)
  starting transfers between devices  31.3 us (35%)
  waiting for transfers between devices  17.8 us (20%)
  local copies, waits for them, and re-layouts  1.76 us (2%)
  between operations  1.45 us (2%)
    pallas_call x10, Pallas kernels, call(): pl.pallas_call(kernel, grid=grid, out_shape=shapes, in_specs=in_specs, ou...  35.4 us
    ppermute x1, waiting for transfers between devices, local(): lax.ppermute(value, 'domain', pairs)  12.3 us
    all_to_all x1, starting transfers between devices, local(): lax.all_to_all(blocks, ('domain', 'band'), split_axis=0, concat_axis=0, t...  6.71 us
    all_to_all x1, starting transfers between devices, local(): lax.all_to_all(message, 'band', split_axis=0, concat_axis=0, tiled=True)  6.04 us
    ppermute x1, starting transfers between devices, local(): link_late = lax.ppermute(late_part, 'domain', link_pairs)  5.12 us
    ppermute x3, starting transfers between devices, swapped(): lax.ppermute(values[k - 1], axis, [(i, i ^ k) for i in range(size)])  3.97 us
    ppermute x1, starting transfers between devices, local(): later_link = lax.ppermute(later_pass, 'domain', link_pairs)  3.68 us
    ppermute x1, waiting for transfers between devices, local(): later_link = lax.ppermute(later_pass, 'domain', link_pairs)  3.5 us
  transfers between devices with their start and end apart: 13, of which 4 were waited for; matrix products, arithmetic and copies ran while one was open for 0% of the time, Pallas kernels for 35%

profile of v25, /device:TPU:1, one launch (start us, length us, event | category | flops | bytes accessed | tf_op | source)
XLA Modules:
  0.0 87.7 jit_solution(4333739173975277235)
XLA Ops:
  0.6 4.0 %shard_map.95 = (bf16[128,64,128]{2,1,0:T(8,128)(2,1)}, bf16[96,64,128]{2,1,0:T(8,128)(2,1)}, bf16[32,64,128]{2,1,0:T(8,128)(2,1)}, bf16[108,64,128]{2,1,0:T(8,128)(2,1)}) custom-call(bf16[64,128,128]{2,1,0:T(8,128)(2,1)} %bitcast.12), custom_call_target="tpu_custom_call" | custom-call | flops 1100000 | bytes 1024 | tf_op jit(solution)/shard_map/pallas_call | solution.py:34
  4.7 6.0 %all-to-all-start = ((bf16[108,64,128]{2,1,0:T(8,128)(2,1)}), bf16[108,64,128]{2,1,0:T(8,128)(2,1)}, u32[]{:S(2)}, u32[]{:S(2)}) async-start(bf16[108,64,128]{2,1,0:T(8,128)(2,1)} %get-tuple-element.27), calls=%async_computation | async-start | bytes 3538944 | tf_op jit(solution)/shard_map/all_to_all | solution.py:426
  10.8 3.3 %collective-permute-start.1 = (bf16[96,64,128]{2,1,0:T(8,128)(2,1)}, bf16[96,64,128]{2,1,0:T(8,128)(2,1)}, u32[]{:S(2)}, u32[]{:S(2)}) collective-permute-start(bf16[96,64,128]{2,1,0:T(8,128)(2,1)} %get-tuple-element.26), channel_id=1, source_target_pairs={{4,8},{8,4},{5,9},{9,5},{6,10},{10,6},{7,11},{11,7},{20,24},{24,20... | collective-permute-start | bytes 4718600 | tf_op jit(solution)/shard_map/ppermute | solution.py:427
  14.8 8.0 %shard_map.96 = (bf16[24,64,128]{2,1,0:T(8,128)(2,1)}, bf16[16,64,128]{2,1,0:T(8,128)(2,1)}, bf16[16,64,128]{2,1,0:T(8,128)(2,1)}, bf16[8,64,128]{2,1,0:T(8,128)(2,1)}) custom-call(s32[384]{0:T(512)} %atom_ref.3, s32[384]{0:T(512)} %line_ref.3, s32[1]{0:T(128)S(6)} %copy.13.count_ref, ...), custom_call_target="tpu_custom_call" | custom-call | flops 1100000 | bytes 1024 | tf_op jit(solution)/shard_map/pallas_call | solution.py:34
  22.8 2.2 %collective-permute-start.3 = (bf16[16,64,128]{2,1,0:T(8,128)(2,1)}, bf16[16,64,128]{2,1,0:T(8,128)(2,1)S(1)}, u32[]{:S(2)}, u32[]{:S(2)}) collective-permute-start(bf16[16,64,128]{2,1,0:T(8,128)(2,1)} %get-tuple-element.30), channel_id=1, source_target_pairs={{4,8},{8,4},{5,9},{9,5},{6,10},{10,6},{7,11},{11,7},{20,24},{24,20... | collective-permute-start | bytes 786440 | tf_op jit(solution)/shard_map/ppermute | solution.py:450
  25.1 12.3 %collective-permute-done.4.refs_2_.refs_0_ = bf16[8,64,128]{2,1,0:T(8,128)(2,1)S(1)} collective-permute-done((bf16[8,64,128]{2,1,0:T(8,128)(2,1)}, bf16[8,64,128]{2,1,0:T(8,128)(2,1)S(1)}, u32[]{:S(2)}, u32[]{:S(2)}) %collective-permute-start.4) | collective-permute-done | bytes 131104 | tf_op jit(solution)/shard_map/ppermute | solution.py:451
  37.4 0.6 copy-done.6
  38.0 0.1 copy-done.4
  38.3 10.2 %shard_map.98 = (f32[128,64,128]{2,1,0:T(8,128)}, bf16[11,64,128]{2,1,0:T(8,128)(2,1)}, bf16[11,64,128]{2,1,0:T(8,128)(2,1)}, bf16[11,64,128]{2,1,0:T(8,128)(2,1)}, bf16[11,64,128]{2,1,0:T(8,128)(2,1)}) custom-call(s32[384]{0:T(512)} %atom_ref.3, s32[384]{0:T(512)} %line_ref.3, s32[1]{0:T(128)S(6)} %copy.13.count_ref, ...), custom_call_target="tpu_custom_call" | custom-call | flops 8800000000 | bytes 1024 | tf_op jit(solution)/shard_map/pallas_call | solution.py:34
  48.5 1.8 %collective-permute-start.6 = (bf16[11,64,128]{2,1,0:T(8,128)(2,1)}, bf16[11,64,128]{2,1,0:T(8,128)(2,1)S(1)}, u32[]{:S(2)}, u32[]{:S(2)}) collective-permute-start(bf16[11,64,128]{2,1,0:T(8,128)(2,1)} %get-tuple-element.37), channel_id=1, source_target_pairs={{0,1},{1,0},{2,3},{3,2},{4,5},{5,4},{6,7},{7,6},{8,9},{9,8},{10,11... | collective-permute-start | bytes 540680 | tf_op jit(solution)/shard_map/ppermute | solution.py:392
  50.3 2.1 %collective-permute-start.7 = (bf16[11,64,128]{2,1,0:T(8,128)(2,1)}, bf16[11,64,128]{2,1,0:T(8,128)(2,1)S(1)}, u32[]{:S(2)}, u32[]{:S(2)}) collective-permute-start(bf16[11,64,128]{2,1,0:T(8,128)(2,1)} %get-tuple-element.38), channel_id=1, source_target_pairs={{0,2},{1,3},{2,0},{3,1},{4,6},{5,7},{6,4},{7,5},{8,10},{9,11},{10,... | collective-permute-start | bytes 540680 | tf_op jit(solution)/shard_map/ppermute | solution.py:392
  52.5 1.6 %shard_map.99 = (bf16[27,256,128]{2,1,0:T(8,128)(2,1)S(1)}, bf16[13,256,128]{2,1,0:T(8,128)(2,1)S(1)}, bf16[32,64,128]{2,1,0:T(8,128)(2,1)S(1)}) custom-call(bf16[108,64,128]{2,1,0:T(8,128)(2,1)} %all-to-all-done.landed, bf16[11,64,128]{2,1,0:T(8,128)(2,1)} %get-tuple-element.32.unread.refs_0_, ...), custom_call_target="tpu_custom_call", output_to_operand_aliasing={{2}: (2, {})} | custom-call | flops 1100000 | bytes 1024 | tf_op jit(solution)/shard_map/pallas_call | solution.py:34
  54.1 3.7 %collective-permute-start.10 = (bf16[13,256,128]{2,1,0:T(8,128)(2,1)S(1)}, bf16[13,256,128]{2,1,0:T(8,128)(2,1)S(1)}, u32[]{:S(2)}, u32[]{:S(2)}) collective-permute-start(bf16[13,256,128]{2,1,0:T(8,128)(2,1)S(1)} %get-tuple-element.42), channel_id=1, source_target_pairs={{4,8},{8,4},{5,9},{9,5},{6,10},{10,6},{7,11},{11,7},{20,24},{24,20... | collective-permute-start | bytes 2555912 | tf_op jit(solution)/shard_map/ppermute | solution.py:511
  57.8 5.1 %collective-permute-start.5 = (bf16[32,64,128]{2,1,0:T(8,128)(2,1)S(1)}, bf16[32,64,128]{2,1,0:T(8,128)(2,1)S(1)}, u32[]{:S(2)}, u32[]{:S(2)}) collective-permute-start(bf16[32,64,128]{2,1,0:T(8,128)(2,1)S(1)} %get-tuple-element.34), channel_id=1, source_target_pairs={{4,8},{8,4},{5,9},{9,5},{6,10},{10,6},{7,11},{11,7},{20,24},{24,20... | collective-permute-start | bytes 1572872 | tf_op jit(solution)/shard_map/ppermute | solution.py:513
  63.0 0.6 collective-permute-done.8.refs_3_
  63.5 1.0 %shard_map.100 = (bf16[7,256,128]{2,1,0:T(8,128)(2,1)S(1)}, bf16[3,256,128]{2,1,0:T(8,128)(2,1)S(1)}, bf16[2,256,128]{2,1,0:T(8,128)(2,1)S(1)}, f32[32,128]{1,0:T(8,128)S(1)}, f32[8,128]{1,0:T(8,128)}) custom-call(bf16[27,256,128]{2,1,0:T(8,128)(2,1)S(1)} %get-tuple-element.36.after_ref.all_ref, f32[16,256]{1,0:T(8,128)S(1)} %bitcast.10, ...), custom_call_target="tpu_custom_call" | custom-call | flops 32999999488 | bytes 1024 | tf_op jit(solution)/shard_map/pallas_call | solution.py:34
  64.6 3.5 %collective-permute-done.10.link_ref = bf16[13,256,128]{2,1,0:T(8,128)(2,1)S(1)} collective-permute-done((bf16[13,256,128]{2,1,0:T(8,128)(2,1)S(1)}, bf16[13,256,128]{2,1,0:T(8,128)(2,1)S(1)}, u32[]{:S(2)}, u32[]{:S(2)}) %collective-permute-start.10) | collective-permute-done | bytes 852000 | tf_op jit(solution)/shard_map/ppermute | solution.py:511
  68.1 1.3 %shard_map.101.begun_ref = f32[2,256,256]{2,1,0:T(8,128)S(1)} custom-call(bf16[27,256,128]{2,1,0:T(8,128)(2,1)S(1)} %get-tuple-element.36.after_ref.all_ref, bf16[13,256,128]{2,1,0:T(8,128)(2,1)S(1)} %collective-permute-done.9.core_ref, bf16[13,256,128]{2,1,0:T(8,128)(2,1)S(1)} %collective-permute-done.10.link_ref, f32[128,128]{1,0:T(8,128)S(1)} %bitcast.7, ...), custom_call_target="tpu_custom_call" | custom-call | flops 1100000 | bytes 1024 | tf_op jit(solution)/shard_map/pallas_call | solution.py:34
  69.4 1.5 %shard_map.102 = (bf16[16,64,128]{2,1,0:T(8,128)(2,1)}, f32[8,128]{1,0:T(8,128)}) custom-call(bf16[7,256,128]{2,1,0:T(8,128)(2,1)S(1)} %get-tuple-element.40.all_ref, bf16[3,256,128]{2,1,0:T(8,128)(2,1)S(1)} %get-tuple-element.41.beside_ref, f32[128,128]{1,0:T(8,128)S(1)} %bitcast.8, f32[2,256,256]{2,1,0:T(8,128)S(1)} %shard_map.101.begun_ref, ...), custom_call_target="tpu_custom_call" | custom-call | flops 1100000 | bytes 1024 | tf_op jit(solution)/shard_map/pallas_call | solution.py:34
  70.9 6.7 %all-to-all-start.1 = ((bf16[16,64,128]{2,1,0:T(8,128)(2,1)}), bf16[16,64,128]{2,1,0:T(8,128)(2,1)S(1)}, u32[]{:S(2)}, u32[]{:S(2)}) async-start(bf16[16,64,128]{2,1,0:T(8,128)(2,1)} %get-tuple-element.47), calls=%async_computation.1 | async-start | bytes 524288 | tf_op jit(solution)/shard_map/all_to_all | solution.py:553
  77.6 0.9 copy-done.3
  78.5 7.1 %shard_map.103 = bf16[64,128,128]{2,1,0:T(8,128)(2,1)} custom-call(bf16[128,64,128]{2,1,0:T(8,128)(2,1)} %get-tuple-element.25.xt_hbm.xt_ref.last_ref.next_ref, bf16[128,64,128]{2,1,0:T(8,128)(2,1)} %get-tuple-element.25.xt_hbm.xt_ref.last_ref.next_ref, bf16[128,64,128]{2,1,0:T(8,128)(2,1)} %get-tuple-element.25.xt_hbm.xt_ref.last_ref.next_ref, ...), custom_call_target="tpu_custom_call" | custom-call | flops 1100000 | bytes 1024 | tf_op jit(solution)/shard_map/pallas_call | solution.py:34
  85.6 1.3 %all-to-all-done.1.parts_ref = bf16[16,64,128]{2,1,0:T(8,128)(2,1)S(1)} async-done(((bf16[16,64,128]{2,1,0:T(8,128)(2,1)}), bf16[16,64,128]{2,1,0:T(8,128)(2,1)S(1)}, u32[]{:S(2)}, u32[]{:S(2)}) %all-to-all-start.1) | async-done | bytes 262176 | tf_op jit(solution)/shard_map/all_to_all | solution.py:553
  87.0 0.7 shard_map.104
  (26 shorter events, 0.6 us)
Async XLA Ops:
  4.6 32.8 %collective-permute-start = (bf16[128,64,128]{2,1,0:T(8,128)(2,1)}, bf16[128,64,128]{2,1,0:T(8,128)(2,1)}, u32[]{:S(2)}, u32[]{:S(2)}) collective-permute-start(bf16[128,64,128]{2,1,0:T(8,128)(2,1)} %get-tuple-element.25.xt_hbm.xt_ref.last_ref.next_ref), channel_id=1, source_target_pairs={{0,4},{4,0},{8,12},{12,8},{1,5},{5,1},{9,13},{13,9},{2,6},{6,2},{1... | collective-permute-start | bytes 6291464 | tf_op jit(solution)/shard_map/ppermute | solution.py:428
  4.7 47.7 %all-to-all-start = ((bf16[108,64,128]{2,1,0:T(8,128)(2,1)}), bf16[108,64,128]{2,1,0:T(8,128)(2,1)}, u32[]{:S(2)}, u32[]{:S(2)}) async-start(bf16[108,64,128]{2,1,0:T(8,128)(2,1)} %get-tuple-element.27), calls=%async_computation | async-start | bytes 3538944 | tf_op jit(solution)/shard_map/all_to_all | solution.py:426
  10.8 26.6 %collective-permute-start.1 = (bf16[96,64,128]{2,1,0:T(8,128)(2,1)}, bf16[96,64,128]{2,1,0:T(8,128)(2,1)}, u32[]{:S(2)}, u32[]{:S(2)}) collective-permute-start(bf16[96,64,128]{2,1,0:T(8,128)(2,1)} %get-tuple-element.26), channel_id=1, source_target_pairs={{4,8},{8,4},{5,9},{9,5},{6,10},{10,6},{7,11},{11,7},{20,24},{24,20... | collective-permute-start | bytes 4718600 | tf_op jit(solution)/shard_map/ppermute | solution.py:427
  22.7 14.7 %collective-permute-start.2 = (bf16[16,64,128]{2,1,0:T(8,128)(2,1)}, bf16[16,64,128]{2,1,0:T(8,128)(2,1)S(1)}, u32[]{:S(2)}, u32[]{:S(2)}) collective-permute-start(bf16[16,64,128]{2,1,0:T(8,128)(2,1)} %get-tuple-element.29), channel_id=1, source_target_pairs={{0,4},{4,0},{8,12},{12,8},{1,5},{5,1},{9,13},{13,9},{2,6},{6,2},{1... | collective-permute-start | bytes 786440 | tf_op jit(solution)/shard_map/ppermute | solution.py:452
  22.8 14.6 %collective-permute-start.3 = (bf16[16,64,128]{2,1,0:T(8,128)(2,1)}, bf16[16,64,128]{2,1,0:T(8,128)(2,1)S(1)}, u32[]{:S(2)}, u32[]{:S(2)}) collective-permute-start(bf16[16,64,128]{2,1,0:T(8,128)(2,1)} %get-tuple-element.30), channel_id=1, source_target_pairs={{4,8},{8,4},{5,9},{9,5},{6,10},{10,6},{7,11},{11,7},{20,24},{24,20... | collective-permute-start | bytes 786440 | tf_op jit(solution)/shard_map/ppermute | solution.py:450
  25.0 12.4 %collective-permute-start.4 = (bf16[8,64,128]{2,1,0:T(8,128)(2,1)}, bf16[8,64,128]{2,1,0:T(8,128)(2,1)S(1)}, u32[]{:S(2)}, u32[]{:S(2)}) collective-permute-start(bf16[8,64,128]{2,1,0:T(8,128)(2,1)} %get-tuple-element.31), channel_id=1, source_target_pairs={{0,8},{4,12},{8,0},{12,4},{1,9},{5,13},{9,1},{13,5},{2,10},{6,14},... | collective-permute-start | bytes 393224 | tf_op jit(solution)/shard_map/ppermute | solution.py:451
  37.4 0.7 copy-start.6
  37.4 0.8 copy-start.4
  37.4 0.9 %copy-start.5 = (bf16[16,64,128]{2,1,0:T(8,128)(2,1)}, bf16[16,64,128]{2,1,0:T(8,128)(2,1)S(1)}, u32[]{:S(2)}) copy-start(bf16[16,64,128]{2,1,0:T(8,128)(2,1)S(1)} %collective-permute-done.3.refs_1_.link_ref) | copy-start | bytes 786436
  38.3 14.2 %copy-start.1 = (bf16[32,64,128]{2,1,0:T(8,128)(2,1)S(1)}, bf16[32,64,128]{2,1,0:T(8,128)(2,1)}, u32[]{:S(2)}) copy-start(bf16[32,64,128]{2,1,0:T(8,128)(2,1)} %get-tuple-element.33.handed) | copy-start | bytes 1572868
  48.5 15.1 %copy-start.2 = (f32[256,16]{0,1:T(8,128)S(1)}, f32[256,16]{0,1:T(8,128)}, u32[]{:S(2)}) copy-start(f32[256,16]{0,1:T(8,128)} %param.14) | copy-start | bytes 49156
  48.5 9.3 %collective-permute-start.6 = (bf16[11,64,128]{2,1,0:T(8,128)(2,1)}, bf16[11,64,128]{2,1,0:T(8,128)(2,1)S(1)}, u32[]{:S(2)}, u32[]{:S(2)}) collective-permute-start(bf16[11,64,128]{2,1,0:T(8,128)(2,1)} %get-tuple-element.37), channel_id=1, source_target_pairs={{0,1},{1,0},{2,3},{3,2},{4,5},{5,4},{6,7},{7,6},{8,9},{9,8},{10,11... | collective-permute-start | bytes 540680 | tf_op jit(solution)/shard_map/ppermute | solution.py:392
  50.3 12.7 %collective-permute-start.7 = (bf16[11,64,128]{2,1,0:T(8,128)(2,1)}, bf16[11,64,128]{2,1,0:T(8,128)(2,1)S(1)}, u32[]{:S(2)}, u32[]{:S(2)}) collective-permute-start(bf16[11,64,128]{2,1,0:T(8,128)(2,1)} %get-tuple-element.38), channel_id=1, source_target_pairs={{0,2},{1,3},{2,0},{3,1},{4,6},{5,7},{6,4},{7,5},{8,10},{9,11},{10,... | collective-permute-start | bytes 540680 | tf_op jit(solution)/shard_map/ppermute | solution.py:392
  52.4 11.2 %collective-permute-start.8 = (bf16[11,64,128]{2,1,0:T(8,128)(2,1)}, bf16[11,64,128]{2,1,0:T(8,128)(2,1)S(1)}, u32[]{:S(2)}, u32[]{:S(2)}) collective-permute-start(bf16[11,64,128]{2,1,0:T(8,128)(2,1)} %get-tuple-element.39), channel_id=1, source_target_pairs={{0,3},{1,2},{2,1},{3,0},{4,7},{5,6},{6,5},{7,4},{8,11},{9,10},{10,... | collective-permute-start | bytes 540680 | tf_op jit(solution)/shard_map/ppermute | solution.py:392
  54.1 14.0 %collective-permute-start.10 = (bf16[13,256,128]{2,1,0:T(8,128)(2,1)S(1)}, bf16[13,256,128]{2,1,0:T(8,128)(2,1)S(1)}, u32[]{:S(2)}, u32[]{:S(2)}) collective-permute-start(bf16[13,256,128]{2,1,0:T(8,128)(2,1)S(1)} %get-tuple-element.42), channel_id=1, source_target_pairs={{4,8},{8,4},{5,9},{9,5},{6,10},{10,6},{7,11},{11,7},{20,24},{24,20... | collective-permute-start | bytes 2555912 | tf_op jit(solution)/shard_map/ppermute | solution.py:511
  57.7 10.4 %collective-permute-start.9 = (bf16[13,256,128]{2,1,0:T(8,128)(2,1)S(1)}, bf16[13,256,128]{2,1,0:T(8,128)(2,1)S(1)}, u32[]{:S(2)}, u32[]{:S(2)}) collective-permute-start(bf16[13,256,128]{2,1,0:T(8,128)(2,1)S(1)} %get-tuple-element.42), channel_id=1, source_target_pairs={{0,4},{4,0},{8,12},{12,8},{1,5},{5,1},{9,13},{13,9},{2,6},{6,2},{1... | collective-permute-start | bytes 2555912 | tf_op jit(solution)/shard_map/ppermute | solution.py:512
  57.8 19.8 %collective-permute-start.5 = (bf16[32,64,128]{2,1,0:T(8,128)(2,1)S(1)}, bf16[32,64,128]{2,1,0:T(8,128)(2,1)S(1)}, u32[]{:S(2)}, u32[]{:S(2)}) collective-permute-start(bf16[32,64,128]{2,1,0:T(8,128)(2,1)S(1)} %get-tuple-element.34), channel_id=1, source_target_pairs={{4,8},{8,4},{5,9},{9,5},{6,10},{10,6},{7,11},{11,7},{20,24},{24,20... | collective-permute-start | bytes 1572872 | tf_op jit(solution)/shard_map/ppermute | solution.py:513
  63.5 4.6 %copy-start = (f32[1,128,128]{2,1,0:T(8,128)S(1)}, f32[1,128,128]{2,1,0:T(8,128)}, u32[]{:S(2)}) copy-start(f32[1,128,128]{2,1,0:T(8,128)} %param.9) | copy-start | bytes 196612
  70.9 16.1 %all-to-all-start.1 = ((bf16[16,64,128]{2,1,0:T(8,128)(2,1)}), bf16[16,64,128]{2,1,0:T(8,128)(2,1)S(1)}, u32[]{:S(2)}, u32[]{:S(2)}) async-start(bf16[16,64,128]{2,1,0:T(8,128)(2,1)} %get-tuple-element.47), calls=%async_computation.1 | async-start | bytes 524288 | tf_op jit(solution)/shard_map/all_to_all | solution.py:553
  77.6 0.9 copy-start.3

commit v26 on v25

--- a/solution.py
+++ b/solution.py
@@ -39,7 +39,7 @@
         out_specs=out_specs,
         scratch_shapes=scratch,
         input_output_aliases=aliases or {},
-        compiler_params=pltpu.CompilerParams(vmem_limit_bytes=room << 20),
+        compiler_params=pltpu.CompilerParams(vmem_limit_bytes=int(room * 2**20)),
         cost_estimate=pl.CostEstimate(flops=int(micros * 1.1e9), bytes_accessed=1 << 10, transcendentals=0),
     )(*args)
 
@@ -400,7 +400,7 @@
     eye = np.eye(cols_z, dtype=np.float32)
     ring = jnp.asarray(3.0 * eye - 0.5 * (np.roll(eye, 1, axis=0) + np.roll(eye, -1, axis=0)), dtype=BF16)
 
-    ahead = share * 3 // 4
+    ahead = share * 5 // 8
     late_lines = lines - ahead * bands
     line_shape, late_shape = (lines, states, cols_z), (late_lines, states, cols_z)
     xt, early_part, late_part, message = call(
@@ -555,7 +555,7 @@
     steps = lines // span
     block = pl.BlockSpec((span, states, cols_z), lambda i: (i, 0, 0))
     (applied,) = call(
-        62,
+        63.5,
         functools.partial(stencil_kernel, share),
         (steps,),
         [

time: 89.1 us -> 86.6 us (0.972)
  starting transfers between devices: 31.3 us -> 26.5 us
  waiting for transfers between devices: 17.8 us -> 20 us
    ppermute x1, waiting for transfers between devices: 12.3 us -> 9.35 us  [local(): lax.ppermute(value, 'domain', pairs)]
    ppermute x1, starting transfers between devices: 5.12 us -> 2.19 us  [local(): link_late = lax.ppermute(late_part, 'domain', link_pairs)]
    all_to_all x1, starting transfers between devices: 6.71 us -> 4.03 us  [local(): lax.all_to_all(blocks, ('domain', 'band'), split_axis=0, concat_axis=0, t...]
    ppermute x3, waiting for transfers between devices: 0.58 us -> 2.83 us  [swapped(): lax.ppermute(values[k - 1], axis, [(i, i ^ k) for i in range(size)])]
    all_to_all x1, waiting for transfers between devices: 0.01 us -> 2 us  [local(): lax.all_to_all(message, 'band', split_axis=0, concat_axis=0, tiled=True)]
    ppermute x1, waiting for transfers between devices: 0.01 us -> 1.6 us  [local(): link_late = lax.ppermute(late_part, 'domain', link_pairs)]
    all_to_all x1, waiting for transfers between devices: 1.35 us -> 0.01 us  [local(): lax.all_to_all(blocks, ('domain', 'band'), split_axis=0, concat_axis=0, t...]
  transfers between devices with their start and end apart: 13 -> 13, of which waited for: 4 -> 6; matrix products, arithmetic and copies ran while one was open for 0% -> 0% of each run, Pallas kernels for 35% -> 36%
where the time goes in v26:
time: 86.6 us; the launch traced here: 85.7 us
  Pallas kernels  36 us (42%)
  starting transfers between devices  26.5 us (31%)
  waiting for transfers between devices  20 us (23%)
  local copies, waits for them, and re-layouts  1.87 us (2%)
  between operations  1.43 us (2%)
    pallas_call x10, Pallas kernels, call(): pl.pallas_call(kernel, grid=grid, out_shape=shapes, in_specs=in_specs, ou...  36 us
    ppermute x1, waiting for transfers between devices, local(): lax.ppermute(value, 'domain', pairs)  9.35 us
    all_to_all x1, starting transfers between devices, local(): lax.all_to_all(message, 'band', split_axis=0, concat_axis=0, tiled=True)  6.04 us
    ppermute x1, starting transfers between devices, local(): later_link = lax.ppermute(later_pass, 'domain', link_pairs)  4.51 us
    ppermute x1, waiting for transfers between devices, local(): later_link = lax.ppermute(later_pass, 'domain', link_pairs)  4.17 us
    all_to_all x1, starting transfers between devices, local(): lax.all_to_all(blocks, ('domain', 'band'), split_axis=0, concat_axis=0, t...  4.03 us
    ppermute x3, starting transfers between devices, swapped(): lax.ppermute(values[k - 1], axis, [(i, i ^ k) for i in range(size)])  3.96 us
    ppermute x1, starting transfers between devices, local(): link_early = lax.ppermute(early_part, 'domain', link_pairs)  3.33 us
  transfers between devices with their start and end apart: 13, of which 6 were waited for; matrix products, arithmetic and copies ran while one was open for 0% of the time, Pallas kernels for 36%

profile of v26, /device:TPU:1, one launch (start us, length us, event | category | flops | bytes accessed | tf_op | source)
XLA Modules:
  0.0 85.7 jit_solution(2873825790102134793)
XLA Ops:
  0.6 4.0 %shard_map.95 = (bf16[128,64,128]{2,1,0:T(8,128)(2,1)}, bf16[80,64,128]{2,1,0:T(8,128)(2,1)}, bf16[48,64,128]{2,1,0:T(8,128)(2,1)}, bf16[108,64,128]{2,1,0:T(8,128)(2,1)}) custom-call(bf16[64,128,128]{2,1,0:T(8,128)(2,1)} %bitcast.12), custom_call_target="tpu_custom_call" | custom-call | flops 1100000 | bytes 1024 | tf_op jit(solution)/shard_map/pallas_call | solution.py:34
  4.7 6.0 %all-to-all-start = ((bf16[108,64,128]{2,1,0:T(8,128)(2,1)}), bf16[108,64,128]{2,1,0:T(8,128)(2,1)}, u32[]{:S(2)}, u32[]{:S(2)}) async-start(bf16[108,64,128]{2,1,0:T(8,128)(2,1)} %get-tuple-element.27), calls=%async_computation | async-start | bytes 3538944 | tf_op jit(solution)/shard_map/all_to_all | solution.py:426
  10.8 3.3 %collective-permute-start.1 = (bf16[80,64,128]{2,1,0:T(8,128)(2,1)}, bf16[80,64,128]{2,1,0:T(8,128)(2,1)}, u32[]{:S(2)}, u32[]{:S(2)}) collective-permute-start(bf16[80,64,128]{2,1,0:T(8,128)(2,1)} %get-tuple-element.26), channel_id=1, source_target_pairs={{4,8},{8,4},{5,9},{9,5},{6,10},{10,6},{7,11},{11,7},{20,24},{24,20... | collective-permute-start | bytes 3932168 | tf_op jit(solution)/shard_map/ppermute | solution.py:427
  14.8 8.2 %shard_map.96 = (bf16[24,64,128]{2,1,0:T(8,128)(2,1)}, bf16[16,64,128]{2,1,0:T(8,128)(2,1)}, bf16[16,64,128]{2,1,0:T(8,128)(2,1)}, bf16[8,64,128]{2,1,0:T(8,128)(2,1)}) custom-call(s32[384]{0:T(512)} %atom_ref.3, s32[384]{0:T(512)} %line_ref.3, s32[1]{0:T(128)S(6)} %copy.13.count_ref, ...), custom_call_target="tpu_custom_call" | custom-call | flops 1100000 | bytes 1024 | tf_op jit(solution)/shard_map/pallas_call | solution.py:34
  23.1 2.1 %collective-permute-start.3 = (bf16[16,64,128]{2,1,0:T(8,128)(2,1)}, bf16[16,64,128]{2,1,0:T(8,128)(2,1)S(1)}, u32[]{:S(2)}, u32[]{:S(2)}) collective-permute-start(bf16[16,64,128]{2,1,0:T(8,128)(2,1)} %get-tuple-element.30), channel_id=1, source_target_pairs={{4,8},{8,4},{5,9},{9,5},{6,10},{10,6},{7,11},{11,7},{20,24},{24,20... | collective-permute-start | bytes 786440 | tf_op jit(solution)/shard_map/ppermute | solution.py:450
  25.2 9.3 %collective-permute-done.4.refs_2_.refs_0_ = bf16[8,64,128]{2,1,0:T(8,128)(2,1)S(1)} collective-permute-done((bf16[8,64,128]{2,1,0:T(8,128)(2,1)}, bf16[8,64,128]{2,1,0:T(8,128)(2,1)S(1)}, u32[]{:S(2)}, u32[]{:S(2)}) %collective-permute-start.4) | collective-permute-done | bytes 131104 | tf_op jit(solution)/shard_map/ppermute | solution.py:451
  34.6 0.6 copy-done.6
  35.5 10.4 %shard_map.98 = (f32[128,64,128]{2,1,0:T(8,128)}, bf16[11,64,128]{2,1,0:T(8,128)(2,1)}, bf16[11,64,128]{2,1,0:T(8,128)(2,1)}, bf16[11,64,128]{2,1,0:T(8,128)(2,1)}, bf16[11,64,128]{2,1,0:T(8,128)(2,1)}) custom-call(s32[384]{0:T(512)} %atom_ref.3, s32[384]{0:T(512)} %line_ref.3, s32[1]{0:T(128)S(6)} %copy.13.count_ref, ...), custom_call_target="tpu_custom_call" | custom-call | flops 8800000000 | bytes 1024 | tf_op jit(solution)/shard_map/pallas_call | solution.py:34
  46.0 1.8 %collective-permute-start.6 = (bf16[11,64,128]{2,1,0:T(8,128)(2,1)}, bf16[11,64,128]{2,1,0:T(8,128)(2,1)S(1)}, u32[]{:S(2)}, u32[]{:S(2)}) collective-permute-start(bf16[11,64,128]{2,1,0:T(8,128)(2,1)} %get-tuple-element.37), channel_id=1, source_target_pairs={{0,1},{1,0},{2,3},{3,2},{4,5},{5,4},{6,7},{7,6},{8,9},{9,8},{10,11... | collective-permute-start | bytes 540680 | tf_op jit(solution)/shard_map/ppermute | solution.py:392
  47.8 2.1 %collective-permute-start.7 = (bf16[11,64,128]{2,1,0:T(8,128)(2,1)}, bf16[11,64,128]{2,1,0:T(8,128)(2,1)S(1)}, u32[]{:S(2)}, u32[]{:S(2)}) collective-permute-start(bf16[11,64,128]{2,1,0:T(8,128)(2,1)} %get-tuple-element.38), channel_id=1, source_target_pairs={{0,2},{1,3},{2,0},{3,1},{4,6},{5,7},{6,4},{7,5},{8,10},{9,11},{10,... | collective-permute-start | bytes 540680 | tf_op jit(solution)/shard_map/ppermute | solution.py:392
  49.9 2.0 %all-to-all-done.landed = bf16[108,64,128]{2,1,0:T(8,128)(2,1)} async-done(((bf16[108,64,128]{2,1,0:T(8,128)(2,1)}), bf16[108,64,128]{2,1,0:T(8,128)(2,1)}, u32[]{:S(2)}, u32[]{:S(2)}) %all-to-all-start) | async-done | bytes 1769504 | tf_op jit(solution)/shard_map/all_to_all | solution.py:426
  51.9 1.6 %shard_map.99 = (bf16[27,256,128]{2,1,0:T(8,128)(2,1)S(1)}, bf16[13,256,128]{2,1,0:T(8,128)(2,1)S(1)}, bf16[48,64,128]{2,1,0:T(8,128)(2,1)S(1)}) custom-call(bf16[108,64,128]{2,1,0:T(8,128)(2,1)} %all-to-all-done.landed, bf16[11,64,128]{2,1,0:T(8,128)(2,1)} %get-tuple-element.32.unread.refs_0_, ...), custom_call_target="tpu_custom_call", output_to_operand_aliasing={{2}: (2, {})} | custom-call | flops 1100000 | bytes 1024 | tf_op jit(solution)/shard_map/pallas_call | solution.py:34
  53.5 4.5 %collective-permute-start.10 = (bf16[13,256,128]{2,1,0:T(8,128)(2,1)S(1)}, bf16[13,256,128]{2,1,0:T(8,128)(2,1)S(1)}, u32[]{:S(2)}, u32[]{:S(2)}) collective-permute-start(bf16[13,256,128]{2,1,0:T(8,128)(2,1)S(1)} %get-tuple-element.42), channel_id=1, source_target_pairs={{4,8},{8,4},{5,9},{9,5},{6,10},{10,6},{7,11},{11,7},{20,24},{24,20... | collective-permute-start | bytes 2555912 | tf_op jit(solution)/shard_map/ppermute | solution.py:511
  58.1 2.5 %collective-permute-done.6.refs_1_ = bf16[11,64,128]{2,1,0:T(8,128)(2,1)S(1)} collective-permute-done((bf16[11,64,128]{2,1,0:T(8,128)(2,1)}, bf16[11,64,128]{2,1,0:T(8,128)(2,1)S(1)}, u32[]{:S(2)}, u32[]{:S(2)}) %collective-permute-start.6) | collective-permute-done | bytes 180256 | tf_op jit(solution)/shard_map/ppermute | solution.py:392
  60.7 2.2 %collective-permute-start.5 = (bf16[48,64,128]{2,1,0:T(8,128)(2,1)S(1)}, bf16[48,64,128]{2,1,0:T(8,128)(2,1)S(1)}, u32[]{:S(2)}, u32[]{:S(2)}) collective-permute-start(bf16[48,64,128]{2,1,0:T(8,128)(2,1)S(1)} %get-tuple-element.34), channel_id=1, source_target_pairs={{4,8},{8,4},{5,9},{9,5},{6,10},{10,6},{7,11},{11,7},{20,24},{24,20... | collective-permute-start | bytes 2359304 | tf_op jit(solution)/shard_map/ppermute | solution.py:513
  63.2 1.1 %shard_map.100 = (bf16[7,256,128]{2,1,0:T(8,128)(2,1)S(1)}, bf16[3,256,128]{2,1,0:T(8,128)(2,1)S(1)}, bf16[2,256,128]{2,1,0:T(8,128)(2,1)S(1)}, f32[32,128]{1,0:T(8,128)S(1)}, f32[8,128]{1,0:T(8,128)}) custom-call(bf16[27,256,128]{2,1,0:T(8,128)(2,1)S(1)} %get-tuple-element.36.after_ref.all_ref, f32[16,256]{1,0:T(8,128)S(1)} %bitcast.10, ...), custom_call_target="tpu_custom_call" | custom-call | flops 32999999488 | bytes 1024 | tf_op jit(solution)/shard_map/pallas_call | solution.py:34
  64.2 4.2 %collective-permute-done.10.link_ref = bf16[13,256,128]{2,1,0:T(8,128)(2,1)S(1)} collective-permute-done((bf16[13,256,128]{2,1,0:T(8,128)(2,1)S(1)}, bf16[13,256,128]{2,1,0:T(8,128)(2,1)S(1)}, u32[]{:S(2)}, u32[]{:S(2)}) %collective-permute-start.10) | collective-permute-done | bytes 852000 | tf_op jit(solution)/shard_map/ppermute | solution.py:511
  68.4 1.3 %shard_map.101.begun_ref = f32[2,256,256]{2,1,0:T(8,128)S(1)} custom-call(bf16[27,256,128]{2,1,0:T(8,128)(2,1)S(1)} %get-tuple-element.36.after_ref.all_ref, bf16[13,256,128]{2,1,0:T(8,128)(2,1)S(1)} %collective-permute-done.9.core_ref, bf16[13,256,128]{2,1,0:T(8,128)(2,1)S(1)} %collective-permute-done.10.link_ref, f32[128,128]{1,0:T(8,128)S(1)} %bitcast.7, ...), custom_call_target="tpu_custom_call" | custom-call | flops 1100000 | bytes 1024 | tf_op jit(solution)/shard_map/pallas_call | solution.py:34
  69.7 1.5 %shard_map.102 = (bf16[16,64,128]{2,1,0:T(8,128)(2,1)}, f32[8,128]{1,0:T(8,128)}) custom-call(bf16[7,256,128]{2,1,0:T(8,128)(2,1)S(1)} %get-tuple-element.40.all_ref, bf16[3,256,128]{2,1,0:T(8,128)(2,1)S(1)} %get-tuple-element.41.beside_ref, f32[128,128]{1,0:T(8,128)S(1)} %bitcast.8, f32[2,256,256]{2,1,0:T(8,128)S(1)} %shard_map.101.begun_ref, ...), custom_call_target="tpu_custom_call" | custom-call | flops 1100000 | bytes 1024 | tf_op jit(solution)/shard_map/pallas_call | solution.py:34
  71.2 4.0 %all-to-all-start.1 = ((bf16[16,64,128]{2,1,0:T(8,128)(2,1)}), bf16[16,64,128]{2,1,0:T(8,128)(2,1)S(1)}, u32[]{:S(2)}, u32[]{:S(2)}) async-start(bf16[16,64,128]{2,1,0:T(8,128)(2,1)} %get-tuple-element.47), calls=%async_computation.1 | async-start | bytes 524288 | tf_op jit(solution)/shard_map/all_to_all | solution.py:553
  75.2 1.6 %collective-permute-done.5.late_ref = bf16[48,64,128]{2,1,0:T(8,128)(2,1)S(1)} collective-permute-done((bf16[48,64,128]{2,1,0:T(8,128)(2,1)S(1)}, bf16[48,64,128]{2,1,0:T(8,128)(2,1)S(1)}, u32[]{:S(2)}, u32[]{:S(2)}) %collective-permute-start.5) | collective-permute-done | bytes 786464 | tf_op jit(solution)/shard_map/ppermute | solution.py:513
  76.8 1.0 %copy-done.3 = bf16[48,64,128]{2,1,0:T(8,128)(2,1)} copy-done((bf16[48,64,128]{2,1,0:T(8,128)(2,1)}, bf16[48,64,128]{2,1,0:T(8,128)(2,1)S(1)}, u32[]{:S(2)}) %copy-start.3) | copy-done | bytes 786456
  77.8 7.1 %shard_map.103 = bf16[64,128,128]{2,1,0:T(8,128)(2,1)} custom-call(bf16[128,64,128]{2,1,0:T(8,128)(2,1)} %get-tuple-element.25.xt_hbm.xt_ref.last_ref.next_ref, bf16[128,64,128]{2,1,0:T(8,128)(2,1)} %get-tuple-element.25.xt_hbm.xt_ref.last_ref.next_ref, bf16[128,64,128]{2,1,0:T(8,128)(2,1)} %get-tuple-element.25.xt_hbm.xt_ref.last_ref.next_ref, ...), custom_call_target="tpu_custom_call" | custom-call | flops 1100000 | bytes 1024 | tf_op jit(solution)/shard_map/pallas_call | solution.py:34
  85.0 0.7 shard_map.104
  (26 shorter events, 1.0 us)
Async XLA Ops:
  4.6 30.0 %collective-permute-start = (bf16[128,64,128]{2,1,0:T(8,128)(2,1)}, bf16[128,64,128]{2,1,0:T(8,128)(2,1)}, u32[]{:S(2)}, u32[]{:S(2)}) collective-permute-start(bf16[128,64,128]{2,1,0:T(8,128)(2,1)} %get-tuple-element.25.xt_hbm.xt_ref.last_ref.next_ref), channel_id=1, source_target_pairs={{0,4},{4,0},{8,12},{12,8},{1,5},{5,1},{9,13},{13,9},{2,6},{6,2},{1... | collective-permute-start | bytes 6291464 | tf_op jit(solution)/shard_map/ppermute | solution.py:428
  4.7 47.2 %all-to-all-start = ((bf16[108,64,128]{2,1,0:T(8,128)(2,1)}), bf16[108,64,128]{2,1,0:T(8,128)(2,1)}, u32[]{:S(2)}, u32[]{:S(2)}) async-start(bf16[108,64,128]{2,1,0:T(8,128)(2,1)} %get-tuple-element.27), calls=%async_computation | async-start | bytes 3538944 | tf_op jit(solution)/shard_map/all_to_all | solution.py:426
  10.8 23.8 %collective-permute-start.1 = (bf16[80,64,128]{2,1,0:T(8,128)(2,1)}, bf16[80,64,128]{2,1,0:T(8,128)(2,1)}, u32[]{:S(2)}, u32[]{:S(2)}) collective-permute-start(bf16[80,64,128]{2,1,0:T(8,128)(2,1)} %get-tuple-element.26), channel_id=1, source_target_pairs={{4,8},{8,4},{5,9},{9,5},{6,10},{10,6},{7,11},{11,7},{20,24},{24,20... | collective-permute-start | bytes 3932168 | tf_op jit(solution)/shard_map/ppermute | solution.py:427
  23.0 11.6 %collective-permute-start.2 = (bf16[16,64,128]{2,1,0:T(8,128)(2,1)}, bf16[16,64,128]{2,1,0:T(8,128)(2,1)S(1)}, u32[]{:S(2)}, u32[]{:S(2)}) collective-permute-start(bf16[16,64,128]{2,1,0:T(8,128)(2,1)} %get-tuple-element.29), channel_id=1, source_target_pairs={{0,4},{4,0},{8,12},{12,8},{1,5},{5,1},{9,13},{13,9},{2,6},{6,2},{1... | collective-permute-start | bytes 786440 | tf_op jit(solution)/shard_map/ppermute | solution.py:452
  23.1 11.5 %collective-permute-start.3 = (bf16[16,64,128]{2,1,0:T(8,128)(2,1)}, bf16[16,64,128]{2,1,0:T(8,128)(2,1)S(1)}, u32[]{:S(2)}, u32[]{:S(2)}) collective-permute-start(bf16[16,64,128]{2,1,0:T(8,128)(2,1)} %get-tuple-element.30), channel_id=1, source_target_pairs={{4,8},{8,4},{5,9},{9,5},{6,10},{10,6},{7,11},{11,7},{20,24},{24,20... | collective-permute-start | bytes 786440 | tf_op jit(solution)/shard_map/ppermute | solution.py:450
  25.1 9.4 %collective-permute-start.4 = (bf16[8,64,128]{2,1,0:T(8,128)(2,1)}, bf16[8,64,128]{2,1,0:T(8,128)(2,1)S(1)}, u32[]{:S(2)}, u32[]{:S(2)}) collective-permute-start(bf16[8,64,128]{2,1,0:T(8,128)(2,1)} %get-tuple-element.31), channel_id=1, source_target_pairs={{0,8},{4,12},{8,0},{12,4},{1,9},{5,13},{9,1},{13,5},{2,10},{6,14},... | collective-permute-start | bytes 393224 | tf_op jit(solution)/shard_map/ppermute | solution.py:451
  34.6 0.7 copy-start.6
  34.6 0.8 copy-start.4
  34.6 0.9 %copy-start.5 = (bf16[16,64,128]{2,1,0:T(8,128)(2,1)}, bf16[16,64,128]{2,1,0:T(8,128)(2,1)S(1)}, u32[]{:S(2)}) copy-start(bf16[16,64,128]{2,1,0:T(8,128)(2,1)S(1)} %collective-permute-done.3.refs_1_.link_ref) | copy-start | bytes 786436
  35.5 16.4 %copy-start = (bf16[48,64,128]{2,1,0:T(8,128)(2,1)S(1)}, bf16[48,64,128]{2,1,0:T(8,128)(2,1)}, u32[]{:S(2)}) copy-start(bf16[48,64,128]{2,1,0:T(8,128)(2,1)} %get-tuple-element.33.handed) | copy-start | bytes 2359300
  45.9 17.2 %copy-start.2 = (f32[256,16]{0,1:T(8,128)S(1)}, f32[256,16]{0,1:T(8,128)}, u32[]{:S(2)}) copy-start(f32[256,16]{0,1:T(8,128)} %param.14) | copy-start | bytes 49156
  46.0 14.7 %collective-permute-start.6 = (bf16[11,64,128]{2,1,0:T(8,128)(2,1)}, bf16[11,64,128]{2,1,0:T(8,128)(2,1)S(1)}, u32[]{:S(2)}, u32[]{:S(2)}) collective-permute-start(bf16[11,64,128]{2,1,0:T(8,128)(2,1)} %get-tuple-element.37), channel_id=1, source_target_pairs={{0,1},{1,0},{2,3},{3,2},{4,5},{5,4},{6,7},{7,6},{8,9},{9,8},{10,11... | collective-permute-start | bytes 540680 | tf_op jit(solution)/shard_map/ppermute | solution.py:392
  47.8 15.4 %collective-permute-start.7 = (bf16[11,64,128]{2,1,0:T(8,128)(2,1)}, bf16[11,64,128]{2,1,0:T(8,128)(2,1)S(1)}, u32[]{:S(2)}, u32[]{:S(2)}) collective-permute-start(bf16[11,64,128]{2,1,0:T(8,128)(2,1)} %get-tuple-element.38), channel_id=1, source_target_pairs={{0,2},{1,3},{2,0},{3,1},{4,6},{5,7},{6,4},{7,5},{8,10},{9,11},{10,... | collective-permute-start | bytes 540680 | tf_op jit(solution)/shard_map/ppermute | solution.py:392
  49.8 13.3 %collective-permute-start.8 = (bf16[11,64,128]{2,1,0:T(8,128)(2,1)}, bf16[11,64,128]{2,1,0:T(8,128)(2,1)S(1)}, u32[]{:S(2)}, u32[]{:S(2)}) collective-permute-start(bf16[11,64,128]{2,1,0:T(8,128)(2,1)} %get-tuple-element.39), channel_id=1, source_target_pairs={{0,3},{1,2},{2,1},{3,0},{4,7},{5,6},{6,5},{7,4},{8,11},{9,10},{10,... | collective-permute-start | bytes 540680 | tf_op jit(solution)/shard_map/ppermute | solution.py:392
  53.5 14.9 %collective-permute-start.10 = (bf16[13,256,128]{2,1,0:T(8,128)(2,1)S(1)}, bf16[13,256,128]{2,1,0:T(8,128)(2,1)S(1)}, u32[]{:S(2)}, u32[]{:S(2)}) collective-permute-start(bf16[13,256,128]{2,1,0:T(8,128)(2,1)S(1)} %get-tuple-element.42), channel_id=1, source_target_pairs={{4,8},{8,4},{5,9},{9,5},{6,10},{10,6},{7,11},{11,7},{20,24},{24,20... | collective-permute-start | bytes 2555912 | tf_op jit(solution)/shard_map/ppermute | solution.py:511
  58.0 10.4 %collective-permute-start.9 = (bf16[13,256,128]{2,1,0:T(8,128)(2,1)S(1)}, bf16[13,256,128]{2,1,0:T(8,128)(2,1)S(1)}, u32[]{:S(2)}, u32[]{:S(2)}) collective-permute-start(bf16[13,256,128]{2,1,0:T(8,128)(2,1)S(1)} %get-tuple-element.42), channel_id=1, source_target_pairs={{0,4},{4,0},{8,12},{12,8},{1,5},{5,1},{9,13},{13,9},{2,6},{6,2},{1... | collective-permute-start | bytes 2555912 | tf_op jit(solution)/shard_map/ppermute | solution.py:512
  60.7 16.2 %collective-permute-start.5 = (bf16[48,64,128]{2,1,0:T(8,128)(2,1)S(1)}, bf16[48,64,128]{2,1,0:T(8,128)(2,1)S(1)}, u32[]{:S(2)}, u32[]{:S(2)}) collective-permute-start(bf16[48,64,128]{2,1,0:T(8,128)(2,1)S(1)} %get-tuple-element.34), channel_id=1, source_target_pairs={{4,8},{8,4},{5,9},{9,5},{6,10},{10,6},{7,11},{11,7},{20,24},{24,20... | collective-permute-start | bytes 2359304 | tf_op jit(solution)/shard_map/ppermute | solution.py:513
  63.2 5.3 %copy-start.1 = (f32[1,128,128]{2,1,0:T(8,128)S(1)}, f32[1,128,128]{2,1,0:T(8,128)}, u32[]{:S(2)}) copy-start(f32[1,128,128]{2,1,0:T(8,128)} %param.9) | copy-start | bytes 196612
  71.2 13.8 %all-to-all-start.1 = ((bf16[16,64,128]{2,1,0:T(8,128)(2,1)}), bf16[16,64,128]{2,1,0:T(8,128)(2,1)S(1)}, u32[]{:S(2)}, u32[]{:S(2)}) async-start(bf16[16,64,128]{2,1,0:T(8,128)(2,1)} %get-tuple-element.47), calls=%async_computation.1 | async-start | bytes 524288 | tf_op jit(solution)/shard_map/all_to_all | solution.py:553
  76.8 1.0 %copy-start.3 = (bf16[48,64,128]{2,1,0:T(8,128)(2,1)}, bf16[48,64,128]{2,1,0:T(8,128)(2,1)S(1)}, u32[]{:S(2)}) copy-start(bf16[48,64,128]{2,1,0:T(8,128)(2,1)S(1)} %collective-permute-done.5.late_ref) | copy-start | bytes 2359300

commit v27 on v26

--- a/solution.py
+++ b/solution.py
@@ -298,22 +298,6 @@
     pass_half(all_ref, pass_hbm, pass_sem)
 
 
-def early_kernel(after_ref, energy_ref, *refs):
-    pieces, (all_ref, beside_ref, projs_ref, table_ref, token, sems) = refs[:-6], refs[-6:]
-    states = pieces[0].shape[1]
-    count, half, held = all_ref.shape[0] - 1, beside_ref.shape[0], projs_ref.shape[0]
-    pairs = []
-    for k, piece in enumerate(pieces):
-        at = pl.ds(pl.multiple_of((lax.axis_index("band") ^ k) * states, states), states)
-        pairs.append((piece.at[pl.ds(0, count)], all_ref.at[pl.ds(0, count), at, :]))
-        pairs.append((piece.at[pl.ds(count, half)], beside_ref.at[:, at, :]))
-        pairs.append((piece.at[pl.ds(count + half, held)], projs_ref.at[:, at, :]))
-    loads = start_all(pairs, sems)
-    all_ref[count] = after_ref[0]
-    table_ref[...] = energy_table(energy_ref)
-    wait_all(loads)
-
-
 def add_products(row, all_ref, beside_refs, pot_ref, acc):
     half = beside_refs[0].shape[0]
     group = 4
@@ -337,19 +321,40 @@
             acc[1] += lax.dot_general(flat_y, flat_x, NT, preferred_element_type=F32)
 
 
-def gram_kernel(first, share, all_ref, core_ref, link_ref, pot_ref, unread, acc):
+def final_kernel(
+    first, share, later_ref, core_ref, link_ref, pot_ref, energy_ref, own_hbm, unread, *refs
+):
+    pieces, (out_ref, token, lines_ref, beside_ref, projs, table, acc, sems) = refs[:-8], refs[-8:]
+    bands, states = len(pieces) + 1, own_hbm.shape[1]
+    band = lax.axis_index("band")
+    half, held = beside_ref.shape[0], projs.shape[0]
+    at = pl.ds(pl.multiple_of(band * states, states), states)
+    loads = start_all(
+        [
+            (own_hbm.at[pl.ds(0, first)], lines_ref.at[pl.ds(0, first), at, :]),
+            (own_hbm.at[pl.ds(first, half)], beside_ref.at[:, at, :]),
+            (own_hbm.at[pl.ds(first + half, held)], projs.at[:, at, :]),
+        ],
+        sems,
+    )
     acc[...] = jnp.zeros_like(acc)
-    add_products(lax.axis_index("band") * share + first, all_ref, (core_ref, link_ref), pot_ref, acc)
-
-
-def final_kernel(bands, share, all_ref, beside_ref, pot_ref, begun_ref, proj_ref, energy_ref, out_ref, token, acc):
-    acc[...] = begun_ref[...]
-    add_products(lax.axis_index("band") * share, all_ref, (beside_ref,), pot_ref, acc)
-    groups = proj_ref.shape[0]
-    first = (lax.axis_index("domain") * bands + lax.axis_index("band")) * groups
-    for g in range(groups):
-        here = proj_ref[g]
-        scaled = (here.astype(F32) * energy_ref[pl.ds(first + g, 1), :]).astype(BF16)
+    add_products(band * share + first, later_ref, (core_ref, link_ref), pot_ref, acc)
+    table[...] = energy_table(energy_ref)
+    lines_ref[first] = later_ref[0]
+    for k, piece in enumerate(pieces, 1):
+        at = pl.ds(pl.multiple_of((band ^ k) * states, states), states)
+        for i in range(first):
+            lines_ref[i, at, :] = piece[i]
+        for i in range(half):
+            beside_ref[i, at, :] = piece[first + i]
+        for i in range(held):
+            projs[i, at, :] = piece[first + half + i]
+    wait_all(loads)
+    add_products(band * share, lines_ref, (beside_ref,), pot_ref, acc)
+    row = (lax.axis_index("domain") * bands + band) * held
+    for g in range(held):
+        here = projs[g]
+        scaled = (here.astype(F32) * table[pl.ds(row + g, 1), :]).astype(BF16)
         acc[1] += lax.dot_general(scaled, here, NT, preferred_element_type=F32)
     hamil = 0.5 * (acc[1] + acc[1].T)
     domains = out_ref.shape[0] // bands
@@ -512,50 +517,41 @@
     later_core = lax.ppermute(later_pass, "domain", core_pairs)
     link_late = lax.ppermute(late_part, "domain", link_pairs)
 
-    early_all, early_beside, projs, energy_table_here, early_token = call(
-        32,
-        early_kernel,
-        (),
-        [NEAR, WHOLE, PINNED] + [FAR] * (bands - 1),
-        [NEAR, NEAR, NEAR, NEAR, PINNED],
-        [
-            ((first + 1, total_states, cols_z), BF16),
-            ((first // 2, total_states, cols_z), BF16),
-            ((held, total_states, LANES), BF16),
-            (energy_rows, F32),
-            token,
-        ],
-        [copies((3 * bands,))],
-        (later_all, energy, own_message, *early),
+    (early_token,) = call(
+        62.2,
+        wait_for,
+        (),
+        [UNREAD] * (bands - 1),
+        [PINNED],
+        [token],
+        [],
+        tuple(early),
         micros=30,
-    )
-    (begun,) = call(
-        32,
-        functools.partial(gram_kernel, first, share),
-        (),
-        [NEAR, WHOLE, WHOLE, WHOLE, PINNED],
-        [NEAR],
-        [((2, total_states, total_states), F32)],
-        [],
-        (later_all, later_core, later_link, pot, early_token),
     )
     parts = domains * bands
     blocks, final_token = call(
         32,
-        functools.partial(final_kernel, bands, share),
-        (),
-        [NEAR, NEAR, WHOLE, NEAR, NEAR, NEAR],
+        functools.partial(final_kernel, first, share),
+        (),
+        [NEAR] + [WHOLE] * 4 + [PINNED, PINNED] + [WHOLE] * (bands - 1),
         [WHOLE, PINNED],
         [((parts, states, 2 * total_states // domains), BF16), token],
-        [pltpu.VMEM((2, total_states, total_states), F32)],
-        (early_all, early_beside, pot, begun, projs, energy_table_here),
+        [
+            pltpu.VMEM((first + 1, total_states, cols_z), BF16),
+            pltpu.VMEM((first // 2, total_states, cols_z), BF16),
+            pltpu.VMEM((held, total_states, LANES), BF16),
+            pltpu.VMEM(energy_rows, F32),
+            pltpu.VMEM((2, total_states, total_states), F32),
+            copies((3,)),
+        ],
+        (later_all, later_core, later_link, pot, energy, own_message, early_token, *early),
     )
     summed = lax.all_to_all(blocks, ("domain", "band"), split_axis=0, concat_axis=0, tiled=True)
     span = 2 * ROWS
     steps = lines // span
     block = pl.BlockSpec((span, states, cols_z), lambda i: (i, 0, 0))
     (applied,) = call(
-        63.5,
+        48,
         functools.partial(stencil_kernel, share),
         (steps,),
         [

time: 86.6 us -> 97.3 us (1.12)
  local copies, waits for them, and re-layouts: 1.87 us -> 9.25 us
  waiting for transfers between devices: 20 us -> 21.4 us
    unnamed x14 -> x34, local copies, waits for them, and re-layouts: 1.87 us -> 9.25 us
    ppermute x1, waiting for transfers between devices: 4.17 us -> 7.23 us  [local(): later_link = lax.ppermute(later_pass, 'domain', link_pairs)]
    ppermute x3, waiting for transfers between devices: 2.83 us -> 0.01 us  [swapped(): lax.ppermute(values[k - 1], axis, [(i, i ^ k) for i in range(size)])]
    all_to_all x1, waiting for transfers between devices: 0.01 us -> 2.57 us  [local(): lax.all_to_all(blocks, ('domain', 'band'), split_axis=0, concat_axis=0, t...]
    ppermute x1, starting transfers between devices: 4.51 us -> 2.32 us  [local(): later_link = lax.ppermute(later_pass, 'domain', link_pairs)]
    ppermute x1, starting transfers between devices: 0.07 us -> 1.93 us  [local(): later_core = lax.ppermute(later_pass, 'domain', core_pairs)]
    ppermute x1, waiting for transfers between devices: 1.6 us -> 0.01 us  [local(): link_late = lax.ppermute(late_part, 'domain', link_pairs)]
    ppermute x1, starting transfers between devices: 2.19 us -> 3.36 us  [local(): link_late = lax.ppermute(late_part, 'domain', link_pairs)]
  transfers between devices with their start and end apart: 13 -> 13, of which waited for: 6 -> 4; matrix products, arithmetic and copies ran while one was open for 0% -> 0% of each run, Pallas kernels for 36% -> 33%
where the time goes in v27:
time: 97.3 us; the launch traced here: 95.7 us
  Pallas kernels  36.6 us (38%)
  starting transfers between devices  26.9 us (28%)
  waiting for transfers between devices  21.4 us (22%)
  local copies, waits for them, and re-layouts  9.25 us (10%)
  between operations  1.51 us (2%)
    pallas_call x9, Pallas kernels, call(): pl.pallas_call(kernel, grid=grid, out_shape=shapes, in_specs=in_specs, ou...  36.6 us
    ppermute x1, waiting for transfers between devices, local(): lax.ppermute(value, 'domain', pairs)  9.34 us
    unnamed x34, local copies, waits for them, and re-layouts  9.25 us
    ppermute x1, waiting for transfers between devices, local(): later_link = lax.ppermute(later_pass, 'domain', link_pairs)  7.23 us
    all_to_all x1, starting transfers between devices, local(): lax.all_to_all(message, 'band', split_axis=0, concat_axis=0, tiled=True)  6.04 us
    ppermute x3, starting transfers between devices, swapped(): lax.ppermute(values[k - 1], axis, [(i, i ^ k) for i in range(size)])  3.96 us
    all_to_all x1, starting transfers between devices, local(): lax.all_to_all(blocks, ('domain', 'band'), split_axis=0, concat_axis=0, t...  3.44 us
    ppermute x1, starting transfers between devices, local(): link_late = lax.ppermute(late_part, 'domain', link_pairs)  3.36 us
  transfers between devices with their start and end apart: 13, of which 4 were waited for; matrix products, arithmetic and copies ran while one was open for 0% of the time, Pallas kernels for 33%

profile of v27, /device:TPU:1, one launch (start us, length us, event | category | flops | bytes accessed | tf_op | source)
XLA Modules:
  0.0 95.7 jit_solution(17831166741505747907)
XLA Ops:
  0.6 4.0 %shard_map.95 = (bf16[128,64,128]{2,1,0:T(8,128)(2,1)}, bf16[80,64,128]{2,1,0:T(8,128)(2,1)}, bf16[48,64,128]{2,1,0:T(8,128)(2,1)}, bf16[108,64,128]{2,1,0:T(8,128)(2,1)}) custom-call(bf16[64,128,128]{2,1,0:T(8,128)(2,1)} %bitcast.11), custom_call_target="tpu_custom_call" | custom-call | flops 1100000 | bytes 1024 | tf_op jit(solution)/shard_map/pallas_call | solution.py:34
  4.7 6.0 %all-to-all-start = ((bf16[108,64,128]{2,1,0:T(8,128)(2,1)}), bf16[108,64,128]{2,1,0:T(8,128)(2,1)}, u32[]{:S(2)}, u32[]{:S(2)}) async-start(bf16[108,64,128]{2,1,0:T(8,128)(2,1)} %get-tuple-element.22), calls=%async_computation | async-start | bytes 3538944 | tf_op jit(solution)/shard_map/all_to_all | solution.py:431
  10.8 3.3 %collective-permute-start.1 = (bf16[80,64,128]{2,1,0:T(8,128)(2,1)}, bf16[80,64,128]{2,1,0:T(8,128)(2,1)}, u32[]{:S(2)}, u32[]{:S(2)}) collective-permute-start(bf16[80,64,128]{2,1,0:T(8,128)(2,1)} %get-tuple-element.21), channel_id=1, source_target_pairs={{4,8},{8,4},{5,9},{9,5},{6,10},{10,6},{7,11},{11,7},{20,24},{24,20... | collective-permute-start | bytes 3932168 | tf_op jit(solution)/shard_map/ppermute | solution.py:432
  14.8 8.0 %shard_map.96 = (bf16[24,64,128]{2,1,0:T(8,128)(2,1)}, bf16[16,64,128]{2,1,0:T(8,128)(2,1)}, bf16[16,64,128]{2,1,0:T(8,128)(2,1)}, bf16[8,64,128]{2,1,0:T(8,128)(2,1)}) custom-call(s32[384]{0:T(512)} %atom_ref.3, s32[384]{0:T(512)} %line_ref.3, s32[1]{0:T(128)S(6)} %copy.13.count_ref, ...), custom_call_target="tpu_custom_call" | custom-call | flops 1100000 | bytes 1024 | tf_op jit(solution)/shard_map/pallas_call | solution.py:34
  22.9 2.3 %collective-permute-start.3 = (bf16[16,64,128]{2,1,0:T(8,128)(2,1)}, bf16[16,64,128]{2,1,0:T(8,128)(2,1)S(1)}, u32[]{:S(2)}, u32[]{:S(2)}) collective-permute-start(bf16[16,64,128]{2,1,0:T(8,128)(2,1)} %get-tuple-element.25), channel_id=1, source_target_pairs={{4,8},{8,4},{5,9},{9,5},{6,10},{10,6},{7,11},{11,7},{20,24},{24,20... | collective-permute-start | bytes 786440 | tf_op jit(solution)/shard_map/ppermute | solution.py:455
  25.2 9.3 %collective-permute-done.4.refs_2_.refs_0_ = bf16[8,64,128]{2,1,0:T(8,128)(2,1)S(1)} collective-permute-done((bf16[8,64,128]{2,1,0:T(8,128)(2,1)}, bf16[8,64,128]{2,1,0:T(8,128)(2,1)S(1)}, u32[]{:S(2)}, u32[]{:S(2)}) %collective-permute-start.4) | collective-permute-done | bytes 131104 | tf_op jit(solution)/shard_map/ppermute | solution.py:456
  35.4 10.3 %shard_map.98 = (f32[128,64,128]{2,1,0:T(8,128)}, bf16[11,64,128]{2,1,0:T(8,128)(2,1)}, bf16[11,64,128]{2,1,0:T(8,128)(2,1)}, bf16[11,64,128]{2,1,0:T(8,128)(2,1)}, bf16[11,64,128]{2,1,0:T(8,128)(2,1)}) custom-call(s32[384]{0:T(512)} %atom_ref.3, s32[384]{0:T(512)} %line_ref.3, s32[1]{0:T(128)S(6)} %copy.13.count_ref, ...), custom_call_target="tpu_custom_call" | custom-call | flops 8800000000 | bytes 1024 | tf_op jit(solution)/shard_map/pallas_call | solution.py:34
  45.7 1.8 %collective-permute-start.8 = (bf16[11,64,128]{2,1,0:T(8,128)(2,1)}, bf16[11,64,128]{2,1,0:T(8,128)(2,1)S(1)}, u32[]{:S(2)}, u32[]{:S(2)}) collective-permute-start(bf16[11,64,128]{2,1,0:T(8,128)(2,1)} %get-tuple-element.33), channel_id=1, source_target_pairs={{0,1},{1,0},{2,3},{3,2},{4,5},{5,4},{6,7},{7,6},{8,9},{9,8},{10,11... | collective-permute-start | bytes 540680 | tf_op jit(solution)/shard_map/ppermute | solution.py:397
  47.5 2.1 %collective-permute-start.9 = (bf16[11,64,128]{2,1,0:T(8,128)(2,1)}, bf16[11,64,128]{2,1,0:T(8,128)(2,1)S(1)}, u32[]{:S(2)}, u32[]{:S(2)}) collective-permute-start(bf16[11,64,128]{2,1,0:T(8,128)(2,1)} %get-tuple-element.34), channel_id=1, source_target_pairs={{0,2},{1,3},{2,0},{3,1},{4,6},{5,7},{6,4},{7,5},{8,10},{9,11},{10,... | collective-permute-start | bytes 540680 | tf_op jit(solution)/shard_map/ppermute | solution.py:397
  49.7 2.2 %all-to-all-done.landed = bf16[108,64,128]{2,1,0:T(8,128)(2,1)} async-done(((bf16[108,64,128]{2,1,0:T(8,128)(2,1)}), bf16[108,64,128]{2,1,0:T(8,128)(2,1)}, u32[]{:S(2)}, u32[]{:S(2)}) %all-to-all-start) | async-done | bytes 1769504 | tf_op jit(solution)/shard_map/all_to_all | solution.py:431
  51.9 2.3 %shard_map.99 = (bf16[27,256,128]{2,1,0:T(8,128)(2,1)S(1)}, bf16[13,256,128]{2,1,0:T(8,128)(2,1)}, bf16[48,64,128]{2,1,0:T(8,128)(2,1)S(1)}) custom-call(bf16[108,64,128]{2,1,0:T(8,128)(2,1)} %all-to-all-done.landed, bf16[11,64,128]{2,1,0:T(8,128)(2,1)} %get-tuple-element.27.unread.own_hbm, ...), custom_call_target="tpu_custom_call", output_to_operand_aliasing={{2}: (2, {})} | custom-call | flops 1100000 | bytes 1024 | tf_op jit(solution)/shard_map/pallas_call | solution.py:34
  54.3 1.2 %copy-done.1 = bf16[27,256,128]{2,1,0:T(8,128)(2,1)} copy-done((bf16[27,256,128]{2,1,0:T(8,128)(2,1)}, bf16[27,256,128]{2,1,0:T(8,128)(2,1)S(1)}, u32[]{:S(2)}) %copy-start.1) | copy-done | bytes 1769496
  56.4 1.9 %collective-permute-start.6 = (bf16[13,256,128]{2,1,0:T(8,128)(2,1)}, bf16[13,256,128]{2,1,0:T(8,128)(2,1)S(1)}, u32[]{:S(2)}, u32[]{:S(2)}) collective-permute-start(bf16[13,256,128]{2,1,0:T(8,128)(2,1)} %get-tuple-element.32), channel_id=1, source_target_pairs={{0,4},{4,0},{8,12},{12,8},{1,5},{5,1},{9,13},{13,9},{2,6},{6,2},{1... | collective-permute-start | bytes 2555912 | tf_op jit(solution)/shard_map/ppermute | solution.py:517
  58.3 2.3 %collective-permute-start.7 = (bf16[13,256,128]{2,1,0:T(8,128)(2,1)}, bf16[13,256,128]{2,1,0:T(8,128)(2,1)}, u32[]{:S(2)}, u32[]{:S(2)}) collective-permute-start(bf16[13,256,128]{2,1,0:T(8,128)(2,1)} %get-tuple-element.32), channel_id=1, source_target_pairs={{4,8},{8,4},{5,9},{9,5},{6,10},{10,6},{7,11},{11,7},{20,24},{24,20... | collective-permute-start | bytes 2555912 | tf_op jit(solution)/shard_map/ppermute | solution.py:516
  60.7 3.4 %collective-permute-start.5 = (bf16[48,64,128]{2,1,0:T(8,128)(2,1)}, bf16[48,64,128]{2,1,0:T(8,128)(2,1)}, u32[]{:S(2)}, u32[]{:S(2)}) collective-permute-start(bf16[48,64,128]{2,1,0:T(8,128)(2,1)} %copy-done.4), channel_id=1, source_target_pairs={{4,8},{8,4},{5,9},{9,5},{6,10},{10,6},{7,11},{11,7},{20,24},{24,20... | collective-permute-start | bytes 2359304 | tf_op jit(solution)/shard_map/ppermute | solution.py:518
  65.4 7.2 %collective-permute-done.7.link_ref = bf16[13,256,128]{2,1,0:T(8,128)(2,1)} collective-permute-done((bf16[13,256,128]{2,1,0:T(8,128)(2,1)}, bf16[13,256,128]{2,1,0:T(8,128)(2,1)}, u32[]{:S(2)}, u32[]{:S(2)}) %collective-permute-start.7) | collective-permute-done | bytes 852000 | tf_op jit(solution)/shard_map/ppermute | solution.py:516
  72.7 1.5 %copy-done.2 = bf16[27,256,128]{2,1,0:T(8,128)(2,1)S(1)} copy-done((bf16[27,256,128]{2,1,0:T(8,128)(2,1)S(1)}, bf16[27,256,128]{2,1,0:T(8,128)(2,1)}, u32[]{:S(2)}) %copy-start.2) | copy-done | bytes 1769496
  74.1 0.9 copy-done.7
  75.1 0.9 copy-done.9
  76.0 0.9 copy-done.11
  77.6 5.0 %shard_map.101 = (bf16[16,64,128]{2,1,0:T(8,128)(2,1)}, f32[8,128]{1,0:T(8,128)}) custom-call(bf16[27,256,128]{2,1,0:T(8,128)(2,1)S(1)} %copy-done.2, bf16[13,256,128]{2,1,0:T(8,128)(2,1)S(1)} %collective-permute-done.6.core_ref, bf16[13,256,128]{2,1,0:T(8,128)(2,1)} %collective-permute-done.7.link_ref, f32[128,128]{1,0:T(8,128)S(1)} %bitcast.6, ...), custom_call_target="tpu_custom_call" | custom-call | flops 1100000 | bytes 1024 | tf_op jit(solution)/shard_map/pallas_call | solution.py:34
  82.6 3.4 %all-to-all-start.1 = ((bf16[16,64,128]{2,1,0:T(8,128)(2,1)}), bf16[16,64,128]{2,1,0:T(8,128)(2,1)S(1)}, u32[]{:S(2)}, u32[]{:S(2)}) async-start(bf16[16,64,128]{2,1,0:T(8,128)(2,1)} %get-tuple-element.37), calls=%async_computation.1 | async-start | bytes 524288 | tf_op jit(solution)/shard_map/all_to_all | solution.py:549
  86.1 6.3 %shard_map.102 = bf16[64,128,128]{2,1,0:T(8,128)(2,1)} custom-call(bf16[128,64,128]{2,1,0:T(8,128)(2,1)S(1)} %copy-done, bf16[128,64,128]{2,1,0:T(8,128)(2,1)S(1)} %copy-done, bf16[128,64,128]{2,1,0:T(8,128)(2,1)S(1)} %copy-done, bf16[128,64,128]{2,1,0:T(8,128)(2,1)} %collective-permute-done.refs_4_.beside_hbm.core_ref, ...), custom_call_target="tpu_custom_call" | custom-call | flops 1100000 | bytes 1024 | tf_op jit(solution)/shard_map/pallas_call | solution.py:34
  92.4 2.6 %all-to-all-done.1.parts_ref = bf16[16,64,128]{2,1,0:T(8,128)(2,1)S(1)} async-done(((bf16[16,64,128]{2,1,0:T(8,128)(2,1)}), bf16[16,64,128]{2,1,0:T(8,128)(2,1)S(1)}, u32[]{:S(2)}, u32[]{:S(2)}) %all-to-all-start.1) | async-done | bytes 262176 | tf_op jit(solution)/shard_map/all_to_all | solution.py:549
  (45 shorter events, 4.9 us)
Async XLA Ops:
  4.6 30.0 %collective-permute-start = (bf16[128,64,128]{2,1,0:T(8,128)(2,1)}, bf16[128,64,128]{2,1,0:T(8,128)(2,1)}, u32[]{:S(2)}, u32[]{:S(2)}) collective-permute-start(bf16[128,64,128]{2,1,0:T(8,128)(2,1)} %get-tuple-element.20.xt_hbm.xt_ref.last_ref.next_ref), channel_id=1, source_target_pairs={{0,4},{4,0},{8,12},{12,8},{1,5},{5,1},{9,13},{13,9},{2,6},{6,2},{1... | collective-permute-start | bytes 6291464 | tf_op jit(solution)/shard_map/ppermute | solution.py:433
  4.7 47.2 %all-to-all-start = ((bf16[108,64,128]{2,1,0:T(8,128)(2,1)}), bf16[108,64,128]{2,1,0:T(8,128)(2,1)}, u32[]{:S(2)}, u32[]{:S(2)}) async-start(bf16[108,64,128]{2,1,0:T(8,128)(2,1)} %get-tuple-element.22), calls=%async_computation | async-start | bytes 3538944 | tf_op jit(solution)/shard_map/all_to_all | solution.py:431
  10.8 23.8 %collective-permute-start.1 = (bf16[80,64,128]{2,1,0:T(8,128)(2,1)}, bf16[80,64,128]{2,1,0:T(8,128)(2,1)}, u32[]{:S(2)}, u32[]{:S(2)}) collective-permute-start(bf16[80,64,128]{2,1,0:T(8,128)(2,1)} %get-tuple-element.21), channel_id=1, source_target_pairs={{4,8},{8,4},{5,9},{9,5},{6,10},{10,6},{7,11},{11,7},{20,24},{24,20... | collective-permute-start | bytes 3932168 | tf_op jit(solution)/shard_map/ppermute | solution.py:432
  22.8 11.8 %collective-permute-start.2 = (bf16[16,64,128]{2,1,0:T(8,128)(2,1)}, bf16[16,64,128]{2,1,0:T(8,128)(2,1)S(1)}, u32[]{:S(2)}, u32[]{:S(2)}) collective-permute-start(bf16[16,64,128]{2,1,0:T(8,128)(2,1)} %get-tuple-element.24), channel_id=1, source_target_pairs={{0,4},{4,0},{8,12},{12,8},{1,5},{5,1},{9,13},{13,9},{2,6},{6,2},{1... | collective-permute-start | bytes 786440 | tf_op jit(solution)/shard_map/ppermute | solution.py:457
  22.9 11.7 %collective-permute-start.3 = (bf16[16,64,128]{2,1,0:T(8,128)(2,1)}, bf16[16,64,128]{2,1,0:T(8,128)(2,1)S(1)}, u32[]{:S(2)}, u32[]{:S(2)}) collective-permute-start(bf16[16,64,128]{2,1,0:T(8,128)(2,1)} %get-tuple-element.25), channel_id=1, source_target_pairs={{4,8},{8,4},{5,9},{9,5},{6,10},{10,6},{7,11},{11,7},{20,24},{24,20... | collective-permute-start | bytes 786440 | tf_op jit(solution)/shard_map/ppermute | solution.py:455
  25.2 9.4 %collective-permute-start.4 = (bf16[8,64,128]{2,1,0:T(8,128)(2,1)}, bf16[8,64,128]{2,1,0:T(8,128)(2,1)S(1)}, u32[]{:S(2)}, u32[]{:S(2)}) collective-permute-start(bf16[8,64,128]{2,1,0:T(8,128)(2,1)} %get-tuple-element.26), channel_id=1, source_target_pairs={{0,8},{4,12},{8,0},{12,4},{1,9},{5,13},{9,1},{13,5},{2,10},{6,14},... | collective-permute-start | bytes 393224 | tf_op jit(solution)/shard_map/ppermute | solution.py:456
  35.4 16.5 %copy-start.3 = (bf16[48,64,128]{2,1,0:T(8,128)(2,1)S(1)}, bf16[48,64,128]{2,1,0:T(8,128)(2,1)}, u32[]{:S(2)}) copy-start(bf16[48,64,128]{2,1,0:T(8,128)(2,1)} %get-tuple-element.28.handed) | copy-start | bytes 2359300
  45.7 15.0 %collective-permute-start.8 = (bf16[11,64,128]{2,1,0:T(8,128)(2,1)}, bf16[11,64,128]{2,1,0:T(8,128)(2,1)S(1)}, u32[]{:S(2)}, u32[]{:S(2)}) collective-permute-start(bf16[11,64,128]{2,1,0:T(8,128)(2,1)} %get-tuple-element.33), channel_id=1, source_target_pairs={{0,1},{1,0},{2,3},{3,2},{4,5},{5,4},{6,7},{7,6},{8,9},{9,8},{10,11... | collective-permute-start | bytes 540680 | tf_op jit(solution)/shard_map/ppermute | solution.py:397
  47.5 16.6 %collective-permute-start.9 = (bf16[11,64,128]{2,1,0:T(8,128)(2,1)}, bf16[11,64,128]{2,1,0:T(8,128)(2,1)S(1)}, u32[]{:S(2)}, u32[]{:S(2)}) collective-permute-start(bf16[11,64,128]{2,1,0:T(8,128)(2,1)} %get-tuple-element.34), channel_id=1, source_target_pairs={{0,2},{1,3},{2,0},{3,1},{4,6},{5,7},{6,4},{7,5},{8,10},{9,11},{10,... | collective-permute-start | bytes 540680 | tf_op jit(solution)/shard_map/ppermute | solution.py:397
  49.6 14.5 %collective-permute-start.10 = (bf16[11,64,128]{2,1,0:T(8,128)(2,1)}, bf16[11,64,128]{2,1,0:T(8,128)(2,1)S(1)}, u32[]{:S(2)}, u32[]{:S(2)}) collective-permute-start(bf16[11,64,128]{2,1,0:T(8,128)(2,1)} %get-tuple-element.35), channel_id=1, source_target_pairs={{0,3},{1,2},{2,1},{3,0},{4,7},{5,6},{6,5},{7,4},{8,11},{9,10},{10,... | collective-permute-start | bytes 540680 | tf_op jit(solution)/shard_map/ppermute | solution.py:397
  54.3 1.3 %copy-start.1 = (bf16[27,256,128]{2,1,0:T(8,128)(2,1)}, bf16[27,256,128]{2,1,0:T(8,128)(2,1)S(1)}, u32[]{:S(2)}) copy-start(bf16[27,256,128]{2,1,0:T(8,128)(2,1)S(1)} %get-tuple-element.31.later_ref) | copy-start | bytes 5308420
  55.5 0.9 copy-start.4
  56.4 9.0 %collective-permute-start.6 = (bf16[13,256,128]{2,1,0:T(8,128)(2,1)}, bf16[13,256,128]{2,1,0:T(8,128)(2,1)S(1)}, u32[]{:S(2)}, u32[]{:S(2)}) collective-permute-start(bf16[13,256,128]{2,1,0:T(8,128)(2,1)} %get-tuple-element.32), channel_id=1, source_target_pairs={{0,4},{4,0},{8,12},{12,8},{1,5},{5,1},{9,13},{13,9},{2,6},{6,2},{1... | collective-permute-start | bytes 2555912 | tf_op jit(solution)/shard_map/ppermute | solution.py:517
  58.3 14.3 %collective-permute-start.7 = (bf16[13,256,128]{2,1,0:T(8,128)(2,1)}, bf16[13,256,128]{2,1,0:T(8,128)(2,1)}, u32[]{:S(2)}, u32[]{:S(2)}) collective-permute-start(bf16[13,256,128]{2,1,0:T(8,128)(2,1)} %get-tuple-element.32), channel_id=1, source_target_pairs={{4,8},{8,4},{5,9},{9,5},{6,10},{10,6},{7,11},{11,7},{20,24},{24,20... | collective-permute-start | bytes 2555912 | tf_op jit(solution)/shard_map/ppermute | solution.py:516
  60.7 3.4 %copy-start.6 = (bf16[11,64,128]{2,1,0:T(8,128)(2,1)}, bf16[11,64,128]{2,1,0:T(8,128)(2,1)S(1)}, u32[]{:S(2)}) copy-start(bf16[11,64,128]{2,1,0:T(8,128)(2,1)S(1)} %collective-permute-done.8.refs_0_) | copy-start | bytes 540676
  60.7 12.0 %copy-start.5 = (f32[1,128,128]{2,1,0:T(8,128)S(1)}, f32[1,128,128]{2,1,0:T(8,128)}, u32[]{:S(2)}) copy-start(f32[1,128,128]{2,1,0:T(8,128)} %param.9) | copy-start | bytes 196612
  60.7 25.4 %collective-permute-start.5 = (bf16[48,64,128]{2,1,0:T(8,128)(2,1)}, bf16[48,64,128]{2,1,0:T(8,128)(2,1)}, u32[]{:S(2)}, u32[]{:S(2)}) collective-permute-start(bf16[48,64,128]{2,1,0:T(8,128)(2,1)} %copy-done.4), channel_id=1, source_target_pairs={{4,8},{8,4},{5,9},{9,5},{6,10},{10,6},{7,11},{11,7},{20,24},{24,20... | collective-permute-start | bytes 2359304 | tf_op jit(solution)/shard_map/ppermute | solution.py:518
  72.7 1.5 %copy-start.2 = (bf16[27,256,128]{2,1,0:T(8,128)(2,1)S(1)}, bf16[27,256,128]{2,1,0:T(8,128)(2,1)}, u32[]{:S(2)}) copy-start(bf16[27,256,128]{2,1,0:T(8,128)(2,1)} %copy-done.1) | copy-start | bytes 5308420
  74.1 0.9 copy-start.7
  75.1 0.9 copy-start.9
  76.0 0.9 copy-start.11
  77.6 8.4 %copy-start = (bf16[128,64,128]{2,1,0:T(8,128)(2,1)S(1)}, bf16[128,64,128]{2,1,0:T(8,128)(2,1)}, u32[]{:S(2)}) copy-start(bf16[128,64,128]{2,1,0:T(8,128)(2,1)} %get-tuple-element.20.xt_hbm.xt_ref.last_ref.next_ref) | copy-start | bytes 6291460
  77.6 8.5 %copy-start.12 = (bf16[128,128]{1,0:T(8,128)(2,1)S(1)}, bf16[128,128]{1,0:T(8,128)(2,1)}, u32[]{:S(2)}) copy-start(bf16[128,128]{1,0:T(8,128)(2,1)} %constant.2.clone.ring_ref) | copy-start | bytes 98308
  82.6 12.3 %all-to-all-start.1 = ((bf16[16,64,128]{2,1,0:T(8,128)(2,1)}), bf16[16,64,128]{2,1,0:T(8,128)(2,1)S(1)}, u32[]{:S(2)}, u32[]{:S(2)}) async-start(bf16[16,64,128]{2,1,0:T(8,128)(2,1)} %get-tuple-element.37), calls=%async_computation.1 | async-start | bytes 524288 | tf_op jit(solution)/shard_map/all_to_all | solution.py:549
  (6 other events, 4.4 us)

commit v28 on v26

--- a/solution.py
+++ b/solution.py
@@ -555,7 +555,7 @@
     steps = lines // span
     block = pl.BlockSpec((span, states, cols_z), lambda i: (i, 0, 0))
     (applied,) = call(
-        63.5,
+        48,
         functools.partial(stencil_kernel, share),
         (steps,),
         [

time: 86.6 us -> 86.7 us (level)
  waiting for transfers between devices: 20 us -> 21.7 us
  Pallas kernels: 36 us -> 34.5 us
  local copies, waits for them, and re-layouts: 1.87 us -> 0.84 us
    pallas_call x10, Pallas kernels: 36 us -> 34.5 us  [call(): pl.pallas_call(kernel, grid=grid, out_shape=shapes, in_specs=in_specs, ou...]
    all_to_all x1, waiting for transfers between devices: 0.01 us -> 1.5 us  [local(): lax.all_to_all(blocks, ('domain', 'band'), split_axis=0, concat_axis=0, t...]
    unnamed x14, local copies, waits for them, and re-layouts: 1.87 us -> 0.84 us
  transfers between devices with their start and end apart: 13 -> 13, of which waited for: 6 -> 7; matrix products, arithmetic and copies ran while one was open for 0% -> 0% of each run, Pallas kernels for 36% -> 35%
where the time goes in v28:
time: 86.7 us; the launch traced here: 85.3 us
  Pallas kernels  34.5 us (40%)
  starting transfers between devices  26.9 us (31%)
  waiting for transfers between devices  21.7 us (25%)
  between operations  1.44 us (2%)
    pallas_call x10, Pallas kernels, call(): pl.pallas_call(kernel, grid=grid, out_shape=shapes, in_specs=in_specs, ou...  34.5 us
    ppermute x1, waiting for transfers between devices, local(): lax.ppermute(value, 'domain', pairs)  9.32 us
    all_to_all x1, starting transfers between devices, local(): lax.all_to_all(message, 'band', split_axis=0, concat_axis=0, tiled=True)  6.04 us
    ppermute x1, starting transfers between devices, local(): later_link = lax.ppermute(later_pass, 'domain', link_pairs)  4.64 us
    ppermute x1, waiting for transfers between devices, local(): later_link = lax.ppermute(later_pass, 'domain', link_pairs)  4.05 us
    ppermute x3, starting transfers between devices, swapped(): lax.ppermute(values[k - 1], axis, [(i, i ^ k) for i in range(size)])  3.97 us
    all_to_all x1, starting transfers between devices, local(): lax.all_to_all(blocks, ('domain', 'band'), split_axis=0, concat_axis=0, t...  3.9 us
    ppermute x1, starting transfers between devices, local(): link_early = lax.ppermute(early_part, 'domain', link_pairs)  3.33 us
  transfers between devices with their start and end apart: 13, of which 7 were waited for; matrix products, arithmetic and copies ran while one was open for 0% of the time, Pallas kernels for 35%

profile of v28, /device:TPU:1, one launch (start us, length us, event | category | flops | bytes accessed | tf_op | source)
XLA Modules:
  0.0 85.3 jit_solution(14498705427641188348)
XLA Ops:
  0.6 4.0 %shard_map.95 = (bf16[128,64,128]{2,1,0:T(8,128)(2,1)}, bf16[80,64,128]{2,1,0:T(8,128)(2,1)}, bf16[48,64,128]{2,1,0:T(8,128)(2,1)}, bf16[108,64,128]{2,1,0:T(8,128)(2,1)}) custom-call(bf16[64,128,128]{2,1,0:T(8,128)(2,1)} %bitcast.12), custom_call_target="tpu_custom_call" | custom-call | flops 1100000 | bytes 1024 | tf_op jit(solution)/shard_map/pallas_call | solution.py:34
  4.7 6.0 %all-to-all-start = ((bf16[108,64,128]{2,1,0:T(8,128)(2,1)}), bf16[108,64,128]{2,1,0:T(8,128)(2,1)}, u32[]{:S(2)}, u32[]{:S(2)}) async-start(bf16[108,64,128]{2,1,0:T(8,128)(2,1)} %get-tuple-element.27), calls=%async_computation | async-start | bytes 3538944 | tf_op jit(solution)/shard_map/all_to_all | solution.py:426
  10.8 3.3 %collective-permute-start.1 = (bf16[80,64,128]{2,1,0:T(8,128)(2,1)}, bf16[80,64,128]{2,1,0:T(8,128)(2,1)}, u32[]{:S(2)}, u32[]{:S(2)}) collective-permute-start(bf16[80,64,128]{2,1,0:T(8,128)(2,1)} %get-tuple-element.26), channel_id=1, source_target_pairs={{4,8},{8,4},{5,9},{9,5},{6,10},{10,6},{7,11},{11,7},{20,24},{24,20... | collective-permute-start | bytes 3932168 | tf_op jit(solution)/shard_map/ppermute | solution.py:427
  14.8 8.0 %shard_map.96 = (bf16[24,64,128]{2,1,0:T(8,128)(2,1)}, bf16[16,64,128]{2,1,0:T(8,128)(2,1)}, bf16[16,64,128]{2,1,0:T(8,128)(2,1)}, bf16[8,64,128]{2,1,0:T(8,128)(2,1)}) custom-call(s32[384]{0:T(512)} %atom_ref.3, s32[384]{0:T(512)} %line_ref.3, s32[1]{0:T(128)S(6)} %copy.13.count_ref, ...), custom_call_target="tpu_custom_call" | custom-call | flops 1100000 | bytes 1024 | tf_op jit(solution)/shard_map/pallas_call | solution.py:34
  22.9 2.3 %collective-permute-start.3 = (bf16[16,64,128]{2,1,0:T(8,128)(2,1)}, bf16[16,64,128]{2,1,0:T(8,128)(2,1)S(1)}, u32[]{:S(2)}, u32[]{:S(2)}) collective-permute-start(bf16[16,64,128]{2,1,0:T(8,128)(2,1)} %get-tuple-element.30), channel_id=1, source_target_pairs={{4,8},{8,4},{5,9},{9,5},{6,10},{10,6},{7,11},{11,7},{20,24},{24,20... | collective-permute-start | bytes 786440 | tf_op jit(solution)/shard_map/ppermute | solution.py:450
  25.3 9.3 %collective-permute-done.4.refs_2_.refs_0_ = bf16[8,64,128]{2,1,0:T(8,128)(2,1)S(1)} collective-permute-done((bf16[8,64,128]{2,1,0:T(8,128)(2,1)}, bf16[8,64,128]{2,1,0:T(8,128)(2,1)S(1)}, u32[]{:S(2)}, u32[]{:S(2)}) %collective-permute-start.4) | collective-permute-done | bytes 131104 | tf_op jit(solution)/shard_map/ppermute | solution.py:451
  35.4 10.1 %shard_map.98 = (f32[128,64,128]{2,1,0:T(8,128)}, bf16[11,64,128]{2,1,0:T(8,128)(2,1)}, bf16[11,64,128]{2,1,0:T(8,128)(2,1)}, bf16[11,64,128]{2,1,0:T(8,128)(2,1)}, bf16[11,64,128]{2,1,0:T(8,128)(2,1)}) custom-call(s32[384]{0:T(512)} %atom_ref.3, s32[384]{0:T(512)} %line_ref.3, s32[1]{0:T(128)S(6)} %copy.13.count_ref, ...), custom_call_target="tpu_custom_call" | custom-call | flops 8800000000 | bytes 1024 | tf_op jit(solution)/shard_map/pallas_call | solution.py:34
  45.6 1.8 %collective-permute-start.6 = (bf16[11,64,128]{2,1,0:T(8,128)(2,1)}, bf16[11,64,128]{2,1,0:T(8,128)(2,1)S(1)}, u32[]{:S(2)}, u32[]{:S(2)}) collective-permute-start(bf16[11,64,128]{2,1,0:T(8,128)(2,1)} %get-tuple-element.37), channel_id=1, source_target_pairs={{0,1},{1,0},{2,3},{3,2},{4,5},{5,4},{6,7},{7,6},{8,9},{9,8},{10,11... | collective-permute-start | bytes 540680 | tf_op jit(solution)/shard_map/ppermute | solution.py:392
  47.4 2.1 %collective-permute-start.7 = (bf16[11,64,128]{2,1,0:T(8,128)(2,1)}, bf16[11,64,128]{2,1,0:T(8,128)(2,1)S(1)}, u32[]{:S(2)}, u32[]{:S(2)}) collective-permute-start(bf16[11,64,128]{2,1,0:T(8,128)(2,1)} %get-tuple-element.38), channel_id=1, source_target_pairs={{0,2},{1,3},{2,0},{3,1},{4,6},{5,7},{6,4},{7,5},{8,10},{9,11},{10,... | collective-permute-start | bytes 540680 | tf_op jit(solution)/shard_map/ppermute | solution.py:392
  49.6 2.4 %all-to-all-done.landed = bf16[108,64,128]{2,1,0:T(8,128)(2,1)} async-done(((bf16[108,64,128]{2,1,0:T(8,128)(2,1)}), bf16[108,64,128]{2,1,0:T(8,128)(2,1)}, u32[]{:S(2)}, u32[]{:S(2)}) %all-to-all-start) | async-done | bytes 1769504 | tf_op jit(solution)/shard_map/all_to_all | solution.py:426
  51.9 1.6 %shard_map.99 = (bf16[27,256,128]{2,1,0:T(8,128)(2,1)S(1)}, bf16[13,256,128]{2,1,0:T(8,128)(2,1)S(1)}, bf16[48,64,128]{2,1,0:T(8,128)(2,1)}) custom-call(bf16[108,64,128]{2,1,0:T(8,128)(2,1)} %all-to-all-done.landed, bf16[11,64,128]{2,1,0:T(8,128)(2,1)} %get-tuple-element.32.unread.refs_0_, ...), custom_call_target="tpu_custom_call", output_to_operand_aliasing={{2}: (2, {})} | custom-call | flops 1100000 | bytes 1024 | tf_op jit(solution)/shard_map/pallas_call | solution.py:34
  53.5 4.6 %collective-permute-start.10 = (bf16[13,256,128]{2,1,0:T(8,128)(2,1)S(1)}, bf16[13,256,128]{2,1,0:T(8,128)(2,1)S(1)}, u32[]{:S(2)}, u32[]{:S(2)}) collective-permute-start(bf16[13,256,128]{2,1,0:T(8,128)(2,1)S(1)} %get-tuple-element.42), channel_id=1, source_target_pairs={{4,8},{8,4},{5,9},{9,5},{6,10},{10,6},{7,11},{11,7},{20,24},{24,20... | collective-permute-start | bytes 2555912 | tf_op jit(solution)/shard_map/ppermute | solution.py:511
  58.2 2.1 %collective-permute-done.6.refs_1_ = bf16[11,64,128]{2,1,0:T(8,128)(2,1)S(1)} collective-permute-done((bf16[11,64,128]{2,1,0:T(8,128)(2,1)}, bf16[11,64,128]{2,1,0:T(8,128)(2,1)S(1)}, u32[]{:S(2)}, u32[]{:S(2)}) %collective-permute-start.6) | collective-permute-done | bytes 180256 | tf_op jit(solution)/shard_map/ppermute | solution.py:392
  60.3 2.4 %collective-permute-start.5 = (bf16[48,64,128]{2,1,0:T(8,128)(2,1)}, bf16[48,64,128]{2,1,0:T(8,128)(2,1)S(1)}, u32[]{:S(2)}, u32[]{:S(2)}) collective-permute-start(bf16[48,64,128]{2,1,0:T(8,128)(2,1)} %get-tuple-element.34), channel_id=1, source_target_pairs={{4,8},{8,4},{5,9},{9,5},{6,10},{10,6},{7,11},{11,7},{20,24},{24,20... | collective-permute-start | bytes 2359304 | tf_op jit(solution)/shard_map/ppermute | solution.py:513
  62.7 0.7 collective-permute-done.7.refs_2_
  63.4 1.1 %shard_map.100 = (bf16[7,256,128]{2,1,0:T(8,128)(2,1)S(1)}, bf16[3,256,128]{2,1,0:T(8,128)(2,1)S(1)}, bf16[2,256,128]{2,1,0:T(8,128)(2,1)S(1)}, f32[32,128]{1,0:T(8,128)S(1)}, f32[8,128]{1,0:T(8,128)}) custom-call(bf16[27,256,128]{2,1,0:T(8,128)(2,1)S(1)} %get-tuple-element.36.after_ref.all_ref, f32[16,256]{1,0:T(8,128)S(1)} %bitcast.10, ...), custom_call_target="tpu_custom_call" | custom-call | flops 32999999488 | bytes 1024 | tf_op jit(solution)/shard_map/pallas_call | solution.py:34
  64.5 4.0 %collective-permute-done.10.link_ref = bf16[13,256,128]{2,1,0:T(8,128)(2,1)S(1)} collective-permute-done((bf16[13,256,128]{2,1,0:T(8,128)(2,1)S(1)}, bf16[13,256,128]{2,1,0:T(8,128)(2,1)S(1)}, u32[]{:S(2)}, u32[]{:S(2)}) %collective-permute-start.10) | collective-permute-done | bytes 852000 | tf_op jit(solution)/shard_map/ppermute | solution.py:511
  68.5 1.3 %shard_map.101.begun_ref = f32[2,256,256]{2,1,0:T(8,128)S(1)} custom-call(bf16[27,256,128]{2,1,0:T(8,128)(2,1)S(1)} %get-tuple-element.36.after_ref.all_ref, bf16[13,256,128]{2,1,0:T(8,128)(2,1)S(1)} %collective-permute-done.9.core_ref, bf16[13,256,128]{2,1,0:T(8,128)(2,1)S(1)} %collective-permute-done.10.link_ref, f32[128,128]{1,0:T(8,128)S(1)} %bitcast.6, ...), custom_call_target="tpu_custom_call" | custom-call | flops 1100000 | bytes 1024 | tf_op jit(solution)/shard_map/pallas_call | solution.py:34
  69.8 1.5 %shard_map.102 = (bf16[16,64,128]{2,1,0:T(8,128)(2,1)}, f32[8,128]{1,0:T(8,128)}) custom-call(bf16[7,256,128]{2,1,0:T(8,128)(2,1)S(1)} %get-tuple-element.40.all_ref, bf16[3,256,128]{2,1,0:T(8,128)(2,1)S(1)} %get-tuple-element.41.beside_ref, f32[128,128]{1,0:T(8,128)S(1)} %bitcast.7, f32[2,256,256]{2,1,0:T(8,128)S(1)} %shard_map.101.begun_ref, ...), custom_call_target="tpu_custom_call" | custom-call | flops 1100000 | bytes 1024 | tf_op jit(solution)/shard_map/pallas_call | solution.py:34
  71.4 3.9 %all-to-all-start.1 = ((bf16[16,64,128]{2,1,0:T(8,128)(2,1)}), bf16[16,64,128]{2,1,0:T(8,128)(2,1)S(1)}, u32[]{:S(2)}, u32[]{:S(2)}) async-start(bf16[16,64,128]{2,1,0:T(8,128)(2,1)} %get-tuple-element.47), calls=%async_computation.1 | async-start | bytes 524288 | tf_op jit(solution)/shard_map/all_to_all | solution.py:553
  75.3 1.7 %collective-permute-done.5.late_ref = bf16[48,64,128]{2,1,0:T(8,128)(2,1)S(1)} collective-permute-done((bf16[48,64,128]{2,1,0:T(8,128)(2,1)}, bf16[48,64,128]{2,1,0:T(8,128)(2,1)S(1)}, u32[]{:S(2)}, u32[]{:S(2)}) %collective-permute-start.5) | collective-permute-done | bytes 786464 | tf_op jit(solution)/shard_map/ppermute | solution.py:513
  77.0 6.1 %shard_map.103 = bf16[64,128,128]{2,1,0:T(8,128)(2,1)} custom-call(bf16[128,64,128]{2,1,0:T(8,128)(2,1)S(1)} %copy-done, bf16[128,64,128]{2,1,0:T(8,128)(2,1)S(1)} %copy-done, bf16[128,64,128]{2,1,0:T(8,128)(2,1)S(1)} %copy-done, bf16[128,64,128]{2,1,0:T(8,128)(2,1)} %collective-permute-done.refs_4_.beside_hbm.core_ref, ...), custom_call_target="tpu_custom_call" | custom-call | flops 1100000 | bytes 1024 | tf_op jit(solution)/shard_map/pallas_call | solution.py:34
  83.1 1.5 %all-to-all-done.1.parts_ref = bf16[16,64,128]{2,1,0:T(8,128)(2,1)S(1)} async-done(((bf16[16,64,128]{2,1,0:T(8,128)(2,1)}), bf16[16,64,128]{2,1,0:T(8,128)(2,1)S(1)}, u32[]{:S(2)}, u32[]{:S(2)}) %all-to-all-start.1) | async-done | bytes 262176 | tf_op jit(solution)/shard_map/all_to_all | solution.py:553
  84.6 0.7 shard_map.104
  (26 shorter events, 1.3 us)
Async XLA Ops:
  4.6 30.0 %collective-permute-start = (bf16[128,64,128]{2,1,0:T(8,128)(2,1)}, bf16[128,64,128]{2,1,0:T(8,128)(2,1)}, u32[]{:S(2)}, u32[]{:S(2)}) collective-permute-start(bf16[128,64,128]{2,1,0:T(8,128)(2,1)} %get-tuple-element.25.xt_hbm.xt_ref.last_ref.next_ref), channel_id=1, source_target_pairs={{0,4},{4,0},{8,12},{12,8},{1,5},{5,1},{9,13},{13,9},{2,6},{6,2},{1... | collective-permute-start | bytes 6291464 | tf_op jit(solution)/shard_map/ppermute | solution.py:428
  4.7 47.2 %all-to-all-start = ((bf16[108,64,128]{2,1,0:T(8,128)(2,1)}), bf16[108,64,128]{2,1,0:T(8,128)(2,1)}, u32[]{:S(2)}, u32[]{:S(2)}) async-start(bf16[108,64,128]{2,1,0:T(8,128)(2,1)} %get-tuple-element.27), calls=%async_computation | async-start | bytes 3538944 | tf_op jit(solution)/shard_map/all_to_all | solution.py:426
  10.8 23.8 %collective-permute-start.1 = (bf16[80,64,128]{2,1,0:T(8,128)(2,1)}, bf16[80,64,128]{2,1,0:T(8,128)(2,1)}, u32[]{:S(2)}, u32[]{:S(2)}) collective-permute-start(bf16[80,64,128]{2,1,0:T(8,128)(2,1)} %get-tuple-element.26), channel_id=1, source_target_pairs={{4,8},{8,4},{5,9},{9,5},{6,10},{10,6},{7,11},{11,7},{20,24},{24,20... | collective-permute-start | bytes 3932168 | tf_op jit(solution)/shard_map/ppermute | solution.py:427
  22.8 11.8 %collective-permute-start.2 = (bf16[16,64,128]{2,1,0:T(8,128)(2,1)}, bf16[16,64,128]{2,1,0:T(8,128)(2,1)S(1)}, u32[]{:S(2)}, u32[]{:S(2)}) collective-permute-start(bf16[16,64,128]{2,1,0:T(8,128)(2,1)} %get-tuple-element.29), channel_id=1, source_target_pairs={{0,4},{4,0},{8,12},{12,8},{1,5},{5,1},{9,13},{13,9},{2,6},{6,2},{1... | collective-permute-start | bytes 786440 | tf_op jit(solution)/shard_map/ppermute | solution.py:452
  22.9 11.7 %collective-permute-start.3 = (bf16[16,64,128]{2,1,0:T(8,128)(2,1)}, bf16[16,64,128]{2,1,0:T(8,128)(2,1)S(1)}, u32[]{:S(2)}, u32[]{:S(2)}) collective-permute-start(bf16[16,64,128]{2,1,0:T(8,128)(2,1)} %get-tuple-element.30), channel_id=1, source_target_pairs={{4,8},{8,4},{5,9},{9,5},{6,10},{10,6},{7,11},{11,7},{20,24},{24,20... | collective-permute-start | bytes 786440 | tf_op jit(solution)/shard_map/ppermute | solution.py:450
  25.2 9.4 %collective-permute-start.4 = (bf16[8,64,128]{2,1,0:T(8,128)(2,1)}, bf16[8,64,128]{2,1,0:T(8,128)(2,1)S(1)}, u32[]{:S(2)}, u32[]{:S(2)}) collective-permute-start(bf16[8,64,128]{2,1,0:T(8,128)(2,1)} %get-tuple-element.31), channel_id=1, source_target_pairs={{0,8},{4,12},{8,0},{12,4},{1,9},{5,13},{9,1},{13,5},{2,10},{6,14},... | collective-permute-start | bytes 393224 | tf_op jit(solution)/shard_map/ppermute | solution.py:451
  34.6 0.6 copy-start.6
  34.6 0.8 copy-start.4
  34.6 0.9 copy-start.5
  45.6 17.8 %copy-start.3 = (f32[256,16]{0,1:T(8,128)S(1)}, f32[256,16]{0,1:T(8,128)}, u32[]{:S(2)}) copy-start(f32[256,16]{0,1:T(8,128)} %param.14) | copy-start | bytes 49156
  45.6 14.8 %collective-permute-start.6 = (bf16[11,64,128]{2,1,0:T(8,128)(2,1)}, bf16[11,64,128]{2,1,0:T(8,128)(2,1)S(1)}, u32[]{:S(2)}, u32[]{:S(2)}) collective-permute-start(bf16[11,64,128]{2,1,0:T(8,128)(2,1)} %get-tuple-element.37), channel_id=1, source_target_pairs={{0,1},{1,0},{2,3},{3,2},{4,5},{5,4},{6,7},{7,6},{8,9},{9,8},{10,11... | collective-permute-start | bytes 540680 | tf_op jit(solution)/shard_map/ppermute | solution.py:392
  47.4 16.0 %collective-permute-start.7 = (bf16[11,64,128]{2,1,0:T(8,128)(2,1)}, bf16[11,64,128]{2,1,0:T(8,128)(2,1)S(1)}, u32[]{:S(2)}, u32[]{:S(2)}) collective-permute-start(bf16[11,64,128]{2,1,0:T(8,128)(2,1)} %get-tuple-element.38), channel_id=1, source_target_pairs={{0,2},{1,3},{2,0},{3,1},{4,6},{5,7},{6,4},{7,5},{8,10},{9,11},{10,... | collective-permute-start | bytes 540680 | tf_op jit(solution)/shard_map/ppermute | solution.py:392
  49.5 13.9 %collective-permute-start.8 = (bf16[11,64,128]{2,1,0:T(8,128)(2,1)}, bf16[11,64,128]{2,1,0:T(8,128)(2,1)S(1)}, u32[]{:S(2)}, u32[]{:S(2)}) collective-permute-start(bf16[11,64,128]{2,1,0:T(8,128)(2,1)} %get-tuple-element.39), channel_id=1, source_target_pairs={{0,3},{1,2},{2,1},{3,0},{4,7},{5,6},{6,5},{7,4},{8,11},{9,10},{10,... | collective-permute-start | bytes 540680 | tf_op jit(solution)/shard_map/ppermute | solution.py:392
  53.5 15.0 %collective-permute-start.10 = (bf16[13,256,128]{2,1,0:T(8,128)(2,1)S(1)}, bf16[13,256,128]{2,1,0:T(8,128)(2,1)S(1)}, u32[]{:S(2)}, u32[]{:S(2)}) collective-permute-start(bf16[13,256,128]{2,1,0:T(8,128)(2,1)S(1)} %get-tuple-element.42), channel_id=1, source_target_pairs={{4,8},{8,4},{5,9},{9,5},{6,10},{10,6},{7,11},{11,7},{20,24},{24,20... | collective-permute-start | bytes 2555912 | tf_op jit(solution)/shard_map/ppermute | solution.py:511
  58.2 10.4 %collective-permute-start.9 = (bf16[13,256,128]{2,1,0:T(8,128)(2,1)S(1)}, bf16[13,256,128]{2,1,0:T(8,128)(2,1)S(1)}, u32[]{:S(2)}, u32[]{:S(2)}) collective-permute-start(bf16[13,256,128]{2,1,0:T(8,128)(2,1)S(1)} %get-tuple-element.42), channel_id=1, source_target_pairs={{0,4},{4,0},{8,12},{12,8},{1,5},{5,1},{9,13},{13,9},{2,6},{6,2},{1... | collective-permute-start | bytes 2555912 | tf_op jit(solution)/shard_map/ppermute | solution.py:512
  60.3 16.6 %collective-permute-start.5 = (bf16[48,64,128]{2,1,0:T(8,128)(2,1)}, bf16[48,64,128]{2,1,0:T(8,128)(2,1)S(1)}, u32[]{:S(2)}, u32[]{:S(2)}) collective-permute-start(bf16[48,64,128]{2,1,0:T(8,128)(2,1)} %get-tuple-element.34), channel_id=1, source_target_pairs={{4,8},{8,4},{5,9},{9,5},{6,10},{10,6},{7,11},{11,7},{20,24},{24,20... | collective-permute-start | bytes 2359304 | tf_op jit(solution)/shard_map/ppermute | solution.py:513
  63.4 5.1 %copy-start.1 = (f32[1,128,128]{2,1,0:T(8,128)S(1)}, f32[1,128,128]{2,1,0:T(8,128)}, u32[]{:S(2)}) copy-start(f32[1,128,128]{2,1,0:T(8,128)} %param.9) | copy-start | bytes 196612
  68.5 8.4 %copy-start = (bf16[128,64,128]{2,1,0:T(8,128)(2,1)S(1)}, bf16[128,64,128]{2,1,0:T(8,128)(2,1)}, u32[]{:S(2)}) copy-start(bf16[128,64,128]{2,1,0:T(8,128)(2,1)} %get-tuple-element.25.xt_hbm.xt_ref.last_ref.next_ref) | copy-start | bytes 6291460
  69.8 7.2 %copy-start.2 = (bf16[128,128]{1,0:T(8,128)(2,1)S(1)}, bf16[128,128]{1,0:T(8,128)(2,1)}, u32[]{:S(2)}) copy-start(bf16[128,128]{1,0:T(8,128)(2,1)} %constant.2.clone.ring_ref) | copy-start | bytes 98308
  71.4 13.2 %all-to-all-start.1 = ((bf16[16,64,128]{2,1,0:T(8,128)(2,1)}), bf16[16,64,128]{2,1,0:T(8,128)(2,1)S(1)}, u32[]{:S(2)}, u32[]{:S(2)}) async-start(bf16[16,64,128]{2,1,0:T(8,128)(2,1)} %get-tuple-element.47), calls=%async_computation.1 | async-start | bytes 524288 | tf_op jit(solution)/shard_map/all_to_all | solution.py:553

commit v29 on v27

--- a/solution.py
+++ b/solution.py
@@ -518,7 +518,7 @@
     link_late = lax.ppermute(late_part, "domain", link_pairs)
 
     (early_token,) = call(
-        62.2,
+        1,
         wait_for,
         (),
         [UNREAD] * (bands - 1),

time: 97.3 us -> 88.5 us (0.910)
  local copies, waits for them, and re-layouts: 9.25 us -> 2.46 us
  Pallas kernels: 36.6 us -> 34.2 us
  waiting for transfers between devices: 21.4 us -> 22.7 us
    unnamed x34 -> x18, local copies, waits for them, and re-layouts: 9.25 us -> 2.46 us
    ppermute x3, waiting for transfers between devices: 0.01 us -> 2.67 us  [swapped(): lax.ppermute(values[k - 1], axis, [(i, i ^ k) for i in range(size)])]
    pallas_call x9, Pallas kernels: 36.6 us -> 34.2 us  [call(): pl.pallas_call(kernel, grid=grid, out_shape=shapes, in_specs=in_specs, ou...]
    ppermute x1, waiting for transfers between devices: 7.23 us -> 5.85 us  [local(): later_link = lax.ppermute(later_pass, 'domain', link_pairs)]
  transfers between devices with their start and end apart: 13 -> 13, of which waited for: 4 -> 7; matrix products, arithmetic and copies ran while one was open for 0% -> 0% of each run, Pallas kernels for 33% -> 34%
where the time goes in v29:
time: 88.5 us; the launch traced here: 87.2 us
  Pallas kernels  34.2 us (39%)
  starting transfers between devices  26.4 us (30%)
  waiting for transfers between devices  22.7 us (26%)
  local copies, waits for them, and re-layouts  2.46 us (3%)
  between operations  1.42 us (2%)
    pallas_call x9, Pallas kernels, call(): pl.pallas_call(kernel, grid=grid, out_shape=shapes, in_specs=in_specs, ou...  34.2 us
    ppermute x1, waiting for transfers between devices, local(): lax.ppermute(value, 'domain', pairs)  9.5 us
    all_to_all x1, starting transfers between devices, local(): lax.all_to_all(message, 'band', split_axis=0, concat_axis=0, tiled=True)  6.04 us
    ppermute x1, waiting for transfers between devices, local(): later_link = lax.ppermute(later_pass, 'domain', link_pairs)  5.85 us
    ppermute x3, starting transfers between devices, swapped(): lax.ppermute(values[k - 1], axis, [(i, i ^ k) for i in range(size)])  3.97 us
    all_to_all x1, starting transfers between devices, local(): lax.all_to_all(blocks, ('domain', 'band'), split_axis=0, concat_axis=0, t...  3.44 us
    ppermute x1, starting transfers between devices, local(): link_early = lax.ppermute(early_part, 'domain', link_pairs)  3.33 us
    ppermute x1, starting transfers between devices, local(): link_late = lax.ppermute(late_part, 'domain', link_pairs)  2.67 us
  transfers between devices with their start and end apart: 13, of which 7 were waited for; matrix products, arithmetic and copies ran while one was open for 0% of the time, Pallas kernels for 34%

profile of v29, /device:TPU:1, one launch (start us, length us, event | category | flops | bytes accessed | tf_op | source)
XLA Modules:
  0.0 87.2 jit_solution(15383614010447169786)
XLA Ops:
  0.6 4.0 %shard_map.95 = (bf16[128,64,128]{2,1,0:T(8,128)(2,1)}, bf16[80,64,128]{2,1,0:T(8,128)(2,1)}, bf16[48,64,128]{2,1,0:T(8,128)(2,1)}, bf16[108,64,128]{2,1,0:T(8,128)(2,1)}) custom-call(bf16[64,128,128]{2,1,0:T(8,128)(2,1)} %bitcast.11), custom_call_target="tpu_custom_call" | custom-call | flops 1100000 | bytes 1024 | tf_op jit(solution)/shard_map/pallas_call | solution.py:34
  4.7 6.0 %all-to-all-start = ((bf16[108,64,128]{2,1,0:T(8,128)(2,1)}), bf16[108,64,128]{2,1,0:T(8,128)(2,1)}, u32[]{:S(2)}, u32[]{:S(2)}) async-start(bf16[108,64,128]{2,1,0:T(8,128)(2,1)} %get-tuple-element.22), calls=%async_computation | async-start | bytes 3538944 | tf_op jit(solution)/shard_map/all_to_all | solution.py:431
  10.8 3.3 %collective-permute-start.1 = (bf16[80,64,128]{2,1,0:T(8,128)(2,1)}, bf16[80,64,128]{2,1,0:T(8,128)(2,1)}, u32[]{:S(2)}, u32[]{:S(2)}) collective-permute-start(bf16[80,64,128]{2,1,0:T(8,128)(2,1)} %get-tuple-element.21), channel_id=1, source_target_pairs={{4,8},{8,4},{5,9},{9,5},{6,10},{10,6},{7,11},{11,7},{20,24},{24,20... | collective-permute-start | bytes 3932168 | tf_op jit(solution)/shard_map/ppermute | solution.py:432
  14.8 8.0 %shard_map.96 = (bf16[24,64,128]{2,1,0:T(8,128)(2,1)}, bf16[16,64,128]{2,1,0:T(8,128)(2,1)}, bf16[16,64,128]{2,1,0:T(8,128)(2,1)}, bf16[8,64,128]{2,1,0:T(8,128)(2,1)}) custom-call(s32[384]{0:T(512)} %atom_ref.3, s32[384]{0:T(512)} %line_ref.3, s32[1]{0:T(128)S(6)} %copy.13.count_ref, ...), custom_call_target="tpu_custom_call" | custom-call | flops 1100000 | bytes 1024 | tf_op jit(solution)/shard_map/pallas_call | solution.py:34
  22.8 2.1 %collective-permute-start.3 = (bf16[16,64,128]{2,1,0:T(8,128)(2,1)}, bf16[16,64,128]{2,1,0:T(8,128)(2,1)S(1)}, u32[]{:S(2)}, u32[]{:S(2)}) collective-permute-start(bf16[16,64,128]{2,1,0:T(8,128)(2,1)} %get-tuple-element.25), channel_id=1, source_target_pairs={{4,8},{8,4},{5,9},{9,5},{6,10},{10,6},{7,11},{11,7},{20,24},{24,20... | collective-permute-start | bytes 786440 | tf_op jit(solution)/shard_map/ppermute | solution.py:455
  25.1 9.5 %collective-permute-done.4.refs_2_.refs_0_ = bf16[8,64,128]{2,1,0:T(8,128)(2,1)S(1)} collective-permute-done((bf16[8,64,128]{2,1,0:T(8,128)(2,1)}, bf16[8,64,128]{2,1,0:T(8,128)(2,1)S(1)}, u32[]{:S(2)}, u32[]{:S(2)}) %collective-permute-start.4) | collective-permute-done | bytes 131104 | tf_op jit(solution)/shard_map/ppermute | solution.py:456
  34.6 0.6 copy-done.8
  35.4 10.1 %shard_map.98 = (f32[128,64,128]{2,1,0:T(8,128)}, bf16[11,64,128]{2,1,0:T(8,128)(2,1)}, bf16[11,64,128]{2,1,0:T(8,128)(2,1)}, bf16[11,64,128]{2,1,0:T(8,128)(2,1)}, bf16[11,64,128]{2,1,0:T(8,128)(2,1)}) custom-call(s32[384]{0:T(512)} %atom_ref.3, s32[384]{0:T(512)} %line_ref.3, s32[1]{0:T(128)S(6)} %copy.13.count_ref, ...), custom_call_target="tpu_custom_call" | custom-call | flops 8800000000 | bytes 1024 | tf_op jit(solution)/shard_map/pallas_call | solution.py:34
  45.6 1.8 %collective-permute-start.8 = (bf16[11,64,128]{2,1,0:T(8,128)(2,1)}, bf16[11,64,128]{2,1,0:T(8,128)(2,1)S(1)}, u32[]{:S(2)}, u32[]{:S(2)}) collective-permute-start(bf16[11,64,128]{2,1,0:T(8,128)(2,1)} %get-tuple-element.33), channel_id=1, source_target_pairs={{0,1},{1,0},{2,3},{3,2},{4,5},{5,4},{6,7},{7,6},{8,9},{9,8},{10,11... | collective-permute-start | bytes 540680 | tf_op jit(solution)/shard_map/ppermute | solution.py:397
  47.4 2.1 %collective-permute-start.9 = (bf16[11,64,128]{2,1,0:T(8,128)(2,1)}, bf16[11,64,128]{2,1,0:T(8,128)(2,1)S(1)}, u32[]{:S(2)}, u32[]{:S(2)}) collective-permute-start(bf16[11,64,128]{2,1,0:T(8,128)(2,1)} %get-tuple-element.34), channel_id=1, source_target_pairs={{0,2},{1,3},{2,0},{3,1},{4,6},{5,7},{6,4},{7,5},{8,10},{9,11},{10,... | collective-permute-start | bytes 540680 | tf_op jit(solution)/shard_map/ppermute | solution.py:397
  49.5 2.4 %all-to-all-done.landed = bf16[108,64,128]{2,1,0:T(8,128)(2,1)} async-done(((bf16[108,64,128]{2,1,0:T(8,128)(2,1)}), bf16[108,64,128]{2,1,0:T(8,128)(2,1)}, u32[]{:S(2)}, u32[]{:S(2)}) %all-to-all-start) | async-done | bytes 1769504 | tf_op jit(solution)/shard_map/all_to_all | solution.py:431
  51.9 1.6 %shard_map.99 = (bf16[27,256,128]{2,1,0:T(8,128)(2,1)S(1)}, bf16[13,256,128]{2,1,0:T(8,128)(2,1)S(1)}, bf16[48,64,128]{2,1,0:T(8,128)(2,1)}) custom-call(bf16[108,64,128]{2,1,0:T(8,128)(2,1)} %all-to-all-done.landed, bf16[11,64,128]{2,1,0:T(8,128)(2,1)} %get-tuple-element.27.unread.own_hbm, ...), custom_call_target="tpu_custom_call", output_to_operand_aliasing={{2}: (2, {})} | custom-call | flops 1100000 | bytes 1024 | tf_op jit(solution)/shard_map/pallas_call | solution.py:34
  53.5 2.4 %collective-permute-start.6 = (bf16[13,256,128]{2,1,0:T(8,128)(2,1)S(1)}, bf16[13,256,128]{2,1,0:T(8,128)(2,1)S(1)}, u32[]{:S(2)}, u32[]{:S(2)}) collective-permute-start(bf16[13,256,128]{2,1,0:T(8,128)(2,1)S(1)} %get-tuple-element.32), channel_id=1, source_target_pairs={{0,4},{4,0},{8,12},{12,8},{1,5},{5,1},{9,13},{13,9},{2,6},{6,2},{1... | collective-permute-start | bytes 2555912 | tf_op jit(solution)/shard_map/ppermute | solution.py:517
  55.9 2.1 %collective-permute-start.7 = (bf16[13,256,128]{2,1,0:T(8,128)(2,1)S(1)}, bf16[13,256,128]{2,1,0:T(8,128)(2,1)S(1)}, u32[]{:S(2)}, u32[]{:S(2)}) collective-permute-start(bf16[13,256,128]{2,1,0:T(8,128)(2,1)S(1)} %get-tuple-element.32), channel_id=1, source_target_pairs={{4,8},{8,4},{5,9},{9,5},{6,10},{10,6},{7,11},{11,7},{20,24},{24,20... | collective-permute-start | bytes 2555912 | tf_op jit(solution)/shard_map/ppermute | solution.py:516
  58.0 2.3 %collective-permute-done.8.refs_0_ = bf16[11,64,128]{2,1,0:T(8,128)(2,1)S(1)} collective-permute-done((bf16[11,64,128]{2,1,0:T(8,128)(2,1)}, bf16[11,64,128]{2,1,0:T(8,128)(2,1)S(1)}, u32[]{:S(2)}, u32[]{:S(2)}) %collective-permute-start.8) | collective-permute-done | bytes 180256 | tf_op jit(solution)/shard_map/ppermute | solution.py:397
  60.4 2.7 %collective-permute-start.5 = (bf16[48,64,128]{2,1,0:T(8,128)(2,1)}, bf16[48,64,128]{2,1,0:T(8,128)(2,1)S(1)}, u32[]{:S(2)}, u32[]{:S(2)}) collective-permute-start(bf16[48,64,128]{2,1,0:T(8,128)(2,1)} %get-tuple-element.29), channel_id=1, source_target_pairs={{4,8},{8,4},{5,9},{9,5},{6,10},{10,6},{7,11},{11,7},{20,24},{24,20... | collective-permute-start | bytes 2359304 | tf_op jit(solution)/shard_map/ppermute | solution.py:518
  63.4 0.7 copy-done.2
  64.1 5.9 %collective-permute-done.7.link_ref = bf16[13,256,128]{2,1,0:T(8,128)(2,1)S(1)} collective-permute-done((bf16[13,256,128]{2,1,0:T(8,128)(2,1)S(1)}, bf16[13,256,128]{2,1,0:T(8,128)(2,1)S(1)}, u32[]{:S(2)}, u32[]{:S(2)}) %collective-permute-start.7) | collective-permute-done | bytes 852000 | tf_op jit(solution)/shard_map/ppermute | solution.py:516
  70.0 0.9 %copy-done.3 = bf16[11,64,128]{2,1,0:T(8,128)(2,1)S(1)} copy-done((bf16[11,64,128]{2,1,0:T(8,128)(2,1)S(1)}, bf16[11,64,128]{2,1,0:T(8,128)(2,1)}, u32[]{:S(2)}) %copy-start.3) | copy-done | bytes 180248
  70.9 3.6 %shard_map.101 = (bf16[16,64,128]{2,1,0:T(8,128)(2,1)}, f32[8,128]{1,0:T(8,128)}) custom-call(bf16[27,256,128]{2,1,0:T(8,128)(2,1)S(1)} %get-tuple-element.31.later_ref, bf16[13,256,128]{2,1,0:T(8,128)(2,1)S(1)} %collective-permute-done.6.core_ref, bf16[13,256,128]{2,1,0:T(8,128)(2,1)S(1)} %collective-permute-done.7.link_ref, f32[128,128]{1,0:T(8,128)S(1)} %bitcast.6, ...), custom_call_target="tpu_custom_call" | custom-call | flops 1100000 | bytes 1024 | tf_op jit(solution)/shard_map/pallas_call | solution.py:34
  74.5 3.4 %all-to-all-start.1 = ((bf16[16,64,128]{2,1,0:T(8,128)(2,1)}), bf16[16,64,128]{2,1,0:T(8,128)(2,1)S(1)}, u32[]{:S(2)}, u32[]{:S(2)}) async-start(bf16[16,64,128]{2,1,0:T(8,128)(2,1)} %get-tuple-element.37), calls=%async_computation.1 | async-start | bytes 524288 | tf_op jit(solution)/shard_map/all_to_all | solution.py:549
  78.4 6.1 %shard_map.102 = bf16[64,128,128]{2,1,0:T(8,128)(2,1)} custom-call(bf16[128,64,128]{2,1,0:T(8,128)(2,1)S(1)} %copy-done, bf16[128,64,128]{2,1,0:T(8,128)(2,1)S(1)} %copy-done, bf16[128,64,128]{2,1,0:T(8,128)(2,1)S(1)} %copy-done, bf16[128,64,128]{2,1,0:T(8,128)(2,1)} %collective-permute-done.refs_4_.beside_hbm.core_ref, ...), custom_call_target="tpu_custom_call" | custom-call | flops 1100000 | bytes 1024 | tf_op jit(solution)/shard_map/pallas_call | solution.py:34
  84.5 1.9 %all-to-all-done.1.parts_ref = bf16[16,64,128]{2,1,0:T(8,128)(2,1)S(1)} async-done(((bf16[16,64,128]{2,1,0:T(8,128)(2,1)}), bf16[16,64,128]{2,1,0:T(8,128)(2,1)S(1)}, u32[]{:S(2)}, u32[]{:S(2)}) %all-to-all-start.1) | async-done | bytes 262176 | tf_op jit(solution)/shard_map/all_to_all | solution.py:549
  86.4 0.7 shard_map.103
  (29 shorter events, 1.4 us)
Async XLA Ops:
  4.6 30.0 %collective-permute-start = (bf16[128,64,128]{2,1,0:T(8,128)(2,1)}, bf16[128,64,128]{2,1,0:T(8,128)(2,1)}, u32[]{:S(2)}, u32[]{:S(2)}) collective-permute-start(bf16[128,64,128]{2,1,0:T(8,128)(2,1)} %get-tuple-element.20.xt_hbm.xt_ref.last_ref.next_ref), channel_id=1, source_target_pairs={{0,4},{4,0},{8,12},{12,8},{1,5},{5,1},{9,13},{13,9},{2,6},{6,2},{1... | collective-permute-start | bytes 6291464 | tf_op jit(solution)/shard_map/ppermute | solution.py:433
  4.7 47.2 %all-to-all-start = ((bf16[108,64,128]{2,1,0:T(8,128)(2,1)}), bf16[108,64,128]{2,1,0:T(8,128)(2,1)}, u32[]{:S(2)}, u32[]{:S(2)}) async-start(bf16[108,64,128]{2,1,0:T(8,128)(2,1)} %get-tuple-element.22), calls=%async_computation | async-start | bytes 3538944 | tf_op jit(solution)/shard_map/all_to_all | solution.py:431
  10.8 23.8 %collective-permute-start.1 = (bf16[80,64,128]{2,1,0:T(8,128)(2,1)}, bf16[80,64,128]{2,1,0:T(8,128)(2,1)}, u32[]{:S(2)}, u32[]{:S(2)}) collective-permute-start(bf16[80,64,128]{2,1,0:T(8,128)(2,1)} %get-tuple-element.21), channel_id=1, source_target_pairs={{4,8},{8,4},{5,9},{9,5},{6,10},{10,6},{7,11},{11,7},{20,24},{24,20... | collective-permute-start | bytes 3932168 | tf_op jit(solution)/shard_map/ppermute | solution.py:432
  22.8 11.8 %collective-permute-start.2 = (bf16[16,64,128]{2,1,0:T(8,128)(2,1)}, bf16[16,64,128]{2,1,0:T(8,128)(2,1)S(1)}, u32[]{:S(2)}, u32[]{:S(2)}) collective-permute-start(bf16[16,64,128]{2,1,0:T(8,128)(2,1)} %get-tuple-element.24), channel_id=1, source_target_pairs={{0,4},{4,0},{8,12},{12,8},{1,5},{5,1},{9,13},{13,9},{2,6},{6,2},{1... | collective-permute-start | bytes 786440 | tf_op jit(solution)/shard_map/ppermute | solution.py:457
  22.8 11.7 %collective-permute-start.3 = (bf16[16,64,128]{2,1,0:T(8,128)(2,1)}, bf16[16,64,128]{2,1,0:T(8,128)(2,1)S(1)}, u32[]{:S(2)}, u32[]{:S(2)}) collective-permute-start(bf16[16,64,128]{2,1,0:T(8,128)(2,1)} %get-tuple-element.25), channel_id=1, source_target_pairs={{4,8},{8,4},{5,9},{9,5},{6,10},{10,6},{7,11},{11,7},{20,24},{24,20... | collective-permute-start | bytes 786440 | tf_op jit(solution)/shard_map/ppermute | solution.py:455
  25.0 9.6 %collective-permute-start.4 = (bf16[8,64,128]{2,1,0:T(8,128)(2,1)}, bf16[8,64,128]{2,1,0:T(8,128)(2,1)S(1)}, u32[]{:S(2)}, u32[]{:S(2)}) collective-permute-start(bf16[8,64,128]{2,1,0:T(8,128)(2,1)} %get-tuple-element.26), channel_id=1, source_target_pairs={{0,8},{4,12},{8,0},{12,4},{1,9},{5,13},{9,1},{13,5},{2,10},{6,14},... | collective-permute-start | bytes 393224 | tf_op jit(solution)/shard_map/ppermute | solution.py:456
  34.6 0.6 copy-start.8
  34.6 0.8 copy-start.6
  34.6 0.9 copy-start.7
  45.6 14.8 %collective-permute-start.8 = (bf16[11,64,128]{2,1,0:T(8,128)(2,1)}, bf16[11,64,128]{2,1,0:T(8,128)(2,1)S(1)}, u32[]{:S(2)}, u32[]{:S(2)}) collective-permute-start(bf16[11,64,128]{2,1,0:T(8,128)(2,1)} %get-tuple-element.33), channel_id=1, source_target_pairs={{0,1},{1,0},{2,3},{3,2},{4,5},{5,4},{6,7},{7,6},{8,9},{9,8},{10,11... | collective-permute-start | bytes 540680 | tf_op jit(solution)/shard_map/ppermute | solution.py:397
  47.4 16.0 %collective-permute-start.9 = (bf16[11,64,128]{2,1,0:T(8,128)(2,1)}, bf16[11,64,128]{2,1,0:T(8,128)(2,1)S(1)}, u32[]{:S(2)}, u32[]{:S(2)}) collective-permute-start(bf16[11,64,128]{2,1,0:T(8,128)(2,1)} %get-tuple-element.34), channel_id=1, source_target_pairs={{0,2},{1,3},{2,0},{3,1},{4,6},{5,7},{6,4},{7,5},{8,10},{9,11},{10,... | collective-permute-start | bytes 540680 | tf_op jit(solution)/shard_map/ppermute | solution.py:397
  49.5 13.9 %collective-permute-start.10 = (bf16[11,64,128]{2,1,0:T(8,128)(2,1)}, bf16[11,64,128]{2,1,0:T(8,128)(2,1)S(1)}, u32[]{:S(2)}, u32[]{:S(2)}) collective-permute-start(bf16[11,64,128]{2,1,0:T(8,128)(2,1)} %get-tuple-element.35), channel_id=1, source_target_pairs={{0,3},{1,2},{2,1},{3,0},{4,7},{5,6},{6,5},{7,4},{8,11},{9,10},{10,... | collective-permute-start | bytes 540680 | tf_op jit(solution)/shard_map/ppermute | solution.py:397
  53.5 10.6 %collective-permute-start.6 = (bf16[13,256,128]{2,1,0:T(8,128)(2,1)S(1)}, bf16[13,256,128]{2,1,0:T(8,128)(2,1)S(1)}, u32[]{:S(2)}, u32[]{:S(2)}) collective-permute-start(bf16[13,256,128]{2,1,0:T(8,128)(2,1)S(1)} %get-tuple-element.32), channel_id=1, source_target_pairs={{0,4},{4,0},{8,12},{12,8},{1,5},{5,1},{9,13},{13,9},{2,6},{6,2},{1... | collective-permute-start | bytes 2555912 | tf_op jit(solution)/shard_map/ppermute | solution.py:517
  55.9 14.0 %collective-permute-start.7 = (bf16[13,256,128]{2,1,0:T(8,128)(2,1)S(1)}, bf16[13,256,128]{2,1,0:T(8,128)(2,1)S(1)}, u32[]{:S(2)}, u32[]{:S(2)}) collective-permute-start(bf16[13,256,128]{2,1,0:T(8,128)(2,1)S(1)} %get-tuple-element.32), channel_id=1, source_target_pairs={{4,8},{8,4},{5,9},{9,5},{6,10},{10,6},{7,11},{11,7},{20,24},{24,20... | collective-permute-start | bytes 2555912 | tf_op jit(solution)/shard_map/ppermute | solution.py:516
  60.4 9.6 %copy-start.1 = (f32[1,128,128]{2,1,0:T(8,128)S(1)}, f32[1,128,128]{2,1,0:T(8,128)}, u32[]{:S(2)}) copy-start(f32[1,128,128]{2,1,0:T(8,128)} %param.9) | copy-start | bytes 196612
  60.4 9.6 %copy-start.5 = (f32[256,16]{0,1:T(8,128)S(1)}, f32[256,16]{0,1:T(8,128)}, u32[]{:S(2)}) copy-start(f32[256,16]{0,1:T(8,128)} %param.14) | copy-start | bytes 49156
  60.4 18.0 %collective-permute-start.5 = (bf16[48,64,128]{2,1,0:T(8,128)(2,1)}, bf16[48,64,128]{2,1,0:T(8,128)(2,1)S(1)}, u32[]{:S(2)}, u32[]{:S(2)}) collective-permute-start(bf16[48,64,128]{2,1,0:T(8,128)(2,1)} %get-tuple-element.29), channel_id=1, source_target_pairs={{4,8},{8,4},{5,9},{9,5},{6,10},{10,6},{7,11},{11,7},{20,24},{24,20... | collective-permute-start | bytes 2359304 | tf_op jit(solution)/shard_map/ppermute | solution.py:518
  63.4 0.7 copy-start.2
  69.9 0.9 %copy-start.3 = (bf16[11,64,128]{2,1,0:T(8,128)(2,1)S(1)}, bf16[11,64,128]{2,1,0:T(8,128)(2,1)}, u32[]{:S(2)}) copy-start(bf16[11,64,128]{2,1,0:T(8,128)(2,1)} %copy-done.2) | copy-start | bytes 540676
  70.9 7.5 %copy-start = (bf16[128,64,128]{2,1,0:T(8,128)(2,1)S(1)}, bf16[128,64,128]{2,1,0:T(8,128)(2,1)}, u32[]{:S(2)}) copy-start(bf16[128,64,128]{2,1,0:T(8,128)(2,1)} %get-tuple-element.20.xt_hbm.xt_ref.last_ref.next_ref) | copy-start | bytes 6291460
  70.9 7.5 %copy-start.4 = (bf16[128,128]{1,0:T(8,128)(2,1)S(1)}, bf16[128,128]{1,0:T(8,128)(2,1)}, u32[]{:S(2)}) copy-start(bf16[128,128]{1,0:T(8,128)(2,1)} %constant.2.clone.ring_ref) | copy-start | bytes 98308
  74.5 11.9 %all-to-all-start.1 = ((bf16[16,64,128]{2,1,0:T(8,128)(2,1)}), bf16[16,64,128]{2,1,0:T(8,128)(2,1)S(1)}, u32[]{:S(2)}, u32[]{:S(2)}) async-start(bf16[16,64,128]{2,1,0:T(8,128)(2,1)} %get-tuple-element.37), calls=%async_computation.1 | async-start | bytes 524288 | tf_op jit(solution)/shard_map/all_to_all | solution.py:549

commit v30 on v28

--- a/solution.py
+++ b/solution.py
@@ -378,7 +378,7 @@
     per_group = LANES // proj_count
     groups = atoms_here // per_group
     share = lines // bands
-    first = 2 * (share * 3 // 32)
+    first = 2 * (share // 8)
     rest = share - first
 
     core_pairs = [(i, i ^ 1) for i in range(domains) if i ^ 1 < domains]

time: 86.7 us -> 90.7 us (1.046)
  starting transfers between devices: 26.9 us -> 36.2 us
  waiting for transfers between devices: 21.7 us -> 16.3 us
    all_to_all x1, starting transfers between devices: 3.9 us -> 11.4 us  [local(): lax.all_to_all(blocks, ('domain', 'band'), split_axis=0, concat_axis=0, t...]
    ppermute x1, waiting for transfers between devices: 4.05 us -> 0.01 us  [local(): later_link = lax.ppermute(later_pass, 'domain', link_pairs)]
    ppermute x1, starting transfers between devices: 2.37 us -> 5.39 us  [local(): link_late = lax.ppermute(late_part, 'domain', link_pairs)]
    all_to_all x1, waiting for transfers between devices: 2.36 us -> 0.01 us  [local(): lax.all_to_all(message, 'band', split_axis=0, concat_axis=0, tiled=True)]
    ppermute x1, waiting for transfers between devices: 1.7 us -> 0.01 us  [local(): link_late = lax.ppermute(late_part, 'domain', link_pairs)]
    all_to_all x1, waiting for transfers between devices: 1.5 us -> 3.17 us  [local(): lax.all_to_all(blocks, ('domain', 'band'), split_axis=0, concat_axis=0, t...]
    ppermute x1, starting transfers between devices: 4.64 us -> 3.5 us  [local(): later_link = lax.ppermute(later_pass, 'domain', link_pairs)]
    ppermute x3, waiting for transfers between devices: 2.78 us -> 3.9 us  [swapped(): lax.ppermute(values[k - 1], axis, [(i, i ^ k) for i in range(size)])]
  transfers between devices with their start and end apart: 13 -> 13, of which waited for: 7 -> 4; matrix products, arithmetic and copies ran while one was open for 0% -> 0% of each run, Pallas kernels for 35% -> 33%
where the time goes in v30:
time: 90.7 us; the launch traced here: 89.4 us
  starting transfers between devices  36.2 us (40%)
  Pallas kernels  34.5 us (38%)
  waiting for transfers between devices  16.3 us (18%)
  between operations  1.49 us (2%)
    pallas_call x10, Pallas kernels, call(): pl.pallas_call(kernel, grid=grid, out_shape=shapes, in_specs=in_specs, ou...  34.5 us
    all_to_all x1, starting transfers between devices, local(): lax.all_to_all(blocks, ('domain', 'band'), split_axis=0, concat_axis=0, t...  11.4 us
    ppermute x1, waiting for transfers between devices, local(): lax.ppermute(value, 'domain', pairs)  9.23 us
    all_to_all x1, starting transfers between devices, local(): lax.all_to_all(message, 'band', split_axis=0, concat_axis=0, tiled=True)  6.04 us
    ppermute x1, starting transfers between devices, local(): link_late = lax.ppermute(late_part, 'domain', link_pairs)  5.39 us
    ppermute x3, starting transfers between devices, swapped(): lax.ppermute(values[k - 1], axis, [(i, i ^ k) for i in range(size)])  3.97 us
    ppermute x3, waiting for transfers between devices, swapped(): lax.ppermute(values[k - 1], axis, [(i, i ^ k) for i in range(size)])  3.9 us
    ppermute x1, starting transfers between devices, local(): later_link = lax.ppermute(later_pass, 'domain', link_pairs)  3.5 us
  transfers between devices with their start and end apart: 13, of which 4 were waited for; matrix products, arithmetic and copies ran while one was open for 0% of the time, Pallas kernels for 33%

profile of v30, /device:TPU:1, one launch (start us, length us, event | category | flops | bytes accessed | tf_op | source)
XLA Modules:
  0.0 89.4 jit_solution(11939282051939790985)
XLA Ops:
  0.6 3.9 %shard_map.95 = (bf16[128,64,128]{2,1,0:T(8,128)(2,1)}, bf16[80,64,128]{2,1,0:T(8,128)(2,1)}, bf16[48,64,128]{2,1,0:T(8,128)(2,1)}, bf16[100,64,128]{2,1,0:T(8,128)(2,1)}) custom-call(bf16[64,128,128]{2,1,0:T(8,128)(2,1)} %bitcast.12), custom_call_target="tpu_custom_call" | custom-call | flops 1100000 | bytes 1024 | tf_op jit(solution)/shard_map/pallas_call | solution.py:34
  4.6 0.1 collective-permute-start
  4.7 6.0 %all-to-all-start = ((bf16[100,64,128]{2,1,0:T(8,128)(2,1)}), bf16[100,64,128]{2,1,0:T(8,128)(2,1)}, u32[]{:S(2)}, u32[]{:S(2)}) async-start(bf16[100,64,128]{2,1,0:T(8,128)(2,1)} %get-tuple-element.27), calls=%async_computation | async-start | bytes 3276800 | tf_op jit(solution)/shard_map/all_to_all | solution.py:426
  10.7 3.3 %collective-permute-start.1 = (bf16[80,64,128]{2,1,0:T(8,128)(2,1)}, bf16[80,64,128]{2,1,0:T(8,128)(2,1)}, u32[]{:S(2)}, u32[]{:S(2)}) collective-permute-start(bf16[80,64,128]{2,1,0:T(8,128)(2,1)} %get-tuple-element.26), channel_id=1, source_target_pairs={{4,8},{8,4},{5,9},{9,5},{6,10},{10,6},{7,11},{11,7},{20,24},{24,20... | collective-permute-start | bytes 3932168 | tf_op jit(solution)/shard_map/ppermute | solution.py:427
  14.7 8.1 %shard_map.96 = (bf16[24,64,128]{2,1,0:T(8,128)(2,1)}, bf16[16,64,128]{2,1,0:T(8,128)(2,1)}, bf16[16,64,128]{2,1,0:T(8,128)(2,1)}, bf16[8,64,128]{2,1,0:T(8,128)(2,1)}) custom-call(s32[384]{0:T(512)} %atom_ref.3, s32[384]{0:T(512)} %line_ref.3, s32[1]{0:T(128)S(6)} %copy.13.count_ref, ...), custom_call_target="tpu_custom_call" | custom-call | flops 1100000 | bytes 1024 | tf_op jit(solution)/shard_map/pallas_call | solution.py:34
  22.9 2.3 %collective-permute-start.3 = (bf16[16,64,128]{2,1,0:T(8,128)(2,1)}, bf16[16,64,128]{2,1,0:T(8,128)(2,1)S(1)}, u32[]{:S(2)}, u32[]{:S(2)}) collective-permute-start(bf16[16,64,128]{2,1,0:T(8,128)(2,1)} %get-tuple-element.30), channel_id=1, source_target_pairs={{4,8},{8,4},{5,9},{9,5},{6,10},{10,6},{7,11},{11,7},{20,24},{24,20... | collective-permute-start | bytes 786440 | tf_op jit(solution)/shard_map/ppermute | solution.py:450
  25.3 9.2 %collective-permute-done.4.refs_2_.refs_0_ = bf16[8,64,128]{2,1,0:T(8,128)(2,1)S(1)} collective-permute-done((bf16[8,64,128]{2,1,0:T(8,128)(2,1)}, bf16[8,64,128]{2,1,0:T(8,128)(2,1)S(1)}, u32[]{:S(2)}, u32[]{:S(2)}) %collective-permute-start.4) | collective-permute-done | bytes 131104 | tf_op jit(solution)/shard_map/ppermute | solution.py:451
  34.6 0.6 copy-done.6
  35.2 0.1 copy-done.4
  35.4 10.4 %shard_map.98 = (f32[128,64,128]{2,1,0:T(8,128)}, bf16[14,64,128]{2,1,0:T(8,128)(2,1)}, bf16[14,64,128]{2,1,0:T(8,128)(2,1)}, bf16[14,64,128]{2,1,0:T(8,128)(2,1)}, bf16[14,64,128]{2,1,0:T(8,128)(2,1)}) custom-call(s32[384]{0:T(512)} %atom_ref.3, s32[384]{0:T(512)} %line_ref.3, s32[1]{0:T(128)S(6)} %copy.13.count_ref, ...), custom_call_target="tpu_custom_call" | custom-call | flops 8800000000 | bytes 1024 | tf_op jit(solution)/shard_map/pallas_call | solution.py:34
  45.8 1.8 %collective-permute-start.6 = (bf16[14,64,128]{2,1,0:T(8,128)(2,1)}, bf16[14,64,128]{2,1,0:T(8,128)(2,1)S(1)}, u32[]{:S(2)}, u32[]{:S(2)}) collective-permute-start(bf16[14,64,128]{2,1,0:T(8,128)(2,1)} %get-tuple-element.37), channel_id=1, source_target_pairs={{0,1},{1,0},{2,3},{3,2},{4,5},{5,4},{6,7},{7,6},{8,9},{9,8},{10,11... | collective-permute-start | bytes 688136 | tf_op jit(solution)/shard_map/ppermute | solution.py:392
  47.6 2.1 %collective-permute-start.7 = (bf16[14,64,128]{2,1,0:T(8,128)(2,1)}, bf16[14,64,128]{2,1,0:T(8,128)(2,1)S(1)}, u32[]{:S(2)}, u32[]{:S(2)}) collective-permute-start(bf16[14,64,128]{2,1,0:T(8,128)(2,1)} %get-tuple-element.38), channel_id=1, source_target_pairs={{0,2},{1,3},{2,0},{3,1},{4,6},{5,7},{6,4},{7,5},{8,10},{9,11},{10,... | collective-permute-start | bytes 688136 | tf_op jit(solution)/shard_map/ppermute | solution.py:392
  49.7 1.5 %shard_map.99 = (bf16[25,256,128]{2,1,0:T(8,128)(2,1)S(1)}, bf16[12,256,128]{2,1,0:T(8,128)(2,1)S(1)}, bf16[48,64,128]{2,1,0:T(8,128)(2,1)}) custom-call(bf16[100,64,128]{2,1,0:T(8,128)(2,1)} %all-to-all-done.landed, bf16[14,64,128]{2,1,0:T(8,128)(2,1)} %get-tuple-element.32.unread.refs_0_, ...), custom_call_target="tpu_custom_call", output_to_operand_aliasing={{2}: (2, {})} | custom-call | flops 1100000 | bytes 1024 | tf_op jit(solution)/shard_map/pallas_call | solution.py:34
  51.2 3.5 %collective-permute-start.10 = (bf16[12,256,128]{2,1,0:T(8,128)(2,1)S(1)}, bf16[12,256,128]{2,1,0:T(8,128)(2,1)S(1)}, u32[]{:S(2)}, u32[]{:S(2)}) collective-permute-start(bf16[12,256,128]{2,1,0:T(8,128)(2,1)S(1)} %get-tuple-element.42), channel_id=1, source_target_pairs={{4,8},{8,4},{5,9},{9,5},{6,10},{10,6},{7,11},{11,7},{20,24},{24,20... | collective-permute-start | bytes 2359304 | tf_op jit(solution)/shard_map/ppermute | solution.py:511
  54.8 2.1 %collective-permute-done.6.refs_1_ = bf16[14,64,128]{2,1,0:T(8,128)(2,1)S(1)} collective-permute-done((bf16[14,64,128]{2,1,0:T(8,128)(2,1)}, bf16[14,64,128]{2,1,0:T(8,128)(2,1)S(1)}, u32[]{:S(2)}, u32[]{:S(2)}) %collective-permute-start.6) | collective-permute-done | bytes 229408 | tf_op jit(solution)/shard_map/ppermute | solution.py:392
  56.9 5.4 %collective-permute-start.5 = (bf16[48,64,128]{2,1,0:T(8,128)(2,1)}, bf16[48,64,128]{2,1,0:T(8,128)(2,1)S(1)}, u32[]{:S(2)}, u32[]{:S(2)}) collective-permute-start(bf16[48,64,128]{2,1,0:T(8,128)(2,1)} %get-tuple-element.34), channel_id=1, source_target_pairs={{4,8},{8,4},{5,9},{9,5},{6,10},{10,6},{7,11},{11,7},{20,24},{24,20... | collective-permute-start | bytes 2359304 | tf_op jit(solution)/shard_map/ppermute | solution.py:513
  62.3 1.8 %collective-permute-done.8.refs_3_ = bf16[14,64,128]{2,1,0:T(8,128)(2,1)S(1)} collective-permute-done((bf16[14,64,128]{2,1,0:T(8,128)(2,1)}, bf16[14,64,128]{2,1,0:T(8,128)(2,1)S(1)}, u32[]{:S(2)}, u32[]{:S(2)}) %collective-permute-start.8) | collective-permute-done | bytes 229408 | tf_op jit(solution)/shard_map/ppermute | solution.py:392
  64.1 1.1 %shard_map.100 = (bf16[9,256,128]{2,1,0:T(8,128)(2,1)S(1)}, bf16[4,256,128]{2,1,0:T(8,128)(2,1)S(1)}, bf16[2,256,128]{2,1,0:T(8,128)(2,1)S(1)}, f32[32,128]{1,0:T(8,128)S(1)}, f32[8,128]{1,0:T(8,128)}) custom-call(bf16[25,256,128]{2,1,0:T(8,128)(2,1)S(1)} %get-tuple-element.36.after_ref.all_ref, f32[16,256]{1,0:T(8,128)S(1)} %bitcast.10, ...), custom_call_target="tpu_custom_call" | custom-call | flops 32999999488 | bytes 1024 | tf_op jit(solution)/shard_map/pallas_call | solution.py:34
  65.2 1.1 %shard_map.101.begun_ref = f32[2,256,256]{2,1,0:T(8,128)S(1)} custom-call(bf16[25,256,128]{2,1,0:T(8,128)(2,1)S(1)} %get-tuple-element.36.after_ref.all_ref, bf16[12,256,128]{2,1,0:T(8,128)(2,1)S(1)} %collective-permute-done.9.core_ref, bf16[12,256,128]{2,1,0:T(8,128)(2,1)S(1)} %collective-permute-done.10.link_ref, f32[128,128]{1,0:T(8,128)S(1)} %bitcast.6, ...), custom_call_target="tpu_custom_call" | custom-call | flops 1100000 | bytes 1024 | tf_op jit(solution)/shard_map/pallas_call | solution.py:34
  66.4 1.5 %shard_map.102 = (bf16[16,64,128]{2,1,0:T(8,128)(2,1)}, f32[8,128]{1,0:T(8,128)}) custom-call(bf16[9,256,128]{2,1,0:T(8,128)(2,1)S(1)} %get-tuple-element.40.all_ref, bf16[4,256,128]{2,1,0:T(8,128)(2,1)S(1)} %get-tuple-element.41.beside_ref, f32[128,128]{1,0:T(8,128)S(1)} %bitcast.7, f32[2,256,256]{2,1,0:T(8,128)S(1)} %shard_map.101.begun_ref, ...), custom_call_target="tpu_custom_call" | custom-call | flops 1100000 | bytes 1024 | tf_op jit(solution)/shard_map/pallas_call | solution.py:34
  67.9 11.4 %all-to-all-start.1 = ((bf16[16,64,128]{2,1,0:T(8,128)(2,1)}), bf16[16,64,128]{2,1,0:T(8,128)(2,1)S(1)}, u32[]{:S(2)}, u32[]{:S(2)}) async-start(bf16[16,64,128]{2,1,0:T(8,128)(2,1)} %get-tuple-element.47), calls=%async_computation.1 | async-start | bytes 524288 | tf_op jit(solution)/shard_map/all_to_all | solution.py:553
  79.4 6.2 %shard_map.103 = bf16[64,128,128]{2,1,0:T(8,128)(2,1)} custom-call(bf16[128,64,128]{2,1,0:T(8,128)(2,1)S(1)} %copy-done, bf16[128,64,128]{2,1,0:T(8,128)(2,1)S(1)} %copy-done, bf16[128,64,128]{2,1,0:T(8,128)(2,1)S(1)} %copy-done, bf16[128,64,128]{2,1,0:T(8,128)(2,1)} %collective-permute-done.refs_4_.beside_hbm.core_ref, ...), custom_call_target="tpu_custom_call" | custom-call | flops 1100000 | bytes 1024 | tf_op jit(solution)/shard_map/pallas_call | solution.py:34
  85.5 3.2 %all-to-all-done.1.parts_ref = bf16[16,64,128]{2,1,0:T(8,128)(2,1)S(1)} async-done(((bf16[16,64,128]{2,1,0:T(8,128)(2,1)}), bf16[16,64,128]{2,1,0:T(8,128)(2,1)S(1)}, u32[]{:S(2)}, u32[]{:S(2)}) %all-to-all-start.1) | async-done | bytes 262176 | tf_op jit(solution)/shard_map/all_to_all | solution.py:553
  88.7 0.7 shard_map.104
  (26 shorter events, 0.4 us)
Async XLA Ops:
  4.6 30.0 %collective-permute-start = (bf16[128,64,128]{2,1,0:T(8,128)(2,1)}, bf16[128,64,128]{2,1,0:T(8,128)(2,1)}, u32[]{:S(2)}, u32[]{:S(2)}) collective-permute-start(bf16[128,64,128]{2,1,0:T(8,128)(2,1)} %get-tuple-element.25.xt_hbm.xt_ref.last_ref.next_ref), channel_id=1, source_target_pairs={{0,4},{4,0},{8,12},{12,8},{1,5},{5,1},{9,13},{13,9},{2,6},{6,2},{1... | collective-permute-start | bytes 6291464 | tf_op jit(solution)/shard_map/ppermute | solution.py:428
  4.7 45.1 %all-to-all-start = ((bf16[100,64,128]{2,1,0:T(8,128)(2,1)}), bf16[100,64,128]{2,1,0:T(8,128)(2,1)}, u32[]{:S(2)}, u32[]{:S(2)}) async-start(bf16[100,64,128]{2,1,0:T(8,128)(2,1)} %get-tuple-element.27), calls=%async_computation | async-start | bytes 3276800 | tf_op jit(solution)/shard_map/all_to_all | solution.py:426
  10.7 23.8 %collective-permute-start.1 = (bf16[80,64,128]{2,1,0:T(8,128)(2,1)}, bf16[80,64,128]{2,1,0:T(8,128)(2,1)}, u32[]{:S(2)}, u32[]{:S(2)}) collective-permute-start(bf16[80,64,128]{2,1,0:T(8,128)(2,1)} %get-tuple-element.26), channel_id=1, source_target_pairs={{4,8},{8,4},{5,9},{9,5},{6,10},{10,6},{7,11},{11,7},{20,24},{24,20... | collective-permute-start | bytes 3932168 | tf_op jit(solution)/shard_map/ppermute | solution.py:427
  22.9 11.7 %collective-permute-start.2 = (bf16[16,64,128]{2,1,0:T(8,128)(2,1)}, bf16[16,64,128]{2,1,0:T(8,128)(2,1)S(1)}, u32[]{:S(2)}, u32[]{:S(2)}) collective-permute-start(bf16[16,64,128]{2,1,0:T(8,128)(2,1)} %get-tuple-element.29), channel_id=1, source_target_pairs={{0,4},{4,0},{8,12},{12,8},{1,5},{5,1},{9,13},{13,9},{2,6},{6,2},{1... | collective-permute-start | bytes 786440 | tf_op jit(solution)/shard_map/ppermute | solution.py:452
  22.9 11.6 %collective-permute-start.3 = (bf16[16,64,128]{2,1,0:T(8,128)(2,1)}, bf16[16,64,128]{2,1,0:T(8,128)(2,1)S(1)}, u32[]{:S(2)}, u32[]{:S(2)}) collective-permute-start(bf16[16,64,128]{2,1,0:T(8,128)(2,1)} %get-tuple-element.30), channel_id=1, source_target_pairs={{4,8},{8,4},{5,9},{9,5},{6,10},{10,6},{7,11},{11,7},{20,24},{24,20... | collective-permute-start | bytes 786440 | tf_op jit(solution)/shard_map/ppermute | solution.py:450
  25.2 9.3 %collective-permute-start.4 = (bf16[8,64,128]{2,1,0:T(8,128)(2,1)}, bf16[8,64,128]{2,1,0:T(8,128)(2,1)S(1)}, u32[]{:S(2)}, u32[]{:S(2)}) collective-permute-start(bf16[8,64,128]{2,1,0:T(8,128)(2,1)} %get-tuple-element.31), channel_id=1, source_target_pairs={{0,8},{4,12},{8,0},{12,4},{1,9},{5,13},{9,1},{13,5},{2,10},{6,14},... | collective-permute-start | bytes 393224 | tf_op jit(solution)/shard_map/ppermute | solution.py:451
  34.5 0.6 copy-start.6
  34.5 0.8 copy-start.4
  34.5 0.8 copy-start.5
  45.8 18.4 %copy-start.3 = (f32[256,16]{0,1:T(8,128)S(1)}, f32[256,16]{0,1:T(8,128)}, u32[]{:S(2)}) copy-start(f32[256,16]{0,1:T(8,128)} %param.14) | copy-start | bytes 49156
  45.8 11.2 %collective-permute-start.6 = (bf16[14,64,128]{2,1,0:T(8,128)(2,1)}, bf16[14,64,128]{2,1,0:T(8,128)(2,1)S(1)}, u32[]{:S(2)}, u32[]{:S(2)}) collective-permute-start(bf16[14,64,128]{2,1,0:T(8,128)(2,1)} %get-tuple-element.37), channel_id=1, source_target_pairs={{0,1},{1,0},{2,3},{3,2},{4,5},{5,4},{6,7},{7,6},{8,9},{9,8},{10,11... | collective-permute-start | bytes 688136 | tf_op jit(solution)/shard_map/ppermute | solution.py:392
  47.6 14.7 %collective-permute-start.7 = (bf16[14,64,128]{2,1,0:T(8,128)(2,1)}, bf16[14,64,128]{2,1,0:T(8,128)(2,1)S(1)}, u32[]{:S(2)}, u32[]{:S(2)}) collective-permute-start(bf16[14,64,128]{2,1,0:T(8,128)(2,1)} %get-tuple-element.38), channel_id=1, source_target_pairs={{0,2},{1,3},{2,0},{3,1},{4,6},{5,7},{6,4},{7,5},{8,10},{9,11},{10,... | collective-permute-start | bytes 688136 | tf_op jit(solution)/shard_map/ppermute | solution.py:392
  49.7 14.4 %collective-permute-start.8 = (bf16[14,64,128]{2,1,0:T(8,128)(2,1)}, bf16[14,64,128]{2,1,0:T(8,128)(2,1)S(1)}, u32[]{:S(2)}, u32[]{:S(2)}) collective-permute-start(bf16[14,64,128]{2,1,0:T(8,128)(2,1)} %get-tuple-element.39), channel_id=1, source_target_pairs={{0,3},{1,2},{2,1},{3,0},{4,7},{5,6},{6,5},{7,4},{8,11},{9,10},{10,... | collective-permute-start | bytes 688136 | tf_op jit(solution)/shard_map/ppermute | solution.py:392
  51.2 14.0 %collective-permute-start.10 = (bf16[12,256,128]{2,1,0:T(8,128)(2,1)S(1)}, bf16[12,256,128]{2,1,0:T(8,128)(2,1)S(1)}, u32[]{:S(2)}, u32[]{:S(2)}) collective-permute-start(bf16[12,256,128]{2,1,0:T(8,128)(2,1)S(1)} %get-tuple-element.42), channel_id=1, source_target_pairs={{4,8},{8,4},{5,9},{9,5},{6,10},{10,6},{7,11},{11,7},{20,24},{24,20... | collective-permute-start | bytes 2359304 | tf_op jit(solution)/shard_map/ppermute | solution.py:511
  54.7 10.5 %collective-permute-start.9 = (bf16[12,256,128]{2,1,0:T(8,128)(2,1)S(1)}, bf16[12,256,128]{2,1,0:T(8,128)(2,1)S(1)}, u32[]{:S(2)}, u32[]{:S(2)}) collective-permute-start(bf16[12,256,128]{2,1,0:T(8,128)(2,1)S(1)} %get-tuple-element.42), channel_id=1, source_target_pairs={{0,4},{4,0},{8,12},{12,8},{1,5},{5,1},{9,13},{13,9},{2,6},{6,2},{1... | collective-permute-start | bytes 2359304 | tf_op jit(solution)/shard_map/ppermute | solution.py:512
  56.9 22.4 %collective-permute-start.5 = (bf16[48,64,128]{2,1,0:T(8,128)(2,1)}, bf16[48,64,128]{2,1,0:T(8,128)(2,1)S(1)}, u32[]{:S(2)}, u32[]{:S(2)}) collective-permute-start(bf16[48,64,128]{2,1,0:T(8,128)(2,1)} %get-tuple-element.34), channel_id=1, source_target_pairs={{4,8},{8,4},{5,9},{9,5},{6,10},{10,6},{7,11},{11,7},{20,24},{24,20... | collective-permute-start | bytes 2359304 | tf_op jit(solution)/shard_map/ppermute | solution.py:513
  64.1 1.1 %copy-start.1 = (f32[1,128,128]{2,1,0:T(8,128)S(1)}, f32[1,128,128]{2,1,0:T(8,128)}, u32[]{:S(2)}) copy-start(f32[1,128,128]{2,1,0:T(8,128)} %param.9) | copy-start | bytes 196612
  65.2 14.1 %copy-start.2 = (bf16[128,128]{1,0:T(8,128)(2,1)S(1)}, bf16[128,128]{1,0:T(8,128)(2,1)}, u32[]{:S(2)}) copy-start(bf16[128,128]{1,0:T(8,128)(2,1)} %constant.2.clone.ring_ref) | copy-start | bytes 98308
  66.4 13.0 %copy-start = (bf16[128,64,128]{2,1,0:T(8,128)(2,1)S(1)}, bf16[128,64,128]{2,1,0:T(8,128)(2,1)}, u32[]{:S(2)}) copy-start(bf16[128,64,128]{2,1,0:T(8,128)(2,1)} %get-tuple-element.25.xt_hbm.xt_ref.last_ref.next_ref) | copy-start | bytes 6291460
  67.9 20.8 %all-to-all-start.1 = ((bf16[16,64,128]{2,1,0:T(8,128)(2,1)}), bf16[16,64,128]{2,1,0:T(8,128)(2,1)S(1)}, u32[]{:S(2)}, u32[]{:S(2)}) async-start(bf16[16,64,128]{2,1,0:T(8,128)(2,1)} %get-tuple-element.47), calls=%async_computation.1 | async-start | bytes 524288 | tf_op jit(solution)/shard_map/all_to_all | solution.py:553
